TPU v7x, 32 devices: a whole 2x2x4 slice. The times are simulated.
32 devices in a mesh: rep: 4 (over z), ctx: 4 (over y, core), shard: 2 (over x).
Axes of the slice: x: 2, y: 2, z: 4, core: 2. Of those that a mesh axis runs over, the one named last changes fastest.
Arguments:
- tokens: bfloat16 [4, 512, 2, 2048], P('rep', 'ctx', 'shard'), may hold values from -6 to 6
- cotangent: bfloat16 [4, 512, 2, 2048], P('rep', 'ctx', 'shard'), may hold values from -6 to 6
- span_order: int32 [4, 2, 8], P('rep', 'shard'), may hold values from 0 to 7, each once within a row
- w_qkv: float32 [2048, 6144], P(('ctx', 'shard')), may hold values from -0.125 to 0.125
- w_out: float32 [2048, 2048], P(('ctx', 'shard')), may hold values from -0.75 to 0.75
- w_up: float32 [2048, 11264], P(('ctx', 'shard')), may hold values from -0.125 to 0.125
- w_down: float32 [5632, 2048], P(('ctx', 'shard')), may hold values from -0.078125 to 0.078125
- norm_params: float32 [7, 2048], replicated, may hold values from -2 to 2, as said below
- m_qkv: float32 [2048, 6144], P(('ctx', 'shard')), may hold values from -64 to 64
- v_qkv: float32 [2048, 6144], P(('ctx', 'shard')), may hold values from 4.096 to 65.536
- m_out: float32 [2048, 2048], P(('ctx', 'shard')), may hold values from -6 to 6
- v_out: float32 [2048, 2048], P(('ctx', 'shard')), may hold values from 0.08192 to 1.2288
- m_up: float32 [2048, 11264], P(('ctx', 'shard')), may hold values from -16 to 16
- v_up: float32 [2048, 11264], P(('ctx', 'shard')), may hold values from 0.32768 to 5.3248
- m_down: float32 [5632, 2048], P(('ctx', 'shard')), may hold values from -24 to 24
- v_down: float32 [5632, 2048], P(('ctx', 'shard')), may hold values from 0.73728 to 12.288
- m_norm: float32 [7, 2048], replicated, may hold values from -80 to 80
- v_norm: float32 [7, 2048], replicated, may hold values from 4.096 to 65.536
Outputs:
- block_output: bfloat16 [4, 512, 2, 2048], P('rep', 'ctx', 'shard')
- input_grad: float32 [4, 512, 2, 2048], P('rep', 'ctx', 'shard')
- new_m_qkv: float32 [2048, 6144], P(('ctx', 'shard'))
- new_v_qkv: float32 [2048, 6144], P(('ctx', 'shard'))
- new_w_qkv: float32 [2048, 6144], P(('ctx', 'shard'))
- new_m_out: float32 [2048, 2048], P(('ctx', 'shard'))
- new_v_out: float32 [2048, 2048], P(('ctx', 'shard'))
- new_w_out: float32 [2048, 2048], P(('ctx', 'shard'))
- new_m_up: float32 [2048, 11264], P(('ctx', 'shard'))
- new_v_up: float32 [2048, 11264], P(('ctx', 'shard'))
- new_w_up: float32 [2048, 11264], P(('ctx', 'shard'))
- new_m_down: float32 [5632, 2048], P(('ctx', 'shard'))
- new_v_down: float32 [5632, 2048], P(('ctx', 'shard'))
- new_w_down: float32 [5632, 2048], P(('ctx', 'shard'))
- new_m_norm: float32 [7, 2048], replicated
- new_v_norm: float32 [7, 2048], replicated
- new_norm_params: float32 [7, 2048], replicated
Inputs may be any that keep to these rules, and one draw needn't show every extreme that they name: `span_order`: each row is a permutation of 0 to 7. `norm_params`: rows 0 and 2 lie between 0.4 and 1.6.
All inputs are finite; a program needn't handle non-finite values.
Results may differ from a plain program's by a relative error of at most 0.018.
Values may be sent and summed in bfloat16 or wider, within the bound.
No kernel may reach another device: no remote copies, remote signals or barrier semaphores. Data moves between devices by JAX's collectives and lax.ppermute only.
A program may use at most 832 MiB of HBM per device.

v0:
```python
import jax
import jax.numpy as jnp
from jax import lax
from jax.sharding import PartitionSpec as P

HEADS = 32
HEAD_DIM = 64
FF = 5632
ROTARY = 16
STEP = 10


eps_norm = 1e-05
masked_score = -1e30
beta_one = 0.9
beta_two = 0.999
adam_eps = 1e-08
weight_decay = 0.1
contract_last = (((1,), (1,)), ((), ()))
contract_first = (((0,), (0,)), ((), ()))


def norm_forward(hidden, gain_row, shift_row):
    centred = hidden - jnp.mean(hidden, axis=-1, keepdims=True)
    inv_scale = lax.rsqrt(jnp.mean(centred * centred, axis=-1, keepdims=True) + eps_norm)
    unit_rows = centred * inv_scale
    return (unit_rows, inv_scale, unit_rows * gain_row + shift_row)


def norm_backward(grad_norm, unit_rows, inv_scale, gain_row):
    scaled = grad_norm * gain_row
    return inv_scale * (
        scaled
        - jnp.mean(scaled, axis=-1, keepdims=True)
        - unit_rows * jnp.mean(scaled * unit_rows, axis=-1, keepdims=True)
    )


def rotary_tables(positions):
    exponent = jnp.arange(ROTARY // 2, dtype=jnp.float32)
    inverse = 10000.0 ** (-2.0 * exponent / ROTARY)
    angles = positions.astype(jnp.float32)[:, None] * inverse[None, :]
    return (jnp.cos(angles)[:, None, :], jnp.sin(angles)[:, None, :])


def rotate(values, cosine_table, sine_table):
    half_rot = ROTARY // 2
    lower_half = values[..., :half_rot]
    upper_half = values[..., half_rot:ROTARY]
    return jnp.concatenate(
        [
            lower_half * cosine_table - upper_half * sine_table,
            upper_half * cosine_table + lower_half * sine_table,
            values[..., ROTARY:],
        ],
        axis=-1,
    )


def unrotate(values, cosine_table, sine_table):
    half_rot = ROTARY // 2
    lower_half = values[..., :half_rot]
    upper_half = values[..., half_rot:ROTARY]
    return jnp.concatenate(
        [
            lower_half * cosine_table + upper_half * sine_table,
            upper_half * cosine_table - lower_half * sine_table,
            values[..., ROTARY:],
        ],
        axis=-1,
    )


def head_blocks(values, group_size):
    row_count = values.shape[0]
    return values.reshape(row_count, HEADS // group_size, group_size, HEAD_DIM).transpose(
        1, 2, 0, 3
    )


def head_merge(values):
    block_count, group_size, row_count, head_size = values.shape
    return values.transpose(2, 0, 1, 3).reshape(row_count, block_count * group_size * head_size)


def block_scores(query_g, key_g, allowed, score_scale):
    scores = (
        jnp.einsum("gtd,gsd->gts", query_g, key_g, preferred_element_type=jnp.float32) * score_scale
    )
    return jnp.where(allowed[None], scores, masked_score)


def attend_block(inputs, allowed, score_scale):
    query_g, key_g, value_g = inputs
    scores = block_scores(query_g, key_g, allowed, score_scale)
    row_peak = jnp.max(scores, axis=-1, keepdims=True)
    exponent = jnp.exp(scores - row_peak)
    row_total = jnp.sum(exponent, axis=-1, keepdims=True)
    prob_low = (exponent / row_total).astype(jnp.bfloat16)
    attended = jnp.einsum("gts,gsd->gtd", prob_low, value_g, preferred_element_type=jnp.float32)
    return (attended, row_peak, row_total)


def attend_back(inputs, allowed, score_scale):
    query_g, key_g, value_g, dout_g, row_peak, row_total = inputs
    scores = block_scores(query_g, key_g, allowed, score_scale)
    probs_full = jnp.exp(scores - row_peak) / row_total
    prob_low = probs_full.astype(jnp.bfloat16)
    dprob = jnp.einsum("gtd,gsd->gts", dout_g, value_g, preferred_element_type=jnp.float32)
    inner = jnp.sum(probs_full * dprob, axis=-1, keepdims=True)
    dscore = (probs_full * (dprob - inner)).astype(jnp.bfloat16)
    dquery = (
        jnp.einsum("gts,gsd->gtd", dscore, key_g, preferred_element_type=jnp.float32) * score_scale
    )
    dkey = (
        jnp.einsum("gts,gtd->gsd", dscore, query_g, preferred_element_type=jnp.float32)
        * score_scale
    )
    dvalue = jnp.einsum("gts,gtd->gsd", prob_low, dout_g, preferred_element_type=jnp.float32)
    return (dquery, dkey, dvalue)


def transposed_product(left_rows, shard_piece):
    return lax.dot_general(
        left_rows, shard_piece, contract_last, preferred_element_type=jnp.float32
    )


def slice_product(acts, grads):
    return lax.dot_general(acts, grads, contract_first, preferred_element_type=jnp.float32)


def adam_update(weight, moment_one, moment_two, grad, step_rate, decay_rate):
    first_new = beta_one * moment_one + (1.0 - beta_one) * grad
    second_new = beta_two * moment_two + (1.0 - beta_two) * grad * grad
    first_hat = first_new / (1.0 - beta_one**STEP)
    second_hat = second_new / (1.0 - beta_two**STEP)
    weight_new = weight - step_rate * (
        first_hat / (jnp.sqrt(second_hat) + adam_eps) + decay_rate * weight
    )
    return (first_new, second_new, weight_new)


def body(
    tokens,
    cotangent,
    span_order,
    w_qkv,
    w_out,
    w_up,
    w_down,
    norm_params,
    m_qkv,
    v_qkv,
    m_out,
    v_out,
    m_up,
    v_up,
    m_down,
    v_down,
    m_norm,
    v_norm,
):
    model_width = tokens.shape[3]
    row_count = tokens.shape[1]
    seq_len = row_count * lax.axis_size("ctx")
    half_rows = row_count // 2
    score_scale = HEAD_DIM ** (-0.5)
    group_size = 4
    input_rows = tokens.reshape(row_count, model_width).astype(jnp.float32)
    grad_low = cotangent.reshape(row_count, model_width)
    order_row = span_order.reshape(-1)
    slot_ids = jnp.arange(seq_len, dtype=jnp.int32)
    span_match = (slot_ids // half_rows)[:, None] == jnp.arange(
        order_row.shape[0], dtype=jnp.int32
    )[None, :]
    span_place = jnp.sum(jnp.where(span_match, order_row[None, :], 0), axis=1)
    pos_all = span_place * half_rows + slot_ids % half_rows
    pos_mine = lax.dynamic_slice_in_dim(pos_all, lax.axis_index("ctx") * row_count, row_count)
    allowed = pos_all[None, :] <= pos_mine[:, None]
    cosine_table, sine_table = rotary_tables(pos_mine)
    heads_shape = (row_count, HEADS, HEAD_DIM)
    qkv_low = w_qkv.astype(jnp.bfloat16)
    out_low = w_out.astype(jnp.bfloat16)
    up_low = w_up.astype(jnp.bfloat16)
    down_low = w_down.astype(jnp.bfloat16)
    full_qkv, full_out = (
        lax.all_gather(qkv_low, ("ctx", "shard"), axis=0, tiled=True),
        lax.all_gather(out_low, ("ctx", "shard"), axis=0, tiled=True),
    )
    unit_one, inv_one, normed_one = norm_forward(input_rows, norm_params[0], norm_params[1])
    norm_low_one = normed_one.astype(jnp.bfloat16)
    qkv_linear = jnp.dot(norm_low_one, full_qkv, preferred_element_type=jnp.float32) + norm_params[
        4:7
    ].reshape(-1)
    query_low = rotate(qkv_linear[:, :model_width].reshape(heads_shape), cosine_table, sine_table)
    query_low = query_low.reshape(row_count, model_width).astype(jnp.bfloat16)
    key_low = rotate(
        qkv_linear[:, model_width : 2 * model_width].reshape(heads_shape), cosine_table, sine_table
    )
    key_low = key_low.reshape(row_count, model_width).astype(jnp.bfloat16)
    value_low = qkv_linear[:, 2 * model_width :].astype(jnp.bfloat16)
    key_all, value_all = (
        lax.all_gather(key_low, "ctx", axis=0, tiled=True),
        lax.all_gather(value_low, "ctx", axis=0, tiled=True),
    )
    query_g = head_blocks(query_low, group_size)
    attended, row_peak, row_total = lax.map(
        lambda inputs: attend_block(inputs, allowed, score_scale),
        (query_g, head_blocks(key_all, group_size), head_blocks(value_all, group_size)),
    )
    attn_low = head_merge(attended).astype(jnp.bfloat16)
    hidden_one = input_rows + jnp.dot(attn_low, full_out, preferred_element_type=jnp.float32)
    unit_two, inv_two, normed_two = norm_forward(hidden_one, norm_params[2], norm_params[3])
    norm_low_two = normed_two.astype(jnp.bfloat16)
    full_up, full_down = (
        lax.all_gather(up_low, ("ctx", "shard"), axis=0, tiled=True),
        lax.all_gather(down_low, ("ctx", "shard"), axis=0, tiled=True),
    )
    gate_up = jnp.dot(norm_low_two, full_up, preferred_element_type=jnp.float32)
    gate_part = gate_up[:, :FF]
    up_part = gate_up[:, FF:]
    silu_gate = jax.nn.silu(gate_part)
    act_low = (silu_gate * up_part).astype(jnp.bfloat16)
    block_output = (
        hidden_one + jnp.dot(act_low, full_down, preferred_element_type=jnp.float32)
    ).astype(jnp.bfloat16)
    grad_act = transposed_product(
        grad_low, lax.all_gather(down_low, ("ctx", "shard"), axis=0, tiled=True)
    )
    gate_sigmoid = jax.nn.sigmoid(gate_part)
    grad_gate = grad_act * up_part * gate_sigmoid * (1.0 + gate_part * (1.0 - gate_sigmoid))
    grad_gate_up = jnp.concatenate([grad_gate, grad_act * silu_gate], axis=1).astype(jnp.bfloat16)
    grad_norm_two = transposed_product(
        grad_gate_up, lax.all_gather(up_low, ("ctx", "shard"), axis=0, tiled=True)
    )
    grad_hidden = grad_low.astype(jnp.float32) + norm_backward(
        grad_norm_two, unit_two, inv_two, norm_params[2]
    )
    grad_branch = grad_hidden.astype(jnp.bfloat16)
    grad_attn = transposed_product(
        grad_branch, lax.all_gather(out_low, ("ctx", "shard"), axis=0, tiled=True)
    )
    key_use, value_use = (
        lax.all_gather(key_low, "ctx", axis=0, tiled=True),
        lax.all_gather(value_low, "ctx", axis=0, tiled=True),
    )
    grad_attn_low = grad_attn.astype(jnp.bfloat16)
    grad_query_g, grad_key_g, grad_value_g = lax.map(
        lambda inputs: attend_back(inputs, allowed, score_scale),
        (
            query_g,
            head_blocks(key_use, group_size),
            head_blocks(value_use, group_size),
            head_blocks(grad_attn_low, group_size),
            row_peak,
            row_total,
        ),
    )
    grad_key_sum, grad_value_sum = (
        lax.psum_scatter(
            head_merge(grad_key_g).astype(jnp.bfloat16), "ctx", scatter_dimension=0, tiled=True
        ).astype(jnp.float32),
        lax.psum_scatter(
            head_merge(grad_value_g).astype(jnp.bfloat16), "ctx", scatter_dimension=0, tiled=True
        ).astype(jnp.float32),
    )
    grad_query = unrotate(head_merge(grad_query_g).reshape(heads_shape), cosine_table, sine_table)
    grad_key = unrotate(grad_key_sum.reshape(heads_shape), cosine_table, sine_table)
    grad_qkv = jnp.concatenate(
        [
            grad_query.reshape(row_count, model_width),
            grad_key.reshape(row_count, model_width),
            grad_value_sum,
        ],
        axis=1,
    ).astype(jnp.bfloat16)
    grad_norm_one = transposed_product(
        grad_qkv, lax.all_gather(qkv_low, ("ctx", "shard"), axis=0, tiled=True)
    )
    input_grad = grad_hidden + norm_backward(grad_norm_one, unit_one, inv_one, norm_params[0])
    bias_grad = jnp.sum(grad_qkv.astype(jnp.float32), axis=0).reshape(3, model_width)
    norm_grad = jnp.concatenate(
        [
            jnp.stack(
                [
                    jnp.sum(grad_norm_one * unit_one, axis=0),
                    jnp.sum(grad_norm_one, axis=0),
                    jnp.sum(grad_norm_two * unit_two, axis=0),
                    jnp.sum(grad_norm_two, axis=0),
                ]
            ),
            bias_grad,
        ],
        axis=0,
    )
    norm_grad = lax.psum(norm_grad, ("rep", "ctx", "shard"))
    grad_rows = lax.psum_scatter(
        jnp.concatenate(
            [
                slice_product(norm_low_one, grad_qkv),
                slice_product(attn_low, grad_branch),
                slice_product(norm_low_two, grad_gate_up),
            ],
            axis=1,
        ).astype(jnp.bfloat16),
        ("ctx", "shard"),
        scatter_dimension=0,
        tiled=True,
    ).astype(jnp.float32)
    grad_down_rows = lax.psum_scatter(
        slice_product(act_low, grad_low).astype(jnp.bfloat16),
        ("ctx", "shard"),
        scatter_dimension=0,
        tiled=True,
    ).astype(jnp.float32)
    grad_rows, grad_down_rows = lax.psum((grad_rows, grad_down_rows), "rep")
    g_qkv = grad_rows[:, : 3 * model_width]
    g_out = grad_rows[:, 3 * model_width : 4 * model_width]
    g_up = grad_rows[:, 4 * model_width :]
    mq, vq, wq = adam_update(w_qkv, m_qkv, v_qkv, g_qkv, 0.03, weight_decay)
    mo, vo, wo = adam_update(w_out, m_out, v_out, g_out, 0.2, weight_decay)
    mu_new, vu_new, wu_new = adam_update(w_up, m_up, v_up, g_up, 0.03, weight_decay)
    md, vd, wd_new = adam_update(w_down, m_down, v_down, grad_down_rows, 0.02, weight_decay)
    mn, vn, wn = adam_update(norm_params, m_norm, v_norm, norm_grad, 0.3, 0.0)
    return (
        block_output.reshape(tokens.shape),
        input_grad.reshape(tokens.shape),
        mq,
        vq,
        wq,
        mo,
        vo,
        wo,
        mu_new,
        vu_new,
        wu_new,
        md,
        vd,
        wd_new,
        mn,
        vn,
        wn,
    )


def solution(mesh):
    placed = (
        P("rep", "ctx", "shard", None),
        P("rep", "ctx", "shard", None),
        P("rep", "shard", None),
        P(("ctx", "shard"), None),
        P(("ctx", "shard"), None),
        P(("ctx", "shard"), None),
        P(("ctx", "shard"), None),
        P(),
        P(("ctx", "shard"), None),
        P(("ctx", "shard"), None),
        P(("ctx", "shard"), None),
        P(("ctx", "shard"), None),
        P(("ctx", "shard"), None),
        P(("ctx", "shard"), None),
        P(("ctx", "shard"), None),
        P(("ctx", "shard"), None),
        P(),
        P(),
    )
    return jax.shard_map(
        body,
        mesh=mesh,
        in_specs=placed,
        out_specs=(
            P("rep", "ctx", "shard", None),
            P("rep", "ctx", "shard", None),
            P(("ctx", "shard"), None),
            P(("ctx", "shard"), None),
            P(("ctx", "shard"), None),
            P(("ctx", "shard"), None),
            P(("ctx", "shard"), None),
            P(("ctx", "shard"), None),
            P(("ctx", "shard"), None),
            P(("ctx", "shard"), None),
            P(("ctx", "shard"), None),
            P(("ctx", "shard"), None),
            P(("ctx", "shard"), None),
            P(("ctx", "shard"), None),
            P(),
            P(),
            P(),
        ),
        check_vma=False,
    )
```

profile of v0, /device:TPU:0, one launch (start us, length us, event | category | flops | bytes accessed | tf_op | source)
XLA Modules:
  0.0 2298.4 jit_solution(11573098838026494219)
XLA Ops:
  7.3 4.9 convert_element_type.108
  12.9 127.5 %all-gather.7.cloned.1.call-done = bf16[2048,6144]{1,0:T(8,128)(2,1)} async-done(((bf16[256,6144]{1,0:T(8,128)(2,1)}), bf16[2048,6144]{1,0:T(8,128)(2,1)}) %all-gather.7.cloned.1.call-update) | async-done | bytes 25165840 | tf_op jit(solution)/shard_map/all_gather | solution.py:188
  140.4 10.1 convolution_add_fusion
  158.9 2.9 convert_element_type.115
  161.8 7.6 convert_element_type.117
  169.5 4.7 convert_element_type.119
  176.3 3.9 copy.63
  180.2 20.7 all-gather.9.cloned.1.call-done
  200.9 26.5 %while.32 = (s32[]{:T(128)}, bf16[8,4,128,64]{2,3,1,0:T(8,128)(2,1)S(1)}, f32[8,4,128,1]{2,1,3,0:T(4,128)S(1)}, f32[8,4,128,1]{2,1,3,0:T(4,128)S(1)}, bf16[8,4,1...) while((s32[]{:T(128)}, ...), condition=%wide.region_6.7_spmd.clone.clone, body=%wide.region_3.6_spmd.clone.sunk.clone | while | flops 69270528 | bytes 4020841 | solution.py:208
  227.4 30.2 %all-gather.13.cloned.1.call-done = bf16[2048,2048]{1,0:T(8,128)(2,1)} async-done(((bf16[256,2048]{1,0:T(8,128)(2,1)}), bf16[2048,2048]{1,0:T(8,128)(2,1)}) %all-gather.13.cloned.1.call-update) | async-done | bytes 8388624 | tf_op jit(solution)/shard_map/all_gather | solution.py:189
  257.6 4.7 fusion.102
  262.7 212.0 %all-gather.15.cloned.1.call-done = bf16[2048,11264]{1,0:T(8,128)(2,1)} async-done(((bf16[256,11264]{1,0:T(8,128)(2,1)}), bf16[2048,11264]{1,0:T(8,128)(2,1)}) %all-gather.15.cloned.1.call-update) | async-done | bytes 46137360 | tf_op jit(solution)/shard_map/all_gather | solution.py:217
  474.6 22.6 fusion.92
  497.3 96.2 %all-gather.17.cloned.1.call-done = bf16[5632,2048]{1,0:T(8,128)(2,1)} async-done(((bf16[704,2048]{1,0:T(8,128)(2,1)}), bf16[5632,2048]{1,0:T(8,128)(2,1)}) %all-gather.17.cloned.1.call-update) | async-done | bytes 23068688 | tf_op jit(solution)/shard_map/all_gather | solution.py:218
  593.4 14.8 multiply_convert_fusion.2
  608.2 23.1 %multiply_reduce_fusion.1 = (f32[2048]{0:T(1024)}, f32[128]{0:T(128)S(1)}, f32[128]{0:T(128)S(1)}, f32[2048]{0:T(1024)}, f32[128,2048]{1,0:T(8,128)}) fusion(f32[128,2048]{1,0:T(8,128)S(1)} %get-tuple-element.345, f32[128]{0:T(128)S(1)} %add_rsqrt_fusion, f32[128]{0:T(128)S(1)} %broadcast_multiply_fusion.4, f32[2048]{0:T(1024)S(1)} %bitcast.243, ...), kind=kOutput, calls=%fused_computation.118 | convolution fusion | flops 5913702400 | bytes 51144704 | tf_op jit(solution)/shard_map/dot_general | solution.py:124
  631.3 1.9 multiply_add_fusion.4
  633.2 7.1 convolution_convert_fusion.4
  640.3 2.0 copy.64
  642.3 69.7 %while.33 = (s32[]{:T(128)}, f32[8,4,128,64]{2,3,1,0:T(8,128)}, bf16[8,4,512,64]{2,3,1,0:T(8,128)(2,1)}, bf16[8,4,512,64]{2,3,1,0:T(8,128)(2,1)}, bf16[8,4,128,6...) while((s32[]{:T(128)}, f32[8,4,128,64]{2,3,1,0:T(8,128)}, ...), condition=%wide.region_13.14_spmd.clone.clone, body=%wide.region_11.13_spmd.clone.sunk.clone | while | flops 170622464 | bytes 10247809 | solution.py:249
  645.6 1.9 fusion.165
  654.3 1.9 fusion.165
  663.0 1.9 fusion.165
  671.7 1.9 fusion.165
  680.4 1.9 fusion.165
  689.2 1.9 fusion.165
  697.9 1.9 fusion.165
  706.6 1.9 fusion.165
  712.0 3.9 copy.67
  716.0 3.9 copy.69
  720.0 12.1 convolution_convert_fusion.1
  733.5 5.8 convolution_convert_fusion.3
  739.3 12.4 copy.65
  751.8 20.7 convolution_convert_fusion
  775.7 6.5 reduce-scatter.15.cloned.1.call-done
  784.8 1.9 pad_maximum_fusion.8
  787.5 18.9 convolution_convert_fusion.2
  806.4 56.0 %pad_maximum_fusion = bf16[2048,19456]{1,0:T(8,128)(2,1)} fusion(bf16[2048,11264]{1,0:T(8,128)(2,1)} %convolution_convert_fusion, bf16[2048,2048]{1,0:T(8,128)(2,1)} %copy.65, bf16[2048,6144]{1,0:T(8,128)(2,1)} %convolution_convert_fusion.2), kind=kLoop, calls=%fused_computation.63 | loop fusion | flops 239075328 | bytes 159383552 | tf_op jit(solution)/shard_map/concatenate | solution.py:299
  862.5 12.7 fusion.54
  875.2 14.4 fusion.71
  890.2 2.0 copy.66
  892.9 40.5 %psum.23 = f32[7,2048]{1,0:T(8,128)S(1)} all-reduce(f32[7,2048]{1,0:T(8,128)S(1)} %concatenate.38), channel_id=1, replica_groups=mesh['rep'=4,'ctx'=4,'shard'=2] {'rep','ctx','shard'}, use_global_device_ids=true, to_apply=%region_27.28 | all-reduce | flops 14336 | bytes 114688 | tf_op jit(solution)/shard_map/psum | solution.py:297
  934.2 444.3 %reduce-scatter.17.cloned.1.call-done = bf16[256,19456]{1,0:T(8,128)(2,1)} async-done(((bf16[2048,19456]{1,0:T(8,128)(2,1)}), bf16[256,19456]{1,0:T(8,128)(2,1)}) %reduce-scatter.17.cloned.1.call-update) | async-done | bytes 9961488
  1378.5 850.0 %all-reduce.3 = (f32[256,19456]{1,0:T(8,128)}, f32[704,2048]{1,0:T(8,128)}) all-reduce(bf16[256,19456]{1,0:T(8,128)(2,1)} %reduce-scatter.17.cloned.1.call-done, bf16[704,2048]{1,0:T(8,128)(2,1)} %reduce-scatter.11.cloned.1.call-done), channel_id=1, replica_groups=mesh['rep'=4,'ctx'=4,'shard'=2] {'rep'}, use_global_device_ids=true, to_apply=%region_19.20 | all-reduce | flops 6422528 | bytes 38535168 | tf_op jit(solution)/shard_map/psum | solution.py:317
  2228.5 17.2 multiply_subtract_fusion.1
  2245.7 7.5 multiply_subtract_fusion.3
  2253.3 23.1 %multiply_subtract_fusion = (f32[256,11264]{1,0:T(8,128)}, f32[256,11264]{1,0:T(8,128)}, f32[256,11264]{1,0:T(8,128)}) fusion(f32[256,11264]{1,0:T(8,128)S(1)} %bitcast.220, f32[256,19456]{1,0:T(8,128)} %get-tuple-element.294, f32[256,11264]{1,0:T(8,128)} %param.35, f32[256,11264]{1,0:T(8,128)} %param.34), kind=kLoop, calls=%fused_computation.69 | loop fusion | flops 43253760 | bytes 80740352 | tf_op jit(solution)/shard_map/sub | solution.py:138
  2276.4 15.0 multiply_subtract_fusion.2
  (226 shorter events, 101.6 us)
Async XLA Ops:
  7.2 5.1 copy-start.10
  7.2 5.1 copy-start
  7.2 133.2 %all-gather.7.cloned.1.call-start = ((), (), s32[]{:S(2)}) async-start(), calls=%async_computation.4 | async-start | bytes 28311552 | tf_op jit(solution)/shard_map/all_gather | solution.py:188
  12.2 164.0 %all-gather.11.cloned.1.call-start = ((), (), s32[]{:S(2)}) async-start(), calls=%async_computation.6 | async-start | bytes 2621440 | tf_op jit(solution)/shard_map/all_gather | solution.py:205
  12.5 138.0 %copy-start.20 = (f32[128]{0:T(128)}, f32[128]{0:T(128)S(1)}, u32[]{:S(2)}) copy-start(f32[128]{0:T(128)S(1)} %broadcast_multiply_fusion.5) | copy-start | bytes 1540
  12.8 137.7 %copy-start.22 = (f32[128]{0:T(128)}, f32[128]{0:T(128)S(1)}, u32[]{:S(2)}) copy-start(f32[128]{0:T(128)S(1)} %add_rsqrt_fusion.1) | copy-start | bytes 1540
  12.8 137.7 %copy-start.6 = (f32[1,2048]{1,0:T(1,128)}, f32[1,2048]{1,0:T(1,128)S(1)}, u32[]{:S(2)}) copy-start(f32[1,2048]{1,0:T(1,128)S(1)} %get-tuple-element.336) | copy-start | bytes 24580
  12.8 137.7 %copy-start.8 = (f32[1,2048]{1,0:T(1,128)}, f32[1,2048]{1,0:T(1,128)S(1)}, u32[]{:S(2)}) copy-start(f32[1,2048]{1,0:T(1,128)S(1)} %get-tuple-element.335) | copy-start | bytes 24580
  140.4 12.8 copy-start.26
  150.6 1.7 copy-start.1
  153.1 47.8 %all-gather.9.cloned.1.call-start = ((), (), s32[]{:S(2)}) async-start(), calls=%async_computation.5 | async-start | bytes 2621440 | tf_op jit(solution)/shard_map/all_gather | solution.py:204
  153.5 5.4 copy-start.18
  153.5 5.4 copy-start.19
  158.9 98.8 %all-gather.13.cloned.1.call-start = ((), (), s32[]{:S(2)}) async-start(), calls=%async_computation.7 | async-start | bytes 9437184 | tf_op jit(solution)/shard_map/all_gather | solution.py:189
  161.8 312.8 %all-gather.15.cloned.1.call-start = ((), (), s32[]{:S(2)}) async-start(), calls=%async_computation.8 | async-start | bytes 51904512 | tf_op jit(solution)/shard_map/all_gather | solution.py:217
  169.5 424.0 %all-gather.17.cloned.1.call-start = ((), (), s32[]{:S(2)}) async-start(), calls=%async_computation.9 | async-start | bytes 25952256 | tf_op jit(solution)/shard_map/all_gather | solution.py:218
  174.2 598.3 %reduce-scatter.13.cloned.1.call-start = ((), (), s32[]{:S(2)}) async-start(), calls=%async_computation.11 | async-start | bytes 2621440
  227.4 35.0 %copy-start.4 = (bf16[8,4,128,64]{2,3,1,0:T(8,128)(2,1)}, bf16[8,4,128,64]{2,3,1,0:T(8,128)(2,1)S(1)}, u32[]{:S(2)}) copy-start(bf16[8,4,128,64]{2,3,1,0:T(8,128)(2,1)S(1)} %get-tuple-element.644) | copy-start | bytes 1572868
  262.4 368.9 %copy-start.12 = (f32[128]{0:T(128)}, f32[128]{0:T(128)S(1)}, u32[]{:S(2)}) copy-start(f32[128]{0:T(128)S(1)} %broadcast_multiply_fusion.4) | copy-start | bytes 1540
  262.7 368.7 %copy-start.14 = (f32[128]{0:T(128)}, f32[128]{0:T(128)S(1)}, u32[]{:S(2)}) copy-start(f32[128]{0:T(128)S(1)} %add_rsqrt_fusion) | copy-start | bytes 1540
  474.6 118.8 %copy-start.5 = (bf16[1,128,1,2048]{3,1,2,0:T(8,128)(2,1)S(1)}, bf16[1,128,1,2048]{3,1,2,0:T(8,128)(2,1)}, u32[]{:S(2)}) copy-start(bf16[1,128,1,2048]{3,1,2,0:T(8,128)(2,1)} %param.23) | copy-start | bytes 1572868
  716.0 66.3 %reduce-scatter.15.cloned.1.call-start = ((), (), s32[]{:S(2)}) async-start(), calls=%async_computation.12 | async-start | bytes 2621440
  720.0 214.2 %reduce-scatter.11.cloned.1.call-start = ((), (), s32[]{:S(2)}) async-start(), calls=%async_computation.10 | async-start | bytes 25952256 | tf_op jit(solution)/shard_map/reduce_scatter | solution.py:311
  732.2 646.3 %reduce-scatter.17.cloned.1.call-start = ((), (), s32[]{:S(2)}) async-start(), calls=%async_computation.13 | async-start | bytes 89653248
  739.3 12.4 copy-start.13
  739.3 12.4 copy-start.15
  772.5 15.0 copy-start.7
  772.5 15.0 copy-start.9
  862.5 12.7 copy-start.21
  862.5 12.7 copy-start.23
  889.6 2.7 copy-start.2
  889.6 2.6 copy-start.3
  889.6 3.2 copy-start.24
  889.7 3.1 copy-start.25
  889.7 43.8 %copy-start.11 = (f32[7,2048]{1,0:T(8,128)S(1)}, f32[7,2048]{1,0:T(8,128)}, u32[]{:S(2)}) copy-start(f32[7,2048]{1,0:T(8,128)} %param.29) | copy-start | bytes 172036
  889.7 43.8 %copy-start.16 = (f32[7,2048]{1,0:T(8,128)S(1)}, f32[7,2048]{1,0:T(8,128)}, u32[]{:S(2)}) copy-start(f32[7,2048]{1,0:T(8,128)} %param.39) | copy-start | bytes 172036
  889.7 43.8 %copy-start.17 = (f32[7,2048]{1,0:T(8,128)S(1)}, f32[7,2048]{1,0:T(8,128)}, u32[]{:S(2)}) copy-start(f32[7,2048]{1,0:T(8,128)} %param.38) | copy-start | bytes 172036
  1378.5 874.7 %slice-start = ((s8[11534336]{0:T(1024)(128)(4,1)}), s8[3145728]{0:T(1024)(128)(4,1)S(1)}, s32[]{:S(2)}) async-start(s8[11534336]{0:T(1024)(128)(4,1)} %bitcast.219), calls=%async_computation.14 | async-start | bytes 6291456
  2228.5 24.7 %slice-start.1 = ((s8[11534336]{0:T(1024)(128)(4,1)}), s8[4194304]{0:T(1024)(128)(4,1)S(1)}, s32[]{:S(2)}) async-start(s8[11534336]{0:T(1024)(128)(4,1)} %bitcast.219), calls=%async_computation.15 | async-start | bytes 8388608
  2228.5 24.7 %slice-start.2 = ((s8[11534336]{0:T(1024)(128)(4,1)}), s8[4194304]{0:T(1024)(128)(4,1)S(1)}, s32[]{:S(2)}) async-start(s8[11534336]{0:T(1024)(128)(4,1)} %bitcast.219), calls=%async_computation.16 | async-start | bytes 8388608
Sparse Core Ops, SparseCore 0:
  12.3 128.0 all-gather.6
  153.2 22.5 all-gather.10
  178.0 22.8 all-gather.8
  203.2 54.3 all-gather.12
  259.9 214.6 all-gather.14
  477.0 116.4 all-gather.16
  716.1 31.4 reduce-scatter.12
  750.8 31.3 reduce-scatter.14
  785.9 146.8 reduce-scatter.10
  936.4 442.1 reduce-scatter.16
where the time goes:
time: 2310 us; the launch traced here: 2300 us
  waiting for transfers between devices  938 us (41%)
  blocking collectives  891 us (39%)
  matrix products  257 us (11%)
  other arithmetic  156 us (7%)
  local copies, waits for them, and re-layouts  40.6 us (2%)
    psum x1, blocking collectives, body(): grad_rows, grad_down_rows = lax.psum((grad_rows, grad_down_rows), 'rep')  850 us
    unnamed x13, waiting for transfers between devices  451 us
    all_gather x1, waiting for transfers between devices, body(): lax.all_gather(up_low, ('ctx', 'shard'), axis=0, tiled=True)  212 us
    all_gather x1, waiting for transfers between devices, body(): lax.all_gather(qkv_low, ('ctx', 'shard'), axis=0, tiled=True)  128 us
    all_gather x1, waiting for transfers between devices, body(): lax.all_gather(down_low, ('ctx', 'shard'), axis=0, tiled=True)  96.2 us
    sub x5, other arithmetic, adam_update(): weight - step_rate * (first_hat / (jnp.sqrt(second_hat) + adam_eps) + dec...  63.5 us
    dot_general x4, matrix products, transposed_product(): lax.dot_general(left_rows, shard_piece, contract_last, preferred_element_...  59.3 us
    dot_general x4, matrix products, slice_product(): lax.dot_general(acts, grads, contract_first, preferred_element_type=jnp.f...  57.6 us
  transfers between devices with their start and end apart: 10, of which 7 were waited for; matrix products, arithmetic and copies ran while one was open for 11% of the time, Pallas kernels for 0%

commit v1 on v0

v1 whole, which is shorter than its diff:
```python
import functools

import jax
import jax.numpy as jnp
from jax import lax
from jax.experimental import pallas as pl
from jax.experimental.pallas import tpu as pltpu
from jax.sharding import PartitionSpec as P

HEADS = 32
HEAD_DIM = 64
FF = 5632
ROTARY = 16
STEP = 10

eps_norm = 1e-05
masked_score = -1e30
beta_one = 0.9
beta_two = 0.999
adam_eps = 1e-08
weight_decay = 0.1
score_scale = HEAD_DIM ** (-0.5)
FIRST = (((0,), (0,)), ((), ()))
LAST = (((1,), (1,)), ((), ()))
PLAIN = (((1,), (0,)), ((), ()))
bf16 = jnp.bfloat16
f32 = jnp.float32


def dot(a, b, dims):
    return lax.dot_general(a, b, dims, preferred_element_type=f32)


def adam_update(weight, moment_one, moment_two, grad, step_rate, decay_rate):
    first_new = beta_one * moment_one + (1.0 - beta_one) * grad
    second_new = beta_two * moment_two + (1.0 - beta_two) * grad * grad
    first_hat = first_new / (1.0 - beta_one**STEP)
    second_hat = second_new / (1.0 - beta_two**STEP)
    weight_new = weight - step_rate * (
        first_hat / (jnp.sqrt(second_hat) + adam_eps) + decay_rate * weight
    )
    return (first_new, second_new, weight_new)


class Plane:
    def __init__(self):
        self.s_size = lax.axis_size("shard")
        self.ctx_size = lax.axis_size("ctx")
        self.y_size = self.ctx_size // 2
        self.ctx = lax.axis_index("ctx")
        self.s = lax.axis_index("shard")
        self.y = self.ctx // 2
        self.c = self.ctx % 2
        self.blocks = self.ctx_size * self.s_size

    def core(self, x):
        return lax.ppermute(x, "ctx", [(i, i ^ 1) for i in range(self.ctx_size)])

    def along(self, x, axis, step):
        if axis == "y":
            return lax.ppermute(x, "ctx", [(i, i ^ (2 * step)) for i in range(self.ctx_size)])
        return lax.ppermute(x, "shard", [(i, i ^ step) for i in range(self.s_size)])

    def index(self, axis):
        return self.y if axis == "y" else self.s

    def steps(self, flip):
        ys = []
        k = self.y_size // 2
        while k:
            ys.append(("y", k))
            k //= 2
        ss = []
        k = self.s_size // 2
        while k:
            ss.append(("s", k))
            k //= 2
        return ys + ss if flip else ss + ys

    def chip_exchange(self, x, take):
        out = [(self.y, self.s, take(self.y, self.s))]
        for ry in range(self.y_size):
            for rs in range(self.s_size):
                if ry or rs:
                    y, s = self.y ^ ry, self.s ^ rs
                    mask = 2 * ry * self.s_size + rs
                    perm = [(i, i ^ mask) for i in range(self.blocks)]
                    out.append((y, s, lax.ppermute(take(y, s), ("ctx", "shard"), perm)))
        return out

    def sum_all(self, x):
        for axis, step in self.steps(False):
            x = x + self.along(x, axis, step)
        return x + self.core(x)

    def scatter_sum(self, p, flip):
        axes = {"y": 1, "s": 2}
        steps = self.steps(flip)
        kept = got = None
        for n, (axis, step) in enumerate(steps):
            ax = axes[axis]
            bit = (self.index(axis) // step) % 2
            kept = lax.dynamic_slice_in_dim(p, bit * step, step, ax)
            send = lax.dynamic_slice_in_dim(p, (1 - bit) * step, step, ax)
            got = self.along(send, axis, step)
            if n + 1 < len(steps):
                p = (kept.astype(f32) + got.astype(f32)).astype(bf16)
        return kept[:, 0, 0], got[:, 0, 0]

    def gather(self, p, flip):
        axes = {"y": 1, "s": 2}
        p = p[:, None, None]
        for axis, step in reversed(self.steps(flip)):
            ax = axes[axis]
            bit = (self.index(axis) // step) % 2
            got = self.along(p, axis, step)
            first = bit == 0
            p = jnp.concatenate([jnp.where(first, p, got), jnp.where(first, got, p)], ax)
        return p


def chain_sum(parts):
    size = lax.axis_size("rep")
    z = lax.axis_index("rep")
    end = (z == 0) | (z == size - 1)
    n = len(parts)
    first, sums, totals, outs = [None] * n, [None] * n, [None] * n, [None] * n
    for k in range(n + 2):
        if k < n:
            g = parts[k]
            r = lax.ppermute(g, "rep", [(0, 1), (3, 2)])
            sums[k] = lax.reduce_precision(g.astype(f32) + r.astype(f32), 8, 7).astype(bf16)
        j = k - 1
        if 0 <= j < n:
            r = lax.ppermute(sums[j], "rep", [(1, 2), (2, 1)])
            totals[j] = lax.reduce_precision(sums[j].astype(f32) + r.astype(f32), 8, 7).astype(bf16)
        j = k - 2
        if 0 <= j < n:
            r = lax.ppermute(totals[j], "rep", [(1, 0), (2, 3)])
            outs[j] = jnp.where(end, r, totals[j])
    return outs


def attend_kernel(kept_ref, got_ref, bias_ref, cos_ref, sin_ref, prow_ref, pcol_ref, qkv_ref, out_ref, peak_ref, total_ref):
    cos, sin = cos_ref[0], sin_ref[0]
    half = ROTARY // 2
    parts = []
    for i in range(3):
        v = kept_ref[i, 0].astype(f32) + got_ref[i, 0].astype(f32) + bias_ref[i, 0]
        if i < 2:
            a, b = v[:half], v[half:ROTARY]
            v = jnp.concatenate([a * cos - b * sin, b * cos + a * sin, v[ROTARY:]], axis=0)
        v = v.astype(bf16)
        qkv_ref[i, 0] = v
        parts.append(v)
    q, k, v = parts
    scores = dot(k, q, FIRST) * score_scale
    scores = jnp.where(pcol_ref[0] <= prow_ref[0], scores, masked_score)
    peak = jnp.max(scores, axis=0, keepdims=True)
    e = jnp.exp(scores - peak)
    total = jnp.sum(e, axis=0, keepdims=True)
    p = (e / total).astype(bf16)
    out_ref[0] = dot(v, p, PLAIN).astype(bf16)
    peak_ref[0, 0] = peak
    total_ref[0, 0] = total


def attend(kept, got, bias, cos, sin, prow, pcol):
    _, heads, hd, t = kept.shape
    seqs, _, seq = prow.shape
    big = pl.BlockSpec((3, 1, hd, seq), lambda s, h: (0, h, 0, s))
    table = pl.BlockSpec((1, ROTARY // 2, seq), lambda s, h: (s, 0, 0))
    stat = pl.BlockSpec((1, 1, 1, seq), lambda s, h: (s, h, 0, 0))
    return pl.pallas_call(
        attend_kernel,
        grid=(seqs, heads),
        in_specs=[
            big,
            big,
            pl.BlockSpec((3, 1, hd, 1), lambda s, h: (0, h, 0, 0)),
            table,
            table,
            pl.BlockSpec((1, 1, seq), lambda s, h: (s, 0, 0)),
            pl.BlockSpec((1, seq, 1), lambda s, h: (s, 0, 0)),
        ],
        out_specs=[big, pl.BlockSpec((1, hd, seq), lambda s, h: (h, 0, s)), stat, stat],
        out_shape=[
            jax.ShapeDtypeStruct((3, heads, hd, t), bf16),
            jax.ShapeDtypeStruct((heads, hd, t), bf16),
            jax.ShapeDtypeStruct((seqs, heads, 1, seq), f32),
            jax.ShapeDtypeStruct((seqs, heads, 1, seq), f32),
        ],
        compiler_params=pltpu.CompilerParams(vmem_limit_bytes=32 * 1024 * 1024),
        cost_estimate=pl.CostEstimate(
            flops=4 * seqs * heads * seq * seq * hd,
            bytes_accessed=16 * 3 * heads * hd * t,
            transcendentals=seqs * heads * seq * seq,
        ),
    )(kept, got, bias, cos, sin, prow, pcol)


def attend_back_kernel(qkv_ref, dout_ref, peak_ref, total_ref, cos_ref, sin_ref, prow_ref, pcol_ref, out_ref):
    cos, sin = cos_ref[0], sin_ref[0]
    half = ROTARY // 2
    q, k, v = qkv_ref[0, 0], qkv_ref[1, 0], qkv_ref[2, 0]
    dout = dout_ref[0]
    scores = dot(k, q, FIRST) * score_scale
    scores = jnp.where(pcol_ref[0] <= prow_ref[0], scores, masked_score)
    p = jnp.exp(scores - peak_ref[0, 0]) / total_ref[0, 0]
    dp = dot(v, dout, FIRST)
    inner = jnp.sum(p * dp, axis=0, keepdims=True)
    ds = (p * (dp - inner)).astype(bf16)

    def back(x):
        a, b = x[:half], x[half:ROTARY]
        return jnp.concatenate([a * cos + b * sin, b * cos - a * sin, x[ROTARY:]], axis=0)

    out_ref[0, 0] = back(dot(k, ds, PLAIN) * score_scale).astype(bf16)
    out_ref[1, 0] = back(dot(q, ds, LAST) * score_scale).astype(bf16)
    out_ref[2, 0] = dot(dout, p.astype(bf16), LAST).astype(bf16)


def attend_back(qkv, dout, peak, total, cos, sin, prow, pcol):
    _, heads, hd, t = qkv.shape
    seqs, _, seq = prow.shape
    big = pl.BlockSpec((3, 1, hd, seq), lambda s, h: (0, h, 0, s))
    table = pl.BlockSpec((1, ROTARY // 2, seq), lambda s, h: (s, 0, 0))
    stat = pl.BlockSpec((1, 1, 1, seq), lambda s, h: (s, h, 0, 0))
    return pl.pallas_call(
        attend_back_kernel,
        grid=(seqs, heads),
        in_specs=[
            big,
            pl.BlockSpec((1, hd, seq), lambda s, h: (h, 0, s)),
            stat,
            stat,
            table,
            table,
            pl.BlockSpec((1, 1, seq), lambda s, h: (s, 0, 0)),
            pl.BlockSpec((1, seq, 1), lambda s, h: (s, 0, 0)),
        ],
        out_specs=big,
        out_shape=jax.ShapeDtypeStruct((3, heads, hd, t), bf16),
        compiler_params=pltpu.CompilerParams(vmem_limit_bytes=32 * 1024 * 1024),
        cost_estimate=pl.CostEstimate(
            flops=10 * seqs * heads * seq * seq * hd,
            bytes_accessed=16 * 3 * heads * hd * t,
            transcendentals=seqs * heads * seq * seq,
        ),
    )(qkv, dout, peak, total, cos, sin, prow, pcol)


def body(
    tokens,
    cotangent,
    span_order,
    w_qkv,
    w_out,
    w_up,
    w_down,
    norm_params,
    m_qkv,
    v_qkv,
    m_out,
    v_out,
    m_up,
    v_up,
    m_down,
    v_down,
    m_norm,
    v_norm,
):
    at = Plane()
    width = tokens.shape[3]
    rows = tokens.shape[1]
    S, Y, nb = at.s_size, at.y_size, at.blocks
    blk = width // nb
    ffb = FF // nb
    heads = blk // HEAD_DIM
    seq = rows * at.ctx_size
    T = S * seq
    H = T // 2
    first = at.c == 0
    my_block = at.ctx * S + at.s

    def pick(pair_axis_array, axis, which):
        return lax.dynamic_index_in_dim(pair_axis_array, which, axis, keepdims=False)

    def chip_rows(w, lead, unit):
        r = w.shape[0]
        w = w.reshape(r, lead * Y, 2, S * unit)
        a, b = w[:, :, 0], w[:, :, 1]
        mine = jnp.where(first, a, b).astype(bf16).reshape(r, -1)
        theirs = jnp.where(first, b, a).astype(bf16).reshape(r, -1)
        return jnp.concatenate([mine, at.core(theirs)], axis=0)

    wq = chip_rows(w_qkv, 3, blk)
    wo = chip_rows(w_out, 1, blk)
    wu = chip_rows(w_up, 2, ffb)
    wo_own = w_out.astype(bf16)
    wd_own = w_down.astype(bf16)

    order = span_order.reshape(1, -1).astype(f32)
    orders = [(at.s, order)]
    for rs in range(1, S):
        orders.append((at.s ^ rs, lax.ppermute(order, "shard", [(i, i ^ rs) for i in range(S)])))
    order_all = jnp.zeros((S, order.shape[1]), f32)
    for s, o in orders:
        order_all = lax.dynamic_update_slice(order_all, o, (s, 0))
    span = rows // 2
    pos = (order_all[:, :, None] * span + jnp.arange(span, dtype=f32)[None, None, :]).reshape(S, seq)
    prow = pos.reshape(S, 1, seq)
    pcol = pos.reshape(S, seq, 1)
    exponent = jnp.arange(ROTARY // 2, dtype=f32)
    inverse = 10000.0 ** (-2.0 * exponent / ROTARY)
    angles = prow * inverse[None, :, None]
    cos, sin = jnp.cos(angles), jnp.sin(angles)

    norm_cols = norm_params.reshape(7, nb, blk).transpose(1, 2, 0)
    own_cols = pick(norm_cols, 0, my_block)
    other_cols = pick(norm_cols, 0, (at.ctx ^ 1) * S + at.s)
    pair_cols = jnp.concatenate([own_cols, other_cols], axis=0)

    x_rows = tokens.reshape(rows, width)
    x_f = x_rows.astype(f32)
    mean = jnp.mean(x_f, axis=1)
    centred = x_f - mean[:, None]
    inv = lax.rsqrt(jnp.mean(centred * centred, axis=1) + eps_norm)
    stats = jnp.stack([mean, inv])

    def to_columns(take, tail):
        got = at.chip_exchange(None, take)
        buf = jnp.zeros((S, Y) + tail, got[0][2].dtype)
        for y, s, v in got:
            buf = lax.dynamic_update_slice(buf, v[None, None], (s, y) + (0,) * len(tail))
        other = at.core(buf)
        return jnp.stack([jnp.where(first, buf, other), jnp.where(first, other, buf)], axis=2)

    xt = x_rows.T.reshape(Y, 2, S, blk, rows)
    x_all = to_columns(
        lambda y, s: lax.dynamic_slice(xt, (y, 0, s, 0, 0), (1, 2, 1, blk, rows)).reshape(2, blk, rows),
        (2, blk, rows),
    )
    st_all = to_columns(lambda y, s: stats, (2, rows))
    x_all = x_all.transpose(3, 4, 0, 1, 2, 5).reshape(2, blk, T)
    x_own = pick(x_all, 0, at.c).astype(f32)
    x_other = pick(x_all, 0, 1 - at.c).astype(f32)
    st_all = st_all.transpose(3, 0, 1, 2, 4).reshape(2, T)
    mean1, inv1 = st_all[0:1], st_all[1:2]
    x_pair = jnp.concatenate([x_own, x_other], axis=0)
    xn1 = ((x_pair - mean1) * inv1 * pair_cols[:, 0:1] + pair_cols[:, 1:2]).astype(bf16)

    cot = cotangent.reshape(2, rows // 2, width)
    cot_parts = [at.gather(cot[k][None], bool(k))[0] for k in range(2)]
    cot_c = jnp.stack(cot_parts, axis=2)
    cot_o = at.core(cot_c)
    cot_all = jnp.stack([jnp.where(first, cot_c, cot_o), jnp.where(first, cot_o, cot_c)], axis=2)
    cot_all = cot_all.transpose(1, 0, 2, 3, 4, 5).reshape(T, width)

    bias = own_cols[:, 4:7].T.reshape(3, heads, HEAD_DIM, 1)
    halves = (slice(0, H), slice(H, T))
    seqs = (slice(0, S // 2), slice(S // 2, S))
    qkvs, attns, peaks, totals = [], [], [], []
    for k in range(2):
        p = dot(wq, xn1[:, halves[k]], FIRST).astype(bf16).reshape(3, Y, S, blk, H)
        kept, got = at.scatter_sum(p, bool(k))
        sq = seqs[k]
        qkv, attn, peak, total = attend(
            kept.reshape(3, heads, HEAD_DIM, H),
            got.reshape(3, heads, HEAD_DIM, H),
            bias,
            cos[sq],
            sin[sq],
            prow[sq],
            pcol[sq],
        )
        qkvs.append(qkv)
        attns.append(attn.reshape(blk, H))
        peaks.append(peak)
        totals.append(total)

    hiddens = []
    for k in range(2):
        pair = jnp.concatenate([attns[k], at.core(attns[k])], axis=0)
        p = dot(wo, pair, FIRST).astype(bf16).reshape(1, Y, S, blk, H)
        kept, got = at.scatter_sum(p, bool(k))
        hiddens.append(x_own[:, halves[k]] + (kept[0].astype(f32) + got[0].astype(f32)))
    hidden = jnp.concatenate(hiddens, axis=1)
    local_mean = jnp.mean(hidden, axis=0, keepdims=True)
    dev = hidden - local_mean
    moments = jnp.concatenate([local_mean, jnp.sum(dev * dev, axis=0, keepdims=True)], axis=0)
    count = blk
    for axis, step in at.steps(False) + [("core", 1)]:
        other = at.core(moments) if axis == "core" else at.along(moments, axis, step)
        gap = moments[0:1] - other[0:1]
        moments = jnp.concatenate(
            [
                0.5 * (moments[0:1] + other[0:1]),
                moments[1:2] + other[1:2] + gap * gap * (count / 2.0),
            ],
            axis=0,
        )
        count *= 2
    mean2 = moments[0:1]
    inv2 = lax.rsqrt(moments[1:2] / width + eps_norm)
    z2 = (hidden - mean2) * inv2
    xn2_own = (z2 * own_cols[:, 2:3] + own_cols[:, 3:4]).astype(bf16)
    xn2 = jnp.concatenate([xn2_own, at.core(xn2_own)], axis=0)

    acts, ggus = [], []
    for k in range(2):
        p = dot(wu, xn2[:, halves[k]], FIRST).astype(bf16).reshape(2, Y, S, ffb, H)
        kept, got = at.scatter_sum(p, bool(k))
        gate = kept[0].astype(f32) + got[0].astype(f32)
        up = kept[1].astype(f32) + got[1].astype(f32)
        sig = jax.nn.sigmoid(gate)
        silu = gate * sig
        acts.append((silu * up).astype(bf16))
        grad_act = dot(wd_own, cot_all[halves[k]], LAST)
        grad_gate = grad_act * up * sig * (1.0 + gate * (1.0 - sig))
        ggus.append(jnp.stack([grad_gate, grad_act * silu]).astype(bf16))
    act = jnp.concatenate(acts, axis=1)
    g_down = dot(act, cot_all, PLAIN).astype(bf16)

    ggu = jnp.concatenate([at.gather(ggus[k], bool(k)) for k in range(2)], axis=4)
    ggu = ggu.reshape(2 * Y * S * ffb, T)
    part = dot(wu, ggu, PLAIN)
    gxn2 = part[:blk] + at.core(part[blk:])
    g_up = dot(xn2, ggu, LAST).astype(bf16)

    def norm_back(grad, z, scale, gain):
        e = grad * gain
        sums = jnp.concatenate(
            [jnp.sum(e, axis=0, keepdims=True), jnp.sum(e * z, axis=0, keepdims=True)], axis=0
        )
        sums = at.sum_all(sums) / width
        return scale * (e - sums[0:1] - z * sums[1:2])

    cot_cols = lax.dynamic_slice_in_dim(cot_all, my_block * blk, blk, 1).T
    grad_hidden = cot_cols.astype(f32) + norm_back(gxn2, z2, inv2, own_cols[:, 2:3])
    grad_branch = grad_hidden.astype(bf16)
    gbrs = [at.gather(grad_branch[:, halves[k]][None], bool(k))[0] for k in range(2)]
    gbr_c = jnp.concatenate(gbrs, axis=3)
    gbr_o = at.core(gbr_c)
    gbr = jnp.stack([jnp.where(first, gbr_c, gbr_o), jnp.where(first, gbr_o, gbr_c)], axis=1)
    gbr = gbr.reshape(width, T)
    attn = jnp.concatenate(attns, axis=1)
    g_out = dot(attn, gbr, LAST).astype(bf16)
    grad_attn = dot(wo_own, gbr, PLAIN).astype(bf16)

    gqkvs = []
    for k in range(2):
        sq = seqs[k]
        gqkvs.append(
            attend_back(
                qkvs[k],
                grad_attn[:, halves[k]].reshape(heads, HEAD_DIM, H),
                peaks[k],
                totals[k],
                cos[sq],
                sin[sq],
                prow[sq],
                pcol[sq],
            ).reshape(3, blk, H)
        )
    gqkv_own = jnp.concatenate(gqkvs, axis=2)
    bias_grad = jnp.sum(gqkv_own.astype(f32), axis=2)
    gqkv = jnp.concatenate([at.gather(gqkvs[k], bool(k)) for k in range(2)], axis=4)
    gqkv = gqkv.reshape(3 * Y * S * blk, T)
    g_qkv = dot(xn1, gqkv, LAST).astype(bf16)
    part = dot(wq, gqkv, PLAIN)
    gxn1 = part[:blk] + at.core(part[blk:])
    z1 = (x_own - mean1) * inv1
    input_grad = grad_hidden + norm_back(gxn1, z1, inv1, own_cols[:, 0:1])

    p = dot(wd_own, act, FIRST).astype(bf16).reshape(Y, 2, S, blk, T)
    theirs = at.core(pick(p, 1, 1 - at.c))
    p = (pick(p, 1, at.c).astype(f32) + theirs.astype(f32)).astype(bf16)[None]
    outs = []
    for k in range(2):
        kept, got = at.scatter_sum(p[..., halves[k]], bool(k))
        outs.append(hiddens[k] + (kept[0].astype(f32) + got[0].astype(f32)))
    out_cols = jnp.concatenate(outs, axis=1).astype(bf16)

    def to_rows(cols):
        split = cols.reshape(blk, S, Y, 2, rows).transpose(1, 2, 3, 0, 4)
        theirs = at.core(pick(split, 2, 1 - at.c))
        mine = pick(split, 2, at.c)
        both = jnp.stack([jnp.where(first, mine, theirs), jnp.where(first, theirs, mine)], axis=2)
        got = at.chip_exchange(
            None,
            lambda y, s: lax.dynamic_slice(both, (s, y, 0, 0, 0), (1, 1, 2, blk, rows)).reshape(2, blk, rows),
        )
        buf = jnp.zeros((Y, 2, S, blk, rows), cols.dtype)
        for y, s, v in got:
            buf = lax.dynamic_update_slice(buf, v[None, :, None], (y, 0, s, 0, 0))
        return buf.reshape(width, rows).T

    block_output = to_rows(out_cols)
    input_rows = to_rows(input_grad)

    def cut(g, n):
        r = g.shape[0] // n
        return [g[i * r : (i + 1) * r] for i in range(n)]

    g_down = jnp.concatenate(chain_sum(cut(g_down, 2)), axis=0)
    g_up = jnp.concatenate(chain_sum(cut(g_up, 4)), axis=0)
    g_out = jnp.concatenate(chain_sum(cut(g_out, 1)), axis=0)
    g_qkv = jnp.concatenate(chain_sum(cut(g_qkv, 4)), axis=0)

    def own_rows(g, lead, unit):
        r = g.shape[0] // 2
        mine = g[:r].reshape(r, lead * Y, S * unit)
        theirs = at.core(g[r:]).reshape(r, lead * Y, S * unit)
        both = jnp.stack([jnp.where(first, mine, theirs), jnp.where(first, theirs, mine)], axis=2)
        return both.reshape(r, -1).astype(f32)

    small = jnp.concatenate(
        [
            jnp.sum(gxn1 * z1, axis=1)[None],
            jnp.sum(gxn1, axis=1)[None],
            jnp.sum(gxn2 * z2, axis=1)[None],
            jnp.sum(gxn2, axis=1)[None],
            bias_grad,
        ],
        axis=0,
    )
    small = small.reshape(7, 1, blk)
    z = lax.axis_index("rep")
    n_rep = lax.axis_size("rep")
    step = 1
    while step < n_rep:
        small = small + lax.ppermute(small, "rep", [(i, i ^ step) for i in range(n_rep)])
        step *= 2
    del z
    got = at.chip_exchange(None, lambda y, s: small)
    buf = jnp.zeros((7, Y, S, blk), f32)
    for y, s, v in got:
        buf = lax.dynamic_update_slice(buf, v[:, None], (0, y, s, 0))
    other = at.core(buf)
    norm_grad = jnp.stack([jnp.where(first, buf, other), jnp.where(first, other, buf)], axis=2)
    norm_grad = norm_grad.reshape(7, width)

    mq, vq, wq_new = adam_update(w_qkv, m_qkv, v_qkv, own_rows(g_qkv, 3, blk), 0.03, weight_decay)
    mo, vo, wo_new = adam_update(w_out, m_out, v_out, g_out.astype(f32), 0.2, weight_decay)
    mu, vu, wu_new = adam_update(w_up, m_up, v_up, own_rows(g_up, 2, ffb), 0.03, weight_decay)
    md, vd, wd_new = adam_update(w_down, m_down, v_down, g_down.astype(f32), 0.02, weight_decay)
    mn, vn, wn = adam_update(norm_params, m_norm, v_norm, norm_grad, 0.3, 0.0)
    return (
        block_output.reshape(tokens.shape),
        input_rows.reshape(tokens.shape),
        mq,
        vq,
        wq_new,
        mo,
        vo,
        wo_new,
        mu,
        vu,
        wu_new,
        md,
        vd,
        wd_new,
        mn,
        vn,
        wn,
    )


def solution(mesh):
    tok = P("rep", "ctx", "shard", None)
    row = P(("ctx", "shard"), None)
    placed = (tok, tok, P("rep", "shard", None)) + (row,) * 4 + (P(),) + (row,) * 8 + (P(), P())
    return jax.shard_map(
        body,
        mesh=mesh,
        in_specs=placed,
        out_specs=(tok, tok) + (row,) * 12 + (P(),) * 3,
        check_vma=False,
    )
```

time: 2310 us -> 1280 us (0.55)
  blocking collectives: 891 us -> 0 us
  waiting for transfers between devices: 938 us -> 606 us
  local copies, waits for them, and re-layouts: 40.6 us -> 258 us
  matrix products: 257 us -> 66.1 us
  starting transfers between devices: 0.94 us -> 130 us
  other arithmetic: 156 us -> 183 us
    psum x2 -> x0, blocking collectives: 891 us -> none  [the longest x1 850 us: body(): grad_rows, grad_down_rows = lax.psum((grad_rows, grad_down_rows), 'rep')]
    ppermute x0 -> x110, waiting for transfers between devices: none -> 606 us  [the longest x11 186 us: chain_sum(): r = lax.ppermute(totals[j], 'rep', [(1, 0), (2, 3)])]
    all_gather x6 -> x0, waiting for transfers between devices: 487 us -> none  [the longest x1 212 us: body(): lax.all_gather(up_low, ('ctx', 'shard'), axis=0, tiled=True)]
    unnamed x13 -> x0, waiting for transfers between devices: 451 us -> none
    dot_general x68 -> x16, matrix products: 257 us -> 66.1 us  [dot(): return lax.dot_general(a, b, dims, preferred_element_type=f32)]
    ppermute x0 -> x110, starting transfers between devices: none -> 130 us  [the longest x11 31.3 us: chain_sum(): r = lax.ppermute(g, 'rep', [(0, 1), (3, 2)])]
    unnamed x65 -> x180, local copies, waits for them, and re-layouts: 14.3 us -> 138 us
    concatenate x5 -> x18, other arithmetic: 59.7 us -> 9.95 us  [the longest x8 5.73 us: gather(): jnp.concatenate([jnp.where(first, p, got), jnp.where(first, got, p)], ax)]
  transfers between devices with their start and end apart: 10 -> 110, of which waited for: 7 -> 46; matrix products, arithmetic and copies ran while one was open for 11% -> 35% of each run, Pallas kernels for 0% -> 1%
where the time goes in v1:
time: 1280 us; the launch traced here: 1260 us
  waiting for transfers between devices  606 us (47%)
  local copies, waits for them, and re-layouts  258 us (20%)
  other arithmetic  183 us (14%)
  starting transfers between devices  130 us (10%)
  matrix products  66.1 us (5%)
  Pallas kernels  18.5 us (1%)
    ppermute x11, waiting for transfers between devices, chain_sum(): r = lax.ppermute(totals[j], 'rep', [(1, 0), (2, 3)])  186 us
    ppermute x19, waiting for transfers between devices, along(): lax.ppermute(x, 'ctx', [(i, i ^ 2 * step) for i in range(self.ctx_size)])  168 us
    ppermute x11, waiting for transfers between devices, chain_sum(): r = lax.ppermute(g, 'rep', [(0, 1), (3, 2)])  166 us
    unnamed x180, local copies, waits for them, and re-layouts  138 us
    ppermute x19, waiting for transfers between devices, along(): return lax.ppermute(x, 'shard', [(i, i ^ step) for i in range(self.s_size)])  70.5 us
    dot_general x16, matrix products, dot(): return lax.dot_general(a, b, dims, preferred_element_type=f32)  66.1 us
    sub x5, other arithmetic, adam_update(): weight - step_rate * (first_hat / (jnp.sqrt(second_hat) + adam_eps) + dec...  56.2 us
    ppermute x11, starting transfers between devices, chain_sum(): r = lax.ppermute(g, 'rep', [(0, 1), (3, 2)])  31.3 us
  transfers between devices with their start and end apart: 110, of which 46 were waited for; matrix products, arithmetic and copies ran while one was open for 35% of the time, Pallas kernels for 1%

profile of v1, /device:TPU:0, one launch (start us, length us, event | category | flops | bytes accessed | tf_op | source)
XLA Modules:
  0.0 1264.6 jit_solution(1801506779771680576)
XLA Ops:
  11.5 6.6 copy.234
  53.0 11.3 dynamic_update_slice.77
  64.8 16.7 %collective-permute-done.17 = bf16[3,1,2,256,512]{4,3,0,2,1:T(8,128)(2,1)} collective-permute-done((bf16[3,1,2,256,512]{4,3,0,2,1:T(8,128)(2,1)}, bf16[3,1,2,256,512]{4,3,0,2,1:T(8,128)(2,1)}, u32[]{:S(2)}, u32[]{:S(2)}) %collective-permute-start.17) | collective-permute-done | bytes 1572896 | tf_op jit(solution)/shard_map/ppermute | solution.py:61
  92.8 12.6 collective-permute-done.18
  114.7 11.9 copy.248
  134.5 7.5 select_convert_fusion.1
  149.8 8.8 collective-permute-done.14
  172.6 7.9 collective-permute-done.23
  207.4 50.6 %collective-permute-done.28 = bf16[2,1,2,704,512]{4,3,2,1,0:T(8,128)(2,1)} collective-permute-done((bf16[2,1,2,704,512]{4,3,2,1,0:T(8,128)(2,1)}, bf16[2,1,2,704,512]{4,3,2,1,0:T(8,128)(2,1)}, u32[]{:S(2)}, u32[]{:S(2)}) %collective-permute-start.28) | collective-permute-done | bytes 2883616 | tf_op jit(solution)/shard_map/ppermute | solution.py:61
  274.2 24.9 %collective-permute-done.29 = bf16[2,1,1,704,512]{4,3,2,1,0:T(8,128)(2,1)S(1)} collective-permute-done((bf16[2,1,1,704,512]{4,3,2,1,0:T(8,128)(2,1)S(1)}, bf16[2,1,1,704,512]{4,3,2,1,0:T(8,128)(2,1)S(1)}, u32[]{:S(2)}, u32[]{:S(2)}) %collective-permute-start.29) | collective-permute-done | bytes 1441824 | tf_op jit(solution)/shard_map/ppermute | solution.py:62
  317.0 7.9 reshape.516
  324.9 7.1 constant_dynamic-slice_fusion.8
  332.0 6.1 copy.254
  349.2 6.7 copy.277
  355.9 6.6 copy.281
  362.4 12.0 copy.284
  374.4 11.9 copy.290
  389.7 6.1 copy.307
  401.7 6.6 collective-permute-done.101
  433.7 62.6 %collective-permute-done.33 = bf16[1,1,2,256,512]{4,3,2,1,0:T(8,128)(2,1)S(1)} collective-permute-done((bf16[1,1,2,256,512]{4,3,2,1,0:T(8,128)(2,1)S(1)}, bf16[1,1,2,256,512]{4,3,2,1,0:T(8,128)(2,1)S(1)}, u32[]{:S(2)}, u32[]{:S(2)}) %collective-permute-start.33) | collective-permute-done | bytes 524320 | tf_op jit(solution)/shard_map/ppermute | solution.py:61
  519.8 10.1 fusion.14
  538.5 6.5 collective-permute-done.37
  551.6 9.3 convolution_convert_fusion
  561.5 6.5 collective-permute-start.85
  600.5 30.1 %collective-permute-done.94 = bf16[128,5632]{1,0:T(8,128)(2,1)S(1)} collective-permute-done((bf16[128,5632]{1,0:T(8,128)(2,1)S(1)}, bf16[128,5632]{1,0:T(8,128)(2,1)S(1)}, u32[]{:S(2)}, u32[]{:S(2)}) %collective-permute-start.94) | collective-permute-done | bytes 1441824 | tf_op jit(solution)/shard_map/ppermute | solution.py:131
  630.7 30.9 %collective-permute-done.91 = bf16[128,5632]{1,0:T(8,128)(2,1)S(1)} collective-permute-done((bf16[128,5632]{1,0:T(8,128)(2,1)S(1)}, bf16[128,5632]{1,0:T(8,128)(2,1)S(1)}, u32[]{:S(2)}, u32[]{:S(2)}) %collective-permute-start.91) | collective-permute-done | bytes 1441824 | tf_op jit(solution)/shard_map/ppermute | solution.py:131
  661.6 30.5 %collective-permute-done.88 = bf16[128,5632]{1,0:T(8,128)(2,1)S(1)} collective-permute-done((bf16[128,5632]{1,0:T(8,128)(2,1)S(1)}, bf16[128,5632]{1,0:T(8,128)(2,1)S(1)}, u32[]{:S(2)}, u32[]{:S(2)}) %collective-permute-start.88) | collective-permute-done | bytes 1441824 | tf_op jit(solution)/shard_map/ppermute | solution.py:131
  697.1 10.6 multiply_subtract_fusion.2
  739.6 91.2 %collective-permute-done.93 = bf16[128,5632]{1,0:T(8,128)(2,1)S(1)} collective-permute-done((bf16[128,5632]{1,0:T(8,128)(2,1)S(1)}, bf16[128,5632]{1,0:T(8,128)(2,1)S(1)}, u32[]{:S(2)}, u32[]{:S(2)}) %collective-permute-start.93) | collective-permute-done | bytes 1441824 | tf_op jit(solution)/shard_map/ppermute | solution.py:139
  831.5 28.5 %collective-permute-done.96 = bf16[128,5632]{1,0:T(8,128)(2,1)S(1)} collective-permute-done((bf16[128,5632]{1,0:T(8,128)(2,1)S(1)}, bf16[128,5632]{1,0:T(8,128)(2,1)S(1)}, u32[]{:S(2)}, u32[]{:S(2)}) %collective-permute-start.96) | collective-permute-done | bytes 1441824 | tf_op jit(solution)/shard_map/ppermute | solution.py:139
  865.7 16.8 %collective-permute-done.82 = bf16[256,2048]{1,0:T(8,128)(2,1)S(1)} collective-permute-done((bf16[256,2048]{1,0:T(8,128)(2,1)S(1)}, bf16[256,2048]{1,0:T(8,128)(2,1)S(1)}, u32[]{:S(2)}, u32[]{:S(2)}) %collective-permute-start.82) | collective-permute-done | bytes 1048608 | tf_op jit(solution)/shard_map/ppermute | solution.py:131
  883.7 15.4 %collective-permute-done.60 = bf16[3,1,2,256,512]{4,3,2,1,0:T(8,128)(2,1)S(1)} collective-permute-done((bf16[3,1,2,256,512]{4,3,2,1,0:T(8,128)(2,1)S(1)}, bf16[3,1,2,256,512]{4,3,2,1,0:T(8,128)(2,1)S(1)}, u32[]{:S(2)}, u32[]{:S(2)}) %collective-permute-start.60) | collective-permute-done | bytes 1572896 | tf_op jit(solution)/shard_map/ppermute | solution.py:61
  915.8 8.6 collective-permute-done.69
  935.1 6.2 collective-permute-done.78
  941.3 16.8 %collective-permute-done.75 = bf16[128,3072]{1,0:T(8,128)(2,1)S(1)} collective-permute-done((bf16[128,3072]{1,0:T(8,128)(2,1)S(1)}, bf16[128,3072]{1,0:T(8,128)(2,1)S(1)}, u32[]{:S(2)}, u32[]{:S(2)}) %collective-permute-start.75) | collective-permute-done | bytes 786464 | tf_op jit(solution)/shard_map/ppermute | solution.py:131
  958.1 15.5 %collective-permute-done.72 = bf16[128,3072]{1,0:T(8,128)(2,1)S(1)} collective-permute-done((bf16[128,3072]{1,0:T(8,128)(2,1)S(1)}, bf16[128,3072]{1,0:T(8,128)(2,1)S(1)}, u32[]{:S(2)}, u32[]{:S(2)}) %collective-permute-start.72) | collective-permute-done | bytes 786464 | tf_op jit(solution)/shard_map/ppermute | solution.py:131
  1016.2 7.9 maximum_convert_fusion
  1024.1 11.9 copy.289
  1039.7 29.7 %multiply_subtract_fusion = (f32[256,11264]{0,1:T(8,128)}, f32[256,11264]{0,1:T(8,128)}, f32[256,11264]{0,1:T(8,128)}) fusion(f32[256,11264]{0,1:T(8,128)} %copy.248, f32[256,4,2,1408]{0,3,2,1:T(8,128)} %copy.289, f32[256,11264]{0,1:T(8,128)} %copy.290, f32[256,11264]{0,1:T(8,128)} %copy.284), kind=kLoop, calls=%fused_computation.5 | loop fusion | flops 43253760 | bytes 80740352 | tf_op jit(solution)/shard_map/sub | solution.py:39
  1069.4 11.9 copy.302
  1081.3 11.9 copy.301
  1093.2 12.0 copy.300
  1132.0 45.6 %collective-permute-done.77 = bf16[128,3072]{1,0:T(8,128)(2,1)S(1)} collective-permute-done((bf16[128,3072]{1,0:T(8,128)(2,1)S(1)}, bf16[128,3072]{1,0:T(8,128)(2,1)S(1)}, u32[]{:S(2)}, u32[]{:S(2)}) %collective-permute-start.77) | collective-permute-done | bytes 786464 | tf_op jit(solution)/shard_map/ppermute | solution.py:139
  1178.2 15.6 %collective-permute-done.80 = bf16[128,3072]{1,0:T(8,128)(2,1)S(1)} collective-permute-done((bf16[128,3072]{1,0:T(8,128)(2,1)S(1)}, bf16[128,3072]{1,0:T(8,128)(2,1)S(1)}, u32[]{:S(2)}, u32[]{:S(2)}) %collective-permute-start.80) | collective-permute-done | bytes 786464 | tf_op jit(solution)/shard_map/ppermute | solution.py:139
  1233.8 11.0 multiply_subtract_fusion.1
  1244.7 6.6 copy.299
  1251.3 6.6 copy.298
  1257.9 6.6 copy.297
  (615 shorter events, 457.8 us)
Async XLA Ops:
  8.0 45.0 %collective-permute-start.12 = (f32[1,8]{1,0:T(1,128)S(1)}, f32[1,8]{1,0:T(1,128)S(1)}, u32[]{:S(2)}, u32[]{:S(2)}) collective-permute-start(f32[1,8]{1,0:T(1,128)S(1)} %get-tuple-element.260), channel_id=1, source_target_pairs={{0,1},{1,0},{2,3},{3,2},{4,5},{5,4},{6,7},{7,6},{8,9},{9,8},{10,11... | collective-permute-start | bytes 104 | tf_op jit(solution)/shard_map/ppermute | solution.py:306
  28.5 102.0 %collective-permute-start.4 = (bf16[256,1024]{0,1:T(8,128)(2,1)}, bf16[256,1024]{0,1:T(8,128)(2,1)}, u32[]{:S(2)}, u32[]{:S(2)}) collective-permute-start(bf16[256,1024]{0,1:T(8,128)(2,1)} %bitcast.18), channel_id=1, source_target_pairs={{0,2},{2,0},{4,6},{6,4},{1,3},{3,1},{5,7},{7,5},{8,10},{10,8},{12,... | collective-permute-start | bytes 1572872 | tf_op jit(solution)/shard_map/ppermute | solution.py:57
  44.5 37.0 %collective-permute-start.17 = (bf16[3,1,2,256,512]{4,3,0,2,1:T(8,128)(2,1)}, bf16[3,1,2,256,512]{4,3,0,2,1:T(8,128)(2,1)}, u32[]{:S(2)}, u32[]{:S(2)}) collective-permute-start(bf16[3,1,2,256,512]{4,3,0,2,1:T(8,128)(2,1)} %copy.306), channel_id=1, source_target_pairs={{0,4},{2,6},{4,0},{6,2},{1,5},{3,7},{5,1},{7,3},{8,12},{10,14},{12... | collective-permute-start | bytes 4718600 | tf_op jit(solution)/shard_map/ppermute | solution.py:61
  51.8 37.6 %collective-permute-start.10 = (bf16[3,2,1,256,512]{4,3,0,2,1:T(8,128)(2,1)}, bf16[3,2,1,256,512]{4,3,0,2,1:T(8,128)(2,1)}, u32[]{:S(2)}, u32[]{:S(2)}) collective-permute-start(bf16[3,2,1,256,512]{4,3,0,2,1:T(8,128)(2,1)} %copy.304), channel_id=1, source_target_pairs={{0,1},{1,0},{2,3},{3,2},{4,5},{5,4},{6,7},{7,6},{8,9},{9,8},{10,11... | collective-permute-start | bytes 4718600 | tf_op jit(solution)/shard_map/ppermute | solution.py:62
  112.7 47.4 %collective-permute-start.39 = (bf16[1,1,1,64,2048]{4,3,1,2,0:T(8,128)(2,1)}, bf16[1,1,1,64,2048]{4,3,1,2,0:T(8,128)(2,1)}, u32[]{:S(2)}, u32[]{:S(2)}) collective-permute-start(bf16[1,1,1,64,2048]{4,3,1,2,0:T(8,128)(2,1)} %get-tuple-element.221), channel_id=1, source_target_pairs={{0,4},{2,6},{4,0},{6,2},{1,5},{3,7},{5,1},{7,3},{8,12},{10,14},{12... | collective-permute-start | bytes 786440 | tf_op jit(solution)/shard_map/ppermute | solution.py:61
  113.2 46.9 %collective-permute-start.41 = (bf16[1,1,1,64,2048]{4,3,1,2,0:T(8,128)(2,1)}, bf16[1,1,1,64,2048]{4,3,1,2,0:T(8,128)(2,1)}, u32[]{:S(2)}, u32[]{:S(2)}) collective-permute-start(bf16[1,1,1,64,2048]{4,3,1,2,0:T(8,128)(2,1)} %get-tuple-element.222), channel_id=1, source_target_pairs={{0,1},{1,0},{2,3},{3,2},{4,5},{5,4},{6,7},{7,6},{8,9},{9,8},{10,11... | collective-permute-start | bytes 786440 | tf_op jit(solution)/shard_map/ppermute | solution.py:62
  142.0 41.2 %collective-permute-start.16 = (bf16[256,5632]{0,1:T(8,128)(2,1)}, bf16[256,5632]{0,1:T(8,128)(2,1)}, u32[]{:S(2)}, u32[]{:S(2)}) collective-permute-start(bf16[256,5632]{0,1:T(8,128)(2,1)} %bitcast.64), channel_id=1, source_target_pairs={{0,2},{2,0},{4,6},{6,4},{1,3},{3,1},{5,7},{7,5},{8,10},{10,8},{12,... | collective-permute-start | bytes 8650760 | tf_op jit(solution)/shard_map/ppermute | solution.py:57
  192.6 65.4 %collective-permute-start.28 = (bf16[2,1,2,704,512]{4,3,2,1,0:T(8,128)(2,1)}, bf16[2,1,2,704,512]{4,3,2,1,0:T(8,128)(2,1)}, u32[]{:S(2)}, u32[]{:S(2)}) collective-permute-start(bf16[2,1,2,704,512]{4,3,2,1,0:T(8,128)(2,1)} %constant_dynamic-slice_fusion.10), channel_id=1, source_target_pairs={{0,4},{2,6},{4,0},{6,2},{1,5},{3,7},{5,1},{7,3},{8,12},{10,14},{12... | collective-permute-start | bytes 8650760 | tf_op jit(solution)/shard_map/ppermute | solution.py:61
  203.4 65.6 %collective-permute-start.26 = (bf16[2,2,1,704,512]{4,3,2,1,0:T(8,128)(2,1)}, bf16[2,2,1,704,512]{4,3,2,1,0:T(8,128)(2,1)}, u32[]{:S(2)}, u32[]{:S(2)}) collective-permute-start(bf16[2,2,1,704,512]{4,3,2,1,0:T(8,128)(2,1)} %constant_dynamic-slice_fusion.12), channel_id=1, source_target_pairs={{0,1},{1,0},{2,3},{3,2},{4,5},{5,4},{6,7},{7,6},{8,9},{9,8},{10,11... | collective-permute-start | bytes 8650760 | tf_op jit(solution)/shard_map/ppermute | solution.py:62
  262.1 37.1 %collective-permute-start.29 = (bf16[2,1,1,704,512]{4,3,2,1,0:T(8,128)(2,1)S(1)}, bf16[2,1,1,704,512]{4,3,2,1,0:T(8,128)(2,1)S(1)}, u32[]{:S(2)}, u32[]{:S(2)}) collective-permute-start(bf16[2,1,1,704,512]{4,3,2,1,0:T(8,128)(2,1)S(1)} %constant_dynamic-slice_fusion.9), channel_id=1, source_target_pairs={{0,1},{1,0},{2,3},{3,2},{4,5},{5,4},{6,7},{7,6},{8,9},{9,8},{10,11... | collective-permute-start | bytes 4325384 | tf_op jit(solution)/shard_map/ppermute | solution.py:62
  302.9 92.9 %collective-permute-start.46 = (bf16[2,1,1,704,512]{4,3,2,1,0:T(8,128)(2,1)}, bf16[2,1,1,704,512]{4,3,2,1,0:T(8,128)(2,1)}, u32[]{:S(2)}, u32[]{:S(2)}) collective-permute-start(bf16[2,1,1,704,512]{4,3,2,1,0:T(8,128)(2,1)} %pad_maximum_fusion.20), channel_id=1, source_target_pairs={{0,1},{1,0},{2,3},{3,2},{4,5},{5,4},{6,7},{7,6},{8,9},{9,8},{10,11... | collective-permute-start | bytes 4325384 | tf_op jit(solution)/shard_map/ppermute | solution.py:62
  338.2 76.5 %collective-permute-start.30 = (bf16[2,2,256,1024]{3,2,1,0:T(8,128)(2,1)}, bf16[2,2,256,1024]{3,2,1,0:T(8,128)(2,1)}, u32[]{:S(2)}, u32[]{:S(2)}) collective-permute-start(bf16[2,2,256,1024]{3,2,1,0:T(8,128)(2,1)} %bitcast.480), channel_id=1, source_target_pairs={{0,2},{2,0},{4,6},{6,4},{1,3},{3,1},{5,7},{7,5},{8,10},{10,8},{12,... | collective-permute-start | bytes 6291464 | tf_op jit(solution)/shard_map/ppermute | solution.py:57
  341.9 59.8 %collective-permute-start.98 = (bf16[352,2048]{1,0:T(8,128)(2,1)}, bf16[352,2048]{1,0:T(8,128)(2,1)}, u32[]{:S(2)}, u32[]{:S(2)}) collective-permute-start(bf16[352,2048]{1,0:T(8,128)(2,1)} %get-tuple-element.163), channel_id=1, source_target_pairs={{0,8},{24,16},{1,9},{25,17},{2,10},{26,18},{3,11},{27,19},{4,12},{... | collective-permute-start | bytes 4325384 | tf_op jit(solution)/shard_map/ppermute | solution.py:131
  346.8 61.6 %collective-permute-start.101 = (bf16[352,2048]{1,0:T(8,128)(2,1)}, bf16[352,2048]{1,0:T(8,128)(2,1)}, u32[]{:S(2)}, u32[]{:S(2)}) collective-permute-start(bf16[352,2048]{1,0:T(8,128)(2,1)} %get-tuple-element.164), channel_id=1, source_target_pairs={{0,8},{24,16},{1,9},{25,17},{2,10},{26,18},{3,11},{27,19},{4,12},{... | collective-permute-start | bytes 4325384 | tf_op jit(solution)/shard_map/ppermute | solution.py:131
  400.7 113.0 %collective-permute-start.47 = (bf16[2,1,2,704,512]{4,3,2,1,0:T(8,128)(2,1)}, bf16[2,1,2,704,512]{4,3,2,1,0:T(8,128)(2,1)}, u32[]{:S(2)}, u32[]{:S(2)}) collective-permute-start(bf16[2,1,2,704,512]{4,3,2,1,0:T(8,128)(2,1)} %pad_maximum_fusion.5), channel_id=1, source_target_pairs={{0,4},{2,6},{4,0},{6,2},{1,5},{3,7},{5,1},{7,3},{8,12},{10,14},{12... | collective-permute-start | bytes 8650760 | tf_op jit(solution)/shard_map/ppermute | solution.py:61
  413.0 94.6 %collective-permute-start.99 = (bf16[352,2048]{1,0:T(8,128)(2,1)}, bf16[352,2048]{1,0:T(8,128)(2,1)}, u32[]{:S(2)}, u32[]{:S(2)}) collective-permute-start(bf16[352,2048]{1,0:T(8,128)(2,1)} %get-tuple-element.161), channel_id=1, source_target_pairs={{8,16},{16,8},{9,17},{17,9},{10,18},{18,10},{11,19},{19,11},{12,20... | collective-permute-start | bytes 4325384 | tf_op jit(solution)/shard_map/ppermute | solution.py:135
  425.0 71.3 %collective-permute-start.33 = (bf16[1,1,2,256,512]{4,3,2,1,0:T(8,128)(2,1)S(1)}, bf16[1,1,2,256,512]{4,3,2,1,0:T(8,128)(2,1)S(1)}, u32[]{:S(2)}, u32[]{:S(2)}) collective-permute-start(bf16[1,1,2,256,512]{4,3,2,1,0:T(8,128)(2,1)S(1)} %constant_dynamic-slice_fusion.4), channel_id=1, source_target_pairs={{0,4},{2,6},{4,0},{6,2},{1,5},{3,7},{5,1},{7,3},{8,12},{10,14},{12... | collective-permute-start | bytes 1572872 | tf_op jit(solution)/shard_map/ppermute | solution.py:61
  428.0 88.0 %collective-permute-start.45 = (bf16[2,2,1,704,512]{4,3,2,1,0:T(8,128)(2,1)}, bf16[2,2,1,704,512]{4,3,2,1,0:T(8,128)(2,1)}, u32[]{:S(2)}, u32[]{:S(2)}) collective-permute-start(bf16[2,2,1,704,512]{4,3,2,1,0:T(8,128)(2,1)} %pad_maximum_fusion.4), channel_id=1, source_target_pairs={{0,1},{1,0},{2,3},{3,2},{4,5},{5,4},{6,7},{7,6},{8,9},{9,8},{10,11... | collective-permute-start | bytes 8650760 | tf_op jit(solution)/shard_map/ppermute | solution.py:62
  432.6 68.8 %collective-permute-start.32 = (bf16[1,1,1,256,512]{4,3,2,1,0:T(8,128)(2,1)S(1)}, bf16[1,1,1,256,512]{4,3,2,1,0:T(8,128)(2,1)S(1)}, u32[]{:S(2)}, u32[]{:S(2)}) collective-permute-start(bf16[1,1,1,256,512]{4,3,2,1,0:T(8,128)(2,1)S(1)} %constant_dynamic-slice_fusion.5), channel_id=1, source_target_pairs={{0,4},{2,6},{4,0},{6,2},{1,5},{3,7},{5,1},{7,3},{8,12},{10,14},{12... | collective-permute-start | bytes 786440 | tf_op jit(solution)/shard_map/ppermute | solution.py:61
  511.2 60.0 %collective-permute-start.100 = (bf16[352,2048]{1,0:T(8,128)(2,1)}, bf16[352,2048]{1,0:T(8,128)(2,1)}, u32[]{:S(2)}, u32[]{:S(2)}) collective-permute-start(bf16[352,2048]{1,0:T(8,128)(2,1)} %reduce-precision_convert_fusion.2), channel_id=1, source_target_pairs={{8,0},{16,24},{9,1},{17,25},{10,2},{18,26},{11,3},{19,27},{12,4},{... | collective-permute-start | bytes 4325384 | tf_op jit(solution)/shard_map/ppermute | solution.py:139
  534.4 43.8 %collective-permute-start.103 = (bf16[352,2048]{1,0:T(8,128)(2,1)}, bf16[352,2048]{1,0:T(8,128)(2,1)}, u32[]{:S(2)}, u32[]{:S(2)}) collective-permute-start(bf16[352,2048]{1,0:T(8,128)(2,1)} %reduce-precision_convert_fusion), channel_id=1, source_target_pairs={{8,0},{16,24},{9,1},{17,25},{10,2},{18,26},{11,3},{19,27},{12,4},{... | collective-permute-start | bytes 4325384 | tf_op jit(solution)/shard_map/ppermute | solution.py:139
  561.5 38.3 %collective-permute-start.85 = (bf16[128,5632]{1,0:T(8,128)(2,1)S(1)}, bf16[128,5632]{1,0:T(8,128)(2,1)S(1)}, u32[]{:S(2)}, u32[]{:S(2)}) collective-permute-start(bf16[128,5632]{1,0:T(8,128)(2,1)S(1)} %get-tuple-element.119), channel_id=1, source_target_pairs={{0,8},{24,16},{1,9},{25,17},{2,10},{26,18},{3,11},{27,19},{4,12},{... | collective-permute-start | bytes 4325384 | tf_op jit(solution)/shard_map/ppermute | solution.py:131
  568.0 62.7 %collective-permute-start.94 = (bf16[128,5632]{1,0:T(8,128)(2,1)S(1)}, bf16[128,5632]{1,0:T(8,128)(2,1)S(1)}, u32[]{:S(2)}, u32[]{:S(2)}) collective-permute-start(bf16[128,5632]{1,0:T(8,128)(2,1)S(1)} %get-tuple-element.120), channel_id=1, source_target_pairs={{0,8},{24,16},{1,9},{25,17},{2,10},{26,18},{3,11},{27,19},{4,12},{... | collective-permute-start | bytes 4325384 | tf_op jit(solution)/shard_map/ppermute | solution.py:131
  569.4 92.2 %collective-permute-start.91 = (bf16[128,5632]{1,0:T(8,128)(2,1)S(1)}, bf16[128,5632]{1,0:T(8,128)(2,1)S(1)}, u32[]{:S(2)}, u32[]{:S(2)}) collective-permute-start(bf16[128,5632]{1,0:T(8,128)(2,1)S(1)} %get-tuple-element.121), channel_id=1, source_target_pairs={{0,8},{24,16},{1,9},{25,17},{2,10},{26,18},{3,11},{27,19},{4,12},{... | collective-permute-start | bytes 4325384 | tf_op jit(solution)/shard_map/ppermute | solution.py:131
  571.3 120.8 %collective-permute-start.88 = (bf16[128,5632]{1,0:T(8,128)(2,1)S(1)}, bf16[128,5632]{1,0:T(8,128)(2,1)S(1)}, u32[]{:S(2)}, u32[]{:S(2)}) collective-permute-start(bf16[128,5632]{1,0:T(8,128)(2,1)S(1)} %get-tuple-element.122), channel_id=1, source_target_pairs={{0,8},{24,16},{1,9},{25,17},{2,10},{26,18},{3,11},{27,19},{4,12},{... | collective-permute-start | bytes 4325384 | tf_op jit(solution)/shard_map/ppermute | solution.py:131
  593.7 115.6 %collective-permute-start.55 = (bf16[1,1,2,256,512]{4,3,2,1,0:T(8,128)(2,1)}, bf16[1,1,2,256,512]{4,3,2,1,0:T(8,128)(2,1)S(1)}, u32[]{:S(2)}, u32[]{:S(2)}) collective-permute-start(bf16[1,1,2,256,512]{4,3,2,1,0:T(8,128)(2,1)} %pad_maximum_fusion.35), channel_id=1, source_target_pairs={{0,4},{2,6},{4,0},{6,2},{1,5},{3,7},{5,1},{7,3},{8,12},{10,14},{12... | collective-permute-start | bytes 1572872 | tf_op jit(solution)/shard_map/ppermute | solution.py:61
  599.8 112.3 %collective-permute-start.53 = (bf16[1,2,1,256,512]{4,3,2,1,0:T(8,128)(2,1)}, bf16[1,2,1,256,512]{4,3,2,1,0:T(8,128)(2,1)}, u32[]{:S(2)}, u32[]{:S(2)}) collective-permute-start(bf16[1,2,1,256,512]{4,3,2,1,0:T(8,128)(2,1)} %pad_maximum_fusion.34), channel_id=1, source_target_pairs={{0,1},{1,0},{2,3},{3,2},{4,5},{5,4},{6,7},{7,6},{8,9},{9,8},{10,11... | collective-permute-start | bytes 1572872 | tf_op jit(solution)/shard_map/ppermute | solution.py:62
  715.9 147.2 %collective-permute-start.87 = (bf16[128,5632]{1,0:T(8,128)(2,1)S(1)}, bf16[128,5632]{1,0:T(8,128)(2,1)}, u32[]{:S(2)}, u32[]{:S(2)}) collective-permute-start(bf16[128,5632]{1,0:T(8,128)(2,1)S(1)} %reduce-precision_convert_fusion.10), channel_id=1, source_target_pairs={{8,0},{16,24},{9,1},{17,25},{10,2},{18,26},{11,3},{19,27},{12,4},{... | collective-permute-start | bytes 4325384 | tf_op jit(solution)/shard_map/ppermute | solution.py:139
  717.5 189.0 %collective-permute-start.90 = (bf16[128,5632]{1,0:T(8,128)(2,1)S(1)}, bf16[128,5632]{1,0:T(8,128)(2,1)}, u32[]{:S(2)}, u32[]{:S(2)}) collective-permute-start(bf16[128,5632]{1,0:T(8,128)(2,1)S(1)} %reduce-precision_convert_fusion.8), channel_id=1, source_target_pairs={{8,0},{16,24},{9,1},{17,25},{10,2},{18,26},{11,3},{19,27},{12,4},{... | collective-permute-start | bytes 4325384 | tf_op jit(solution)/shard_map/ppermute | solution.py:139
  719.2 111.6 %collective-permute-start.93 = (bf16[128,5632]{1,0:T(8,128)(2,1)S(1)}, bf16[128,5632]{1,0:T(8,128)(2,1)S(1)}, u32[]{:S(2)}, u32[]{:S(2)}) collective-permute-start(bf16[128,5632]{1,0:T(8,128)(2,1)S(1)} %reduce-precision_convert_fusion.6), channel_id=1, source_target_pairs={{8,0},{16,24},{9,1},{17,25},{10,2},{18,26},{11,3},{19,27},{12,4},{... | collective-permute-start | bytes 4325384 | tf_op jit(solution)/shard_map/ppermute | solution.py:139
  720.9 139.1 %collective-permute-start.96 = (bf16[128,5632]{1,0:T(8,128)(2,1)S(1)}, bf16[128,5632]{1,0:T(8,128)(2,1)S(1)}, u32[]{:S(2)}, u32[]{:S(2)}) collective-permute-start(bf16[128,5632]{1,0:T(8,128)(2,1)S(1)} %reduce-precision_convert_fusion.4), channel_id=1, source_target_pairs={{8,0},{16,24},{9,1},{17,25},{10,2},{18,26},{11,3},{19,27},{12,4},{... | collective-permute-start | bytes 4325384 | tf_op jit(solution)/shard_map/ppermute | solution.py:139
  732.0 129.9 %collective-permute-start.59 = (bf16[3,1,1,256,512]{4,3,2,1,0:T(8,128)(2,1)S(1)}, bf16[3,1,1,256,512]{4,3,2,1,0:T(8,128)(2,1)S(1)}, u32[]{:S(2)}, u32[]{:S(2)}) collective-permute-start(bf16[3,1,1,256,512]{4,3,2,1,0:T(8,128)(2,1)S(1)} %bitcast.428), channel_id=1, source_target_pairs={{0,1},{1,0},{2,3},{3,2},{4,5},{5,4},{6,7},{7,6},{8,9},{9,8},{10,11... | collective-permute-start | bytes 2359304 | tf_op jit(solution)/shard_map/ppermute | solution.py:62
  861.9 120.4 %collective-permute-start.97 = (bf16[256,5632]{1,0:T(8,128)(2,1)S(1)}, bf16[256,5632]{1,0:T(8,128)(2,1)S(1)}, u32[]{:S(2)}, u32[]{:S(2)}) collective-permute-start(bf16[256,5632]{1,0:T(8,128)(2,1)S(1)} %pad_maximum_fusion.7), channel_id=1, source_target_pairs={{0,2},{2,0},{4,6},{6,4},{1,3},{3,1},{5,7},{7,5},{8,10},{10,8},{12,... | collective-permute-start | bytes 8650760 | tf_op jit(solution)/shard_map/ppermute | solution.py:57
  862.2 36.9 %collective-permute-start.60 = (bf16[3,1,2,256,512]{4,3,2,1,0:T(8,128)(2,1)S(1)}, bf16[3,1,2,256,512]{4,3,2,1,0:T(8,128)(2,1)S(1)}, u32[]{:S(2)}, u32[]{:S(2)}) collective-permute-start(bf16[3,1,2,256,512]{4,3,2,1,0:T(8,128)(2,1)S(1)} %pad_maximum_fusion.15), channel_id=1, source_target_pairs={{0,4},{2,6},{4,0},{6,2},{1,5},{3,7},{5,1},{7,3},{8,12},{10,14},{12... | collective-permute-start | bytes 4718600 | tf_op jit(solution)/shard_map/ppermute | solution.py:61
  908.4 69.6 %collective-permute-start.84 = (bf16[256,2048]{1,0:T(8,128)(2,1)S(1)}, bf16[256,2048]{1,0:T(8,128)(2,1)S(1)}, u32[]{:S(2)}, u32[]{:S(2)}) collective-permute-start(bf16[256,2048]{1,0:T(8,128)(2,1)S(1)} %reduce-precision_convert_fusion.12), channel_id=1, source_target_pairs={{8,0},{16,24},{9,1},{17,25},{10,2},{18,26},{11,3},{19,27},{12,4},{... | collective-permute-start | bytes 3145736 | tf_op jit(solution)/shard_map/ppermute | solution.py:139
  914.4 43.7 %collective-permute-start.75 = (bf16[128,3072]{1,0:T(8,128)(2,1)S(1)}, bf16[128,3072]{1,0:T(8,128)(2,1)S(1)}, u32[]{:S(2)}, u32[]{:S(2)}) collective-permute-start(bf16[128,3072]{1,0:T(8,128)(2,1)S(1)} %get-tuple-element.151), channel_id=1, source_target_pairs={{0,8},{24,16},{1,9},{25,17},{2,10},{26,18},{3,11},{27,19},{4,12},{... | collective-permute-start | bytes 2359304 | tf_op jit(solution)/shard_map/ppermute | solution.py:131
  924.4 49.2 %collective-permute-start.72 = (bf16[128,3072]{1,0:T(8,128)(2,1)S(1)}, bf16[128,3072]{1,0:T(8,128)(2,1)S(1)}, u32[]{:S(2)}, u32[]{:S(2)}) collective-permute-start(bf16[128,3072]{1,0:T(8,128)(2,1)S(1)} %get-tuple-element.152), channel_id=1, source_target_pairs={{0,8},{24,16},{1,9},{25,17},{2,10},{26,18},{3,11},{27,19},{4,12},{... | collective-permute-start | bytes 2359304 | tf_op jit(solution)/shard_map/ppermute | solution.py:131
  941.3 62.2 %collective-permute-start.61 = (f32[256,1024]{1,0:T(8,128)S(1)}, f32[256,1024]{1,0:T(8,128)}, u32[]{:S(2)}, u32[]{:S(2)}) collective-permute-start(f32[256,1024]{1,0:T(8,128)S(1)} %slice.380), channel_id=1, source_target_pairs={{0,2},{2,0},{4,6},{6,4},{1,3},{3,1},{5,7},{7,5},{8,10},{10,8},{12,... | collective-permute-start | bytes 3145736 | tf_op jit(solution)/shard_map/ppermute | solution.py:57
  976.1 141.9 %collective-permute-start.70 = (bf16[128,3072]{1,0:T(8,128)(2,1)}, bf16[128,3072]{1,0:T(8,128)(2,1)}, u32[]{:S(2)}, u32[]{:S(2)}) collective-permute-start(bf16[128,3072]{1,0:T(8,128)(2,1)} %get-tuple-element.145), channel_id=1, source_target_pairs={{8,16},{16,8},{9,17},{17,9},{10,18},{18,10},{11,19},{19,11},{12,20... | collective-permute-start | bytes 2359304 | tf_op jit(solution)/shard_map/ppermute | solution.py:135
  1036.0 72.5 %collective-permute-start.108 = (f32[7,1,256]{2,1,0:T(1,128)S(1)}, f32[7,1,256]{2,1,0:T(1,128)S(1)}, u32[]{:S(2)}, u32[]{:S(2)}) collective-permute-start(f32[7,1,256]{2,1,0:T(1,128)S(1)} %add.696), channel_id=1, source_target_pairs={{0,5},{1,4},{2,7},{3,6},{4,1},{5,0},{6,3},{7,2},{8,13},{9,12},{10,... | collective-permute-start | bytes 21512 | tf_op jit(solution)/shard_map/ppermute | solution.py:88
  1037.1 69.8 %collective-permute-start.107 = (f32[7,1,256]{2,1,0:T(1,128)S(1)}, f32[7,1,256]{2,1,0:T(1,128)S(1)}, u32[]{:S(2)}, u32[]{:S(2)}) collective-permute-start(f32[7,1,256]{2,1,0:T(1,128)S(1)} %add.696), channel_id=1, source_target_pairs={{0,4},{1,5},{2,6},{3,7},{4,0},{5,1},{6,2},{7,3},{8,12},{9,13},{10,... | collective-permute-start | bytes 21512 | tf_op jit(solution)/shard_map/ppermute | solution.py:88
  1038.3 67.0 %collective-permute-start.106 = (f32[7,1,256]{2,1,0:T(1,128)S(1)}, f32[7,1,256]{2,1,0:T(1,128)S(1)}, u32[]{:S(2)}, u32[]{:S(2)}) collective-permute-start(f32[7,1,256]{2,1,0:T(1,128)S(1)} %add.696), channel_id=1, source_target_pairs={{0,1},{1,0},{2,3},{3,2},{4,5},{5,4},{6,7},{7,6},{8,9},{9,8},{10,11... | collective-permute-start | bytes 21512 | tf_op jit(solution)/shard_map/ppermute | solution.py:88
  1039.6 70.7 %collective-permute-start.64 = (f32[2,1024]{1,0:T(2,128)S(1)}, f32[2,1024]{1,0:T(2,128)S(1)}, u32[]{:S(2)}, u32[]{:S(2)}) collective-permute-start(f32[2,1024]{1,0:T(2,128)S(1)} %fusion.139), channel_id=1, source_target_pairs={{0,2},{2,0},{4,6},{6,4},{1,3},{3,1},{5,7},{7,5},{8,10},{10,8},{12,... | collective-permute-start | bytes 24584 | tf_op jit(solution)/shard_map/ppermute | solution.py:57
  1119.5 96.0 %collective-permute-start.71 = (bf16[128,3072]{1,0:T(8,128)(2,1)S(1)}, bf16[128,3072]{1,0:T(8,128)(2,1)}, u32[]{:S(2)}, u32[]{:S(2)}) collective-permute-start(bf16[128,3072]{1,0:T(8,128)(2,1)S(1)} %reduce-precision_convert_fusion.20), channel_id=1, source_target_pairs={{8,0},{16,24},{9,1},{17,25},{10,2},{18,26},{11,3},{19,27},{12,4},{... | collective-permute-start | bytes 2359304 | tf_op jit(solution)/shard_map/ppermute | solution.py:139
  1123.2 93.6 %collective-permute-start.74 = (bf16[128,3072]{1,0:T(8,128)(2,1)}, bf16[128,3072]{1,0:T(8,128)(2,1)}, u32[]{:S(2)}, u32[]{:S(2)}) collective-permute-start(bf16[128,3072]{1,0:T(8,128)(2,1)} %reduce-precision_convert_fusion.18), channel_id=1, source_target_pairs={{8,0},{16,24},{9,1},{17,25},{10,2},{18,26},{11,3},{19,27},{12,4},{... | collective-permute-start | bytes 2359304 | tf_op jit(solution)/shard_map/ppermute | solution.py:139
  1125.8 51.8 %collective-permute-start.77 = (bf16[128,3072]{1,0:T(8,128)(2,1)S(1)}, bf16[128,3072]{1,0:T(8,128)(2,1)S(1)}, u32[]{:S(2)}, u32[]{:S(2)}) collective-permute-start(bf16[128,3072]{1,0:T(8,128)(2,1)S(1)} %reduce-precision_convert_fusion.16), channel_id=1, source_target_pairs={{8,0},{16,24},{9,1},{17,25},{10,2},{18,26},{11,3},{19,27},{12,4},{... | collective-permute-start | bytes 2359304 | tf_op jit(solution)/shard_map/ppermute | solution.py:139
  1128.4 65.4 %collective-permute-start.80 = (bf16[128,3072]{1,0:T(8,128)(2,1)S(1)}, bf16[128,3072]{1,0:T(8,128)(2,1)S(1)}, u32[]{:S(2)}, u32[]{:S(2)}) collective-permute-start(bf16[128,3072]{1,0:T(8,128)(2,1)S(1)} %reduce-precision_convert_fusion.14), channel_id=1, source_target_pairs={{8,0},{16,24},{9,1},{17,25},{10,2},{18,26},{11,3},{19,27},{12,4},{... | collective-permute-start | bytes 2359304 | tf_op jit(solution)/shard_map/ppermute | solution.py:139
  1131.0 65.0 %collective-permute-start.68 = (f32[2,256,128]{2,1,0:T(8,128)S(1)}, f32[2,256,128]{2,1,0:T(8,128)S(1)}, u32[]{:S(2)}, u32[]{:S(2)}) collective-permute-start(f32[2,256,128]{2,1,0:T(8,128)S(1)} %get-tuple-element.179), channel_id=1, source_target_pairs={{0,5},{1,4},{2,7},{3,6},{4,1},{5,0},{6,3},{7,2},{8,13},{9,12},{10,... | collective-permute-start | bytes 786440 | tf_op jit(solution)/shard_map/ppermute | solution.py:88
  (142 other events, 1913.4 us)

commit v2 on v1

v2 whole, which is shorter than its diff:
```python
import functools

import jax
import jax.numpy as jnp
from jax import lax
from jax.experimental import pallas as pl
from jax.experimental.pallas import tpu as pltpu
from jax.sharding import PartitionSpec as P

HEADS = 32
HEAD_DIM = 64
FF = 5632
ROTARY = 16
STEP = 10

eps_norm = 1e-05
masked_score = -1e30
beta_one = 0.9
beta_two = 0.999
adam_eps = 1e-08
weight_decay = 0.1
score_scale = HEAD_DIM ** (-0.5)
FIRST = (((0,), (0,)), ((), ()))
LAST = (((1,), (1,)), ((), ()))
PLAIN = (((1,), (0,)), ((), ()))
bf16 = jnp.bfloat16
f32 = jnp.float32


def dot(a, b, dims):
    return lax.dot_general(a, b, dims, preferred_element_type=f32)


def adam_update(weight, moment_one, moment_two, grad, step_rate, decay_rate):
    first_new = beta_one * moment_one + (1.0 - beta_one) * grad
    second_new = beta_two * moment_two + (1.0 - beta_two) * grad * grad
    first_hat = first_new / (1.0 - beta_one**STEP)
    second_hat = second_new / (1.0 - beta_two**STEP)
    weight_new = weight - step_rate * (
        first_hat / (jnp.sqrt(second_hat) + adam_eps) + decay_rate * weight
    )
    return (first_new, second_new, weight_new)


class Plane:
    def __init__(self):
        self.s_size = lax.axis_size("shard")
        self.ctx_size = lax.axis_size("ctx")
        self.y_size = self.ctx_size // 2
        self.ctx = lax.axis_index("ctx")
        self.s = lax.axis_index("shard")
        self.y = self.ctx // 2
        self.c = self.ctx % 2
        self.blocks = self.ctx_size * self.s_size

    def core(self, x):
        return lax.ppermute(x, "ctx", [(i, i ^ 1) for i in range(self.ctx_size)])

    def along(self, x, axis, step):
        if axis == "y":
            return lax.ppermute(x, "ctx", [(i, i ^ (2 * step)) for i in range(self.ctx_size)])
        return lax.ppermute(x, "shard", [(i, i ^ step) for i in range(self.s_size)])

    def index(self, axis):
        return self.y if axis == "y" else self.s

    def steps(self, flip):
        ys = []
        k = self.y_size // 2
        while k:
            ys.append(("y", k))
            k //= 2
        ss = []
        k = self.s_size // 2
        while k:
            ss.append(("s", k))
            k //= 2
        return ys + ss if flip else ss + ys

    def chip_exchange(self, x, take):
        out = [(self.y, self.s, take(self.y, self.s))]
        for ry in range(self.y_size):
            for rs in range(self.s_size):
                if ry or rs:
                    y, s = self.y ^ ry, self.s ^ rs
                    mask = 2 * ry * self.s_size + rs
                    perm = [(i, i ^ mask) for i in range(self.blocks)]
                    out.append((y, s, lax.ppermute(take(y, s), ("ctx", "shard"), perm)))
        return out

    def sum_all(self, x):
        for axis, step in self.steps(False):
            x = x + self.along(x, axis, step)
        return x + self.core(x)

    def scatter_sum(self, p, flip):
        axes = {"y": 1, "s": 2}
        steps = self.steps(flip)
        kept = got = None
        for n, (axis, step) in enumerate(steps):
            ax = axes[axis]
            bit = (self.index(axis) // step) % 2
            kept = lax.dynamic_slice_in_dim(p, bit * step, step, ax)
            send = lax.dynamic_slice_in_dim(p, (1 - bit) * step, step, ax)
            got = self.along(send, axis, step)
            if n + 1 < len(steps):
                p = (kept.astype(f32) + got.astype(f32)).astype(bf16)
        return kept[:, 0, 0], got[:, 0, 0]

    def gather(self, p, flip):
        axes = {"y": 1, "s": 2}
        p = p[:, None, None]
        for axis, step in reversed(self.steps(flip)):
            ax = axes[axis]
            bit = (self.index(axis) // step) % 2
            got = self.along(p, axis, step)
            first = bit == 0
            p = jnp.concatenate([jnp.where(first, p, got), jnp.where(first, got, p)], ax)
        return p


class Order:
    def __init__(self):
        self.last = None

    def __call__(self, stage, *args):
        if self.last is not None:
            args, self.last = lax.optimization_barrier((args, self.last))
        out = stage(*args)
        self.last = jax.tree.leaves(out)[0]
        return out


class RepSum:
    def __init__(self, order):
        self.order = order
        size = lax.axis_size("rep")
        z = lax.axis_index("rep")
        self.end = (z == 0) | (z == size - 1)
        self.queue = []
        self.one = self.two = self.three = None
        self.done = {}

    def push(self, name, g):
        self.queue.append((name, g))

    def add(self, a, b):
        return self.order(
            lambda a, b: lax.reduce_precision(a.astype(f32) + b.astype(f32), 8, 7).astype(bf16), a, b
        )

    def tick(self):
        if self.three:
            name, total, got = self.three
            self.done[name] = jnp.where(self.end, got, total)
            self.three = None
        if self.two:
            name, part, got = self.two
            total = self.add(part, got)
            self.three = (name, total, lax.ppermute(total, "rep", [(1, 0), (2, 3)]))
            self.two = None
        if self.one:
            name, part, got = self.one
            part = self.add(part, got)
            self.two = (name, part, lax.ppermute(part, "rep", [(1, 2), (2, 1)]))
            self.one = None
        if self.queue:
            name, g = self.queue.pop(0)
            self.one = (name, g, lax.ppermute(g, "rep", [(0, 1), (3, 2)]))

    def drain(self, name):
        while name not in self.done:
            self.tick()
        return self.done[name]


def split_kernel(core_ref, w_ref, mine_ref, theirs_ref):
    unit = mine_ref.shape[1]
    w = w_ref[...].astype(bf16)
    first = core_ref[0] == 0
    a, b = w[:, :unit], w[:, unit:]
    mine_ref[...] = jnp.where(first, a, b)
    theirs_ref[...] = jnp.where(first, b, a)


def split_columns(w, core, lead, unit, count):
    rows = w.shape[0]
    half = pl.BlockSpec((rows, unit), lambda j, core: (0, j))
    out = jax.ShapeDtypeStruct((rows, count * unit), bf16)
    return pl.pallas_call(
        split_kernel,
        grid_spec=pltpu.PrefetchScalarGridSpec(
            num_scalar_prefetch=1,
            grid=(count,),
            in_specs=[pl.BlockSpec((rows, 2 * unit), lambda j, core: (0, lead + j))],
            out_specs=[half, half],
        ),
        out_shape=[out, out],
        compiler_params=pltpu.CompilerParams(vmem_limit_bytes=32 * 1024 * 1024),
        cost_estimate=pl.CostEstimate(flops=0, bytes_accessed=12 * rows * count * unit, transcendentals=0),
    )(core, w)


def adam_kernel(rate, core_ref, w_ref, m_ref, v_ref, mine_ref, theirs_ref, new_m_ref, new_v_ref, new_w_ref):
    mine = core_ref[0] == pl.program_id(2)
    grad = jnp.where(mine, mine_ref[...], theirs_ref[...]).astype(f32)
    new_m, new_v, new_w = adam_update(w_ref[...], m_ref[...], v_ref[...], grad, rate, weight_decay)
    new_m_ref[...] = new_m
    new_v_ref[...] = new_v
    new_w_ref[...] = new_w


def adam_columns(w, m, v, mine, theirs, core, unit, rate):
    rows, width = w.shape
    rb = min(rows, 128)
    whole = pl.BlockSpec((rb, unit), lambda i, g, j, core: (i, 2 * g + j))
    half = pl.BlockSpec((rb, unit), lambda i, g, j, core: (i, g))
    out = jax.ShapeDtypeStruct((rows, width), f32)
    return pl.pallas_call(
        functools.partial(adam_kernel, rate),
        grid_spec=pltpu.PrefetchScalarGridSpec(
            num_scalar_prefetch=1,
            grid=(rows // rb, width // (2 * unit), 2),
            in_specs=[whole, whole, whole, half, half],
            out_specs=[whole, whole, whole],
        ),
        out_shape=[out, out, out],
        compiler_params=pltpu.CompilerParams(vmem_limit_bytes=32 * 1024 * 1024),
        cost_estimate=pl.CostEstimate(flops=20 * rows * width, bytes_accessed=28 * rows * width, transcendentals=0),
    )(core, w, m, v, mine, theirs)


def attend_kernel(kept_ref, got_ref, bias_ref, cos_ref, sin_ref, prow_ref, pcol_ref, qkv_ref, out_ref, peak_ref, total_ref):
    cos, sin = cos_ref[0], sin_ref[0]
    half = ROTARY // 2
    parts = []
    for i in range(3):
        v = kept_ref[i, 0].astype(f32) + got_ref[i, 0].astype(f32) + bias_ref[i, 0]
        if i < 2:
            a, b = v[:half], v[half:ROTARY]
            v = jnp.concatenate([a * cos - b * sin, b * cos + a * sin, v[ROTARY:]], axis=0)
        v = v.astype(bf16)
        qkv_ref[i, 0] = v
        parts.append(v)
    q, k, v = parts
    scores = dot(k, q, FIRST) * score_scale
    scores = jnp.where(pcol_ref[0] <= prow_ref[0], scores, masked_score)
    peak = jnp.max(scores, axis=0, keepdims=True)
    e = jnp.exp(scores - peak)
    total = jnp.sum(e, axis=0, keepdims=True)
    p = (e / total).astype(bf16)
    out_ref[0] = dot(v, p, PLAIN).astype(bf16)
    peak_ref[0, 0] = peak
    total_ref[0, 0] = total


def attend(kept, got, bias, cos, sin, prow, pcol):
    _, heads, hd, t = kept.shape
    seqs, _, seq = prow.shape
    big = pl.BlockSpec((3, 1, hd, seq), lambda s, h: (0, h, 0, s))
    table = pl.BlockSpec((1, ROTARY // 2, seq), lambda s, h: (s, 0, 0))
    stat = pl.BlockSpec((1, 1, 1, seq), lambda s, h: (s, h, 0, 0))
    return pl.pallas_call(
        attend_kernel,
        grid=(seqs, heads),
        in_specs=[
            big,
            big,
            pl.BlockSpec((3, 1, hd, 1), lambda s, h: (0, h, 0, 0)),
            table,
            table,
            pl.BlockSpec((1, 1, seq), lambda s, h: (s, 0, 0)),
            pl.BlockSpec((1, seq, 1), lambda s, h: (s, 0, 0)),
        ],
        out_specs=[big, pl.BlockSpec((1, hd, seq), lambda s, h: (h, 0, s)), stat, stat],
        out_shape=[
            jax.ShapeDtypeStruct((3, heads, hd, t), bf16),
            jax.ShapeDtypeStruct((heads, hd, t), bf16),
            jax.ShapeDtypeStruct((seqs, heads, 1, seq), f32),
            jax.ShapeDtypeStruct((seqs, heads, 1, seq), f32),
        ],
        compiler_params=pltpu.CompilerParams(vmem_limit_bytes=32 * 1024 * 1024),
        cost_estimate=pl.CostEstimate(
            flops=4 * seqs * heads * seq * seq * hd,
            bytes_accessed=16 * 3 * heads * hd * t,
            transcendentals=seqs * heads * seq * seq,
        ),
    )(kept, got, bias, cos, sin, prow, pcol)


def attend_back_kernel(qkv_ref, dout_ref, peak_ref, total_ref, cos_ref, sin_ref, prow_ref, pcol_ref, out_ref):
    cos, sin = cos_ref[0], sin_ref[0]
    half = ROTARY // 2
    q, k, v = qkv_ref[0, 0], qkv_ref[1, 0], qkv_ref[2, 0]
    dout = dout_ref[0]
    scores = dot(k, q, FIRST) * score_scale
    scores = jnp.where(pcol_ref[0] <= prow_ref[0], scores, masked_score)
    p = jnp.exp(scores - peak_ref[0, 0]) / total_ref[0, 0]
    dp = dot(v, dout, FIRST)
    inner = jnp.sum(p * dp, axis=0, keepdims=True)
    ds = (p * (dp - inner)).astype(bf16)

    def back(x):
        a, b = x[:half], x[half:ROTARY]
        return jnp.concatenate([a * cos + b * sin, b * cos - a * sin, x[ROTARY:]], axis=0)

    out_ref[0, 0] = back(dot(k, ds, PLAIN) * score_scale).astype(bf16)
    out_ref[1, 0] = back(dot(q, ds, LAST) * score_scale).astype(bf16)
    out_ref[2, 0] = dot(dout, p.astype(bf16), LAST).astype(bf16)


def attend_back(qkv, dout, peak, total, cos, sin, prow, pcol):
    _, heads, hd, t = qkv.shape
    seqs, _, seq = prow.shape
    big = pl.BlockSpec((3, 1, hd, seq), lambda s, h: (0, h, 0, s))
    table = pl.BlockSpec((1, ROTARY // 2, seq), lambda s, h: (s, 0, 0))
    stat = pl.BlockSpec((1, 1, 1, seq), lambda s, h: (s, h, 0, 0))
    return pl.pallas_call(
        attend_back_kernel,
        grid=(seqs, heads),
        in_specs=[
            big,
            pl.BlockSpec((1, hd, seq), lambda s, h: (h, 0, s)),
            stat,
            stat,
            table,
            table,
            pl.BlockSpec((1, 1, seq), lambda s, h: (s, 0, 0)),
            pl.BlockSpec((1, seq, 1), lambda s, h: (s, 0, 0)),
        ],
        out_specs=big,
        out_shape=jax.ShapeDtypeStruct((3, heads, hd, t), bf16),
        compiler_params=pltpu.CompilerParams(vmem_limit_bytes=32 * 1024 * 1024),
        cost_estimate=pl.CostEstimate(
            flops=10 * seqs * heads * seq * seq * hd,
            bytes_accessed=16 * 3 * heads * hd * t,
            transcendentals=seqs * heads * seq * seq,
        ),
    )(qkv, dout, peak, total, cos, sin, prow, pcol)


def body(
    tokens,
    cotangent,
    span_order,
    w_qkv,
    w_out,
    w_up,
    w_down,
    norm_params,
    m_qkv,
    v_qkv,
    m_out,
    v_out,
    m_up,
    v_up,
    m_down,
    v_down,
    m_norm,
    v_norm,
):
    at = Plane()
    do = Order()
    reps = RepSum(do)
    width = tokens.shape[3]
    rows = tokens.shape[1]
    S, Y, nb = at.s_size, at.y_size, at.blocks
    blk = width // nb
    ffb = FF // nb
    heads = blk // HEAD_DIM
    seq = rows * at.ctx_size
    T = S * seq
    H = T // 2
    first = at.c == 0
    core = at.c.reshape(1)
    my_block = at.ctx * S + at.s
    halves = (slice(0, H), slice(H, T))
    seqs = (slice(0, S // 2), slice(S // 2, S))

    def pick(x, axis, which):
        return lax.dynamic_index_in_dim(x, which, axis, keepdims=False)

    def in_order(mine, theirs, axis):
        return jnp.stack([jnp.where(first, mine, theirs), jnp.where(first, theirs, mine)], axis=axis)

    x_rows = tokens.reshape(rows, width)
    xt = do(lambda x: x.T.reshape(Y, 2, S, blk, rows), x_rows)
    x_got = at.chip_exchange(
        None, lambda y, s: lax.dynamic_slice(xt, (y, 0, s, 0, 0), (1, 2, 1, blk, rows)).reshape(2, blk, rows)
    )

    def row_stats(x):
        x = x.astype(f32)
        mean = jnp.mean(x, axis=1)
        centred = x - mean[:, None]
        return jnp.stack([mean, lax.rsqrt(jnp.mean(centred * centred, axis=1) + eps_norm)])

    stats = do(row_stats, x_rows)
    st_got = at.chip_exchange(None, lambda y, s: stats)
    order = span_order.reshape(1, -1).astype(f32)
    orders = [(at.s, order)]
    for rs in range(1, S):
        orders.append((at.s ^ rs, lax.ppermute(order, "shard", [(i, i ^ rs) for i in range(S)])))

    def chip_rows(w, lead, unit, count):
        mine, theirs = do(lambda w: split_columns(w, core, lead, unit, count), w)
        return mine, at.core(theirs)

    wq_mine, wq_got = chip_rows(w_qkv, 0, S * blk, 3 * Y)

    norm_cols = norm_params.reshape(7, nb, blk).transpose(1, 2, 0)
    own_cols = pick(norm_cols, 0, my_block)
    other_cols = pick(norm_cols, 0, (at.ctx ^ 1) * S + at.s)
    pair_cols = jnp.concatenate([own_cols, other_cols], axis=0)
    bias = own_cols[:, 4:7].T.reshape(3, heads, HEAD_DIM, 1)

    def place(got, tail):
        buf = jnp.zeros((S, Y) + tail, got[0][2].dtype)
        for y, s, v in got:
            buf = lax.dynamic_update_slice(buf, v[None, None], (s, y) + (0,) * len(tail))
        return buf

    x_buf, st_buf = do(
        lambda x, st: (place(x, (2, blk, rows)), place(st, (2, rows))), x_got, st_got
    )
    x_other, st_other = at.core(x_buf), at.core(st_buf)
    cot = cotangent.reshape(2, rows // 2, width)
    cot0, cot1, _ = lax.optimization_barrier((cot[0], cot[1], x_buf))
    cot_parts = [at.gather(v[None], bool(k))[0] for k, v in enumerate((cot0, cot1))]
    wq = do(lambda a, b: jnp.concatenate([a, b], axis=0), wq_mine, wq_got)

    def first_norm(mine, theirs, st_mine, st_theirs, cols):
        x = in_order(mine, theirs, 2).transpose(3, 4, 0, 1, 2, 5).reshape(2, blk, T)
        st = in_order(st_mine, st_theirs, 2).transpose(3, 0, 1, 2, 4).reshape(2, T)
        x_own = pick(x, 0, at.c)
        x_pair = jnp.concatenate([x_own, pick(x, 0, 1 - at.c)], axis=0).astype(f32)
        xn = ((x_pair - st[0:1]) * st[1:2] * cols[:, 0:1] + cols[:, 1:2]).astype(bf16)
        return xn, x_own, st

    xn1, x_own, st = do(first_norm, x_buf, x_other, st_buf, st_other, pair_cols)
    mean1, inv1 = st[0:1], st[1:2]

    def split_send(p, flip):
        axis, step = at.steps(flip)[0]
        ax = {"y": 1, "s": 2}[axis]
        bit = (at.index(axis) // step) % 2
        send = lax.dynamic_slice_in_dim(p, (1 - bit) * step, step, ax)
        return lax.dynamic_slice_in_dim(p, bit * step, step, ax), at.along(send, axis, step)

    def scatter_rest(kept, got, flip):
        for axis, step in at.steps(flip)[1:]:
            ax = {"y": 1, "s": 2}[axis]
            bit = (at.index(axis) // step) % 2
            p = do(lambda a, b: (a.astype(f32) + b.astype(f32)).astype(bf16), kept, got)
            send = lax.dynamic_slice_in_dim(p, (1 - bit) * step, step, ax)
            kept, got = lax.dynamic_slice_in_dim(p, bit * step, step, ax), at.along(send, axis, step)
        return kept[:, 0, 0], got[:, 0, 0]

    flying = []
    for k in range(2):
        p = do(lambda w, x: dot(w, x, FIRST).astype(bf16), wq, xn1[:, halves[k]])
        flying.append(split_send(p.reshape(3, Y, S, blk, H), bool(k)))

    wo_mine, wo_got = chip_rows(w_out, 0, S * blk, Y)
    wg_mine, wg_got = chip_rows(w_up, 0, S * ffb, Y)
    wu_mine, wu_got = chip_rows(w_up, Y, S * ffb, Y)
    wo_own = do(lambda w: w.astype(bf16), w_out)
    wd_own = do(lambda w: w.astype(bf16), w_down)
    wo = do(lambda a, b: jnp.concatenate([a, b], axis=0), wo_mine, wo_got)
    wg = do(lambda a, b: jnp.concatenate([a, b], axis=0), wg_mine, wg_got)
    wu = do(lambda a, b: jnp.concatenate([a, b], axis=0), wu_mine, wu_got)

    def positions(orders):
        order_all = jnp.zeros((S, order.shape[1]), f32)
        for s, o in orders:
            order_all = lax.dynamic_update_slice(order_all, o, (s, 0))
        span = rows // 2
        pos = order_all[:, :, None] * span + jnp.arange(span, dtype=f32)[None, None, :]
        pos = pos.reshape(S, seq)
        prow, pcol = pos.reshape(S, 1, seq), pos.reshape(S, seq, 1)
        exponent = jnp.arange(ROTARY // 2, dtype=f32)
        inverse = 10000.0 ** (-2.0 * exponent / ROTARY)
        angles = prow * inverse[None, :, None]
        return jnp.cos(angles), jnp.sin(angles), prow, pcol

    cos, sin, prow, pcol = do(positions, orders)
    flying = [scatter_rest(*flying[k], bool(k)) for k in range(2)]

    qkvs, attns, attn_got, peaks, totals = [], [], [], [], []
    for k in range(2):
        sq = seqs[k]
        shape = (3, heads, HEAD_DIM, H)
        qkv, attn, peak, total = do(
            attend, flying[k][0].reshape(shape), flying[k][1].reshape(shape), bias, cos[sq], sin[sq], prow[sq], pcol[sq]
        )
        qkvs.append(qkv)
        attns.append(attn.reshape(blk, H))
        attn_got.append(at.core(attns[k]))
        peaks.append(peak)
        totals.append(total)

    flying = []
    for k in range(2):
        p = do(
            lambda w, a, b: dot(w, jnp.concatenate([a, b], axis=0), FIRST).astype(bf16), wo, attns[k], attn_got[k]
        )
        flying.append(split_send(p.reshape(1, Y, S, blk, H), bool(k)))
    flying = [scatter_rest(*flying[k], bool(k)) for k in range(2)]

    def residual(x, a0, b0, a1, b1):
        a, b = jnp.concatenate([a0[0], a1[0]], axis=1), jnp.concatenate([b0[0], b1[0]], axis=1)
        hidden = x.astype(f32) + (a.astype(f32) + b.astype(f32))
        local_mean = jnp.mean(hidden, axis=0, keepdims=True)
        dev = hidden - local_mean
        return hidden, jnp.concatenate([local_mean, jnp.sum(dev * dev, axis=0, keepdims=True)], axis=0)

    hidden, moments = do(residual, x_own, *flying[0], *flying[1])
    count = blk
    for axis, step in at.steps(False) + [("core", 1)]:
        other = at.core(moments) if axis == "core" else at.along(moments, axis, step)
        gap = moments[0:1] - other[0:1]
        moments = jnp.concatenate(
            [0.5 * (moments[0:1] + other[0:1]), moments[1:2] + other[1:2] + gap * gap * (count / 2.0)], axis=0
        )
        count *= 2

    def second_norm(hidden, moments, cols):
        inv2 = lax.rsqrt(moments[1:2] / width + eps_norm)
        z2 = (hidden - moments[0:1]) * inv2
        return (z2 * cols[:, 2:3] + cols[:, 3:4]).astype(bf16), z2, inv2

    xn2_own, z2, inv2 = do(second_norm, hidden, moments, own_cols)
    xn2 = do(lambda a, b: jnp.concatenate([a, b], axis=0), xn2_own, at.core(xn2_own))

    flying = []
    for k, w in enumerate((wg, wu)):
        p = do(lambda w, x: dot(w, x, FIRST).astype(bf16), w, xn2)
        flying.append(split_send(p.reshape(1, Y, S, ffb, T), bool(k)))

    cot_c = do(lambda a, b: jnp.stack([a, b], axis=2), *cot_parts)

    def all_cotangents(mine, theirs):
        return in_order(mine, theirs, 2).transpose(1, 0, 2, 3, 4, 5).reshape(T, width)

    cot_all = do(all_cotangents, cot_c, at.core(cot_c))
    grad_act = do(lambda w, c: dot(w, c, LAST), wd_own, cot_all)
    cot_cols = do(lambda c: lax.dynamic_slice_in_dim(c, my_block * blk, blk, 1).T, cot_all)
    flying = [scatter_rest(*flying[k], bool(k)) for k in range(2)]

    def gated(ga, gb, ua, ub, grad_act):
        gate = ga[0].astype(f32) + gb[0].astype(f32)
        up = ua[0].astype(f32) + ub[0].astype(f32)
        sig = jax.nn.sigmoid(gate)
        silu = gate * sig
        grad_gate = grad_act * up * sig * (1.0 + gate * (1.0 - sig))
        return grad_gate.astype(bf16), (grad_act * silu).astype(bf16), (silu * up).astype(bf16)

    ggate, gup, act = do(gated, *flying[0], *flying[1], grad_act)

    def gather_steps(x, hold=None):
        parts = [x[:, halves[k]][None, None] for k in range(2)]
        n = len(at.steps(False))
        state = {"parts": parts, "got": None}

        def start(i):
            got = []
            for k in range(2):
                axis, step = list(reversed(at.steps(bool(k))))[i]
                got.append((axis, step, at.along(state["parts"][k], axis, step)))
            state["got"] = got

        def finish():
            def join(parts, got):
                out = []
                for k in range(2):
                    axis, step, _ = state["got"][k]
                    ax = {"y": 0, "s": 1}[axis]
                    low = (at.index(axis) // step) % 2 == 0
                    a, b = parts[k], got[k]
                    out.append(jnp.concatenate([jnp.where(low, a, b), jnp.where(low, b, a)], ax))
                return out

            state["parts"] = do(join, state["parts"], [g[2] for g in state["got"]])

        def result():
            return jnp.concatenate(state["parts"], axis=3)

        return n, start, finish, result

    def cut(g, n):
        r = g.shape[0] // n
        return [g[i * r : (i + 1) * r] for i in range(n)]

    n, start, finish, gate_all = gather_steps(ggate)
    start(0)
    g_down = do(lambda a, c: dot(a, c, PLAIN).astype(bf16), act, cot_all)
    for i, g in enumerate(cut(g_down, 4)):
        reps.push(("down", i), g)
    reps.tick()
    out_part = do(lambda w, a: dot(w, a, FIRST).astype(bf16), wd_own, act).reshape(Y, 2, S, blk, T)
    out_theirs = at.core(pick(out_part, 1, 1 - at.c))
    finish()
    for i in range(1, n):
        start(i)
        reps.tick()
        if i < n - 1:
            finish()
    n, start_up, finish_up, up_all = gather_steps(gup)
    out_sum = do(
        lambda a, b: (a.astype(f32) + b.astype(f32)).astype(bf16), pick(out_part, 1, at.c), out_theirs
    )
    finish()
    start_up(0)
    ggate_all = do(lambda x: x.reshape(Y * S * ffb, T), gate_all())
    reps.tick()
    part_gate = do(lambda w, g: dot(w, g, PLAIN), wg, ggate_all)
    g_gate = do(lambda x, g: dot(x, g, LAST).astype(bf16), xn2, ggate_all)
    for i, g in enumerate(reversed(cut(g_gate, 4))):
        reps.push(("gate", 3 - i), g)
    finish_up()
    for i in range(1, n):
        start_up(i)
        reps.tick()
        finish_up()
    gup_all = do(lambda x: x.reshape(Y * S * ffb, T), up_all())
    part = do(lambda w, g, p: dot(w, g, PLAIN) + p, wu, gup_all, part_gate)
    part_theirs = at.core(part[blk:])
    reps.tick()
    gxn2 = do(lambda a, b: a + b, part[:blk], part_theirs)

    def norm_sums(grad, z, gain):
        e = grad * gain
        return jnp.concatenate(
            [jnp.sum(e, axis=0, keepdims=True), jnp.sum(e * z, axis=0, keepdims=True)], axis=0
        )

    def norm_back(grad, z, scale, gain, sums):
        e = grad * gain
        return scale * (e - sums[0:1] / width - z * (sums[1:2] / width))

    sums = at.sum_all(do(norm_sums, gxn2, z2, own_cols[:, 2:3]))
    g_up = do(lambda x, g: dot(x, g, LAST).astype(bf16), xn2, gup_all)
    for i, g in enumerate(reversed(cut(g_up, 4))):
        reps.push(("up", 3 - i), g)

    def branch(cot, grad, z, scale, gain, sums):
        grad_hidden = cot.astype(f32) + norm_back(grad, z, scale, gain, sums)
        return grad_hidden.astype(bf16), grad_hidden

    grad_branch, grad_hidden = do(branch, cot_cols, gxn2, z2, inv2, own_cols[:, 2:3], sums)
    n, start, finish, branch_all = gather_steps(grad_branch)
    for i in range(n):
        start(i)
        if i == 0:
            reps.tick()
        finish()
    gbr_c = do(lambda x: x, branch_all())
    gbr_o = at.core(gbr_c)
    gbr = do(lambda a, b: in_order(a, b, 1).reshape(width, T), gbr_c, gbr_o)
    grad_attn = do(lambda w, g: dot(w, g, PLAIN).astype(bf16), wo_own, gbr)

    gqkvs = []
    for k in range(2):
        sq = seqs[k]
        gqkvs.append(
            do(
                attend_back,
                qkvs[k],
                grad_attn[:, halves[k]].reshape(heads, HEAD_DIM, H),
                peaks[k],
                totals[k],
                cos[sq],
                sin[sq],
                prow[sq],
                pcol[sq],
            ).reshape(3, blk, H)
        )
    gqkv_own = jnp.concatenate(gqkvs, axis=2)
    part = None
    for third in (2, 1, 0):
        n, start, finish, third_all = gather_steps(gqkv_own[third])
        start(0)
        if third == 2:
            attn = jnp.concatenate(attns, axis=1)
            g_out = do(lambda a, g: dot(a, g, LAST).astype(bf16), attn, gbr)
            reps.push(("out", 0), g_out)
        reps.tick()
        finish()
        for i in range(1, n):
            start(i)
            reps.tick()
            finish()
        g_all = do(lambda x: x.reshape(Y * S * blk, T), third_all())
        cols = slice(third * Y * S * blk, (third + 1) * Y * S * blk)
        if part is None:
            part = do(lambda w, g: dot(w, g, PLAIN), wq[:, cols], g_all)
        else:
            part = do(lambda w, g, p: dot(w, g, PLAIN) + p, wq[:, cols], g_all, part)
        g = do(lambda x, g: dot(x, g, LAST).astype(bf16), xn1, g_all)
        for i, g in enumerate(reversed(cut(g, 2))):
            reps.push(("qkv", third, 1 - i), g)

    part_theirs = at.core(part[blk:])
    reps.tick()
    gxn1 = do(lambda a, b: a + b, part[:blk], part_theirs)

    def first_sums(x, st, grad, gain):
        z1 = (x.astype(f32) - st[0:1]) * st[1:2]
        return norm_sums(grad, z1, gain), z1

    sums, z1 = do(first_sums, x_own, st, gxn1, own_cols[:, 0:1])
    sums = at.sum_all(sums)

    def small_grads(gxn1, z1, gxn2, z2, gqkv):
        return jnp.concatenate(
            [
                jnp.sum(gxn1 * z1, axis=1)[None],
                jnp.sum(gxn1, axis=1)[None],
                jnp.sum(gxn2 * z2, axis=1)[None],
                jnp.sum(gxn2, axis=1)[None],
                jnp.sum(gqkv.astype(f32), axis=2),
            ],
            axis=0,
        )

    small = do(small_grads, gxn1, z1, gxn2, z2, gqkv_own)
    n_rep = lax.axis_size("rep")
    step = 1
    while step < n_rep:
        small = small + lax.ppermute(small, "rep", [(i, i ^ step) for i in range(n_rep)])
        step *= 2
    small_got = at.chip_exchange(None, lambda y, s: small)
    reps.tick()
    input_grad = do(
        lambda h, grad, z, scale, gain, sums: h + norm_back(grad, z, scale, gain, sums),
        grad_hidden,
        gxn1,
        z1,
        st[1:2],
        own_cols[:, 0:1],
        sums,
    )

    def to_rows(cols):
        split = cols.reshape(blk, S, Y, 2, rows).transpose(1, 2, 3, 0, 4)
        theirs = at.core(pick(split, 2, 1 - at.c))
        both = in_order(pick(split, 2, at.c), theirs, 2)
        return at.chip_exchange(
            None, lambda y, s: lax.dynamic_slice(both, (s, y, 0, 0, 0), (1, 1, 2, blk, rows)).reshape(2, blk, rows)
        )

    def rows_done(got):
        buf = jnp.zeros((Y, 2, S, blk, rows), got[0][2].dtype)
        for y, s, v in got:
            buf = lax.dynamic_update_slice(buf, v[None, :, None], (y, 0, s, 0, 0))
        return buf.reshape(width, rows).T

    in_got = to_rows(input_grad)

    flying = [split_send(out_sum[None][..., halves[k]], bool(k)) for k in range(2)]
    reps.tick()
    flying = [scatter_rest(*flying[k], bool(k)) for k in range(2)]
    reps.tick()

    def output(hidden, a0, b0, a1, b1):
        a, b = jnp.concatenate([a0[0], a1[0]], axis=1), jnp.concatenate([b0[0], b1[0]], axis=1)
        return (hidden + (a.astype(f32) + b.astype(f32))).astype(bf16)

    out_got = to_rows(do(output, hidden, *flying[0], *flying[1]))
    reps.tick()

    down = [reps.drain(("down", i)) for i in range(4)]
    md, vd, wd_new = do(
        lambda g, *a: adam_update(*a, g.astype(f32), 0.02, weight_decay),
        jnp.concatenate(down, axis=0),
        w_down,
        m_down,
        v_down,
    )
    gates = [reps.drain(("gate", i)) for i in (3, 2, 1, 0)][::-1]
    ups = [reps.drain(("up", i)) for i in (3, 2, 1, 0)][::-1]
    g_up_all = do(
        lambda a, b: jnp.concatenate([jnp.concatenate(a, axis=0), jnp.concatenate(b, axis=0)], axis=1), gates, ups
    )
    r = g_up_all.shape[0] // 2
    got = at.core(g_up_all[r:])
    reps.tick()
    mu, vu, wu_new = do(
        lambda w, m, v, a, b: adam_columns(w, m, v, a, b, core, S * ffb, 0.03), w_up, m_up, v_up, g_up_all[:r], got
    )
    g_out = reps.drain(("out", 0))
    mo, vo, wo_new = do(
        lambda g, *a: adam_update(*a, g.astype(f32), 0.2, weight_decay), g_out, w_out, m_out, v_out
    )
    block_output = do(rows_done, out_got)
    input_rows = do(rows_done, in_got)
    buf = jnp.zeros((7, Y, S, blk), f32)
    for y, s, v in small_got:
        buf = lax.dynamic_update_slice(buf, v.reshape(7, 1, 1, blk), (0, y, s, 0))
    norm_grad = in_order(buf, at.core(buf), 2).reshape(7, width)
    mn, vn, wn = do(lambda *a: adam_update(*a, 0.3, 0.0), norm_params, m_norm, v_norm, norm_grad)

    theirs = [reps.drain(("qkv", third, 1)) for third in (2, 1, 0)][::-1]
    mine = [reps.drain(("qkv", third, 0)) for third in (2, 1, 0)][::-1]
    got = at.core(jnp.concatenate(theirs, axis=1))
    mq, vq, wq_new = do(
        lambda w, m, v, a, b: adam_columns(w, m, v, a, b, core, S * blk, 0.03),
        w_qkv,
        m_qkv,
        v_qkv,
        jnp.concatenate(mine, axis=1),
        got,
    )
    return (
        block_output.reshape(tokens.shape),
        input_rows.reshape(tokens.shape),
        mq,
        vq,
        wq_new,
        mo,
        vo,
        wo_new,
        mu,
        vu,
        wu_new,
        md,
        vd,
        wd_new,
        mn,
        vn,
        wn,
    )


def solution(mesh):
    tok = P("rep", "ctx", "shard", None)
    row = P(("ctx", "shard"), None)
    placed = (tok, tok, P("rep", "shard", None)) + (row,) * 4 + (P(),) + (row,) * 8 + (P(), P())
    return jax.shard_map(
        body,
        mesh=mesh,
        in_specs=placed,
        out_specs=(tok, tok) + (row,) * 12 + (P(),) * 3,
        check_vma=False,
    )
```

time: 1280 us -> 1080 us (0.84)
  waiting for transfers between devices: 606 us -> 418 us
  local copies, waits for them, and re-layouts: 258 us -> 130 us
  starting transfers between devices: 130 us -> 236 us
  Pallas kernels: 18.5 us -> 65.9 us
  other arithmetic: 183 us -> 150 us
    ppermute x33 -> x57, waiting for transfers between devices: 353 us -> 207 us  [the longest x19 184 us: tick(): self.three = (name, total, lax.ppermute(total, 'rep', [(1, 0), (2, 3)]))]
    unnamed x180 -> x214, local copies, waits for them, and re-layouts: 138 us -> 37.7 us
    ppermute x19 -> x25, waiting for transfers between devices: 168 us -> 76.4 us  [along(): lax.ppermute(x, 'ctx', [(i, i ^ 2 * step) for i in range(self.ctx_size)])]
    ppermute x33 -> x57, starting transfers between devices: 60.6 us -> 139 us  [the longest x19 94.9 us: tick(): self.one = (name, g, lax.ppermute(g, 'rep', [(0, 1), (3, 2)]))]
    ppermute x19 -> x25, waiting for transfers between devices: 70.5 us -> 126 us  [along(): return lax.ppermute(x, 'shard', [(i, i ^ step) for i in range(self.s_size)])]
    pallas_call x0 -> x6, Pallas kernels: none -> 47.4 us  [the longest x2 41.6 us: adam_columns(): pl.pallas_call(functools.partial(adam_kernel, rate), grid_spec=pltpu.Pref...]
    sub x5 -> x3, other arithmetic: 56.2 us -> 15.3 us  [adam_update(): weight - step_rate * (first_hat / (jnp.sqrt(second_hat) + adam_eps) + dec...]
    concatenate x8 -> x28, other arithmetic: 4.2 us -> 33.8 us  [the longest x1 21.7 us: body(): jnp.concatenate([jnp.concatenate(a, axis=0), jnp.concatenate(b, axis=0)],...]
  transfers between devices with their start and end apart: 110 -> 147, of which waited for: 46 -> 55; matrix products, arithmetic and copies ran while one was open for 35% -> 26% of each run, Pallas kernels for 1% -> 5%
where the time goes in v2:
time: 1080 us; the launch traced here: 1070 us
  waiting for transfers between devices  418 us (39%)
  starting transfers between devices  236 us (22%)
  other arithmetic  150 us (14%)
  local copies, waits for them, and re-layouts  130 us (12%)
  Pallas kernels  65.9 us (6%)
  matrix products  65.7 us (6%)
    ppermute x19, waiting for transfers between devices, tick(): self.three = (name, total, lax.ppermute(total, 'rep', [(1, 0), (2, 3)]))  184 us
    ppermute x25, waiting for transfers between devices, along(): return lax.ppermute(x, 'shard', [(i, i ^ step) for i in range(self.s_size)])  126 us
    ppermute x19, starting transfers between devices, tick(): self.one = (name, g, lax.ppermute(g, 'rep', [(0, 1), (3, 2)]))  94.9 us
    ppermute x25, waiting for transfers between devices, along(): lax.ppermute(x, 'ctx', [(i, i ^ 2 * step) for i in range(self.ctx_size)])  76.4 us
    dot_general x21, matrix products, dot(): return lax.dot_general(a, b, dims, preferred_element_type=f32)  65.7 us
    pallas_call x2, Pallas kernels, adam_columns(): pl.pallas_call(functools.partial(adam_kernel, rate), grid_spec=pltpu.Pref...  41.6 us
    convert_element_type x38, other arithmetic, add(): lax.reduce_precision(a.astype(f32) + b.astype(f32), 8, 7).astype(bf16)  38.7 us
    unnamed x214, local copies, waits for them, and re-layouts  37.7 us
  transfers between devices with their start and end apart: 147, of which 55 were waited for; matrix products, arithmetic and copies ran while one was open for 26% of the time, Pallas kernels for 5%

profile of v2, /device:TPU:0, one launch (start us, length us, event | category | flops | bytes accessed | tf_op | source)
XLA Modules:
  0.0 1070.9 jit_solution(1585379503494656997)
XLA Ops:
  34.4 5.6 convolution_convert_fusion.5
  40.0 5.5 convolution_convert_fusion.4
  59.2 4.8 convert_element_type.567
  80.6 21.7 %collective-permute-done.10 = bf16[3,2,1,256,512]{4,3,0,2,1:T(8,128)(2,1)} collective-permute-done((bf16[3,2,1,256,512]{4,3,0,2,1:T(8,128)(2,1)}, bf16[3,2,1,256,512]{4,3,0,2,1:T(8,128)(2,1)}, u32[]{:S(2)}, u32[]{:S(2)}) %collective-permute-start.10) | collective-permute-done | bytes 1572896 | tf_op jit(solution)/shard_map/ppermute | solution.py:62
  112.0 14.1 %collective-permute-done.14 = bf16[3,1,1,256,512]{4,3,0,2,1:T(8,128)(2,1)} collective-permute-done((bf16[3,1,1,256,512]{4,3,0,2,1:T(8,128)(2,1)}, bf16[3,1,1,256,512]{4,3,0,2,1:T(8,128)(2,1)}, u32[]{:S(2)}, u32[]{:S(2)}) %collective-permute-start.14) | collective-permute-done | bytes 786464 | tf_op jit(solution)/shard_map/ppermute | solution.py:61
  143.3 9.7 collective-permute-done.18
  187.9 5.5 convolution_convert_fusion
  208.8 4.8 fusion.84
  213.6 6.4 copy.156
  221.8 41.4 %collective-permute-done.27 = bf16[1,2,1,704,1024]{4,3,2,1,0:T(8,128)(2,1)} collective-permute-done((bf16[1,2,1,704,1024]{4,3,2,1,0:T(8,128)(2,1)}, bf16[1,2,1,704,1024]{4,3,2,1,0:T(8,128)(2,1)}, u32[]{:S(2)}, u32[]{:S(2)}) %collective-permute-start.27) | collective-permute-done | bytes 2883616 | tf_op jit(solution)/shard_map/ppermute | solution.py:62
  274.9 31.1 %collective-permute-done.35 = bf16[1,1,1,704,1024]{4,3,2,1,0:T(8,128)(2,1)S(1)} collective-permute-done((bf16[1,1,1,704,1024]{4,3,2,1,0:T(8,128)(2,1)S(1)}, bf16[1,1,1,704,1024]{4,3,2,1,0:T(8,128)(2,1)S(1)}, u32[]{:S(2)}, u32[]{:S(2)}) %collective-permute-start.35) | collective-permute-done | bytes 1441824 | tf_op jit(solution)/shard_map/ppermute | solution.py:62
  338.1 4.9 collective-permute-done.37
  350.2 15.8 %collective-permute-done.44 = bf16[1,2,704,512]{3,2,1,0:T(8,128)(2,1)} collective-permute-done((bf16[1,2,704,512]{3,2,1,0:T(8,128)(2,1)}, bf16[1,2,704,512]{3,2,1,0:T(8,128)(2,1)}, u32[]{:S(2)}, u32[]{:S(2)}) %collective-permute-start.44) | collective-permute-done | bytes 1441824 | tf_op jit(solution)/shard_map/ppermute | solution.py:61
  384.5 4.5 convolution_convert_fusion.3
  397.1 12.4 %collective-permute-start.52 = (bf16[176,2048]{1,0:T(8,128)(2,1)}, bf16[176,2048]{1,0:T(8,128)(2,1)S(1)}, u32[]{:S(2)}, u32[]{:S(2)}) collective-permute-start(bf16[176,2048]{1,0:T(8,128)(2,1)} %get-tuple-element.590), channel_id=1, source_target_pairs={{0,8},{24,16},{1,9},{25,17},{2,10},{26,18},{3,11},{27,19},{4,12},{... | collective-permute-start | bytes 2162696 | tf_op jit(solution)/shard_map/ppermute | solution.py:169
  422.3 5.0 convolution_add_fusion
  438.9 9.3 collective-permute-start.59
  454.2 8.0 collective-permute-done.59
  473.3 7.0 collective-permute-start.66
  485.6 17.9 %collective-permute-done.117 = bf16[176,2048]{1,0:T(8,128)(2,1)S(1)} collective-permute-done((bf16[176,2048]{1,0:T(8,128)(2,1)S(1)}, bf16[176,2048]{1,0:T(8,128)(2,1)S(1)}, u32[]{:S(2)}, u32[]{:S(2)}) %collective-permute-start.117) | collective-permute-done | bytes 720928 | tf_op jit(solution)/shard_map/ppermute | solution.py:160
  503.6 10.6 collective-permute-done.118
  517.2 11.8 %collective-permute-done.119 = bf16[176,2048]{1,0:T(8,128)(2,1)S(1)} collective-permute-done((bf16[176,2048]{1,0:T(8,128)(2,1)S(1)}, bf16[176,2048]{1,0:T(8,128)(2,1)S(1)}, u32[]{:S(2)}, u32[]{:S(2)}) %collective-permute-start.119) | collective-permute-done | bytes 720928 | tf_op jit(solution)/shard_map/ppermute | solution.py:160
  538.6 5.3 shard_map.311
  545.2 5.1 shard_map.312
  550.3 4.6 convolution_convert_fusion.8
  572.0 15.4 %collective-permute-done.111 = bf16[128,2816]{1,0:T(8,128)(2,1)S(1)} collective-permute-done((bf16[128,2816]{1,0:T(8,128)(2,1)S(1)}, bf16[128,2816]{1,0:T(8,128)(2,1)S(1)}, u32[]{:S(2)}, u32[]{:S(2)}) %collective-permute-start.111) | collective-permute-done | bytes 720928 | tf_op jit(solution)/shard_map/ppermute | solution.py:160
  589.4 7.5 collective-permute-done.69
  610.3 8.6 collective-permute-start.75
  620.5 11.7 %collective-permute-done.110 = bf16[128,2816]{1,0:T(8,128)(2,1)S(1)} collective-permute-done((bf16[128,2816]{1,0:T(8,128)(2,1)S(1)}, bf16[128,2816]{1,0:T(8,128)(2,1)S(1)}, u32[]{:S(2)}, u32[]{:S(2)}) %collective-permute-start.110) | collective-permute-done | bytes 720928 | tf_op jit(solution)/shard_map/ppermute | solution.py:160
  636.3 7.7 collective-permute-done.85
  644.0 13.0 %collective-permute-start.74 = (bf16[128,2816]{1,0:T(8,128)(2,1)S(1)}, bf16[128,2816]{1,0:T(8,128)(2,1)S(1)}, u32[]{:S(2)}, u32[]{:S(2)}) collective-permute-start(bf16[128,2816]{1,0:T(8,128)(2,1)S(1)} %copy-done.50), channel_id=1, source_target_pairs={{0,8},{24,16},{1,9},{25,17},{2,10},{26,18},{3,11},{27,19},{4,12},{... | collective-permute-start | bytes 2162696 | tf_op jit(solution)/shard_map/ppermute | solution.py:169
  663.9 6.4 collective-permute-done.109
  681.5 27.5 %collective-permute-done.108 = bf16[128,2816]{1,0:T(8,128)(2,1)S(1)} collective-permute-done((bf16[128,2816]{1,0:T(8,128)(2,1)S(1)}, bf16[128,2816]{1,0:T(8,128)(2,1)S(1)}, u32[]{:S(2)}, u32[]{:S(2)}) %collective-permute-start.108) | collective-permute-done | bytes 720928 | tf_op jit(solution)/shard_map/ppermute | solution.py:160
  715.9 7.0 collective-permute-done.91
  736.4 16.2 %collective-permute-start.132 = (f32[7,256]{1,0:T(8,128)S(1)}, f32[7,256]{1,0:T(8,128)S(1)}, u32[]{:S(2)}, u32[]{:S(2)}) collective-permute-start(f32[7,256]{1,0:T(8,128)S(1)} %concatenate.239), channel_id=1, source_target_pairs={{0,8},{8,0},{16,24},{24,16},{1,9},{9,1},{17,25},{25,17},{2,10},{10... | collective-permute-start | bytes 21512 | tf_op jit(solution)/shard_map/ppermute | solution.py:730
  776.8 10.3 collective-permute-done.73
  797.7 9.8 collective-permute-done.112
  864.3 9.8 collective-permute-start.129
  881.2 10.7 %multiply_subtract_fusion = (f32[704,2048]{1,0:T(8,128)}, f32[704,2048]{1,0:T(8,128)}, f32[704,2048]{1,0:T(8,128)}) fusion(f32[704,2048]{1,0:T(8,128)S(1)} %bitcast.402, bf16[704,2048]{1,0:T(8,128)(2,1)S(1)} %copy-done.20, f32[704,2048]{1,0:T(8,128)} %param.33, f32[704,2048]{1,0:T(8,128)} %param.32), kind=kLoop, calls=%fused_computation.7 | loop fusion | flops 23068672 | bytes 37486592 | tf_op jit(solution)/shard_map/sub | solution.py:39
  892.0 21.7 %maximum_maximum_fusion.2 = bf16[512,5632]{1,0:T(8,128)(2,1)S(1)} fusion(bf16[128,2816]{1,0:T(8,128)(2,1)S(1)} %copy-done.45, bf16[128,2816]{1,0:T(8,128)(2,1)S(1)} %copy-done.46, bf16[128,2816]{1,0:T(8,128)(2,1)S(1)} %copy-done.47, bf16[128,2816]{1,0:T(8,128)(2,1)S(1)} %copy-done.48, bf16[128,2816]{1,0:T(8,128)(2,1)S(1)} %copy-done.41, ...), kind=kLoop, calls=%fused_computation.6 | loop fusion | flops 46137344 | bytes 11534336 | tf_op jit(solution)/shard_map/concatenate | solution.py:783
  923.2 8.1 collective-permute-done.145
  932.0 17.8 %collective-permute-done.142 = bf16[256,1024]{1,0:T(8,128)(2,1)S(1)} collective-permute-done((bf16[256,1024]{1,0:T(8,128)(2,1)S(1)}, bf16[256,1024]{1,0:T(8,128)(2,1)S(1)}, u32[]{:S(2)}, u32[]{:S(2)}) %collective-permute-start.142) | collective-permute-done | bytes 524320 | tf_op jit(solution)/shard_map/ppermute | solution.py:160
  955.4 15.9 %collective-permute-done.144 = bf16[256,1024]{1,0:T(8,128)(2,1)S(1)} collective-permute-done((bf16[256,1024]{1,0:T(8,128)(2,1)S(1)}, bf16[256,1024]{1,0:T(8,128)(2,1)S(1)}, u32[]{:S(2)}, u32[]{:S(2)}) %collective-permute-start.144) | collective-permute-done | bytes 524320 | tf_op jit(solution)/shard_map/ppermute | solution.py:160
  972.1 9.3 collective-permute-done.141
  985.4 10.7 collective-permute-done.143
  998.7 11.1 %collective-permute-done.140 = bf16[256,1024]{1,0:T(8,128)(2,1)S(1)} collective-permute-done((bf16[256,1024]{1,0:T(8,128)(2,1)S(1)}, bf16[256,1024]{1,0:T(8,128)(2,1)S(1)}, u32[]{:S(2)}, u32[]{:S(2)}) %collective-permute-start.140) | collective-permute-done | bytes 524320 | tf_op jit(solution)/shard_map/ppermute | solution.py:160
  1010.1 28.0 %shard_map.313 = (f32[256,11264]{1,0:T(8,128)}, f32[256,11264]{1,0:T(8,128)}, f32[256,11264]{1,0:T(8,128)}) custom-call(s32[1]{0:T(128)} %bitcast.11.core_ref, f32[256,11264]{1,0:T(8,128)S(1)} %bitcast.385, f32[256,11264]{1,0:T(8,128)} %m_ref, f32[256,11264]{1,0:T(8,128)} %v_ref, bf16[256,5632]{1,0:T(8,128)(2,1)S(1)} %get-tuple-element.772.mine_ref, ...), custom_call_target="tpu_custom_call" | custom-call | flops 57671680 | bytes 80740352 | tf_op jit(solution)/shard_map/pallas_call | solution.py:219
  1056.9 13.6 %shard_map.314 = (f32[256,6144]{1,0:T(8,128)}, f32[256,6144]{1,0:T(8,128)}, f32[256,6144]{1,0:T(8,128)}) custom-call(s32[1]{0:T(128)} %bitcast.11.core_ref, f32[256,6144]{1,0:T(8,128)S(1)} %copy-done.1, f32[256,6144]{1,0:T(8,128)S(1)} %copy-done.4, f32[256,6144]{1,0:T(8,128)S(1)} %copy-done.5, bf16[256,3072]{1,0:T(8,128)(2,1)S(1)} %pad_maximum_fusion.5.mine_ref, ...), custom_call_target="tpu_custom_call" | custom-call | flops 31457280 | bytes 44040192 | tf_op jit(solution)/shard_map/pallas_call | solution.py:219
  (807 shorter events, 496.0 us)
Async XLA Ops:
  49.1 29.6 %collective-permute-start.11 = (f32[1,8]{1,0:T(1,128)}, f32[1,8]{1,0:T(1,128)}, u32[]{:S(2)}, u32[]{:S(2)}) collective-permute-start(f32[1,8]{1,0:T(1,128)} %convert_bitcast_fusion), channel_id=1, source_target_pairs={{0,1},{1,0},{2,3},{3,2},{4,5},{5,4},{6,7},{7,6},{8,9},{9,8},{10,11... | collective-permute-start | bytes 104 | tf_op jit(solution)/shard_map/ppermute | solution.py:403
  65.5 36.8 %collective-permute-start.10 = (bf16[3,2,1,256,512]{4,3,0,2,1:T(8,128)(2,1)}, bf16[3,2,1,256,512]{4,3,0,2,1:T(8,128)(2,1)}, u32[]{:S(2)}, u32[]{:S(2)}) collective-permute-start(bf16[3,2,1,256,512]{4,3,0,2,1:T(8,128)(2,1)} %copy.179), channel_id=1, source_target_pairs={{0,1},{1,0},{2,3},{3,2},{4,5},{5,4},{6,7},{7,6},{8,9},{9,8},{10,11... | collective-permute-start | bytes 4718600 | tf_op jit(solution)/shard_map/ppermute | solution.py:62
  70.1 36.8 %collective-permute-start.15 = (bf16[3,1,2,256,512]{4,3,0,2,1:T(8,128)(2,1)}, bf16[3,1,2,256,512]{4,3,0,2,1:T(8,128)(2,1)}, u32[]{:S(2)}, u32[]{:S(2)}) collective-permute-start(bf16[3,1,2,256,512]{4,3,0,2,1:T(8,128)(2,1)} %copy.181), channel_id=1, source_target_pairs={{0,4},{2,6},{4,0},{6,2},{1,5},{3,7},{5,1},{7,3},{8,12},{10,14},{12... | collective-permute-start | bytes 4718600 | tf_op jit(solution)/shard_map/ppermute | solution.py:61
  198.1 65.2 %collective-permute-start.27 = (bf16[1,2,1,704,1024]{4,3,2,1,0:T(8,128)(2,1)}, bf16[1,2,1,704,1024]{4,3,2,1,0:T(8,128)(2,1)}, u32[]{:S(2)}, u32[]{:S(2)}) collective-permute-start(bf16[1,2,1,704,1024]{4,3,2,1,0:T(8,128)(2,1)} %get-tuple-element.859), channel_id=1, source_target_pairs={{0,1},{1,0},{2,3},{3,2},{4,5},{5,4},{6,7},{7,6},{8,9},{9,8},{10,11... | collective-permute-start | bytes 8650760 | tf_op jit(solution)/shard_map/ppermute | solution.py:62
  201.9 65.7 %collective-permute-start.34 = (bf16[1,1,2,704,1024]{4,3,2,1,0:T(8,128)(2,1)}, bf16[1,1,2,704,1024]{4,3,2,1,0:T(8,128)(2,1)}, u32[]{:S(2)}, u32[]{:S(2)}) collective-permute-start(bf16[1,1,2,704,1024]{4,3,2,1,0:T(8,128)(2,1)} %get-tuple-element.857), channel_id=1, source_target_pairs={{0,4},{2,6},{4,0},{6,2},{1,5},{3,7},{5,1},{7,3},{8,12},{10,14},{12... | collective-permute-start | bytes 8650760 | tf_op jit(solution)/shard_map/ppermute | solution.py:61
  272.7 33.3 %collective-permute-start.35 = (bf16[1,1,1,704,1024]{4,3,2,1,0:T(8,128)(2,1)S(1)}, bf16[1,1,1,704,1024]{4,3,2,1,0:T(8,128)(2,1)S(1)}, u32[]{:S(2)}, u32[]{:S(2)}) collective-permute-start(bf16[1,1,1,704,1024]{4,3,2,1,0:T(8,128)(2,1)S(1)} %get-tuple-element.894), channel_id=1, source_target_pairs={{0,1},{1,0},{2,3},{3,2},{4,5},{5,4},{6,7},{7,6},{8,9},{9,8},{10,11... | collective-permute-start | bytes 4325384 | tf_op jit(solution)/shard_map/ppermute | solution.py:62
  273.4 32.9 %collective-permute-start.33 = (bf16[1,1,1,704,1024]{4,3,2,1,0:T(8,128)(2,1)S(1)}, bf16[1,1,1,704,1024]{4,3,2,1,0:T(8,128)(2,1)S(1)}, u32[]{:S(2)}, u32[]{:S(2)}) collective-permute-start(bf16[1,1,1,704,1024]{4,3,2,1,0:T(8,128)(2,1)S(1)} %get-tuple-element.896), channel_id=1, source_target_pairs={{0,4},{2,6},{4,0},{6,2},{1,5},{3,7},{5,1},{7,3},{8,12},{10,14},{12... | collective-permute-start | bytes 4325384 | tf_op jit(solution)/shard_map/ppermute | solution.py:61
  331.2 34.8 %collective-permute-start.44 = (bf16[1,2,704,512]{3,2,1,0:T(8,128)(2,1)}, bf16[1,2,704,512]{3,2,1,0:T(8,128)(2,1)}, u32[]{:S(2)}, u32[]{:S(2)}) collective-permute-start(bf16[1,2,704,512]{3,2,1,0:T(8,128)(2,1)} %pad_maximum_fusion.8), channel_id=1, source_target_pairs={{0,4},{2,6},{4,0},{6,2},{1,5},{3,7},{5,1},{7,3},{8,12},{10,14},{12... | collective-permute-start | bytes 4325384 | tf_op jit(solution)/shard_map/ppermute | solution.py:61
  333.1 37.3 %collective-permute-start.43 = (bf16[2,1,704,512]{3,2,1,0:T(8,128)(2,1)}, bf16[2,1,704,512]{3,2,1,0:T(8,128)(2,1)}, u32[]{:S(2)}, u32[]{:S(2)}) collective-permute-start(bf16[2,1,704,512]{3,2,1,0:T(8,128)(2,1)} %pad_maximum_fusion.7), channel_id=1, source_target_pairs={{0,1},{1,0},{2,3},{3,2},{4,5},{5,4},{6,7},{7,6},{8,9},{9,8},{10,11... | collective-permute-start | bytes 4325384 | tf_op jit(solution)/shard_map/ppermute | solution.py:62
  334.5 42.7 %collective-permute-start.45 = (bf16[176,2048]{1,0:T(8,128)(2,1)}, bf16[176,2048]{1,0:T(8,128)(2,1)S(1)}, u32[]{:S(2)}, u32[]{:S(2)}) collective-permute-start(bf16[176,2048]{1,0:T(8,128)(2,1)} %get-tuple-element.566), channel_id=1, source_target_pairs={{0,8},{24,16},{1,9},{25,17},{2,10},{26,18},{3,11},{27,19},{4,12},{... | collective-permute-start | bytes 2162696 | tf_op jit(solution)/shard_map/ppermute | solution.py:169
  343.0 46.1 %collective-permute-start.41 = (bf16[1,1,704,512]{3,2,1,0:T(8,128)(2,1)S(1)}, bf16[1,1,704,512]{3,2,1,0:T(8,128)(2,1)S(1)}, u32[]{:S(2)}, u32[]{:S(2)}) collective-permute-start(bf16[1,1,704,512]{3,2,1,0:T(8,128)(2,1)S(1)} %get-tuple-element.572), channel_id=1, source_target_pairs={{0,4},{2,6},{4,0},{6,2},{1,5},{3,7},{5,1},{7,3},{8,12},{10,14},{12... | collective-permute-start | bytes 2162696 | tf_op jit(solution)/shard_map/ppermute | solution.py:61
  345.6 43.4 %collective-permute-start.42 = (bf16[1,1,704,512]{3,2,1,0:T(8,128)(2,1)S(1)}, bf16[1,1,704,512]{3,2,1,0:T(8,128)(2,1)S(1)}, u32[]{:S(2)}, u32[]{:S(2)}) collective-permute-start(bf16[1,1,704,512]{3,2,1,0:T(8,128)(2,1)S(1)} %get-tuple-element.574), channel_id=1, source_target_pairs={{0,1},{1,0},{2,3},{3,2},{4,5},{5,4},{6,7},{7,6},{8,9},{9,8},{10,11... | collective-permute-start | bytes 2162696 | tf_op jit(solution)/shard_map/ppermute | solution.py:62
  366.0 45.0 %collective-permute-start.49 = (bf16[176,2048]{1,0:T(8,128)(2,1)}, bf16[176,2048]{1,0:T(8,128)(2,1)}, u32[]{:S(2)}, u32[]{:S(2)}) collective-permute-start(bf16[176,2048]{1,0:T(8,128)(2,1)} %get-tuple-element.578), channel_id=1, source_target_pairs={{0,8},{24,16},{1,9},{25,17},{2,10},{26,18},{3,11},{27,19},{4,12},{... | collective-permute-start | bytes 2162696 | tf_op jit(solution)/shard_map/ppermute | solution.py:169
  378.3 31.2 %collective-permute-start.50 = (bf16[176,2048]{1,0:T(8,128)(2,1)}, bf16[176,2048]{1,0:T(8,128)(2,1)}, u32[]{:S(2)}, u32[]{:S(2)}) collective-permute-start(bf16[176,2048]{1,0:T(8,128)(2,1)} %reduce-precision_convert_fusion.23), channel_id=1, source_target_pairs={{8,16},{16,8},{9,17},{17,9},{10,18},{18,10},{11,19},{19,11},{12,20... | collective-permute-start | bytes 2162696 | tf_op jit(solution)/shard_map/ppermute | solution.py:165
  397.1 32.2 %collective-permute-start.52 = (bf16[176,2048]{1,0:T(8,128)(2,1)}, bf16[176,2048]{1,0:T(8,128)(2,1)S(1)}, u32[]{:S(2)}, u32[]{:S(2)}) collective-permute-start(bf16[176,2048]{1,0:T(8,128)(2,1)} %get-tuple-element.590), channel_id=1, source_target_pairs={{0,8},{24,16},{1,9},{25,17},{2,10},{26,18},{3,11},{27,19},{4,12},{... | collective-permute-start | bytes 2162696 | tf_op jit(solution)/shard_map/ppermute | solution.py:169
  433.4 409.9 %collective-permute-start.40 = (bf16[1,2,1,256,512]{4,3,2,1,0:T(8,128)(2,1)}, bf16[1,2,1,256,512]{4,3,2,1,0:T(8,128)(2,1)}, u32[]{:S(2)}, u32[]{:S(2)}) collective-permute-start(bf16[1,2,1,256,512]{4,3,2,1,0:T(8,128)(2,1)} %get-tuple-element.955), channel_id=1, source_target_pairs={{0,1},{1,0},{2,3},{3,2},{4,5},{5,4},{6,7},{7,6},{8,9},{9,8},{10,11... | collective-permute-start | bytes 1572872 | tf_op jit(solution)/shard_map/ppermute | solution.py:62
  437.6 42.7 %collective-permute-start.116 = (bf16[176,2048]{1,0:T(8,128)(2,1)S(1)}, bf16[176,2048]{1,0:T(8,128)(2,1)S(1)}, u32[]{:S(2)}, u32[]{:S(2)}) collective-permute-start(bf16[176,2048]{1,0:T(8,128)(2,1)S(1)} %copy-done.37), channel_id=1, source_target_pairs={{8,0},{16,24},{9,1},{17,25},{10,2},{18,26},{11,3},{19,27},{12,4},{... | collective-permute-start | bytes 2162696 | tf_op jit(solution)/shard_map/ppermute | solution.py:160
  473.3 83.1 %collective-permute-start.66 = (bf16[128,2816]{1,0:T(8,128)(2,1)}, bf16[128,2816]{1,0:T(8,128)(2,1)}, u32[]{:S(2)}, u32[]{:S(2)}) collective-permute-start(bf16[128,2816]{1,0:T(8,128)(2,1)} %get-tuple-element.646), channel_id=1, source_target_pairs={{0,8},{24,16},{1,9},{25,17},{2,10},{26,18},{3,11},{27,19},{4,12},{... | collective-permute-start | bytes 2162696 | tf_op jit(solution)/shard_map/ppermute | solution.py:169
  480.3 88.2 %collective-permute-start.70 = (bf16[128,2816]{1,0:T(8,128)(2,1)}, bf16[128,2816]{1,0:T(8,128)(2,1)}, u32[]{:S(2)}, u32[]{:S(2)}) collective-permute-start(bf16[128,2816]{1,0:T(8,128)(2,1)} %get-tuple-element.654), channel_id=1, source_target_pairs={{0,8},{24,16},{1,9},{25,17},{2,10},{26,18},{3,11},{27,19},{4,12},{... | collective-permute-start | bytes 2162696 | tf_op jit(solution)/shard_map/ppermute | solution.py:169
  483.9 30.4 %collective-permute-start.118 = (bf16[176,2048]{1,0:T(8,128)(2,1)S(1)}, bf16[176,2048]{1,0:T(8,128)(2,1)S(1)}, u32[]{:S(2)}, u32[]{:S(2)}) collective-permute-start(bf16[176,2048]{1,0:T(8,128)(2,1)S(1)} %reduce-precision_convert_fusion.20), channel_id=1, source_target_pairs={{8,0},{16,24},{9,1},{17,25},{10,2},{18,26},{11,3},{19,27},{12,4},{... | collective-permute-start | bytes 2162696 | tf_op jit(solution)/shard_map/ppermute | solution.py:160
  503.5 29.6 %collective-permute-start.63 = (bf16[2,2,256,1024]{3,2,1,0:T(8,128)(2,1)S(1)}, bf16[2,2,256,1024]{3,2,1,0:T(8,128)(2,1)S(1)}, u32[]{:S(2)}, u32[]{:S(2)}) collective-permute-start(bf16[2,2,256,1024]{3,2,1,0:T(8,128)(2,1)S(1)} %maximum_maximum_fusion.3), channel_id=1, source_target_pairs={{0,2},{2,0},{4,6},{6,4},{1,3},{3,1},{5,7},{7,5},{8,10},{10,8},{12,... | collective-permute-start | bytes 6291464 | tf_op jit(solution)/shard_map/ppermute | solution.py:57
  529.0 76.1 %collective-permute-start.78 = (bf16[128,2816]{1,0:T(8,128)(2,1)}, bf16[128,2816]{1,0:T(8,128)(2,1)}, u32[]{:S(2)}, u32[]{:S(2)}) collective-permute-start(bf16[128,2816]{1,0:T(8,128)(2,1)} %get-tuple-element.667), channel_id=1, source_target_pairs={{0,8},{24,16},{1,9},{25,17},{2,10},{26,18},{3,11},{27,19},{4,12},{... | collective-permute-start | bytes 2162696 | tf_op jit(solution)/shard_map/ppermute | solution.py:169
  563.1 71.7 %collective-permute-start.77 = (bf16[128,2816]{1,0:T(8,128)(2,1)S(1)}, bf16[128,2816]{1,0:T(8,128)(2,1)S(1)}, u32[]{:S(2)}, u32[]{:S(2)}) collective-permute-start(bf16[128,2816]{1,0:T(8,128)(2,1)S(1)} %copy-done.53), channel_id=1, source_target_pairs={{0,8},{24,16},{1,9},{25,17},{2,10},{26,18},{3,11},{27,19},{4,12},{... | collective-permute-start | bytes 2162696 | tf_op jit(solution)/shard_map/ppermute | solution.py:169
  568.5 29.7 %collective-permute-start.68 = (bf16[2,1,256,512]{3,2,1,0:T(8,128)(2,1)S(1)}, bf16[2,1,256,512]{3,2,1,0:T(8,128)(2,1)S(1)}, u32[]{:S(2)}, u32[]{:S(2)}) collective-permute-start(bf16[2,1,256,512]{3,2,1,0:T(8,128)(2,1)S(1)} %pad_maximum_fusion.16), channel_id=1, source_target_pairs={{0,1},{1,0},{2,3},{3,2},{4,5},{5,4},{6,7},{7,6},{8,9},{9,8},{10,11... | collective-permute-start | bytes 1572872 | tf_op jit(solution)/shard_map/ppermute | solution.py:62
  596.8 77.4 %collective-permute-start.76 = (bf16[128,2816]{1,0:T(8,128)(2,1)S(1)}, bf16[128,2816]{1,0:T(8,128)(2,1)S(1)}, u32[]{:S(2)}, u32[]{:S(2)}) collective-permute-start(bf16[128,2816]{1,0:T(8,128)(2,1)S(1)} %copy-done.52), channel_id=1, source_target_pairs={{0,8},{24,16},{1,9},{25,17},{2,10},{26,18},{3,11},{27,19},{4,12},{... | collective-permute-start | bytes 2162696 | tf_op jit(solution)/shard_map/ppermute | solution.py:169
  610.3 103.4 %collective-permute-start.75 = (bf16[128,2816]{1,0:T(8,128)(2,1)S(1)}, bf16[128,2816]{1,0:T(8,128)(2,1)S(1)}, u32[]{:S(2)}, u32[]{:S(2)}) collective-permute-start(bf16[128,2816]{1,0:T(8,128)(2,1)S(1)} %copy-done.51), channel_id=1, source_target_pairs={{0,8},{24,16},{1,9},{25,17},{2,10},{26,18},{3,11},{27,19},{4,12},{... | collective-permute-start | bytes 2162696 | tf_op jit(solution)/shard_map/ppermute | solution.py:169
  644.0 87.1 %collective-permute-start.74 = (bf16[128,2816]{1,0:T(8,128)(2,1)S(1)}, bf16[128,2816]{1,0:T(8,128)(2,1)S(1)}, u32[]{:S(2)}, u32[]{:S(2)}) collective-permute-start(bf16[128,2816]{1,0:T(8,128)(2,1)S(1)} %copy-done.50), channel_id=1, source_target_pairs={{0,8},{24,16},{1,9},{25,17},{2,10},{26,18},{3,11},{27,19},{4,12},{... | collective-permute-start | bytes 2162696 | tf_op jit(solution)/shard_map/ppermute | solution.py:169
  678.2 30.7 %collective-permute-start.108 = (bf16[128,2816]{1,0:T(8,128)(2,1)S(1)}, bf16[128,2816]{1,0:T(8,128)(2,1)S(1)}, u32[]{:S(2)}, u32[]{:S(2)}) collective-permute-start(bf16[128,2816]{1,0:T(8,128)(2,1)S(1)} %reduce-precision_convert_fusion.10), channel_id=1, source_target_pairs={{8,0},{16,24},{9,1},{17,25},{10,2},{18,26},{11,3},{19,27},{12,4},{... | collective-permute-start | bytes 2162696 | tf_op jit(solution)/shard_map/ppermute | solution.py:160
  680.6 30.7 %collective-permute-start.86 = (bf16[128,2816]{1,0:T(8,128)(2,1)S(1)}, bf16[128,2816]{1,0:T(8,128)(2,1)S(1)}, u32[]{:S(2)}, u32[]{:S(2)}) collective-permute-start(bf16[128,2816]{1,0:T(8,128)(2,1)S(1)} %reduce-precision_convert_fusion.7), channel_id=1, source_target_pairs={{8,16},{16,8},{9,17},{17,9},{10,18},{18,10},{11,19},{19,11},{12,20... | collective-permute-start | bytes 2162696 | tf_op jit(solution)/shard_map/ppermute | solution.py:165
  709.0 43.6 %collective-permute-start.115 = (bf16[128,2816]{1,0:T(8,128)(2,1)}, bf16[128,2816]{1,0:T(8,128)(2,1)}, u32[]{:S(2)}, u32[]{:S(2)}) collective-permute-start(bf16[128,2816]{1,0:T(8,128)(2,1)} %reduce-precision_convert_fusion.8), channel_id=1, source_target_pairs={{8,0},{16,24},{9,1},{17,25},{10,2},{18,26},{11,3},{19,27},{12,4},{... | collective-permute-start | bytes 2162696 | tf_op jit(solution)/shard_map/ppermute | solution.py:160
  722.9 46.3 %collective-permute-start.114 = (bf16[128,2816]{1,0:T(8,128)(2,1)}, bf16[128,2816]{1,0:T(8,128)(2,1)}, u32[]{:S(2)}, u32[]{:S(2)}) collective-permute-start(bf16[128,2816]{1,0:T(8,128)(2,1)} %reduce-precision_convert_fusion.6), channel_id=1, source_target_pairs={{8,0},{16,24},{9,1},{17,25},{10,2},{18,26},{11,3},{19,27},{12,4},{... | collective-permute-start | bytes 2162696 | tf_op jit(solution)/shard_map/ppermute | solution.py:160
  775.4 32.1 %collective-permute-start.112 = (bf16[128,2816]{1,0:T(8,128)(2,1)}, bf16[128,2816]{1,0:T(8,128)(2,1)}, u32[]{:S(2)}, u32[]{:S(2)}) collective-permute-start(bf16[128,2816]{1,0:T(8,128)(2,1)} %reduce-precision_convert_fusion.2), channel_id=1, source_target_pairs={{8,0},{16,24},{9,1},{17,25},{10,2},{18,26},{11,3},{19,27},{12,4},{... | collective-permute-start | bytes 2162696 | tf_op jit(solution)/shard_map/ppermute | solution.py:160
  788.7 47.0 %collective-permute-start.94 = (bf16[256,2048]{1,0:T(8,128)(2,1)S(1)}, bf16[256,2048]{1,0:T(8,128)(2,1)}, u32[]{:S(2)}, u32[]{:S(2)}) collective-permute-start(bf16[256,2048]{1,0:T(8,128)(2,1)S(1)} %reduce-precision_convert_fusion.1), channel_id=1, source_target_pairs={{8,16},{16,8},{9,17},{17,9},{10,18},{18,10},{11,19},{19,11},{12,20... | collective-permute-start | bytes 3145736 | tf_op jit(solution)/shard_map/ppermute | solution.py:165
  810.9 34.2 %collective-permute-start.99 = (bf16[1,1,2,256,512]{4,3,2,1,0:T(8,128)(2,1)}, bf16[1,1,2,256,512]{4,3,2,1,0:T(8,128)(2,1)}, u32[]{:S(2)}, u32[]{:S(2)}) collective-permute-start(bf16[1,1,2,256,512]{4,3,2,1,0:T(8,128)(2,1)} %get-tuple-element.937), channel_id=1, source_target_pairs={{0,4},{2,6},{4,0},{6,2},{1,5},{3,7},{5,1},{7,3},{8,12},{10,14},{12... | collective-permute-start | bytes 1572872 | tf_op jit(solution)/shard_map/ppermute | solution.py:61
  816.0 34.6 %collective-permute-start.101 = (bf16[256,1024]{1,0:T(8,128)(2,1)}, bf16[256,1024]{1,0:T(8,128)(2,1)}, u32[]{:S(2)}, u32[]{:S(2)}) collective-permute-start(bf16[256,1024]{1,0:T(8,128)(2,1)} %get-tuple-element.744), channel_id=1, source_target_pairs={{0,8},{24,16},{1,9},{25,17},{2,10},{26,18},{3,11},{27,19},{4,12},{... | collective-permute-start | bytes 1572872 | tf_op jit(solution)/shard_map/ppermute | solution.py:169
  835.7 42.3 %collective-permute-start.120 = (bf16[256,1024]{1,0:T(8,128)(2,1)}, bf16[256,1024]{1,0:T(8,128)(2,1)}, u32[]{:S(2)}, u32[]{:S(2)}) collective-permute-start(bf16[256,1024]{1,0:T(8,128)(2,1)} %get-tuple-element.753), channel_id=1, source_target_pairs={{0,8},{24,16},{1,9},{25,17},{2,10},{26,18},{3,11},{27,19},{4,12},{... | collective-permute-start | bytes 1572872 | tf_op jit(solution)/shard_map/ppermute | solution.py:169
  839.6 77.6 %collective-permute-start.123 = (bf16[256,1024]{1,0:T(8,128)(2,1)}, bf16[256,1024]{1,0:T(8,128)(2,1)}, u32[]{:S(2)}, u32[]{:S(2)}) collective-permute-start(bf16[256,1024]{1,0:T(8,128)(2,1)} %get-tuple-element.767), channel_id=1, source_target_pairs={{0,8},{24,16},{1,9},{25,17},{2,10},{26,18},{3,11},{27,19},{4,12},{... | collective-permute-start | bytes 1572872 | tf_op jit(solution)/shard_map/ppermute | solution.py:169
  845.2 76.4 %collective-permute-start.130 = (bf16[256,1024]{1,0:T(8,128)(2,1)}, bf16[256,1024]{1,0:T(8,128)(2,1)}, u32[]{:S(2)}, u32[]{:S(2)}) collective-permute-start(bf16[256,1024]{1,0:T(8,128)(2,1)} %get-tuple-element.805), channel_id=1, source_target_pairs={{0,8},{24,16},{1,9},{25,17},{2,10},{26,18},{3,11},{27,19},{4,12},{... | collective-permute-start | bytes 1572872 | tf_op jit(solution)/shard_map/ppermute | solution.py:169
  864.3 88.5 %collective-permute-start.129 = (bf16[256,1024]{1,0:T(8,128)(2,1)S(1)}, bf16[256,1024]{1,0:T(8,128)(2,1)}, u32[]{:S(2)}, u32[]{:S(2)}) collective-permute-start(bf16[256,1024]{1,0:T(8,128)(2,1)S(1)} %copy-done.60), channel_id=1, source_target_pairs={{0,8},{24,16},{1,9},{25,17},{2,10},{26,18},{3,11},{27,19},{4,12},{... | collective-permute-start | bytes 1572872 | tf_op jit(solution)/shard_map/ppermute | solution.py:169
  875.0 44.2 %collective-permute-start.107 = (bf16[256,2048]{1,0:T(8,128)(2,1)S(1)}, bf16[256,2048]{1,0:T(8,128)(2,1)S(1)}, u32[]{:S(2)}, u32[]{:S(2)}) collective-permute-start(bf16[256,2048]{1,0:T(8,128)(2,1)S(1)} %reduce-precision_convert_fusion), channel_id=1, source_target_pairs={{8,0},{16,24},{9,1},{17,25},{10,2},{18,26},{11,3},{19,27},{12,4},{... | collective-permute-start | bytes 3145736 | tf_op jit(solution)/shard_map/ppermute | solution.py:160
  879.5 34.5 %collective-permute-start.124 = (bf16[256,1024]{1,0:T(8,128)(2,1)S(1)}, bf16[256,1024]{1,0:T(8,128)(2,1)}, u32[]{:S(2)}, u32[]{:S(2)}) collective-permute-start(bf16[256,1024]{1,0:T(8,128)(2,1)S(1)} %reduce-precision_convert_fusion.33), channel_id=1, source_target_pairs={{8,16},{16,8},{9,17},{17,9},{10,18},{18,10},{11,19},{19,11},{12,20... | collective-permute-start | bytes 1572872 | tf_op jit(solution)/shard_map/ppermute | solution.py:165
  917.2 124.8 %collective-permute-start.104 = (bf16[2,256,128]{2,1,0:T(8,128)(2,1)}, bf16[2,256,128]{2,1,0:T(8,128)(2,1)S(1)}, u32[]{:S(2)}, u32[]{:S(2)}) collective-permute-start(bf16[2,256,128]{2,1,0:T(8,128)(2,1)} %get-tuple-element.977), channel_id=1, source_target_pairs={{0,1},{1,0},{2,3},{3,2},{4,5},{5,4},{6,7},{7,6},{8,9},{9,8},{10,11... | collective-permute-start | bytes 393224 | tf_op jit(solution)/shard_map/ppermute | solution.py:88
  920.1 29.7 %collective-permute-start.142 = (bf16[256,1024]{1,0:T(8,128)(2,1)S(1)}, bf16[256,1024]{1,0:T(8,128)(2,1)S(1)}, u32[]{:S(2)}, u32[]{:S(2)}) collective-permute-start(bf16[256,1024]{1,0:T(8,128)(2,1)S(1)} %reduce-precision_convert_fusion.34), channel_id=1, source_target_pairs={{8,0},{16,24},{9,1},{17,25},{10,2},{18,26},{11,3},{19,27},{12,4},{... | collective-permute-start | bytes 1572872 | tf_op jit(solution)/shard_map/ppermute | solution.py:160
  921.6 88.4 %collective-permute-start.122 = (bf16[256,5632]{1,0:T(8,128)(2,1)S(1)}, bf16[256,5632]{1,0:T(8,128)(2,1)S(1)}, u32[]{:S(2)}, u32[]{:S(2)}) collective-permute-start(bf16[256,5632]{1,0:T(8,128)(2,1)S(1)} %get-tuple-element.852), channel_id=1, source_target_pairs={{0,2},{2,0},{4,6},{6,4},{1,3},{3,1},{5,7},{7,5},{8,10},{10,8},{12,... | collective-permute-start | bytes 8650760 | tf_op jit(solution)/shard_map/ppermute | solution.py:57
  949.8 92.2 %collective-permute-start.105 = (bf16[2,256,128]{2,1,0:T(8,128)(2,1)}, bf16[2,256,128]{2,1,0:T(8,128)(2,1)S(1)}, u32[]{:S(2)}, u32[]{:S(2)}) collective-permute-start(bf16[2,256,128]{2,1,0:T(8,128)(2,1)} %get-tuple-element.976), channel_id=1, source_target_pairs={{0,4},{1,5},{2,6},{3,7},{4,0},{5,1},{6,2},{7,3},{8,12},{9,13},{10,... | collective-permute-start | bytes 393224 | tf_op jit(solution)/shard_map/ppermute | solution.py:88
  952.8 28.6 %collective-permute-start.141 = (bf16[256,1024]{1,0:T(8,128)(2,1)S(1)}, bf16[256,1024]{1,0:T(8,128)(2,1)S(1)}, u32[]{:S(2)}, u32[]{:S(2)}) collective-permute-start(bf16[256,1024]{1,0:T(8,128)(2,1)S(1)} %reduce-precision_convert_fusion.30), channel_id=1, source_target_pairs={{8,0},{16,24},{9,1},{17,25},{10,2},{18,26},{11,3},{19,27},{12,4},{... | collective-permute-start | bytes 1572872 | tf_op jit(solution)/shard_map/ppermute | solution.py:160
  983.0 59.0 %collective-permute-start.106 = (bf16[2,256,128]{2,1,0:T(8,128)(2,1)}, bf16[2,256,128]{2,1,0:T(8,128)(2,1)}, u32[]{:S(2)}, u32[]{:S(2)}) collective-permute-start(bf16[2,256,128]{2,1,0:T(8,128)(2,1)} %get-tuple-element.974), channel_id=1, source_target_pairs={{0,5},{1,4},{2,7},{3,6},{4,1},{5,0},{6,3},{7,2},{8,13},{9,12},{10,... | collective-permute-start | bytes 393224 | tf_op jit(solution)/shard_map/ppermute | solution.py:88
  1009.8 38.7 %collective-permute-start.146 = (bf16[256,3072]{1,0:T(8,128)(2,1)}, bf16[256,3072]{1,0:T(8,128)(2,1)S(1)}, u32[]{:S(2)}, u32[]{:S(2)}) collective-permute-start(bf16[256,3072]{1,0:T(8,128)(2,1)} %pad_maximum_fusion.6), channel_id=1, source_target_pairs={{0,2},{2,0},{4,6},{6,4},{1,3},{3,1},{5,7},{7,5},{8,10},{10,8},{12,... | collective-permute-start | bytes 4718600 | tf_op jit(solution)/shard_map/ppermute | solution.py:57
  (201 other events, 2067.3 us)

commit v3 on v2

v3 whole, which is shorter than its diff:
```python
import functools

import jax
import jax.numpy as jnp
from jax import lax
from jax.experimental import pallas as pl
from jax.experimental.pallas import tpu as pltpu
from jax.sharding import PartitionSpec as P

HEADS = 32
HEAD_DIM = 64
FF = 5632
ROTARY = 16
STEP = 10

eps_norm = 1e-05
masked_score = -1e30
beta_one = 0.9
beta_two = 0.999
adam_eps = 1e-08
weight_decay = 0.1
score_scale = HEAD_DIM ** (-0.5)
FIRST = (((0,), (0,)), ((), ()))
LAST = (((1,), (1,)), ((), ()))
PLAIN = (((1,), (0,)), ((), ()))
bf16 = jnp.bfloat16
f32 = jnp.float32


def dot(a, b, dims):
    return lax.dot_general(a, b, dims, preferred_element_type=f32)


def adam_update(weight, moment_one, moment_two, grad, step_rate, decay_rate):
    first_new = beta_one * moment_one + (1.0 - beta_one) * grad
    second_new = beta_two * moment_two + (1.0 - beta_two) * grad * grad
    first_hat = first_new / (1.0 - beta_one**STEP)
    second_hat = second_new / (1.0 - beta_two**STEP)
    weight_new = weight - step_rate * (
        first_hat / (jnp.sqrt(second_hat) + adam_eps) + decay_rate * weight
    )
    return (first_new, second_new, weight_new)


class Plane:
    def __init__(self):
        self.s_size = lax.axis_size("shard")
        self.ctx_size = lax.axis_size("ctx")
        self.y_size = self.ctx_size // 2
        self.ctx = lax.axis_index("ctx")
        self.s = lax.axis_index("shard")
        self.y = self.ctx // 2
        self.c = self.ctx % 2
        self.blocks = self.ctx_size * self.s_size

    def core(self, x):
        return lax.ppermute(x, "ctx", [(i, i ^ 1) for i in range(self.ctx_size)])

    def along(self, x, axis, step):
        if axis == "y":
            return lax.ppermute(x, "ctx", [(i, i ^ (2 * step)) for i in range(self.ctx_size)])
        return lax.ppermute(x, "shard", [(i, i ^ step) for i in range(self.s_size)])

    def index(self, axis):
        return self.y if axis == "y" else self.s

    def steps(self, flip):
        ys = []
        k = self.y_size // 2
        while k:
            ys.append(("y", k))
            k //= 2
        ss = []
        k = self.s_size // 2
        while k:
            ss.append(("s", k))
            k //= 2
        return ys + ss if flip else ss + ys

    def chip_exchange(self, x, take):
        out = [(self.y, self.s, take(self.y, self.s))]
        for ry in range(self.y_size):
            for rs in range(self.s_size):
                if ry or rs:
                    y, s = self.y ^ ry, self.s ^ rs
                    mask = 2 * ry * self.s_size + rs
                    perm = [(i, i ^ mask) for i in range(self.blocks)]
                    out.append((y, s, lax.ppermute(take(y, s), ("ctx", "shard"), perm)))
        return out

    def sum_all(self, x):
        for axis, step in self.steps(False):
            x = x + self.along(x, axis, step)
        return x + self.core(x)

    def scatter_sum(self, p, flip):
        axes = {"y": 1, "s": 2}
        steps = self.steps(flip)
        kept = got = None
        for n, (axis, step) in enumerate(steps):
            ax = axes[axis]
            bit = (self.index(axis) // step) % 2
            kept = lax.dynamic_slice_in_dim(p, bit * step, step, ax)
            send = lax.dynamic_slice_in_dim(p, (1 - bit) * step, step, ax)
            got = self.along(send, axis, step)
            if n + 1 < len(steps):
                p = (kept.astype(f32) + got.astype(f32)).astype(bf16)
        return kept[:, 0, 0], got[:, 0, 0]

    def gather(self, p, flip):
        axes = {"y": 1, "s": 2}
        p = p[:, None, None]
        for axis, step in reversed(self.steps(flip)):
            ax = axes[axis]
            bit = (self.index(axis) // step) % 2
            got = self.along(p, axis, step)
            first = bit == 0
            p = jnp.concatenate([jnp.where(first, p, got), jnp.where(first, got, p)], ax)
        return p


class Order:
    def __init__(self):
        self.last = None

    def __call__(self, stage, *args):
        if self.last is not None:
            args, self.last = lax.optimization_barrier((args, self.last))
        out = stage(*args)
        self.last = jax.tree.leaves(out)[0]
        return out


class RepSum:
    def __init__(self, order):
        self.order = order
        z = lax.axis_index("rep")
        self.end = (z == 0) | (z == lax.axis_size("rep") - 1)
        self.queue = []
        self.outer = None
        self.inner = None
        self.done = {}

    def push(self, name, g):
        self.queue.append((name, g))

    def busy(self):
        return bool(self.queue or self.outer or self.inner)

    def tick(self):
        outer, inner = self.outer, self.inner
        new = self.queue.pop(0) if self.queue else None
        values = {}
        if outer and outer["in"]:
            values["g"], values["g_got"] = outer["in"][1], outer["in_got"]
        if outer and outer["out"]:
            values["t"], values["t_got"] = outer["out"][1], outer["out_got"]
        if inner:
            values["s"], values["s_got"] = inner[1], inner[2]
        if new:
            values["new"] = new[1]
        both = new and inner and new[1].shape == inner[1].shape

        def stage(v):
            def add(a, b):
                return lax.reduce_precision(a.astype(f32) + b.astype(f32), 8, 7).astype(bf16)

            out = {}
            if "s" in v:
                out["total"] = add(v["s"], v["s_got"])
            if "g" in v:
                out["sum"] = add(v["g"], v["g_got"])
            if "t" in v:
                out["out"] = jnp.where(self.end, v["t_got"], v["t"])
            if both:
                out["send"] = jnp.where(self.end, v["new"], out["total"])
            elif "new" in v:
                out["new"] = v["new"]
            return out

        out = self.order(stage, values)
        if outer and outer["out"]:
            self.done[outer["out"][0]] = out["out"]
        self.outer = None
        if new or inner:
            o = {"in": None, "out": None}
            if both:
                o["in_got"] = o["out_got"] = lax.ppermute(out["send"], "rep", [(0, 1), (1, 0), (2, 3), (3, 2)])
            else:
                if new:
                    o["in_got"] = lax.ppermute(out["new"], "rep", [(0, 1), (3, 2)])
                if inner:
                    o["out_got"] = lax.ppermute(out["total"], "rep", [(1, 0), (2, 3)])
            if new:
                o["in"] = new
            if inner:
                o["out"] = (inner[0], out["total"])
            self.outer = o
        self.inner = None
        if outer and outer["in"]:
            self.inner = (outer["in"][0], out["sum"], lax.ppermute(out["sum"], "rep", [(1, 2), (2, 1)]))


def split_kernel(core_ref, w_ref, mine_ref, theirs_ref):
    unit = mine_ref.shape[0]
    first = core_ref[0] == 0
    a, b = w_ref[:, :unit], w_ref[:, unit:]
    mine_ref[...] = jnp.where(first, a, b).T.astype(bf16)
    theirs_ref[...] = jnp.where(first, b, a).T.astype(bf16)


def split_columns(w, core, lead, unit, count):
    rows = w.shape[0]
    half = pl.BlockSpec((unit, rows), lambda j, core: (j, 0))
    out = jax.ShapeDtypeStruct((count * unit, rows), bf16)
    return pl.pallas_call(
        split_kernel,
        grid_spec=pltpu.PrefetchScalarGridSpec(
            num_scalar_prefetch=1,
            grid=(count,),
            in_specs=[pl.BlockSpec((rows, 2 * unit), lambda j, core: (0, lead + j))],
            out_specs=[half, half],
        ),
        out_shape=[out, out],
        compiler_params=pltpu.CompilerParams(vmem_limit_bytes=32 * 1024 * 1024),
        cost_estimate=pl.CostEstimate(flops=0, bytes_accessed=12 * rows * count * unit, transcendentals=0),
    )(core, w)


def adam_kernel(rate, two, core_ref, w_ref, m_ref, v_ref, *refs):
    if two:
        mine = core_ref[0] == pl.program_id(1)
        grad = jnp.where(mine, refs[0][...], refs[1][...]).astype(f32)
    else:
        grad = refs[0][...].astype(f32)
    new_m_ref, new_v_ref, new_w_ref = refs[-3:]
    new_m, new_v, new_w = adam_update(w_ref[...], m_ref[...], v_ref[...], grad, rate, weight_decay)
    new_m_ref[...] = new_m
    new_v_ref[...] = new_v
    new_w_ref[...] = new_w


def adam_part(state, grads, core, rate, prev, row_block, col_first, unit):
    w, m, v = state
    two = len(grads) == 2
    rb = grads[0].shape[0]
    count = grads[0].shape[1] // unit
    if two:
        grid = (count, 2)
        whole = pl.BlockSpec((rb, unit), lambda g, j, core: (row_block, 2 * (col_first + g) + j))
        half = pl.BlockSpec((rb, unit), lambda g, j, core: (0, g))
    else:
        grid = (count,)
        whole = pl.BlockSpec((rb, unit), lambda g, core: (row_block, g))
        half = pl.BlockSpec((rb, unit), lambda g, core: (0, g))
    out = jax.ShapeDtypeStruct(w.shape, f32)
    extra, aliases = [], {}
    if prev is not None:
        extra = list(prev)
        aliases = {4 + len(grads) + i: i for i in range(3)}
    n = rb * count * unit * len(grads)
    return pl.pallas_call(
        functools.partial(adam_kernel, rate, two),
        grid_spec=pltpu.PrefetchScalarGridSpec(
            num_scalar_prefetch=1,
            grid=grid,
            in_specs=[whole] * 3 + [half] * len(grads) + [pl.BlockSpec(memory_space=pl.ANY)] * len(extra),
            out_specs=[whole] * 3,
        ),
        out_shape=[out] * 3,
        input_output_aliases=aliases,
        compiler_params=pltpu.CompilerParams(vmem_limit_bytes=32 * 1024 * 1024),
        cost_estimate=pl.CostEstimate(flops=20 * n, bytes_accessed=28 * n, transcendentals=0),
    )(core, w, m, v, *grads, *extra)


def attend_kernel(kept_ref, got_ref, bias_ref, cos_ref, sin_ref, prow_ref, pcol_ref, qkv_ref, out_ref, peak_ref, total_ref):
    cos, sin = cos_ref[0], sin_ref[0]
    half = ROTARY // 2
    parts = []
    for i in range(3):
        v = kept_ref[i, 0].astype(f32) + got_ref[i, 0].astype(f32) + bias_ref[i, 0]
        if i < 2:
            a, b = v[:half], v[half:ROTARY]
            v = jnp.concatenate([a * cos - b * sin, b * cos + a * sin, v[ROTARY:]], axis=0)
        v = v.astype(bf16)
        qkv_ref[i, 0] = v
        parts.append(v)
    q, k, v = parts
    scores = dot(k, q, FIRST) * score_scale
    scores = jnp.where(pcol_ref[0] <= prow_ref[0], scores, masked_score)
    peak = jnp.max(scores, axis=0, keepdims=True)
    e = jnp.exp(scores - peak)
    total = jnp.sum(e, axis=0, keepdims=True)
    p = (e / total).astype(bf16)
    out_ref[0] = dot(v, p, PLAIN).astype(bf16)
    peak_ref[0, 0] = peak
    total_ref[0, 0] = total


def attend(kept, got, bias, cos, sin, prow, pcol):
    _, heads, hd, t = kept.shape
    seqs, _, seq = prow.shape
    big = pl.BlockSpec((3, 1, hd, seq), lambda s, h: (0, h, 0, s))
    table = pl.BlockSpec((1, ROTARY // 2, seq), lambda s, h: (s, 0, 0))
    stat = pl.BlockSpec((1, 1, 1, seq), lambda s, h: (s, h, 0, 0))
    return pl.pallas_call(
        attend_kernel,
        grid=(seqs, heads),
        in_specs=[
            big,
            big,
            pl.BlockSpec((3, 1, hd, 1), lambda s, h: (0, h, 0, 0)),
            table,
            table,
            pl.BlockSpec((1, 1, seq), lambda s, h: (s, 0, 0)),
            pl.BlockSpec((1, seq, 1), lambda s, h: (s, 0, 0)),
        ],
        out_specs=[big, pl.BlockSpec((1, hd, seq), lambda s, h: (h, 0, s)), stat, stat],
        out_shape=[
            jax.ShapeDtypeStruct((3, heads, hd, t), bf16),
            jax.ShapeDtypeStruct((heads, hd, t), bf16),
            jax.ShapeDtypeStruct((seqs, heads, 1, seq), f32),
            jax.ShapeDtypeStruct((seqs, heads, 1, seq), f32),
        ],
        compiler_params=pltpu.CompilerParams(vmem_limit_bytes=32 * 1024 * 1024),
        cost_estimate=pl.CostEstimate(
            flops=4 * seqs * heads * seq * seq * hd,
            bytes_accessed=16 * 3 * heads * hd * t,
            transcendentals=seqs * heads * seq * seq,
        ),
    )(kept, got, bias, cos, sin, prow, pcol)


def attend_back_kernel(qkv_ref, dout_ref, peak_ref, total_ref, cos_ref, sin_ref, prow_ref, pcol_ref, out_ref):
    cos, sin = cos_ref[0], sin_ref[0]
    half = ROTARY // 2
    q, k, v = qkv_ref[0, 0], qkv_ref[1, 0], qkv_ref[2, 0]
    dout = dout_ref[0]
    scores = dot(k, q, FIRST) * score_scale
    scores = jnp.where(pcol_ref[0] <= prow_ref[0], scores, masked_score)
    p = jnp.exp(scores - peak_ref[0, 0]) / total_ref[0, 0]
    dp = dot(v, dout, FIRST)
    inner = jnp.sum(p * dp, axis=0, keepdims=True)
    ds = (p * (dp - inner)).astype(bf16)

    def back(x):
        a, b = x[:half], x[half:ROTARY]
        return jnp.concatenate([a * cos + b * sin, b * cos - a * sin, x[ROTARY:]], axis=0)

    out_ref[0, 0] = back(dot(k, ds, PLAIN) * score_scale).astype(bf16)
    out_ref[1, 0] = back(dot(q, ds, LAST) * score_scale).astype(bf16)
    out_ref[2, 0] = dot(dout, p.astype(bf16), LAST).astype(bf16)


def attend_back(qkv, dout, peak, total, cos, sin, prow, pcol):
    _, heads, hd, t = qkv.shape
    seqs, _, seq = prow.shape
    big = pl.BlockSpec((3, 1, hd, seq), lambda s, h: (0, h, 0, s))
    table = pl.BlockSpec((1, ROTARY // 2, seq), lambda s, h: (s, 0, 0))
    stat = pl.BlockSpec((1, 1, 1, seq), lambda s, h: (s, h, 0, 0))
    return pl.pallas_call(
        attend_back_kernel,
        grid=(seqs, heads),
        in_specs=[
            big,
            pl.BlockSpec((1, hd, seq), lambda s, h: (h, 0, s)),
            stat,
            stat,
            table,
            table,
            pl.BlockSpec((1, 1, seq), lambda s, h: (s, 0, 0)),
            pl.BlockSpec((1, seq, 1), lambda s, h: (s, 0, 0)),
        ],
        out_specs=big,
        out_shape=jax.ShapeDtypeStruct((3, heads, hd, t), bf16),
        compiler_params=pltpu.CompilerParams(vmem_limit_bytes=32 * 1024 * 1024),
        cost_estimate=pl.CostEstimate(
            flops=10 * seqs * heads * seq * seq * hd,
            bytes_accessed=16 * 3 * heads * hd * t,
            transcendentals=seqs * heads * seq * seq,
        ),
    )(qkv, dout, peak, total, cos, sin, prow, pcol)


def body(
    tokens,
    cotangent,
    span_order,
    w_qkv,
    w_out,
    w_up,
    w_down,
    norm_params,
    m_qkv,
    v_qkv,
    m_out,
    v_out,
    m_up,
    v_up,
    m_down,
    v_down,
    m_norm,
    v_norm,
):
    at = Plane()
    do = Order()
    reps = RepSum(do)
    width = tokens.shape[3]
    rows = tokens.shape[1]
    S, Y, nb = at.s_size, at.y_size, at.blocks
    plane = ("ctx", "shard")
    blk = width // nb
    ffb = FF // nb
    heads = blk // HEAD_DIM
    seq = rows * at.ctx_size
    T = S * seq
    H = T // 2
    first = at.c == 0
    core = at.c.reshape(1)
    my_block = at.ctx * S + at.s
    halves = (slice(0, H), slice(H, T))
    seqs = (slice(0, S // 2), slice(S // 2, S))

    def pick(x, axis, which):
        return lax.dynamic_index_in_dim(x, which, axis, keepdims=False)

    def in_order(mine, theirs, axis):
        return jnp.stack([jnp.where(first, mine, theirs), jnp.where(first, theirs, mine)], axis=axis)

    def join(a, b):
        return jnp.concatenate([a, b], axis=0)

    x_rows = tokens.reshape(rows, width)
    order = span_order.reshape(-1).astype(f32)
    span = rows // 2

    def pack(x, order):
        xf = x.astype(f32)
        mean = jnp.mean(xf, axis=1)
        centred = xf - mean[:, None]
        inv = lax.rsqrt(jnp.mean(centred * centred, axis=1) + eps_norm)
        mine = lax.dynamic_slice_in_dim(order, 2 * at.ctx, 2)
        place = jnp.repeat(mine, span)
        terms = []
        for v in (mean, inv):
            for _ in range(3):
                t = lax.reduce_precision(v, 8, 7)
                terms.append(t)
                v = v - t
        extra = jnp.stack(terms + [place] + [jnp.zeros_like(place)] * 9).astype(bf16)
        blocks = x.T.reshape(nb, blk, rows)
        return jnp.concatenate([blocks, jnp.broadcast_to(extra[None], (nb, 16, rows))], axis=1)

    packed = do(pack, x_rows, order)
    got = lax.all_to_all(packed, plane, split_axis=0, concat_axis=0, tiled=True)

    def chip_rows(w, lead, unit, count):
        mine, theirs = do(lambda w: split_columns(w, core, lead, unit, count), w)
        return mine, at.core(theirs)

    def lanes(a, b):
        return jnp.concatenate([a, b], axis=1)

    wq_parts = chip_rows(w_qkv, 0, S * blk, 3 * Y)
    norm_cols = norm_params.reshape(7, nb, blk).transpose(1, 2, 0)
    own_cols = pick(norm_cols, 0, my_block)
    other_cols = pick(norm_cols, 0, (at.ctx ^ 1) * S + at.s)
    pair_cols = join(own_cols, other_cols)
    bias = own_cols[:, 4:7].T.reshape(3, heads, HEAD_DIM, 1)
    wq = do(lanes, *wq_parts)

    def first_step(flip):
        axis, step = at.steps(flip)[0]
        return axis, step, {"y": 1, "s": 2}[axis], (at.index(axis) // step) % 2

    def send_keep(w, pre, unit, flip):
        _, step, ax, bit = first_step(flip)
        w = w.reshape(pre, Y, S, unit, w.shape[1])
        cut = [lax.dynamic_slice_in_dim(w, b * step, step, ax) for b in (1 - bit, bit)]
        return [c.reshape(-1, c.shape[-1]) for c in cut]

    wq_cut = [do(lambda w, k=k: send_keep(w, 3, blk, bool(k)), wq) for k in range(2)]

    def arrange(got):
        x = got.reshape(at.ctx_size, S, blk + 16, rows).transpose(2, 1, 0, 3).reshape(blk + 16, T)
        x_own, extra = x[:blk], x[blk:].astype(f32)
        mean = extra[0:1] + extra[1:2] + extra[2:3]
        inv = extra[3:4] + extra[4:5] + extra[5:6]
        return x_own, mean, inv, extra[6:7]

    x_own, mean1, inv1, place = do(arrange, got)
    x_other = at.core(x_own)

    def first_norm(mine, theirs, mean, inv, cols):
        x = join(mine, theirs).astype(f32)
        return ((x - mean) * inv * cols[:, 0:1] + cols[:, 1:2]).astype(bf16)

    xn1 = do(first_norm, x_own, x_other, mean1, inv1, pair_cols)

    def send_products(cut, xs, shapes):
        got = []
        for k in range(2):
            axis, step, _, _ = first_step(bool(k))
            p = do(lambda w, x: dot(w, x, PLAIN).astype(bf16), cut[k][0], xs[k]).reshape(shapes[k])
            got.append(at.along(p, axis, step))
        kept = []
        for k in range(2):
            p = do(lambda w, x: dot(w, x, PLAIN).astype(bf16), cut[k][1], xs[k])
            kept.append(p.reshape(shapes[k]))
        return list(zip(kept, got))

    def half_shape(pre, unit, t, flip):
        _, step, ax, _ = first_step(flip)
        shape = [pre, Y, S, unit, t]
        shape[ax] = step
        return tuple(shape)

    def scatter_rest(pairs):
        for i in range(1, len(at.steps(False))):
            out = []
            for k in range(2):
                kept, got = pairs[k]
                axis, step = at.steps(bool(k))[i]
                ax = {"y": 1, "s": 2}[axis]
                bit = (at.index(axis) // step) % 2

                def cut(a, b):
                    p = (a.astype(f32) + b.astype(f32)).astype(bf16)
                    return [lax.dynamic_slice_in_dim(p, n * step, step, ax) for n in (1 - bit, bit)]

                send, kept = do(cut, kept, got)
                out.append((kept, at.along(send, axis, step)))
            pairs = out
        return [(kept[:, 0, 0], got[:, 0, 0]) for kept, got in pairs]

    flying = send_products(
        wq_cut, [xn1[:, h] for h in halves], [half_shape(3, blk, H, bool(k)) for k in range(2)]
    )

    wo_parts = chip_rows(w_out, 0, S * blk, Y)
    wg_parts = chip_rows(w_up, 0, S * ffb, Y)
    wo = do(lanes, *wo_parts)
    wu_parts = chip_rows(w_up, Y, S * ffb, Y)
    wg = do(lanes, *wg_parts)
    wg_cut = do(lambda w: send_keep(w, 1, ffb, False), wg)

    def positions(place):
        pos = place.reshape(S, seq) * span + (jnp.arange(seq) % span).astype(f32)[None, :]
        prow, pcol = pos.reshape(S, 1, seq), pos.reshape(S, seq, 1)
        exponent = jnp.arange(ROTARY // 2, dtype=f32)
        inverse = 10000.0 ** (-2.0 * exponent / ROTARY)
        angles = prow * inverse[None, :, None]
        return jnp.cos(angles), jnp.sin(angles), prow, pcol

    cos, sin, prow, pcol = do(positions, place)
    flying = scatter_rest(flying)
    wu = do(lanes, *wu_parts)
    wu_cut = do(lambda w: send_keep(w, 1, ffb, True), wu)

    def gather_steps(parts, row_axis):
        n = len(at.steps(False))
        state = {"parts": list(parts)}

        def start(i):
            state["got"] = []
            state["at"] = []
            for k in range(2):
                axis, step = list(reversed(at.steps(bool(k))))[i]
                state["at"].append((axis, step))
                state["got"].append(at.along(state["parts"][k], axis, step))

        def finish():
            def put(parts, got):
                out = []
                for k in range(2):
                    axis, step = state["at"][k]
                    ax = {"y": 0, "s": 1}[axis]
                    low = (at.index(axis) // step) % 2 == 0
                    a, b = parts[k], got[k]
                    out.append(jnp.concatenate([jnp.where(low, a, b), jnp.where(low, b, a)], ax))
                return out

            state["parts"] = do(put, state["parts"], state["got"])

        def result():
            return jnp.concatenate(state["parts"], axis=row_axis)

        return n, start, finish, result

    qkvs, attns, attn_got, peaks, totals = [], [], [], [], []
    for k in range(2):
        sq = seqs[k]
        shape = (3, heads, HEAD_DIM, H)
        qkv, attn, peak, total = do(
            attend, flying[k][0].reshape(shape), flying[k][1].reshape(shape), bias, cos[sq], sin[sq], prow[sq], pcol[sq]
        )
        qkvs.append(qkv)
        attns.append(attn.reshape(blk, H))
        attn_got.append(at.core(attns[k]))
        peaks.append(peak)
        totals.append(total)

    wo5 = wo.reshape(1, Y, S, blk, wo.shape[1])
    flying = []
    for k in range(2):
        axis, step, ax, bit = first_step(bool(k))

        def product(w, a, b):
            p = dot(w, join(a, b), PLAIN).astype(bf16).reshape(1, Y, S, blk, H)
            return [lax.dynamic_slice_in_dim(p, n * step, step, ax) for n in (1 - bit, bit)]

        send, kept = do(product, wo, attns[k], attn_got[k])
        flying.append((kept, at.along(send, axis, step)))
    flying = scatter_rest(flying)
    cot = cotangent.reshape(2, rows // 2, width)
    cot_pair, _ = lax.optimization_barrier((cot, flying[1][0]))
    cot_n, cot_start, cot_finish, cot_done = gather_steps([cot_pair[k][None, None] for k in range(2)], 2)

    def residual(x, a0, b0, a1, b1):
        a, b = lanes(a0[0], a1[0]), lanes(b0[0], b1[0])
        hidden = x.astype(f32) + (a.astype(f32) + b.astype(f32))
        local_mean = jnp.mean(hidden, axis=0, keepdims=True)
        dev = hidden - local_mean
        return hidden, join(local_mean, jnp.sum(dev * dev, axis=0, keepdims=True))

    hidden, moments = do(residual, x_own, *flying[0], *flying[1])
    cot_start(0)
    count = blk
    for axis, step in at.steps(False) + [("core", 1)]:
        other = at.core(moments) if axis == "core" else at.along(moments, axis, step)

        def merge(a, b):
            gap = a[0:1] - b[0:1]
            return join(0.5 * (a[0:1] + b[0:1]), a[1:2] + b[1:2] + gap * gap * (count / 2.0))

        moments = do(merge, moments, other)
        count *= 2

    def second_norm(hidden, moments, cols):
        inv2 = lax.rsqrt(moments[1:2] / width + eps_norm)
        z2 = (hidden - moments[0:1]) * inv2
        return (z2 * cols[:, 2:3] + cols[:, 3:4]).astype(bf16), z2, inv2

    xn2_own, z2, inv2 = do(second_norm, hidden, moments, own_cols)
    xn2 = do(join, xn2_own, at.core(xn2_own))

    flying = send_products(
        [wg_cut, wu_cut], [xn2, xn2], [half_shape(1, ffb, T, bool(k)) for k in range(2)]
    )

    for i in range(1, cot_n):
        cot_finish()
        cot_start(i)
    wo_own = do(lambda w: w.astype(bf16), w_out)
    wd_own = do(lambda w: w.astype(bf16), w_down)

    def gain_products(wg, wu, cols):
        g, b = cols[:, 2], cols[:, 3]
        terms = []
        for v in (g, b):
            t = lax.reduce_precision(v, 8, 7)
            terms += [t, v - t]
        terms = jnp.stack(terms).astype(bf16)
        out = []
        for w in (wg, wu):
            p = dot(w, terms, LAST)
            out.append(jnp.stack([p[:, 0] + p[:, 1], p[:, 2] + p[:, 3]]).reshape(2, Y, S, ffb))
        return jnp.concatenate(out, axis=0)

    gains = do(gain_products, wg, wu, pair_cols)
    for axis, step in at.steps(False):
        ax = {"y": 1, "s": 2}[axis]
        bit = (at.index(axis) // step) % 2
        send = lax.dynamic_slice_in_dim(gains, (1 - bit) * step, step, ax)
        kept = lax.dynamic_slice_in_dim(gains, bit * step, step, ax)
        gains = do(lambda a, b: a + b, kept, at.along(send, axis, step))
    gains = do(lambda g: g.reshape(4, ffb, 1), gains)
    cot_finish()
    cot_c = do(lambda x: x, cot_done())

    def all_cotangents(mine, theirs):
        both = in_order(mine.reshape(Y, S, rows, width), theirs.reshape(Y, S, rows, width), 2)
        return both.transpose(1, 0, 2, 3, 4).reshape(T, width)

    cot_all = do(all_cotangents, cot_c, at.core(cot_c))
    grad_act = do(lambda w, c: dot(w, c, LAST), wd_own, cot_all)
    cot_cols = do(lambda c: lax.dynamic_slice_in_dim(c, my_block * blk, blk, 1).T, cot_all)
    flying = scatter_rest(flying)

    def gated(ga, gb, ua, ub, grad_act, gains):
        gate = ga[0].astype(f32) + gb[0].astype(f32)
        up = ua[0].astype(f32) + ub[0].astype(f32)
        sig = jax.nn.sigmoid(gate)
        silu = gate * sig
        ggate = (grad_act * up * sig * (1.0 + gate * (1.0 - sig))).astype(bf16)
        gup = (grad_act * silu).astype(bf16)
        return ggate, gup, (silu * up).astype(bf16), gate, up

    ggate, gup, act, gate, up = do(gated, *flying[0], *flying[1], grad_act, gains)

    def parts_of(count, want):
        return max(n for n in range(1, want + 1) if count % (16 * n) == 0)

    n_down, n_up, n_out, n_qkv = parts_of(ffb, 4), parts_of(blk, 2), parts_of(blk, 2), parts_of(blk, 4)

    def cut(g, n):
        r = g.shape[0] // n
        return [g[i * r : (i + 1) * r] for i in range(n)]

    def quarter_heads(x):
        return [x[:, h][None, None] for h in halves]

    n, start, finish, gate_all = gather_steps(quarter_heads(ggate), 3)
    start(0)
    g_down = do(lambda a, c: dot(a, c, PLAIN).astype(bf16), act, cot_all)
    for i, g in enumerate(cut(g_down, n_down)):
        reps.push(("down", i), g)
    reps.tick()

    def norm_sums2(ggate, gup, gate, up, gains):
        a, b = ggate.astype(f32), gup.astype(f32)
        e = jnp.sum(a * gains[0] + b * gains[2], axis=0, keepdims=True)
        ez = jnp.sum(a * (gate - gains[1]) + b * (up - gains[3]), axis=0, keepdims=True)
        return join(e, ez)

    sums = do(norm_sums2, ggate, gup, gate, up, gains)
    steps2 = at.steps(False) + [("core", 1)]

    def sum_step(sums, axis, step):
        other = at.core(sums) if axis == "core" else at.along(sums, axis, step)
        return do(lambda a, b: a + b, sums, other)

    finish()
    start(1)
    reps.tick()
    for axis, step in steps2:
        sums = sum_step(sums, axis, step)
    reps.tick()
    for i in range(2, n):
        finish()
        start(i)
    n, start_up, finish_up, up_all = gather_steps(quarter_heads(gup), 3)
    finish()
    start_up(0)
    reps.tick()
    ggate_all = do(lambda x: x.reshape(Y * S * ffb, T), gate_all())
    part_gate = do(lambda w, g: dot(w, g, FIRST), wg, ggate_all)
    g_gate = do(lambda x, g: dot(x, g, LAST).astype(bf16), xn2, ggate_all)

    def push_pairs(name, g, n):
        r = g.shape[0] // (2 * n)
        for i in range(n):
            reps.push((name, "theirs", i), g[(n + i) * r : (n + i + 1) * r])
            reps.push((name, "mine", i), g[i * r : (i + 1) * r])

    push_pairs("gate", g_gate, n_up)
    finish_up()
    for i in range(1, n):
        start_up(i)
        reps.tick()
        if i == 1:
            out_part = do(lambda w, a: dot(w, a, FIRST).astype(bf16), wd_own, act).reshape(Y, 2, S, blk, T)
            reps.tick()
        finish_up()
    gup_all = do(lambda x: x.reshape(Y * S * ffb, T), up_all())
    part = do(lambda w, g, p: dot(w, g, FIRST) + p, wu, gup_all, part_gate)
    part_theirs = at.core(part[blk:])
    reps.tick()

    def branch(a, b, cot, z, scale, gain, sums):
        gxn2 = a + b
        e = gxn2 * gain
        grad_hidden = cot.astype(f32) + scale * (e - sums[0:1] / width - z * (sums[1:2] / width))
        return grad_hidden.astype(bf16), grad_hidden, gxn2

    grad_branch, grad_hidden, gxn2 = do(
        branch, part[:blk], part_theirs, cot_cols, z2, inv2, own_cols[:, 2:3], sums
    )
    n, start, finish, branch_all = gather_steps(quarter_heads(grad_branch), 3)
    start(0)
    g_up = do(lambda x, g: dot(x, g, LAST).astype(bf16), xn2, gup_all)
    push_pairs("up", g_up, n_up)
    finish()
    for i in range(1, n):
        start(i)
        if i == 1:
            reps.tick()
        finish()
    gbr_c = do(lambda x: x, branch_all())
    gbr_o = at.core(gbr_c)
    gbr = do(lambda a, b: in_order(a, b, 1).reshape(width, T), gbr_c, gbr_o)
    grad_attn = do(lambda w, g: dot(w, g, PLAIN).astype(bf16), wo_own, gbr)

    gqkvs = []
    for k in range(2):
        sq = seqs[k]
        gqkvs.append(
            do(
                attend_back,
                qkvs[k],
                grad_attn[:, halves[k]].reshape(heads, HEAD_DIM, H),
                peaks[k],
                totals[k],
                cos[sq],
                sin[sq],
                prow[sq],
                pcol[sq],
            ).reshape(3, blk, H)
        )
        if k == 0:
            reps.tick()
    n, start, finish, gqkv_done = gather_steps([g.reshape(1, 1, 3 * blk, H) for g in gqkvs], 3)
    start(0)
    attn = lanes(*attns)
    g_out = do(lambda a, g: dot(a, g, LAST).astype(bf16), attn, gbr)
    for i, g in enumerate(cut(g_out, n_out)):
        reps.push(("out", i), g)
    reps.tick()
    finish()
    for i in range(1, n):
        start(i)
        if i == 1:
            reps.tick()
            reps.tick()
        finish()

    def qkv_columns(x):
        return x.reshape(Y, S, 3, blk, T).transpose(2, 0, 1, 3, 4).reshape(3 * Y * S * blk, T)

    gqkv = do(qkv_columns, gqkv_done())
    g_qkv = do(lambda x, g: dot(x, g, LAST).astype(bf16), xn1, gqkv)
    push_pairs("qkv", g_qkv, n_qkv)
    reps.tick()
    part = do(lambda w, g: dot(w, g, FIRST), wq, gqkv)
    part_theirs = at.core(part[blk:])

    jobs = []
    results = {"down": None, "out": None, "up": None, "qkv": None}
    states = {
        "down": (w_down, m_down, v_down),
        "out": (w_out, m_out, v_out),
        "up": (w_up, m_up, v_up),
        "qkv": (w_qkv, m_qkv, v_qkv),
    }
    rates = {"down": 0.02, "out": 0.2, "up": 0.03, "qkv": 0.03}
    received = {}
    for i in range(n_down):
        jobs.append(("down", [("down", i)], i, 0, min(512, width)))
    for part_name, lead in (("gate", 0), ("up", Y)):
        for i in range(n_up):
            jobs.append(("up", [(part_name, "mine", i), (part_name, "theirs", i)], i, lead, S * ffb))
    for i in range(n_out):
        jobs.append(("out", [("out", i)], i, 0, min(512, width)))
    for i in range(n_qkv):
        jobs.append(("qkv", [("qkv", "mine", i), ("qkv", "theirs", i)], i, 0, S * blk))

    def exchange():
        for name in list(reps.done):
            if name[1] == "theirs" and name not in received:
                received[name] = at.core(reps.done[name])

    def update(limit):
        exchange()
        while jobs and limit:
            name, needs, i, lead, unit = jobs[0]
            if not all(k in reps.done for k in needs):
                return
            grads = [received[k] if k[1] == "theirs" else reps.done[k] for k in needs]
            results[name] = do(
                lambda s, g, prev: adam_part(s, g, core, rates[name], prev, i, lead, unit),
                states[name],
                grads,
                results[name],
            )
            jobs.pop(0)
            limit -= 1

    reps.tick()

    def first_back(a, b, x, mean, inv, gain, gxn2, z2, gqkv0, gqkv1):
        gxn1 = a + b
        z1 = (x.astype(f32) - mean) * inv
        e = gxn1 * gain
        sums = join(jnp.sum(e, axis=0, keepdims=True), jnp.sum(e * z1, axis=0, keepdims=True))
        small = jnp.concatenate(
            [
                jnp.sum(gxn1 * z1, axis=1)[None],
                jnp.sum(gxn1, axis=1)[None],
                jnp.sum(gxn2 * z2, axis=1)[None],
                jnp.sum(gxn2, axis=1)[None],
                jnp.sum(gqkv0.astype(f32), axis=2) + jnp.sum(gqkv1.astype(f32), axis=2),
            ],
            axis=0,
        )
        return sums, small, gxn1, z1

    sums, small, gxn1, z1 = do(
        first_back, part[:blk], part_theirs, x_own, mean1, inv1, own_cols[:, 0:1], gxn2, z2, *gqkvs
    )
    for axis, step in steps2:
        sums = sum_step(sums, axis, step)
    input_grad = do(
        lambda h, grad, z, scale, gain, sums: h
        + scale * (grad * gain - sums[0:1] / width - z * (sums[1:2] / width)),
        grad_hidden,
        gxn1,
        z1,
        inv1,
        own_cols[:, 0:1],
        sums,
    )
    reps.tick()

    def to_rows(cols):
        split = do(lambda c: c.reshape(blk, S, at.ctx_size, rows).transpose(2, 1, 0, 3).reshape(nb, blk, rows), cols)
        got = lax.all_to_all(split, plane, split_axis=0, concat_axis=0, tiled=True)
        return do(lambda g: g.reshape(width, rows).T, got)

    out_theirs = at.core(pick(out_part, 1, 1 - at.c))
    input_rows = to_rows(input_grad)
    reps.tick()
    update(2)
    flying = []
    out_sum = do(
        lambda a, b: (a.astype(f32) + b.astype(f32)).astype(bf16)[None], pick(out_part, 1, at.c), out_theirs
    )
    for k in range(2):
        axis, step, ax, bit = first_step(bool(k))
        p = out_sum[..., halves[k]]
        send = lax.dynamic_slice_in_dim(p, (1 - bit) * step, step, ax)
        flying.append((lax.dynamic_slice_in_dim(p, bit * step, step, ax), at.along(send, axis, step)))
    reps.tick()
    update(2)
    flying = scatter_rest(flying)

    def output(hidden, a0, b0, a1, b1):
        a, b = lanes(a0[0], a1[0]), lanes(b0[0], b1[0])
        return (hidden + (a.astype(f32) + b.astype(f32))).astype(bf16)

    reps.tick()
    update(2)
    block_output = to_rows(do(output, hidden, *flying[0], *flying[1]))
    reps.tick()
    update(2)

    n_rep = lax.axis_size("rep")
    step = 1
    while step < n_rep:
        other = lax.ppermute(small, "rep", [(i, i ^ step) for i in range(n_rep)])
        small = do(lambda a, b: a + b, small, other)
        step *= 2
    reps.tick()
    update(2)
    sent = do(lambda s: jnp.broadcast_to(s.reshape(1, 7, blk), (nb, 7, blk)), small)
    got = lax.all_to_all(sent, plane, split_axis=0, concat_axis=0, tiled=True)
    norm_grad = got.transpose(1, 0, 2).reshape(7, width)
    mn, vn, wn = do(lambda *a: adam_update(*a, 0.3, 0.0), norm_params, m_norm, v_norm, norm_grad)

    while reps.busy():
        reps.tick()
        update(2)
    update(len(jobs))
    return (
        (block_output.reshape(tokens.shape), input_rows.reshape(tokens.shape))
        + tuple(results["qkv"])
        + tuple(results["out"])
        + tuple(results["up"])
        + tuple(results["down"])
        + (mn, vn, wn)
    )


def solution(mesh):
    tok = P("rep", "ctx", "shard", None)
    row = P(("ctx", "shard"), None)
    placed = (tok, tok, P("rep", "shard", None)) + (row,) * 4 + (P(),) + (row,) * 8 + (P(), P())
    return jax.shard_map(
        body,
        mesh=mesh,
        in_specs=placed,
        out_specs=(tok, tok) + (row,) * 12 + (P(),) * 3,
        check_vma=False,
    )
```

time: 1080 us -> 945 us (0.88)
  waiting for transfers between devices: 418 us -> 299 us
  Pallas kernels: 65.9 us -> 96.5 us
  starting transfers between devices: 236 us -> 207 us
  other arithmetic: 150 us -> 122 us
    ppermute x75 -> x54, waiting for transfers between devices: 213 us -> 121 us  [the longest x14 75 us: tick(): lax.ppermute(out['send'], 'rep', [(0, 1), (1, 0), (2, 3), (3, 2)])]
    ppermute x75 -> x54, starting transfers between devices: 179 us -> 138 us  [the longest x8 62.5 us: tick(): o['in_got'] = lax.ppermute(out['new'], 'rep', [(0, 1), (3, 2)])]
    pallas_call x2 -> x14, Pallas kernels: 41.6 us -> 69.7 us  [adam_part(): pl.pallas_call(functools.partial(adam_kernel, rate, two), grid_spec=pltpu...]
    concatenate x33 -> x24, other arithmetic: 34 us -> 8.31 us  [the longest x5 4.53 us: result(): return jnp.concatenate(state['parts'], axis=row_axis)]
    dynamic_update_slice x22 -> x0, local copies, waits for them, and re-layouts: 22.7 us -> none  [the longest x8 17.2 us: rows_done(): buf = lax.dynamic_update_slice(buf, v[None, :, None], (y, 0, s, 0, 0))]
    ppermute x25 -> x22, waiting for transfers between devices: 76.4 us -> 54.3 us  [along(): lax.ppermute(x, 'ctx', [(i, i ^ 2 * step) for i in range(self.ctx_size)])]
    ppermute x25 -> x22, waiting for transfers between devices: 126 us -> 105 us  [along(): return lax.ppermute(x, 'shard', [(i, i ^ step) for i in range(self.s_size)])]
    select_n x48 -> x56, other arithmetic: 22 us -> 41 us  [the longest x22 20.8 us: stage(): out['out'] = jnp.where(self.end, v['t_got'], v['t'])]
  transfers between devices with their start and end apart: 147 -> 126, of which waited for: 55 -> 50; matrix products, arithmetic and copies ran while one was open for 26% -> 26% of each run, Pallas kernels for 5% -> 9%
where the time goes in v3:
time: 945 us; the launch traced here: 931 us
  waiting for transfers between devices  299 us (32%)
  starting transfers between devices  207 us (22%)
  local copies, waits for them, and re-layouts  137 us (14%)
  other arithmetic  122 us (13%)
  Pallas kernels  96.5 us (10%)
  matrix products  65.5 us (7%)
    ppermute x22, waiting for transfers between devices, along(): return lax.ppermute(x, 'shard', [(i, i ^ step) for i in range(self.s_size)])  105 us
    ppermute x14, waiting for transfers between devices, tick(): lax.ppermute(out['send'], 'rep', [(0, 1), (1, 0), (2, 3), (3, 2)])  75 us
    pallas_call x14, Pallas kernels, adam_part(): pl.pallas_call(functools.partial(adam_kernel, rate, two), grid_spec=pltpu...  69.7 us
    dot_general x23, matrix products, dot(): return lax.dot_general(a, b, dims, preferred_element_type=f32)  65.5 us
    ppermute x8, starting transfers between devices, tick(): o['in_got'] = lax.ppermute(out['new'], 'rep', [(0, 1), (3, 2)])  62.5 us
    ppermute x22, waiting for transfers between devices, along(): lax.ppermute(x, 'ctx', [(i, i ^ 2 * step) for i in range(self.ctx_size)])  54.3 us
    unnamed x298, local copies, waits for them, and re-layouts  52.1 us
    ppermute x14, starting transfers between devices, tick(): lax.ppermute(out['send'], 'rep', [(0, 1), (1, 0), (2, 3), (3, 2)])  42.2 us
  transfers between devices with their start and end apart: 126, of which 50 were waited for; matrix products, arithmetic and copies ran while one was open for 26% of the time, Pallas kernels for 9%

profile of v3, /device:TPU:0, one launch (start us, length us, event | category | flops | bytes accessed | tf_op | source)
XLA Modules:
  0.0 930.6 jit_solution(4408117874213069320)
XLA Ops:
  11.4 4.8 all-to-all-start
  53.2 4.3 copy-done
  66.2 19.5 %collective-permute-done.3 = bf16[3,2,1,256,512]{4,3,0,2,1:T(8,128)(2,1)} collective-permute-done((bf16[3,2,1,256,512]{4,3,0,2,1:T(8,128)(2,1)}, bf16[3,2,1,256,512]{4,3,0,2,1:T(8,128)(2,1)}, u32[]{:S(2)}, u32[]{:S(2)}) %collective-permute-start.3) | collective-permute-done | bytes 1572896 | tf_op jit(solution)/shard_map/ppermute | solution.py:62
  97.9 10.0 %collective-permute-done.5 = bf16[3,1,1,256,512]{4,3,0,2,1:T(8,128)(2,1)S(1)} collective-permute-done((bf16[3,1,1,256,512]{4,3,0,2,1:T(8,128)(2,1)S(1)}, bf16[3,1,1,256,512]{4,3,0,2,1:T(8,128)(2,1)S(1)}, u32[]{:S(2)}, u32[]{:S(2)}) %collective-permute-start.5) | collective-permute-done | bytes 786464 | tf_op jit(solution)/shard_map/ppermute | solution.py:61
  123.0 4.9 shard_map.310
  134.1 10.5 %collective-permute-done.10 = bf16[1,2,1,256,512]{4,3,2,1,0:T(8,128)(2,1)S(1)} collective-permute-done((bf16[1,2,1,256,512]{4,3,2,1,0:T(8,128)(2,1)S(1)}, bf16[1,2,1,256,512]{4,3,2,1,0:T(8,128)(2,1)S(1)}, u32[]{:S(2)}, u32[]{:S(2)}) %collective-permute-start.10) | collective-permute-done | bytes 524320 | tf_op jit(solution)/shard_map/ppermute | solution.py:62
  149.5 5.5 collective-permute-done.14
  217.2 11.1 %copy.153 = bf16[2,2,2,128,2048]{3,2,1,0,4:T(2,128)(2,1)} copy(bf16[2,2,2,128,2048]{4,3,0,1,2:T(8,128)(2,1)} %maximum_bitcast_fusion) | data formatting | bytes 8388608 | tf_op jit(solution)/shard_map/transpose | solution.py:684
  228.4 7.7 reshape.569
  236.1 7.9 fusion.58
  245.9 27.0 %collective-permute-done.21 = bf16[1,2,1,704,1024]{4,3,2,1,0:T(8,128)(2,1)} collective-permute-done((bf16[1,2,1,704,1024]{4,3,2,1,0:T(8,128)(2,1)}, bf16[1,2,1,704,1024]{4,3,2,1,0:T(8,128)(2,1)}, u32[]{:S(2)}, u32[]{:S(2)}) %collective-permute-start.21) | collective-permute-done | bytes 2883616 | tf_op jit(solution)/shard_map/ppermute | solution.py:62
  287.5 29.6 %collective-permute-done.29 = bf16[1,1,1,704,1024]{4,3,2,1,0:T(8,128)(2,1)} collective-permute-done((bf16[1,1,1,704,1024]{4,3,2,1,0:T(8,128)(2,1)}, bf16[1,1,1,704,1024]{4,3,2,1,0:T(8,128)(2,1)}, u32[]{:S(2)}, u32[]{:S(2)}) %collective-permute-start.29) | collective-permute-done | bytes 1441824 | tf_op jit(solution)/shard_map/ppermute | solution.py:62
  339.4 4.4 collective-permute-done.32
  345.8 4.4 collective-permute-done.30
  350.2 4.6 collective-permute-start.33
  368.5 22.8 %collective-permute-done.41 = bf16[1,2,704,512]{3,2,1,0:T(8,128)(2,1)S(1)} collective-permute-done((bf16[1,2,704,512]{3,2,1,0:T(8,128)(2,1)S(1)}, bf16[1,2,704,512]{3,2,1,0:T(8,128)(2,1)S(1)}, u32[]{:S(2)}, u32[]{:S(2)}) %collective-permute-start.41) | collective-permute-done | bytes 1441824 | tf_op jit(solution)/shard_map/ppermute | solution.py:61
  395.0 11.2 %collective-permute-done.38 = bf16[176,2048]{1,0:T(8,128)(2,1)S(1)} collective-permute-done((bf16[176,2048]{1,0:T(8,128)(2,1)S(1)}, bf16[176,2048]{1,0:T(8,128)(2,1)S(1)}, u32[]{:S(2)}, u32[]{:S(2)}) %collective-permute-start.38) | collective-permute-done | bytes 720928 | tf_op jit(solution)/shard_map/ppermute | solution.py:188
  426.1 4.7 collective-permute-start.49
  448.0 11.1 %collective-permute-start.53 = (bf16[128,2816]{1,0:T(8,128)(2,1)S(1)}, bf16[128,2816]{1,0:T(8,128)(2,1)S(1)}, u32[]{:S(2)}, u32[]{:S(2)}) collective-permute-start(bf16[128,2816]{1,0:T(8,128)(2,1)S(1)} %get-tuple-element.791), channel_id=1, source_target_pairs={{0,8},{24,16},{1,9},{25,17},{2,10},{26,18},{3,11},{27,19},{4,12},{... | collective-permute-start | bytes 2162696 | tf_op jit(solution)/shard_map/ppermute | solution.py:191
  466.4 6.6 collective-permute-done.53
  493.6 6.6 collective-permute-done.59
  515.4 5.1 shard_map.311
  521.6 4.4 collective-permute-done.63
  529.4 5.1 shard_map.312
  545.2 12.5 %collective-permute-done.67 = bf16[128,2816]{1,0:T(8,128)(2,1)S(1)} collective-permute-done((bf16[128,2816]{1,0:T(8,128)(2,1)S(1)}, bf16[128,2816]{1,0:T(8,128)(2,1)S(1)}, u32[]{:S(2)}, u32[]{:S(2)}) %collective-permute-start.67) | collective-permute-done | bytes 720928 | tf_op jit(solution)/shard_map/ppermute | solution.py:188
  558.9 4.2 collective-permute-start.71
  567.6 9.8 %collective-permute-done.71 = bf16[128,2816]{1,0:T(8,128)(2,1)S(1)} collective-permute-done((bf16[128,2816]{1,0:T(8,128)(2,1)S(1)}, bf16[128,2816]{1,0:T(8,128)(2,1)S(1)}, u32[]{:S(2)}, u32[]{:S(2)}) %collective-permute-start.71) | collective-permute-done | bytes 720928 | tf_op jit(solution)/shard_map/ppermute | solution.py:188
  578.5 4.2 collective-permute-start.73
  583.7 12.5 %collective-permute-done.73 = bf16[128,2816]{1,0:T(8,128)(2,1)S(1)} collective-permute-done((bf16[128,2816]{1,0:T(8,128)(2,1)S(1)}, bf16[128,2816]{1,0:T(8,128)(2,1)S(1)}, u32[]{:S(2)}, u32[]{:S(2)}) %collective-permute-start.73) | collective-permute-done | bytes 720928 | tf_op jit(solution)/shard_map/ppermute | solution.py:188
  630.8 4.4 collective-permute-done.79
  635.2 7.8 collective-permute-start.80
  660.6 18.2 %collective-permute-start.87 = (bf16[64,3072]{1,0:T(8,128)(2,1)}, bf16[64,3072]{1,0:T(8,128)(2,1)}, u32[]{:S(2)}, u32[]{:S(2)}) collective-permute-start(bf16[64,3072]{1,0:T(8,128)(2,1)} %get-tuple-element.929), channel_id=1, source_target_pairs={{0,8},{24,16},{1,9},{25,17},{2,10},{26,18},{3,11},{27,19},{4,12},{... | collective-permute-start | bytes 1179656 | tf_op jit(solution)/shard_map/ppermute | solution.py:191
  681.6 4.4 all-to-all-start.1
  693.0 7.9 all-to-all-done.1
  703.5 8.4 collective-permute-start.91
  738.8 5.4 collective-permute-done.93
  771.6 8.0 shard_map.317
  779.6 8.0 shard_map.318
  809.0 4.3 copy-done.1
  813.3 7.2 shard_map.319
  820.4 7.9 shard_map.320
  857.5 7.3 collective-permute-done.109
  878.9 5.3 shard_map.323
  884.2 5.4 shard_map.324
  893.4 8.3 collective-permute-done.115
  904.0 5.4 shard_map.325
  914.8 10.2 %collective-permute-done.120 = bf16[64,3072]{1,0:T(8,128)(2,1)S(1)} collective-permute-done((bf16[64,3072]{1,0:T(8,128)(2,1)S(1)}, bf16[64,3072]{1,0:T(8,128)(2,1)S(1)}, u32[]{:S(2)}, u32[]{:S(2)}) %collective-permute-start.120) | collective-permute-done | bytes 393248 | tf_op jit(solution)/shard_map/ppermute | solution.py:193
  925.1 5.4 shard_map.326
  (813 shorter events, 510.7 us)
Async XLA Ops:
  49.0 36.7 %collective-permute-start.3 = (bf16[3,2,1,256,512]{4,3,0,2,1:T(8,128)(2,1)}, bf16[3,2,1,256,512]{4,3,0,2,1:T(8,128)(2,1)}, u32[]{:S(2)}, u32[]{:S(2)}) collective-permute-start(bf16[3,2,1,256,512]{4,3,0,2,1:T(8,128)(2,1)} %copy.143), channel_id=1, source_target_pairs={{0,1},{1,0},{2,3},{3,2},{4,5},{5,4},{6,7},{7,6},{8,9},{9,8},{10,11... | collective-permute-start | bytes 4718600 | tf_op jit(solution)/shard_map/ppermute | solution.py:62
  49.9 39.8 %collective-permute-start.7 = (bf16[3,1,2,256,512]{4,3,0,2,1:T(8,128)(2,1)}, bf16[3,1,2,256,512]{4,3,0,2,1:T(8,128)(2,1)}, u32[]{:S(2)}, u32[]{:S(2)}) collective-permute-start(bf16[3,1,2,256,512]{4,3,0,2,1:T(8,128)(2,1)} %copy.146), channel_id=1, source_target_pairs={{0,4},{2,6},{4,0},{6,2},{1,5},{3,7},{5,1},{7,3},{8,12},{10,14},{12... | collective-permute-start | bytes 4718600 | tf_op jit(solution)/shard_map/ppermute | solution.py:61
  59.6 34.1 %collective-permute-start.6 = (bf16[2816,256]{1,0:T(8,128)(2,1)}, bf16[2816,256]{1,0:T(8,128)(2,1)}, u32[]{:S(2)}, u32[]{:S(2)}) collective-permute-start(bf16[2816,256]{1,0:T(8,128)(2,1)} %get-tuple-element.614), channel_id=1, source_target_pairs={{0,2},{2,0},{4,6},{6,4},{1,3},{3,1},{5,7},{7,5},{8,10},{10,8},{12,... | collective-permute-start | bytes 4325384 | tf_op jit(solution)/shard_map/ppermute | solution.py:57
  92.8 26.5 %collective-permute-start.9 = (bf16[3,1,1,256,512]{4,3,0,2,1:T(8,128)(2,1)}, bf16[3,1,1,256,512]{4,3,0,2,1:T(8,128)(2,1)}, u32[]{:S(2)}, u32[]{:S(2)}) collective-permute-start(bf16[3,1,1,256,512]{4,3,0,2,1:T(8,128)(2,1)} %get-tuple-element.1256), channel_id=1, source_target_pairs={{0,1},{1,0},{2,3},{3,2},{4,5},{5,4},{6,7},{7,6},{8,9},{9,8},{10,11... | collective-permute-start | bytes 2359304 | tf_op jit(solution)/shard_map/ppermute | solution.py:62
  207.7 65.2 %collective-permute-start.21 = (bf16[1,2,1,704,1024]{4,3,2,1,0:T(8,128)(2,1)}, bf16[1,2,1,704,1024]{4,3,2,1,0:T(8,128)(2,1)}, u32[]{:S(2)}, u32[]{:S(2)}) collective-permute-start(bf16[1,2,1,704,1024]{4,3,2,1,0:T(8,128)(2,1)} %bitcast.72), channel_id=1, source_target_pairs={{0,1},{1,0},{2,3},{3,2},{4,5},{5,4},{6,7},{7,6},{8,9},{9,8},{10,11... | collective-permute-start | bytes 8650760 | tf_op jit(solution)/shard_map/ppermute | solution.py:62
  209.0 68.5 %collective-permute-start.28 = (bf16[1,1,2,704,1024]{4,3,2,1,0:T(8,128)(2,1)}, bf16[1,1,2,704,1024]{4,3,2,1,0:T(8,128)(2,1)}, u32[]{:S(2)}, u32[]{:S(2)}) collective-permute-start(bf16[1,1,2,704,1024]{4,3,2,1,0:T(8,128)(2,1)} %bitcast.84), channel_id=1, source_target_pairs={{0,4},{2,6},{4,0},{6,2},{1,5},{3,7},{5,1},{7,3},{8,12},{10,14},{12... | collective-permute-start | bytes 8650760 | tf_op jit(solution)/shard_map/ppermute | solution.py:61
  283.5 33.5 %collective-permute-start.29 = (bf16[1,1,1,704,1024]{4,3,2,1,0:T(8,128)(2,1)}, bf16[1,1,1,704,1024]{4,3,2,1,0:T(8,128)(2,1)}, u32[]{:S(2)}, u32[]{:S(2)}) collective-permute-start(bf16[1,1,1,704,1024]{4,3,2,1,0:T(8,128)(2,1)} %get-tuple-element.1237), channel_id=1, source_target_pairs={{0,1},{1,0},{2,3},{3,2},{4,5},{5,4},{6,7},{7,6},{8,9},{9,8},{10,11... | collective-permute-start | bytes 4325384 | tf_op jit(solution)/shard_map/ppermute | solution.py:62
  284.9 33.3 %collective-permute-start.27 = (bf16[1,1,1,704,1024]{4,3,2,1,0:T(8,128)(2,1)}, bf16[1,1,1,704,1024]{4,3,2,1,0:T(8,128)(2,1)}, u32[]{:S(2)}, u32[]{:S(2)}) collective-permute-start(bf16[1,1,1,704,1024]{4,3,2,1,0:T(8,128)(2,1)} %get-tuple-element.1239), channel_id=1, source_target_pairs={{0,4},{2,6},{4,0},{6,2},{1,5},{3,7},{5,1},{7,3},{8,12},{10,14},{12... | collective-permute-start | bytes 4325384 | tf_op jit(solution)/shard_map/ppermute | solution.py:61
  344.4 49.0 %collective-permute-start.40 = (bf16[2,1,704,512]{3,2,1,0:T(8,128)(2,1)S(1)}, bf16[2,1,704,512]{3,2,1,0:T(8,128)(2,1)S(1)}, u32[]{:S(2)}, u32[]{:S(2)}) collective-permute-start(bf16[2,1,704,512]{3,2,1,0:T(8,128)(2,1)S(1)} %pad_maximum_fusion.3), channel_id=1, source_target_pairs={{0,1},{1,0},{2,3},{3,2},{4,5},{5,4},{6,7},{7,6},{8,9},{9,8},{10,11... | collective-permute-start | bytes 4325384 | tf_op jit(solution)/shard_map/ppermute | solution.py:62
  356.8 34.6 %collective-permute-start.41 = (bf16[1,2,704,512]{3,2,1,0:T(8,128)(2,1)S(1)}, bf16[1,2,704,512]{3,2,1,0:T(8,128)(2,1)S(1)}, u32[]{:S(2)}, u32[]{:S(2)}) collective-permute-start(bf16[1,2,704,512]{3,2,1,0:T(8,128)(2,1)S(1)} %pad_maximum_fusion.4), channel_id=1, source_target_pairs={{0,4},{2,6},{4,0},{6,2},{1,5},{3,7},{5,1},{7,3},{8,12},{10,14},{12... | collective-permute-start | bytes 4325384 | tf_op jit(solution)/shard_map/ppermute | solution.py:61
  361.3 57.9 %collective-permute-start.45 = (bf16[1,1,704,512]{3,2,1,0:T(8,128)(2,1)S(1)}, bf16[1,1,704,512]{3,2,1,0:T(8,128)(2,1)S(1)}, u32[]{:S(2)}, u32[]{:S(2)}) collective-permute-start(bf16[1,1,704,512]{3,2,1,0:T(8,128)(2,1)S(1)} %get-tuple-element.754), channel_id=1, source_target_pairs={{0,1},{1,0},{2,3},{3,2},{4,5},{5,4},{6,7},{7,6},{8,9},{9,8},{10,11... | collective-permute-start | bytes 2162696 | tf_op jit(solution)/shard_map/ppermute | solution.py:62
  362.3 56.9 %collective-permute-start.44 = (bf16[1,1,704,512]{3,2,1,0:T(8,128)(2,1)S(1)}, bf16[1,1,704,512]{3,2,1,0:T(8,128)(2,1)S(1)}, u32[]{:S(2)}, u32[]{:S(2)}) collective-permute-start(bf16[1,1,704,512]{3,2,1,0:T(8,128)(2,1)S(1)} %get-tuple-element.747), channel_id=1, source_target_pairs={{0,4},{2,6},{4,0},{6,2},{1,5},{3,7},{5,1},{7,3},{8,12},{10,14},{12... | collective-permute-start | bytes 2162696 | tf_op jit(solution)/shard_map/ppermute | solution.py:61
  367.4 27.6 %collective-permute-start.39 = (bf16[176,2048]{1,0:T(8,128)(2,1)S(1)}, bf16[176,2048]{1,0:T(8,128)(2,1)S(1)}, u32[]{:S(2)}, u32[]{:S(2)}) collective-permute-start(bf16[176,2048]{1,0:T(8,128)(2,1)S(1)} %reduce-precision_convert_fusion.21), channel_id=1, source_target_pairs={{8,16},{16,8},{9,17},{17,9},{10,18},{18,10},{11,19},{19,11},{12,20... | collective-permute-start | bytes 2162696 | tf_op jit(solution)/shard_map/ppermute | solution.py:201
  419.5 28.6 %collective-permute-start.48 = (bf16[1,2,704,512]{3,2,1,0:T(8,128)(2,1)S(1)}, bf16[1,2,704,512]{3,2,1,0:T(8,128)(2,1)S(1)}, u32[]{:S(2)}, u32[]{:S(2)}) collective-permute-start(bf16[1,2,704,512]{3,2,1,0:T(8,128)(2,1)S(1)} %pad_maximum_fusion.6), channel_id=1, source_target_pairs={{0,4},{2,6},{4,0},{6,2},{1,5},{3,7},{5,1},{7,3},{8,12},{10,14},{12... | collective-permute-start | bytes 4325384 | tf_op jit(solution)/shard_map/ppermute | solution.py:61
  421.3 37.9 %collective-permute-start.47 = (bf16[2,1,704,512]{3,2,1,0:T(8,128)(2,1)S(1)}, bf16[2,1,704,512]{3,2,1,0:T(8,128)(2,1)S(1)}, u32[]{:S(2)}, u32[]{:S(2)}) collective-permute-start(bf16[2,1,704,512]{3,2,1,0:T(8,128)(2,1)S(1)} %pad_maximum_fusion.5), channel_id=1, source_target_pairs={{0,1},{1,0},{2,3},{3,2},{4,5},{5,4},{6,7},{7,6},{8,9},{9,8},{10,11... | collective-permute-start | bytes 4325384 | tf_op jit(solution)/shard_map/ppermute | solution.py:62
  444.2 285.2 %collective-permute-start.46 = (bf16[2,2,256,1024]{3,2,1,0:T(8,128)(2,1)}, bf16[2,2,256,1024]{3,2,1,0:T(8,128)(2,1)}, u32[]{:S(2)}, u32[]{:S(2)}) collective-permute-start(bf16[2,2,256,1024]{3,2,1,0:T(8,128)(2,1)} %get-tuple-element.1197), channel_id=1, source_target_pairs={{0,2},{2,0},{4,6},{6,4},{1,3},{3,1},{5,7},{7,5},{8,10},{10,8},{12,... | collective-permute-start | bytes 6291464 | tf_op jit(solution)/shard_map/ppermute | solution.py:57
  444.5 22.0 %collective-permute-start.55 = (bf16[176,2048]{1,0:T(8,128)(2,1)S(1)}, bf16[176,2048]{1,0:T(8,128)(2,1)S(1)}, u32[]{:S(2)}, u32[]{:S(2)}) collective-permute-start(bf16[176,2048]{1,0:T(8,128)(2,1)S(1)} %reduce-precision_convert_fusion.15), channel_id=1, source_target_pairs={{8,0},{16,24},{9,1},{17,25},{10,2},{18,26},{11,3},{19,27},{12,4},{... | collective-permute-start | bytes 2162696 | tf_op jit(solution)/shard_map/ppermute | solution.py:193
  445.9 20.5 %collective-permute-start.54 = (bf16[128,2816]{1,0:T(8,128)(2,1)S(1)}, bf16[128,2816]{1,0:T(8,128)(2,1)S(1)}, u32[]{:S(2)}, u32[]{:S(2)}) collective-permute-start(bf16[128,2816]{1,0:T(8,128)(2,1)S(1)} %reduce-precision_convert_fusion.16), channel_id=1, source_target_pairs={{8,16},{16,8},{9,17},{17,9},{10,18},{18,10},{11,19},{19,11},{12,20... | collective-permute-start | bytes 2162696 | tf_op jit(solution)/shard_map/ppermute | solution.py:201
  448.0 25.0 %collective-permute-start.53 = (bf16[128,2816]{1,0:T(8,128)(2,1)S(1)}, bf16[128,2816]{1,0:T(8,128)(2,1)S(1)}, u32[]{:S(2)}, u32[]{:S(2)}) collective-permute-start(bf16[128,2816]{1,0:T(8,128)(2,1)S(1)} %get-tuple-element.791), channel_id=1, source_target_pairs={{0,8},{24,16},{1,9},{25,17},{2,10},{26,18},{3,11},{27,19},{4,12},{... | collective-permute-start | bytes 2162696 | tf_op jit(solution)/shard_map/ppermute | solution.py:191
  473.2 19.4 %collective-permute-start.61 = (bf16[128,2816]{1,0:T(8,128)(2,1)S(1)}, bf16[128,2816]{1,0:T(8,128)(2,1)S(1)}, u32[]{:S(2)}, u32[]{:S(2)}) collective-permute-start(bf16[128,2816]{1,0:T(8,128)(2,1)S(1)} %reduce-precision_convert_fusion.13), channel_id=1, source_target_pairs={{8,16},{16,8},{9,17},{17,9},{10,18},{18,10},{11,19},{19,11},{12,20... | collective-permute-start | bytes 2162696 | tf_op jit(solution)/shard_map/ppermute | solution.py:201
  507.0 19.0 %collective-permute-start.63 = (bf16[128,2816]{1,0:T(8,128)(2,1)}, bf16[128,2816]{1,0:T(8,128)(2,1)}, u32[]{:S(2)}, u32[]{:S(2)}) collective-permute-start(bf16[128,2816]{1,0:T(8,128)(2,1)} %get-tuple-element.1177), channel_id=1, source_target_pairs={{0,8},{8,0},{16,24},{24,16},{1,9},{9,1},{17,25},{25,17},{2,10},{10... | collective-permute-start | bytes 2162696 | tf_op jit(solution)/shard_map/ppermute | solution.py:188
  520.6 43.4 %collective-permute-start.65 = (bf16[1,1,768,512]{3,2,1,0:T(8,128)(2,1)S(1)}, bf16[1,1,768,512]{3,2,1,0:T(8,128)(2,1)}, u32[]{:S(2)}, u32[]{:S(2)}) collective-permute-start(bf16[1,1,768,512]{3,2,1,0:T(8,128)(2,1)S(1)} %bitcast.277), channel_id=1, source_target_pairs={{0,4},{2,6},{4,0},{6,2},{1,5},{3,7},{5,1},{7,3},{8,12},{10,14},{12... | collective-permute-start | bytes 2359304 | tf_op jit(solution)/shard_map/ppermute | solution.py:61
  538.4 19.3 %collective-permute-start.67 = (bf16[128,2816]{1,0:T(8,128)(2,1)S(1)}, bf16[128,2816]{1,0:T(8,128)(2,1)S(1)}, u32[]{:S(2)}, u32[]{:S(2)}) collective-permute-start(bf16[128,2816]{1,0:T(8,128)(2,1)S(1)} %get-tuple-element.1175), channel_id=1, source_target_pairs={{0,8},{8,0},{16,24},{24,16},{1,9},{9,1},{17,25},{25,17},{2,10},{10... | collective-permute-start | bytes 2162696 | tf_op jit(solution)/shard_map/ppermute | solution.py:188
  541.9 22.1 %collective-permute-start.66 = (bf16[1,1,768,512]{3,2,1,0:T(8,128)(2,1)S(1)}, bf16[1,1,768,512]{3,2,1,0:T(8,128)(2,1)S(1)}, u32[]{:S(2)}, u32[]{:S(2)}) collective-permute-start(bf16[1,1,768,512]{3,2,1,0:T(8,128)(2,1)S(1)} %bitcast.280), channel_id=1, source_target_pairs={{0,1},{1,0},{2,3},{3,2},{4,5},{5,4},{6,7},{7,6},{8,9},{9,8},{10,11... | collective-permute-start | bytes 2359304 | tf_op jit(solution)/shard_map/ppermute | solution.py:62
  564.3 39.5 %collective-permute-start.70 = (bf16[1,2,768,512]{3,2,1,0:T(8,128)(2,1)S(1)}, bf16[1,2,768,512]{3,2,1,0:T(8,128)(2,1)S(1)}, u32[]{:S(2)}, u32[]{:S(2)}) collective-permute-start(bf16[1,2,768,512]{3,2,1,0:T(8,128)(2,1)S(1)} %pad_maximum_fusion.2), channel_id=1, source_target_pairs={{0,4},{2,6},{4,0},{6,2},{1,5},{3,7},{5,1},{7,3},{8,12},{10,14},{12... | collective-permute-start | bytes 4718600 | tf_op jit(solution)/shard_map/ppermute | solution.py:61
  566.7 37.1 %collective-permute-start.69 = (bf16[2,1,768,512]{3,2,1,0:T(8,128)(2,1)S(1)}, bf16[2,1,768,512]{3,2,1,0:T(8,128)(2,1)S(1)}, u32[]{:S(2)}, u32[]{:S(2)}) collective-permute-start(bf16[2,1,768,512]{3,2,1,0:T(8,128)(2,1)S(1)} %pad_maximum_fusion.1), channel_id=1, source_target_pairs={{0,1},{1,0},{2,3},{3,2},{4,5},{5,4},{6,7},{7,6},{8,9},{9,8},{10,11... | collective-permute-start | bytes 4718600 | tf_op jit(solution)/shard_map/ppermute | solution.py:62
  630.8 137.4 %collective-permute-start.98 = (bf16[128,2816]{1,0:T(8,128)(2,1)}, bf16[128,2816]{1,0:T(8,128)(2,1)}, u32[]{:S(2)}, u32[]{:S(2)}) collective-permute-start(bf16[128,2816]{1,0:T(8,128)(2,1)} %broadcast_select_fusion.28), channel_id=1, source_target_pairs={{0,2},{2,0},{4,6},{6,4},{1,3},{3,1},{5,7},{7,5},{8,10},{10,8},{12,... | collective-permute-start | bytes 2162696 | tf_op jit(solution)/shard_map/ppermute | solution.py:57
  635.2 24.6 %collective-permute-start.80 = (bf16[128,2048]{1,0:T(8,128)(2,1)}, bf16[128,2048]{1,0:T(8,128)(2,1)}, u32[]{:S(2)}, u32[]{:S(2)}) collective-permute-start(bf16[128,2048]{1,0:T(8,128)(2,1)} %get-tuple-element.901), channel_id=1, source_target_pairs={{0,8},{24,16},{1,9},{25,17},{2,10},{26,18},{3,11},{27,19},{4,12},{... | collective-permute-start | bytes 1572872 | tf_op jit(solution)/shard_map/ppermute | solution.py:191
  660.6 42.9 %collective-permute-start.87 = (bf16[64,3072]{1,0:T(8,128)(2,1)}, bf16[64,3072]{1,0:T(8,128)(2,1)}, u32[]{:S(2)}, u32[]{:S(2)}) collective-permute-start(bf16[64,3072]{1,0:T(8,128)(2,1)} %get-tuple-element.929), channel_id=1, source_target_pairs={{0,8},{24,16},{1,9},{25,17},{2,10},{26,18},{3,11},{27,19},{4,12},{... | collective-permute-start | bytes 1179656 | tf_op jit(solution)/shard_map/ppermute | solution.py:191
  681.6 19.3 %all-to-all-start.1 = ((f32[8,256,128]{2,1,0:T(8,128)}), f32[8,256,128]{2,1,0:T(8,128)}, u32[]{:S(2)}, u32[]{:S(2)}) async-start(f32[8,256,128]{2,1,0:T(8,128)} %bitcast.128), calls=%async_computation.1 | async-start | bytes 2097152 | tf_op jit(solution)/shard_map/all_to_all | solution.py:917
  703.4 76.2 %collective-permute-start.97 = (bf16[128,2816]{1,0:T(8,128)(2,1)}, bf16[128,2816]{1,0:T(8,128)(2,1)}, u32[]{:S(2)}, u32[]{:S(2)}) collective-permute-start(bf16[128,2816]{1,0:T(8,128)(2,1)} %broadcast_select_fusion.24), channel_id=1, source_target_pairs={{0,2},{2,0},{4,6},{6,4},{1,3},{3,1},{5,7},{7,5},{8,10},{10,8},{12,... | collective-permute-start | bytes 2162696 | tf_op jit(solution)/shard_map/ppermute | solution.py:57
  703.5 33.8 %collective-permute-start.91 = (bf16[64,3072]{1,0:T(8,128)(2,1)}, bf16[64,3072]{1,0:T(8,128)(2,1)S(1)}, u32[]{:S(2)}, u32[]{:S(2)}) collective-permute-start(bf16[64,3072]{1,0:T(8,128)(2,1)} %get-tuple-element.960), channel_id=1, source_target_pairs={{0,8},{24,16},{1,9},{25,17},{2,10},{26,18},{3,11},{27,19},{4,12},{... | collective-permute-start | bytes 1179656 | tf_op jit(solution)/shard_map/ppermute | solution.py:191
  713.1 22.6 %collective-permute-start.92 = (bf16[64,3072]{1,0:T(8,128)(2,1)S(1)}, bf16[64,3072]{1,0:T(8,128)(2,1)S(1)}, u32[]{:S(2)}, u32[]{:S(2)}) collective-permute-start(bf16[64,3072]{1,0:T(8,128)(2,1)S(1)} %reduce-precision_convert_fusion.43), channel_id=1, source_target_pairs={{8,16},{16,8},{9,17},{17,9},{10,18},{18,10},{11,19},{19,11},{12,20... | collective-permute-start | bytes 1179656 | tf_op jit(solution)/shard_map/ppermute | solution.py:201
  735.6 21.9 %collective-permute-start.95 = (bf16[1,1,2,256,512]{4,3,2,1,0:T(8,128)(2,1)}, bf16[1,1,2,256,512]{4,3,2,1,0:T(8,128)(2,1)}, u32[]{:S(2)}, u32[]{:S(2)}) collective-permute-start(bf16[1,1,2,256,512]{4,3,2,1,0:T(8,128)(2,1)} %get-tuple-element.1271), channel_id=1, source_target_pairs={{0,4},{2,6},{4,0},{6,2},{1,5},{3,7},{5,1},{7,3},{8,12},{10,14},{12... | collective-permute-start | bytes 1572872 | tf_op jit(solution)/shard_map/ppermute | solution.py:61
  757.5 30.6 %collective-permute-start.94 = (bf16[1,1,1,256,512]{4,3,2,1,0:T(8,128)(2,1)S(1)}, bf16[1,1,1,256,512]{4,3,2,1,0:T(8,128)(2,1)S(1)}, u32[]{:S(2)}, u32[]{:S(2)}) collective-permute-start(bf16[1,1,1,256,512]{4,3,2,1,0:T(8,128)(2,1)S(1)} %get-tuple-element.1294), channel_id=1, source_target_pairs={{0,4},{2,6},{4,0},{6,2},{1,5},{3,7},{5,1},{7,3},{8,12},{10,14},{12... | collective-permute-start | bytes 786440 | tf_op jit(solution)/shard_map/ppermute | solution.py:61
  760.3 27.4 %collective-permute-start.96 = (bf16[1,1,1,256,512]{4,3,2,1,0:T(8,128)(2,1)S(1)}, bf16[1,1,1,256,512]{4,3,2,1,0:T(8,128)(2,1)S(1)}, u32[]{:S(2)}, u32[]{:S(2)}) collective-permute-start(bf16[1,1,1,256,512]{4,3,2,1,0:T(8,128)(2,1)S(1)} %get-tuple-element.1292), channel_id=1, source_target_pairs={{0,1},{1,0},{2,3},{3,2},{4,5},{5,4},{6,7},{7,6},{8,9},{9,8},{10,11... | collective-permute-start | bytes 786440 | tf_op jit(solution)/shard_map/ppermute | solution.py:62
  764.7 32.7 %collective-permute-start.102 = (bf16[64,3072]{1,0:T(8,128)(2,1)}, bf16[64,3072]{1,0:T(8,128)(2,1)}, u32[]{:S(2)}, u32[]{:S(2)}) collective-permute-start(bf16[64,3072]{1,0:T(8,128)(2,1)} %reduce-precision_convert_fusion.39), channel_id=1, source_target_pairs={{8,16},{16,8},{9,17},{17,9},{10,18},{18,10},{11,19},{19,11},{12,20... | collective-permute-start | bytes 1179656 | tf_op jit(solution)/shard_map/ppermute | solution.py:201
  768.3 29.2 %collective-permute-start.101 = (bf16[64,3072]{1,0:T(8,128)(2,1)}, bf16[64,3072]{1,0:T(8,128)(2,1)}, u32[]{:S(2)}, u32[]{:S(2)}) collective-permute-start(bf16[64,3072]{1,0:T(8,128)(2,1)} %get-tuple-element.1164), channel_id=1, source_target_pairs={{0,8},{8,0},{16,24},{24,16},{1,9},{9,1},{17,25},{25,17},{2,10},{10... | collective-permute-start | bytes 1179656 | tf_op jit(solution)/shard_map/ppermute | solution.py:188
  779.6 29.4 %collective-permute-start.107 = (bf16[128,2816]{1,0:T(8,128)(2,1)}, bf16[128,2816]{1,0:T(8,128)(2,1)S(1)}, u32[]{:S(2)}, u32[]{:S(2)}) collective-permute-start(bf16[128,2816]{1,0:T(8,128)(2,1)} %broadcast_select_fusion.20), channel_id=1, source_target_pairs={{0,2},{2,0},{4,6},{6,4},{1,3},{3,1},{5,7},{7,5},{8,10},{10,8},{12,... | collective-permute-start | bytes 2162696 | tf_op jit(solution)/shard_map/ppermute | solution.py:57
  787.6 32.8 %collective-permute-start.106 = (bf16[128,2816]{1,0:T(8,128)(2,1)}, bf16[128,2816]{1,0:T(8,128)(2,1)}, u32[]{:S(2)}, u32[]{:S(2)}) collective-permute-start(bf16[128,2816]{1,0:T(8,128)(2,1)} %broadcast_select_fusion.17), channel_id=1, source_target_pairs={{0,2},{2,0},{4,6},{6,4},{1,3},{3,1},{5,7},{7,5},{8,10},{10,8},{12,... | collective-permute-start | bytes 2162696 | tf_op jit(solution)/shard_map/ppermute | solution.py:57
  788.1 40.2 %collective-permute-start.105 = (f32[7,256]{1,0:T(8,128)S(1)}, f32[7,256]{1,0:T(8,128)S(1)}, u32[]{:S(2)}, u32[]{:S(2)}) collective-permute-start(f32[7,256]{1,0:T(8,128)S(1)} %concatenate.199), channel_id=1, source_target_pairs={{0,8},{8,0},{16,24},{24,16},{1,9},{9,1},{17,25},{25,17},{2,10},{10... | collective-permute-start | bytes 21512 | tf_op jit(solution)/shard_map/ppermute | solution.py:950
  793.2 39.8 %all-to-all-start.2 = ((bf16[8,256,128]{2,1,0:T(8,128)(2,1)}), bf16[8,256,128]{2,1,0:T(8,128)(2,1)}, u32[]{:S(2)}, u32[]{:S(2)}) async-start(bf16[8,256,128]{2,1,0:T(8,128)(2,1)} %bitcast.307), calls=%async_computation.2 | async-start | bytes 1048576 | tf_op jit(solution)/shard_map/all_to_all | solution.py:917
  799.5 35.6 %collective-permute-start.104 = (bf16[64,3072]{1,0:T(8,128)(2,1)}, bf16[64,3072]{1,0:T(8,128)(2,1)}, u32[]{:S(2)}, u32[]{:S(2)}) collective-permute-start(bf16[64,3072]{1,0:T(8,128)(2,1)} %reduce-precision_convert_fusion.37), channel_id=1, source_target_pairs={{8,16},{16,8},{9,17},{17,9},{10,18},{18,10},{11,19},{19,11},{12,20... | collective-permute-start | bytes 1179656 | tf_op jit(solution)/shard_map/ppermute | solution.py:201
  803.4 31.7 %collective-permute-start.103 = (bf16[64,3072]{1,0:T(8,128)(2,1)}, bf16[64,3072]{1,0:T(8,128)(2,1)}, u32[]{:S(2)}, u32[]{:S(2)}) collective-permute-start(bf16[64,3072]{1,0:T(8,128)(2,1)} %get-tuple-element.1162), channel_id=1, source_target_pairs={{0,8},{8,0},{16,24},{24,16},{1,9},{9,1},{17,25},{25,17},{2,10},{10... | collective-permute-start | bytes 1179656 | tf_op jit(solution)/shard_map/ppermute | solution.py:188
  831.4 39.1 %collective-permute-start.114 = (bf16[64,3072]{1,0:T(8,128)(2,1)}, bf16[64,3072]{1,0:T(8,128)(2,1)S(1)}, u32[]{:S(2)}, u32[]{:S(2)}) collective-permute-start(bf16[64,3072]{1,0:T(8,128)(2,1)} %broadcast_select_fusion.66), channel_id=1, source_target_pairs={{0,2},{2,0},{4,6},{6,4},{1,3},{3,1},{5,7},{7,5},{8,10},{10,8},{12,... | collective-permute-start | bytes 1179656 | tf_op jit(solution)/shard_map/ppermute | solution.py:57
  837.0 47.2 %collective-permute-start.113 = (bf16[64,3072]{1,0:T(8,128)(2,1)}, bf16[64,3072]{1,0:T(8,128)(2,1)S(1)}, u32[]{:S(2)}, u32[]{:S(2)}) collective-permute-start(bf16[64,3072]{1,0:T(8,128)(2,1)} %broadcast_select_fusion.61), channel_id=1, source_target_pairs={{0,2},{2,0},{4,6},{6,4},{1,3},{3,1},{5,7},{7,5},{8,10},{10,8},{12,... | collective-permute-start | bytes 1179656 | tf_op jit(solution)/shard_map/ppermute | solution.py:57
  864.9 24.7 %collective-permute-start.112 = (bf16[64,3072]{1,0:T(8,128)(2,1)S(1)}, bf16[64,3072]{1,0:T(8,128)(2,1)S(1)}, u32[]{:S(2)}, u32[]{:S(2)}) collective-permute-start(bf16[64,3072]{1,0:T(8,128)(2,1)S(1)} %reduce-precision_convert_fusion.33), channel_id=1, source_target_pairs={{8,16},{16,8},{9,17},{17,9},{10,18},{18,10},{11,19},{19,11},{12,20... | collective-permute-start | bytes 1179656 | tf_op jit(solution)/shard_map/ppermute | solution.py:201
  867.0 22.6 %collective-permute-start.111 = (bf16[64,3072]{1,0:T(8,128)(2,1)S(1)}, bf16[64,3072]{1,0:T(8,128)(2,1)S(1)}, u32[]{:S(2)}, u32[]{:S(2)}) collective-permute-start(bf16[64,3072]{1,0:T(8,128)(2,1)S(1)} %get-tuple-element.1158), channel_id=1, source_target_pairs={{0,8},{8,0},{16,24},{24,16},{1,9},{9,1},{17,25},{25,17},{2,10},{10... | collective-permute-start | bytes 1179656 | tf_op jit(solution)/shard_map/ppermute | solution.py:188
  (223 other events, 1995.4 us)

commit v4 on v3

--- a/solution.py
+++ b/solution.py
@@ -129,6 +129,9 @@
         out = stage(*args)
         self.last = jax.tree.leaves(out)[0]
         return out
+
+
+SMALL = pl.CostEstimate(flops=1024, bytes_accessed=1024, transcendentals=0)
 
 
 class RepSum:
@@ -223,16 +226,111 @@
         ),
         out_shape=[out, out],
         compiler_params=pltpu.CompilerParams(vmem_limit_bytes=32 * 1024 * 1024),
-        cost_estimate=pl.CostEstimate(flops=0, bytes_accessed=12 * rows * count * unit, transcendentals=0),
+        cost_estimate=SMALL,
     )(core, w)
 
 
+def arrange_kernel(at_ref, a_ref, b_ref, c_ref, d_ref, send_ref, keep_ref):
+    send_ref[...] = jnp.concatenate([a_ref[...], b_ref[...]], axis=1)
+    keep_ref[...] = jnp.concatenate([c_ref[...], d_ref[...]], axis=1)
+
+
+def arrange(mine, got, place, pre, y_size, s_size, unit, flip):
+    r = mine.shape[1]
+    half = pre * y_size * s_size // 2
+
+    def block(i, place, keep):
+        p = i % pre
+        i = i // pre
+        if flip:
+            s, y = i % s_size, i // s_size
+            bit = place[0] // (y_size // 2)
+            bit = bit if keep else 1 - bit
+            y = y + bit * (y_size // 2)
+        else:
+            y, s = i % y_size, i // y_size
+            bit = place[1] // (s_size // 2)
+            bit = bit if keep else 1 - bit
+            s = s + bit * (s_size // 2)
+        return ((p * y_size + y) * s_size + s, 0)
+
+    def spec(keep):
+        return pl.BlockSpec((unit, r), lambda i, place: block(i, place, keep))
+
+    out = jax.ShapeDtypeStruct((half * unit, 2 * r), bf16)
+    out_spec = pl.BlockSpec((unit, 2 * r), lambda i, place: (i, 0))
+    return pl.pallas_call(
+        arrange_kernel,
+        grid_spec=pltpu.PrefetchScalarGridSpec(
+            num_scalar_prefetch=1,
+            grid=(half,),
+            in_specs=[spec(False), spec(False), spec(True), spec(True)],
+            out_specs=[out_spec, out_spec],
+        ),
+        out_shape=[out, out],
+        compiler_params=pltpu.CompilerParams(vmem_limit_bytes=32 * 1024 * 1024),
+        cost_estimate=SMALL,
+    )(place, mine, got, mine, got)
+
+
+def add_split_kernel(bit_ref, a_ref, b_ref, c_ref, d_ref, send_ref, keep_ref):
+    send_ref[...] = (a_ref[...].astype(f32) + b_ref[...].astype(f32)).astype(bf16)
+    keep_ref[...] = (c_ref[...].astype(f32) + d_ref[...].astype(f32)).astype(bf16)
+
+
+def add_split(kept, got, bit):
+    rows, t = kept.shape
+    half = rows // 2
+    n = max(n for n in (1, 2, 3, 4) if half % (16 * n) == 0)
+    rb = half // n
+    away = pl.BlockSpec((rb, t), lambda i, bit: ((1 - bit[0]) * n + i, 0))
+    here = pl.BlockSpec((rb, t), lambda i, bit: (bit[0] * n + i, 0))
+    out = jax.ShapeDtypeStruct((half, t), bf16)
+    out_spec = pl.BlockSpec((rb, t), lambda i, bit: (i, 0))
+    return pl.pallas_call(
+        add_split_kernel,
+        grid_spec=pltpu.PrefetchScalarGridSpec(
+            num_scalar_prefetch=1,
+            grid=(n,),
+            in_specs=[away, away, here, here],
+            out_specs=[out_spec, out_spec],
+        ),
+        out_shape=[out, out],
+        compiler_params=pltpu.CompilerParams(vmem_limit_bytes=48 * 1024 * 1024),
+        cost_estimate=SMALL,
+    )(bit, kept, got, kept, got)
+
+
+def token_rows_kernel(core_ref, a_ref, b_ref, c_ref, d_ref, out_ref):
+    mine = core_ref[0] == pl.program_id(2)
+    half = out_ref.shape[0] // 2
+    out_ref[:half] = jnp.where(mine, a_ref[0, 0], c_ref[0, 0])
+    out_ref[half:] = jnp.where(mine, b_ref[0, 0], d_ref[0, 0])
+
+
+def token_rows(mine, theirs, core):
+    y_size, s_size, rows, width = mine[0].shape
+    part = pl.BlockSpec((1, 1, rows, width), lambda s, y, c, core: (y, s, 0, 0))
+    return pl.pallas_call(
+        token_rows_kernel,
+        grid_spec=pltpu.PrefetchScalarGridSpec(
+            num_scalar_prefetch=1,
+            grid=(s_size, y_size, 2),
+            in_specs=[part] * 4,
+            out_specs=pl.BlockSpec((2 * rows, width), lambda s, y, c, core: ((s * y_size + y) * 2 + c, 0)),
+        ),
+        out_shape=jax.ShapeDtypeStruct((s_size * y_size * 4 * rows, width), bf16),
+        compiler_params=pltpu.CompilerParams(vmem_limit_bytes=32 * 1024 * 1024),
+        cost_estimate=SMALL,
+    )(core, *mine, *theirs)
+
+
 def adam_kernel(rate, two, core_ref, w_ref, m_ref, v_ref, *refs):
+    grad = refs[0][...].astype(f32)
     if two:
-        mine = core_ref[0] == pl.program_id(1)
-        grad = jnp.where(mine, refs[0][...], refs[1][...]).astype(f32)
-    else:
-        grad = refs[0][...].astype(f32)
+        other = refs[1][...].astype(f32)
+        mine = core_ref[0] == 0
+        grad = jnp.concatenate([jnp.where(mine, grad, other), jnp.where(mine, other, grad)], axis=1)
     new_m_ref, new_v_ref, new_w_ref = refs[-3:]
     new_m, new_v, new_w = adam_update(w_ref[...], m_ref[...], v_ref[...], grad, rate, weight_decay)
     new_m_ref[...] = new_m
@@ -245,38 +343,31 @@
     two = len(grads) == 2
     rb = grads[0].shape[0]
     count = grads[0].shape[1] // unit
-    if two:
-        grid = (count, 2)
-        whole = pl.BlockSpec((rb, unit), lambda g, j, core: (row_block, 2 * (col_first + g) + j))
-        half = pl.BlockSpec((rb, unit), lambda g, j, core: (0, g))
-    else:
-        grid = (count,)
-        whole = pl.BlockSpec((rb, unit), lambda g, core: (row_block, g))
-        half = pl.BlockSpec((rb, unit), lambda g, core: (0, g))
+    whole = pl.BlockSpec((rb, unit * len(grads)), lambda g, core: (row_block, col_first + g))
+    half = pl.BlockSpec((rb, unit), lambda g, core: (0, g))
     out = jax.ShapeDtypeStruct(w.shape, f32)
     extra, aliases = [], {}
     if prev is not None:
         extra = list(prev)
         aliases = {4 + len(grads) + i: i for i in range(3)}
-    n = rb * count * unit * len(grads)
     return pl.pallas_call(
         functools.partial(adam_kernel, rate, two),
         grid_spec=pltpu.PrefetchScalarGridSpec(
             num_scalar_prefetch=1,
-            grid=grid,
+            grid=(count,),
             in_specs=[whole] * 3 + [half] * len(grads) + [pl.BlockSpec(memory_space=pl.ANY)] * len(extra),
             out_specs=[whole] * 3,
         ),
         out_shape=[out] * 3,
         input_output_aliases=aliases,
-        compiler_params=pltpu.CompilerParams(vmem_limit_bytes=32 * 1024 * 1024),
-        cost_estimate=pl.CostEstimate(flops=20 * n, bytes_accessed=28 * n, transcendentals=0),
+        compiler_params=pltpu.CompilerParams(vmem_limit_bytes=48 * 1024 * 1024),
+        cost_estimate=SMALL,
     )(core, w, m, v, *grads, *extra)
 
 
-def attend_kernel(kept_ref, got_ref, bias_ref, cos_ref, sin_ref, prow_ref, pcol_ref, qkv_ref, out_ref, peak_ref, total_ref):
-    cos, sin = cos_ref[0], sin_ref[0]
+def attend_kernel(kept_ref, got_ref, bias_ref, table_ref, qkv_ref, out_ref, stat_ref):
     half = ROTARY // 2
+    cos, sin, pos = table_ref[0, :half], table_ref[0, half:ROTARY], table_ref[0, ROTARY:]
     parts = []
     for i in range(3):
         v = kept_ref[i, 0].astype(f32) + got_ref[i, 0].astype(f32) + bias_ref[i, 0]
@@ -288,22 +379,21 @@
         parts.append(v)
     q, k, v = parts
     scores = dot(k, q, FIRST) * score_scale
-    scores = jnp.where(pcol_ref[0] <= prow_ref[0], scores, masked_score)
+    scores = jnp.where(pos.T[:, :1] <= pos[:1], scores, masked_score)
     peak = jnp.max(scores, axis=0, keepdims=True)
     e = jnp.exp(scores - peak)
     total = jnp.sum(e, axis=0, keepdims=True)
     p = (e / total).astype(bf16)
     out_ref[0] = dot(v, p, PLAIN).astype(bf16)
-    peak_ref[0, 0] = peak
-    total_ref[0, 0] = total
-
-
-def attend(kept, got, bias, cos, sin, prow, pcol):
+    stat_ref[0, 0] = jnp.concatenate([peak, total], axis=0)
+
+
+def attend(kept, got, bias, table):
     _, heads, hd, t = kept.shape
-    seqs, _, seq = prow.shape
+    seqs, _, seq = table.shape
     big = pl.BlockSpec((3, 1, hd, seq), lambda s, h: (0, h, 0, s))
-    table = pl.BlockSpec((1, ROTARY // 2, seq), lambda s, h: (s, 0, 0))
-    stat = pl.BlockSpec((1, 1, 1, seq), lambda s, h: (s, h, 0, 0))
+    table_spec = pl.BlockSpec((1, table.shape[1], seq), lambda s, h: (s, 0, 0))
+    stat = pl.BlockSpec((1, 1, 2, seq), lambda s, h: (s, h, 0, 0))
     return pl.pallas_call(
         attend_kernel,
         grid=(seqs, heads),
@@ -311,35 +401,27 @@
             big,
             big,
             pl.BlockSpec((3, 1, hd, 1), lambda s, h: (0, h, 0, 0)),
-            table,
-            table,
-            pl.BlockSpec((1, 1, seq), lambda s, h: (s, 0, 0)),
-            pl.BlockSpec((1, seq, 1), lambda s, h: (s, 0, 0)),
+            table_spec,
         ],
-        out_specs=[big, pl.BlockSpec((1, hd, seq), lambda s, h: (h, 0, s)), stat, stat],
+        out_specs=[big, pl.BlockSpec((1, hd, seq), lambda s, h: (h, 0, s)), stat],
         out_shape=[
             jax.ShapeDtypeStruct((3, heads, hd, t), bf16),
             jax.ShapeDtypeStruct((heads, hd, t), bf16),
-            jax.ShapeDtypeStruct((seqs, heads, 1, seq), f32),
-            jax.ShapeDtypeStruct((seqs, heads, 1, seq), f32),
+            jax.ShapeDtypeStruct((seqs, heads, 2, seq), f32),
         ],
         compiler_params=pltpu.CompilerParams(vmem_limit_bytes=32 * 1024 * 1024),
-        cost_estimate=pl.CostEstimate(
-            flops=4 * seqs * heads * seq * seq * hd,
-            bytes_accessed=16 * 3 * heads * hd * t,
-            transcendentals=seqs * heads * seq * seq,
-        ),
-    )(kept, got, bias, cos, sin, prow, pcol)
-
-
-def attend_back_kernel(qkv_ref, dout_ref, peak_ref, total_ref, cos_ref, sin_ref, prow_ref, pcol_ref, out_ref):
-    cos, sin = cos_ref[0], sin_ref[0]
+        cost_estimate=SMALL,
+    )(kept, got, bias, table)
+
+
+def attend_back_kernel(qkv_ref, dout_ref, stat_ref, table_ref, out_ref):
     half = ROTARY // 2
+    cos, sin, pos = table_ref[0, :half], table_ref[0, half:ROTARY], table_ref[0, ROTARY:]
     q, k, v = qkv_ref[0, 0], qkv_ref[1, 0], qkv_ref[2, 0]
     dout = dout_ref[0]
     scores = dot(k, q, FIRST) * score_scale
-    scores = jnp.where(pcol_ref[0] <= prow_ref[0], scores, masked_score)
-    p = jnp.exp(scores - peak_ref[0, 0]) / total_ref[0, 0]
+    scores = jnp.where(pos.T[:, :1] <= pos[:1], scores, masked_score)
+    p = jnp.exp(scores - stat_ref[0, 0, :1]) / stat_ref[0, 0, 1:]
     dp = dot(v, dout, FIRST)
     inner = jnp.sum(p * dp, axis=0, keepdims=True)
     ds = (p * (dp - inner)).astype(bf16)
@@ -353,12 +435,12 @@
     out_ref[2, 0] = dot(dout, p.astype(bf16), LAST).astype(bf16)
 
 
-def attend_back(qkv, dout, peak, total, cos, sin, prow, pcol):
+def attend_back(qkv, dout, stats, table):
     _, heads, hd, t = qkv.shape
-    seqs, _, seq = prow.shape
+    seqs, _, seq = table.shape
     big = pl.BlockSpec((3, 1, hd, seq), lambda s, h: (0, h, 0, s))
-    table = pl.BlockSpec((1, ROTARY // 2, seq), lambda s, h: (s, 0, 0))
-    stat = pl.BlockSpec((1, 1, 1, seq), lambda s, h: (s, h, 0, 0))
+    table_spec = pl.BlockSpec((1, table.shape[1], seq), lambda s, h: (s, 0, 0))
+    stat = pl.BlockSpec((1, 1, 2, seq), lambda s, h: (s, h, 0, 0))
     return pl.pallas_call(
         attend_back_kernel,
         grid=(seqs, heads),
@@ -366,21 +448,13 @@
             big,
             pl.BlockSpec((1, hd, seq), lambda s, h: (h, 0, s)),
             stat,
-            stat,
-            table,
-            table,
-            pl.BlockSpec((1, 1, seq), lambda s, h: (s, 0, 0)),
-            pl.BlockSpec((1, seq, 1), lambda s, h: (s, 0, 0)),
+            table_spec,
         ],
         out_specs=big,
         out_shape=jax.ShapeDtypeStruct((3, heads, hd, t), bf16),
         compiler_params=pltpu.CompilerParams(vmem_limit_bytes=32 * 1024 * 1024),
-        cost_estimate=pl.CostEstimate(
-            flops=10 * seqs * heads * seq * seq * hd,
-            bytes_accessed=16 * 3 * heads * hd * t,
-            transcendentals=seqs * heads * seq * seq,
-        ),
-    )(qkv, dout, peak, total, cos, sin, prow, pcol)
+        cost_estimate=SMALL,
+    )(qkv, dout, stats, table)
 
 
 def body(
@@ -431,6 +505,9 @@
     def join(a, b):
         return jnp.concatenate([a, b], axis=0)
 
+    def lanes(a, b):
+        return jnp.concatenate([a, b], axis=1)
+
     x_rows = tokens.reshape(rows, width)
     order = span_order.reshape(-1).astype(f32)
     span = rows // 2
@@ -459,37 +536,27 @@
         mine, theirs = do(lambda w: split_columns(w, core, lead, unit, count), w)
         return mine, at.core(theirs)
 
-    def lanes(a, b):
-        return jnp.concatenate([a, b], axis=1)
-
     wq_parts = chip_rows(w_qkv, 0, S * blk, 3 * Y)
     norm_cols = norm_params.reshape(7, nb, blk).transpose(1, 2, 0)
     own_cols = pick(norm_cols, 0, my_block)
     other_cols = pick(norm_cols, 0, (at.ctx ^ 1) * S + at.s)
     pair_cols = join(own_cols, other_cols)
     bias = own_cols[:, 4:7].T.reshape(3, heads, HEAD_DIM, 1)
-    wq = do(lanes, *wq_parts)
-
-    def first_step(flip):
-        axis, step = at.steps(flip)[0]
-        return axis, step, {"y": 1, "s": 2}[axis], (at.index(axis) // step) % 2
-
-    def send_keep(w, pre, unit, flip):
-        _, step, ax, bit = first_step(flip)
-        w = w.reshape(pre, Y, S, unit, w.shape[1])
-        cut = [lax.dynamic_slice_in_dim(w, b * step, step, ax) for b in (1 - bit, bit)]
-        return [c.reshape(-1, c.shape[-1]) for c in cut]
-
-    wq_cut = [do(lambda w, k=k: send_keep(w, 3, blk, bool(k)), wq) for k in range(2)]
-
-    def arrange(got):
+    spot = jnp.stack([at.y, at.s])
+
+    def cut_weights(parts, pre, unit, flip):
+        return do(lambda a, b: arrange(a, b, spot, pre, Y, S, unit, flip), *parts)
+
+    wq_cut = [cut_weights(wq_parts, 3, blk, bool(k)) for k in range(2)]
+
+    def columns(got):
         x = got.reshape(at.ctx_size, S, blk + 16, rows).transpose(2, 1, 0, 3).reshape(blk + 16, T)
         x_own, extra = x[:blk], x[blk:].astype(f32)
         mean = extra[0:1] + extra[1:2] + extra[2:3]
         inv = extra[3:4] + extra[4:5] + extra[5:6]
         return x_own, mean, inv, extra[6:7]
 
-    x_own, mean1, inv1, place = do(arrange, got)
+    x_own, mean1, inv1, place = do(columns, got)
     x_other = at.core(x_own)
 
     def first_norm(mine, theirs, mean, inv, cols):
@@ -498,65 +565,46 @@
 
     xn1 = do(first_norm, x_own, x_other, mean1, inv1, pair_cols)
 
-    def send_products(cut, xs, shapes):
-        got = []
+    def send_products(cut, xs):
+        got, kept = [], []
         for k in range(2):
-            axis, step, _, _ = first_step(bool(k))
-            p = do(lambda w, x: dot(w, x, PLAIN).astype(bf16), cut[k][0], xs[k]).reshape(shapes[k])
+            axis, step = at.steps(bool(k))[0]
+            p = do(lambda w, x: dot(w, x, PLAIN).astype(bf16), cut[k][0], xs[k])
             got.append(at.along(p, axis, step))
-        kept = []
         for k in range(2):
-            p = do(lambda w, x: dot(w, x, PLAIN).astype(bf16), cut[k][1], xs[k])
-            kept.append(p.reshape(shapes[k]))
+            kept.append(do(lambda w, x: dot(w, x, PLAIN).astype(bf16), cut[k][1], xs[k]))
         return list(zip(kept, got))
-
-    def half_shape(pre, unit, t, flip):
-        _, step, ax, _ = first_step(flip)
-        shape = [pre, Y, S, unit, t]
-        shape[ax] = step
-        return tuple(shape)
 
     def scatter_rest(pairs):
         for i in range(1, len(at.steps(False))):
             out = []
             for k in range(2):
-                kept, got = pairs[k]
                 axis, step = at.steps(bool(k))[i]
-                ax = {"y": 1, "s": 2}[axis]
                 bit = (at.index(axis) // step) % 2
-
-                def cut(a, b):
-                    p = (a.astype(f32) + b.astype(f32)).astype(bf16)
-                    return [lax.dynamic_slice_in_dim(p, n * step, step, ax) for n in (1 - bit, bit)]
-
-                send, kept = do(cut, kept, got)
+                send, kept = do(lambda a, b: add_split(a, b, bit.reshape(1)), *pairs[k])
                 out.append((kept, at.along(send, axis, step)))
             pairs = out
-        return [(kept[:, 0, 0], got[:, 0, 0]) for kept, got in pairs]
-
-    flying = send_products(
-        wq_cut, [xn1[:, h] for h in halves], [half_shape(3, blk, H, bool(k)) for k in range(2)]
-    )
+        return pairs
+
+    flying = send_products(wq_cut, [xn1[:, h] for h in halves])
 
     wo_parts = chip_rows(w_out, 0, S * blk, Y)
     wg_parts = chip_rows(w_up, 0, S * ffb, Y)
-    wo = do(lanes, *wo_parts)
     wu_parts = chip_rows(w_up, Y, S * ffb, Y)
-    wg = do(lanes, *wg_parts)
-    wg_cut = do(lambda w: send_keep(w, 1, ffb, False), wg)
+    wo_cut = [cut_weights(wo_parts, 1, blk, bool(k)) for k in range(2)]
 
     def positions(place):
         pos = place.reshape(S, seq) * span + (jnp.arange(seq) % span).astype(f32)[None, :]
-        prow, pcol = pos.reshape(S, 1, seq), pos.reshape(S, seq, 1)
+        prow = pos.reshape(S, 1, seq)
         exponent = jnp.arange(ROTARY // 2, dtype=f32)
         inverse = 10000.0 ** (-2.0 * exponent / ROTARY)
         angles = prow * inverse[None, :, None]
-        return jnp.cos(angles), jnp.sin(angles), prow, pcol
-
-    cos, sin, prow, pcol = do(positions, place)
+        return jnp.concatenate([jnp.cos(angles), jnp.sin(angles), jnp.broadcast_to(prow, (S, 8, seq))], axis=1)
+
+    table = do(positions, place)
     flying = scatter_rest(flying)
-    wu = do(lanes, *wu_parts)
-    wu_cut = do(lambda w: send_keep(w, 1, ffb, True), wu)
+    wg_cut = cut_weights(wg_parts, 1, ffb, False)
+    wu_cut = cut_weights(wu_parts, 1, ffb, True)
 
     def gather_steps(parts, row_axis):
         n = len(at.steps(False))
@@ -586,39 +634,25 @@
         def result():
             return jnp.concatenate(state["parts"], axis=row_axis)
 
-        return n, start, finish, result
-
-    qkvs, attns, attn_got, peaks, totals = [], [], [], [], []
+        return n, start, finish, state if row_axis is None else result
+
+    qkvs, attns, attn_got, stats = [], [], [], []
     for k in range(2):
-        sq = seqs[k]
         shape = (3, heads, HEAD_DIM, H)
-        qkv, attn, peak, total = do(
-            attend, flying[k][0].reshape(shape), flying[k][1].reshape(shape), bias, cos[sq], sin[sq], prow[sq], pcol[sq]
-        )
+        qkv, attn, stat = do(attend, flying[k][0].reshape(shape), flying[k][1].reshape(shape), bias, table[seqs[k]])
         qkvs.append(qkv)
         attns.append(attn.reshape(blk, H))
         attn_got.append(at.core(attns[k]))
-        peaks.append(peak)
-        totals.append(total)
-
-    wo5 = wo.reshape(1, Y, S, blk, wo.shape[1])
-    flying = []
-    for k in range(2):
-        axis, step, ax, bit = first_step(bool(k))
-
-        def product(w, a, b):
-            p = dot(w, join(a, b), PLAIN).astype(bf16).reshape(1, Y, S, blk, H)
-            return [lax.dynamic_slice_in_dim(p, n * step, step, ax) for n in (1 - bit, bit)]
-
-        send, kept = do(product, wo, attns[k], attn_got[k])
-        flying.append((kept, at.along(send, axis, step)))
-    flying = scatter_rest(flying)
+        stats.append(stat)
+
+    pairs = [do(join, attns[k], attn_got[k]) for k in range(2)]
+    flying = scatter_rest(send_products(wo_cut, pairs))
     cot = cotangent.reshape(2, rows // 2, width)
     cot_pair, _ = lax.optimization_barrier((cot, flying[1][0]))
-    cot_n, cot_start, cot_finish, cot_done = gather_steps([cot_pair[k][None, None] for k in range(2)], 2)
+    cot_n, cot_start, cot_finish, cot_state = gather_steps([cot_pair[k][None, None] for k in range(2)], None)
 
     def residual(x, a0, b0, a1, b1):
-        a, b = lanes(a0[0], a1[0]), lanes(b0[0], b1[0])
+        a, b = lanes(a0, a1), lanes(b0, b1)
         hidden = x.astype(f32) + (a.astype(f32) + b.astype(f32))
         local_mean = jnp.mean(hidden, axis=0, keepdims=True)
         dev = hidden - local_mean
@@ -645,15 +679,17 @@
     xn2_own, z2, inv2 = do(second_norm, hidden, moments, own_cols)
     xn2 = do(join, xn2_own, at.core(xn2_own))
 
-    flying = send_products(
-        [wg_cut, wu_cut], [xn2, xn2], [half_shape(1, ffb, T, bool(k)) for k in range(2)]
-    )
+    flying = send_products([wg_cut, wu_cut], [xn2, xn2])
 
     for i in range(1, cot_n):
         cot_finish()
         cot_start(i)
     wo_own = do(lambda w: w.astype(bf16), w_out)
     wd_own = do(lambda w: w.astype(bf16), w_down)
+    wq = do(lanes, *wq_parts)
+
+    wg = do(lanes, *wg_parts)
+    wu = do(lanes, *wu_parts)
 
     def gain_products(wg, wu, cols):
         g, b = cols[:, 2], cols[:, 3]
@@ -677,20 +713,15 @@
         gains = do(lambda a, b: a + b, kept, at.along(send, axis, step))
     gains = do(lambda g: g.reshape(4, ffb, 1), gains)
     cot_finish()
-    cot_c = do(lambda x: x, cot_done())
-
-    def all_cotangents(mine, theirs):
-        both = in_order(mine.reshape(Y, S, rows, width), theirs.reshape(Y, S, rows, width), 2)
-        return both.transpose(1, 0, 2, 3, 4).reshape(T, width)
-
-    cot_all = do(all_cotangents, cot_c, at.core(cot_c))
+    cot_theirs = [at.core(p) for p in cot_state["parts"]]
+    cot_all = do(lambda a, b: token_rows(a, b, core), cot_state["parts"], cot_theirs)
     grad_act = do(lambda w, c: dot(w, c, LAST), wd_own, cot_all)
     cot_cols = do(lambda c: lax.dynamic_slice_in_dim(c, my_block * blk, blk, 1).T, cot_all)
     flying = scatter_rest(flying)
 
     def gated(ga, gb, ua, ub, grad_act, gains):
-        gate = ga[0].astype(f32) + gb[0].astype(f32)
-        up = ua[0].astype(f32) + ub[0].astype(f32)
+        gate = ga.astype(f32) + gb.astype(f32)
+        up = ua.astype(f32) + ub.astype(f32)
         sig = jax.nn.sigmoid(gate)
         silu = gate * sig
         ggate = (grad_act * up * sig * (1.0 + gate * (1.0 - sig))).astype(bf16)
@@ -702,11 +733,61 @@
     def parts_of(count, want):
         return max(n for n in range(1, want + 1) if count % (16 * n) == 0)
 
-    n_down, n_up, n_out, n_qkv = parts_of(ffb, 4), parts_of(blk, 2), parts_of(blk, 2), parts_of(blk, 4)
-
-    def cut(g, n):
-        r = g.shape[0] // n
-        return [g[i * r : (i + 1) * r] for i in range(n)]
+    def even(count, want):
+        n = parts_of(count, want)
+        return [(k * (count // n), count // n) for k in range(n)]
+
+    down_rows, up_rows, out_rows = even(ffb, 4), even(blk, 2), even(blk, 2)
+    qkv_rows = [(0, blk // 2), (blk // 2, blk // 4), (3 * blk // 4, blk // 4)]
+
+    def push_rows(name, g, rows):
+        for k, (at_row, count) in enumerate(rows):
+            reps.push((name, "all", k), g[at_row : at_row + count])
+
+    def push_pairs(name, g, rows):
+        for k, (at_row, count) in enumerate(rows):
+            reps.push((name, "theirs", k), g[blk + at_row : blk + at_row + count])
+            reps.push((name, "mine", k), g[at_row : at_row + count])
+
+    results = {"down": None, "out": None, "up": None, "qkv": None}
+    states = {
+        "down": (w_down, m_down, v_down),
+        "out": (w_out, m_out, v_out),
+        "up": (w_up, m_up, v_up),
+        "qkv": (w_qkv, m_qkv, v_qkv),
+    }
+    rates = {"down": 0.02, "out": 0.2, "up": 0.03, "qkv": 0.03}
+    jobs = []
+    for k, (at_row, count) in enumerate(down_rows):
+        jobs.append(("down", [("down", "all", k)], at_row // count, 0, min(512, width)))
+    for part_name, lead in (("gate", 0), ("up", Y)):
+        for k, (at_row, count) in enumerate(up_rows):
+            jobs.append(
+                ("up", [(part_name, "mine", k), (part_name, "theirs", k)], at_row // count, lead, S * ffb)
+            )
+    for k, (at_row, count) in enumerate(out_rows):
+        jobs.append(("out", [("out", "all", k)], at_row // count, 0, min(512, width)))
+    for k, (at_row, count) in enumerate(qkv_rows):
+        jobs.append(("qkv", [("qkv", "mine", k), ("qkv", "theirs", k)], at_row // count, 0, S * blk))
+    received = {}
+
+    def update(limit):
+        for name in list(reps.done):
+            if name[1] == "theirs" and name not in received:
+                received[name] = at.core(reps.done[name])
+        while jobs and limit:
+            name, needs, row_block, lead, unit = jobs[0]
+            if not all(k in reps.done for k in needs):
+                return
+            grads = [received[k] if k[1] == "theirs" else reps.done[k] for k in needs]
+            results[name] = do(
+                lambda s, g, prev: adam_part(s, g, core, rates[name], prev, row_block, lead, unit),
+                states[name],
+                grads,
+                results[name],
+            )
+            jobs.pop(0)
+            limit -= 1
 
     def quarter_heads(x):
         return [x[:, h][None, None] for h in halves]
@@ -714,8 +795,7 @@
     n, start, finish, gate_all = gather_steps(quarter_heads(ggate), 3)
     start(0)
     g_down = do(lambda a, c: dot(a, c, PLAIN).astype(bf16), act, cot_all)
-    for i, g in enumerate(cut(g_down, n_down)):
-        reps.push(("down", i), g)
+    push_rows("down", g_down, down_rows)
     reps.tick()
 
     def norm_sums2(ggate, gup, gate, up, gains):
@@ -747,20 +827,14 @@
     ggate_all = do(lambda x: x.reshape(Y * S * ffb, T), gate_all())
     part_gate = do(lambda w, g: dot(w, g, FIRST), wg, ggate_all)
     g_gate = do(lambda x, g: dot(x, g, LAST).astype(bf16), xn2, ggate_all)
-
-    def push_pairs(name, g, n):
-        r = g.shape[0] // (2 * n)
-        for i in range(n):
-            reps.push((name, "theirs", i), g[(n + i) * r : (n + i + 1) * r])
-            reps.push((name, "mine", i), g[i * r : (i + 1) * r])
-
-    push_pairs("gate", g_gate, n_up)
+    push_pairs("gate", g_gate, up_rows)
     finish_up()
     for i in range(1, n):
         start_up(i)
         reps.tick()
         if i == 1:
-            out_part = do(lambda w, a: dot(w, a, FIRST).astype(bf16), wd_own, act).reshape(Y, 2, S, blk, T)
+            out_part = do(lambda w, a: dot(w, a, FIRST).astype(bf16), wd_own, act).reshape(Y, 2, S * blk, T)
+            out_theirs = at.core(pick(out_part, 1, 1 - at.c))
             reps.tick()
         finish_up()
     gup_all = do(lambda x: x.reshape(Y * S * ffb, T), up_all())
@@ -780,7 +854,7 @@
     n, start, finish, branch_all = gather_steps(quarter_heads(grad_branch), 3)
     start(0)
     g_up = do(lambda x, g: dot(x, g, LAST).astype(bf16), xn2, gup_all)
-    push_pairs("up", g_up, n_up)
+    push_pairs("up", g_up, up_rows)
     finish()
     for i in range(1, n):
         start(i)
@@ -791,91 +865,41 @@
     gbr_o = at.core(gbr_c)
     gbr = do(lambda a, b: in_order(a, b, 1).reshape(width, T), gbr_c, gbr_o)
     grad_attn = do(lambda w, g: dot(w, g, PLAIN).astype(bf16), wo_own, gbr)
+    reps.tick()
 
     gqkvs = []
     for k in range(2):
-        sq = seqs[k]
-        gqkvs.append(
-            do(
-                attend_back,
-                qkvs[k],
-                grad_attn[:, halves[k]].reshape(heads, HEAD_DIM, H),
-                peaks[k],
-                totals[k],
-                cos[sq],
-                sin[sq],
-                prow[sq],
-                pcol[sq],
-            ).reshape(3, blk, H)
-        )
+        dout = grad_attn[:, halves[k]].reshape(heads, HEAD_DIM, H)
+        gqkvs.append(do(attend_back, qkvs[k], dout, stats[k], table[seqs[k]]).reshape(3, blk, H))
         if k == 0:
             reps.tick()
     n, start, finish, gqkv_done = gather_steps([g.reshape(1, 1, 3 * blk, H) for g in gqkvs], 3)
     start(0)
     attn = lanes(*attns)
     g_out = do(lambda a, g: dot(a, g, LAST).astype(bf16), attn, gbr)
-    for i, g in enumerate(cut(g_out, n_out)):
-        reps.push(("out", i), g)
-    reps.tick()
+    push_rows("out", g_out, out_rows)
+    reps.tick()
+    update(2)
     finish()
     for i in range(1, n):
         start(i)
         if i == 1:
             reps.tick()
+            update(2)
             reps.tick()
+            update(1)
         finish()
 
     def qkv_columns(x):
         return x.reshape(Y, S, 3, blk, T).transpose(2, 0, 1, 3, 4).reshape(3 * Y * S * blk, T)
 
     gqkv = do(qkv_columns, gqkv_done())
+    reps.tick()
     g_qkv = do(lambda x, g: dot(x, g, LAST).astype(bf16), xn1, gqkv)
-    push_pairs("qkv", g_qkv, n_qkv)
-    reps.tick()
+    push_pairs("qkv", g_qkv, qkv_rows)
     part = do(lambda w, g: dot(w, g, FIRST), wq, gqkv)
     part_theirs = at.core(part[blk:])
-
-    jobs = []
-    results = {"down": None, "out": None, "up": None, "qkv": None}
-    states = {
-        "down": (w_down, m_down, v_down),
-        "out": (w_out, m_out, v_out),
-        "up": (w_up, m_up, v_up),
-        "qkv": (w_qkv, m_qkv, v_qkv),
-    }
-    rates = {"down": 0.02, "out": 0.2, "up": 0.03, "qkv": 0.03}
-    received = {}
-    for i in range(n_down):
-        jobs.append(("down", [("down", i)], i, 0, min(512, width)))
-    for part_name, lead in (("gate", 0), ("up", Y)):
-        for i in range(n_up):
-            jobs.append(("up", [(part_name, "mine", i), (part_name, "theirs", i)], i, lead, S * ffb))
-    for i in range(n_out):
-        jobs.append(("out", [("out", i)], i, 0, min(512, width)))
-    for i in range(n_qkv):
-        jobs.append(("qkv", [("qkv", "mine", i), ("qkv", "theirs", i)], i, 0, S * blk))
-
-    def exchange():
-        for name in list(reps.done):
-            if name[1] == "theirs" and name not in received:
-                received[name] = at.core(reps.done[name])
-
-    def update(limit):
-        exchange()
-        while jobs and limit:
-            name, needs, i, lead, unit = jobs[0]
-            if not all(k in reps.done for k in needs):
-                return
-            grads = [received[k] if k[1] == "theirs" else reps.done[k] for k in needs]
-            results[name] = do(
-                lambda s, g, prev: adam_part(s, g, core, rates[name], prev, i, lead, unit),
-                states[name],
-                grads,
-                results[name],
-            )
-            jobs.pop(0)
-            limit -= 1
-
+    update(1)
     reps.tick()
 
     def first_back(a, b, x, mean, inv, gain, gxn2, z2, gqkv0, gqkv1):
@@ -900,6 +924,7 @@
     )
     for axis, step in steps2:
         sums = sum_step(sums, axis, step)
+    reps.tick()
     input_grad = do(
         lambda h, grad, z, scale, gain, sums: h
         + scale * (grad * gain - sums[0:1] / width - z * (sums[1:2] / width)),
@@ -910,39 +935,33 @@
         own_cols[:, 0:1],
         sums,
     )
-    reps.tick()
 
     def to_rows(cols):
         split = do(lambda c: c.reshape(blk, S, at.ctx_size, rows).transpose(2, 1, 0, 3).reshape(nb, blk, rows), cols)
         got = lax.all_to_all(split, plane, split_axis=0, concat_axis=0, tiled=True)
         return do(lambda g: g.reshape(width, rows).T, got)
 
-    out_theirs = at.core(pick(out_part, 1, 1 - at.c))
+    update(1)
     input_rows = to_rows(input_grad)
     reps.tick()
-    update(2)
-    flying = []
-    out_sum = do(
-        lambda a, b: (a.astype(f32) + b.astype(f32)).astype(bf16)[None], pick(out_part, 1, at.c), out_theirs
+    update(1)
+
+    kept, got = pick(out_part, 1, at.c).reshape(-1, T), out_theirs.reshape(-1, T)
+    for k, (axis, step) in enumerate(at.steps(True)):
+        bit = (at.index(axis) // step) % 2
+        send, kept = do(lambda a, b: add_split(a, b, bit.reshape(1)), kept, got)
+        got = at.along(send, axis, step)
+        if k < 2:
+            reps.tick()
+            update(1)
+    out_cols = do(
+        lambda h, a, b: (h + (a.astype(f32) + b.astype(f32))).astype(bf16), hidden, kept, got
     )
-    for k in range(2):
-        axis, step, ax, bit = first_step(bool(k))
-        p = out_sum[..., halves[k]]
-        send = lax.dynamic_slice_in_dim(p, (1 - bit) * step, step, ax)
-        flying.append((lax.dynamic_slice_in_dim(p, bit * step, step, ax), at.along(send, axis, step)))
-    reps.tick()
-    update(2)
-    flying = scatter_rest(flying)
-
-    def output(hidden, a0, b0, a1, b1):
-        a, b = lanes(a0[0], a1[0]), lanes(b0[0], b1[0])
-        return (hidden + (a.astype(f32) + b.astype(f32))).astype(bf16)
-
-    reps.tick()
-    update(2)
-    block_output = to_rows(do(output, hidden, *flying[0], *flying[1]))
-    reps.tick()
-    update(2)
+    reps.tick()
+    update(1)
+    block_output = to_rows(out_cols)
+    reps.tick()
+    update(1)
 
     n_rep = lax.axis_size("rep")
     step = 1
@@ -950,8 +969,6 @@
         other = lax.ppermute(small, "rep", [(i, i ^ step) for i in range(n_rep)])
         small = do(lambda a, b: a + b, small, other)
         step *= 2
-    reps.tick()
-    update(2)
     sent = do(lambda s: jnp.broadcast_to(s.reshape(1, 7, blk), (nb, 7, blk)), small)
     got = lax.all_to_all(sent, plane, split_axis=0, concat_axis=0, tiled=True)
     norm_grad = got.transpose(1, 0, 2).reshape(7, width)

time: 945 us -> 906 us (0.959)
  other arithmetic: 122 us -> 76.4 us
  local copies, waits for them, and re-layouts: 137 us -> 92 us
  Pallas kernels: 96.5 us -> 141 us
  waiting for transfers between devices: 299 us -> 325 us
  starting transfers between devices: 207 us -> 190 us
    pallas_call x0 -> x15, Pallas kernels: none -> 32.4 us  [the longest x8 18.4 us: add_split(): pl.pallas_call(add_split_kernel, grid_spec=pltpu.PrefetchScalarGridSpec(n...]
    ppermute x8 -> x10, waiting for transfers between devices: 29.2 us -> 49.4 us  [tick(): o['out_got'] = lax.ppermute(out['total'], 'rep', [(1, 0), (2, 3)])]
    dynamic_slice x16 -> x0, local copies, waits for them, and re-layouts: 15 us -> none  [the longest x4 7.3 us: send_keep(): lax.dynamic_slice_in_dim(w, b * step, step, ax)]
    convert_element_type x10 -> x2, other arithmetic: 15.1 us -> 1 us  [the longest x1 0.77 us: columns(): x_own, extra = (x[:blk], x[blk:].astype(f32))]
    select_n x22 -> x20, other arithmetic: 20.8 us -> 8.84 us  [stage(): out['out'] = jnp.where(self.end, v['t_got'], v['t'])]
    reshape x3 -> x0, local copies, waits for them, and re-layouts: 11.8 us -> none  [the longest x1 7.7 us: all_cotangents(): return both.transpose(1, 0, 2, 3, 4).reshape(T, width)]
    transpose x1 -> x0, local copies, waits for them, and re-layouts: 11.1 us -> none  [all_cotangents(): return both.transpose(1, 0, 2, 3, 4).reshape(T, width)]
    ppermute x22 -> x21, waiting for transfers between devices: 54.3 us -> 65.3 us  [along(): lax.ppermute(x, 'ctx', [(i, i ^ 2 * step) for i in range(self.ctx_size)])]
  transfers between devices with their start and end apart: 126 -> 122, of which waited for: 50 -> 52; matrix products, arithmetic and copies ran while one was open for 26% -> 19% of each run, Pallas kernels for 9% -> 14%
where the time goes in v4:
time: 906 us; the launch traced here: 893 us
  waiting for transfers between devices  325 us (36%)
  starting transfers between devices  190 us (21%)
  Pallas kernels  141 us (16%)
  local copies, waits for them, and re-layouts  92 us (10%)
  other arithmetic  76.4 us (8%)
  matrix products  64.5 us (7%)
    ppermute x21, waiting for transfers between devices, along(): return lax.ppermute(x, 'shard', [(i, i ^ step) for i in range(self.s_size)])  110 us
    pallas_call x13, Pallas kernels, adam_part(): pl.pallas_call(functools.partial(adam_kernel, rate, two), grid_spec=pltpu...  78.6 us
    ppermute x21, waiting for transfers between devices, along(): lax.ppermute(x, 'ctx', [(i, i ^ 2 * step) for i in range(self.ctx_size)])  65.3 us
    ppermute x10, waiting for transfers between devices, tick(): lax.ppermute(out['send'], 'rep', [(0, 1), (1, 0), (2, 3), (3, 2)])  64.7 us
    dot_general x25, matrix products, dot(): return lax.dot_general(a, b, dims, preferred_element_type=f32)  64.5 us
    ppermute x10, starting transfers between devices, tick(): o['in_got'] = lax.ppermute(out['new'], 'rep', [(0, 1), (3, 2)])  61.7 us
    ppermute x10, waiting for transfers between devices, tick(): o['out_got'] = lax.ppermute(out['total'], 'rep', [(1, 0), (2, 3)])  49.4 us
    unnamed x281, local copies, waits for them, and re-layouts  44.2 us
  transfers between devices with their start and end apart: 122, of which 52 were waited for; matrix products, arithmetic and copies ran while one was open for 19% of the time, Pallas kernels for 14%

profile of v4, /device:TPU:0, one launch (start us, length us, event | category | flops | bytes accessed | tf_op | source)
XLA Modules:
  0.0 892.6 jit_solution(10479266809256899637)
XLA Ops:
  12.8 4.8 all-to-all-start
  66.2 9.5 %collective-permute-done.3.b_ref.d_ref = bf16[1536,512]{1,0:T(8,128)(2,1)} collective-permute-done((bf16[1536,512]{1,0:T(8,128)(2,1)}, bf16[1536,512]{1,0:T(8,128)(2,1)}, u32[]{:S(2)}, u32[]{:S(2)}) %collective-permute-start.3) | collective-permute-done | bytes 1572896 | tf_op jit(solution)/shard_map/ppermute | solution.py:62
  102.8 5.1 shard_map.317
  111.6 4.5 shard_map.318
  122.2 11.4 %collective-permute-done.11.b_ref.d_ref = bf16[512,512]{1,0:T(8,128)(2,1)S(1)} collective-permute-done((bf16[512,512]{1,0:T(8,128)(2,1)S(1)}, bf16[512,512]{1,0:T(8,128)(2,1)S(1)}, u32[]{:S(2)}, u32[]{:S(2)}) %collective-permute-start.11) | collective-permute-done | bytes 524320 | tf_op jit(solution)/shard_map/ppermute | solution.py:62
  137.1 5.7 collective-permute-done.14
  204.3 4.6 shard_map.321
  210.9 4.9 fusion.46
  215.8 6.5 copy.112
  223.4 35.4 %collective-permute-done.21.b_ref.d_ref = bf16[1408,1024]{1,0:T(8,128)(2,1)} collective-permute-done((bf16[1408,1024]{1,0:T(8,128)(2,1)}, bf16[1408,1024]{1,0:T(8,128)(2,1)}, u32[]{:S(2)}, u32[]{:S(2)}) %collective-permute-start.21) | collective-permute-done | bytes 2883616 | tf_op jit(solution)/shard_map/ppermute | solution.py:62
  269.8 28.4 %collective-permute-done.30 = bf16[704,1024]{1,0:T(8,128)(2,1)} collective-permute-done((bf16[704,1024]{1,0:T(8,128)(2,1)}, bf16[704,1024]{1,0:T(8,128)(2,1)}, u32[]{:S(2)}, u32[]{:S(2)}) %collective-permute-start.30) | collective-permute-done | bytes 1441824 | tf_op jit(solution)/shard_map/ppermute | solution.py:62
  339.5 24.7 %collective-permute-done.42 = bf16[1,2,704,512]{3,2,1,0:T(8,128)(2,1)S(1)} collective-permute-done((bf16[1,2,704,512]{3,2,1,0:T(8,128)(2,1)S(1)}, bf16[1,2,704,512]{3,2,1,0:T(8,128)(2,1)S(1)}, u32[]{:S(2)}, u32[]{:S(2)}) %collective-permute-start.42) | collective-permute-done | bytes 1441824 | tf_op jit(solution)/shard_map/ppermute | solution.py:61
  367.8 11.7 %collective-permute-done.39 = bf16[176,2048]{1,0:T(8,128)(2,1)S(1)} collective-permute-done((bf16[176,2048]{1,0:T(8,128)(2,1)S(1)}, bf16[176,2048]{1,0:T(8,128)(2,1)S(1)}, u32[]{:S(2)}, u32[]{:S(2)}) %collective-permute-start.39) | collective-permute-done | bytes 720928 | tf_op jit(solution)/shard_map/ppermute | solution.py:191
  381.2 4.7 collective-permute-start.43
  411.3 9.3 %collective-permute-done.52 = bf16[176,2048]{1,0:T(8,128)(2,1)S(1)} collective-permute-done((bf16[176,2048]{1,0:T(8,128)(2,1)S(1)}, bf16[176,2048]{1,0:T(8,128)(2,1)S(1)}, u32[]{:S(2)}, u32[]{:S(2)}) %collective-permute-start.52) | collective-permute-done | bytes 720928 | tf_op jit(solution)/shard_map/ppermute | solution.py:196
  423.1 8.9 collective-permute-start.54
  461.4 6.1 collective-permute-done.60
  477.8 12.8 %collective-permute-done.64 = bf16[128,2816]{1,0:T(8,128)(2,1)S(1)} collective-permute-done((bf16[128,2816]{1,0:T(8,128)(2,1)S(1)}, bf16[128,2816]{1,0:T(8,128)(2,1)S(1)}, u32[]{:S(2)}, u32[]{:S(2)}) %collective-permute-start.64) | collective-permute-done | bytes 720928 | tf_op jit(solution)/shard_map/ppermute | solution.py:191
  495.9 5.5 shard_map.324
  502.9 7.7 collective-permute-done.66
  511.6 5.5 shard_map.325
  518.4 4.7 collective-permute-start.68
  526.6 13.0 %collective-permute-done.68 = bf16[128,2816]{1,0:T(8,128)(2,1)S(1)} collective-permute-done((bf16[128,2816]{1,0:T(8,128)(2,1)S(1)}, bf16[128,2816]{1,0:T(8,128)(2,1)S(1)}, u32[]{:S(2)}, u32[]{:S(2)}) %collective-permute-start.68) | collective-permute-done | bytes 720928 | tf_op jit(solution)/shard_map/ppermute | solution.py:191
  542.3 5.0 shard_map.326
  547.3 5.1 shard_map.327
  558.7 13.0 %collective-permute-done.70 = bf16[128,2816]{1,0:T(8,128)(2,1)S(1)} collective-permute-done((bf16[128,2816]{1,0:T(8,128)(2,1)S(1)}, bf16[128,2816]{1,0:T(8,128)(2,1)S(1)}, u32[]{:S(2)}, u32[]{:S(2)}) %collective-permute-start.70) | collective-permute-done | bytes 720928 | tf_op jit(solution)/shard_map/ppermute | solution.py:191
  579.7 5.0 shard_map.328
  584.6 5.0 shard_map.329
  598.8 6.9 shard_map.330
  605.9 17.9 %collective-permute-done.80 = bf16[1,2,768,512]{3,2,1,0:T(8,128)(2,1)} collective-permute-done((bf16[1,2,768,512]{3,2,1,0:T(8,128)(2,1)S(1)}, bf16[1,2,768,512]{3,2,1,0:T(8,128)(2,1)}, u32[]{:S(2)}, u32[]{:S(2)}) %collective-permute-start.80) | collective-permute-done | bytes 1572896 | tf_op jit(solution)/shard_map/ppermute | solution.py:61
  633.5 7.0 collective-permute-done.78
  640.6 6.6 collective-permute-start.82
  647.2 6.6 convolution_convert_fusion
  657.5 5.3 fusion.48
  665.7 7.4 shard_map.331
  674.1 10.7 %collective-permute-done.84 = bf16[128,2816]{1,0:T(8,128)(2,1)S(1)} collective-permute-done((bf16[128,2816]{1,0:T(8,128)(2,1)S(1)}, bf16[128,2816]{1,0:T(8,128)(2,1)S(1)}, u32[]{:S(2)}, u32[]{:S(2)}) %collective-permute-start.84) | collective-permute-done | bytes 720928 | tf_op jit(solution)/shard_map/ppermute | solution.py:196
  697.4 7.4 collective-permute-done.94
  704.8 9.2 %collective-permute-start.95 = (bf16[128,3072]{1,0:T(8,128)(2,1)}, bf16[128,3072]{1,0:T(8,128)(2,1)}, u32[]{:S(2)}, u32[]{:S(2)}) collective-permute-start(bf16[128,3072]{1,0:T(8,128)(2,1)} %get-tuple-element.1018), channel_id=1, source_target_pairs={{0,8},{24,16},{1,9},{25,17},{2,10},{26,18},{3,11},{27,19},{4,12},{... | collective-permute-start | bytes 2359304 | tf_op jit(solution)/shard_map/ppermute | solution.py:194
  715.3 7.2 shard_map.332
  741.8 5.0 all-to-all-done.1
  757.0 15.7 %collective-permute-start.99 = (bf16[64,3072]{1,0:T(8,128)(2,1)S(1)}, bf16[64,3072]{1,0:T(8,128)(2,1)S(1)}, u32[]{:S(2)}, u32[]{:S(2)}) collective-permute-start(bf16[64,3072]{1,0:T(8,128)(2,1)S(1)} %copy-done.101), channel_id=1, source_target_pairs={{0,8},{24,16},{1,9},{25,17},{2,10},{26,18},{3,11},{27,19},{4,12},{... | collective-permute-start | bytes 1179656 | tf_op jit(solution)/shard_map/ppermute | solution.py:194
  772.7 7.0 shard_map.333
  800.1 7.5 collective-permute-done.98.b_ref.d_ref
  828.4 9.6 %shard_map.338 = (f32[256,6144]{1,0:T(8,128)}, f32[256,6144]{1,0:T(8,128)}, f32[256,6144]{1,0:T(8,128)}) custom-call(s32[1]{0:T(128)} %bitcast.8.core_ref, f32[256,6144]{1,0:T(8,128)} %w_ref.16, f32[256,6144]{1,0:T(8,128)} %m_ref.12, f32[256,6144]{1,0:T(8,128)} %v_ref.12, bf16[128,3072]{1,0:T(8,128)(2,1)S(1)} %broadcast_select_fusion.13.refs_0_, ...), custom_call_target="tpu_custom_call" | custom-call | flops 1024 | bytes 1024 | tf_op jit(solution)/shard_map/pallas_call | solution.py:353
  839.3 6.2 shard_map.339
  863.8 8.5 all-to-all-done.2
  874.8 11.1 %collective-permute-done.116 = bf16[64,3072]{1,0:T(8,128)(2,1)S(1)} collective-permute-done((bf16[64,3072]{1,0:T(8,128)(2,1)S(1)}, bf16[64,3072]{1,0:T(8,128)(2,1)S(1)}, u32[]{:S(2)}, u32[]{:S(2)}) %collective-permute-start.116) | collective-permute-done | bytes 393248 | tf_op jit(solution)/shard_map/ppermute | solution.py:196
  886.0 6.2 shard_map.340
  (764 shorter events, 451.2 us)
Async XLA Ops:
  39.0 36.8 %collective-permute-start.3 = (bf16[1536,512]{1,0:T(8,128)(2,1)}, bf16[1536,512]{1,0:T(8,128)(2,1)}, u32[]{:S(2)}, u32[]{:S(2)}) collective-permute-start(bf16[1536,512]{1,0:T(8,128)(2,1)} %convolution_convert_fusion.12), channel_id=1, source_target_pairs={{0,1},{1,0},{2,3},{3,2},{4,5},{5,4},{6,7},{7,6},{8,9},{9,8},{10,11... | collective-permute-start | bytes 4718600 | tf_op jit(solution)/shard_map/ppermute | solution.py:62
  42.1 40.1 %collective-permute-start.7 = (bf16[1536,512]{1,0:T(8,128)(2,1)}, bf16[1536,512]{1,0:T(8,128)(2,1)}, u32[]{:S(2)}, u32[]{:S(2)}) collective-permute-start(bf16[1536,512]{1,0:T(8,128)(2,1)} %convolution_convert_fusion.11), channel_id=1, source_target_pairs={{0,4},{2,6},{4,0},{6,2},{1,5},{3,7},{5,1},{7,3},{8,12},{10,14},{12... | collective-permute-start | bytes 4718600 | tf_op jit(solution)/shard_map/ppermute | solution.py:61
  56.5 33.0 %collective-permute-start.6 = (bf16[2816,256]{1,0:T(8,128)(2,1)}, bf16[2816,256]{1,0:T(8,128)(2,1)}, u32[]{:S(2)}, u32[]{:S(2)}) collective-permute-start(bf16[2816,256]{1,0:T(8,128)(2,1)} %get-tuple-element.618), channel_id=1, source_target_pairs={{0,2},{2,0},{4,6},{6,4},{1,3},{3,1},{5,7},{7,5},{8,10},{10,8},{12,... | collective-permute-start | bytes 4325384 | tf_op jit(solution)/shard_map/ppermute | solution.py:57
  59.2 35.9 %collective-permute-start.5 = (bf16[2816,256]{1,0:T(8,128)(2,1)}, bf16[2816,256]{1,0:T(8,128)(2,1)}, u32[]{:S(2)}, u32[]{:S(2)}) collective-permute-start(bf16[2816,256]{1,0:T(8,128)(2,1)} %get-tuple-element.617), channel_id=1, source_target_pairs={{0,2},{2,0},{4,6},{6,4},{1,3},{3,1},{5,7},{7,5},{8,10},{10,8},{12,... | collective-permute-start | bytes 4325384 | tf_op jit(solution)/shard_map/ppermute | solution.py:57
  81.6 19.1 %collective-permute-start.4 = (bf16[768,512]{1,0:T(8,128)(2,1)}, bf16[768,512]{1,0:T(8,128)(2,1)}, u32[]{:S(2)}, u32[]{:S(2)}) collective-permute-start(bf16[768,512]{1,0:T(8,128)(2,1)} %get-tuple-element.616), channel_id=1, source_target_pairs={{0,4},{2,6},{4,0},{6,2},{1,5},{3,7},{5,1},{7,3},{8,12},{10,14},{12... | collective-permute-start | bytes 2359304 | tf_op jit(solution)/shard_map/ppermute | solution.py:61
  88.0 21.5 %collective-permute-start.9 = (bf16[768,512]{1,0:T(8,128)(2,1)}, bf16[768,512]{1,0:T(8,128)(2,1)}, u32[]{:S(2)}, u32[]{:S(2)}) collective-permute-start(bf16[768,512]{1,0:T(8,128)(2,1)} %get-tuple-element.621), channel_id=1, source_target_pairs={{0,1},{1,0},{2,3},{3,2},{4,5},{5,4},{6,7},{7,6},{8,9},{9,8},{10,11... | collective-permute-start | bytes 2359304 | tf_op jit(solution)/shard_map/ppermute | solution.py:62
  173.1 25.4 %collective-permute-start.22 = (bf16[2,1,64,2048]{3,2,1,0:T(8,128)(2,1)}, bf16[2,1,64,2048]{3,2,1,0:T(8,128)(2,1)}, u32[]{:S(2)}, u32[]{:S(2)}) collective-permute-start(bf16[2,1,64,2048]{3,2,1,0:T(8,128)(2,1)} %pad_maximum_fusion.10), channel_id=1, source_target_pairs={{0,1},{1,0},{2,3},{3,2},{4,5},{5,4},{6,7},{7,6},{8,9},{9,8},{10,11... | collective-permute-start | bytes 1572872 | tf_op jit(solution)/shard_map/ppermute | solution.py:62
  175.4 23.1 %collective-permute-start.23 = (bf16[1,2,64,2048]{3,2,1,0:T(8,128)(2,1)}, bf16[1,2,64,2048]{3,2,1,0:T(8,128)(2,1)}, u32[]{:S(2)}, u32[]{:S(2)}) collective-permute-start(bf16[1,2,64,2048]{3,2,1,0:T(8,128)(2,1)} %pad_maximum_fusion.11), channel_id=1, source_target_pairs={{0,4},{2,6},{4,0},{6,2},{1,5},{3,7},{5,1},{7,3},{8,12},{10,14},{12... | collective-permute-start | bytes 1572872 | tf_op jit(solution)/shard_map/ppermute | solution.py:61
  195.3 68.5 %collective-permute-start.29 = (bf16[1408,1024]{1,0:T(8,128)(2,1)}, bf16[1408,1024]{1,0:T(8,128)(2,1)}, u32[]{:S(2)}, u32[]{:S(2)}) collective-permute-start(bf16[1408,1024]{1,0:T(8,128)(2,1)} %convolution_convert_fusion.6), channel_id=1, source_target_pairs={{0,4},{2,6},{4,0},{6,2},{1,5},{3,7},{5,1},{7,3},{8,12},{10,14},{12... | collective-permute-start | bytes 8650760 | tf_op jit(solution)/shard_map/ppermute | solution.py:61
  196.6 62.2 %collective-permute-start.21 = (bf16[1408,1024]{1,0:T(8,128)(2,1)}, bf16[1408,1024]{1,0:T(8,128)(2,1)}, u32[]{:S(2)}, u32[]{:S(2)}) collective-permute-start(bf16[1408,1024]{1,0:T(8,128)(2,1)} %convolution_convert_fusion.7), channel_id=1, source_target_pairs={{0,1},{1,0},{2,3},{3,2},{4,5},{5,4},{6,7},{7,6},{8,9},{9,8},{10,11... | collective-permute-start | bytes 8650760 | tf_op jit(solution)/shard_map/ppermute | solution.py:62
  267.8 30.4 %collective-permute-start.30 = (bf16[704,1024]{1,0:T(8,128)(2,1)}, bf16[704,1024]{1,0:T(8,128)(2,1)}, u32[]{:S(2)}, u32[]{:S(2)}) collective-permute-start(bf16[704,1024]{1,0:T(8,128)(2,1)} %get-tuple-element.726), channel_id=1, source_target_pairs={{0,1},{1,0},{2,3},{3,2},{4,5},{5,4},{6,7},{7,6},{8,9},{9,8},{10,11... | collective-permute-start | bytes 4325384 | tf_op jit(solution)/shard_map/ppermute | solution.py:62
  268.7 30.1 %collective-permute-start.28 = (bf16[704,1024]{1,0:T(8,128)(2,1)}, bf16[704,1024]{1,0:T(8,128)(2,1)}, u32[]{:S(2)}, u32[]{:S(2)}) collective-permute-start(bf16[704,1024]{1,0:T(8,128)(2,1)} %get-tuple-element.722), channel_id=1, source_target_pairs={{0,4},{2,6},{4,0},{6,2},{1,5},{3,7},{5,1},{7,3},{8,12},{10,14},{12... | collective-permute-start | bytes 4325384 | tf_op jit(solution)/shard_map/ppermute | solution.py:61
  319.0 47.4 %collective-permute-start.41 = (bf16[2,1,704,512]{3,2,1,0:T(8,128)(2,1)S(1)}, bf16[2,1,704,512]{3,2,1,0:T(8,128)(2,1)S(1)}, u32[]{:S(2)}, u32[]{:S(2)}) collective-permute-start(bf16[2,1,704,512]{3,2,1,0:T(8,128)(2,1)S(1)} %pad_maximum_fusion.3), channel_id=1, source_target_pairs={{0,1},{1,0},{2,3},{3,2},{4,5},{5,4},{6,7},{7,6},{8,9},{9,8},{10,11... | collective-permute-start | bytes 4325384 | tf_op jit(solution)/shard_map/ppermute | solution.py:62
  331.0 33.2 %collective-permute-start.42 = (bf16[1,2,704,512]{3,2,1,0:T(8,128)(2,1)S(1)}, bf16[1,2,704,512]{3,2,1,0:T(8,128)(2,1)S(1)}, u32[]{:S(2)}, u32[]{:S(2)}) collective-permute-start(bf16[1,2,704,512]{3,2,1,0:T(8,128)(2,1)S(1)} %pad_maximum_fusion.4), channel_id=1, source_target_pairs={{0,4},{2,6},{4,0},{6,2},{1,5},{3,7},{5,1},{7,3},{8,12},{10,14},{12... | collective-permute-start | bytes 4325384 | tf_op jit(solution)/shard_map/ppermute | solution.py:61
  335.1 57.6 %collective-permute-start.46 = (bf16[1,1,704,512]{3,2,1,0:T(8,128)(2,1)S(1)}, bf16[1,1,704,512]{3,2,1,0:T(8,128)(2,1)S(1)}, u32[]{:S(2)}, u32[]{:S(2)}) collective-permute-start(bf16[1,1,704,512]{3,2,1,0:T(8,128)(2,1)S(1)} %get-tuple-element.779), channel_id=1, source_target_pairs={{0,1},{1,0},{2,3},{3,2},{4,5},{5,4},{6,7},{7,6},{8,9},{9,8},{10,11... | collective-permute-start | bytes 2162696 | tf_op jit(solution)/shard_map/ppermute | solution.py:62
  335.9 56.7 %collective-permute-start.45 = (bf16[1,1,704,512]{3,2,1,0:T(8,128)(2,1)S(1)}, bf16[1,1,704,512]{3,2,1,0:T(8,128)(2,1)S(1)}, u32[]{:S(2)}, u32[]{:S(2)}) collective-permute-start(bf16[1,1,704,512]{3,2,1,0:T(8,128)(2,1)S(1)} %get-tuple-element.774), channel_id=1, source_target_pairs={{0,4},{2,6},{4,0},{6,2},{1,5},{3,7},{5,1},{7,3},{8,12},{10,14},{12... | collective-permute-start | bytes 2162696 | tf_op jit(solution)/shard_map/ppermute | solution.py:61
  338.3 29.5 %collective-permute-start.40 = (bf16[176,2048]{1,0:T(8,128)(2,1)S(1)}, bf16[176,2048]{1,0:T(8,128)(2,1)S(1)}, u32[]{:S(2)}, u32[]{:S(2)}) collective-permute-start(bf16[176,2048]{1,0:T(8,128)(2,1)S(1)} %reduce-precision_convert_fusion.25), channel_id=1, source_target_pairs={{8,16},{16,8},{9,17},{17,9},{10,18},{18,10},{11,19},{19,11},{12,20... | collective-permute-start | bytes 2162696 | tf_op jit(solution)/shard_map/ppermute | solution.py:204
  392.9 39.1 %collective-permute-start.49 = (bf16[1,2,704,512]{3,2,1,0:T(8,128)(2,1)S(1)}, bf16[1,2,704,512]{3,2,1,0:T(8,128)(2,1)S(1)}, u32[]{:S(2)}, u32[]{:S(2)}) collective-permute-start(bf16[1,2,704,512]{3,2,1,0:T(8,128)(2,1)S(1)} %pad_maximum_fusion.6), channel_id=1, source_target_pairs={{0,4},{2,6},{4,0},{6,2},{1,5},{3,7},{5,1},{7,3},{8,12},{10,14},{12... | collective-permute-start | bytes 4325384 | tf_op jit(solution)/shard_map/ppermute | solution.py:61
  394.1 37.9 %collective-permute-start.48 = (bf16[2,1,704,512]{3,2,1,0:T(8,128)(2,1)S(1)}, bf16[2,1,704,512]{3,2,1,0:T(8,128)(2,1)S(1)}, u32[]{:S(2)}, u32[]{:S(2)}) collective-permute-start(bf16[2,1,704,512]{3,2,1,0:T(8,128)(2,1)S(1)} %pad_maximum_fusion.5), channel_id=1, source_target_pairs={{0,1},{1,0},{2,3},{3,2},{4,5},{5,4},{6,7},{7,6},{8,9},{9,8},{10,11... | collective-permute-start | bytes 4325384 | tf_op jit(solution)/shard_map/ppermute | solution.py:62
  399.4 21.3 %collective-permute-start.50 = (bf16[128,2816]{1,0:T(8,128)(2,1)S(1)}, bf16[128,2816]{1,0:T(8,128)(2,1)S(1)}, u32[]{:S(2)}, u32[]{:S(2)}) collective-permute-start(bf16[128,2816]{1,0:T(8,128)(2,1)S(1)} %get-tuple-element.794), channel_id=1, source_target_pairs={{0,8},{24,16},{1,9},{25,17},{2,10},{26,18},{3,11},{27,19},{4,12},{... | collective-permute-start | bytes 2162696 | tf_op jit(solution)/shard_map/ppermute | solution.py:194
  440.7 19.8 %collective-permute-start.62 = (bf16[128,2816]{1,0:T(8,128)(2,1)S(1)}, bf16[128,2816]{1,0:T(8,128)(2,1)S(1)}, u32[]{:S(2)}, u32[]{:S(2)}) collective-permute-start(bf16[128,2816]{1,0:T(8,128)(2,1)S(1)} %reduce-precision_convert_fusion.17), channel_id=1, source_target_pairs={{8,16},{16,8},{9,17},{17,9},{10,18},{18,10},{11,19},{19,11},{12,20... | collective-permute-start | bytes 2162696 | tf_op jit(solution)/shard_map/ppermute | solution.py:204
  470.1 124.3 %collective-permute-start.81 = (bf16[128,2816]{1,0:T(8,128)(2,1)}, bf16[128,2816]{1,0:T(8,128)(2,1)S(1)}, u32[]{:S(2)}, u32[]{:S(2)}) collective-permute-start(bf16[128,2816]{1,0:T(8,128)(2,1)} %broadcast_select_fusion.30), channel_id=1, source_target_pairs={{0,2},{2,0},{4,6},{6,4},{1,3},{3,1},{5,7},{7,5},{8,10},{10,8},{12,... | collective-permute-start | bytes 2162696 | tf_op jit(solution)/shard_map/ppermute | solution.py:57
  471.8 18.9 %collective-permute-start.64 = (bf16[128,2816]{1,0:T(8,128)(2,1)S(1)}, bf16[128,2816]{1,0:T(8,128)(2,1)S(1)}, u32[]{:S(2)}, u32[]{:S(2)}) collective-permute-start(bf16[128,2816]{1,0:T(8,128)(2,1)S(1)} %get-tuple-element.1161), channel_id=1, source_target_pairs={{0,8},{8,0},{16,24},{24,16},{1,9},{9,1},{17,25},{25,17},{2,10},{10... | collective-permute-start | bytes 2162696 | tf_op jit(solution)/shard_map/ppermute | solution.py:191
  501.4 51.4 %collective-permute-start.72 = (bf16[1,1,768,512]{3,2,1,0:T(8,128)(2,1)S(1)}, bf16[1,1,768,512]{3,2,1,0:T(8,128)(2,1)}, u32[]{:S(2)}, u32[]{:S(2)}) collective-permute-start(bf16[1,1,768,512]{3,2,1,0:T(8,128)(2,1)S(1)} %bitcast.195), channel_id=1, source_target_pairs={{0,4},{2,6},{4,0},{6,2},{1,5},{3,7},{5,1},{7,3},{8,12},{10,14},{12... | collective-permute-start | bytes 2359304 | tf_op jit(solution)/shard_map/ppermute | solution.py:61
  511.6 152.8 %collective-permute-start.85 = (bf16[128,2816]{1,0:T(8,128)(2,1)}, bf16[128,2816]{1,0:T(8,128)(2,1)S(1)}, u32[]{:S(2)}, u32[]{:S(2)}) collective-permute-start(bf16[128,2816]{1,0:T(8,128)(2,1)} %broadcast_select_fusion.26), channel_id=1, source_target_pairs={{0,2},{2,0},{4,6},{6,4},{1,3},{3,1},{5,7},{7,5},{8,10},{10,8},{12,... | collective-permute-start | bytes 2162696 | tf_op jit(solution)/shard_map/ppermute | solution.py:57
  518.4 21.2 %collective-permute-start.68 = (bf16[128,2816]{1,0:T(8,128)(2,1)S(1)}, bf16[128,2816]{1,0:T(8,128)(2,1)S(1)}, u32[]{:S(2)}, u32[]{:S(2)}) collective-permute-start(bf16[128,2816]{1,0:T(8,128)(2,1)S(1)} %get-tuple-element.1157), channel_id=1, source_target_pairs={{0,8},{8,0},{16,24},{24,16},{1,9},{9,1},{17,25},{25,17},{2,10},{10... | collective-permute-start | bytes 2162696 | tf_op jit(solution)/shard_map/ppermute | solution.py:191
  525.3 30.9 %collective-permute-start.73 = (bf16[1,1,768,512]{3,2,1,0:T(8,128)(2,1)S(1)}, bf16[1,1,768,512]{3,2,1,0:T(8,128)(2,1)S(1)}, u32[]{:S(2)}, u32[]{:S(2)}) collective-permute-start(bf16[1,1,768,512]{3,2,1,0:T(8,128)(2,1)S(1)} %bitcast.198), channel_id=1, source_target_pairs={{0,1},{1,0},{2,3},{3,2},{4,5},{5,4},{6,7},{7,6},{8,9},{9,8},{10,11... | collective-permute-start | bytes 2359304 | tf_op jit(solution)/shard_map/ppermute | solution.py:62
  557.6 67.5 %collective-permute-start.79 = (bf16[2,1,768,512]{3,2,1,0:T(8,128)(2,1)S(1)}, bf16[2,1,768,512]{3,2,1,0:T(8,128)(2,1)}, u32[]{:S(2)}, u32[]{:S(2)}) collective-permute-start(bf16[2,1,768,512]{3,2,1,0:T(8,128)(2,1)S(1)} %pad_maximum_fusion.1), channel_id=1, source_target_pairs={{0,1},{1,0},{2,3},{3,2},{4,5},{5,4},{6,7},{7,6},{8,9},{9,8},{10,11... | collective-permute-start | bytes 4718600 | tf_op jit(solution)/shard_map/ppermute | solution.py:62
  589.6 34.2 %collective-permute-start.80 = (bf16[1,2,768,512]{3,2,1,0:T(8,128)(2,1)S(1)}, bf16[1,2,768,512]{3,2,1,0:T(8,128)(2,1)}, u32[]{:S(2)}, u32[]{:S(2)}) collective-permute-start(bf16[1,2,768,512]{3,2,1,0:T(8,128)(2,1)S(1)} %pad_maximum_fusion.2), channel_id=1, source_target_pairs={{0,4},{2,6},{4,0},{6,2},{1,5},{3,7},{5,1},{7,3},{8,12},{10,14},{12... | collective-permute-start | bytes 4718600 | tf_op jit(solution)/shard_map/ppermute | solution.py:61
  593.3 122.0 %collective-permute-start.87 = (bf16[128,2816]{1,0:T(8,128)(2,1)}, bf16[128,2816]{1,0:T(8,128)(2,1)S(1)}, u32[]{:S(2)}, u32[]{:S(2)}) collective-permute-start(bf16[128,2816]{1,0:T(8,128)(2,1)} %broadcast_select_fusion.21), channel_id=1, source_target_pairs={{0,2},{2,0},{4,6},{6,4},{1,3},{3,1},{5,7},{7,5},{8,10},{10,8},{12,... | collective-permute-start | bytes 2162696 | tf_op jit(solution)/shard_map/ppermute | solution.py:57
  594.3 39.2 %collective-permute-start.76 = (bf16[128,2048]{1,0:T(8,128)(2,1)S(1)}, bf16[128,2048]{1,0:T(8,128)(2,1)}, u32[]{:S(2)}, u32[]{:S(2)}) collective-permute-start(bf16[128,2048]{1,0:T(8,128)(2,1)S(1)} %get-tuple-element.936), channel_id=1, source_target_pairs={{0,8},{24,16},{1,9},{25,17},{2,10},{26,18},{3,11},{27,19},{4,12},{... | collective-permute-start | bytes 1572872 | tf_op jit(solution)/shard_map/ppermute | solution.py:194
  640.6 33.5 %collective-permute-start.82 = (bf16[128,2048]{1,0:T(8,128)(2,1)}, bf16[128,2048]{1,0:T(8,128)(2,1)}, u32[]{:S(2)}, u32[]{:S(2)}) collective-permute-start(bf16[128,2048]{1,0:T(8,128)(2,1)} %get-tuple-element.974), channel_id=1, source_target_pairs={{0,8},{24,16},{1,9},{25,17},{2,10},{26,18},{3,11},{27,19},{4,12},{... | collective-permute-start | bytes 1572872 | tf_op jit(solution)/shard_map/ppermute | solution.py:194
  662.9 24.2 %collective-permute-start.88 = (f32[256,1024]{1,0:T(8,128)S(1)}, f32[256,1024]{1,0:T(8,128)S(1)}, u32[]{:S(2)}, u32[]{:S(2)}) collective-permute-start(f32[256,1024]{1,0:T(8,128)S(1)} %get-tuple-element.1215), channel_id=1, source_target_pairs={{0,2},{2,0},{4,6},{6,4},{1,3},{3,1},{5,7},{7,5},{8,10},{10,8},{12,... | collective-permute-start | bytes 3145736 | tf_op jit(solution)/shard_map/ppermute | solution.py:57
  664.3 20.4 %collective-permute-start.84 = (bf16[128,2816]{1,0:T(8,128)(2,1)S(1)}, bf16[128,2816]{1,0:T(8,128)(2,1)S(1)}, u32[]{:S(2)}, u32[]{:S(2)}) collective-permute-start(bf16[128,2816]{1,0:T(8,128)(2,1)S(1)} %reduce-precision_convert_fusion.4), channel_id=1, source_target_pairs={{8,0},{16,24},{9,1},{17,25},{10,2},{18,26},{11,3},{19,27},{12,4},{... | collective-permute-start | bytes 2162696 | tf_op jit(solution)/shard_map/ppermute | solution.py:196
  685.6 19.2 %collective-permute-start.92 = (bf16[128,3072]{1,0:T(8,128)(2,1)S(1)}, bf16[128,3072]{1,0:T(8,128)(2,1)S(1)}, u32[]{:S(2)}, u32[]{:S(2)}) collective-permute-start(bf16[128,3072]{1,0:T(8,128)(2,1)S(1)} %get-tuple-element.996), channel_id=1, source_target_pairs={{0,8},{24,16},{1,9},{25,17},{2,10},{26,18},{3,11},{27,19},{4,12},{... | collective-permute-start | bytes 2359304 | tf_op jit(solution)/shard_map/ppermute | solution.py:194
  697.0 82.7 %collective-permute-start.47 = (bf16[2,512,1024]{2,1,0:T(8,128)(2,1)}, bf16[2,512,1024]{2,1,0:T(8,128)(2,1)}, u32[]{:S(2)}, u32[]{:S(2)}) collective-permute-start(bf16[2,512,1024]{2,1,0:T(8,128)(2,1)} %get-tuple-element.1181), channel_id=1, source_target_pairs={{0,2},{2,0},{4,6},{6,4},{1,3},{3,1},{5,7},{7,5},{8,10},{10,8},{12,... | collective-permute-start | bytes 6291464 | tf_op jit(solution)/shard_map/ppermute | solution.py:57
  704.8 52.2 %collective-permute-start.86 = (bf16[128,2816]{1,0:T(8,128)(2,1)}, bf16[128,2816]{1,0:T(8,128)(2,1)}, u32[]{:S(2)}, u32[]{:S(2)}) collective-permute-start(bf16[128,2816]{1,0:T(8,128)(2,1)} %broadcast_select_fusion.19), channel_id=1, source_target_pairs={{0,2},{2,0},{4,6},{6,4},{1,3},{3,1},{5,7},{7,5},{8,10},{10,8},{12,... | collective-permute-start | bytes 2162696 | tf_op jit(solution)/shard_map/ppermute | solution.py:57
  704.8 45.9 %collective-permute-start.95 = (bf16[128,3072]{1,0:T(8,128)(2,1)}, bf16[128,3072]{1,0:T(8,128)(2,1)}, u32[]{:S(2)}, u32[]{:S(2)}) collective-permute-start(bf16[128,3072]{1,0:T(8,128)(2,1)} %get-tuple-element.1018), channel_id=1, source_target_pairs={{0,8},{24,16},{1,9},{25,17},{2,10},{26,18},{3,11},{27,19},{4,12},{... | collective-permute-start | bytes 2359304 | tf_op jit(solution)/shard_map/ppermute | solution.py:194
  727.6 19.2 %all-to-all-start.1 = ((f32[8,256,128]{2,1,0:T(8,128)}), f32[8,256,128]{2,1,0:T(8,128)}, u32[]{:S(2)}, u32[]{:S(2)}) async-start(f32[8,256,128]{2,1,0:T(8,128)} %bitcast.222), calls=%async_computation.1 | async-start | bytes 2097152 | tf_op jit(solution)/shard_map/all_to_all | solution.py:941
  750.7 94.8 %collective-permute-start.113 = (f32[7,256]{1,0:T(8,128)}, f32[7,256]{1,0:T(8,128)}, u32[]{:S(2)}, u32[]{:S(2)}) collective-permute-start(f32[7,256]{1,0:T(8,128)} %concatenate.187), channel_id=1, source_target_pairs={{0,8},{8,0},{16,24},{24,16},{1,9},{9,1},{17,25},{25,17},{2,10},{10... | collective-permute-start | bytes 21512 | tf_op jit(solution)/shard_map/ppermute | solution.py:969
  752.4 34.5 %collective-permute-start.101 = (bf16[128,3072]{1,0:T(8,128)(2,1)S(1)}, bf16[128,3072]{1,0:T(8,128)(2,1)S(1)}, u32[]{:S(2)}, u32[]{:S(2)}) collective-permute-start(bf16[128,3072]{1,0:T(8,128)(2,1)S(1)} %reduce-precision_convert_fusion.1), channel_id=1, source_target_pairs={{8,0},{16,24},{9,1},{17,25},{10,2},{18,26},{11,3},{19,27},{12,4},{... | collective-permute-start | bytes 2359304 | tf_op jit(solution)/shard_map/ppermute | solution.py:196
  755.4 31.5 %collective-permute-start.100 = (bf16[128,3072]{1,0:T(8,128)(2,1)S(1)}, bf16[128,3072]{1,0:T(8,128)(2,1)}, u32[]{:S(2)}, u32[]{:S(2)}) collective-permute-start(bf16[128,3072]{1,0:T(8,128)(2,1)S(1)} %reduce-precision_convert_fusion.2), channel_id=1, source_target_pairs={{8,16},{16,8},{9,17},{17,9},{10,18},{18,10},{11,19},{19,11},{12,20... | collective-permute-start | bytes 2359304 | tf_op jit(solution)/shard_map/ppermute | solution.py:204
  757.0 29.9 %collective-permute-start.99 = (bf16[64,3072]{1,0:T(8,128)(2,1)S(1)}, bf16[64,3072]{1,0:T(8,128)(2,1)S(1)}, u32[]{:S(2)}, u32[]{:S(2)}) collective-permute-start(bf16[64,3072]{1,0:T(8,128)(2,1)S(1)} %copy-done.101), channel_id=1, source_target_pairs={{0,8},{24,16},{1,9},{25,17},{2,10},{26,18},{3,11},{27,19},{4,12},{... | collective-permute-start | bytes 1179656 | tf_op jit(solution)/shard_map/ppermute | solution.py:194
  783.9 23.7 %collective-permute-start.98 = (bf16[512,1024]{1,0:T(8,128)(2,1)S(1)}, bf16[512,1024]{1,0:T(8,128)(2,1)S(1)}, u32[]{:S(2)}, u32[]{:S(2)}) collective-permute-start(bf16[512,1024]{1,0:T(8,128)(2,1)S(1)} %get-tuple-element.1015), channel_id=1, source_target_pairs={{0,4},{2,6},{4,0},{6,2},{1,5},{3,7},{5,1},{7,3},{8,12},{10,14},{12... | collective-permute-start | bytes 3145736 | tf_op jit(solution)/shard_map/ppermute | solution.py:61
  787.0 22.5 %collective-permute-start.103 = (bf16[64,3072]{1,0:T(8,128)(2,1)S(1)}, bf16[64,3072]{1,0:T(8,128)(2,1)S(1)}, u32[]{:S(2)}, u32[]{:S(2)}) collective-permute-start(bf16[64,3072]{1,0:T(8,128)(2,1)S(1)} %copy-done.100), channel_id=1, source_target_pairs={{0,8},{24,16},{1,9},{25,17},{2,10},{26,18},{3,11},{27,19},{4,12},{... | collective-permute-start | bytes 1179656 | tf_op jit(solution)/shard_map/ppermute | solution.py:194
  791.8 19.4 %collective-permute-start.105 = (bf16[128,3072]{1,0:T(8,128)(2,1)S(1)}, bf16[128,3072]{1,0:T(8,128)(2,1)S(1)}, u32[]{:S(2)}, u32[]{:S(2)}) collective-permute-start(bf16[128,3072]{1,0:T(8,128)(2,1)S(1)} %reduce-precision_convert_fusion), channel_id=1, source_target_pairs={{8,0},{16,24},{9,1},{17,25},{10,2},{18,26},{11,3},{19,27},{12,4},{... | collective-permute-start | bytes 2359304 | tf_op jit(solution)/shard_map/ppermute | solution.py:196
  807.7 20.7 %collective-permute-start.106 = (bf16[128,3072]{1,0:T(8,128)(2,1)S(1)}, bf16[128,3072]{1,0:T(8,128)(2,1)S(1)}, u32[]{:S(2)}, u32[]{:S(2)}) collective-permute-start(bf16[128,3072]{1,0:T(8,128)(2,1)S(1)} %broadcast_select_fusion.12), channel_id=1, source_target_pairs={{0,2},{2,0},{4,6},{6,4},{1,3},{3,1},{5,7},{7,5},{8,10},{10,8},{12,... | collective-permute-start | bytes 2359304 | tf_op jit(solution)/shard_map/ppermute | solution.py:57
  846.9 26.4 %collective-permute-start.112 = (bf16[64,3072]{1,0:T(8,128)(2,1)S(1)}, bf16[64,3072]{1,0:T(8,128)(2,1)S(1)}, u32[]{:S(2)}, u32[]{:S(2)}) collective-permute-start(bf16[64,3072]{1,0:T(8,128)(2,1)S(1)} %reduce-precision_convert_fusion.33), channel_id=1, source_target_pairs={{8,0},{16,24},{9,1},{17,25},{10,2},{18,26},{11,3},{19,27},{12,4},{... | collective-permute-start | bytes 1179656 | tf_op jit(solution)/shard_map/ppermute | solution.py:196
  (210 other events, 1924.7 us)

commit v5 on v4

--- a/solution.py
+++ b/solution.py
@@ -140,68 +140,87 @@
         z = lax.axis_index("rep")
         self.end = (z == 0) | (z == lax.axis_size("rep") - 1)
         self.queue = []
-        self.outer = None
-        self.inner = None
+        self.flight = []
         self.done = {}
 
     def push(self, name, g):
         self.queue.append((name, g))
 
     def busy(self):
-        return bool(self.queue or self.outer or self.inner)
+        return bool(self.queue or self.flight)
 
     def tick(self):
-        outer, inner = self.outer, self.inner
+        old = {}
+        if len(self.flight) == 2 or (self.flight and not self.queue):
+            old = self.flight.pop(0)
         new = self.queue.pop(0) if self.queue else None
         values = {}
-        if outer and outer["in"]:
-            values["g"], values["g_got"] = outer["in"][1], outer["in_got"]
-        if outer and outer["out"]:
-            values["t"], values["t_got"] = outer["out"][1], outer["out_got"]
-        if inner:
-            values["s"], values["s_got"] = inner[1], inner[2]
+        if "in" in old:
+            values["g"], values["g_got"] = old["in"][1], old["in_got"]
+        if "mid" in old:
+            values["s"], values["s_got"] = old["mid"][1], old["mid_got"]
         if new:
             values["new"] = new[1]
-        both = new and inner and new[1].shape == inner[1].shape
+        both = new and "mid" in old and new[1].shape == old["mid"][1].shape
+        if "out" in old:
+            values["out_got"] = old["out_got"]
 
         def stage(v):
             def add(a, b):
                 return lax.reduce_precision(a.astype(f32) + b.astype(f32), 8, 7).astype(bf16)
 
             out = {}
+            if "g" in v:
+                out["a_sum"] = add(v["g"], v["g_got"])
             if "s" in v:
-                out["total"] = add(v["s"], v["s_got"])
-            if "g" in v:
-                out["sum"] = add(v["g"], v["g_got"])
-            if "t" in v:
-                out["out"] = jnp.where(self.end, v["t_got"], v["t"])
-            if both:
-                out["send"] = jnp.where(self.end, v["new"], out["total"])
-            elif "new" in v:
+                total = add(v["s"], v["s_got"])
+                out["total"] = jnp.where(self.end, v["new"], total) if both else total
+            if "new" in v and not both:
                 out["new"] = v["new"]
+            if "out_got" in v:
+                out["z_got"] = v["out_got"]
             return out
 
+        if not values:
+            return
         out = self.order(stage, values)
-        if outer and outer["out"]:
-            self.done[outer["out"][0]] = out["out"]
-        self.outer = None
-        if new or inner:
-            o = {"in": None, "out": None}
-            if both:
-                o["in_got"] = o["out_got"] = lax.ppermute(out["send"], "rep", [(0, 1), (1, 0), (2, 3), (3, 2)])
-            else:
-                if new:
-                    o["in_got"] = lax.ppermute(out["new"], "rep", [(0, 1), (3, 2)])
-                if inner:
-                    o["out_got"] = lax.ppermute(out["total"], "rep", [(1, 0), (2, 3)])
+        if "out" in old:
+            self.done[old["out"][0]] = (old["out"][1], out["z_got"])
+        slot = {}
+        if both:
+            got = lax.ppermute(out["total"], "rep", [(0, 1), (1, 0), (2, 3), (3, 2)])
+            slot = {"in": new, "in_got": got, "out": (old["mid"][0], out["total"]), "out_got": got}
+        else:
             if new:
-                o["in"] = new
-            if inner:
-                o["out"] = (inner[0], out["total"])
-            self.outer = o
-        self.inner = None
-        if outer and outer["in"]:
-            self.inner = (outer["in"][0], out["sum"], lax.ppermute(out["sum"], "rep", [(1, 2), (2, 1)]))
+                slot["in"] = new
+                slot["in_got"] = lax.ppermute(out["new"], "rep", [(0, 1), (3, 2)])
+            if "mid" in old:
+                slot["out"] = (old["mid"][0], out["total"])
+                slot["out_got"] = lax.ppermute(out["total"], "rep", [(1, 0), (2, 3)])
+        if "in" in old:
+            slot["mid"] = (old["in"][0], out["a_sum"])
+            slot["mid_got"] = lax.ppermute(out["a_sum"], "rep", [(1, 2), (2, 1)])
+        if slot:
+            self.flight.append(slot)
+
+
+def cast_kernel(w_ref, out_ref):
+    out_ref[...] = w_ref[...].astype(bf16)
+
+
+def cast(w):
+    rows, width = w.shape
+    unit = max(n for n in (128, 256, 512, 1024, 1408, 2048, 2816) if width % n == 0)
+    spec = pl.BlockSpec((rows, unit), lambda i: (0, i))
+    return pl.pallas_call(
+        cast_kernel,
+        grid=(width // unit,),
+        in_specs=[spec],
+        out_specs=spec,
+        out_shape=jax.ShapeDtypeStruct(w.shape, bf16),
+        compiler_params=pltpu.CompilerParams(vmem_limit_bytes=48 * 1024 * 1024),
+        cost_estimate=SMALL,
+    )(w)
 
 
 def split_kernel(core_ref, w_ref, mine_ref, theirs_ref):
@@ -301,36 +320,8 @@
     )(bit, kept, got, kept, got)
 
 
-def token_rows_kernel(core_ref, a_ref, b_ref, c_ref, d_ref, out_ref):
-    mine = core_ref[0] == pl.program_id(2)
-    half = out_ref.shape[0] // 2
-    out_ref[:half] = jnp.where(mine, a_ref[0, 0], c_ref[0, 0])
-    out_ref[half:] = jnp.where(mine, b_ref[0, 0], d_ref[0, 0])
-
-
-def token_rows(mine, theirs, core):
-    y_size, s_size, rows, width = mine[0].shape
-    part = pl.BlockSpec((1, 1, rows, width), lambda s, y, c, core: (y, s, 0, 0))
-    return pl.pallas_call(
-        token_rows_kernel,
-        grid_spec=pltpu.PrefetchScalarGridSpec(
-            num_scalar_prefetch=1,
-            grid=(s_size, y_size, 2),
-            in_specs=[part] * 4,
-            out_specs=pl.BlockSpec((2 * rows, width), lambda s, y, c, core: ((s * y_size + y) * 2 + c, 0)),
-        ),
-        out_shape=jax.ShapeDtypeStruct((s_size * y_size * 4 * rows, width), bf16),
-        compiler_params=pltpu.CompilerParams(vmem_limit_bytes=32 * 1024 * 1024),
-        cost_estimate=SMALL,
-    )(core, *mine, *theirs)
-
-
-def adam_kernel(rate, two, core_ref, w_ref, m_ref, v_ref, *refs):
-    grad = refs[0][...].astype(f32)
-    if two:
-        other = refs[1][...].astype(f32)
-        mine = core_ref[0] == 0
-        grad = jnp.concatenate([jnp.where(mine, grad, other), jnp.where(mine, other, grad)], axis=1)
+def adam_kernel(rate, end_ref, w_ref, m_ref, v_ref, total_ref, got_ref, *refs):
+    grad = jnp.where(end_ref[0] == 1, got_ref[...], total_ref[...]).astype(f32)
     new_m_ref, new_v_ref, new_w_ref = refs[-3:]
     new_m, new_v, new_w = adam_update(w_ref[...], m_ref[...], v_ref[...], grad, rate, weight_decay)
     new_m_ref[...] = new_m
@@ -338,31 +329,29 @@
     new_w_ref[...] = new_w
 
 
-def adam_part(state, grads, core, rate, prev, row_block, col_first, unit):
+def adam_part(state, grads, end, rate, prev, row_block, lead, unit):
     w, m, v = state
-    two = len(grads) == 2
-    rb = grads[0].shape[0]
-    count = grads[0].shape[1] // unit
-    whole = pl.BlockSpec((rb, unit * len(grads)), lambda g, core: (row_block, col_first + g))
-    half = pl.BlockSpec((rb, unit), lambda g, core: (0, g))
+    rb, width = grads[0].shape
+    whole = pl.BlockSpec((rb, unit), lambda g, end: (row_block, lead + g))
+    part = pl.BlockSpec((rb, unit), lambda g, end: (0, g))
     out = jax.ShapeDtypeStruct(w.shape, f32)
     extra, aliases = [], {}
     if prev is not None:
         extra = list(prev)
-        aliases = {4 + len(grads) + i: i for i in range(3)}
+        aliases = {6 + i: i for i in range(3)}
     return pl.pallas_call(
-        functools.partial(adam_kernel, rate, two),
+        functools.partial(adam_kernel, rate),
         grid_spec=pltpu.PrefetchScalarGridSpec(
             num_scalar_prefetch=1,
-            grid=(count,),
-            in_specs=[whole] * 3 + [half] * len(grads) + [pl.BlockSpec(memory_space=pl.ANY)] * len(extra),
+            grid=(width // unit,),
+            in_specs=[whole] * 3 + [part] * 2 + [pl.BlockSpec(memory_space=pl.ANY)] * len(extra),
             out_specs=[whole] * 3,
         ),
         out_shape=[out] * 3,
         input_output_aliases=aliases,
         compiler_params=pltpu.CompilerParams(vmem_limit_bytes=48 * 1024 * 1024),
         cost_estimate=SMALL,
-    )(core, w, m, v, *grads, *extra)
+    )(end, w, m, v, *grads, *extra)
 
 
 def attend_kernel(kept_ref, got_ref, bias_ref, table_ref, qkv_ref, out_ref, stat_ref):
@@ -530,6 +519,7 @@
         return jnp.concatenate([blocks, jnp.broadcast_to(extra[None], (nb, 16, rows))], axis=1)
 
     packed = do(pack, x_rows, order)
+    cot_all = lax.all_gather(cotangent.reshape(rows, width), ("shard", "ctx"), axis=0, tiled=True)
     got = lax.all_to_all(packed, plane, split_axis=0, concat_axis=0, tiled=True)
 
     def chip_rows(w, lead, unit, count):
@@ -564,6 +554,7 @@
         return ((x - mean) * inv * cols[:, 0:1] + cols[:, 1:2]).astype(bf16)
 
     xn1 = do(first_norm, x_own, x_other, mean1, inv1, pair_cols)
+    xn1_own = xn1[:blk]
 
     def send_products(cut, xs):
         got, kept = [], []
@@ -606,36 +597,6 @@
     wg_cut = cut_weights(wg_parts, 1, ffb, False)
     wu_cut = cut_weights(wu_parts, 1, ffb, True)
 
-    def gather_steps(parts, row_axis):
-        n = len(at.steps(False))
-        state = {"parts": list(parts)}
-
-        def start(i):
-            state["got"] = []
-            state["at"] = []
-            for k in range(2):
-                axis, step = list(reversed(at.steps(bool(k))))[i]
-                state["at"].append((axis, step))
-                state["got"].append(at.along(state["parts"][k], axis, step))
-
-        def finish():
-            def put(parts, got):
-                out = []
-                for k in range(2):
-                    axis, step = state["at"][k]
-                    ax = {"y": 0, "s": 1}[axis]
-                    low = (at.index(axis) // step) % 2 == 0
-                    a, b = parts[k], got[k]
-                    out.append(jnp.concatenate([jnp.where(low, a, b), jnp.where(low, b, a)], ax))
-                return out
-
-            state["parts"] = do(put, state["parts"], state["got"])
-
-        def result():
-            return jnp.concatenate(state["parts"], axis=row_axis)
-
-        return n, start, finish, state if row_axis is None else result
-
     qkvs, attns, attn_got, stats = [], [], [], []
     for k in range(2):
         shape = (3, heads, HEAD_DIM, H)
@@ -647,10 +608,6 @@
 
     pairs = [do(join, attns[k], attn_got[k]) for k in range(2)]
     flying = scatter_rest(send_products(wo_cut, pairs))
-    cot = cotangent.reshape(2, rows // 2, width)
-    cot_pair, _ = lax.optimization_barrier((cot, flying[1][0]))
-    cot_n, cot_start, cot_finish, cot_state = gather_steps([cot_pair[k][None, None] for k in range(2)], None)
-
     def residual(x, a0, b0, a1, b1):
         a, b = lanes(a0, a1), lanes(b0, b1)
         hidden = x.astype(f32) + (a.astype(f32) + b.astype(f32))
@@ -659,7 +616,6 @@
         return hidden, join(local_mean, jnp.sum(dev * dev, axis=0, keepdims=True))
 
     hidden, moments = do(residual, x_own, *flying[0], *flying[1])
-    cot_start(0)
     count = blk
     for axis, step in at.steps(False) + [("core", 1)]:
         other = at.core(moments) if axis == "core" else at.along(moments, axis, step)
@@ -681,42 +637,24 @@
 
     flying = send_products([wg_cut, wu_cut], [xn2, xn2])
 
-    for i in range(1, cot_n):
-        cot_finish()
-        cot_start(i)
-    wo_own = do(lambda w: w.astype(bf16), w_out)
-    wd_own = do(lambda w: w.astype(bf16), w_down)
-    wq = do(lanes, *wq_parts)
-
-    wg = do(lanes, *wg_parts)
-    wu = do(lanes, *wu_parts)
-
-    def gain_products(wg, wu, cols):
-        g, b = cols[:, 2], cols[:, 3]
+    wu_nat = do(cast, w_up)
+
+    def gain_products(w, cols):
         terms = []
-        for v in (g, b):
+        for v in (cols[:, 2], cols[:, 3]):
             t = lax.reduce_precision(v, 8, 7)
             terms += [t, v - t]
-        terms = jnp.stack(terms).astype(bf16)
-        out = []
-        for w in (wg, wu):
-            p = dot(w, terms, LAST)
-            out.append(jnp.stack([p[:, 0] + p[:, 1], p[:, 2] + p[:, 3]]).reshape(2, Y, S, ffb))
-        return jnp.concatenate(out, axis=0)
-
-    gains = do(gain_products, wg, wu, pair_cols)
-    for axis, step in at.steps(False):
-        ax = {"y": 1, "s": 2}[axis]
-        bit = (at.index(axis) // step) % 2
-        send = lax.dynamic_slice_in_dim(gains, (1 - bit) * step, step, ax)
-        kept = lax.dynamic_slice_in_dim(gains, bit * step, step, ax)
-        gains = do(lambda a, b: a + b, kept, at.along(send, axis, step))
-    gains = do(lambda g: g.reshape(4, ffb, 1), gains)
-    cot_finish()
-    cot_theirs = [at.core(p) for p in cot_state["parts"]]
-    cot_all = do(lambda a, b: token_rows(a, b, core), cot_state["parts"], cot_theirs)
+        p = dot(jnp.stack(terms).astype(bf16), w, PLAIN)
+        p = jnp.stack([p[0] + p[1], p[2] + p[3]])
+        return p.reshape(2, 2, nb, ffb).transpose(2, 1, 0, 3).reshape(nb, 4, ffb)
+
+    gains = do(gain_products, wu_nat, own_cols)
+    gains = lax.psum_scatter(gains, plane, scatter_dimension=0, tiled=True).reshape(4, ffb, 1)
+    wd_own = do(cast, w_down)
     grad_act = do(lambda w, c: dot(w, c, LAST), wd_own, cot_all)
     cot_cols = do(lambda c: lax.dynamic_slice_in_dim(c, my_block * blk, blk, 1).T, cot_all)
+    wo_own = do(cast, w_out)
+    wq_nat = do(cast, w_qkv)
     flying = scatter_rest(flying)
 
     def gated(ga, gb, ua, ub, grad_act, gains):
@@ -737,17 +675,12 @@
         n = parts_of(count, want)
         return [(k * (count // n), count // n) for k in range(n)]
 
-    down_rows, up_rows, out_rows = even(ffb, 4), even(blk, 2), even(blk, 2)
-    qkv_rows = [(0, blk // 2), (blk // 2, blk // 4), (3 * blk // 4, blk // 4)]
-
-    def push_rows(name, g, rows):
+    down_rows, up_rows, out_rows = even(ffb, 4), even(blk, 4), even(blk, 2)
+    thirds = {2: even(blk, 2), 1: even(blk, 2), 0: even(blk, 4)}
+
+    def push(name, g, rows):
         for k, (at_row, count) in enumerate(rows):
-            reps.push((name, "all", k), g[at_row : at_row + count])
-
-    def push_pairs(name, g, rows):
-        for k, (at_row, count) in enumerate(rows):
-            reps.push((name, "theirs", k), g[blk + at_row : blk + at_row + count])
-            reps.push((name, "mine", k), g[at_row : at_row + count])
+            reps.push((name, k), g[at_row : at_row + count])
 
     results = {"down": None, "out": None, "up": None, "qkv": None}
     states = {
@@ -758,44 +691,38 @@
     }
     rates = {"down": 0.02, "out": 0.2, "up": 0.03, "qkv": 0.03}
     jobs = []
-    for k, (at_row, count) in enumerate(down_rows):
-        jobs.append(("down", [("down", "all", k)], at_row // count, 0, min(512, width)))
-    for part_name, lead in (("gate", 0), ("up", Y)):
-        for k, (at_row, count) in enumerate(up_rows):
-            jobs.append(
-                ("up", [(part_name, "mine", k), (part_name, "theirs", k)], at_row // count, lead, S * ffb)
-            )
-    for k, (at_row, count) in enumerate(out_rows):
-        jobs.append(("out", [("out", "all", k)], at_row // count, 0, min(512, width)))
-    for k, (at_row, count) in enumerate(qkv_rows):
-        jobs.append(("qkv", [("qkv", "mine", k), ("qkv", "theirs", k)], at_row // count, 0, S * blk))
-    received = {}
+    wide = FF // 4
+    for name, state, lead, unit, cuts in (
+        [("down", "down", 0, 1024, down_rows), ("gate", "up", 0, wide, up_rows), ("up", "up", FF // wide, wide, up_rows)]
+        + [("out", "out", 0, 1024, out_rows)]
+        + [(third, "qkv", third * width // 1024, 1024, thirds[third]) for third in (2, 1, 0)]
+    ):
+        for k, (at_row, count) in enumerate(cuts):
+            jobs.append((state, (name, k), at_row // count, lead, unit))
+    end = reps.end.astype(jnp.int32).reshape(1)
 
     def update(limit):
-        for name in list(reps.done):
-            if name[1] == "theirs" and name not in received:
-                received[name] = at.core(reps.done[name])
-        while jobs and limit:
-            name, needs, row_block, lead, unit = jobs[0]
-            if not all(k in reps.done for k in needs):
-                return
-            grads = [received[k] if k[1] == "theirs" else reps.done[k] for k in needs]
+        while jobs and limit and jobs[0][1] in reps.done:
+            name, key, row_block, lead, unit = jobs.pop(0)
             results[name] = do(
-                lambda s, g, prev: adam_part(s, g, core, rates[name], prev, row_block, lead, unit),
+                lambda s, g, prev: adam_part(s, g, end, rates[name], prev, row_block, lead, unit),
                 states[name],
-                grads,
+                reps.done[key],
                 results[name],
             )
-            jobs.pop(0)
             limit -= 1
 
-    def quarter_heads(x):
-        return [x[:, h][None, None] for h in halves]
-
-    n, start, finish, gate_all = gather_steps(quarter_heads(ggate), 3)
-    start(0)
+    def everywhere(x):
+        return lax.all_gather(x, plane, axis=0, tiled=True)
+
+    def ticks(n):
+        for _ in range(n):
+            reps.tick()
+
+    ggate_all = everywhere(ggate)
+    gup_all = everywhere(gup)
     g_down = do(lambda a, c: dot(a, c, PLAIN).astype(bf16), act, cot_all)
-    push_rows("down", g_down, down_rows)
+    push("down", g_down, down_rows)
     reps.tick()
 
     def norm_sums2(ggate, gup, gate, up, gains):
@@ -805,126 +732,81 @@
         return join(e, ez)
 
     sums = do(norm_sums2, ggate, gup, gate, up, gains)
+    reps.tick()
     steps2 = at.steps(False) + [("core", 1)]
 
     def sum_step(sums, axis, step):
         other = at.core(sums) if axis == "core" else at.along(sums, axis, step)
         return do(lambda a, b: a + b, sums, other)
 
-    finish()
-    start(1)
-    reps.tick()
     for axis, step in steps2:
         sums = sum_step(sums, axis, step)
     reps.tick()
-    for i in range(2, n):
-        finish()
-        start(i)
-    n, start_up, finish_up, up_all = gather_steps(quarter_heads(gup), 3)
-    finish()
-    start_up(0)
-    reps.tick()
-    ggate_all = do(lambda x: x.reshape(Y * S * ffb, T), gate_all())
-    part_gate = do(lambda w, g: dot(w, g, FIRST), wg, ggate_all)
-    g_gate = do(lambda x, g: dot(x, g, LAST).astype(bf16), xn2, ggate_all)
-    push_pairs("gate", g_gate, up_rows)
-    finish_up()
-    for i in range(1, n):
-        start_up(i)
-        reps.tick()
-        if i == 1:
-            out_part = do(lambda w, a: dot(w, a, FIRST).astype(bf16), wd_own, act).reshape(Y, 2, S * blk, T)
-            out_theirs = at.core(pick(out_part, 1, 1 - at.c))
-            reps.tick()
-        finish_up()
-    gup_all = do(lambda x: x.reshape(Y * S * ffb, T), up_all())
-    part = do(lambda w, g, p: dot(w, g, FIRST) + p, wu, gup_all, part_gate)
-    part_theirs = at.core(part[blk:])
-    reps.tick()
-
-    def branch(a, b, cot, z, scale, gain, sums):
-        gxn2 = a + b
+    out_part = do(lambda w, a: dot(w, a, FIRST).astype(bf16), wd_own, act)
+    ticks(2)
+    part_gate = do(lambda w, g: dot(w, g, PLAIN), wu_nat[:, :FF], ggate_all)
+    g_gate = do(lambda x, g: dot(x, g, LAST).astype(bf16), xn2_own, ggate_all)
+    push("gate", g_gate, up_rows)
+    ticks(4)
+    update(1)
+    reps.tick()
+    gxn2 = do(lambda w, g, p: dot(w, g, PLAIN) + p, wu_nat[:, FF:], gup_all, part_gate)
+
+    def branch(gxn2, cot, z, scale, gain, sums):
         e = gxn2 * gain
         grad_hidden = cot.astype(f32) + scale * (e - sums[0:1] / width - z * (sums[1:2] / width))
-        return grad_hidden.astype(bf16), grad_hidden, gxn2
-
-    grad_branch, grad_hidden, gxn2 = do(
-        branch, part[:blk], part_theirs, cot_cols, z2, inv2, own_cols[:, 2:3], sums
-    )
-    n, start, finish, branch_all = gather_steps(quarter_heads(grad_branch), 3)
-    start(0)
-    g_up = do(lambda x, g: dot(x, g, LAST).astype(bf16), xn2, gup_all)
-    push_pairs("up", g_up, up_rows)
-    finish()
-    for i in range(1, n):
-        start(i)
-        if i == 1:
-            reps.tick()
-        finish()
-    gbr_c = do(lambda x: x, branch_all())
-    gbr_o = at.core(gbr_c)
-    gbr = do(lambda a, b: in_order(a, b, 1).reshape(width, T), gbr_c, gbr_o)
+        return grad_hidden.astype(bf16), grad_hidden
+
+    grad_branch, grad_hidden = do(branch, gxn2, cot_cols, z2, inv2, own_cols[:, 2:3], sums)
+    gbr = everywhere(grad_branch)
+    g_up = do(lambda x, g: dot(x, g, LAST).astype(bf16), xn2_own, gup_all)
+    push("up", g_up, up_rows)
+    reps.tick()
+    update(2)
+    reps.tick()
+    update(1)
     grad_attn = do(lambda w, g: dot(w, g, PLAIN).astype(bf16), wo_own, gbr)
-    reps.tick()
 
     gqkvs = []
     for k in range(2):
         dout = grad_attn[:, halves[k]].reshape(heads, HEAD_DIM, H)
-        gqkvs.append(do(attend_back, qkvs[k], dout, stats[k], table[seqs[k]]).reshape(3, blk, H))
+        gqkvs.append(do(attend_back, qkvs[k], dout, stats[k], table[seqs[k]]))
         if k == 0:
             reps.tick()
-    n, start, finish, gqkv_done = gather_steps([g.reshape(1, 1, 3 * blk, H) for g in gqkvs], 3)
-    start(0)
+    gqkv_own = do(lambda a, b: [lanes(a[i].reshape(blk, H), b[i].reshape(blk, H)) for i in range(3)], *gqkvs)
+    gathered = {third: everywhere(gqkv_own[third]) for third in (2, 1, 0)}
+    out_sum = lax.psum_scatter(out_part, plane, scatter_dimension=0, tiled=True)
     attn = lanes(*attns)
     g_out = do(lambda a, g: dot(a, g, LAST).astype(bf16), attn, gbr)
-    push_rows("out", g_out, out_rows)
-    reps.tick()
-    update(2)
-    finish()
-    for i in range(1, n):
-        start(i)
-        if i == 1:
-            reps.tick()
-            update(2)
-            reps.tick()
-            update(1)
-        finish()
-
-    def qkv_columns(x):
-        return x.reshape(Y, S, 3, blk, T).transpose(2, 0, 1, 3, 4).reshape(3 * Y * S * blk, T)
-
-    gqkv = do(qkv_columns, gqkv_done())
-    reps.tick()
-    g_qkv = do(lambda x, g: dot(x, g, LAST).astype(bf16), xn1, gqkv)
-    push_pairs("qkv", g_qkv, qkv_rows)
-    part = do(lambda w, g: dot(w, g, FIRST), wq, gqkv)
-    part_theirs = at.core(part[blk:])
-    update(1)
-    reps.tick()
-
-    def first_back(a, b, x, mean, inv, gain, gxn2, z2, gqkv0, gqkv1):
-        gxn1 = a + b
+    push("out", g_out, out_rows)
+    gxn1 = None
+    for third in (2, 1, 0):
+        reps.tick()
+        update(1)
+        reps.tick()
+        g_all = gathered[third]
+        w_third = wq_nat[:, third * width : (third + 1) * width]
+        if gxn1 is None:
+            gxn1 = do(lambda w, g: dot(w, g, PLAIN), w_third, g_all)
+        else:
+            gxn1 = do(lambda w, g, p: dot(w, g, PLAIN) + p, w_third, g_all, gxn1)
+        g = do(lambda x, g: dot(x, g, LAST).astype(bf16), xn1_own, g_all)
+        push(third, g, thirds[third])
+    reps.tick()
+
+    def first_back(gxn1, x, mean, inv, gain, gxn2, z2, parts):
         z1 = (x.astype(f32) - mean) * inv
         e = gxn1 * gain
         sums = join(jnp.sum(e, axis=0, keepdims=True), jnp.sum(e * z1, axis=0, keepdims=True))
-        small = jnp.concatenate(
-            [
-                jnp.sum(gxn1 * z1, axis=1)[None],
-                jnp.sum(gxn1, axis=1)[None],
-                jnp.sum(gxn2 * z2, axis=1)[None],
-                jnp.sum(gxn2, axis=1)[None],
-                jnp.sum(gqkv0.astype(f32), axis=2) + jnp.sum(gqkv1.astype(f32), axis=2),
-            ],
-            axis=0,
-        )
-        return sums, small, gxn1, z1
-
-    sums, small, gxn1, z1 = do(
-        first_back, part[:blk], part_theirs, x_own, mean1, inv1, own_cols[:, 0:1], gxn2, z2, *gqkvs
-    )
+        small = [gxn1 * z1, gxn1, gxn2 * z2, gxn2] + [p.astype(f32) for p in parts]
+        small = jnp.stack([jnp.sum(p, axis=1) for p in small])
+        return sums, small, z1
+
+    sums, small, z1 = do(first_back, gxn1, x_own, mean1, inv1, own_cols[:, 0:1], gxn2, z2, gqkv_own)
     for axis, step in steps2:
         sums = sum_step(sums, axis, step)
     reps.tick()
+    update(1)
     input_grad = do(
         lambda h, grad, z, scale, gain, sums: h
         + scale * (grad * gain - sums[0:1] / width - z * (sums[1:2] / width)),
@@ -935,28 +817,16 @@
         own_cols[:, 0:1],
         sums,
     )
+    out_cols = do(lambda h, a: (h + a.astype(f32)).astype(bf16), hidden, out_sum)
+    reps.tick()
+    update(1)
 
     def to_rows(cols):
         split = do(lambda c: c.reshape(blk, S, at.ctx_size, rows).transpose(2, 1, 0, 3).reshape(nb, blk, rows), cols)
         got = lax.all_to_all(split, plane, split_axis=0, concat_axis=0, tiled=True)
         return do(lambda g: g.reshape(width, rows).T, got)
 
-    update(1)
     input_rows = to_rows(input_grad)
-    reps.tick()
-    update(1)
-
-    kept, got = pick(out_part, 1, at.c).reshape(-1, T), out_theirs.reshape(-1, T)
-    for k, (axis, step) in enumerate(at.steps(True)):
-        bit = (at.index(axis) // step) % 2
-        send, kept = do(lambda a, b: add_split(a, b, bit.reshape(1)), kept, got)
-        got = at.along(send, axis, step)
-        if k < 2:
-            reps.tick()
-            update(1)
-    out_cols = do(
-        lambda h, a, b: (h + (a.astype(f32) + b.astype(f32))).astype(bf16), hidden, kept, got
-    )
     reps.tick()
     update(1)
     block_output = to_rows(out_cols)
@@ -976,7 +846,7 @@
 
     while reps.busy():
         reps.tick()
-        update(2)
+        update(1)
     update(len(jobs))
     return (
         (block_output.reshape(tokens.shape), input_rows.reshape(tokens.shape))

time: 906 us -> 898 us (level)
  waiting for transfers between devices: 325 us -> 204 us
  matrix products: 64.5 us -> 115 us
  other arithmetic: 76.4 us -> 94.2 us
  Pallas kernels: 141 us -> 155 us
  between operations: 4.03 us -> 16.6 us
  starting transfers between devices: 190 us -> 200 us
    ppermute x21 -> x9, waiting for transfers between devices: 65.3 us -> 7.45 us  [along(): lax.ppermute(x, 'ctx', [(i, i ^ 2 * step) for i in range(self.ctx_size)])]
    ppermute x50 -> x61, waiting for transfers between devices: 121 us -> 65.3 us  [the longest x17 29.5 us: tick(): slot['in_got'] = lax.ppermute(out['new'], 'rep', [(0, 1), (3, 2)])]
    unnamed x0 -> x10, waiting for transfers between devices: none -> 51.3 us
    dot_general x25 -> x28, matrix products: 64.5 us -> 115 us  [dot(): return lax.dot_general(a, b, dims, preferred_element_type=f32)]
    ppermute x21 -> x9, waiting for transfers between devices: 110 us -> 62.8 us  [along(): return lax.ppermute(x, 'shard', [(i, i ^ step) for i in range(self.s_size)])]
    convert_element_type x30 -> x39, other arithmetic: 19.5 us -> 48.6 us  [add(): lax.reduce_precision(a.astype(f32) + b.astype(f32), 8, 7).astype(bf16)]
    ppermute x50 -> x61, starting transfers between devices: 127 us -> 155 us  [the longest x17 92.5 us: tick(): slot['in_got'] = lax.ppermute(out['new'], 'rep', [(0, 1), (3, 2)])]
    pallas_call x14 -> x26, Pallas kernels: 83.2 us -> 102 us  [the longest x22 90.2 us: adam_part(): pl.pallas_call(functools.partial(adam_kernel, rate), grid_spec=pltpu.Pref...]
  transfers between devices with their start and end apart: 122 -> 105, of which waited for: 52 -> 38; matrix products, arithmetic and copies ran while one was open for 19% -> 28% of each run, Pallas kernels for 14% -> 14%
where the time goes in v5:
time: 898 us; the launch traced here: 884 us
  waiting for transfers between devices  204 us (23%)
  starting transfers between devices  200 us (22%)
  Pallas kernels  155 us (17%)
  matrix products  115 us (13%)
  local copies, waits for them, and re-layouts  99.3 us (11%)
  other arithmetic  94.2 us (10%)
  between operations  16.6 us (2%)
    dot_general x28, matrix products, dot(): return lax.dot_general(a, b, dims, preferred_element_type=f32)  115 us
    ppermute x17, starting transfers between devices, tick(): slot['in_got'] = lax.ppermute(out['new'], 'rep', [(0, 1), (3, 2)])  92.5 us
    pallas_call x22, Pallas kernels, adam_part(): pl.pallas_call(functools.partial(adam_kernel, rate), grid_spec=pltpu.Pref...  90.2 us
    ppermute x9, waiting for transfers between devices, along(): return lax.ppermute(x, 'shard', [(i, i ^ step) for i in range(self.s_size)])  62.8 us
    unnamed x10, waiting for transfers between devices  51.3 us
    convert_element_type x39, other arithmetic, add(): lax.reduce_precision(a.astype(f32) + b.astype(f32), 8, 7).astype(bf16)  48.6 us
    unnamed x335, local copies, waits for them, and re-layouts  46.2 us
    ppermute x17, waiting for transfers between devices, tick(): slot['in_got'] = lax.ppermute(out['new'], 'rep', [(0, 1), (3, 2)])  29.5 us
  transfers between devices with their start and end apart: 105, of which 38 were waited for; matrix products, arithmetic and copies ran while one was open for 28% of the time, Pallas kernels for 14%

profile of v5, /device:TPU:0, one launch (start us, length us, event | category | flops | bytes accessed | tf_op | source)
XLA Modules:
  0.0 884.3 jit_solution(2006708715453493458)
XLA Ops:
  19.4 4.8 all-to-all-start
  65.8 11.8 %collective-permute-done.3.b_ref.d_ref = bf16[1536,512]{1,0:T(8,128)(2,1)} collective-permute-done((bf16[1536,512]{1,0:T(8,128)(2,1)}, bf16[1536,512]{1,0:T(8,128)(2,1)}, u32[]{:S(2)}, u32[]{:S(2)}) %collective-permute-start.3) | collective-permute-done | bytes 1572896 | tf_op jit(solution)/shard_map/ppermute | solution.py:62
  125.8 16.3 %collective-permute-done.11.b_ref.d_ref = bf16[512,512]{1,0:T(8,128)(2,1)S(1)} collective-permute-done((bf16[512,512]{1,0:T(8,128)(2,1)S(1)}, bf16[512,512]{1,0:T(8,128)(2,1)S(1)}, u32[]{:S(2)}, u32[]{:S(2)}) %collective-permute-start.11) | collective-permute-done | bytes 524320 | tf_op jit(solution)/shard_map/ppermute | solution.py:62
  145.8 7.3 collective-permute-done.14
  186.2 5.2 shard_map.321
  199.5 7.8 fusion.59
  215.8 22.0 %collective-permute-done.19.b_ref.d_ref = bf16[1408,1024]{1,0:T(8,128)(2,1)} collective-permute-done((bf16[1408,1024]{1,0:T(8,128)(2,1)}, bf16[1408,1024]{1,0:T(8,128)(2,1)}, u32[]{:S(2)}, u32[]{:S(2)}) %collective-permute-start.19) | collective-permute-done | bytes 2883616 | tf_op jit(solution)/shard_map/ppermute | solution.py:62
  252.0 50.6 %all-reduce.3.cloned.1.call-done = f32[8,4,704]{2,1,0:T(4,128)} async-done(((f32[8,4,704]{2,1,0:T(4,128)}), f32[8,4,704]{2,1,0:T(4,128)}) %all-reduce.3.cloned.1.call-update) | async-done | bytes 90128
  304.6 6.9 multiply_convert_fusion
  312.9 5.7 convolution_convert_fusion.7
  334.2 5.7 fusion.40
  343.2 7.7 collective-permute-done.23
  352.7 7.0 collective-permute-start.27
  359.7 5.0 convolution_convert_fusion.2
  369.4 7.2 collective-permute-start.30
  376.6 5.2 collective-permute-done.27
  388.7 10.6 %fusion.60 = f32[256,1024]{1,0:T(8,128)} fusion(bf16[256,5632]{1,0:T(8,128)(2,1)} %get-tuple-element.773, bf16[5632,1024]{1,0:T(8,128)(2,1)} %all-gather.11.cloned.1.call-done), kind=kOutput, calls=%fused_computation.229 | convolution fusion | flops 2952790016 | bytes 15466496 | tf_op jit(solution)/shard_map/dot_general | solution.py:31
  399.3 12.3 %convolution_convert_fusion.1 = bf16[256,5632]{1,0:T(8,128)(2,1)S(1)} fusion(bf16[256,1024]{1,0:T(8,128)(2,1)S(1)} %copy-done.134, bf16[5632,1024]{1,0:T(8,128)(2,1)} %all-gather.11.cloned.1.call-done), kind=kOutput, calls=%fused_computation.1 | convolution fusion | flops 2954231808 | bytes 14942208 | tf_op jit(solution)/shard_map/dot_general | solution.py:31
  417.7 8.3 collective-permute-start.32
  430.2 4.6 collective-permute-start.40
  434.9 6.1 collective-permute-done.33.got_ref
  443.1 7.2 collective-permute-done.41.got_ref
  453.1 4.6 collective-permute-start.37
  475.7 8.6 convolution_add_fusion.2
  485.9 12.5 %convolution_convert_fusion = bf16[256,5632]{1,0:T(8,128)(2,1)S(1)} fusion(bf16[256,1024]{1,0:T(8,128)(2,1)S(1)} %copy-done.135, bf16[5632,1024]{1,0:T(8,128)(2,1)} %all-gather.9.cloned.1.call-done), kind=kOutput, calls=%fused_computation | convolution fusion | flops 2954231808 | bytes 14942208 | tf_op jit(solution)/shard_map/dot_general | solution.py:31
  536.1 5.5 shard_map.331
  543.8 5.5 shard_map.332
  577.1 6.4 collective-permute-start.54
  583.5 5.0 shard_map.333
  595.0 8.6 collective-permute-start.51
  603.6 4.9 fusion.61
  616.5 5.4 shard_map.334
  628.8 5.3 collective-permute-start.59
  635.6 5.7 convolution_add_fusion.1
  644.1 4.8 collective-permute-start.56
  652.4 5.1 shard_map.335
  662.4 5.2 all-gather.15.cloned.1.call-done
  674.6 4.8 collective-permute-start.62
  681.8 8.7 collective-permute-done.62
  703.8 4.9 collective-permute-start.70
  715.9 5.1 shard_map.336
  732.7 8.9 %collective-permute-start.75 = (bf16[64,2048]{1,0:T(8,128)(2,1)}, bf16[64,2048]{1,0:T(8,128)(2,1)}, u32[]{:S(2)}, u32[]{:S(2)}) collective-permute-start(bf16[64,2048]{1,0:T(8,128)(2,1)} %get-tuple-element.1035), channel_id=1, source_target_pairs={{0,8},{24,16},{1,9},{25,17},{2,10},{26,18},{3,11},{27,19},{4,12},{... | collective-permute-start | bytes 786440 | tf_op jit(solution)/shard_map/ppermute | solution.py:196
  741.6 5.1 shard_map.337
  776.5 5.2 shard_map.338
  781.7 5.0 shard_map.339
  800.7 8.3 collective-permute-start.81
  825.6 5.3 shard_map.340
  842.4 5.4 collective-permute-done.86.got_ref
  (739 shorter events, 482.6 us)
Async XLA Ops:
  24.2 175.3 %all-gather.21.cloned.1.call-start = ((), (), s32[]{:S(2)}) async-start(), calls=%async_computation.12 | async-start | bytes 4718592 | tf_op jit(solution)/shard_map/all_gather | solution.py:522
  40.7 36.8 %collective-permute-start.3 = (bf16[1536,512]{1,0:T(8,128)(2,1)}, bf16[1536,512]{1,0:T(8,128)(2,1)}, u32[]{:S(2)}, u32[]{:S(2)}) collective-permute-start(bf16[1536,512]{1,0:T(8,128)(2,1)} %convolution_convert_fusion.11), channel_id=1, source_target_pairs={{0,1},{1,0},{2,3},{3,2},{4,5},{5,4},{6,7},{7,6},{8,9},{9,8},{10,11... | collective-permute-start | bytes 4718600 | tf_op jit(solution)/shard_map/ppermute | solution.py:62
  43.9 40.1 %collective-permute-start.7 = (bf16[1536,512]{1,0:T(8,128)(2,1)}, bf16[1536,512]{1,0:T(8,128)(2,1)}, u32[]{:S(2)}, u32[]{:S(2)}) collective-permute-start(bf16[1536,512]{1,0:T(8,128)(2,1)} %convolution_convert_fusion.10), channel_id=1, source_target_pairs={{0,4},{2,6},{4,0},{6,2},{1,5},{3,7},{5,1},{7,3},{8,12},{10,14},{12... | collective-permute-start | bytes 4718600 | tf_op jit(solution)/shard_map/ppermute | solution.py:61
  59.8 32.6 %collective-permute-start.6 = (bf16[2816,256]{1,0:T(8,128)(2,1)}, bf16[2816,256]{1,0:T(8,128)(2,1)}, u32[]{:S(2)}, u32[]{:S(2)}) collective-permute-start(bf16[2816,256]{1,0:T(8,128)(2,1)} %get-tuple-element.657), channel_id=1, source_target_pairs={{0,2},{2,0},{4,6},{6,4},{1,3},{3,1},{5,7},{7,5},{8,10},{10,8},{12,... | collective-permute-start | bytes 4325384 | tf_op jit(solution)/shard_map/ppermute | solution.py:57
  60.3 35.2 %collective-permute-start.5 = (bf16[2816,256]{1,0:T(8,128)(2,1)}, bf16[2816,256]{1,0:T(8,128)(2,1)}, u32[]{:S(2)}, u32[]{:S(2)}) collective-permute-start(bf16[2816,256]{1,0:T(8,128)(2,1)} %get-tuple-element.656), channel_id=1, source_target_pairs={{0,2},{2,0},{4,6},{6,4},{1,3},{3,1},{5,7},{7,5},{8,10},{10,8},{12,... | collective-permute-start | bytes 4325384 | tf_op jit(solution)/shard_map/ppermute | solution.py:57
  119.7 182.9 %all-reduce.3.cloned.1.call-start = ((), (), s32[]{:S(2)}) async-start(), calls=%async_computation.13 | async-start | bytes 196608
  173.0 64.9 %collective-permute-start.19 = (bf16[1408,1024]{1,0:T(8,128)(2,1)}, bf16[1408,1024]{1,0:T(8,128)(2,1)}, u32[]{:S(2)}, u32[]{:S(2)}) collective-permute-start(bf16[1408,1024]{1,0:T(8,128)(2,1)} %convolution_convert_fusion.6), channel_id=1, source_target_pairs={{0,1},{1,0},{2,3},{3,2},{4,5},{5,4},{6,7},{7,6},{8,9},{9,8},{10,11... | collective-permute-start | bytes 8650760 | tf_op jit(solution)/shard_map/ppermute | solution.py:62
  176.3 65.4 %collective-permute-start.21 = (bf16[1408,1024]{1,0:T(8,128)(2,1)}, bf16[1408,1024]{1,0:T(8,128)(2,1)}, u32[]{:S(2)}, u32[]{:S(2)}) collective-permute-start(bf16[1408,1024]{1,0:T(8,128)(2,1)} %convolution_convert_fusion.5), channel_id=1, source_target_pairs={{0,4},{2,6},{4,0},{6,2},{1,5},{3,7},{5,1},{7,3},{8,12},{10,14},{12... | collective-permute-start | bytes 8650760 | tf_op jit(solution)/shard_map/ppermute | solution.py:61
  246.9 57.7 %collective-permute-start.22 = (bf16[704,1024]{1,0:T(8,128)(2,1)}, bf16[704,1024]{1,0:T(8,128)(2,1)}, u32[]{:S(2)}, u32[]{:S(2)}) collective-permute-start(bf16[704,1024]{1,0:T(8,128)(2,1)} %get-tuple-element.743), channel_id=1, source_target_pairs={{0,1},{1,0},{2,3},{3,2},{4,5},{5,4},{6,7},{7,6},{8,9},{9,8},{10,11... | collective-permute-start | bytes 4325384 | tf_op jit(solution)/shard_map/ppermute | solution.py:62
  248.3 56.3 %collective-permute-start.20 = (bf16[704,1024]{1,0:T(8,128)(2,1)}, bf16[704,1024]{1,0:T(8,128)(2,1)}, u32[]{:S(2)}, u32[]{:S(2)}) collective-permute-start(bf16[704,1024]{1,0:T(8,128)(2,1)} %get-tuple-element.739), channel_id=1, source_target_pairs={{0,4},{2,6},{4,0},{6,2},{1,5},{3,7},{5,1},{7,3},{8,12},{10,14},{12... | collective-permute-start | bytes 4325384 | tf_op jit(solution)/shard_map/ppermute | solution.py:61
  250.7 137.9 %all-gather.11.cloned.1.call-start = ((), (), s32[]{:S(2)}) async-start(), calls=%async_computation.7 | async-start | bytes 12976128 | tf_op jit(solution)/shard_map/all_gather | solution.py:716
  311.5 164.1 %all-gather.9.cloned.1.call-start = ((), (), s32[]{:S(2)}) async-start(), calls=%async_computation.6 | async-start | bytes 12976128 | tf_op jit(solution)/shard_map/all_gather | solution.py:716
  312.1 220.1 %all-gather.13.cloned.1.call-start = ((), (), s32[]{:S(2)}) async-start(), calls=%async_computation.8 | async-start | bytes 4718592 | tf_op jit(solution)/shard_map/all_gather | solution.py:716
  340.0 26.3 %collective-permute-start.29 = (bf16[176,2048]{1,0:T(8,128)(2,1)S(1)}, bf16[176,2048]{1,0:T(8,128)(2,1)}, u32[]{:S(2)}, u32[]{:S(2)}) collective-permute-start(bf16[176,2048]{1,0:T(8,128)(2,1)S(1)} %copy-done.126), channel_id=1, source_target_pairs={{0,8},{24,16},{1,9},{25,17},{2,10},{26,18},{3,11},{27,19},{4,12},{... | collective-permute-start | bytes 2162696 | tf_op jit(solution)/shard_map/ppermute | solution.py:196
  352.7 29.1 %collective-permute-start.27 = (bf16[176,2048]{1,0:T(8,128)(2,1)}, bf16[176,2048]{1,0:T(8,128)(2,1)}, u32[]{:S(2)}, u32[]{:S(2)}) collective-permute-start(bf16[176,2048]{1,0:T(8,128)(2,1)} %get-tuple-element.771), channel_id=1, source_target_pairs={{0,8},{24,16},{1,9},{25,17},{2,10},{26,18},{3,11},{27,19},{4,12},{... | collective-permute-start | bytes 2162696 | tf_op jit(solution)/shard_map/ppermute | solution.py:196
  367.9 44.9 %collective-permute-start.31 = (bf16[176,2048]{1,0:T(8,128)(2,1)S(1)}, bf16[176,2048]{1,0:T(8,128)(2,1)}, u32[]{:S(2)}, u32[]{:S(2)}) collective-permute-start(bf16[176,2048]{1,0:T(8,128)(2,1)S(1)} %reduce-precision_convert_fusion.22), channel_id=1, source_target_pairs={{8,16},{16,8},{9,17},{17,9},{10,18},{18,10},{11,19},{19,11},{12,20... | collective-permute-start | bytes 2162696 | tf_op jit(solution)/shard_map/ppermute | solution.py:202
  369.4 43.3 %collective-permute-start.30 = (bf16[176,2048]{1,0:T(8,128)(2,1)}, bf16[176,2048]{1,0:T(8,128)(2,1)}, u32[]{:S(2)}, u32[]{:S(2)}) collective-permute-start(bf16[176,2048]{1,0:T(8,128)(2,1)} %get-tuple-element.781), channel_id=1, source_target_pairs={{0,8},{24,16},{1,9},{25,17},{2,10},{26,18},{3,11},{27,19},{4,12},{... | collective-permute-start | bytes 2162696 | tf_op jit(solution)/shard_map/ppermute | solution.py:196
  383.4 43.9 %collective-permute-start.35 = (bf16[176,2048]{1,0:T(8,128)(2,1)S(1)}, bf16[176,2048]{1,0:T(8,128)(2,1)}, u32[]{:S(2)}, u32[]{:S(2)}) collective-permute-start(bf16[176,2048]{1,0:T(8,128)(2,1)S(1)} %reduce-precision_convert_fusion.18.total_ref), channel_id=1, source_target_pairs={{8,0},{16,24},{9,1},{17,25},{10,2},{18,26},{11,3},{19,27},{12,4},{... | collective-permute-start | bytes 2162696 | tf_op jit(solution)/shard_map/ppermute | solution.py:199
  387.1 40.2 %collective-permute-start.36 = (bf16[176,2048]{1,0:T(8,128)(2,1)}, bf16[176,2048]{1,0:T(8,128)(2,1)}, u32[]{:S(2)}, u32[]{:S(2)}) collective-permute-start(bf16[176,2048]{1,0:T(8,128)(2,1)} %reduce-precision_convert_fusion.21), channel_id=1, source_target_pairs={{8,16},{16,8},{9,17},{17,9},{10,18},{18,10},{11,19},{19,11},{12,20... | collective-permute-start | bytes 2162696 | tf_op jit(solution)/shard_map/ppermute | solution.py:202
  458.7 41.0 %collective-permute-start.43 = (bf16[64,5632]{1,0:T(8,128)(2,1)}, bf16[64,5632]{1,0:T(8,128)(2,1)}, u32[]{:S(2)}, u32[]{:S(2)}) collective-permute-start(bf16[64,5632]{1,0:T(8,128)(2,1)} %reduce-precision_convert_fusion.14), channel_id=1, source_target_pairs={{8,16},{16,8},{9,17},{17,9},{10,18},{18,10},{11,19},{19,11},{12,20... | collective-permute-start | bytes 2162696 | tf_op jit(solution)/shard_map/ppermute | solution.py:202
  460.3 39.5 %collective-permute-start.42 = (bf16[64,5632]{1,0:T(8,128)(2,1)}, bf16[64,5632]{1,0:T(8,128)(2,1)}, u32[]{:S(2)}, u32[]{:S(2)}) collective-permute-start(bf16[64,5632]{1,0:T(8,128)(2,1)} %get-tuple-element.821), channel_id=1, source_target_pairs={{0,8},{24,16},{1,9},{25,17},{2,10},{26,18},{3,11},{27,19},{4,12},{... | collective-permute-start | bytes 2162696 | tf_op jit(solution)/shard_map/ppermute | solution.py:196
  474.1 51.2 %collective-permute-start.45 = (bf16[64,5632]{1,0:T(8,128)(2,1)}, bf16[64,5632]{1,0:T(8,128)(2,1)}, u32[]{:S(2)}, u32[]{:S(2)}) collective-permute-start(bf16[64,5632]{1,0:T(8,128)(2,1)} %reduce-precision_convert_fusion.13), channel_id=1, source_target_pairs={{8,16},{16,8},{9,17},{17,9},{10,18},{18,10},{11,19},{19,11},{12,20... | collective-permute-start | bytes 2162696 | tf_op jit(solution)/shard_map/ppermute | solution.py:202
  485.8 117.8 %all-gather.19.cloned.1.call-start = ((), (), s32[]{:S(2)}) async-start(), calls=%async_computation.11 | async-start | bytes 4718592 | tf_op jit(solution)/shard_map/all_gather | solution.py:716
  502.8 38.8 %collective-permute-start.46 = (bf16[64,5632]{1,0:T(8,128)(2,1)}, bf16[64,5632]{1,0:T(8,128)(2,1)}, u32[]{:S(2)}, u32[]{:S(2)}) collective-permute-start(bf16[64,5632]{1,0:T(8,128)(2,1)} %fusion.8.total_ref), channel_id=1, source_target_pairs={{0,8},{8,0},{16,24},{24,16},{1,9},{9,1},{17,25},{25,17},{2,10},{10... | collective-permute-start | bytes 2162696 | tf_op jit(solution)/shard_map/ppermute | solution.py:191
  511.3 30.3 %collective-permute-start.47 = (bf16[64,5632]{1,0:T(8,128)(2,1)}, bf16[64,5632]{1,0:T(8,128)(2,1)}, u32[]{:S(2)}, u32[]{:S(2)}) collective-permute-start(bf16[64,5632]{1,0:T(8,128)(2,1)} %reduce-precision_convert_fusion.12), channel_id=1, source_target_pairs={{8,16},{16,8},{9,17},{17,9},{10,18},{18,10},{11,19},{19,11},{12,20... | collective-permute-start | bytes 2162696 | tf_op jit(solution)/shard_map/ppermute | solution.py:202
  551.8 77.0 %all-gather.17.cloned.1.call-start = ((), (), s32[]{:S(2)}) async-start(), calls=%async_computation.10 | async-start | bytes 4718592 | tf_op jit(solution)/shard_map/all_gather | solution.py:716
  553.8 113.8 %all-gather.15.cloned.1.call-start = ((), (), s32[]{:S(2)}) async-start(), calls=%async_computation.9 | async-start | bytes 4718592 | tf_op jit(solution)/shard_map/all_gather | solution.py:716
  555.7 167.7 %reduce-scatter.2.cloned.1.call-start = ((), (), s32[]{:S(2)}) async-start(), calls=%async_computation.5 | async-start | bytes 4718592 | tf_op jit(solution)/shard_map/reduce_scatter | solution.py:778
  563.2 27.8 %collective-permute-start.49 = (bf16[64,5632]{1,0:T(8,128)(2,1)}, bf16[64,5632]{1,0:T(8,128)(2,1)S(1)}, u32[]{:S(2)}, u32[]{:S(2)}) collective-permute-start(bf16[64,5632]{1,0:T(8,128)(2,1)} %reduce-precision_convert_fusion.8), channel_id=1, source_target_pairs={{8,16},{16,8},{9,17},{17,9},{10,18},{18,10},{11,19},{19,11},{12,20... | collective-permute-start | bytes 2162696 | tf_op jit(solution)/shard_map/ppermute | solution.py:202
  575.4 34.4 %collective-permute-start.55 = (bf16[64,5632]{1,0:T(8,128)(2,1)}, bf16[64,5632]{1,0:T(8,128)(2,1)}, u32[]{:S(2)}, u32[]{:S(2)}) collective-permute-start(bf16[64,5632]{1,0:T(8,128)(2,1)} %reduce-precision_convert_fusion.6), channel_id=1, source_target_pairs={{8,16},{16,8},{9,17},{17,9},{10,18},{18,10},{11,19},{19,11},{12,20... | collective-permute-start | bytes 2162696 | tf_op jit(solution)/shard_map/ppermute | solution.py:202
  577.1 32.7 %collective-permute-start.54 = (bf16[64,5632]{1,0:T(8,128)(2,1)}, bf16[64,5632]{1,0:T(8,128)(2,1)}, u32[]{:S(2)}, u32[]{:S(2)}) collective-permute-start(bf16[64,5632]{1,0:T(8,128)(2,1)} %get-tuple-element.905), channel_id=1, source_target_pairs={{0,8},{24,16},{1,9},{25,17},{2,10},{26,18},{3,11},{27,19},{4,12},{... | collective-permute-start | bytes 2162696 | tf_op jit(solution)/shard_map/ppermute | solution.py:196
  591.2 31.8 %collective-permute-start.52 = (bf16[64,5632]{1,0:T(8,128)(2,1)S(1)}, bf16[64,5632]{1,0:T(8,128)(2,1)}, u32[]{:S(2)}, u32[]{:S(2)}) collective-permute-start(bf16[64,5632]{1,0:T(8,128)(2,1)S(1)} %reduce-precision_convert_fusion.4.total_ref), channel_id=1, source_target_pairs={{8,0},{16,24},{9,1},{17,25},{10,2},{18,26},{11,3},{19,27},{12,4},{... | collective-permute-start | bytes 2162696 | tf_op jit(solution)/shard_map/ppermute | solution.py:199
  593.5 29.5 %collective-permute-start.53 = (bf16[64,5632]{1,0:T(8,128)(2,1)}, bf16[64,5632]{1,0:T(8,128)(2,1)}, u32[]{:S(2)}, u32[]{:S(2)}) collective-permute-start(bf16[64,5632]{1,0:T(8,128)(2,1)} %reduce-precision_convert_fusion.5), channel_id=1, source_target_pairs={{8,16},{16,8},{9,17},{17,9},{10,18},{18,10},{11,19},{19,11},{12,20... | collective-permute-start | bytes 2162696 | tf_op jit(solution)/shard_map/ppermute | solution.py:202
  595.0 28.0 %collective-permute-start.51 = (bf16[128,2048]{1,0:T(8,128)(2,1)}, bf16[128,2048]{1,0:T(8,128)(2,1)}, u32[]{:S(2)}, u32[]{:S(2)}) collective-permute-start(bf16[128,2048]{1,0:T(8,128)(2,1)} %get-tuple-element.916), channel_id=1, source_target_pairs={{0,8},{24,16},{1,9},{25,17},{2,10},{26,18},{3,11},{27,19},{4,12},{... | collective-permute-start | bytes 1572872 | tf_op jit(solution)/shard_map/ppermute | solution.py:196
  611.3 38.7 %collective-permute-start.60 = (bf16[64,5632]{1,0:T(8,128)(2,1)S(1)}, bf16[64,5632]{1,0:T(8,128)(2,1)}, u32[]{:S(2)}, u32[]{:S(2)}) collective-permute-start(bf16[64,5632]{1,0:T(8,128)(2,1)S(1)} %reduce-precision_convert_fusion.1.total_ref), channel_id=1, source_target_pairs={{8,0},{16,24},{9,1},{17,25},{10,2},{18,26},{11,3},{19,27},{12,4},{... | collective-permute-start | bytes 2162696 | tf_op jit(solution)/shard_map/ppermute | solution.py:199
  615.0 35.0 %collective-permute-start.61 = (bf16[64,5632]{1,0:T(8,128)(2,1)}, bf16[64,5632]{1,0:T(8,128)(2,1)}, u32[]{:S(2)}, u32[]{:S(2)}) collective-permute-start(bf16[64,5632]{1,0:T(8,128)(2,1)} %reduce-precision_convert_fusion.3), channel_id=1, source_target_pairs={{8,16},{16,8},{9,17},{17,9},{10,18},{18,10},{11,19},{19,11},{12,20... | collective-permute-start | bytes 2162696 | tf_op jit(solution)/shard_map/ppermute | solution.py:202
  624.3 33.1 %collective-permute-start.58 = (bf16[128,2048]{1,0:T(8,128)(2,1)S(1)}, bf16[128,2048]{1,0:T(8,128)(2,1)}, u32[]{:S(2)}, u32[]{:S(2)}) collective-permute-start(bf16[128,2048]{1,0:T(8,128)(2,1)S(1)} %reduce-precision_convert_fusion.35), channel_id=1, source_target_pairs={{8,16},{16,8},{9,17},{17,9},{10,18},{18,10},{11,19},{19,11},{12,20... | collective-permute-start | bytes 1572872 | tf_op jit(solution)/shard_map/ppermute | solution.py:202
  650.9 30.9 %collective-permute-start.64 = (bf16[128,2048]{1,0:T(8,128)(2,1)}, bf16[128,2048]{1,0:T(8,128)(2,1)}, u32[]{:S(2)}, u32[]{:S(2)}) collective-permute-start(bf16[128,2048]{1,0:T(8,128)(2,1)} %reduce-precision_convert_fusion.34), channel_id=1, source_target_pairs={{8,16},{16,8},{9,17},{17,9},{10,18},{18,10},{11,19},{19,11},{12,20... | collective-permute-start | bytes 1572872 | tf_op jit(solution)/shard_map/ppermute | solution.py:202
  660.9 52.5 %collective-permute-start.69 = (bf16[128,2048]{1,0:T(8,128)(2,1)}, bf16[128,2048]{1,0:T(8,128)(2,1)}, u32[]{:S(2)}, u32[]{:S(2)}) collective-permute-start(bf16[128,2048]{1,0:T(8,128)(2,1)} %reduce-precision_convert_fusion.33), channel_id=1, source_target_pairs={{8,16},{16,8},{9,17},{17,9},{10,18},{18,10},{11,19},{19,11},{12,20... | collective-permute-start | bytes 1572872 | tf_op jit(solution)/shard_map/ppermute | solution.py:202
  699.4 26.4 %collective-permute-start.71 = (bf16[128,2048]{1,0:T(8,128)(2,1)}, bf16[128,2048]{1,0:T(8,128)(2,1)}, u32[]{:S(2)}, u32[]{:S(2)}) collective-permute-start(bf16[128,2048]{1,0:T(8,128)(2,1)} %reduce-precision_convert_fusion.32), channel_id=1, source_target_pairs={{8,16},{16,8},{9,17},{17,9},{10,18},{18,10},{11,19},{19,11},{12,20... | collective-permute-start | bytes 1572872 | tf_op jit(solution)/shard_map/ppermute | solution.py:202
  714.4 60.3 %collective-permute-start.74 = (bf16[128,2048]{1,0:T(8,128)(2,1)}, bf16[128,2048]{1,0:T(8,128)(2,1)}, u32[]{:S(2)}, u32[]{:S(2)}) collective-permute-start(bf16[128,2048]{1,0:T(8,128)(2,1)} %reduce-precision_convert_fusion.30), channel_id=1, source_target_pairs={{8,16},{16,8},{9,17},{17,9},{10,18},{18,10},{11,19},{19,11},{12,20... | collective-permute-start | bytes 1572872 | tf_op jit(solution)/shard_map/ppermute | solution.py:202
  728.0 37.6 %collective-permute-start.76 = (bf16[128,2048]{1,0:T(8,128)(2,1)}, bf16[128,2048]{1,0:T(8,128)(2,1)}, u32[]{:S(2)}, u32[]{:S(2)}) collective-permute-start(bf16[128,2048]{1,0:T(8,128)(2,1)} %reduce-precision_convert_fusion.26.total_ref), channel_id=1, source_target_pairs={{8,0},{16,24},{9,1},{17,25},{10,2},{18,26},{11,3},{19,27},{12,4},{... | collective-permute-start | bytes 1572872 | tf_op jit(solution)/shard_map/ppermute | solution.py:199
  731.3 36.9 %collective-permute-start.77 = (bf16[128,2048]{1,0:T(8,128)(2,1)}, bf16[128,2048]{1,0:T(8,128)(2,1)}, u32[]{:S(2)}, u32[]{:S(2)}) collective-permute-start(bf16[128,2048]{1,0:T(8,128)(2,1)} %reduce-precision_convert_fusion.28), channel_id=1, source_target_pairs={{8,16},{16,8},{9,17},{17,9},{10,18},{18,10},{11,19},{19,11},{12,20... | collective-permute-start | bytes 1572872 | tf_op jit(solution)/shard_map/ppermute | solution.py:202
  732.7 29.3 %collective-permute-start.75 = (bf16[64,2048]{1,0:T(8,128)(2,1)}, bf16[64,2048]{1,0:T(8,128)(2,1)}, u32[]{:S(2)}, u32[]{:S(2)}) collective-permute-start(bf16[64,2048]{1,0:T(8,128)(2,1)} %get-tuple-element.1035), channel_id=1, source_target_pairs={{0,8},{24,16},{1,9},{25,17},{2,10},{26,18},{3,11},{27,19},{4,12},{... | collective-permute-start | bytes 786440 | tf_op jit(solution)/shard_map/ppermute | solution.py:196
  770.0 60.8 %collective-permute-start.80 = (bf16[64,2048]{1,0:T(8,128)(2,1)}, bf16[64,2048]{1,0:T(8,128)(2,1)}, u32[]{:S(2)}, u32[]{:S(2)}) collective-permute-start(bf16[64,2048]{1,0:T(8,128)(2,1)} %reduce-precision_convert_fusion.42), channel_id=1, source_target_pairs={{8,16},{16,8},{9,17},{17,9},{10,18},{18,10},{11,19},{19,11},{12,20... | collective-permute-start | bytes 786440 | tf_op jit(solution)/shard_map/ppermute | solution.py:202
  789.0 31.2 %collective-permute-start.82 = (bf16[128,2048]{1,0:T(8,128)(2,1)S(1)}, bf16[128,2048]{1,0:T(8,128)(2,1)}, u32[]{:S(2)}, u32[]{:S(2)}) collective-permute-start(bf16[128,2048]{1,0:T(8,128)(2,1)S(1)} %reduce-precision_convert_fusion.24.total_ref), channel_id=1, source_target_pairs={{8,0},{16,24},{9,1},{17,25},{10,2},{18,26},{11,3},{19,27},{12,4},{... | collective-permute-start | bytes 1572872 | tf_op jit(solution)/shard_map/ppermute | solution.py:199
  798.1 32.8 %collective-permute-start.79 = (bf16[128,2048]{1,0:T(8,128)(2,1)}, bf16[128,2048]{1,0:T(8,128)(2,1)}, u32[]{:S(2)}, u32[]{:S(2)}) collective-permute-start(bf16[128,2048]{1,0:T(8,128)(2,1)} %reduce-precision_convert_fusion.25.total_ref), channel_id=1, source_target_pairs={{8,0},{16,24},{9,1},{17,25},{10,2},{18,26},{11,3},{19,27},{12,4},{... | collective-permute-start | bytes 1572872 | tf_op jit(solution)/shard_map/ppermute | solution.py:199
  813.2 37.7 %all-to-all-start.2 = ((bf16[8,256,128]{2,1,0:T(8,128)(2,1)}), bf16[8,256,128]{2,1,0:T(8,128)(2,1)}, u32[]{:S(2)}, u32[]{:S(2)}) async-start(bf16[8,256,128]{2,1,0:T(8,128)(2,1)} %bitcast.192), calls=%async_computation.3 | async-start | bytes 1048576 | tf_op jit(solution)/shard_map/all_to_all | solution.py:826
  (222 other events, 2132.1 us)
Sparse Core Ops, SparseCore 0:
  119.8 45.4 all-gather.20
  250.9 51.7 all-reduce.2
  311.7 68.6 all-gather.10
  382.8 67.6 all-gather.8
  486.0 38.7 all-gather.12
  551.9 38.0 all-gather.18
  592.1 36.7 all-gather.16
  630.8 36.7 all-gather.14
  671.9 51.4 reduce-scatter.1

commit v6 on v4

--- a/solution.py
+++ b/solution.py
@@ -140,68 +140,87 @@
         z = lax.axis_index("rep")
         self.end = (z == 0) | (z == lax.axis_size("rep") - 1)
         self.queue = []
-        self.outer = None
-        self.inner = None
+        self.flight = []
         self.done = {}
 
     def push(self, name, g):
         self.queue.append((name, g))
 
     def busy(self):
-        return bool(self.queue or self.outer or self.inner)
+        return bool(self.queue or self.flight)
 
     def tick(self):
-        outer, inner = self.outer, self.inner
+        old = {}
+        if len(self.flight) == 2 or (self.flight and not self.queue):
+            old = self.flight.pop(0)
         new = self.queue.pop(0) if self.queue else None
         values = {}
-        if outer and outer["in"]:
-            values["g"], values["g_got"] = outer["in"][1], outer["in_got"]
-        if outer and outer["out"]:
-            values["t"], values["t_got"] = outer["out"][1], outer["out_got"]
-        if inner:
-            values["s"], values["s_got"] = inner[1], inner[2]
+        if "in" in old:
+            values["g"], values["g_got"] = old["in"][1], old["in_got"]
+        if "mid" in old:
+            values["s"], values["s_got"] = old["mid"][1], old["mid_got"]
         if new:
             values["new"] = new[1]
-        both = new and inner and new[1].shape == inner[1].shape
+        both = new and "mid" in old and new[1].shape == old["mid"][1].shape
+        if "out" in old:
+            values["out_got"] = old["out_got"]
 
         def stage(v):
             def add(a, b):
                 return lax.reduce_precision(a.astype(f32) + b.astype(f32), 8, 7).astype(bf16)
 
             out = {}
+            if "g" in v:
+                out["a_sum"] = add(v["g"], v["g_got"])
             if "s" in v:
-                out["total"] = add(v["s"], v["s_got"])
-            if "g" in v:
-                out["sum"] = add(v["g"], v["g_got"])
-            if "t" in v:
-                out["out"] = jnp.where(self.end, v["t_got"], v["t"])
-            if both:
-                out["send"] = jnp.where(self.end, v["new"], out["total"])
-            elif "new" in v:
+                total = add(v["s"], v["s_got"])
+                out["total"] = jnp.where(self.end, v["new"], total) if both else total
+            if "new" in v and not both:
                 out["new"] = v["new"]
+            if "out_got" in v:
+                out["z_got"] = v["out_got"]
             return out
 
+        if not values:
+            return
         out = self.order(stage, values)
-        if outer and outer["out"]:
-            self.done[outer["out"][0]] = out["out"]
-        self.outer = None
-        if new or inner:
-            o = {"in": None, "out": None}
-            if both:
-                o["in_got"] = o["out_got"] = lax.ppermute(out["send"], "rep", [(0, 1), (1, 0), (2, 3), (3, 2)])
-            else:
-                if new:
-                    o["in_got"] = lax.ppermute(out["new"], "rep", [(0, 1), (3, 2)])
-                if inner:
-                    o["out_got"] = lax.ppermute(out["total"], "rep", [(1, 0), (2, 3)])
+        if "out" in old:
+            self.done[old["out"][0]] = jnp.where(self.end, out["z_got"], old["out"][1])
+        slot = {}
+        if both:
+            got = lax.ppermute(out["total"], "rep", [(0, 1), (1, 0), (2, 3), (3, 2)])
+            slot = {"in": new, "in_got": got, "out": (old["mid"][0], out["total"]), "out_got": got}
+        else:
             if new:
-                o["in"] = new
-            if inner:
-                o["out"] = (inner[0], out["total"])
-            self.outer = o
-        self.inner = None
-        if outer and outer["in"]:
-            self.inner = (outer["in"][0], out["sum"], lax.ppermute(out["sum"], "rep", [(1, 2), (2, 1)]))
+                slot["in"] = new
+                slot["in_got"] = lax.ppermute(out["new"], "rep", [(0, 1), (3, 2)])
+            if "mid" in old:
+                slot["out"] = (old["mid"][0], out["total"])
+                slot["out_got"] = lax.ppermute(out["total"], "rep", [(1, 0), (2, 3)])
+        if "in" in old:
+            slot["mid"] = (old["in"][0], out["a_sum"])
+            slot["mid_got"] = lax.ppermute(out["a_sum"], "rep", [(1, 2), (2, 1)])
+        if slot:
+            self.flight.append(slot)
+
+
+def cast_kernel(w_ref, out_ref):
+    out_ref[...] = w_ref[...].astype(bf16)
+
+
+def cast(w):
+    rows, width = w.shape
+    unit = max(n for n in (128, 256, 512, 1024, 1408, 2048, 2816) if width % n == 0)
+    spec = pl.BlockSpec((rows, unit), lambda i: (0, i))
+    return pl.pallas_call(
+        cast_kernel,
+        grid=(width // unit,),
+        in_specs=[spec],
+        out_specs=spec,
+        out_shape=jax.ShapeDtypeStruct(w.shape, bf16),
+        compiler_params=pltpu.CompilerParams(vmem_limit_bytes=48 * 1024 * 1024),
+        cost_estimate=SMALL,
+    )(w)
 
 
 def split_kernel(core_ref, w_ref, mine_ref, theirs_ref):
@@ -271,6 +290,25 @@
         compiler_params=pltpu.CompilerParams(vmem_limit_bytes=32 * 1024 * 1024),
         cost_estimate=SMALL,
     )(place, mine, got, mine, got)
+
+
+def lanes_kernel(a_ref, b_ref, out_ref):
+    out_ref[...] = jnp.concatenate([a_ref[...], b_ref[...]], axis=1)
+
+
+def side_by_side(a, b):
+    rows, width = a.shape
+    n = max(n for n in (1, 2, 4, 8) if rows % (16 * n) == 0)
+    spec = pl.BlockSpec((rows // n, width), lambda i: (i, 0))
+    return pl.pallas_call(
+        lanes_kernel,
+        grid=(n,),
+        in_specs=[spec, spec],
+        out_specs=pl.BlockSpec((rows // n, 2 * width), lambda i: (i, 0)),
+        out_shape=jax.ShapeDtypeStruct((rows, 2 * width), bf16),
+        compiler_params=pltpu.CompilerParams(vmem_limit_bytes=48 * 1024 * 1024),
+        cost_estimate=SMALL,
+    )(a, b)
 
 
 def add_split_kernel(bit_ref, a_ref, b_ref, c_ref, d_ref, send_ref, keep_ref):
@@ -301,30 +339,6 @@
     )(bit, kept, got, kept, got)
 
 
-def token_rows_kernel(core_ref, a_ref, b_ref, c_ref, d_ref, out_ref):
-    mine = core_ref[0] == pl.program_id(2)
-    half = out_ref.shape[0] // 2
-    out_ref[:half] = jnp.where(mine, a_ref[0, 0], c_ref[0, 0])
-    out_ref[half:] = jnp.where(mine, b_ref[0, 0], d_ref[0, 0])
-
-
-def token_rows(mine, theirs, core):
-    y_size, s_size, rows, width = mine[0].shape
-    part = pl.BlockSpec((1, 1, rows, width), lambda s, y, c, core: (y, s, 0, 0))
-    return pl.pallas_call(
-        token_rows_kernel,
-        grid_spec=pltpu.PrefetchScalarGridSpec(
-            num_scalar_prefetch=1,
-            grid=(s_size, y_size, 2),
-            in_specs=[part] * 4,
-            out_specs=pl.BlockSpec((2 * rows, width), lambda s, y, c, core: ((s * y_size + y) * 2 + c, 0)),
-        ),
-        out_shape=jax.ShapeDtypeStruct((s_size * y_size * 4 * rows, width), bf16),
-        compiler_params=pltpu.CompilerParams(vmem_limit_bytes=32 * 1024 * 1024),
-        cost_estimate=SMALL,
-    )(core, *mine, *theirs)
-
-
 def adam_kernel(rate, two, core_ref, w_ref, m_ref, v_ref, *refs):
     grad = refs[0][...].astype(f32)
     if two:
@@ -338,13 +352,12 @@
     new_w_ref[...] = new_w
 
 
-def adam_part(state, grads, core, rate, prev, row_block, col_first, unit):
+def adam_part(state, grads, core, rate, prev, row_first, lead, unit, rb):
     w, m, v = state
     two = len(grads) == 2
-    rb = grads[0].shape[0]
-    count = grads[0].shape[1] // unit
-    whole = pl.BlockSpec((rb, unit * len(grads)), lambda g, core: (row_block, col_first + g))
-    half = pl.BlockSpec((rb, unit), lambda g, core: (0, g))
+    rows, width = grads[0].shape
+    whole = pl.BlockSpec((rb, unit * len(grads)), lambda i, g, core: (row_first // rb + i, lead + g))
+    half = pl.BlockSpec((rb, unit), lambda i, g, core: (i, g))
     out = jax.ShapeDtypeStruct(w.shape, f32)
     extra, aliases = [], {}
     if prev is not None:
@@ -354,7 +367,7 @@
         functools.partial(adam_kernel, rate, two),
         grid_spec=pltpu.PrefetchScalarGridSpec(
             num_scalar_prefetch=1,
-            grid=(count,),
+            grid=(rows // rb, width // unit),
             in_specs=[whole] * 3 + [half] * len(grads) + [pl.BlockSpec(memory_space=pl.ANY)] * len(extra),
             out_specs=[whole] * 3,
         ),
@@ -530,6 +543,7 @@
         return jnp.concatenate([blocks, jnp.broadcast_to(extra[None], (nb, 16, rows))], axis=1)
 
     packed = do(pack, x_rows, order)
+    cot_all = lax.all_gather(cotangent.reshape(rows, width), ("shard", "ctx"), axis=0, tiled=True)
     got = lax.all_to_all(packed, plane, split_axis=0, concat_axis=0, tiled=True)
 
     def chip_rows(w, lead, unit, count):
@@ -634,7 +648,7 @@
         def result():
             return jnp.concatenate(state["parts"], axis=row_axis)
 
-        return n, start, finish, state if row_axis is None else result
+        return n, start, finish, result
 
     qkvs, attns, attn_got, stats = [], [], [], []
     for k in range(2):
@@ -647,10 +661,6 @@
 
     pairs = [do(join, attns[k], attn_got[k]) for k in range(2)]
     flying = scatter_rest(send_products(wo_cut, pairs))
-    cot = cotangent.reshape(2, rows // 2, width)
-    cot_pair, _ = lax.optimization_barrier((cot, flying[1][0]))
-    cot_n, cot_start, cot_finish, cot_state = gather_steps([cot_pair[k][None, None] for k in range(2)], None)
-
     def residual(x, a0, b0, a1, b1):
         a, b = lanes(a0, a1), lanes(b0, b1)
         hidden = x.astype(f32) + (a.astype(f32) + b.astype(f32))
@@ -659,7 +669,6 @@
         return hidden, join(local_mean, jnp.sum(dev * dev, axis=0, keepdims=True))
 
     hidden, moments = do(residual, x_own, *flying[0], *flying[1])
-    cot_start(0)
     count = blk
     for axis, step in at.steps(False) + [("core", 1)]:
         other = at.core(moments) if axis == "core" else at.along(moments, axis, step)
@@ -681,15 +690,9 @@
 
     flying = send_products([wg_cut, wu_cut], [xn2, xn2])
 
-    for i in range(1, cot_n):
-        cot_finish()
-        cot_start(i)
-    wo_own = do(lambda w: w.astype(bf16), w_out)
-    wd_own = do(lambda w: w.astype(bf16), w_down)
-    wq = do(lanes, *wq_parts)
-
-    wg = do(lanes, *wg_parts)
-    wu = do(lanes, *wu_parts)
+    wd_own = do(cast, w_down)
+    wg = do(side_by_side, *wg_parts)
+    wu = do(side_by_side, *wu_parts)
 
     def gain_products(wg, wu, cols):
         g, b = cols[:, 2], cols[:, 3]
@@ -712,11 +715,10 @@
         kept = lax.dynamic_slice_in_dim(gains, bit * step, step, ax)
         gains = do(lambda a, b: a + b, kept, at.along(send, axis, step))
     gains = do(lambda g: g.reshape(4, ffb, 1), gains)
-    cot_finish()
-    cot_theirs = [at.core(p) for p in cot_state["parts"]]
-    cot_all = do(lambda a, b: token_rows(a, b, core), cot_state["parts"], cot_theirs)
     grad_act = do(lambda w, c: dot(w, c, LAST), wd_own, cot_all)
     cot_cols = do(lambda c: lax.dynamic_slice_in_dim(c, my_block * blk, blk, 1).T, cot_all)
+    wo_own = do(cast, w_out)
+    wq = do(side_by_side, *wq_parts)
     flying = scatter_rest(flying)
 
     def gated(ga, gb, ua, ub, grad_act, gains):
@@ -737,12 +739,8 @@
         n = parts_of(count, want)
         return [(k * (count // n), count // n) for k in range(n)]
 
-    down_rows, up_rows, out_rows = even(ffb, 4), even(blk, 2), even(blk, 2)
+    out_rows = even(blk, 2)
     qkv_rows = [(0, blk // 2), (blk // 2, blk // 4), (3 * blk // 4, blk // 4)]
-
-    def push_rows(name, g, rows):
-        for k, (at_row, count) in enumerate(rows):
-            reps.push((name, "all", k), g[at_row : at_row + count])
 
     def push_pairs(name, g, rows):
         for k, (at_row, count) in enumerate(rows):
@@ -757,37 +755,40 @@
         "qkv": (w_qkv, m_qkv, v_qkv),
     }
     rates = {"down": 0.02, "out": 0.2, "up": 0.03, "qkv": 0.03}
+
+    def adam(name, grads, row_first, lead, unit, rb):
+        results[name] = do(
+            lambda s, g, prev: adam_part(s, g, core, rates[name], prev, row_first, lead, unit, rb),
+            states[name],
+            grads,
+            results[name],
+        )
+
     jobs = []
-    for k, (at_row, count) in enumerate(down_rows):
-        jobs.append(("down", [("down", "all", k)], at_row // count, 0, min(512, width)))
-    for part_name, lead in (("gate", 0), ("up", Y)):
-        for k, (at_row, count) in enumerate(up_rows):
-            jobs.append(
-                ("up", [(part_name, "mine", k), (part_name, "theirs", k)], at_row // count, lead, S * ffb)
-            )
     for k, (at_row, count) in enumerate(out_rows):
-        jobs.append(("out", [("out", "all", k)], at_row // count, 0, min(512, width)))
+        jobs.append(("out", [("out", k)], at_row, count, 1024))
     for k, (at_row, count) in enumerate(qkv_rows):
-        jobs.append(("qkv", [("qkv", "mine", k), ("qkv", "theirs", k)], at_row // count, 0, S * blk))
+        jobs.append(("qkv", [("qkv", "mine", k), ("qkv", "theirs", k)], at_row, count, S * blk))
     received = {}
 
     def update(limit):
         for name in list(reps.done):
             if name[1] == "theirs" and name not in received:
                 received[name] = at.core(reps.done[name])
-        while jobs and limit:
-            name, needs, row_block, lead, unit = jobs[0]
-            if not all(k in reps.done for k in needs):
-                return
-            grads = [received[k] if k[1] == "theirs" else reps.done[k] for k in needs]
-            results[name] = do(
-                lambda s, g, prev: adam_part(s, g, core, rates[name], prev, row_block, lead, unit),
-                states[name],
-                grads,
-                results[name],
-            )
-            jobs.pop(0)
+        while jobs and limit and all(k in reps.done for k in jobs[0][1]):
+            name, needs, at_row, count, unit = jobs.pop(0)
+            adam(name, [received[k] if k[1] == "theirs" else reps.done[k] for k in needs], at_row, 0, unit, count)
             limit -= 1
+
+    def ticks(n):
+        for _ in range(n):
+            reps.tick()
+
+    def rep_scatter(g):
+        return lax.psum_scatter(g, "rep", scatter_dimension=0, tiled=True)
+
+    def rep_gather(g):
+        return lax.all_gather(do(lambda g: g, g), "rep", axis=0, tiled=True)
 
     def quarter_heads(x):
         return [x[:, h][None, None] for h in halves]
@@ -795,8 +796,7 @@
     n, start, finish, gate_all = gather_steps(quarter_heads(ggate), 3)
     start(0)
     g_down = do(lambda a, c: dot(a, c, PLAIN).astype(bf16), act, cot_all)
-    push_rows("down", g_down, down_rows)
-    reps.tick()
+    g_down = rep_scatter(g_down)
 
     def norm_sums2(ggate, gup, gate, up, gains):
         a, b = ggate.astype(f32), gup.astype(f32)
@@ -813,34 +813,29 @@
 
     finish()
     start(1)
-    reps.tick()
     for axis, step in steps2:
         sums = sum_step(sums, axis, step)
-    reps.tick()
     for i in range(2, n):
         finish()
         start(i)
     n, start_up, finish_up, up_all = gather_steps(quarter_heads(gup), 3)
     finish()
     start_up(0)
-    reps.tick()
     ggate_all = do(lambda x: x.reshape(Y * S * ffb, T), gate_all())
-    part_gate = do(lambda w, g: dot(w, g, FIRST), wg, ggate_all)
-    g_gate = do(lambda x, g: dot(x, g, LAST).astype(bf16), xn2, ggate_all)
-    push_pairs("gate", g_gate, up_rows)
     finish_up()
     for i in range(1, n):
         start_up(i)
-        reps.tick()
         if i == 1:
+            g_gate = do(lambda x, g: dot(x, g, LAST).astype(bf16), xn2, ggate_all)
+            g_down = rep_gather(g_down)
+            g_gate = rep_scatter(do(lambda g: g, g_gate))
+            part_gate = do(lambda w, g: dot(w, g, FIRST), wg, ggate_all)
             out_part = do(lambda w, a: dot(w, a, FIRST).astype(bf16), wd_own, act).reshape(Y, 2, S * blk, T)
             out_theirs = at.core(pick(out_part, 1, 1 - at.c))
-            reps.tick()
         finish_up()
     gup_all = do(lambda x: x.reshape(Y * S * ffb, T), up_all())
     part = do(lambda w, g, p: dot(w, g, FIRST) + p, wu, gup_all, part_gate)
     part_theirs = at.core(part[blk:])
-    reps.tick()
 
     def branch(a, b, cot, z, scale, gain, sums):
         gxn2 = a + b
@@ -854,53 +849,55 @@
     n, start, finish, branch_all = gather_steps(quarter_heads(grad_branch), 3)
     start(0)
     g_up = do(lambda x, g: dot(x, g, LAST).astype(bf16), xn2, gup_all)
-    push_pairs("up", g_up, up_rows)
     finish()
     for i in range(1, n):
         start(i)
-        if i == 1:
-            reps.tick()
         finish()
     gbr_c = do(lambda x: x, branch_all())
     gbr_o = at.core(gbr_c)
     gbr = do(lambda a, b: in_order(a, b, 1).reshape(width, T), gbr_c, gbr_o)
     grad_attn = do(lambda w, g: dot(w, g, PLAIN).astype(bf16), wo_own, gbr)
-    reps.tick()
 
     gqkvs = []
     for k in range(2):
         dout = grad_attn[:, halves[k]].reshape(heads, HEAD_DIM, H)
         gqkvs.append(do(attend_back, qkvs[k], dout, stats[k], table[seqs[k]]).reshape(3, blk, H))
-        if k == 0:
-            reps.tick()
     n, start, finish, gqkv_done = gather_steps([g.reshape(1, 1, 3 * blk, H) for g in gqkvs], 3)
     start(0)
     attn = lanes(*attns)
     g_out = do(lambda a, g: dot(a, g, LAST).astype(bf16), attn, gbr)
-    push_rows("out", g_out, out_rows)
-    reps.tick()
-    update(2)
+    for k, (at_row, count) in enumerate(out_rows):
+        reps.push(("out", k), g_out[at_row : at_row + count])
+    adam("down", [g_down], 0, 0, 1024, ffb // 4 if ffb % 64 == 0 else ffb)
     finish()
     for i in range(1, n):
         start(i)
         if i == 1:
+            g_gate = rep_gather(g_gate)
+            g_up = rep_scatter(do(lambda g: g, g_up))
             reps.tick()
-            update(2)
-            reps.tick()
-            update(1)
         finish()
 
     def qkv_columns(x):
         return x.reshape(Y, S, 3, blk, T).transpose(2, 0, 1, 3, 4).reshape(3 * Y * S * blk, T)
 
     gqkv = do(qkv_columns, gqkv_done())
-    reps.tick()
     g_qkv = do(lambda x, g: dot(x, g, LAST).astype(bf16), xn1, gqkv)
     push_pairs("qkv", g_qkv, qkv_rows)
+    ticks(1)
     part = do(lambda w, g: dot(w, g, FIRST), wq, gqkv)
     part_theirs = at.core(part[blk:])
-    update(1)
-    reps.tick()
+    ticks(1)
+
+    def split_rows(g):
+        return do(lambda g: (g[:blk], g[blk:]), g)
+
+    def adam_ff(g, lead):
+        mine, theirs = split_rows(g)
+        adam("up", [mine, at.core(theirs)], 0, lead, S * ffb, min(blk, 128))
+
+    adam_ff(g_gate, 0)
+    ticks(1)
 
     def first_back(a, b, x, mean, inv, gain, gxn2, z2, gqkv0, gqkv1):
         gxn1 = a + b
@@ -924,7 +921,7 @@
     )
     for axis, step in steps2:
         sums = sum_step(sums, axis, step)
-    reps.tick()
+    ticks(1)
     input_grad = do(
         lambda h, grad, z, scale, gain, sums: h
         + scale * (grad * gain - sums[0:1] / width - z * (sums[1:2] / width)),
@@ -943,6 +940,7 @@
 
     update(1)
     input_rows = to_rows(input_grad)
+    g_up = rep_gather(g_up)
     reps.tick()
     update(1)
 
@@ -974,9 +972,11 @@
     norm_grad = got.transpose(1, 0, 2).reshape(7, width)
     mn, vn, wn = do(lambda *a: adam_update(*a, 0.3, 0.0), norm_params, m_norm, v_norm, norm_grad)
 
+    ticks(2)
+    adam_ff(g_up, Y)
     while reps.busy():
         reps.tick()
-        update(2)
+        update(1)
     update(len(jobs))
     return (
         (block_output.reshape(tokens.shape), input_rows.reshape(tokens.shape))

time: 906 us -> 903 us (level)
  starting transfers between devices: 190 us -> 125 us
  waiting for transfers between devices: 325 us -> 387 us
  between operations: 4.03 us -> 17 us
  other arithmetic: 76.4 us -> 65.1 us
  matrix products: 64.5 us -> 74 us
    ppermute x50 -> x24, starting transfers between devices: 127 us -> 62.5 us  [the longest x8 43.3 us: tick(): slot['in_got'] = lax.ppermute(out['new'], 'rep', [(0, 1), (3, 2)])]
    ppermute x21 -> x19, waiting for transfers between devices: 110 us -> 167 us  [along(): return lax.ppermute(x, 'shard', [(i, i ^ step) for i in range(self.s_size)])]
    ppermute x50 -> x24, waiting for transfers between devices: 121 us -> 103 us  [the longest x8 55.3 us: tick(): slot['in_got'] = lax.ppermute(out['new'], 'rep', [(0, 1), (3, 2)])]
    select_n x30 -> x8, other arithmetic: 14.8 us -> 2.48 us  [tick(): self.done[old['out'][0]] = jnp.where(self.end, out['z_got'], old['out'][1])]
    all_gather x0 -> x4, waiting for transfers between devices: none -> 10.7 us  [the longest x3 10.7 us: rep_gather(): return lax.all_gather(do(lambda g: g, g), 'rep', axis=0, tiled=True)]
    all_to_all x2, waiting for transfers between devices: 13.5 us -> 2.85 us  [to_rows(): got = lax.all_to_all(split, plane, split_axis=0, concat_axis=0, tiled=True)]
    reduce_scatter x0 -> x3, waiting for transfers between devices: none -> 10.5 us  [rep_scatter(): return lax.psum_scatter(g, 'rep', scatter_dimension=0, tiled=True)]
    dot_general x25, matrix products: 64.5 us -> 74 us  [dot(): return lax.dot_general(a, b, dims, preferred_element_type=f32)]
  transfers between devices with their start and end apart: 122 -> 95, of which waited for: 52 -> 49; matrix products, arithmetic and copies ran while one was open for 19% -> 18% of each run, Pallas kernels for 14% -> 14%
where the time goes in v6:
time: 903 us; the launch traced here: 891 us
  waiting for transfers between devices  387 us (43%)
  Pallas kernels  138 us (15%)
  starting transfers between devices  125 us (14%)
  local copies, waits for them, and re-layouts  85.3 us (9%)
  matrix products  74 us (8%)
  other arithmetic  65.1 us (7%)
  between operations  17 us (2%)
    ppermute x19, waiting for transfers between devices, along(): return lax.ppermute(x, 'shard', [(i, i ^ step) for i in range(self.s_size)])  167 us
    dot_general x25, matrix products, dot(): return lax.dot_general(a, b, dims, preferred_element_type=f32)  74 us
    ppermute x19, waiting for transfers between devices, along(): lax.ppermute(x, 'ctx', [(i, i ^ 2 * step) for i in range(self.ctx_size)])  72.7 us
    pallas_call x8, Pallas kernels, adam_part(): pl.pallas_call(functools.partial(adam_kernel, rate, two), grid_spec=pltpu...  70.2 us
    ppermute x8, waiting for transfers between devices, tick(): slot['in_got'] = lax.ppermute(out['new'], 'rep', [(0, 1), (3, 2)])  55.3 us
    ppermute x8, waiting for transfers between devices, tick(): slot['out_got'] = lax.ppermute(out['total'], 'rep', [(1, 0), (2, 3)])  47.6 us
    unnamed x253, local copies, waits for them, and re-layouts  45.9 us
    ppermute x8, starting transfers between devices, tick(): slot['in_got'] = lax.ppermute(out['new'], 'rep', [(0, 1), (3, 2)])  43.3 us
  transfers between devices with their start and end apart: 95, of which 49 were waited for; matrix products, arithmetic and copies ran while one was open for 18% of the time, Pallas kernels for 14%

profile of v6, /device:TPU:0, one launch (start us, length us, event | category | flops | bytes accessed | tf_op | source)
XLA Modules:
  0.0 890.7 jit_solution(13466839690526667516)
XLA Ops:
  19.4 4.8 all-to-all-start
  67.1 11.4 %collective-permute-done.3.b_ref.d_ref = bf16[1536,512]{1,0:T(8,128)(2,1)} collective-permute-done((bf16[1536,512]{1,0:T(8,128)(2,1)}, bf16[1536,512]{1,0:T(8,128)(2,1)}, u32[]{:S(2)}, u32[]{:S(2)}) %collective-permute-start.3) | collective-permute-done | bytes 1572896 | tf_op jit(solution)/shard_map/ppermute | solution.py:62
  105.5 4.5 shard_map.317
  113.7 5.1 shard_map.318
  128.5 16.6 %collective-permute-done.11.b_ref.d_ref = bf16[512,512]{1,0:T(8,128)(2,1)S(1)} collective-permute-done((bf16[512,512]{1,0:T(8,128)(2,1)S(1)}, bf16[512,512]{1,0:T(8,128)(2,1)S(1)}, u32[]{:S(2)}, u32[]{:S(2)}) %collective-permute-start.11) | collective-permute-done | bytes 524320 | tf_op jit(solution)/shard_map/ppermute | solution.py:62
  148.4 7.8 collective-permute-done.14
  205.9 36.4 %collective-permute-done.20 = f32[4,2,1,704]{3,2,1,0:T(1,128)S(1)} collective-permute-done((f32[4,2,1,704]{3,2,1,0:T(1,128)S(1)}, f32[4,2,1,704]{3,2,1,0:T(1,128)S(1)}, u32[]{:S(2)}, u32[]{:S(2)}) %collective-permute-start.20) | collective-permute-done | bytes 22560 | tf_op jit(solution)/shard_map/ppermute | solution.py:62
  246.1 7.9 fusion.45
  264.5 4.4 shard_map.327
  272.7 30.0 %collective-permute-done.24 = bf16[704,1024]{1,0:T(8,128)(2,1)} collective-permute-done((bf16[704,1024]{1,0:T(8,128)(2,1)}, bf16[704,1024]{1,0:T(8,128)(2,1)}, u32[]{:S(2)}, u32[]{:S(2)}) %collective-permute-start.24) | collective-permute-done | bytes 1441824 | tf_op jit(solution)/shard_map/ppermute | solution.py:62
  303.7 6.7 multiply_convert_fusion
  312.8 4.5 convolution_convert_fusion.8
  320.1 4.3 fusion.1
  324.4 9.2 %collective-permute-done.26 = bf16[1,1,704,512]{3,2,1,0:T(8,128)(2,1)S(1)} collective-permute-done((bf16[1,1,704,512]{3,2,1,0:T(8,128)(2,1)}, bf16[1,1,704,512]{3,2,1,0:T(8,128)(2,1)S(1)}, u32[]{:S(2)}, u32[]{:S(2)}) %collective-permute-start.26) | collective-permute-done | bytes 720928 | tf_op jit(solution)/shard_map/ppermute | solution.py:62
  338.6 27.9 %collective-permute-done.29 = f32[2,1024]{1,0:T(2,128)S(1)} collective-permute-done((f32[2,1024]{1,0:T(2,128)S(1)}, f32[2,1024]{1,0:T(2,128)S(1)}, u32[]{:S(2)}, u32[]{:S(2)}) %collective-permute-start.29) | collective-permute-done | bytes 8224 | tf_op jit(solution)/shard_map/ppermute | solution.py:62
  374.4 14.5 %collective-permute-done.33 = bf16[1,1,704,512]{3,2,1,0:T(8,128)(2,1)S(1)} collective-permute-done((bf16[1,1,704,512]{3,2,1,0:T(8,128)(2,1)S(1)}, bf16[1,1,704,512]{3,2,1,0:T(8,128)(2,1)S(1)}, u32[]{:S(2)}, u32[]{:S(2)}) %collective-permute-start.33) | collective-permute-done | bytes 720928 | tf_op jit(solution)/shard_map/ppermute | solution.py:62
  394.5 4.5 convolution_convert_fusion.2
  399.1 6.7 fusion.46
  405.9 5.0 convolution_convert_fusion.3
  410.9 15.4 %collective-permute-done.36 = bf16[1,2,704,512]{3,2,1,0:T(8,128)(2,1)} collective-permute-done((bf16[1,2,704,512]{3,2,1,0:T(8,128)(2,1)}, bf16[1,2,704,512]{3,2,1,0:T(8,128)(2,1)}, u32[]{:S(2)}, u32[]{:S(2)}) %collective-permute-start.36) | collective-permute-done | bytes 1441824 | tf_op jit(solution)/shard_map/ppermute | solution.py:61
  441.8 4.7 convolution_convert_fusion.1
  450.9 10.9 %collective-permute-done.41 = bf16[1,2,256,512]{3,2,1,0:T(8,128)(2,1)S(1)} collective-permute-done((bf16[1,2,256,512]{3,2,1,0:T(8,128)(2,1)S(1)}, bf16[1,2,256,512]{3,2,1,0:T(8,128)(2,1)S(1)}, u32[]{:S(2)}, u32[]{:S(2)}) %collective-permute-start.41) | collective-permute-done | bytes 524320 | tf_op jit(solution)/shard_map/ppermute | solution.py:61
  472.5 5.6 shard_map.328
  478.2 5.4 shard_map.329
  490.7 14.8 %shard_map.330 = (f32[704,2048]{1,0:T(8,128)}, f32[704,2048]{1,0:T(8,128)}, f32[704,2048]{1,0:T(8,128)}) custom-call(s32[1]{0:T(128)} %bitcast.8.core_ref, f32[704,2048]{1,0:T(8,128)} %w_ref.6, f32[704,2048]{1,0:T(8,128)} %m_ref, f32[704,2048]{1,0:T(8,128)} %v_ref, bf16[704,2048]{1,0:T(8,128)(2,1)S(1)} %copy-done.21), custom_call_target="tpu_custom_call" | custom-call | flops 1024 | bytes 1024 | tf_op jit(solution)/shard_map/pallas_call | solution.py:366
  506.5 10.5 %reduce-scatter.6.cloned.1.call-done = bf16[128,2816]{1,0:T(8,128)(2,1)} async-done(((bf16[512,2816]{1,0:T(8,128)(2,1)}), bf16[128,2816]{1,0:T(8,128)(2,1)}) %reduce-scatter.6.cloned.1.call-update) | async-done | bytes 720912 | tf_op jit(solution)/shard_map/reduce_scatter | solution.py:788
  526.3 29.5 %collective-permute-done.46 = bf16[1,2,768,512]{3,2,1,0:T(8,128)(2,1)} collective-permute-done((bf16[1,2,768,512]{3,2,1,0:T(8,128)(2,1)}, bf16[1,2,768,512]{3,2,1,0:T(8,128)(2,1)}, u32[]{:S(2)}, u32[]{:S(2)}) %collective-permute-start.46) | collective-permute-done | bytes 1572896 | tf_op jit(solution)/shard_map/ppermute | solution.py:61
  573.2 10.7 %all-gather.8.cloned.1.call-done = bf16[512,2816]{1,0:T(8,128)(2,1)} async-done(((bf16[128,2816]{1,0:T(8,128)(2,1)}), bf16[512,2816]{1,0:T(8,128)(2,1)}) %all-gather.8.cloned.1.call-update) | async-done | bytes 2883600 | tf_op jit(solution)/shard_map/all_gather | solution.py:791
  586.9 4.7 collective-permute-start.47
  591.6 13.7 %shard_map.331 = (f32[256,11264]{1,0:T(8,128)}, f32[256,11264]{1,0:T(8,128)}, f32[256,11264]{1,0:T(8,128)}) custom-call(s32[1]{0:T(128)} %bitcast.8.core_ref, f32[256,11264]{1,0:T(8,128)} %w_ref.11, f32[256,11264]{1,0:T(8,128)} %m_ref.5, f32[256,11264]{1,0:T(8,128)} %v_ref.5, bf16[256,2816]{1,0:T(8,128)(2,1)S(1)} %get-tuple-element.672.refs_0_, ...), custom_call_target="tpu_custom_call" | custom-call | flops 1024 | bytes 1024 | tf_op jit(solution)/shard_map/pallas_call | solution.py:366
  605.3 9.0 %collective-permute-done.47 = bf16[128,2048]{1,0:T(8,128)(2,1)S(1)} collective-permute-done((bf16[128,2048]{1,0:T(8,128)(2,1)S(1)}, bf16[128,2048]{1,0:T(8,128)(2,1)S(1)}, u32[]{:S(2)}, u32[]{:S(2)}) %collective-permute-start.47) | collective-permute-done | bytes 524320 | tf_op jit(solution)/shard_map/ppermute | solution.py:196
  616.5 4.4 collective-permute-start.56
  621.1 4.4 dynamic-slice_bitcast_fusion
  629.7 26.0 %collective-permute-done.56 = bf16[128,3072]{1,0:T(8,128)(2,1)S(1)} collective-permute-done((bf16[128,3072]{1,0:T(8,128)(2,1)}, bf16[128,3072]{1,0:T(8,128)(2,1)S(1)}, u32[]{:S(2)}, u32[]{:S(2)}) %collective-permute-start.56) | collective-permute-done | bytes 786464 | tf_op jit(solution)/shard_map/ppermute | solution.py:196
  668.6 5.2 collective-permute-start.50
  686.1 4.9 collective-permute-start.59
  697.1 8.9 %collective-permute-done.59 = bf16[64,3072]{1,0:T(8,128)(2,1)S(1)} collective-permute-done((bf16[64,3072]{1,0:T(8,128)(2,1)}, bf16[64,3072]{1,0:T(8,128)(2,1)S(1)}, u32[]{:S(2)}, u32[]{:S(2)}) %collective-permute-start.59) | collective-permute-done | bytes 393248 | tf_op jit(solution)/shard_map/ppermute | solution.py:196
  707.9 17.4 %collective-permute-done.60 = bf16[128,2048]{1,0:T(8,128)(2,1)S(1)} collective-permute-done((bf16[128,2048]{1,0:T(8,128)(2,1)}, bf16[128,2048]{1,0:T(8,128)(2,1)S(1)}, u32[]{:S(2)}, u32[]{:S(2)}) %collective-permute-start.60) | collective-permute-done | bytes 524320 | tf_op jit(solution)/shard_map/ppermute | solution.py:199
  737.9 8.1 collective-permute-done.63
  746.0 4.4 collective-permute-start.66
  750.4 10.0 %collective-permute-done.64 = bf16[128,2048]{1,0:T(8,128)(2,1)S(1)} collective-permute-done((bf16[128,2048]{1,0:T(8,128)(2,1)S(1)}, bf16[128,2048]{1,0:T(8,128)(2,1)S(1)}, u32[]{:S(2)}, u32[]{:S(2)}) %collective-permute-start.64) | collective-permute-done | bytes 524320 | tf_op jit(solution)/shard_map/ppermute | solution.py:199
  766.8 6.1 collective-permute-done.62
  773.9 12.9 %collective-permute-start.69 = (bf16[64,3072]{1,0:T(8,128)(2,1)S(1)}, bf16[64,3072]{1,0:T(8,128)(2,1)S(1)}, u32[]{:S(2)}, u32[]{:S(2)}) collective-permute-start(bf16[64,3072]{1,0:T(8,128)(2,1)S(1)} %copy-done.92), channel_id=1, source_target_pairs={{0,8},{24,16},{1,9},{25,17},{2,10},{26,18},{3,11},{27,19},{4,12},{... | collective-permute-start | bytes 1179656 | tf_op jit(solution)/shard_map/ppermute | solution.py:196
  793.0 12.6 %collective-permute-done.70 = bf16[128,3072]{1,0:T(8,128)(2,1)S(1)} collective-permute-done((bf16[128,3072]{1,0:T(8,128)(2,1)S(1)}, bf16[128,3072]{1,0:T(8,128)(2,1)S(1)}, u32[]{:S(2)}, u32[]{:S(2)}) %collective-permute-start.70) | collective-permute-done | bytes 786464 | tf_op jit(solution)/shard_map/ppermute | solution.py:199
  805.8 9.8 %shard_map.336 = (f32[256,6144]{1,0:T(8,128)}, f32[256,6144]{1,0:T(8,128)}, f32[256,6144]{1,0:T(8,128)}) custom-call(s32[1]{0:T(128)} %bitcast.8.core_ref, f32[256,6144]{1,0:T(8,128)} %w_ref.13, f32[256,6144]{1,0:T(8,128)} %m_ref.7, f32[256,6144]{1,0:T(8,128)} %v_ref.7, bf16[128,3072]{1,0:T(8,128)(2,1)S(1)} %broadcast_select_fusion.13.refs_0_, ...), custom_call_target="tpu_custom_call" | custom-call | flops 1024 | bytes 1024 | tf_op jit(solution)/shard_map/pallas_call | solution.py:366
  852.4 13.0 %shard_map.337 = (f32[256,11264]{1,0:T(8,128)}, f32[256,11264]{1,0:T(8,128)}, f32[256,11264]{1,0:T(8,128)}) custom-call(s32[1]{0:T(128)} %bitcast.8.core_ref, f32[256,11264]{1,0:T(8,128)} %w_ref.11, f32[256,11264]{1,0:T(8,128)} %m_ref.5, f32[256,11264]{1,0:T(8,128)} %v_ref.5, ...), custom_call_target="tpu_custom_call", output_to_operand_aliasing={{0}: (6, {}), {1}: (7, {}), {2}: (8, {})} | custom-call | flops 1024 | bytes 1024 | tf_op jit(solution)/shard_map/pallas_call | solution.py:366
  869.1 6.3 shard_map.338
  877.2 6.2 shard_map.339
  (634 shorter events, 366.0 us)
Async XLA Ops:
  24.2 221.9 %all-gather.12.cloned.1.call-start = ((), (), s32[]{:S(2)}) async-start(), calls=%async_computation.13 | async-start | bytes 4718592 | tf_op jit(solution)/shard_map/all_gather | solution.py:546
  41.7 36.7 %collective-permute-start.3 = (bf16[1536,512]{1,0:T(8,128)(2,1)}, bf16[1536,512]{1,0:T(8,128)(2,1)}, u32[]{:S(2)}, u32[]{:S(2)}) collective-permute-start(bf16[1536,512]{1,0:T(8,128)(2,1)} %convolution_convert_fusion.12), channel_id=1, source_target_pairs={{0,1},{1,0},{2,3},{3,2},{4,5},{5,4},{6,7},{7,6},{8,9},{9,8},{10,11... | collective-permute-start | bytes 4718600 | tf_op jit(solution)/shard_map/ppermute | solution.py:62
  44.8 40.1 %collective-permute-start.7 = (bf16[1536,512]{1,0:T(8,128)(2,1)}, bf16[1536,512]{1,0:T(8,128)(2,1)}, u32[]{:S(2)}, u32[]{:S(2)}) collective-permute-start(bf16[1536,512]{1,0:T(8,128)(2,1)} %convolution_convert_fusion.11), channel_id=1, source_target_pairs={{0,4},{2,6},{4,0},{6,2},{1,5},{3,7},{5,1},{7,3},{8,12},{10,14},{12... | collective-permute-start | bytes 4718600 | tf_op jit(solution)/shard_map/ppermute | solution.py:61
  57.4 34.9 %collective-permute-start.6 = (bf16[2816,256]{1,0:T(8,128)(2,1)}, bf16[2816,256]{1,0:T(8,128)(2,1)S(1)}, u32[]{:S(2)}, u32[]{:S(2)}) collective-permute-start(bf16[2816,256]{1,0:T(8,128)(2,1)} %get-tuple-element.467), channel_id=1, source_target_pairs={{0,2},{2,0},{4,6},{6,4},{1,3},{3,1},{5,7},{7,5},{8,10},{10,8},{12,... | collective-permute-start | bytes 4325384 | tf_op jit(solution)/shard_map/ppermute | solution.py:57
  60.1 35.2 %collective-permute-start.5 = (bf16[2816,256]{1,0:T(8,128)(2,1)}, bf16[2816,256]{1,0:T(8,128)(2,1)}, u32[]{:S(2)}, u32[]{:S(2)}) collective-permute-start(bf16[2816,256]{1,0:T(8,128)(2,1)} %get-tuple-element.466), channel_id=1, source_target_pairs={{0,2},{2,0},{4,6},{6,4},{1,3},{3,1},{5,7},{7,5},{8,10},{10,8},{12,... | collective-permute-start | bytes 4325384 | tf_op jit(solution)/shard_map/ppermute | solution.py:57
  90.7 20.2 %collective-permute-start.9 = (bf16[768,512]{1,0:T(8,128)(2,1)}, bf16[768,512]{1,0:T(8,128)(2,1)}, u32[]{:S(2)}, u32[]{:S(2)}) collective-permute-start(bf16[768,512]{1,0:T(8,128)(2,1)} %get-tuple-element.470), channel_id=1, source_target_pairs={{0,1},{1,0},{2,3},{3,2},{4,5},{5,4},{6,7},{7,6},{8,9},{9,8},{10,11... | collective-permute-start | bytes 2359304 | tf_op jit(solution)/shard_map/ppermute | solution.py:62
  122.9 276.2 %reduce-scatter.4.cloned.1.call-start = ((), (), s32[]{:S(2)}) async-start(), calls=%async_computation.7 | async-start | bytes 3604480 | tf_op jit(solution)/shard_map/reduce_scatter | solution.py:788
  125.6 19.5 %collective-permute-start.11 = (bf16[512,512]{1,0:T(8,128)(2,1)S(1)}, bf16[512,512]{1,0:T(8,128)(2,1)S(1)}, u32[]{:S(2)}, u32[]{:S(2)}) collective-permute-start(bf16[512,512]{1,0:T(8,128)(2,1)S(1)} %convolution_convert_fusion.17), channel_id=1, source_target_pairs={{0,1},{1,0},{2,3},{3,2},{4,5},{5,4},{6,7},{7,6},{8,9},{9,8},{10,11... | collective-permute-start | bytes 1572872 | tf_op jit(solution)/shard_map/ppermute | solution.py:62
  127.0 19.2 %collective-permute-start.13 = (bf16[512,512]{1,0:T(8,128)(2,1)S(1)}, bf16[512,512]{1,0:T(8,128)(2,1)S(1)}, u32[]{:S(2)}, u32[]{:S(2)}) collective-permute-start(bf16[512,512]{1,0:T(8,128)(2,1)S(1)} %convolution_convert_fusion.16), channel_id=1, source_target_pairs={{0,4},{2,6},{4,0},{6,2},{1,5},{3,7},{5,1},{7,3},{8,12},{10,14},{12... | collective-permute-start | bytes 1572872 | tf_op jit(solution)/shard_map/ppermute | solution.py:61
  177.0 83.4 %collective-permute-start.19 = (bf16[1408,1024]{1,0:T(8,128)(2,1)}, bf16[1408,1024]{1,0:T(8,128)(2,1)}, u32[]{:S(2)}, u32[]{:S(2)}) collective-permute-start(bf16[1408,1024]{1,0:T(8,128)(2,1)} %convolution_convert_fusion.7), channel_id=1, source_target_pairs={{0,1},{1,0},{2,3},{3,2},{4,5},{5,4},{6,7},{7,6},{8,9},{9,8},{10,11... | collective-permute-start | bytes 8650760 | tf_op jit(solution)/shard_map/ppermute | solution.py:62
  180.4 84.1 %collective-permute-start.23 = (bf16[1408,1024]{1,0:T(8,128)(2,1)}, bf16[1408,1024]{1,0:T(8,128)(2,1)}, u32[]{:S(2)}, u32[]{:S(2)}) collective-permute-start(bf16[1408,1024]{1,0:T(8,128)(2,1)} %convolution_convert_fusion.6), channel_id=1, source_target_pairs={{0,4},{2,6},{4,0},{6,2},{1,5},{3,7},{5,1},{7,3},{8,12},{10,14},{12... | collective-permute-start | bytes 8650760 | tf_op jit(solution)/shard_map/ppermute | solution.py:61
  203.8 38.5 %collective-permute-start.20 = (f32[4,2,1,704]{3,2,1,0:T(1,128)S(1)}, f32[4,2,1,704]{3,2,1,0:T(1,128)S(1)}, u32[]{:S(2)}, u32[]{:S(2)}) collective-permute-start(f32[4,2,1,704]{3,2,1,0:T(1,128)S(1)} %get-tuple-element.929), channel_id=1, source_target_pairs={{0,1},{1,0},{2,3},{3,2},{4,5},{5,4},{6,7},{7,6},{8,9},{9,8},{10,11... | collective-permute-start | bytes 67592 | tf_op jit(solution)/shard_map/ppermute | solution.py:62
  270.0 32.7 %collective-permute-start.24 = (bf16[704,1024]{1,0:T(8,128)(2,1)}, bf16[704,1024]{1,0:T(8,128)(2,1)}, u32[]{:S(2)}, u32[]{:S(2)}) collective-permute-start(bf16[704,1024]{1,0:T(8,128)(2,1)} %get-tuple-element.562), channel_id=1, source_target_pairs={{0,1},{1,0},{2,3},{3,2},{4,5},{5,4},{6,7},{7,6},{8,9},{9,8},{10,11... | collective-permute-start | bytes 4325384 | tf_op jit(solution)/shard_map/ppermute | solution.py:62
  271.0 32.7 %collective-permute-start.22 = (bf16[704,1024]{1,0:T(8,128)(2,1)}, bf16[704,1024]{1,0:T(8,128)(2,1)}, u32[]{:S(2)}, u32[]{:S(2)}) collective-permute-start(bf16[704,1024]{1,0:T(8,128)(2,1)} %get-tuple-element.558), channel_id=1, source_target_pairs={{0,4},{2,6},{4,0},{6,2},{1,5},{3,7},{5,1},{7,3},{8,12},{10,14},{12... | collective-permute-start | bytes 4325384 | tf_op jit(solution)/shard_map/ppermute | solution.py:61
  317.3 171.5 %all-gather.6.cloned.1.call-start = ((), (), s32[]{:S(2)}) async-start(), calls=%async_computation.8 | async-start | bytes 3604480 | tf_op jit(solution)/shard_map/all_gather | solution.py:791
  334.4 38.6 %collective-permute-start.28 = (bf16[1,2,704,512]{3,2,1,0:T(8,128)(2,1)S(1)}, bf16[1,2,704,512]{3,2,1,0:T(8,128)(2,1)S(1)}, u32[]{:S(2)}, u32[]{:S(2)}) collective-permute-start(bf16[1,2,704,512]{3,2,1,0:T(8,128)(2,1)S(1)} %pad_maximum_fusion.4), channel_id=1, source_target_pairs={{0,4},{2,6},{4,0},{6,2},{1,5},{3,7},{5,1},{7,3},{8,12},{10,14},{12... | collective-permute-start | bytes 4325384 | tf_op jit(solution)/shard_map/ppermute | solution.py:61
  336.5 36.5 %collective-permute-start.27 = (bf16[2,1,704,512]{3,2,1,0:T(8,128)(2,1)S(1)}, bf16[2,1,704,512]{3,2,1,0:T(8,128)(2,1)S(1)}, u32[]{:S(2)}, u32[]{:S(2)}) collective-permute-start(bf16[2,1,704,512]{3,2,1,0:T(8,128)(2,1)S(1)} %pad_maximum_fusion.3), channel_id=1, source_target_pairs={{0,1},{1,0},{2,3},{3,2},{4,5},{5,4},{6,7},{7,6},{8,9},{9,8},{10,11... | collective-permute-start | bytes 4325384 | tf_op jit(solution)/shard_map/ppermute | solution.py:62
  337.9 28.6 %collective-permute-start.29 = (f32[2,1024]{1,0:T(2,128)S(1)}, f32[2,1024]{1,0:T(2,128)S(1)}, u32[]{:S(2)}, u32[]{:S(2)}) collective-permute-start(f32[2,1024]{1,0:T(2,128)S(1)} %pad_maximum_fusion.17), channel_id=1, source_target_pairs={{0,1},{1,0},{2,3},{3,2},{4,5},{5,4},{6,7},{7,6},{8,9},{9,8},{10,11... | collective-permute-start | bytes 24584 | tf_op jit(solution)/shard_map/ppermute | solution.py:62
  391.4 34.9 %collective-permute-start.35 = (bf16[2,1,704,512]{3,2,1,0:T(8,128)(2,1)}, bf16[2,1,704,512]{3,2,1,0:T(8,128)(2,1)}, u32[]{:S(2)}, u32[]{:S(2)}) collective-permute-start(bf16[2,1,704,512]{3,2,1,0:T(8,128)(2,1)} %pad_maximum_fusion.5), channel_id=1, source_target_pairs={{0,1},{1,0},{2,3},{3,2},{4,5},{5,4},{6,7},{7,6},{8,9},{9,8},{10,11... | collective-permute-start | bytes 4325384 | tf_op jit(solution)/shard_map/ppermute | solution.py:62
  393.3 33.0 %collective-permute-start.36 = (bf16[1,2,704,512]{3,2,1,0:T(8,128)(2,1)}, bf16[1,2,704,512]{3,2,1,0:T(8,128)(2,1)}, u32[]{:S(2)}, u32[]{:S(2)}) collective-permute-start(bf16[1,2,704,512]{3,2,1,0:T(8,128)(2,1)} %pad_maximum_fusion.6), channel_id=1, source_target_pairs={{0,4},{2,6},{4,0},{6,2},{1,5},{3,7},{5,1},{7,3},{8,12},{10,14},{12... | collective-permute-start | bytes 4325384 | tf_op jit(solution)/shard_map/ppermute | solution.py:61
  399.0 117.9 %reduce-scatter.6.cloned.1.call-start = ((), (), s32[]{:S(2)}) async-start(), calls=%async_computation.9 | async-start | bytes 3604480 | tf_op jit(solution)/shard_map/reduce_scatter | solution.py:788
  450.8 133.0 %all-gather.8.cloned.1.call-start = ((), (), s32[]{:S(2)}) async-start(), calls=%async_computation.10 | async-start | bytes 3604480 | tf_op jit(solution)/shard_map/all_gather | solution.py:791
  483.6 21.8 %collective-permute-start.44 = (bf16[1,1,768,512]{3,2,1,0:T(8,128)(2,1)S(1)}, bf16[1,1,768,512]{3,2,1,0:T(8,128)(2,1)S(1)}, u32[]{:S(2)}, u32[]{:S(2)}) collective-permute-start(bf16[1,1,768,512]{3,2,1,0:T(8,128)(2,1)S(1)} %bitcast.194), channel_id=1, source_target_pairs={{0,1},{1,0},{2,3},{3,2},{4,5},{5,4},{6,7},{7,6},{8,9},{9,8},{10,11... | collective-permute-start | bytes 2359304 | tf_op jit(solution)/shard_map/ppermute | solution.py:62
  484.6 20.9 %collective-permute-start.43 = (bf16[1,1,768,512]{3,2,1,0:T(8,128)(2,1)S(1)}, bf16[1,1,768,512]{3,2,1,0:T(8,128)(2,1)S(1)}, u32[]{:S(2)}, u32[]{:S(2)}) collective-permute-start(bf16[1,1,768,512]{3,2,1,0:T(8,128)(2,1)S(1)} %bitcast.191), channel_id=1, source_target_pairs={{0,4},{2,6},{4,0},{6,2},{1,5},{3,7},{5,1},{7,3},{8,12},{10,14},{12... | collective-permute-start | bytes 2359304 | tf_op jit(solution)/shard_map/ppermute | solution.py:61
  517.0 169.1 %reduce-scatter.8.cloned.1.call-start = ((), (), s32[]{:S(2)}) async-start(), calls=%async_computation.11 | async-start | bytes 3604480 | tf_op jit(solution)/shard_map/reduce_scatter | solution.py:788
  519.6 36.3 %collective-permute-start.46 = (bf16[1,2,768,512]{3,2,1,0:T(8,128)(2,1)}, bf16[1,2,768,512]{3,2,1,0:T(8,128)(2,1)}, u32[]{:S(2)}, u32[]{:S(2)}) collective-permute-start(bf16[1,2,768,512]{3,2,1,0:T(8,128)(2,1)} %pad_maximum_fusion.2), channel_id=1, source_target_pairs={{0,4},{2,6},{4,0},{6,2},{1,5},{3,7},{5,1},{7,3},{8,12},{10,14},{12... | collective-permute-start | bytes 4718600 | tf_op jit(solution)/shard_map/ppermute | solution.py:61
  521.0 35.8 %collective-permute-start.45 = (bf16[2,1,768,512]{3,2,1,0:T(8,128)(2,1)S(1)}, bf16[2,1,768,512]{3,2,1,0:T(8,128)(2,1)}, u32[]{:S(2)}, u32[]{:S(2)}) collective-permute-start(bf16[2,1,768,512]{3,2,1,0:T(8,128)(2,1)S(1)} %pad_maximum_fusion.1), channel_id=1, source_target_pairs={{0,1},{1,0},{2,3},{3,2},{4,5},{5,4},{6,7},{7,6},{8,9},{9,8},{10,11... | collective-permute-start | bytes 4718600 | tf_op jit(solution)/shard_map/ppermute | solution.py:62
  523.6 47.6 %collective-permute-start.48 = (bf16[128,2048]{1,0:T(8,128)(2,1)}, bf16[128,2048]{1,0:T(8,128)(2,1)S(1)}, u32[]{:S(2)}, u32[]{:S(2)}) collective-permute-start(bf16[128,2048]{1,0:T(8,128)(2,1)} %get-tuple-element.666), channel_id=1, source_target_pairs={{0,8},{24,16},{1,9},{25,17},{2,10},{26,18},{3,11},{27,19},{4,12},{... | collective-permute-start | bytes 1572872 | tf_op jit(solution)/shard_map/ppermute | solution.py:196
  586.1 28.3 %collective-permute-start.52 = (f32[256,1024]{1,0:T(8,128)S(1)}, f32[256,1024]{1,0:T(8,128)S(1)}, u32[]{:S(2)}, u32[]{:S(2)}) collective-permute-start(f32[256,1024]{1,0:T(8,128)S(1)} %get-tuple-element.885), channel_id=1, source_target_pairs={{0,2},{2,0},{4,6},{6,4},{1,3},{3,1},{5,7},{7,5},{8,10},{10,8},{12,... | collective-permute-start | bytes 3145736 | tf_op jit(solution)/shard_map/ppermute | solution.py:57
  586.9 27.4 %collective-permute-start.47 = (bf16[128,2048]{1,0:T(8,128)(2,1)S(1)}, bf16[128,2048]{1,0:T(8,128)(2,1)S(1)}, u32[]{:S(2)}, u32[]{:S(2)}) collective-permute-start(bf16[128,2048]{1,0:T(8,128)(2,1)S(1)} %copy-done.91), channel_id=1, source_target_pairs={{0,8},{24,16},{1,9},{25,17},{2,10},{26,18},{3,11},{27,19},{4,12},{... | collective-permute-start | bytes 1572872 | tf_op jit(solution)/shard_map/ppermute | solution.py:196
  616.5 39.2 %collective-permute-start.56 = (bf16[128,3072]{1,0:T(8,128)(2,1)}, bf16[128,3072]{1,0:T(8,128)(2,1)S(1)}, u32[]{:S(2)}, u32[]{:S(2)}) collective-permute-start(bf16[128,3072]{1,0:T(8,128)(2,1)} %get-tuple-element.691), channel_id=1, source_target_pairs={{0,8},{24,16},{1,9},{25,17},{2,10},{26,18},{3,11},{27,19},{4,12},{... | collective-permute-start | bytes 2359304 | tf_op jit(solution)/shard_map/ppermute | solution.py:196
  625.5 68.2 %collective-permute-start.34 = (bf16[2,512,1024]{2,1,0:T(8,128)(2,1)}, bf16[2,512,1024]{2,1,0:T(8,128)(2,1)}, u32[]{:S(2)}, u32[]{:S(2)}) collective-permute-start(bf16[2,512,1024]{2,1,0:T(8,128)(2,1)} %get-tuple-element.859), channel_id=1, source_target_pairs={{0,2},{2,0},{4,6},{6,4},{1,3},{3,1},{5,7},{7,5},{8,10},{10,8},{12,... | collective-permute-start | bytes 6291464 | tf_op jit(solution)/shard_map/ppermute | solution.py:57
  668.5 172.6 %all-gather.10.cloned.1.call-start = ((), (), s32[]{:S(2)}) async-start(), calls=%async_computation.12 | async-start | bytes 3604480 | tf_op jit(solution)/shard_map/all_gather | solution.py:791
  668.6 22.4 %collective-permute-start.50 = (bf16[128,3072]{1,0:T(8,128)(2,1)}, bf16[128,3072]{1,0:T(8,128)(2,1)}, u32[]{:S(2)}, u32[]{:S(2)}) collective-permute-start(bf16[128,3072]{1,0:T(8,128)(2,1)} %get-tuple-element.701), channel_id=1, source_target_pairs={{0,8},{24,16},{1,9},{25,17},{2,10},{26,18},{3,11},{27,19},{4,12},{... | collective-permute-start | bytes 2359304 | tf_op jit(solution)/shard_map/ppermute | solution.py:196
  676.7 138.9 %collective-permute-start.76 = (f32[7,256]{1,0:T(8,128)S(1)}, f32[7,256]{1,0:T(8,128)S(1)}, u32[]{:S(2)}, u32[]{:S(2)}) collective-permute-start(f32[7,256]{1,0:T(8,128)S(1)} %concatenate.159), channel_id=1, source_target_pairs={{0,8},{8,0},{16,24},{24,16},{1,9},{9,1},{17,25},{25,17},{2,10},{10... | collective-permute-start | bytes 21512 | tf_op jit(solution)/shard_map/ppermute | solution.py:967
  676.8 48.6 %collective-permute-start.61 = (bf16[128,3072]{1,0:T(8,128)(2,1)}, bf16[128,3072]{1,0:T(8,128)(2,1)}, u32[]{:S(2)}, u32[]{:S(2)}) collective-permute-start(bf16[128,3072]{1,0:T(8,128)(2,1)} %reduce-precision_convert_fusion.3), channel_id=1, source_target_pairs={{8,16},{16,8},{9,17},{17,9},{10,18},{18,10},{11,19},{19,11},{12,20... | collective-permute-start | bytes 2359304 | tf_op jit(solution)/shard_map/ppermute | solution.py:202
  686.1 20.0 %collective-permute-start.59 = (bf16[64,3072]{1,0:T(8,128)(2,1)}, bf16[64,3072]{1,0:T(8,128)(2,1)S(1)}, u32[]{:S(2)}, u32[]{:S(2)}) collective-permute-start(bf16[64,3072]{1,0:T(8,128)(2,1)} %get-tuple-element.711), channel_id=1, source_target_pairs={{0,8},{24,16},{1,9},{25,17},{2,10},{26,18},{3,11},{27,19},{4,12},{... | collective-permute-start | bytes 1179656 | tf_op jit(solution)/shard_map/ppermute | solution.py:196
  691.0 34.4 %collective-permute-start.60 = (bf16[128,2048]{1,0:T(8,128)(2,1)}, bf16[128,2048]{1,0:T(8,128)(2,1)S(1)}, u32[]{:S(2)}, u32[]{:S(2)}) collective-permute-start(bf16[128,2048]{1,0:T(8,128)(2,1)} %reduce-precision_convert_fusion.5), channel_id=1, source_target_pairs={{8,0},{16,24},{9,1},{17,25},{10,2},{18,26},{11,3},{19,27},{12,4},{... | collective-permute-start | bytes 1572872 | tf_op jit(solution)/shard_map/ppermute | solution.py:199
  693.7 68.0 %collective-permute-start.65 = (bf16[128,3072]{1,0:T(8,128)(2,1)S(1)}, bf16[128,3072]{1,0:T(8,128)(2,1)S(1)}, u32[]{:S(2)}, u32[]{:S(2)}) collective-permute-start(bf16[128,3072]{1,0:T(8,128)(2,1)S(1)} %reduce-precision_convert_fusion.2), channel_id=1, source_target_pairs={{8,16},{16,8},{9,17},{17,9},{10,18},{18,10},{11,19},{19,11},{12,20... | collective-permute-start | bytes 2359304 | tf_op jit(solution)/shard_map/ppermute | solution.py:202
  706.0 30.8 %collective-permute-start.58 = (bf16[512,1024]{1,0:T(8,128)(2,1)S(1)}, bf16[512,1024]{1,0:T(8,128)(2,1)S(1)}, u32[]{:S(2)}, u32[]{:S(2)}) collective-permute-start(bf16[512,1024]{1,0:T(8,128)(2,1)S(1)} %get-tuple-element.706), channel_id=1, source_target_pairs={{0,4},{2,6},{4,0},{6,2},{1,5},{3,7},{5,1},{7,3},{8,12},{10,14},{12... | collective-permute-start | bytes 3145736 | tf_op jit(solution)/shard_map/ppermute | solution.py:61
  725.6 20.4 %collective-permute-start.63 = (bf16[64,3072]{1,0:T(8,128)(2,1)S(1)}, bf16[64,3072]{1,0:T(8,128)(2,1)S(1)}, u32[]{:S(2)}, u32[]{:S(2)}) collective-permute-start(bf16[64,3072]{1,0:T(8,128)(2,1)S(1)} %copy-done.94), channel_id=1, source_target_pairs={{0,8},{24,16},{1,9},{25,17},{2,10},{26,18},{3,11},{27,19},{4,12},{... | collective-permute-start | bytes 1179656 | tf_op jit(solution)/shard_map/ppermute | solution.py:196
  730.9 29.5 %collective-permute-start.64 = (bf16[128,2048]{1,0:T(8,128)(2,1)S(1)}, bf16[128,2048]{1,0:T(8,128)(2,1)S(1)}, u32[]{:S(2)}, u32[]{:S(2)}) collective-permute-start(bf16[128,2048]{1,0:T(8,128)(2,1)S(1)} %reduce-precision_convert_fusion.4), channel_id=1, source_target_pairs={{8,0},{16,24},{9,1},{17,25},{10,2},{18,26},{11,3},{19,27},{12,4},{... | collective-permute-start | bytes 1572872 | tf_op jit(solution)/shard_map/ppermute | solution.py:199
  736.8 37.0 %collective-permute-start.68 = (bf16[64,3072]{1,0:T(8,128)(2,1)S(1)}, bf16[64,3072]{1,0:T(8,128)(2,1)S(1)}, u32[]{:S(2)}, u32[]{:S(2)}) collective-permute-start(bf16[64,3072]{1,0:T(8,128)(2,1)S(1)} %reduce-precision_convert_fusion.15), channel_id=1, source_target_pairs={{8,16},{16,8},{9,17},{17,9},{10,18},{18,10},{11,19},{19,11},{12,20... | collective-permute-start | bytes 1179656 | tf_op jit(solution)/shard_map/ppermute | solution.py:202
  746.0 40.8 %collective-permute-start.66 = (bf16[64,3072]{1,0:T(8,128)(2,1)S(1)}, bf16[64,3072]{1,0:T(8,128)(2,1)S(1)}, u32[]{:S(2)}, u32[]{:S(2)}) collective-permute-start(bf16[64,3072]{1,0:T(8,128)(2,1)S(1)} %copy-done.93), channel_id=1, source_target_pairs={{0,8},{24,16},{1,9},{25,17},{2,10},{26,18},{3,11},{27,19},{4,12},{... | collective-permute-start | bytes 1179656 | tf_op jit(solution)/shard_map/ppermute | solution.py:196
  760.4 27.7 %collective-permute-start.67 = (bf16[128,3072]{1,0:T(8,128)(2,1)S(1)}, bf16[128,3072]{1,0:T(8,128)(2,1)S(1)}, u32[]{:S(2)}, u32[]{:S(2)}) collective-permute-start(bf16[128,3072]{1,0:T(8,128)(2,1)S(1)} %reduce-precision_convert_fusion.1), channel_id=1, source_target_pairs={{8,0},{16,24},{9,1},{17,25},{10,2},{18,26},{11,3},{19,27},{12,4},{... | collective-permute-start | bytes 2359304 | tf_op jit(solution)/shard_map/ppermute | solution.py:199
  788.2 45.2 %collective-permute-start.75 = (bf16[64,3072]{1,0:T(8,128)(2,1)S(1)}, bf16[64,3072]{1,0:T(8,128)(2,1)}, u32[]{:S(2)}, u32[]{:S(2)}) collective-permute-start(bf16[64,3072]{1,0:T(8,128)(2,1)S(1)} %reduce-precision_convert_fusion.13), channel_id=1, source_target_pairs={{8,16},{16,8},{9,17},{17,9},{10,18},{18,10},{11,19},{19,11},{12,20... | collective-permute-start | bytes 1179656 | tf_op jit(solution)/shard_map/ppermute | solution.py:202
  847.1 28.4 %collective-permute-start.79 = (bf16[64,3072]{1,0:T(8,128)(2,1)}, bf16[64,3072]{1,0:T(8,128)(2,1)S(1)}, u32[]{:S(2)}, u32[]{:S(2)}) collective-permute-start(bf16[64,3072]{1,0:T(8,128)(2,1)} %reduce-precision_convert_fusion.8), channel_id=1, source_target_pairs={{8,0},{16,24},{9,1},{17,25},{10,2},{18,26},{11,3},{19,27},{12,4},{... | collective-permute-start | bytes 1179656 | tf_op jit(solution)/shard_map/ppermute | solution.py:199
  848.4 20.8 %collective-permute-start.81 = (bf16[64,3072]{1,0:T(8,128)(2,1)}, bf16[64,3072]{1,0:T(8,128)(2,1)S(1)}, u32[]{:S(2)}, u32[]{:S(2)}) collective-permute-start(bf16[64,3072]{1,0:T(8,128)(2,1)} %reduce-precision_convert_fusion.9), channel_id=1, source_target_pairs={{8,0},{16,24},{9,1},{17,25},{10,2},{18,26},{11,3},{19,27},{12,4},{... | collective-permute-start | bytes 1179656 | tf_op jit(solution)/shard_map/ppermute | solution.py:199
  (170 other events, 1451.1 us)
Sparse Core Ops, SparseCore 0:
  123.0 45.1 all-gather.11
  317.4 57.3 reduce-scatter.3
  399.2 60.0 all-gather.5
  462.0 54.8 reduce-scatter.5
  518.4 65.4 all-gather.7
  586.0 82.4 reduce-scatter.7
  686.2 80.9 all-gather.9

commit v7 on v6

--- a/solution.py
+++ b/solution.py
@@ -141,6 +141,7 @@
         self.end = (z == 0) | (z == lax.axis_size("rep") - 1)
         self.queue = []
         self.flight = []
+        self.depth = 1
         self.done = {}
 
     def push(self, name, g):
@@ -151,7 +152,7 @@
 
     def tick(self):
         old = {}
-        if len(self.flight) == 2 or (self.flight and not self.queue):
+        if len(self.flight) >= self.depth or (self.flight and not self.queue):
             old = self.flight.pop(0)
         new = self.queue.pop(0) if self.queue else None
         values = {}
@@ -650,6 +651,31 @@
 
         return n, start, finish, result
 
+    def gain_products(wg, wu, cols):
+        terms = []
+        for v in (cols[:, 2], cols[:, 3]):
+            t = lax.reduce_precision(v, 8, 7)
+            terms += [t, v - t]
+        terms = jnp.stack(terms).astype(bf16)
+        out = []
+        for mine, theirs in (wg, wu):
+            p = dot(terms[:, :blk], mine, LAST) + dot(terms[:, blk:], theirs, LAST)
+            out.append(jnp.stack([p[0] + p[1], p[2] + p[3]]).reshape(2, Y, S, ffb))
+        return jnp.concatenate(out, axis=0)
+
+    gains = do(gain_products, wg_parts, wu_parts, pair_cols)
+    gain_steps = list(at.steps(False))
+
+    def gain_step(gains):
+        axis, step = gain_steps.pop(0)
+        ax = {"y": 1, "s": 2}[axis]
+        bit = (at.index(axis) // step) % 2
+        send = lax.dynamic_slice_in_dim(gains, (1 - bit) * step, step, ax)
+        kept = lax.dynamic_slice_in_dim(gains, bit * step, step, ax)
+        return kept, at.along(send, axis, step)
+
+    gains = gain_step(gains)
+
     qkvs, attns, attn_got, stats = [], [], [], []
     for k in range(2):
         shape = (3, heads, HEAD_DIM, H)
@@ -658,6 +684,14 @@
         attns.append(attn.reshape(blk, H))
         attn_got.append(at.core(attns[k]))
         stats.append(stat)
+        gains = do(lambda a, b: a + b, *gains)
+        if gain_steps:
+            gains = gain_step(gains)
+        else:
+            gains = (gains, jnp.zeros_like(gains))
+    while gain_steps:
+        gains = gain_step(do(lambda a, b: a + b, *gains))
+    gains = do(lambda a, b: (a + b).reshape(4, ffb, 1), *gains)
 
     pairs = [do(join, attns[k], attn_got[k]) for k in range(2)]
     flying = scatter_rest(send_products(wo_cut, pairs))
@@ -691,33 +725,11 @@
     flying = send_products([wg_cut, wu_cut], [xn2, xn2])
 
     wd_own = do(cast, w_down)
-    wg = do(side_by_side, *wg_parts)
-    wu = do(side_by_side, *wu_parts)
-
-    def gain_products(wg, wu, cols):
-        g, b = cols[:, 2], cols[:, 3]
-        terms = []
-        for v in (g, b):
-            t = lax.reduce_precision(v, 8, 7)
-            terms += [t, v - t]
-        terms = jnp.stack(terms).astype(bf16)
-        out = []
-        for w in (wg, wu):
-            p = dot(w, terms, LAST)
-            out.append(jnp.stack([p[:, 0] + p[:, 1], p[:, 2] + p[:, 3]]).reshape(2, Y, S, ffb))
-        return jnp.concatenate(out, axis=0)
-
-    gains = do(gain_products, wg, wu, pair_cols)
-    for axis, step in at.steps(False):
-        ax = {"y": 1, "s": 2}[axis]
-        bit = (at.index(axis) // step) % 2
-        send = lax.dynamic_slice_in_dim(gains, (1 - bit) * step, step, ax)
-        kept = lax.dynamic_slice_in_dim(gains, bit * step, step, ax)
-        gains = do(lambda a, b: a + b, kept, at.along(send, axis, step))
-    gains = do(lambda g: g.reshape(4, ffb, 1), gains)
     grad_act = do(lambda w, c: dot(w, c, LAST), wd_own, cot_all)
     cot_cols = do(lambda c: lax.dynamic_slice_in_dim(c, my_block * blk, blk, 1).T, cot_all)
     wo_own = do(cast, w_out)
+    wg = do(side_by_side, *wg_parts)
+    wu = do(side_by_side, *wu_parts)
     wq = do(side_by_side, *wq_parts)
     flying = scatter_rest(flying)
 
@@ -739,7 +751,7 @@
         n = parts_of(count, want)
         return [(k * (count // n), count // n) for k in range(n)]
 
-    out_rows = even(blk, 2)
+    down_rows, up_rows, out_rows = even(ffb, 2), [(0, blk)], [(0, blk)]
     qkv_rows = [(0, blk // 2), (blk // 2, blk // 4), (3 * blk // 4, blk // 4)]
 
     def push_pairs(name, g, rows):
@@ -765,10 +777,15 @@
         )
 
     jobs = []
+    for k, (at_row, count) in enumerate(down_rows):
+        jobs.append(("down", [("down", k)], at_row, 0, count, 1024))
+    for name, lead in (("gate", 0), ("up", Y)):
+        for k, (at_row, count) in enumerate(up_rows):
+            jobs.append(("up", [(name, "mine", k), (name, "theirs", k)], at_row, lead, count, S * ffb))
     for k, (at_row, count) in enumerate(out_rows):
-        jobs.append(("out", [("out", k)], at_row, count, 1024))
+        jobs.append(("out", [("out", k)], at_row, 0, count, 1024))
     for k, (at_row, count) in enumerate(qkv_rows):
-        jobs.append(("qkv", [("qkv", "mine", k), ("qkv", "theirs", k)], at_row, count, S * blk))
+        jobs.append(("qkv", [("qkv", "mine", k), ("qkv", "theirs", k)], at_row, 0, count, S * blk))
     received = {}
 
     def update(limit):
@@ -776,27 +793,24 @@
             if name[1] == "theirs" and name not in received:
                 received[name] = at.core(reps.done[name])
         while jobs and limit and all(k in reps.done for k in jobs[0][1]):
-            name, needs, at_row, count, unit = jobs.pop(0)
-            adam(name, [received[k] if k[1] == "theirs" else reps.done[k] for k in needs], at_row, 0, unit, count)
+            name, needs, at_row, lead, count, unit = jobs.pop(0)
+            rb = max(n for n in range(8, min(count, 176) + 1, 8) if count % n == 0 and at_row % n == 0)
+            adam(name, [received[k] if k[1] == "theirs" else reps.done[k] for k in needs], at_row, lead, unit, rb)
             limit -= 1
 
     def ticks(n):
         for _ in range(n):
             reps.tick()
 
-    def rep_scatter(g):
-        return lax.psum_scatter(g, "rep", scatter_dimension=0, tiled=True)
-
-    def rep_gather(g):
-        return lax.all_gather(do(lambda g: g, g), "rep", axis=0, tiled=True)
-
     def quarter_heads(x):
         return [x[:, h][None, None] for h in halves]
 
     n, start, finish, gate_all = gather_steps(quarter_heads(ggate), 3)
     start(0)
     g_down = do(lambda a, c: dot(a, c, PLAIN).astype(bf16), act, cot_all)
-    g_down = rep_scatter(g_down)
+    for k, (at_row, count) in enumerate(down_rows):
+        reps.push(("down", k), g_down[at_row : at_row + count])
+    ticks(1)
 
     def norm_sums2(ggate, gup, gate, up, gains):
         a, b = ggate.astype(f32), gup.astype(f32)
@@ -807,19 +821,27 @@
     sums = do(norm_sums2, ggate, gup, gate, up, gains)
     steps2 = at.steps(False) + [("core", 1)]
 
+    def sum_send(sums, axis, step):
+        return at.core(sums) if axis == "core" else at.along(sums, axis, step)
+
     def sum_step(sums, axis, step):
-        other = at.core(sums) if axis == "core" else at.along(sums, axis, step)
-        return do(lambda a, b: a + b, sums, other)
-
-    finish()
-    start(1)
-    for axis, step in steps2:
-        sums = sum_step(sums, axis, step)
-    for i in range(2, n):
+        return do(lambda a, b: a + b, sums, sum_send(sums, axis, step))
+
+    tiny = list(steps2)
+    sums_got = sum_send(sums, *tiny[0])
+    for i in range(1, n):
         finish()
+        sums = do(lambda a, b: a + b, sums, sums_got)
+        tiny.pop(0)
         start(i)
+        sums_got = sum_send(sums, *tiny[0])
+        ticks(1)
     n, start_up, finish_up, up_all = gather_steps(quarter_heads(gup), 3)
     finish()
+    for axis, step in tiny:
+        sums = do(lambda a, b: a + b, sums, sums_got)
+        if (axis, step) != tiny[-1]:
+            sums_got = sum_send(sums, *tiny[tiny.index((axis, step)) + 1])
     start_up(0)
     ggate_all = do(lambda x: x.reshape(Y * S * ffb, T), gate_all())
     finish_up()
@@ -827,11 +849,10 @@
         start_up(i)
         if i == 1:
             g_gate = do(lambda x, g: dot(x, g, LAST).astype(bf16), xn2, ggate_all)
-            g_down = rep_gather(g_down)
-            g_gate = rep_scatter(do(lambda g: g, g_gate))
+            push_pairs("gate", g_gate, up_rows)
             part_gate = do(lambda w, g: dot(w, g, FIRST), wg, ggate_all)
-            out_part = do(lambda w, a: dot(w, a, FIRST).astype(bf16), wd_own, act).reshape(Y, 2, S * blk, T)
-            out_theirs = at.core(pick(out_part, 1, 1 - at.c))
+            out_part = do(lambda w, a: dot(w, a, FIRST).astype(bf16), wd_own, act)
+            ticks(1)
         finish_up()
     gup_all = do(lambda x: x.reshape(Y * S * ffb, T), up_all())
     part = do(lambda w, g, p: dot(w, g, FIRST) + p, wu, gup_all, part_gate)
@@ -849,9 +870,12 @@
     n, start, finish, branch_all = gather_steps(quarter_heads(grad_branch), 3)
     start(0)
     g_up = do(lambda x, g: dot(x, g, LAST).astype(bf16), xn2, gup_all)
+    push_pairs("up", g_up, up_rows)
     finish()
     for i in range(1, n):
         start(i)
+        if i == 1:
+            ticks(1)
         finish()
     gbr_c = do(lambda x: x, branch_all())
     gbr_o = at.core(gbr_c)
@@ -868,14 +892,14 @@
     g_out = do(lambda a, g: dot(a, g, LAST).astype(bf16), attn, gbr)
     for k, (at_row, count) in enumerate(out_rows):
         reps.push(("out", k), g_out[at_row : at_row + count])
-    adam("down", [g_down], 0, 0, 1024, ffb // 4 if ffb % 64 == 0 else ffb)
+    ticks(1)
     finish()
     for i in range(1, n):
         start(i)
         if i == 1:
-            g_gate = rep_gather(g_gate)
-            g_up = rep_scatter(do(lambda g: g, g_up))
-            reps.tick()
+            update(1)
+            ticks(1)
+            update(1)
         finish()
 
     def qkv_columns(x):
@@ -884,19 +908,12 @@
     gqkv = do(qkv_columns, gqkv_done())
     g_qkv = do(lambda x, g: dot(x, g, LAST).astype(bf16), xn1, gqkv)
     push_pairs("qkv", g_qkv, qkv_rows)
-    ticks(1)
     part = do(lambda w, g: dot(w, g, FIRST), wq, gqkv)
     part_theirs = at.core(part[blk:])
+    out_sum = lax.psum_scatter(out_part, plane, scatter_dimension=0, tiled=True)
+    reps.depth = 2
     ticks(1)
-
-    def split_rows(g):
-        return do(lambda g: (g[:blk], g[blk:]), g)
-
-    def adam_ff(g, lead):
-        mine, theirs = split_rows(g)
-        adam("up", [mine, at.core(theirs)], 0, lead, S * ffb, min(blk, 128))
-
-    adam_ff(g_gate, 0)
+    update(1)
     ticks(1)
 
     def first_back(a, b, x, mean, inv, gain, gxn2, z2, gqkv0, gqkv1):
@@ -938,42 +955,30 @@
         got = lax.all_to_all(split, plane, split_axis=0, concat_axis=0, tiled=True)
         return do(lambda g: g.reshape(width, rows).T, got)
 
+    input_rows = to_rows(input_grad)
+    ticks(1)
     update(1)
-    input_rows = to_rows(input_grad)
-    g_up = rep_gather(g_up)
-    reps.tick()
+    ticks(1)
+    everyone = ("rep",) + plane
+    small_all = lax.all_gather(small[None], everyone, axis=0, tiled=True)
     update(1)
-
-    kept, got = pick(out_part, 1, at.c).reshape(-1, T), out_theirs.reshape(-1, T)
-    for k, (axis, step) in enumerate(at.steps(True)):
-        bit = (at.index(axis) // step) % 2
-        send, kept = do(lambda a, b: add_split(a, b, bit.reshape(1)), kept, got)
-        got = at.along(send, axis, step)
-        if k < 2:
-            reps.tick()
-            update(1)
-    out_cols = do(
-        lambda h, a, b: (h + (a.astype(f32) + b.astype(f32))).astype(bf16), hidden, kept, got
-    )
-    reps.tick()
+    ticks(1)
+
+    out_cols = do(lambda h, a: (h + a.astype(f32)).astype(bf16), hidden, out_sum)
+    block_output = to_rows(out_cols)
+    ticks(1)
     update(1)
-    block_output = to_rows(out_cols)
-    reps.tick()
+    ticks(1)
     update(1)
 
-    n_rep = lax.axis_size("rep")
-    step = 1
-    while step < n_rep:
-        other = lax.ppermute(small, "rep", [(i, i ^ step) for i in range(n_rep)])
-        small = do(lambda a, b: a + b, small, other)
-        step *= 2
-    sent = do(lambda s: jnp.broadcast_to(s.reshape(1, 7, blk), (nb, 7, blk)), small)
-    got = lax.all_to_all(sent, plane, split_axis=0, concat_axis=0, tiled=True)
-    norm_grad = got.transpose(1, 0, 2).reshape(7, width)
-    mn, vn, wn = do(lambda *a: adam_update(*a, 0.3, 0.0), norm_params, m_norm, v_norm, norm_grad)
-
-    ticks(2)
-    adam_ff(g_up, Y)
+    def norm_update(every, *a):
+        every = every.reshape(lax.axis_size("rep"), nb, 7, blk)
+        total = every[0]
+        for k in range(1, every.shape[0]):
+            total = total + every[k]
+        return adam_update(*a, total.transpose(1, 0, 2).reshape(7, width), 0.3, 0.0)
+
+    mn, vn, wn = do(norm_update, small_all, norm_params, m_norm, v_norm)
     while reps.busy():
         reps.tick()
         update(1)

time: 903 us -> 920 us (1.019)
  waiting for transfers between devices: 387 us -> 295 us
  blocking collectives: 0 us -> 77.1 us
  other arithmetic: 65.1 us -> 88.6 us
  starting transfers between devices: 125 us -> 137 us
  local copies, waits for them, and re-layouts: 85.3 us -> 73.7 us
    all_gather x0 -> x1, blocking collectives: none -> 77.1 us  [body(): small_all = lax.all_gather(small[None], everyone, axis=0, tiled=True)]
    ppermute x19 -> x18, waiting for transfers between devices: 72.7 us -> 32.1 us  [along(): lax.ppermute(x, 'ctx', [(i, i ^ 2 * step) for i in range(self.ctx_size)])]
    ppermute x8 -> x11, waiting for transfers between devices: 55.3 us -> 16.1 us  [tick(): slot['in_got'] = lax.ppermute(out['new'], 'rep', [(0, 1), (3, 2)])]
    ppermute x8 -> x11, waiting for transfers between devices: 47.6 us -> 83.7 us  [tick(): slot['out_got'] = lax.ppermute(out['total'], 'rep', [(1, 0), (2, 3)])]
    ppermute x19 -> x18, waiting for transfers between devices: 167 us -> 136 us  [along(): return lax.ppermute(x, 'shard', [(i, i ^ step) for i in range(self.s_size)])]
    convert_element_type x16 -> x24, other arithmetic: 15.1 us -> 32 us  [add(): lax.reduce_precision(a.astype(f32) + b.astype(f32), 8, 7).astype(bf16)]
    ppermute x2, waiting for transfers between devices: 0.47 us -> 13.7 us  [tick(): got = lax.ppermute(out['total'], 'rep', [(0, 1), (1, 0), (2, 3), (3, 2)])]
    all_gather x3 -> x0, waiting for transfers between devices: 10.7 us -> none  [rep_gather(): return lax.all_gather(do(lambda g: g, g), 'rep', axis=0, tiled=True)]
  transfers between devices with their start and end apart: 95 -> 97, of which waited for: 49 -> 43; matrix products, arithmetic and copies ran while one was open for 18% -> 20% of each run, Pallas kernels for 14% -> 14%
where the time goes in v7:
time: 920 us; the launch traced here: 907 us
  waiting for transfers between devices  295 us (32%)
  Pallas kernels  140 us (15%)
  starting transfers between devices  137 us (15%)
  other arithmetic  88.6 us (10%)
  matrix products  79.1 us (9%)
  blocking collectives  77.1 us (8%)
  local copies, waits for them, and re-layouts  73.7 us (8%)
  between operations  16.7 us (2%)
    ppermute x18, waiting for transfers between devices, along(): return lax.ppermute(x, 'shard', [(i, i ^ step) for i in range(self.s_size)])  136 us
    ppermute x11, waiting for transfers between devices, tick(): slot['out_got'] = lax.ppermute(out['total'], 'rep', [(1, 0), (2, 3)])  83.7 us
    dot_general x27, matrix products, dot(): return lax.dot_general(a, b, dims, preferred_element_type=f32)  79.1 us
    all_gather x1, blocking collectives, body(): small_all = lax.all_gather(small[None], everyone, axis=0, tiled=True)  77.1 us
    pallas_call x8, Pallas kernels, adam_part(): pl.pallas_call(functools.partial(adam_kernel, rate, two), grid_spec=pltpu...  69.8 us
    ppermute x11, starting transfers between devices, tick(): slot['in_got'] = lax.ppermute(out['new'], 'rep', [(0, 1), (3, 2)])  42.7 us
    unnamed x259, local copies, waits for them, and re-layouts  35.7 us
    ppermute x18, waiting for transfers between devices, along(): lax.ppermute(x, 'ctx', [(i, i ^ 2 * step) for i in range(self.ctx_size)])  32.1 us
  transfers between devices with their start and end apart: 97, of which 43 were waited for; matrix products, arithmetic and copies ran while one was open for 20% of the time, Pallas kernels for 14%

profile of v7, /device:TPU:0, one launch (start us, length us, event | category | flops | bytes accessed | tf_op | source)
XLA Modules:
  0.0 907.2 jit_solution(9987468612513094264)
XLA Ops:
  19.4 4.8 all-to-all-start
  74.6 7.7 collective-permute-done.3.b_ref.d_ref
  111.1 5.1 shard_map.317
  125.0 4.8 shard_map.318
  136.6 14.4 %collective-permute-done.13.b_ref.d_ref = bf16[512,512]{1,0:T(8,128)(2,1)S(1)} collective-permute-done((bf16[512,512]{1,0:T(8,128)(2,1)S(1)}, bf16[512,512]{1,0:T(8,128)(2,1)S(1)}, u32[]{:S(2)}, u32[]{:S(2)}) %collective-permute-start.13) | collective-permute-done | bytes 524320 | tf_op jit(solution)/shard_map/ppermute | solution.py:62
  154.0 12.0 %collective-permute-done.16 = bf16[256,512]{1,0:T(8,128)(2,1)S(1)} collective-permute-done((bf16[256,512]{1,0:T(8,128)(2,1)S(1)}, bf16[256,512]{1,0:T(8,128)(2,1)S(1)}, u32[]{:S(2)}, u32[]{:S(2)}) %collective-permute-start.16) | collective-permute-done | bytes 262176 | tf_op jit(solution)/shard_map/ppermute | solution.py:62
  187.3 5.0 convolution_convert_fusion.5.a_ref.c_ref
  200.1 7.9 fusion.51
  211.1 4.1 shard_map.323
  224.5 22.3 %collective-permute-done.21.b_ref.d_ref = bf16[1408,1024]{1,0:T(8,128)(2,1)} collective-permute-done((bf16[1408,1024]{1,0:T(8,128)(2,1)}, bf16[1408,1024]{1,0:T(8,128)(2,1)}, u32[]{:S(2)}, u32[]{:S(2)}) %collective-permute-start.21) | collective-permute-done | bytes 2883616 | tf_op jit(solution)/shard_map/ppermute | solution.py:62
  256.8 31.3 %collective-permute-done.24 = bf16[704,1024]{1,0:T(8,128)(2,1)} collective-permute-done((bf16[704,1024]{1,0:T(8,128)(2,1)}, bf16[704,1024]{1,0:T(8,128)(2,1)}, u32[]{:S(2)}, u32[]{:S(2)}) %collective-permute-start.24) | collective-permute-done | bytes 1441824 | tf_op jit(solution)/shard_map/ppermute | solution.py:62
  303.7 5.7 collective-permute-done.26
  313.4 28.1 %collective-permute-done.30 = f32[2,1024]{1,0:T(2,128)S(1)} collective-permute-done((f32[2,1024]{1,0:T(2,128)S(1)}, f32[2,1024]{1,0:T(2,128)S(1)}, u32[]{:S(2)}, u32[]{:S(2)}) %collective-permute-start.30) | collective-permute-done | bytes 8224 | tf_op jit(solution)/shard_map/ppermute | solution.py:62
  350.3 6.2 collective-permute-start.37
  358.3 5.5 collective-permute-done.34
  369.9 4.5 convolution_convert_fusion.2
  374.4 4.5 fusion.52
  378.9 5.0 convolution_convert_fusion.3
  389.0 12.3 %collective-permute-done.36 = bf16[1,2,704,512]{3,2,1,0:T(8,128)(2,1)} collective-permute-done((bf16[1,2,704,512]{3,2,1,0:T(8,128)(2,1)}, bf16[1,2,704,512]{3,2,1,0:T(8,128)(2,1)}, u32[]{:S(2)}, u32[]{:S(2)}) %collective-permute-start.36) | collective-permute-done | bytes 1441824 | tf_op jit(solution)/shard_map/ppermute | solution.py:61
  415.4 6.2 collective-permute-start.44
  426.1 4.8 convolution_convert_fusion.1
  433.5 17.9 %collective-permute-done.45 = bf16[352,2048]{1,0:T(8,128)(2,1)S(1)} collective-permute-done((bf16[352,2048]{1,0:T(8,128)(2,1)S(1)}, bf16[352,2048]{1,0:T(8,128)(2,1)S(1)}, u32[]{:S(2)}, u32[]{:S(2)}) %collective-permute-start.45) | collective-permute-done | bytes 1441824 | tf_op jit(solution)/shard_map/ppermute | solution.py:200
  455.7 10.4 %collective-permute-done.43 = bf16[1,2,256,512]{3,2,1,0:T(8,128)(2,1)S(1)} collective-permute-done((bf16[1,2,256,512]{3,2,1,0:T(8,128)(2,1)S(1)}, bf16[1,2,256,512]{3,2,1,0:T(8,128)(2,1)S(1)}, u32[]{:S(2)}, u32[]{:S(2)}) %collective-permute-start.43) | collective-permute-done | bytes 524320 | tf_op jit(solution)/shard_map/ppermute | solution.py:61
  474.0 6.7 collective-permute-start.50
  486.6 5.5 shard_map.328
  492.1 5.5 shard_map.329
  502.5 8.0 collective-permute-done.51
  518.4 5.7 collective-permute-done.49
  526.9 8.1 shard_map.330
  535.0 11.1 %collective-permute-done.55 = bf16[256,2816]{1,0:T(8,128)(2,1)S(1)} collective-permute-done((bf16[256,2816]{1,0:T(8,128)(2,1)S(1)}, bf16[256,2816]{1,0:T(8,128)(2,1)S(1)}, u32[]{:S(2)}, u32[]{:S(2)}) %collective-permute-start.55) | collective-permute-done | bytes 1441824 | tf_op jit(solution)/shard_map/ppermute | solution.py:192
  552.9 6.6 collective-permute-start.57
  559.5 8.1 shard_map.331
  575.5 6.6 convolution_convert_fusion
  611.3 10.9 %collective-permute-done.66 = bf16[256,2048]{1,0:T(8,128)(2,1)S(1)} collective-permute-done((bf16[256,2048]{1,0:T(8,128)(2,1)S(1)}, bf16[256,2048]{1,0:T(8,128)(2,1)S(1)}, u32[]{:S(2)}, u32[]{:S(2)}) %collective-permute-start.66) | collective-permute-done | bytes 1048608 | tf_op jit(solution)/shard_map/ppermute | solution.py:197
  627.9 4.2 all-to-all-start.1
  634.0 77.1 %all-gather.2 = f32[32,7,256]{2,1,0:T(8,128)} all-gather(f32[1,7,256]{2,1,0:T(8,128)S(1)} %bitcast.228), channel_id=3, replica_groups=mesh['rep'=4,'ctx'=4,'shard'=2] {'rep','ctx','shard'}, dimensions={0}, use_global_device_ids=true | all-gather | bytes 236544 | tf_op jit(solution)/shard_map/all_gather | solution.py:963
  720.9 13.2 %shard_map.332 = (f32[256,11264]{1,0:T(8,128)}, f32[256,11264]{1,0:T(8,128)}, f32[256,11264]{1,0:T(8,128)}) custom-call(s32[1]{0:T(128)} %bitcast.8.core_ref, f32[256,11264]{1,0:T(8,128)} %w_ref.9, f32[256,11264]{1,0:T(8,128)} %m_ref.3, f32[256,11264]{1,0:T(8,128)} %v_ref.3, bf16[256,2816]{1,0:T(8,128)(2,1)S(1)} %broadcast_select_fusion.7.refs_0_, ...), custom_call_target="tpu_custom_call" | custom-call | flops 1024 | bytes 1024 | tf_op jit(solution)/shard_map/pallas_call | solution.py:367
  749.6 19.7 %collective-permute-done.74 = bf16[256,2048]{1,0:T(8,128)(2,1)S(1)} collective-permute-done((bf16[256,2048]{1,0:T(8,128)(2,1)S(1)}, bf16[256,2048]{1,0:T(8,128)(2,1)S(1)}, u32[]{:S(2)}, u32[]{:S(2)}) %collective-permute-start.74) | collective-permute-done | bytes 1048608 | tf_op jit(solution)/shard_map/ppermute | solution.py:200
  772.8 21.8 %collective-permute-done.68 = bf16[256,2816]{1,0:T(8,128)(2,1)S(1)} collective-permute-done((bf16[256,2816]{1,0:T(8,128)(2,1)S(1)}, bf16[256,2816]{1,0:T(8,128)(2,1)S(1)}, u32[]{:S(2)}, u32[]{:S(2)}) %collective-permute-start.68) | collective-permute-done | bytes 1441824 | tf_op jit(solution)/shard_map/ppermute | solution.py:200
  805.1 4.1 all-to-all-start.2
  817.1 4.8 collective-permute-start.76
  822.0 13.0 %shard_map.333 = (f32[256,11264]{1,0:T(8,128)}, f32[256,11264]{1,0:T(8,128)}, f32[256,11264]{1,0:T(8,128)}) custom-call(s32[1]{0:T(128)} %bitcast.8.core_ref, f32[256,11264]{1,0:T(8,128)} %w_ref.9, f32[256,11264]{1,0:T(8,128)} %m_ref.3, f32[256,11264]{1,0:T(8,128)} %v_ref.3, ...), custom_call_target="tpu_custom_call", output_to_operand_aliasing={{0}: (6, {}), {1}: (7, {}), {2}: (8, {})} | custom-call | flops 1024 | bytes 1024 | tf_op jit(solution)/shard_map/pallas_call | solution.py:367
  844.6 5.5 shard_map.334
  850.9 8.5 collective-permute-done.77
  864.0 9.6 %shard_map.335 = (f32[256,6144]{1,0:T(8,128)}, f32[256,6144]{1,0:T(8,128)}, f32[256,6144]{1,0:T(8,128)}) custom-call(s32[1]{0:T(128)} %bitcast.8.core_ref, f32[256,6144]{1,0:T(8,128)} %w_ref.13, f32[256,6144]{1,0:T(8,128)} %m_ref.7, f32[256,6144]{1,0:T(8,128)} %v_ref.7, bf16[128,3072]{1,0:T(8,128)(2,1)S(1)} %broadcast_select_fusion.20.refs_0_, ...), custom_call_target="tpu_custom_call" | custom-call | flops 1024 | bytes 1024 | tf_op jit(solution)/shard_map/pallas_call | solution.py:367
  878.2 6.2 shard_map.336
  887.8 4.4 collective-permute-done.88
  894.0 6.2 shard_map.337
  (656 shorter events, 378.9 us)
Async XLA Ops:
  24.2 175.9 %all-gather.5.cloned.1.call-start = ((), (), s32[]{:S(2)}) async-start(), calls=%async_computation.5 | async-start | bytes 4718592 | tf_op jit(solution)/shard_map/all_gather | solution.py:547
  45.5 36.8 %collective-permute-start.3 = (bf16[1536,512]{1,0:T(8,128)(2,1)}, bf16[1536,512]{1,0:T(8,128)(2,1)}, u32[]{:S(2)}, u32[]{:S(2)}) collective-permute-start(bf16[1536,512]{1,0:T(8,128)(2,1)} %convolution_convert_fusion.12), channel_id=1, source_target_pairs={{0,1},{1,0},{2,3},{3,2},{4,5},{5,4},{6,7},{7,6},{8,9},{9,8},{10,11... | collective-permute-start | bytes 4718600 | tf_op jit(solution)/shard_map/ppermute | solution.py:62
  48.6 40.2 %collective-permute-start.7 = (bf16[1536,512]{1,0:T(8,128)(2,1)}, bf16[1536,512]{1,0:T(8,128)(2,1)}, u32[]{:S(2)}, u32[]{:S(2)}) collective-permute-start(bf16[1536,512]{1,0:T(8,128)(2,1)} %convolution_convert_fusion.11), channel_id=1, source_target_pairs={{0,4},{2,6},{4,0},{6,2},{1,5},{3,7},{5,1},{7,3},{8,12},{10,14},{12... | collective-permute-start | bytes 4718600 | tf_op jit(solution)/shard_map/ppermute | solution.py:61
  58.8 35.4 %collective-permute-start.5 = (bf16[2816,256]{1,0:T(8,128)(2,1)}, bf16[2816,256]{1,0:T(8,128)(2,1)}, u32[]{:S(2)}, u32[]{:S(2)}) collective-permute-start(bf16[2816,256]{1,0:T(8,128)(2,1)} %get-tuple-element.479), channel_id=1, source_target_pairs={{0,2},{2,0},{4,6},{6,4},{1,3},{3,1},{5,7},{7,5},{8,10},{10,8},{12,... | collective-permute-start | bytes 4325384 | tf_op jit(solution)/shard_map/ppermute | solution.py:57
  62.1 34.2 %collective-permute-start.6 = (bf16[2816,256]{1,0:T(8,128)(2,1)}, bf16[2816,256]{1,0:T(8,128)(2,1)}, u32[]{:S(2)}, u32[]{:S(2)}) collective-permute-start(bf16[2816,256]{1,0:T(8,128)(2,1)} %get-tuple-element.480), channel_id=1, source_target_pairs={{0,2},{2,0},{4,6},{6,4},{1,3},{3,1},{5,7},{7,5},{8,10},{10,8},{12,... | collective-permute-start | bytes 4325384 | tf_op jit(solution)/shard_map/ppermute | solution.py:57
  93.4 28.8 %collective-permute-start.11 = (bf16[768,512]{1,0:T(8,128)(2,1)}, bf16[768,512]{1,0:T(8,128)(2,1)}, u32[]{:S(2)}, u32[]{:S(2)}) collective-permute-start(bf16[768,512]{1,0:T(8,128)(2,1)} %get-tuple-element.483), channel_id=1, source_target_pairs={{0,1},{1,0},{2,3},{3,2},{4,5},{5,4},{6,7},{7,6},{8,9},{9,8},{10,11... | collective-permute-start | bytes 2359304 | tf_op jit(solution)/shard_map/ppermute | solution.py:62
  122.1 676.8 %reduce-scatter.2.cloned.1.call-start = ((), (), s32[]{:S(2)}) async-start(), calls=%async_computation.4 | async-start | bytes 4718592 | tf_op jit(solution)/shard_map/reduce_scatter | solution.py:913
  182.0 64.9 %collective-permute-start.21 = (bf16[1408,1024]{1,0:T(8,128)(2,1)}, bf16[1408,1024]{1,0:T(8,128)(2,1)}, u32[]{:S(2)}, u32[]{:S(2)}) collective-permute-start(bf16[1408,1024]{1,0:T(8,128)(2,1)} %convolution_convert_fusion.7), channel_id=1, source_target_pairs={{0,1},{1,0},{2,3},{3,2},{4,5},{5,4},{6,7},{7,6},{8,9},{9,8},{10,11... | collective-permute-start | bytes 8650760 | tf_op jit(solution)/shard_map/ppermute | solution.py:62
  186.7 64.6 %collective-permute-start.23 = (bf16[1408,1024]{1,0:T(8,128)(2,1)}, bf16[1408,1024]{1,0:T(8,128)(2,1)}, u32[]{:S(2)}, u32[]{:S(2)}) collective-permute-start(bf16[1408,1024]{1,0:T(8,128)(2,1)} %convolution_convert_fusion.6), channel_id=1, source_target_pairs={{0,4},{2,6},{4,0},{6,2},{1,5},{3,7},{5,1},{7,3},{8,12},{10,14},{12... | collective-permute-start | bytes 8650760 | tf_op jit(solution)/shard_map/ppermute | solution.py:61
  255.2 32.8 %collective-permute-start.24 = (bf16[704,1024]{1,0:T(8,128)(2,1)}, bf16[704,1024]{1,0:T(8,128)(2,1)}, u32[]{:S(2)}, u32[]{:S(2)}) collective-permute-start(bf16[704,1024]{1,0:T(8,128)(2,1)} %get-tuple-element.579), channel_id=1, source_target_pairs={{0,1},{1,0},{2,3},{3,2},{4,5},{5,4},{6,7},{7,6},{8,9},{9,8},{10,11... | collective-permute-start | bytes 4325384 | tf_op jit(solution)/shard_map/ppermute | solution.py:62
  256.1 32.9 %collective-permute-start.22 = (bf16[704,1024]{1,0:T(8,128)(2,1)}, bf16[704,1024]{1,0:T(8,128)(2,1)}, u32[]{:S(2)}, u32[]{:S(2)}) collective-permute-start(bf16[704,1024]{1,0:T(8,128)(2,1)} %get-tuple-element.575), channel_id=1, source_target_pairs={{0,4},{2,6},{4,0},{6,2},{1,5},{3,7},{5,1},{7,3},{8,12},{10,14},{12... | collective-permute-start | bytes 4325384 | tf_op jit(solution)/shard_map/ppermute | solution.py:61
  298.4 49.5 %collective-permute-start.29 = (bf16[352,2048]{1,0:T(8,128)(2,1)S(1)}, bf16[352,2048]{1,0:T(8,128)(2,1)S(1)}, u32[]{:S(2)}, u32[]{:S(2)}) collective-permute-start(bf16[352,2048]{1,0:T(8,128)(2,1)S(1)} %get-tuple-element.599), channel_id=1, source_target_pairs={{0,8},{24,16},{1,9},{25,17},{2,10},{26,18},{3,11},{27,19},{4,12},{... | collective-permute-start | bytes 4325384 | tf_op jit(solution)/shard_map/ppermute | solution.py:197
  310.0 40.3 %collective-permute-start.28 = (bf16[1,2,704,512]{3,2,1,0:T(8,128)(2,1)S(1)}, bf16[1,2,704,512]{3,2,1,0:T(8,128)(2,1)S(1)}, u32[]{:S(2)}, u32[]{:S(2)}) collective-permute-start(bf16[1,2,704,512]{3,2,1,0:T(8,128)(2,1)S(1)} %pad_maximum_fusion.4), channel_id=1, source_target_pairs={{0,4},{2,6},{4,0},{6,2},{1,5},{3,7},{5,1},{7,3},{8,12},{10,14},{12... | collective-permute-start | bytes 4325384 | tf_op jit(solution)/shard_map/ppermute | solution.py:61
  311.3 45.2 %collective-permute-start.27 = (bf16[2,1,704,512]{3,2,1,0:T(8,128)(2,1)S(1)}, bf16[2,1,704,512]{3,2,1,0:T(8,128)(2,1)S(1)}, u32[]{:S(2)}, u32[]{:S(2)}) collective-permute-start(bf16[2,1,704,512]{3,2,1,0:T(8,128)(2,1)S(1)} %pad_maximum_fusion.3), channel_id=1, source_target_pairs={{0,1},{1,0},{2,3},{3,2},{4,5},{5,4},{6,7},{7,6},{8,9},{9,8},{10,11... | collective-permute-start | bytes 4325384 | tf_op jit(solution)/shard_map/ppermute | solution.py:62
  312.4 29.1 %collective-permute-start.30 = (f32[2,1024]{1,0:T(2,128)S(1)}, f32[2,1024]{1,0:T(2,128)S(1)}, u32[]{:S(2)}, u32[]{:S(2)}) collective-permute-start(f32[2,1024]{1,0:T(2,128)S(1)} %pad_maximum_fusion.17), channel_id=1, source_target_pairs={{0,1},{1,0},{2,3},{3,2},{4,5},{5,4},{6,7},{7,6},{8,9},{9,8},{10,11... | collective-permute-start | bytes 24584 | tf_op jit(solution)/shard_map/ppermute | solution.py:62
  348.5 38.6 %collective-permute-start.38 = (bf16[352,2048]{1,0:T(8,128)(2,1)S(1)}, bf16[352,2048]{1,0:T(8,128)(2,1)}, u32[]{:S(2)}, u32[]{:S(2)}) collective-permute-start(bf16[352,2048]{1,0:T(8,128)(2,1)S(1)} %reduce-precision_convert_fusion.11), channel_id=1, source_target_pairs={{8,16},{16,8},{9,17},{17,9},{10,18},{18,10},{11,19},{19,11},{12,20... | collective-permute-start | bytes 4325384 | tf_op jit(solution)/shard_map/ppermute | solution.py:203
  350.3 36.8 %collective-permute-start.37 = (bf16[352,2048]{1,0:T(8,128)(2,1)S(1)}, bf16[352,2048]{1,0:T(8,128)(2,1)}, u32[]{:S(2)}, u32[]{:S(2)}) collective-permute-start(bf16[352,2048]{1,0:T(8,128)(2,1)S(1)} %get-tuple-element.621), channel_id=1, source_target_pairs={{0,8},{24,16},{1,9},{25,17},{2,10},{26,18},{3,11},{27,19},{4,12},{... | collective-permute-start | bytes 4325384 | tf_op jit(solution)/shard_map/ppermute | solution.py:197
  365.9 35.4 %collective-permute-start.35 = (bf16[2,1,704,512]{3,2,1,0:T(8,128)(2,1)}, bf16[2,1,704,512]{3,2,1,0:T(8,128)(2,1)}, u32[]{:S(2)}, u32[]{:S(2)}) collective-permute-start(bf16[2,1,704,512]{3,2,1,0:T(8,128)(2,1)} %pad_maximum_fusion.5), channel_id=1, source_target_pairs={{0,1},{1,0},{2,3},{3,2},{4,5},{5,4},{6,7},{7,6},{8,9},{9,8},{10,11... | collective-permute-start | bytes 4325384 | tf_op jit(solution)/shard_map/ppermute | solution.py:62
  368.3 32.9 %collective-permute-start.36 = (bf16[1,2,704,512]{3,2,1,0:T(8,128)(2,1)}, bf16[1,2,704,512]{3,2,1,0:T(8,128)(2,1)}, u32[]{:S(2)}, u32[]{:S(2)}) collective-permute-start(bf16[1,2,704,512]{3,2,1,0:T(8,128)(2,1)} %pad_maximum_fusion.6), channel_id=1, source_target_pairs={{0,4},{2,6},{4,0},{6,2},{1,5},{3,7},{5,1},{7,3},{8,12},{10,14},{12... | collective-permute-start | bytes 4325384 | tf_op jit(solution)/shard_map/ppermute | solution.py:61
  411.2 40.3 %collective-permute-start.46 = (bf16[352,2048]{1,0:T(8,128)(2,1)S(1)}, bf16[352,2048]{1,0:T(8,128)(2,1)S(1)}, u32[]{:S(2)}, u32[]{:S(2)}) collective-permute-start(bf16[352,2048]{1,0:T(8,128)(2,1)S(1)} %reduce-precision_convert_fusion.10), channel_id=1, source_target_pairs={{8,16},{16,8},{9,17},{17,9},{10,18},{18,10},{11,19},{19,11},{12,20... | collective-permute-start | bytes 4325384 | tf_op jit(solution)/shard_map/ppermute | solution.py:203
  414.1 37.3 %collective-permute-start.45 = (bf16[352,2048]{1,0:T(8,128)(2,1)S(1)}, bf16[352,2048]{1,0:T(8,128)(2,1)S(1)}, u32[]{:S(2)}, u32[]{:S(2)}) collective-permute-start(bf16[352,2048]{1,0:T(8,128)(2,1)S(1)} %reduce-precision_convert_fusion.9), channel_id=1, source_target_pairs={{8,0},{16,24},{9,1},{17,25},{10,2},{18,26},{11,3},{19,27},{12,4},{... | collective-permute-start | bytes 4325384 | tf_op jit(solution)/shard_map/ppermute | solution.py:200
  415.4 37.3 %collective-permute-start.44 = (bf16[256,2816]{1,0:T(8,128)(2,1)S(1)}, bf16[256,2816]{1,0:T(8,128)(2,1)S(1)}, u32[]{:S(2)}, u32[]{:S(2)}) collective-permute-start(bf16[256,2816]{1,0:T(8,128)(2,1)S(1)} %get-tuple-element.647), channel_id=1, source_target_pairs={{0,8},{24,16},{1,9},{25,17},{2,10},{26,18},{3,11},{27,19},{4,12},{... | collective-permute-start | bytes 4325384 | tf_op jit(solution)/shard_map/ppermute | solution.py:197
  432.3 33.8 %collective-permute-start.42 = (bf16[2,1,256,512]{3,2,1,0:T(8,128)(2,1)S(1)}, bf16[2,1,256,512]{3,2,1,0:T(8,128)(2,1)S(1)}, u32[]{:S(2)}, u32[]{:S(2)}) collective-permute-start(bf16[2,1,256,512]{3,2,1,0:T(8,128)(2,1)S(1)} %pad_maximum_fusion.8), channel_id=1, source_target_pairs={{0,1},{1,0},{2,3},{3,2},{4,5},{5,4},{6,7},{7,6},{8,9},{9,8},{10,11... | collective-permute-start | bytes 1572872 | tf_op jit(solution)/shard_map/ppermute | solution.py:62
  471.2 39.4 %collective-permute-start.52 = (bf16[256,2816]{1,0:T(8,128)(2,1)S(1)}, bf16[256,2816]{1,0:T(8,128)(2,1)S(1)}, u32[]{:S(2)}, u32[]{:S(2)}) collective-permute-start(bf16[256,2816]{1,0:T(8,128)(2,1)S(1)} %copy-done.86), channel_id=1, source_target_pairs={{8,16},{16,8},{9,17},{17,9},{10,18},{18,10},{11,19},{19,11},{12,20... | collective-permute-start | bytes 4325384 | tf_op jit(solution)/shard_map/ppermute | solution.py:203
  472.7 37.8 %collective-permute-start.51 = (bf16[352,2048]{1,0:T(8,128)(2,1)S(1)}, bf16[352,2048]{1,0:T(8,128)(2,1)S(1)}, u32[]{:S(2)}, u32[]{:S(2)}) collective-permute-start(bf16[352,2048]{1,0:T(8,128)(2,1)S(1)} %reduce-precision_convert_fusion.7), channel_id=1, source_target_pairs={{8,0},{16,24},{9,1},{17,25},{10,2},{18,26},{11,3},{19,27},{12,4},{... | collective-permute-start | bytes 4325384 | tf_op jit(solution)/shard_map/ppermute | solution.py:200
  474.0 37.8 %collective-permute-start.50 = (bf16[256,2816]{1,0:T(8,128)(2,1)S(1)}, bf16[256,2816]{1,0:T(8,128)(2,1)S(1)}, u32[]{:S(2)}, u32[]{:S(2)}) collective-permute-start(bf16[256,2816]{1,0:T(8,128)(2,1)S(1)} %copy-done.83), channel_id=1, source_target_pairs={{0,8},{24,16},{1,9},{25,17},{2,10},{26,18},{3,11},{27,19},{4,12},{... | collective-permute-start | bytes 4325384 | tf_op jit(solution)/shard_map/ppermute | solution.py:197
  512.4 33.7 %collective-permute-start.55 = (bf16[256,2816]{1,0:T(8,128)(2,1)S(1)}, bf16[256,2816]{1,0:T(8,128)(2,1)S(1)}, u32[]{:S(2)}, u32[]{:S(2)}) collective-permute-start(bf16[256,2816]{1,0:T(8,128)(2,1)S(1)} %fusion.5), channel_id=1, source_target_pairs={{0,8},{8,0},{16,24},{24,16},{1,9},{9,1},{17,25},{25,17},{2,10},{10... | collective-permute-start | bytes 4325384 | tf_op jit(solution)/shard_map/ppermute | solution.py:192
  516.4 29.7 %collective-permute-start.56 = (bf16[256,2816]{1,0:T(8,128)(2,1)}, bf16[256,2816]{1,0:T(8,128)(2,1)}, u32[]{:S(2)}, u32[]{:S(2)}) collective-permute-start(bf16[256,2816]{1,0:T(8,128)(2,1)} %reduce-precision_convert_fusion.6), channel_id=1, source_target_pairs={{8,16},{16,8},{9,17},{17,9},{10,18},{18,10},{11,19},{19,11},{12,20... | collective-permute-start | bytes 4325384 | tf_op jit(solution)/shard_map/ppermute | solution.py:203
  524.5 43.1 %collective-permute-start.53 = (bf16[2,1,768,512]{3,2,1,0:T(8,128)(2,1)S(1)}, bf16[2,1,768,512]{3,2,1,0:T(8,128)(2,1)}, u32[]{:S(2)}, u32[]{:S(2)}) collective-permute-start(bf16[2,1,768,512]{3,2,1,0:T(8,128)(2,1)S(1)} %pad_maximum_fusion.1), channel_id=1, source_target_pairs={{0,1},{1,0},{2,3},{3,2},{4,5},{5,4},{6,7},{7,6},{8,9},{9,8},{10,11... | collective-permute-start | bytes 4718600 | tf_op jit(solution)/shard_map/ppermute | solution.py:62
  526.3 41.3 %collective-permute-start.54 = (bf16[1,2,768,512]{3,2,1,0:T(8,128)(2,1)S(1)}, bf16[1,2,768,512]{3,2,1,0:T(8,128)(2,1)}, u32[]{:S(2)}, u32[]{:S(2)}) collective-permute-start(bf16[1,2,768,512]{3,2,1,0:T(8,128)(2,1)S(1)} %pad_maximum_fusion.2), channel_id=1, source_target_pairs={{0,4},{2,6},{4,0},{6,2},{1,5},{3,7},{5,1},{7,3},{8,12},{10,14},{12... | collective-permute-start | bytes 4718600 | tf_op jit(solution)/shard_map/ppermute | solution.py:61
  547.7 42.0 %collective-permute-start.58 = (bf16[256,2816]{1,0:T(8,128)(2,1)}, bf16[256,2816]{1,0:T(8,128)(2,1)}, u32[]{:S(2)}, u32[]{:S(2)}) collective-permute-start(bf16[256,2816]{1,0:T(8,128)(2,1)} %reduce-precision_convert_fusion.4), channel_id=1, source_target_pairs={{8,16},{16,8},{9,17},{17,9},{10,18},{18,10},{11,19},{19,11},{12,20... | collective-permute-start | bytes 4325384 | tf_op jit(solution)/shard_map/ppermute | solution.py:203
  552.9 36.8 %collective-permute-start.57 = (bf16[256,2816]{1,0:T(8,128)(2,1)}, bf16[256,2816]{1,0:T(8,128)(2,1)S(1)}, u32[]{:S(2)}, u32[]{:S(2)}) collective-permute-start(bf16[256,2816]{1,0:T(8,128)(2,1)} %fusion.6), channel_id=1, source_target_pairs={{0,8},{8,0},{16,24},{24,16},{1,9},{9,1},{17,25},{25,17},{2,10},{10... | collective-permute-start | bytes 4325384 | tf_op jit(solution)/shard_map/ppermute | solution.py:192
  595.2 125.8 %collective-permute-start.72 = (bf16[256,2816]{1,0:T(8,128)(2,1)}, bf16[256,2816]{1,0:T(8,128)(2,1)}, u32[]{:S(2)}, u32[]{:S(2)}) collective-permute-start(bf16[256,2816]{1,0:T(8,128)(2,1)} %broadcast_select_fusion.6), channel_id=1, source_target_pairs={{0,2},{2,0},{4,6},{6,4},{1,3},{3,1},{5,7},{7,5},{8,10},{10,8},{12,... | collective-permute-start | bytes 4325384 | tf_op jit(solution)/shard_map/ppermute | solution.py:57
  601.6 115.7 %collective-permute-start.61 = (bf16[256,2816]{1,0:T(8,128)(2,1)}, bf16[256,2816]{1,0:T(8,128)(2,1)}, u32[]{:S(2)}, u32[]{:S(2)}) collective-permute-start(bf16[256,2816]{1,0:T(8,128)(2,1)} %reduce-precision_convert_fusion.1), channel_id=1, source_target_pairs={{8,16},{16,8},{9,17},{17,9},{10,18},{18,10},{11,19},{19,11},{12,20... | collective-permute-start | bytes 4325384 | tf_op jit(solution)/shard_map/ppermute | solution.py:203
  603.4 112.6 %collective-permute-start.59 = (bf16[128,3072]{1,0:T(8,128)(2,1)}, bf16[128,3072]{1,0:T(8,128)(2,1)}, u32[]{:S(2)}, u32[]{:S(2)}) collective-permute-start(bf16[128,3072]{1,0:T(8,128)(2,1)} %get-tuple-element.743), channel_id=1, source_target_pairs={{0,8},{24,16},{1,9},{25,17},{2,10},{26,18},{3,11},{27,19},{4,12},{... | collective-permute-start | bytes 2359304 | tf_op jit(solution)/shard_map/ppermute | solution.py:197
  609.7 107.6 %collective-permute-start.60 = (bf16[256,2816]{1,0:T(8,128)(2,1)}, bf16[256,2816]{1,0:T(8,128)(2,1)}, u32[]{:S(2)}, u32[]{:S(2)}) collective-permute-start(bf16[256,2816]{1,0:T(8,128)(2,1)} %reduce-precision_convert_fusion.2), channel_id=1, source_target_pairs={{8,0},{16,24},{9,1},{17,25},{10,2},{18,26},{11,3},{19,27},{12,4},{... | collective-permute-start | bytes 4325384 | tf_op jit(solution)/shard_map/ppermute | solution.py:200
  627.9 84.8 %all-to-all-start.1 = ((f32[8,256,128]{2,1,0:T(8,128)}), f32[8,256,128]{2,1,0:T(8,128)}, u32[]{:S(2)}, u32[]{:S(2)}) async-start(f32[8,256,128]{2,1,0:T(8,128)} %bitcast.82), calls=%async_computation.2 | async-start | bytes 2097152 | tf_op jit(solution)/shard_map/all_to_all | solution.py:955
  717.3 55.4 %collective-permute-start.67 = (bf16[64,3072]{1,0:T(8,128)(2,1)}, bf16[64,3072]{1,0:T(8,128)(2,1)S(1)}, u32[]{:S(2)}, u32[]{:S(2)}) collective-permute-start(bf16[64,3072]{1,0:T(8,128)(2,1)} %get-tuple-element.756), channel_id=1, source_target_pairs={{0,8},{24,16},{1,9},{25,17},{2,10},{26,18},{3,11},{27,19},{4,12},{... | collective-permute-start | bytes 1179656 | tf_op jit(solution)/shard_map/ppermute | solution.py:197
  720.2 52.5 %collective-permute-start.69 = (bf16[128,3072]{1,0:T(8,128)(2,1)S(1)}, bf16[128,3072]{1,0:T(8,128)(2,1)S(1)}, u32[]{:S(2)}, u32[]{:S(2)}) collective-permute-start(bf16[128,3072]{1,0:T(8,128)(2,1)S(1)} %reduce-precision_convert_fusion.17), channel_id=1, source_target_pairs={{8,16},{16,8},{9,17},{17,9},{10,18},{18,10},{11,19},{19,11},{12,20... | collective-permute-start | bytes 2359304 | tf_op jit(solution)/shard_map/ppermute | solution.py:203
  748.2 46.3 %collective-permute-start.68 = (bf16[256,2816]{1,0:T(8,128)(2,1)S(1)}, bf16[256,2816]{1,0:T(8,128)(2,1)S(1)}, u32[]{:S(2)}, u32[]{:S(2)}) collective-permute-start(bf16[256,2816]{1,0:T(8,128)(2,1)S(1)} %reduce-precision_convert_fusion), channel_id=1, source_target_pairs={{8,0},{16,24},{9,1},{17,25},{10,2},{18,26},{11,3},{19,27},{12,4},{... | collective-permute-start | bytes 4325384 | tf_op jit(solution)/shard_map/ppermute | solution.py:200
  749.5 67.6 %collective-permute-start.82 = (bf16[256,2816]{1,0:T(8,128)(2,1)}, bf16[256,2816]{1,0:T(8,128)(2,1)S(1)}, u32[]{:S(2)}, u32[]{:S(2)}) collective-permute-start(bf16[256,2816]{1,0:T(8,128)(2,1)} %broadcast_select_fusion.4), channel_id=1, source_target_pairs={{0,2},{2,0},{4,6},{6,4},{1,3},{3,1},{5,7},{7,5},{8,10},{10,8},{12,... | collective-permute-start | bytes 4325384 | tf_op jit(solution)/shard_map/ppermute | solution.py:57
  770.1 80.8 %collective-permute-start.78 = (bf16[64,3072]{1,0:T(8,128)(2,1)}, bf16[64,3072]{1,0:T(8,128)(2,1)}, u32[]{:S(2)}, u32[]{:S(2)}) collective-permute-start(bf16[64,3072]{1,0:T(8,128)(2,1)} %reduce-precision_convert_fusion.24), channel_id=1, source_target_pairs={{8,16},{16,8},{9,17},{17,9},{10,18},{18,10},{11,19},{19,11},{12,20... | collective-permute-start | bytes 1179656 | tf_op jit(solution)/shard_map/ppermute | solution.py:203
  797.5 39.6 %collective-permute-start.81 = (bf16[64,3072]{1,0:T(8,128)(2,1)}, bf16[64,3072]{1,0:T(8,128)(2,1)}, u32[]{:S(2)}, u32[]{:S(2)}) collective-permute-start(bf16[64,3072]{1,0:T(8,128)(2,1)} %reduce-precision_convert_fusion.25), channel_id=1, source_target_pairs={{8,16},{16,8},{9,17},{17,9},{10,18},{18,10},{11,19},{19,11},{12,20... | collective-permute-start | bytes 1179656 | tf_op jit(solution)/shard_map/ppermute | solution.py:203
  805.1 30.0 %all-to-all-start.2 = ((bf16[8,256,128]{2,1,0:T(8,128)(2,1)}), bf16[8,256,128]{2,1,0:T(8,128)(2,1)}, u32[]{:S(2)}, u32[]{:S(2)}) async-start(bf16[8,256,128]{2,1,0:T(8,128)(2,1)} %bitcast.212), calls=%async_computation.3 | async-start | bytes 1048576 | tf_op jit(solution)/shard_map/all_to_all | solution.py:955
  809.2 29.4 %collective-permute-start.79 = (bf16[64,3072]{1,0:T(8,128)(2,1)}, bf16[64,3072]{1,0:T(8,128)(2,1)}, u32[]{:S(2)}, u32[]{:S(2)}) collective-permute-start(bf16[64,3072]{1,0:T(8,128)(2,1)} %get-tuple-element.790), channel_id=1, source_target_pairs={{0,8},{24,16},{1,9},{25,17},{2,10},{26,18},{3,11},{27,19},{4,12},{... | collective-permute-start | bytes 1179656 | tf_op jit(solution)/shard_map/ppermute | solution.py:197
  817.1 33.8 %collective-permute-start.76 = (bf16[64,3072]{1,0:T(8,128)(2,1)}, bf16[64,3072]{1,0:T(8,128)(2,1)}, u32[]{:S(2)}, u32[]{:S(2)}) collective-permute-start(bf16[64,3072]{1,0:T(8,128)(2,1)} %get-tuple-element.801), channel_id=1, source_target_pairs={{0,8},{24,16},{1,9},{25,17},{2,10},{26,18},{3,11},{27,19},{4,12},{... | collective-permute-start | bytes 1179656 | tf_op jit(solution)/shard_map/ppermute | solution.py:197
  841.2 32.3 %collective-permute-start.86 = (bf16[64,3072]{1,0:T(8,128)(2,1)S(1)}, bf16[64,3072]{1,0:T(8,128)(2,1)S(1)}, u32[]{:S(2)}, u32[]{:S(2)}) collective-permute-start(bf16[64,3072]{1,0:T(8,128)(2,1)S(1)} %reduce-precision_convert_fusion.23), channel_id=1, source_target_pairs={{8,16},{16,8},{9,17},{17,9},{10,18},{18,10},{11,19},{19,11},{12,20... | collective-permute-start | bytes 1179656 | tf_op jit(solution)/shard_map/ppermute | solution.py:203
  843.2 30.4 %collective-permute-start.85 = (bf16[64,3072]{1,0:T(8,128)(2,1)S(1)}, bf16[64,3072]{1,0:T(8,128)(2,1)S(1)}, u32[]{:S(2)}, u32[]{:S(2)}) collective-permute-start(bf16[64,3072]{1,0:T(8,128)(2,1)S(1)} %reduce-precision_convert_fusion.20), channel_id=1, source_target_pairs={{8,0},{16,24},{9,1},{17,25},{10,2},{18,26},{11,3},{19,27},{12,4},{... | collective-permute-start | bytes 1179656 | tf_op jit(solution)/shard_map/ppermute | solution.py:200
  (175 other events, 1361.8 us)
Sparse Core Ops, SparseCore 0:
  122.2 45.9 all-gather.4
  469.0 59.4 reduce-scatter.1

commit v8 on v7

--- a/solution.py
+++ b/solution.py
@@ -293,20 +293,81 @@
     )(place, mine, got, mine, got)
 
 
-def lanes_kernel(a_ref, b_ref, out_ref):
-    out_ref[...] = jnp.concatenate([a_ref[...], b_ref[...]], axis=1)
-
-
-def side_by_side(a, b):
+def product_kernel(dims, a_ref, b_ref, *refs):
+    p = dot(a_ref[...], b_ref[...], dims)
+    if len(refs) == 2:
+        p = p + refs[0][...]
+    refs[-1][...] = p.astype(refs[-1].dtype)
+
+
+def mm(a, b, dims, dtype, tm=None, tn=None, add=None):
+    (ca,), (cb,) = dims[0]
+    m, k, n = a.shape[1 - ca], a.shape[ca], b.shape[1 - cb]
+    tm, tn = tm or m, tn or n
+    a_block = [0, 0]
+    a_block[ca], a_block[1 - ca] = k, tm
+    b_block = [0, 0]
+    b_block[cb], b_block[1 - cb] = k, tn
+    out = pl.BlockSpec((tm, tn), lambda i, j: (i, j))
+    return pl.pallas_call(
+        functools.partial(product_kernel, dims),
+        grid=(m // tm, n // tn),
+        in_specs=[
+            pl.BlockSpec(tuple(a_block), (lambda i, j: (0, i)) if ca == 0 else (lambda i, j: (i, 0))),
+            pl.BlockSpec(tuple(b_block), (lambda i, j: (0, j)) if cb == 0 else (lambda i, j: (j, 0))),
+        ]
+        + ([] if add is None else [out]),
+        out_specs=out,
+        out_shape=jax.ShapeDtypeStruct((m, n), dtype),
+        compiler_params=pltpu.CompilerParams(vmem_limit_bytes=48 * 1024 * 1024),
+        cost_estimate=SMALL,
+    )(*((a, b) if add is None else (a, b, add)))
+
+
+def last_step_kernel(bits_ref, own0_ref, got0_ref, own1_ref, got1_ref, out_ref):
+    y, s = pl.program_id(1), pl.program_id(2)
+    half = own0_ref.shape[3]
+    ys, ss = bits_ref[2], bits_ref[3]
+    a = jnp.where(s // ss == bits_ref[1], own0_ref[0, 0], got0_ref[0, 0])
+    b = jnp.where(y // ys == bits_ref[0], own1_ref[0, 0], got1_ref[0, 0])
+    out_ref[0, 0, 0, :, :half] = a
+    out_ref[0, 0, 0, :, half:] = b
+
+
+def last_step(parts, got, bits, pre, y_size, s_size):
+    rows, half = parts[0].shape[2] // pre, parts[0].shape[3]
+    along_s = pl.BlockSpec((1, 1, rows, half), lambda p, y, s, bits: (y, s % (s_size // 2), p, 0))
+    along_y = pl.BlockSpec((1, 1, rows, half), lambda p, y, s, bits: (y % (y_size // 2), s, p, 0))
+    return pl.pallas_call(
+        last_step_kernel,
+        grid_spec=pltpu.PrefetchScalarGridSpec(
+            num_scalar_prefetch=1,
+            grid=(pre, y_size, s_size),
+            in_specs=[along_s, along_s, along_y, along_y],
+            out_specs=pl.BlockSpec((1, 1, 1, rows, 2 * half), lambda p, y, s, bits: (p, y, s, 0, 0)),
+        ),
+        out_shape=jax.ShapeDtypeStruct((pre, y_size, s_size, rows, 2 * half), bf16),
+        compiler_params=pltpu.CompilerParams(vmem_limit_bytes=48 * 1024 * 1024),
+        cost_estimate=SMALL,
+    )(bits, parts[0], got[0], parts[1], got[1])
+
+
+def stack_turned_kernel(a_ref, b_ref, out_ref):
+    r = a_ref.shape[1]
+    out_ref[:r] = a_ref[...].T
+    out_ref[r:] = b_ref[...].T
+
+
+def stack_turned(a, b):
     rows, width = a.shape
-    n = max(n for n in (1, 2, 4, 8) if rows % (16 * n) == 0)
+    n = max(n for n in (1, 2, 4, 6, 8, 11) if rows % (128 * n) == 0)
     spec = pl.BlockSpec((rows // n, width), lambda i: (i, 0))
     return pl.pallas_call(
-        lanes_kernel,
+        stack_turned_kernel,
         grid=(n,),
         in_specs=[spec, spec],
-        out_specs=pl.BlockSpec((rows // n, 2 * width), lambda i: (i, 0)),
-        out_shape=jax.ShapeDtypeStruct((rows, 2 * width), bf16),
+        out_specs=pl.BlockSpec((2 * width, rows // n), lambda i: (0, i)),
+        out_shape=jax.ShapeDtypeStruct((2 * width, rows), bf16),
         compiler_params=pltpu.CompilerParams(vmem_limit_bytes=48 * 1024 * 1024),
         cost_estimate=SMALL,
     )(a, b)
@@ -618,14 +679,14 @@
 
     table = do(positions, place)
     flying = scatter_rest(flying)
-    wg_cut = cut_weights(wg_parts, 1, ffb, False)
-    wu_cut = cut_weights(wu_parts, 1, ffb, True)
-
-    def gather_steps(parts, row_axis):
+
+    def gather_steps(parts, pre):
         n = len(at.steps(False))
         state = {"parts": list(parts)}
 
-        def start(i):
+        def start(i, after=None):
+            if after is not None:
+                state["parts"], _ = lax.optimization_barrier((state["parts"], after))
             state["got"] = []
             state["at"] = []
             for k in range(2):
@@ -647,9 +708,24 @@
             state["parts"] = do(put, state["parts"], state["got"])
 
         def result():
-            return jnp.concatenate(state["parts"], axis=row_axis)
+            ys, ss = Y // 2, S // 2
+            bits = jnp.stack([at.y // ys, at.s // ss, jnp.int32(ys), jnp.int32(ss)]).astype(jnp.int32)
+            return do(lambda p, g: last_step(p, g, bits, pre, Y, S), state["parts"], state["got"])
 
         return n, start, finish, result
+
+    qkvs, attns, attn_got, stats = [], [], [], []
+    for k in range(2):
+        shape = (3, heads, HEAD_DIM, H)
+        qkv, attn, stat = do(attend, flying[k][0].reshape(shape), flying[k][1].reshape(shape), bias, table[seqs[k]])
+        qkvs.append(qkv)
+        attns.append(attn.reshape(blk, H))
+        attn_got.append(at.core(attns[k]))
+        stats.append(stat)
+    pairs = [do(join, attns[k], attn_got[k]) for k in range(2)]
+    flying = send_products(wo_cut, pairs)
+    wg_cut = cut_weights(wg_parts, 1, ffb, False)
+    wu_cut = cut_weights(wu_parts, 1, ffb, True)
 
     def gain_products(wg, wu, cols):
         terms = []
@@ -674,27 +750,7 @@
         kept = lax.dynamic_slice_in_dim(gains, bit * step, step, ax)
         return kept, at.along(send, axis, step)
 
-    gains = gain_step(gains)
-
-    qkvs, attns, attn_got, stats = [], [], [], []
-    for k in range(2):
-        shape = (3, heads, HEAD_DIM, H)
-        qkv, attn, stat = do(attend, flying[k][0].reshape(shape), flying[k][1].reshape(shape), bias, table[seqs[k]])
-        qkvs.append(qkv)
-        attns.append(attn.reshape(blk, H))
-        attn_got.append(at.core(attns[k]))
-        stats.append(stat)
-        gains = do(lambda a, b: a + b, *gains)
-        if gain_steps:
-            gains = gain_step(gains)
-        else:
-            gains = (gains, jnp.zeros_like(gains))
-    while gain_steps:
-        gains = gain_step(do(lambda a, b: a + b, *gains))
-    gains = do(lambda a, b: (a + b).reshape(4, ffb, 1), *gains)
-
-    pairs = [do(join, attns[k], attn_got[k]) for k in range(2)]
-    flying = scatter_rest(send_products(wo_cut, pairs))
+    flying = scatter_rest(flying)
     def residual(x, a0, b0, a1, b1):
         a, b = lanes(a0, a1), lanes(b0, b1)
         hidden = x.astype(f32) + (a.astype(f32) + b.astype(f32))
@@ -719,18 +775,23 @@
         z2 = (hidden - moments[0:1]) * inv2
         return (z2 * cols[:, 2:3] + cols[:, 3:4]).astype(bf16), z2, inv2
 
+    gains = gain_step(gains)
     xn2_own, z2, inv2 = do(second_norm, hidden, moments, own_cols)
     xn2 = do(join, xn2_own, at.core(xn2_own))
 
     flying = send_products([wg_cut, wu_cut], [xn2, xn2])
 
     wd_own = do(cast, w_down)
-    grad_act = do(lambda w, c: dot(w, c, LAST), wd_own, cot_all)
+    wg = do(stack_turned, *wg_parts)
+    wu = do(stack_turned, *wu_parts)
+    grad_act = do(lambda w, c: mm(w, c, LAST, f32, tn=256), wd_own, cot_all)
     cot_cols = do(lambda c: lax.dynamic_slice_in_dim(c, my_block * blk, blk, 1).T, cot_all)
     wo_own = do(cast, w_out)
-    wg = do(side_by_side, *wg_parts)
-    wu = do(side_by_side, *wu_parts)
-    wq = do(side_by_side, *wq_parts)
+    wq = do(stack_turned, *wq_parts)
+    gains = do(lambda a, b: a + b, *gains)
+    while gain_steps:
+        gains = do(lambda a, b: a + b, *gain_step(gains))
+    gains = do(lambda g: g.reshape(4, ffb, 1), gains)
     flying = scatter_rest(flying)
 
     def gated(ga, gb, ua, ub, grad_act, gains):
@@ -751,8 +812,7 @@
         n = parts_of(count, want)
         return [(k * (count // n), count // n) for k in range(n)]
 
-    down_rows, up_rows, out_rows = even(ffb, 2), [(0, blk)], [(0, blk)]
-    qkv_rows = [(0, blk // 2), (blk // 2, blk // 4), (3 * blk // 4, blk // 4)]
+    down_rows, up_rows = even(ffb, 2), [(0, blk)]
 
     def push_pairs(name, g, rows):
         for k, (at_row, count) in enumerate(rows):
@@ -782,10 +842,13 @@
     for name, lead in (("gate", 0), ("up", Y)):
         for k, (at_row, count) in enumerate(up_rows):
             jobs.append(("up", [(name, "mine", k), (name, "theirs", k)], at_row, lead, count, S * ffb))
-    for k, (at_row, count) in enumerate(out_rows):
-        jobs.append(("out", [("out", k)], at_row, 0, count, 1024))
-    for k, (at_row, count) in enumerate(qkv_rows):
-        jobs.append(("qkv", [("qkv", "mine", k), ("qkv", "theirs", k)], at_row, 0, count, S * blk))
+    for k in range(2):
+        jobs.append(("out", [("out", k)], 0, k, blk, width // 2))
+    for third in (2, 1, 0):
+        for k, (at_row, count) in enumerate(up_rows):
+            jobs.append(
+                ("qkv", [(third, "mine", k), (third, "theirs", k)], at_row, third * Y, count, S * blk)
+            )
     received = {}
 
     def update(limit):
@@ -802,12 +865,14 @@
         for _ in range(n):
             reps.tick()
 
+    wide = 2 * FF // 8
+
     def quarter_heads(x):
         return [x[:, h][None, None] for h in halves]
 
-    n, start, finish, gate_all = gather_steps(quarter_heads(ggate), 3)
+    n, start, finish, gate_all = gather_steps(quarter_heads(ggate), 1)
     start(0)
-    g_down = do(lambda a, c: dot(a, c, PLAIN).astype(bf16), act, cot_all)
+    g_down = do(lambda a, c: mm(a, c, PLAIN, bf16, tn=512), act, cot_all)
     for k, (at_row, count) in enumerate(down_rows):
         reps.push(("down", k), g_down[at_row : at_row + count])
     ticks(1)
@@ -828,35 +893,35 @@
         return do(lambda a, b: a + b, sums, sum_send(sums, axis, step))
 
     tiny = list(steps2)
-    sums_got = sum_send(sums, *tiny[0])
+    sums_got = sum_send(sums, *tiny.pop(0))
     for i in range(1, n):
         finish()
         sums = do(lambda a, b: a + b, sums, sums_got)
-        tiny.pop(0)
-        start(i)
-        sums_got = sum_send(sums, *tiny[0])
+        sums_got = sum_send(sums, *tiny.pop(0))
+        start(i, sums)
         ticks(1)
-    n, start_up, finish_up, up_all = gather_steps(quarter_heads(gup), 3)
-    finish()
-    for axis, step in tiny:
-        sums = do(lambda a, b: a + b, sums, sums_got)
-        if (axis, step) != tiny[-1]:
-            sums_got = sum_send(sums, *tiny[tiny.index((axis, step)) + 1])
-    start_up(0)
-    ggate_all = do(lambda x: x.reshape(Y * S * ffb, T), gate_all())
+    n, start_up, finish_up, up_all = gather_steps(quarter_heads(gup), 1)
+    ggate_all = gate_all().reshape(Y * S * ffb, T)
+    sums = do(lambda a, b: a + b, sums, sums_got)
+    start_up(0, sums)
+    while tiny:
+        sums = sum_step(sums, *tiny.pop(0))
+    g_gate = do(lambda x, g: mm(x, g, LAST, bf16, tn=wide), xn2, ggate_all)
+    push_pairs("gate", g_gate, up_rows)
     finish_up()
     for i in range(1, n):
         start_up(i)
         if i == 1:
-            g_gate = do(lambda x, g: dot(x, g, LAST).astype(bf16), xn2, ggate_all)
-            push_pairs("gate", g_gate, up_rows)
-            part_gate = do(lambda w, g: dot(w, g, FIRST), wg, ggate_all)
-            out_part = do(lambda w, a: dot(w, a, FIRST).astype(bf16), wd_own, act)
             ticks(1)
-        finish_up()
-    gup_all = do(lambda x: x.reshape(Y * S * ffb, T), up_all())
-    part = do(lambda w, g, p: dot(w, g, FIRST) + p, wu, gup_all, part_gate)
+            part_gate = do(lambda w, g: mm(w, g, PLAIN, f32, tn=256), wg, ggate_all)
+            out_part = do(lambda w, a: mm(w, a, FIRST, bf16, tm=512), wd_own, act)
+            update(1)
+        if i < n - 1:
+            finish_up()
+    gup_all = up_all().reshape(Y * S * ffb, T)
+    part = do(lambda w, g, p: dot(w, g, PLAIN) + p, wu, gup_all, part_gate)
     part_theirs = at.core(part[blk:])
+    ticks(1)
 
     def branch(a, b, cot, z, scale, gain, sums):
         gxn2 = a + b
@@ -867,17 +932,18 @@
     grad_branch, grad_hidden, gxn2 = do(
         branch, part[:blk], part_theirs, cot_cols, z2, inv2, own_cols[:, 2:3], sums
     )
-    n, start, finish, branch_all = gather_steps(quarter_heads(grad_branch), 3)
+    n, start, finish, branch_all = gather_steps(quarter_heads(grad_branch), 1)
     start(0)
-    g_up = do(lambda x, g: dot(x, g, LAST).astype(bf16), xn2, gup_all)
+    g_up = do(lambda x, g: mm(x, g, LAST, bf16, tn=wide), xn2, gup_all)
     push_pairs("up", g_up, up_rows)
     finish()
     for i in range(1, n):
         start(i)
         if i == 1:
             ticks(1)
-        finish()
-    gbr_c = do(lambda x: x, branch_all())
+        if i < n - 1:
+            finish()
+    gbr_c = branch_all()[0]
     gbr_o = at.core(gbr_c)
     gbr = do(lambda a, b: in_order(a, b, 1).reshape(width, T), gbr_c, gbr_o)
     grad_attn = do(lambda w, g: dot(w, g, PLAIN).astype(bf16), wo_own, gbr)
@@ -889,9 +955,9 @@
     n, start, finish, gqkv_done = gather_steps([g.reshape(1, 1, 3 * blk, H) for g in gqkvs], 3)
     start(0)
     attn = lanes(*attns)
-    g_out = do(lambda a, g: dot(a, g, LAST).astype(bf16), attn, gbr)
-    for k, (at_row, count) in enumerate(out_rows):
-        reps.push(("out", k), g_out[at_row : at_row + count])
+    for k in range(2):
+        g_out = do(lambda a, g: mm(a, g, LAST, bf16, tn=512), attn, gbr[k * width // 2 : (k + 1) * width // 2])
+        reps.push(("out", k), g_out)
     ticks(1)
     finish()
     for i in range(1, n):
@@ -900,15 +966,15 @@
             update(1)
             ticks(1)
             update(1)
-        finish()
-
-    def qkv_columns(x):
-        return x.reshape(Y, S, 3, blk, T).transpose(2, 0, 1, 3, 4).reshape(3 * Y * S * blk, T)
-
-    gqkv = do(qkv_columns, gqkv_done())
-    g_qkv = do(lambda x, g: dot(x, g, LAST).astype(bf16), xn1, gqkv)
-    push_pairs("qkv", g_qkv, qkv_rows)
-    part = do(lambda w, g: dot(w, g, FIRST), wq, gqkv)
+        if i < n - 1:
+            finish()
+    gqkv = gqkv_done().reshape(3, Y * S * blk, T)
+    for third in (2, 1, 0):
+        g = do(lambda x, g: dot(x, g, LAST).astype(bf16), xn1, gqkv[third])
+        push_pairs(third, g, up_rows)
+        if third == 2:
+            ticks(1)
+    part = do(lambda w, g: dot(w, g, PLAIN), wq, gqkv.reshape(3 * Y * S * blk, T))
     part_theirs = at.core(part[blk:])
     out_sum = lax.psum_scatter(out_part, plane, scatter_dimension=0, tiled=True)
     reps.depth = 2
@@ -959,10 +1025,16 @@
     ticks(1)
     update(1)
     ticks(1)
-    everyone = ("rep",) + plane
-    small_all = lax.all_gather(small[None], everyone, axis=0, tiled=True)
+    n_rep = lax.axis_size("rep")
+    step = 1
+    while step < n_rep:
+        other = lax.ppermute(small, "rep", [(i, i ^ step) for i in range(n_rep)])
+        small = do(lambda a, b: a + b, small, other)
+        step *= 2
     update(1)
     ticks(1)
+    sent = do(lambda s: jnp.broadcast_to(s.reshape(1, 7, blk), (nb, 7, blk)), small)
+    small_all = lax.all_to_all(sent, plane, split_axis=0, concat_axis=0, tiled=True)
 
     out_cols = do(lambda h, a: (h + a.astype(f32)).astype(bf16), hidden, out_sum)
     block_output = to_rows(out_cols)
@@ -972,11 +1044,7 @@
     update(1)
 
     def norm_update(every, *a):
-        every = every.reshape(lax.axis_size("rep"), nb, 7, blk)
-        total = every[0]
-        for k in range(1, every.shape[0]):
-            total = total + every[k]
-        return adam_update(*a, total.transpose(1, 0, 2).reshape(7, width), 0.3, 0.0)
+        return adam_update(*a, every.transpose(1, 0, 2).reshape(7, width), 0.3, 0.0)
 
     mn, vn, wn = do(norm_update, small_all, norm_params, m_norm, v_norm)
     while reps.busy():

time: 920 us -> 866 us (0.941)
  blocking collectives: 77.1 us -> 0 us
  Pallas kernels: 140 us -> 190 us
  waiting for transfers between devices: 295 us -> 257 us
  matrix products: 79.1 us -> 47.3 us
  local copies, waits for them, and re-layouts: 73.7 us -> 105 us
    all_gather x1 -> x0, blocking collectives: 77.1 us -> none  [body(): small_all = lax.all_gather(small[None], everyone, axis=0, tiled=True)]
    pallas_call x3 -> x15, Pallas kernels: 11.8 us -> 63.8 us  [the longest x8 35.8 us: mm(): pl.pallas_call(functools.partial(product_kernel, dims), grid=(m // tm, n...]
    ppermute x11 -> x8, waiting for transfers between devices: 83.7 us -> 32.3 us  [tick(): slot['out_got'] = lax.ppermute(out['total'], 'rep', [(1, 0), (2, 3)])]
    ppermute x18, waiting for transfers between devices: 136 us -> 102 us  [along(): return lax.ppermute(x, 'shard', [(i, i ^ step) for i in range(self.s_size)])]
    ppermute x11 -> x8, waiting for transfers between devices: 16.1 us -> 48.4 us  [tick(): slot['in_got'] = lax.ppermute(out['new'], 'rep', [(0, 1), (3, 2)])]
    dot_general x27 -> x22, matrix products: 79.1 us -> 47.3 us  [dot(): return lax.dot_general(a, b, dims, preferred_element_type=f32)]
    unnamed x259 -> x295, local copies, waits for them, and re-layouts: 35.7 us -> 55.5 us
    optimization_barrier x2 -> x4, local copies, waits for them, and re-layouts: 1.08 us -> 14.6 us  [__call__(): args, self.last = lax.optimization_barrier((args, self.last))]
  transfers between devices with their start and end apart: 97 -> 99, of which waited for: 43 -> 39; matrix products, arithmetic and copies ran while one was open for 20% -> 20% of each run, Pallas kernels for 14% -> 21%
where the time goes in v8:
time: 866 us; the launch traced here: 852 us
  waiting for transfers between devices  257 us (30%)
  Pallas kernels  190 us (22%)
  starting transfers between devices  145 us (17%)
  local copies, waits for them, and re-layouts  105 us (12%)
  other arithmetic  91.5 us (11%)
  matrix products  47.3 us (5%)
  between operations  16.8 us (2%)
    ppermute x18, waiting for transfers between devices, along(): return lax.ppermute(x, 'shard', [(i, i ^ step) for i in range(self.s_size)])  102 us
    pallas_call x9, Pallas kernels, adam_part(): pl.pallas_call(functools.partial(adam_kernel, rate, two), grid_spec=pltpu...  67.6 us
    unnamed x295, local copies, waits for them, and re-layouts  55.5 us
    ppermute x8, waiting for transfers between devices, tick(): slot['in_got'] = lax.ppermute(out['new'], 'rep', [(0, 1), (3, 2)])  48.4 us
    dot_general x22, matrix products, dot(): return lax.dot_general(a, b, dims, preferred_element_type=f32)  47.3 us
    ppermute x8, starting transfers between devices, tick(): slot['in_got'] = lax.ppermute(out['new'], 'rep', [(0, 1), (3, 2)])  42.6 us
    pallas_call x8, Pallas kernels, mm(): pl.pallas_call(functools.partial(product_kernel, dims), grid=(m // tm, n...  35.8 us
    ppermute x8, waiting for transfers between devices, tick(): slot['out_got'] = lax.ppermute(out['total'], 'rep', [(1, 0), (2, 3)])  32.3 us
  transfers between devices with their start and end apart: 99, of which 39 were waited for; matrix products, arithmetic and copies ran while one was open for 20% of the time, Pallas kernels for 21%

profile of v8, /device:TPU:0, one launch (start us, length us, event | category | flops | bytes accessed | tf_op | source)
XLA Modules:
  0.0 852.3 jit_solution(11720052775157641553)
XLA Ops:
  71.9 9.5 %collective-permute-done.3.b_ref.d_ref = bf16[1536,512]{1,0:T(8,128)(2,1)} collective-permute-done((bf16[1536,512]{1,0:T(8,128)(2,1)}, bf16[1536,512]{1,0:T(8,128)(2,1)}, u32[]{:S(2)}, u32[]{:S(2)}) %collective-permute-start.3) | collective-permute-done | bytes 1572896 | tf_op jit(solution)/shard_map/ppermute | solution.py:62
  95.8 10.5 %collective-permute-done.4 = bf16[768,512]{1,0:T(8,128)(2,1)} collective-permute-done((bf16[768,512]{1,0:T(8,128)(2,1)}, bf16[768,512]{1,0:T(8,128)(2,1)}, u32[]{:S(2)}, u32[]{:S(2)}) %collective-permute-start.4) | collective-permute-done | bytes 786464 | tf_op jit(solution)/shard_map/ppermute | solution.py:61
  109.1 5.1 shard_map.315
  118.6 5.1 shard_map.316
  146.8 5.8 collective-permute-done.9.b_ref.d_ref
  159.1 12.8 %collective-permute-done.14 = bf16[256,512]{1,0:T(8,128)(2,1)S(1)} collective-permute-done((bf16[256,512]{1,0:T(8,128)(2,1)S(1)}, bf16[256,512]{1,0:T(8,128)(2,1)S(1)}, u32[]{:S(2)}, u32[]{:S(2)}) %collective-permute-start.14) | collective-permute-done | bytes 262176 | tf_op jit(solution)/shard_map/ppermute | solution.py:62
  194.3 5.0 convolution_convert_fusion.1.a_ref.c_ref
  213.7 6.4 copy.103.b_ref
  222.0 5.6 shard_map.324
  233.9 19.8 %collective-permute-done.20 = f32[4,2,1,704]{3,2,1,0:T(1,128)S(1)} collective-permute-done((f32[4,2,1,704]{3,2,1,0:T(1,128)S(1)}, f32[4,2,1,704]{3,2,1,0:T(1,128)S(1)}, u32[]{:S(2)}, u32[]{:S(2)}) %collective-permute-start.20) | collective-permute-done | bytes 22560 | tf_op jit(solution)/shard_map/ppermute | solution.py:62
  269.0 31.0 %collective-permute-done.24 = bf16[704,1024]{1,0:T(8,128)(2,1)S(1)} collective-permute-done((bf16[704,1024]{1,0:T(8,128)(2,1)}, bf16[704,1024]{1,0:T(8,128)(2,1)S(1)}, u32[]{:S(2)}, u32[]{:S(2)}) %collective-permute-start.24) | collective-permute-done | bytes 1441824 | tf_op jit(solution)/shard_map/ppermute | solution.py:62
  301.7 6.7 multiply_convert_fusion
  311.7 6.4 copy.104.b_ref
  319.5 5.5 shard_map.329
  339.6 18.1 %collective-permute-done.30 = bf16[352,2048]{1,0:T(8,128)(2,1)S(1)} collective-permute-done((bf16[352,2048]{1,0:T(8,128)(2,1)S(1)}, bf16[352,2048]{1,0:T(8,128)(2,1)S(1)}, u32[]{:S(2)}, u32[]{:S(2)}) %collective-permute-start.30) | collective-permute-done | bytes 1441824 | tf_op jit(solution)/shard_map/ppermute | solution.py:197
  358.3 7.6 collective-permute-done.28.got0_ref
  373.2 4.9 collective-permute-start.31
  378.2 5.7 shard_map.331
  390.2 19.1 %collective-permute-done.31 = bf16[352,2048]{1,0:T(8,128)(2,1)S(1)} collective-permute-done((bf16[352,2048]{1,0:T(8,128)(2,1)S(1)}, bf16[352,2048]{1,0:T(8,128)(2,1)S(1)}, u32[]{:S(2)}, u32[]{:S(2)}) %collective-permute-start.31) | collective-permute-done | bytes 1441824 | tf_op jit(solution)/shard_map/ppermute | solution.py:197
  416.1 7.4 collective-permute-start.40
  423.6 6.0 shard_map.332
  430.9 5.3 shard_map.333
  436.2 7.4 shard_map.334
  443.6 5.2 convolution_add_fusion.2
  459.8 7.6 collective-permute-start.47
  471.0 5.7 shard_map.335
  481.2 10.4 %collective-permute-done.48 = bf16[352,2048]{1,0:T(8,128)(2,1)S(1)} collective-permute-done((bf16[352,2048]{1,0:T(8,128)(2,1)S(1)}, bf16[352,2048]{1,0:T(8,128)(2,1)S(1)}, u32[]{:S(2)}, u32[]{:S(2)}) %collective-permute-start.48) | collective-permute-done | bytes 1441824 | tf_op jit(solution)/shard_map/ppermute | solution.py:200
  491.6 6.6 collective-permute-done.47
  516.5 5.7 shard_map.337
  522.2 5.5 shard_map.338
  531.0 12.3 %collective-permute-done.53 = bf16[256,2816]{1,0:T(8,128)(2,1)} collective-permute-done((bf16[256,2816]{1,0:T(8,128)(2,1)}, bf16[256,2816]{1,0:T(8,128)(2,1)}, u32[]{:S(2)}, u32[]{:S(2)}) %collective-permute-start.53) | collective-permute-done | bytes 1441824 | tf_op jit(solution)/shard_map/ppermute | solution.py:192
  556.5 11.6 %collective-permute-done.52 = bf16[1,1,768,512]{3,2,1,0:T(8,128)(2,1)S(1)} collective-permute-done((bf16[1,1,768,512]{3,2,1,0:T(8,128)(2,1)S(1)}, bf16[1,1,768,512]{3,2,1,0:T(8,128)(2,1)S(1)}, u32[]{:S(2)}, u32[]{:S(2)}) %collective-permute-start.52) | collective-permute-done | bytes 786464 | tf_op jit(solution)/shard_map/ppermute | solution.py:62
  571.5 7.6 shard_map.341
  587.0 8.1 shard_map.342
  595.1 11.3 %collective-permute-done.56.got1_ref = bf16[1,2,768,512]{3,2,1,0:T(8,128)(2,1)} collective-permute-done((bf16[1,2,768,512]{3,2,1,0:T(8,128)(2,1)S(1)}, bf16[1,2,768,512]{3,2,1,0:T(8,128)(2,1)}, u32[]{:S(2)}, u32[]{:S(2)}) %collective-permute-start.56) | collective-permute-done | bytes 1572896 | tf_op jit(solution)/shard_map/ppermute | solution.py:61
  609.6 9.1 %shard_map.343 = bf16[3,2,2,256,1024]{4,3,2,1,0:T(8,128)(2,1)} custom-call(s32[4]{0:T(128)S(1)} %pad_add_fusion.1.bits_ref, bf16[2,1,768,512]{3,2,1,0:T(8,128)(2,1)S(1)} %pad_maximum_fusion.1.own0_ref, bf16[2,1,768,512]{3,2,1,0:T(8,128)(2,1)S(1)} %collective-permute-done.55.got0_ref, bf16[1,2,768,512]{3,2,1,0:T(8,128)(2,1)S(1)} %pad_maximum_fusion.2.own1_ref, ...), custom_call_target="tpu_custom_call" | custom-call | flops 1024 | bytes 1024 | tf_op jit(solution)/shard_map/pallas_call | solution.py:341
  629.7 6.4 collective-permute-start.63
  642.9 13.1 %shard_map.344 = (f32[256,11264]{1,0:T(8,128)}, f32[256,11264]{1,0:T(8,128)}, f32[256,11264]{1,0:T(8,128)}) custom-call(s32[1]{0:T(128)} %bitcast.8.core_ref, f32[256,11264]{1,0:T(8,128)} %w_ref.9, f32[256,11264]{1,0:T(8,128)} %m_ref.3, f32[256,11264]{1,0:T(8,128)} %v_ref.3, bf16[256,2816]{1,0:T(8,128)(2,1)S(1)} %broadcast_select_fusion.5.refs_0_, ...), custom_call_target="tpu_custom_call" | custom-call | flops 1024 | bytes 1024 | tf_op jit(solution)/shard_map/pallas_call | solution.py:428
  658.8 11.1 %collective-permute-done.64 = bf16[256,2816]{1,0:T(8,128)(2,1)S(1)} collective-permute-done((bf16[256,2816]{1,0:T(8,128)(2,1)S(1)}, bf16[256,2816]{1,0:T(8,128)(2,1)S(1)}, u32[]{:S(2)}, u32[]{:S(2)}) %collective-permute-start.64) | collective-permute-done | bytes 1441824 | tf_op jit(solution)/shard_map/ppermute | solution.py:200
  692.9 7.5 collective-permute-start.72
  719.4 13.1 %shard_map.345 = (f32[256,11264]{1,0:T(8,128)}, f32[256,11264]{1,0:T(8,128)}, f32[256,11264]{1,0:T(8,128)}) custom-call(s32[1]{0:T(128)} %bitcast.8.core_ref, f32[256,11264]{1,0:T(8,128)} %w_ref.9, f32[256,11264]{1,0:T(8,128)} %m_ref.3, f32[256,11264]{1,0:T(8,128)} %v_ref.3, ...), custom_call_target="tpu_custom_call", output_to_operand_aliasing={{0}: (6, {}), {1}: (7, {}), {2}: (8, {})} | custom-call | flops 1024 | bytes 1024 | tf_op jit(solution)/shard_map/pallas_call | solution.py:428
  745.3 5.2 collective-permute-done.77
  758.4 6.4 collective-permute-done.82
  771.4 5.4 collective-permute-start.80
  797.6 6.7 shard_map.348
  818.1 6.2 shard_map.349
  831.9 7.0 collective-permute-done.89
  839.0 6.3 shard_map.350
  (700 shorter events, 417.9 us)
Async XLA Ops:
  24.2 189.5 %all-gather.3.cloned.1.call-start = ((), (), s32[]{:S(2)}) async-start(), calls=%async_computation.6 | async-start | bytes 4718592 | tf_op jit(solution)/shard_map/all_gather | solution.py:608
  44.7 36.7 %collective-permute-start.3 = (bf16[1536,512]{1,0:T(8,128)(2,1)}, bf16[1536,512]{1,0:T(8,128)(2,1)}, u32[]{:S(2)}, u32[]{:S(2)}) collective-permute-start(bf16[1536,512]{1,0:T(8,128)(2,1)} %convolution_convert_fusion.7), channel_id=1, source_target_pairs={{0,1},{1,0},{2,3},{3,2},{4,5},{5,4},{6,7},{7,6},{8,9},{9,8},{10,11... | collective-permute-start | bytes 4718600 | tf_op jit(solution)/shard_map/ppermute | solution.py:62
  47.8 40.1 %collective-permute-start.5 = (bf16[1536,512]{1,0:T(8,128)(2,1)}, bf16[1536,512]{1,0:T(8,128)(2,1)}, u32[]{:S(2)}, u32[]{:S(2)}) collective-permute-start(bf16[1536,512]{1,0:T(8,128)(2,1)} %convolution_convert_fusion.6), channel_id=1, source_target_pairs={{0,4},{2,6},{4,0},{6,2},{1,5},{3,7},{5,1},{7,3},{8,12},{10,14},{12... | collective-permute-start | bytes 4718600 | tf_op jit(solution)/shard_map/ppermute | solution.py:61
  127.8 657.9 %reduce-scatter.2.cloned.1.call-start = ((), (), s32[]{:S(2)}) async-start(), calls=%async_computation.5 | async-start | bytes 4718592 | tf_op jit(solution)/shard_map/reduce_scatter | solution.py:979
  188.4 69.1 %collective-permute-start.19 = (bf16[1408,1024]{1,0:T(8,128)(2,1)}, bf16[1408,1024]{1,0:T(8,128)(2,1)}, u32[]{:S(2)}, u32[]{:S(2)}) collective-permute-start(bf16[1408,1024]{1,0:T(8,128)(2,1)} %convolution_convert_fusion.3), channel_id=1, source_target_pairs={{0,1},{1,0},{2,3},{3,2},{4,5},{5,4},{6,7},{7,6},{8,9},{9,8},{10,11... | collective-permute-start | bytes 8650760 | tf_op jit(solution)/shard_map/ppermute | solution.py:62
  192.8 68.9 %collective-permute-start.23 = (bf16[1408,1024]{1,0:T(8,128)(2,1)}, bf16[1408,1024]{1,0:T(8,128)(2,1)}, u32[]{:S(2)}, u32[]{:S(2)}) collective-permute-start(bf16[1408,1024]{1,0:T(8,128)(2,1)} %convolution_convert_fusion.2), channel_id=1, source_target_pairs={{0,4},{2,6},{4,0},{6,2},{1,5},{3,7},{5,1},{7,3},{8,12},{10,14},{12... | collective-permute-start | bytes 8650760 | tf_op jit(solution)/shard_map/ppermute | solution.py:61
  193.6 60.1 %collective-permute-start.20 = (f32[4,2,1,704]{3,2,1,0:T(1,128)S(1)}, f32[4,2,1,704]{3,2,1,0:T(1,128)S(1)}, u32[]{:S(2)}, u32[]{:S(2)}) collective-permute-start(f32[4,2,1,704]{3,2,1,0:T(1,128)S(1)} %get-tuple-element.992), channel_id=1, source_target_pairs={{0,1},{1,0},{2,3},{3,2},{4,5},{5,4},{6,7},{7,6},{8,9},{9,8},{10,11... | collective-permute-start | bytes 67592 | tf_op jit(solution)/shard_map/ppermute | solution.py:62
  267.2 32.8 %collective-permute-start.24 = (bf16[704,1024]{1,0:T(8,128)(2,1)}, bf16[704,1024]{1,0:T(8,128)(2,1)S(1)}, u32[]{:S(2)}, u32[]{:S(2)}) collective-permute-start(bf16[704,1024]{1,0:T(8,128)(2,1)} %get-tuple-element.602), channel_id=1, source_target_pairs={{0,1},{1,0},{2,3},{3,2},{4,5},{5,4},{6,7},{7,6},{8,9},{9,8},{10,11... | collective-permute-start | bytes 4325384 | tf_op jit(solution)/shard_map/ppermute | solution.py:62
  268.3 32.3 %collective-permute-start.22 = (bf16[704,1024]{1,0:T(8,128)(2,1)}, bf16[704,1024]{1,0:T(8,128)(2,1)S(1)}, u32[]{:S(2)}, u32[]{:S(2)}) collective-permute-start(bf16[704,1024]{1,0:T(8,128)(2,1)} %get-tuple-element.598), channel_id=1, source_target_pairs={{0,4},{2,6},{4,0},{6,2},{1,5},{3,7},{5,1},{7,3},{8,12},{10,14},{12... | collective-permute-start | bytes 4325384 | tf_op jit(solution)/shard_map/ppermute | solution.py:61
  325.4 32.3 %collective-permute-start.30 = (bf16[352,2048]{1,0:T(8,128)(2,1)S(1)}, bf16[352,2048]{1,0:T(8,128)(2,1)S(1)}, u32[]{:S(2)}, u32[]{:S(2)}) collective-permute-start(bf16[352,2048]{1,0:T(8,128)(2,1)S(1)} %get-tuple-element.624), channel_id=1, source_target_pairs={{0,8},{24,16},{1,9},{25,17},{2,10},{26,18},{3,11},{27,19},{4,12},{... | collective-permute-start | bytes 4325384 | tf_op jit(solution)/shard_map/ppermute | solution.py:197
  336.4 29.5 %collective-permute-start.28 = (bf16[2,1,704,512]{3,2,1,0:T(8,128)(2,1)S(1)}, bf16[2,1,704,512]{3,2,1,0:T(8,128)(2,1)S(1)}, u32[]{:S(2)}, u32[]{:S(2)}) collective-permute-start(bf16[2,1,704,512]{3,2,1,0:T(8,128)(2,1)S(1)} %pad_maximum_fusion.3.own0_ref), channel_id=1, source_target_pairs={{0,1},{1,0},{2,3},{3,2},{4,5},{5,4},{6,7},{7,6},{8,9},{9,8},{10,11... | collective-permute-start | bytes 4325384 | tf_op jit(solution)/shard_map/ppermute | solution.py:62
  337.3 29.2 %collective-permute-start.29 = (bf16[1,2,704,512]{3,2,1,0:T(8,128)(2,1)S(1)}, bf16[1,2,704,512]{3,2,1,0:T(8,128)(2,1)S(1)}, u32[]{:S(2)}, u32[]{:S(2)}) collective-permute-start(bf16[1,2,704,512]{3,2,1,0:T(8,128)(2,1)S(1)} %pad_maximum_fusion.4.own1_ref), channel_id=1, source_target_pairs={{0,4},{2,6},{4,0},{6,2},{1,5},{3,7},{5,1},{7,3},{8,12},{10,14},{12... | collective-permute-start | bytes 4325384 | tf_op jit(solution)/shard_map/ppermute | solution.py:61
  338.7 31.3 %collective-permute-start.32 = (f32[2,1024]{1,0:T(2,128)S(1)}, f32[2,1024]{1,0:T(2,128)S(1)}, u32[]{:S(2)}, u32[]{:S(2)}) collective-permute-start(f32[2,1024]{1,0:T(2,128)S(1)} %add.438), channel_id=1, source_target_pairs={{0,4},{2,6},{4,0},{6,2},{1,5},{3,7},{5,1},{7,3},{8,12},{10,14},{12... | collective-permute-start | bytes 24584 | tf_op jit(solution)/shard_map/ppermute | solution.py:61
  373.2 36.1 %collective-permute-start.31 = (bf16[352,2048]{1,0:T(8,128)(2,1)S(1)}, bf16[352,2048]{1,0:T(8,128)(2,1)S(1)}, u32[]{:S(2)}, u32[]{:S(2)}) collective-permute-start(bf16[352,2048]{1,0:T(8,128)(2,1)S(1)} %get-tuple-element.641), channel_id=1, source_target_pairs={{0,8},{24,16},{1,9},{25,17},{2,10},{26,18},{3,11},{27,19},{4,12},{... | collective-permute-start | bytes 4325384 | tf_op jit(solution)/shard_map/ppermute | solution.py:197
  385.3 50.9 %collective-permute-start.38 = (bf16[1,2,704,512]{3,2,1,0:T(8,128)(2,1)}, bf16[1,2,704,512]{3,2,1,0:T(8,128)(2,1)}, u32[]{:S(2)}, u32[]{:S(2)}) collective-permute-start(bf16[1,2,704,512]{3,2,1,0:T(8,128)(2,1)} %pad_maximum_fusion.6.own1_ref), channel_id=1, source_target_pairs={{0,4},{2,6},{4,0},{6,2},{1,5},{3,7},{5,1},{7,3},{8,12},{10,14},{12... | collective-permute-start | bytes 4325384 | tf_op jit(solution)/shard_map/ppermute | solution.py:61
  387.4 48.8 %collective-permute-start.37 = (bf16[2,1,704,512]{3,2,1,0:T(8,128)(2,1)}, bf16[2,1,704,512]{3,2,1,0:T(8,128)(2,1)}, u32[]{:S(2)}, u32[]{:S(2)}) collective-permute-start(bf16[2,1,704,512]{3,2,1,0:T(8,128)(2,1)} %pad_maximum_fusion.5.own0_ref), channel_id=1, source_target_pairs={{0,1},{1,0},{2,3},{3,2},{4,5},{5,4},{6,7},{7,6},{8,9},{9,8},{10,11... | collective-permute-start | bytes 4325384 | tf_op jit(solution)/shard_map/ppermute | solution.py:62
  411.0 38.0 %collective-permute-start.41 = (bf16[352,2048]{1,0:T(8,128)(2,1)}, bf16[352,2048]{1,0:T(8,128)(2,1)}, u32[]{:S(2)}, u32[]{:S(2)}) collective-permute-start(bf16[352,2048]{1,0:T(8,128)(2,1)} %reduce-precision_convert_fusion.9), channel_id=1, source_target_pairs={{8,0},{16,24},{9,1},{17,25},{10,2},{18,26},{11,3},{19,27},{12,4},{... | collective-permute-start | bytes 4325384 | tf_op jit(solution)/shard_map/ppermute | solution.py:200
  414.4 34.7 %collective-permute-start.42 = (bf16[352,2048]{1,0:T(8,128)(2,1)}, bf16[352,2048]{1,0:T(8,128)(2,1)}, u32[]{:S(2)}, u32[]{:S(2)}) collective-permute-start(bf16[352,2048]{1,0:T(8,128)(2,1)} %reduce-precision_convert_fusion.10), channel_id=1, source_target_pairs={{8,16},{16,8},{9,17},{17,9},{10,18},{18,10},{11,19},{19,11},{12,20... | collective-permute-start | bytes 4325384 | tf_op jit(solution)/shard_map/ppermute | solution.py:203
  416.1 36.7 %collective-permute-start.40 = (bf16[256,2816]{1,0:T(8,128)(2,1)}, bf16[256,2816]{1,0:T(8,128)(2,1)}, u32[]{:S(2)}, u32[]{:S(2)}) collective-permute-start(bf16[256,2816]{1,0:T(8,128)(2,1)} %get-tuple-element.659), channel_id=1, source_target_pairs={{0,8},{24,16},{1,9},{25,17},{2,10},{26,18},{3,11},{27,19},{4,12},{... | collective-permute-start | bytes 4325384 | tf_op jit(solution)/shard_map/ppermute | solution.py:197
  455.3 36.3 %collective-permute-start.48 = (bf16[352,2048]{1,0:T(8,128)(2,1)S(1)}, bf16[352,2048]{1,0:T(8,128)(2,1)S(1)}, u32[]{:S(2)}, u32[]{:S(2)}) collective-permute-start(bf16[352,2048]{1,0:T(8,128)(2,1)S(1)} %reduce-precision_convert_fusion.7), channel_id=1, source_target_pairs={{8,0},{16,24},{9,1},{17,25},{10,2},{18,26},{11,3},{19,27},{12,4},{... | collective-permute-start | bytes 4325384 | tf_op jit(solution)/shard_map/ppermute | solution.py:200
  459.0 32.6 %collective-permute-start.49 = (bf16[256,2816]{1,0:T(8,128)(2,1)S(1)}, bf16[256,2816]{1,0:T(8,128)(2,1)S(1)}, u32[]{:S(2)}, u32[]{:S(2)}) collective-permute-start(bf16[256,2816]{1,0:T(8,128)(2,1)S(1)} %reduce-precision_convert_fusion.8), channel_id=1, source_target_pairs={{8,16},{16,8},{9,17},{17,9},{10,18},{18,10},{11,19},{19,11},{12,20... | collective-permute-start | bytes 4325384 | tf_op jit(solution)/shard_map/ppermute | solution.py:203
  459.8 38.4 %collective-permute-start.47 = (bf16[256,2816]{1,0:T(8,128)(2,1)S(1)}, bf16[256,2816]{1,0:T(8,128)(2,1)S(1)}, u32[]{:S(2)}, u32[]{:S(2)}) collective-permute-start(bf16[256,2816]{1,0:T(8,128)(2,1)S(1)} %copy-done.110), channel_id=1, source_target_pairs={{0,8},{24,16},{1,9},{25,17},{2,10},{26,18},{3,11},{27,19},{4,12},{... | collective-permute-start | bytes 4325384 | tf_op jit(solution)/shard_map/ppermute | solution.py:197
  504.3 39.0 %collective-permute-start.54 = (bf16[256,2816]{1,0:T(8,128)(2,1)}, bf16[256,2816]{1,0:T(8,128)(2,1)}, u32[]{:S(2)}, u32[]{:S(2)}) collective-permute-start(bf16[256,2816]{1,0:T(8,128)(2,1)} %reduce-precision_convert_fusion.6), channel_id=1, source_target_pairs={{8,16},{16,8},{9,17},{17,9},{10,18},{18,10},{11,19},{19,11},{12,20... | collective-permute-start | bytes 4325384 | tf_op jit(solution)/shard_map/ppermute | solution.py:203
  507.9 35.4 %collective-permute-start.53 = (bf16[256,2816]{1,0:T(8,128)(2,1)}, bf16[256,2816]{1,0:T(8,128)(2,1)}, u32[]{:S(2)}, u32[]{:S(2)}) collective-permute-start(bf16[256,2816]{1,0:T(8,128)(2,1)} %fusion.7), channel_id=1, source_target_pairs={{0,8},{8,0},{16,24},{24,16},{1,9},{9,1},{17,25},{25,17},{2,10},{10... | collective-permute-start | bytes 4325384 | tf_op jit(solution)/shard_map/ppermute | solution.py:192
  548.5 33.0 %collective-permute-start.57 = (bf16[256,2816]{1,0:T(8,128)(2,1)}, bf16[256,2816]{1,0:T(8,128)(2,1)S(1)}, u32[]{:S(2)}, u32[]{:S(2)}) collective-permute-start(bf16[256,2816]{1,0:T(8,128)(2,1)} %fusion.8), channel_id=1, source_target_pairs={{0,8},{8,0},{16,24},{24,16},{1,9},{9,1},{17,25},{25,17},{2,10},{10... | collective-permute-start | bytes 4325384 | tf_op jit(solution)/shard_map/ppermute | solution.py:192
  552.0 29.5 %collective-permute-start.58 = (bf16[256,2816]{1,0:T(8,128)(2,1)S(1)}, bf16[256,2816]{1,0:T(8,128)(2,1)}, u32[]{:S(2)}, u32[]{:S(2)}) collective-permute-start(bf16[256,2816]{1,0:T(8,128)(2,1)S(1)} %reduce-precision_convert_fusion.4), channel_id=1, source_target_pairs={{8,16},{16,8},{9,17},{17,9},{10,18},{18,10},{11,19},{19,11},{12,20... | collective-permute-start | bytes 4325384 | tf_op jit(solution)/shard_map/ppermute | solution.py:203
  556.5 86.1 %collective-permute-start.66 = (bf16[256,2816]{1,0:T(8,128)(2,1)}, bf16[256,2816]{1,0:T(8,128)(2,1)S(1)}, u32[]{:S(2)}, u32[]{:S(2)}) collective-permute-start(bf16[256,2816]{1,0:T(8,128)(2,1)} %broadcast_select_fusion.4), channel_id=1, source_target_pairs={{0,2},{2,0},{4,6},{6,4},{1,3},{3,1},{5,7},{7,5},{8,10},{10,8},{12,... | collective-permute-start | bytes 4325384 | tf_op jit(solution)/shard_map/ppermute | solution.py:57
  569.0 40.7 %collective-permute-start.55 = (bf16[2,1,768,512]{3,2,1,0:T(8,128)(2,1)S(1)}, bf16[2,1,768,512]{3,2,1,0:T(8,128)(2,1)S(1)}, u32[]{:S(2)}, u32[]{:S(2)}) collective-permute-start(bf16[2,1,768,512]{3,2,1,0:T(8,128)(2,1)S(1)} %pad_maximum_fusion.1.own0_ref), channel_id=1, source_target_pairs={{0,1},{1,0},{2,3},{3,2},{4,5},{5,4},{6,7},{7,6},{8,9},{9,8},{10,11... | collective-permute-start | bytes 4718600 | tf_op jit(solution)/shard_map/ppermute | solution.py:62
  570.6 35.7 %collective-permute-start.56 = (bf16[1,2,768,512]{3,2,1,0:T(8,128)(2,1)S(1)}, bf16[1,2,768,512]{3,2,1,0:T(8,128)(2,1)}, u32[]{:S(2)}, u32[]{:S(2)}) collective-permute-start(bf16[1,2,768,512]{3,2,1,0:T(8,128)(2,1)S(1)} %pad_maximum_fusion.2.own1_ref), channel_id=1, source_target_pairs={{0,4},{2,6},{4,0},{6,2},{1,5},{3,7},{5,1},{7,3},{8,12},{10,14},{12... | collective-permute-start | bytes 4718600 | tf_op jit(solution)/shard_map/ppermute | solution.py:61
  583.3 40.5 %collective-permute-start.60 = (bf16[256,2816]{1,0:T(8,128)(2,1)S(1)}, bf16[256,2816]{1,0:T(8,128)(2,1)}, u32[]{:S(2)}, u32[]{:S(2)}) collective-permute-start(bf16[256,2816]{1,0:T(8,128)(2,1)S(1)} %reduce-precision_convert_fusion.1), channel_id=1, source_target_pairs={{8,0},{16,24},{9,1},{17,25},{10,2},{18,26},{11,3},{19,27},{12,4},{... | collective-permute-start | bytes 4325384 | tf_op jit(solution)/shard_map/ppermute | solution.py:200
  585.0 38.9 %collective-permute-start.61 = (bf16[256,2816]{1,0:T(8,128)(2,1)S(1)}, bf16[256,2816]{1,0:T(8,128)(2,1)}, u32[]{:S(2)}, u32[]{:S(2)}) collective-permute-start(bf16[256,2816]{1,0:T(8,128)(2,1)S(1)} %reduce-precision_convert_fusion.2), channel_id=1, source_target_pairs={{8,16},{16,8},{9,17},{17,9},{10,18},{18,10},{11,19},{19,11},{12,20... | collective-permute-start | bytes 4325384 | tf_op jit(solution)/shard_map/ppermute | solution.py:203
  624.0 34.7 %collective-permute-start.65 = (bf16[256,1024]{1,0:T(8,128)(2,1)S(1)}, bf16[256,1024]{1,0:T(8,128)(2,1)S(1)}, u32[]{:S(2)}, u32[]{:S(2)}) collective-permute-start(bf16[256,1024]{1,0:T(8,128)(2,1)S(1)} %reduce-precision_convert_fusion.27), channel_id=1, source_target_pairs={{8,16},{16,8},{9,17},{17,9},{10,18},{18,10},{11,19},{19,11},{12,20... | collective-permute-start | bytes 1572872 | tf_op jit(solution)/shard_map/ppermute | solution.py:203
  629.7 29.1 %collective-permute-start.63 = (bf16[256,1024]{1,0:T(8,128)(2,1)S(1)}, bf16[256,1024]{1,0:T(8,128)(2,1)S(1)}, u32[]{:S(2)}, u32[]{:S(2)}) collective-permute-start(bf16[256,1024]{1,0:T(8,128)(2,1)S(1)} %shard_map.340), channel_id=1, source_target_pairs={{0,8},{24,16},{1,9},{25,17},{2,10},{26,18},{3,11},{27,19},{4,12},{... | collective-permute-start | bytes 1572872 | tf_op jit(solution)/shard_map/ppermute | solution.py:197
  637.8 32.1 %collective-permute-start.64 = (bf16[256,2816]{1,0:T(8,128)(2,1)S(1)}, bf16[256,2816]{1,0:T(8,128)(2,1)S(1)}, u32[]{:S(2)}, u32[]{:S(2)}) collective-permute-start(bf16[256,2816]{1,0:T(8,128)(2,1)S(1)} %reduce-precision_convert_fusion), channel_id=1, source_target_pairs={{8,0},{16,24},{9,1},{17,25},{10,2},{18,26},{11,3},{19,27},{12,4},{... | collective-permute-start | bytes 4325384 | tf_op jit(solution)/shard_map/ppermute | solution.py:200
  642.8 28.3 %collective-permute-start.62 = (f32[256,1024]{1,0:T(8,128)S(1)}, f32[256,1024]{1,0:T(8,128)S(1)}, u32[]{:S(2)}, u32[]{:S(2)}) collective-permute-start(f32[256,1024]{1,0:T(8,128)S(1)} %get-tuple-element.948), channel_id=1, source_target_pairs={{0,2},{2,0},{4,6},{6,4},{1,3},{3,1},{5,7},{7,5},{8,10},{10,8},{12,... | collective-permute-start | bytes 3145736 | tf_op jit(solution)/shard_map/ppermute | solution.py:57
  676.9 40.0 %collective-permute-start.74 = (bf16[256,2816]{1,0:T(8,128)(2,1)}, bf16[256,2816]{1,0:T(8,128)(2,1)S(1)}, u32[]{:S(2)}, u32[]{:S(2)}) collective-permute-start(bf16[256,2816]{1,0:T(8,128)(2,1)} %broadcast_select_fusion.2), channel_id=1, source_target_pairs={{0,2},{2,0},{4,6},{6,4},{1,3},{3,1},{5,7},{7,5},{8,10},{10,8},{12,... | collective-permute-start | bytes 4325384 | tf_op jit(solution)/shard_map/ppermute | solution.py:57
  676.9 37.9 %collective-permute-start.76 = (bf16[256,1024]{1,0:T(8,128)(2,1)}, bf16[256,1024]{1,0:T(8,128)(2,1)}, u32[]{:S(2)}, u32[]{:S(2)}) collective-permute-start(bf16[256,1024]{1,0:T(8,128)(2,1)} %reduce-precision_convert_fusion.26), channel_id=1, source_target_pairs={{8,16},{16,8},{9,17},{17,9},{10,18},{18,10},{11,19},{19,11},{12,20... | collective-permute-start | bytes 1572872 | tf_op jit(solution)/shard_map/ppermute | solution.py:203
  680.4 29.9 %collective-permute-start.75 = (bf16[256,1024]{1,0:T(8,128)(2,1)}, bf16[256,1024]{1,0:T(8,128)(2,1)}, u32[]{:S(2)}, u32[]{:S(2)}) collective-permute-start(bf16[256,1024]{1,0:T(8,128)(2,1)} %fusion.11), channel_id=1, source_target_pairs={{0,8},{8,0},{16,24},{24,16},{1,9},{9,1},{17,25},{25,17},{2,10},{10... | collective-permute-start | bytes 1572872 | tf_op jit(solution)/shard_map/ppermute | solution.py:192
  683.0 49.4 %collective-permute-start.73 = (bf16[256,1024]{1,0:T(8,128)(2,1)}, bf16[256,1024]{1,0:T(8,128)(2,1)}, u32[]{:S(2)}, u32[]{:S(2)}) collective-permute-start(bf16[256,1024]{1,0:T(8,128)(2,1)} %reduce-precision_convert_fusion.25), channel_id=1, source_target_pairs={{8,16},{16,8},{9,17},{17,9},{10,18},{18,10},{11,19},{19,11},{12,20... | collective-permute-start | bytes 1572872 | tf_op jit(solution)/shard_map/ppermute | solution.py:203
  692.9 39.6 %collective-permute-start.72 = (bf16[256,1024]{1,0:T(8,128)(2,1)}, bf16[256,1024]{1,0:T(8,128)(2,1)}, u32[]{:S(2)}, u32[]{:S(2)}) collective-permute-start(bf16[256,1024]{1,0:T(8,128)(2,1)} %get-tuple-element.807), channel_id=1, source_target_pairs={{0,8},{24,16},{1,9},{25,17},{2,10},{26,18},{3,11},{27,19},{4,12},{... | collective-permute-start | bytes 1572872 | tf_op jit(solution)/shard_map/ppermute | solution.py:197
  716.2 39.5 %collective-permute-start.79 = (bf16[256,1024]{1,0:T(8,128)(2,1)S(1)}, bf16[256,1024]{1,0:T(8,128)(2,1)S(1)}, u32[]{:S(2)}, u32[]{:S(2)}) collective-permute-start(bf16[256,1024]{1,0:T(8,128)(2,1)S(1)} %reduce-precision_convert_fusion.23), channel_id=1, source_target_pairs={{8,16},{16,8},{9,17},{17,9},{10,18},{18,10},{11,19},{19,11},{12,20... | collective-permute-start | bytes 1572872 | tf_op jit(solution)/shard_map/ppermute | solution.py:203
  733.8 31.0 %collective-permute-start.83 = (bf16[256,1024]{1,0:T(8,128)(2,1)S(1)}, bf16[256,1024]{1,0:T(8,128)(2,1)S(1)}, u32[]{:S(2)}, u32[]{:S(2)}) collective-permute-start(bf16[256,1024]{1,0:T(8,128)(2,1)S(1)} %reduce-precision_convert_fusion.22), channel_id=1, source_target_pairs={{8,16},{16,8},{9,17},{17,9},{10,18},{18,10},{11,19},{19,11},{12,20... | collective-permute-start | bytes 1572872 | tf_op jit(solution)/shard_map/ppermute | solution.py:203
  756.7 34.2 %collective-permute-start.81 = (bf16[256,1024]{1,0:T(8,128)(2,1)}, bf16[256,1024]{1,0:T(8,128)(2,1)}, u32[]{:S(2)}, u32[]{:S(2)}) collective-permute-start(bf16[256,1024]{1,0:T(8,128)(2,1)} %reduce-precision_convert_fusion.20), channel_id=1, source_target_pairs={{8,16},{16,8},{9,17},{17,9},{10,18},{18,10},{11,19},{19,11},{12,20... | collective-permute-start | bytes 1572872 | tf_op jit(solution)/shard_map/ppermute | solution.py:203
  765.7 43.4 %collective-permute-start.86 = (bf16[256,1024]{1,0:T(8,128)(2,1)}, bf16[256,1024]{1,0:T(8,128)(2,1)}, u32[]{:S(2)}, u32[]{:S(2)}) collective-permute-start(bf16[256,1024]{1,0:T(8,128)(2,1)} %reduce-precision_convert_fusion.14), channel_id=1, source_target_pairs={{8,0},{16,24},{9,1},{17,25},{10,2},{18,26},{11,3},{19,27},{12,4},{... | collective-permute-start | bytes 1572872 | tf_op jit(solution)/shard_map/ppermute | solution.py:200
  768.0 41.1 %collective-permute-start.87 = (bf16[256,1024]{1,0:T(8,128)(2,1)}, bf16[256,1024]{1,0:T(8,128)(2,1)}, u32[]{:S(2)}, u32[]{:S(2)}) collective-permute-start(bf16[256,1024]{1,0:T(8,128)(2,1)} %reduce-precision_convert_fusion.17), channel_id=1, source_target_pairs={{8,16},{16,8},{9,17},{17,9},{10,18},{18,10},{11,19},{19,11},{12,20... | collective-permute-start | bytes 1572872 | tf_op jit(solution)/shard_map/ppermute | solution.py:203
  770.3 25.8 %collective-permute-start.88 = (bf16[256,1024]{1,0:T(8,128)(2,1)}, bf16[256,1024]{1,0:T(8,128)(2,1)}, u32[]{:S(2)}, u32[]{:S(2)}) collective-permute-start(bf16[256,1024]{1,0:T(8,128)(2,1)} %broadcast_select_fusion.22), channel_id=1, source_target_pairs={{0,2},{2,0},{4,6},{6,4},{1,3},{3,1},{5,7},{7,5},{8,10},{10,8},{12,... | collective-permute-start | bytes 1572872 | tf_op jit(solution)/shard_map/ppermute | solution.py:57
  777.5 26.8 %all-to-all-start.3 = ((f32[8,7,256]{2,1,0:T(8,128)}), f32[8,7,256]{2,1,0:T(8,128)S(1)}, u32[]{:S(2)}, u32[]{:S(2)}) async-start(f32[8,7,256]{2,1,0:T(8,128)} %broadcast_in_dim.83), calls=%async_computation.4 | async-start | bytes 131072 | tf_op jit(solution)/shard_map/all_to_all | solution.py:1037
  804.2 25.6 %all-to-all-start.2 = ((bf16[8,256,128]{2,1,0:T(8,128)(2,1)}), bf16[8,256,128]{2,1,0:T(8,128)(2,1)}, u32[]{:S(2)}, u32[]{:S(2)}) async-start(bf16[8,256,128]{2,1,0:T(8,128)(2,1)} %bitcast.94), calls=%async_computation.3 | async-start | bytes 1048576 | tf_op jit(solution)/shard_map/all_to_all | solution.py:1021
  (195 other events, 1575.1 us)
Sparse Core Ops, SparseCore 0:
  127.9 48.4 all-gather.2
  502.7 55.7 reduce-scatter.1

commit v9 on v8

--- a/solution.py
+++ b/solution.py
@@ -222,6 +222,83 @@
         compiler_params=pltpu.CompilerParams(vmem_limit_bytes=48 * 1024 * 1024),
         cost_estimate=SMALL,
     )(w)
+
+
+class PairSum:
+    def __init__(self, order, g):
+        self.order = order
+        self.even = lax.axis_index("rep") % 2 == 0
+        half = g.shape[0] // 2
+
+        def cut(g):
+            a, b = g[:half], g[half:]
+            return jnp.where(self.even, b, a), jnp.where(self.even, a, b)
+
+        send, self.kept = order(cut, g)
+        self.got = self.exchange(send, 1)
+        self.stage = 0
+
+    def exchange(self, x, step):
+        return lax.ppermute(x, "rep", [(i, i ^ step) for i in range(lax.axis_size("rep"))])
+
+    def step(self):
+        def add(a, b):
+            return lax.reduce_precision(a.astype(f32) + b.astype(f32), 8, 7).astype(bf16)
+
+        def put(a, b):
+            return jnp.where(self.even, a, b), jnp.where(self.even, b, a)
+
+        if self.stage < 2:
+            self.kept = self.order(add, self.kept, self.got)
+            self.got = self.exchange(self.kept, 2 - self.stage)
+        else:
+            self.done = self.order(put, self.kept, self.got)
+        self.stage += 1
+
+
+def gated_kernel(ga_ref, gb_ref, ua_ref, ub_ref, grad_ref, gains_ref, g0_ref, g1_ref, u0_ref, u1_ref, act_ref, sums_ref):
+    half = g0_ref.shape[1]
+    gate = ga_ref[...].astype(f32) + gb_ref[...].astype(f32)
+    up = ua_ref[...].astype(f32) + ub_ref[...].astype(f32)
+    sig = jax.nn.sigmoid(gate)
+    silu = gate * sig
+    grad = grad_ref[...]
+    act_ref[...] = (silu * up).astype(bf16)
+    ggate = (grad * up * sig * (1.0 + gate * (1.0 - sig))).astype(bf16)
+    gup = (grad * silu).astype(bf16)
+    g0_ref[...] = ggate[:, :half]
+    g1_ref[...] = ggate[:, half:]
+    u0_ref[...] = gup[:, :half]
+    u1_ref[...] = gup[:, half:]
+    a, b = ggate.astype(f32), gup.astype(f32)
+    e = jnp.sum(a * gains_ref[0] + b * gains_ref[2], axis=0, keepdims=True)
+    ez = jnp.sum(a * (gate - gains_ref[1]) + b * (up - gains_ref[3]), axis=0, keepdims=True)
+    both = jnp.concatenate([e, ez], axis=0)
+
+    @pl.when(pl.program_id(0) == 0)
+    def _():
+        sums_ref[...] = both
+
+    @pl.when(pl.program_id(0) > 0)
+    def _():
+        sums_ref[...] += both
+
+
+def gated(ga, gb, ua, ub, grad_act, gains):
+    rows, t = grad_act.shape
+    n = max(n for n in (1, 2, 4) if rows % (16 * n) == 0)
+    whole = pl.BlockSpec((rows // n, t), lambda i: (i, 0))
+    half = pl.BlockSpec((rows // n, t // 2), lambda i: (i, 0))
+    out_half = jax.ShapeDtypeStruct((rows, t // 2), bf16)
+    return pl.pallas_call(
+        gated_kernel,
+        grid=(n,),
+        in_specs=[whole] * 5 + [pl.BlockSpec((4, rows // n, 1), lambda i: (0, i, 0))],
+        out_specs=[half] * 4 + [whole, pl.BlockSpec((2, t), lambda i: (0, 0))],
+        out_shape=[out_half] * 4 + [jax.ShapeDtypeStruct((rows, t), bf16), jax.ShapeDtypeStruct((2, t), f32)],
+        compiler_params=pltpu.CompilerParams(vmem_limit_bytes=56 * 1024 * 1024),
+        cost_estimate=SMALL,
+    )(ga, gb, ua, ub, grad_act, gains)
 
 
 def split_kernel(core_ref, w_ref, mine_ref, theirs_ref):
@@ -784,6 +861,7 @@
     wd_own = do(cast, w_down)
     wg = do(stack_turned, *wg_parts)
     wu = do(stack_turned, *wu_parts)
+    cot_all = do(lambda c: c, cot_all)
     grad_act = do(lambda w, c: mm(w, c, LAST, f32, tn=256), wd_own, cot_all)
     cot_cols = do(lambda c: lax.dynamic_slice_in_dim(c, my_block * blk, blk, 1).T, cot_all)
     wo_own = do(cast, w_out)
@@ -794,16 +872,7 @@
     gains = do(lambda g: g.reshape(4, ffb, 1), gains)
     flying = scatter_rest(flying)
 
-    def gated(ga, gb, ua, ub, grad_act, gains):
-        gate = ga.astype(f32) + gb.astype(f32)
-        up = ua.astype(f32) + ub.astype(f32)
-        sig = jax.nn.sigmoid(gate)
-        silu = gate * sig
-        ggate = (grad_act * up * sig * (1.0 + gate * (1.0 - sig))).astype(bf16)
-        gup = (grad_act * silu).astype(bf16)
-        return ggate, gup, (silu * up).astype(bf16), gate, up
-
-    ggate, gup, act, gate, up = do(gated, *flying[0], *flying[1], grad_act, gains)
+    gate0, gate1, up0, up1, act, sums = do(gated, *flying[0], *flying[1], grad_act, gains)
 
     def parts_of(count, want):
         return max(n for n in range(1, want + 1) if count % (16 * n) == 0)
@@ -842,13 +911,6 @@
     for name, lead in (("gate", 0), ("up", Y)):
         for k, (at_row, count) in enumerate(up_rows):
             jobs.append(("up", [(name, "mine", k), (name, "theirs", k)], at_row, lead, count, S * ffb))
-    for k in range(2):
-        jobs.append(("out", [("out", k)], 0, k, blk, width // 2))
-    for third in (2, 1, 0):
-        for k, (at_row, count) in enumerate(up_rows):
-            jobs.append(
-                ("qkv", [(third, "mine", k), (third, "theirs", k)], at_row, third * Y, count, S * blk)
-            )
     received = {}
 
     def update(limit):
@@ -870,20 +932,13 @@
     def quarter_heads(x):
         return [x[:, h][None, None] for h in halves]
 
-    n, start, finish, gate_all = gather_steps(quarter_heads(ggate), 1)
+    n, start, finish, gate_all = gather_steps([gate0[None, None], gate1[None, None]], 1)
     start(0)
     g_down = do(lambda a, c: mm(a, c, PLAIN, bf16, tn=512), act, cot_all)
     for k, (at_row, count) in enumerate(down_rows):
         reps.push(("down", k), g_down[at_row : at_row + count])
     ticks(1)
 
-    def norm_sums2(ggate, gup, gate, up, gains):
-        a, b = ggate.astype(f32), gup.astype(f32)
-        e = jnp.sum(a * gains[0] + b * gains[2], axis=0, keepdims=True)
-        ez = jnp.sum(a * (gate - gains[1]) + b * (up - gains[3]), axis=0, keepdims=True)
-        return join(e, ez)
-
-    sums = do(norm_sums2, ggate, gup, gate, up, gains)
     steps2 = at.steps(False) + [("core", 1)]
 
     def sum_send(sums, axis, step):
@@ -900,7 +955,7 @@
         sums_got = sum_send(sums, *tiny.pop(0))
         start(i, sums)
         ticks(1)
-    n, start_up, finish_up, up_all = gather_steps(quarter_heads(gup), 1)
+    n, start_up, finish_up, up_all = gather_steps([up0[None, None], up1[None, None]], 1)
     ggate_all = gate_all().reshape(Y * S * ffb, T)
     sums = do(lambda a, b: a + b, sums, sums_got)
     start_up(0, sums)
@@ -921,7 +976,6 @@
     gup_all = up_all().reshape(Y * S * ffb, T)
     part = do(lambda w, g, p: dot(w, g, PLAIN) + p, wu, gup_all, part_gate)
     part_theirs = at.core(part[blk:])
-    ticks(1)
 
     def branch(a, b, cot, z, scale, gain, sums):
         gxn2 = a + b
@@ -934,6 +988,7 @@
     )
     n, start, finish, branch_all = gather_steps(quarter_heads(grad_branch), 1)
     start(0)
+    ticks(1)
     g_up = do(lambda x, g: mm(x, g, LAST, bf16, tn=wide), xn2, gup_all)
     push_pairs("up", g_up, up_rows)
     finish()
@@ -955,32 +1010,31 @@
     n, start, finish, gqkv_done = gather_steps([g.reshape(1, 1, 3 * blk, H) for g in gqkvs], 3)
     start(0)
     attn = lanes(*attns)
-    for k in range(2):
-        g_out = do(lambda a, g: mm(a, g, LAST, bf16, tn=512), attn, gbr[k * width // 2 : (k + 1) * width // 2])
-        reps.push(("out", k), g_out)
+    g_out = do(lambda a, g: mm(a, g, LAST, bf16, tn=512), attn, gbr)
+    out_pair = PairSum(do, g_out)
     ticks(1)
     finish()
     for i in range(1, n):
         start(i)
         if i == 1:
+            out_pair.step()
             update(1)
             ticks(1)
+            out_pair.step()
             update(1)
         if i < n - 1:
             finish()
     gqkv = gqkv_done().reshape(3, Y * S * blk, T)
+    pairs = []
     for third in (2, 1, 0):
         g = do(lambda x, g: dot(x, g, LAST).astype(bf16), xn1, gqkv[third])
-        push_pairs(third, g, up_rows)
-        if third == 2:
-            ticks(1)
+        pairs.append(PairSum(do, g))
+    ticks(1)
     part = do(lambda w, g: dot(w, g, PLAIN), wq, gqkv.reshape(3 * Y * S * blk, T))
     part_theirs = at.core(part[blk:])
+    pairs[0].step()
+    out_pair.step()
     out_sum = lax.psum_scatter(out_part, plane, scatter_dimension=0, tiled=True)
-    reps.depth = 2
-    ticks(1)
-    update(1)
-    ticks(1)
 
     def first_back(a, b, x, mean, inv, gain, gxn2, z2, gqkv0, gqkv1):
         gxn1 = a + b
@@ -1002,9 +1056,11 @@
     sums, small, gxn1, z1 = do(
         first_back, part[:blk], part_theirs, x_own, mean1, inv1, own_cols[:, 0:1], gxn2, z2, *gqkvs
     )
-    for axis, step in steps2:
+    sums = sum_step(sums, *steps2[0])
+    pairs[1].step()
+    for axis, step in steps2[1:]:
         sums = sum_step(sums, axis, step)
-    ticks(1)
+    pairs[2].step()
     input_grad = do(
         lambda h, grad, z, scale, gain, sums: h
         + scale * (grad * gain - sums[0:1] / width - z * (sums[1:2] / width)),
@@ -1021,36 +1077,45 @@
         got = lax.all_to_all(split, plane, split_axis=0, concat_axis=0, tiled=True)
         return do(lambda g: g.reshape(width, rows).T, got)
 
-    input_rows = to_rows(input_grad)
+    def adam_qkv(third, pair):
+        mine, theirs = pair.done
+        adam("qkv", [mine, at.core(theirs)], 0, third * Y, S * blk, min(blk, 128))
+
     ticks(1)
     update(1)
-    ticks(1)
+    pairs[0].step()
     n_rep = lax.axis_size("rep")
     step = 1
     while step < n_rep:
         other = lax.ppermute(small, "rep", [(i, i ^ step) for i in range(n_rep)])
         small = do(lambda a, b: a + b, small, other)
         step *= 2
+    for k, g in enumerate(out_pair.done):
+        adam("out", [g], k * blk // 2, 0, width // 2, blk // 2)
+    ticks(1)
+    input_rows = to_rows(input_grad)
+    pairs[1].step()
     update(1)
-    ticks(1)
-    sent = do(lambda s: jnp.broadcast_to(s.reshape(1, 7, blk), (nb, 7, blk)), small)
-    small_all = lax.all_to_all(sent, plane, split_axis=0, concat_axis=0, tiled=True)
-
-    out_cols = do(lambda h, a: (h + a.astype(f32)).astype(bf16), hidden, out_sum)
-    block_output = to_rows(out_cols)
-    ticks(1)
-    update(1)
-    ticks(1)
-    update(1)
-
-    def norm_update(every, *a):
-        return adam_update(*a, every.transpose(1, 0, 2).reshape(7, width), 0.3, 0.0)
-
-    mn, vn, wn = do(norm_update, small_all, norm_params, m_norm, v_norm)
     while reps.busy():
         reps.tick()
         update(1)
+    out_cols = do(lambda h, a: (h + a.astype(f32)).astype(bf16), hidden, out_sum)
+    pairs[0].step()
+    adam_qkv(2, pairs[0])
+    pairs[2].step()
+    pairs[1].step()
     update(len(jobs))
+    block_output = to_rows(out_cols)
+    adam_qkv(1, pairs[1])
+    sent = do(lambda s: jnp.broadcast_to(s.reshape(1, 7, blk), (nb, 7, blk)), small)
+    small_all = lax.all_to_all(sent, plane, split_axis=0, concat_axis=0, tiled=True)
+
+    def norm_update(every, *a):
+        return adam_update(*a, every.transpose(1, 0, 2).reshape(7, width), 0.3, 0.0)
+
+    mn, vn, wn = do(norm_update, small_all, norm_params, m_norm, v_norm)
+    pairs[2].step()
+    adam_qkv(0, pairs[2])
     return (
         (block_output.reshape(tokens.shape), input_rows.reshape(tokens.shape))
         + tuple(results["qkv"])

time: 866 us -> 913 us (1.054)
  waiting for transfers between devices: 257 us -> 360 us
  starting transfers between devices: 145 us -> 104 us
  other arithmetic: 91.5 us -> 68.3 us
    ppermute x0 -> x12, waiting for transfers between devices: none -> 61.6 us  [exchange(): lax.ppermute(x, 'rep', [(i, i ^ step) for i in range(lax.axis_size('rep'))])]
    ppermute x18, waiting for transfers between devices: 102 us -> 48.3 us  [along(): return lax.ppermute(x, 'shard', [(i, i ^ step) for i in range(self.s_size)])]
    ppermute x18, waiting for transfers between devices: 31.6 us -> 71.6 us  [along(): lax.ppermute(x, 'ctx', [(i, i ^ 2 * step) for i in range(self.ctx_size)])]
    ppermute x8 -> x4, waiting for transfers between devices: 32.3 us -> 68.3 us  [tick(): slot['out_got'] = lax.ppermute(out['total'], 'rep', [(1, 0), (2, 3)])]
    ppermute x8 -> x4, starting transfers between devices: 42.6 us -> 20.5 us  [tick(): slot['in_got'] = lax.ppermute(out['new'], 'rep', [(0, 1), (3, 2)])]
    ppermute x0 -> x12, starting transfers between devices: none -> 17.2 us  [exchange(): lax.ppermute(x, 'rep', [(i, i ^ step) for i in range(lax.axis_size('rep'))])]
    ppermute x8 -> x4, waiting for transfers between devices: 48.4 us -> 62.6 us  [tick(): slot['in_got'] = lax.ppermute(out['new'], 'rep', [(0, 1), (3, 2)])]
    all_to_all x2, waiting for transfers between devices: 4.44 us -> 17.9 us  [to_rows(): got = lax.all_to_all(split, plane, split_axis=0, concat_axis=0, tiled=True)]
  transfers between devices with their start and end apart: 99 -> 90, of which waited for: 39 -> 42; matrix products, arithmetic and copies ran while one was open for 20% -> 16% of each run, Pallas kernels for 21% -> 20%
where the time goes in v9:
time: 913 us; the launch traced here: 901 us
  waiting for transfers between devices  360 us (39%)
  Pallas kernels  196 us (21%)
  starting transfers between devices  104 us (11%)
  local copies, waits for them, and re-layouts  102 us (11%)
  other arithmetic  68.3 us (7%)
  matrix products  45.4 us (5%)
  between operations  16.5 us (2%)
    ppermute x18, waiting for transfers between devices, along(): lax.ppermute(x, 'ctx', [(i, i ^ 2 * step) for i in range(self.ctx_size)])  71.6 us
    pallas_call x9, Pallas kernels, adam_part(): pl.pallas_call(functools.partial(adam_kernel, rate, two), grid_spec=pltpu...  69.1 us
    ppermute x4, waiting for transfers between devices, tick(): slot['out_got'] = lax.ppermute(out['total'], 'rep', [(1, 0), (2, 3)])  68.3 us
    ppermute x4, waiting for transfers between devices, tick(): slot['in_got'] = lax.ppermute(out['new'], 'rep', [(0, 1), (3, 2)])  62.6 us
    ppermute x12, waiting for transfers between devices, exchange(): lax.ppermute(x, 'rep', [(i, i ^ step) for i in range(lax.axis_size('rep'))])  61.6 us
    unnamed x290, local copies, waits for them, and re-layouts  58.2 us
    ppermute x18, waiting for transfers between devices, along(): return lax.ppermute(x, 'shard', [(i, i ^ step) for i in range(self.s_size)])  48.3 us
    dot_general x22, matrix products, dot(): return lax.dot_general(a, b, dims, preferred_element_type=f32)  45.4 us
  transfers between devices with their start and end apart: 90, of which 42 were waited for; matrix products, arithmetic and copies ran while one was open for 16% of the time, Pallas kernels for 20%

profile of v9, /device:TPU:0, one launch (start us, length us, event | category | flops | bytes accessed | tf_op | source)
XLA Modules:
  0.0 900.7 jit_solution(10145291916574751810)
XLA Ops:
  73.4 9.5 %collective-permute-done.3.b_ref.d_ref = bf16[1536,512]{1,0:T(8,128)(2,1)} collective-permute-done((bf16[1536,512]{1,0:T(8,128)(2,1)}, bf16[1536,512]{1,0:T(8,128)(2,1)}, u32[]{:S(2)}, u32[]{:S(2)}) %collective-permute-start.3) | collective-permute-done | bytes 1572896 | tf_op jit(solution)/shard_map/ppermute | solution.py:62
  97.4 10.5 %collective-permute-done.4 = bf16[768,512]{1,0:T(8,128)(2,1)} collective-permute-done((bf16[768,512]{1,0:T(8,128)(2,1)}, bf16[768,512]{1,0:T(8,128)(2,1)}, u32[]{:S(2)}, u32[]{:S(2)}) %collective-permute-start.4) | collective-permute-done | bytes 786464 | tf_op jit(solution)/shard_map/ppermute | solution.py:61
  110.7 5.1 shard_map.315
  120.2 5.1 shard_map.316
  147.5 6.6 collective-permute-done.9.b_ref.d_ref
  160.6 10.7 %collective-permute-done.12 = bf16[256,512]{1,0:T(8,128)(2,1)S(1)} collective-permute-done((bf16[256,512]{1,0:T(8,128)(2,1)S(1)}, bf16[256,512]{1,0:T(8,128)(2,1)S(1)}, u32[]{:S(2)}, u32[]{:S(2)}) %collective-permute-start.12) | collective-permute-done | bytes 262176 | tf_op jit(solution)/shard_map/ppermute | solution.py:61
  196.3 5.0 convolution_convert_fusion.1.a_ref.c_ref
  215.8 6.4 copy.118.b_ref
  224.0 5.6 shard_map.324.grad_ref
  238.0 17.0 %collective-permute-done.20 = f32[4,2,1,704]{3,0,2,1:T(4,128)S(1)} collective-permute-done((f32[4,2,1,704]{3,0,2,1:T(4,128)S(1)}, f32[4,2,1,704]{3,0,2,1:T(4,128)S(1)}, u32[]{:S(2)}, u32[]{:S(2)}) %collective-permute-start.20) | collective-permute-done | bytes 22560 | tf_op jit(solution)/shard_map/ppermute | solution.py:62
  268.1 26.1 %collective-permute-done.22.gb_ref = bf16[704,1024]{1,0:T(8,128)(2,1)S(1)} collective-permute-done((bf16[704,1024]{1,0:T(8,128)(2,1)S(1)}, bf16[704,1024]{1,0:T(8,128)(2,1)S(1)}, u32[]{:S(2)}, u32[]{:S(2)}) %collective-permute-start.22) | collective-permute-done | bytes 1441824 | tf_op jit(solution)/shard_map/ppermute | solution.py:61
  300.9 8.3 shard_map.329
  311.1 6.5 copy.120.b_ref
  317.6 5.4 shard_map.330
  333.2 22.9 %collective-permute-done.30 = bf16[352,2048]{1,0:T(8,128)(2,1)S(1)} collective-permute-done((bf16[352,2048]{1,0:T(8,128)(2,1)S(1)}, bf16[352,2048]{1,0:T(8,128)(2,1)S(1)}, u32[]{:S(2)}, u32[]{:S(2)}) %collective-permute-start.30) | collective-permute-done | bytes 1441824 | tf_op jit(solution)/shard_map/ppermute | solution.py:197
  372.0 5.7 shard_map.332
  384.1 19.0 %collective-permute-done.31 = bf16[352,2048]{1,0:T(8,128)(2,1)S(1)} collective-permute-done((bf16[352,2048]{1,0:T(8,128)(2,1)S(1)}, bf16[352,2048]{1,0:T(8,128)(2,1)S(1)}, u32[]{:S(2)}, u32[]{:S(2)}) %collective-permute-start.31) | collective-permute-done | bytes 1441824 | tf_op jit(solution)/shard_map/ppermute | solution.py:197
  406.6 5.8 shard_map.333
  413.7 5.5 collective-permute-start.39
  419.2 5.3 shard_map.334
  424.5 6.9 shard_map.335
  431.5 5.2 convolution_add_fusion.2
  443.0 5.9 collective-permute-done.39
  448.9 24.7 %collective-permute-done.40 = bf16[352,2048]{1,0:T(8,128)(2,1)S(1)} collective-permute-done((bf16[352,2048]{1,0:T(8,128)(2,1)S(1)}, bf16[352,2048]{1,0:T(8,128)(2,1)S(1)}, u32[]{:S(2)}, u32[]{:S(2)}) %collective-permute-start.40) | collective-permute-done | bytes 1441824 | tf_op jit(solution)/shard_map/ppermute | solution.py:200
  477.1 6.9 collective-permute-start.43
  488.0 5.7 shard_map.336
  497.9 14.8 %collective-permute-done.43 = bf16[256,2816]{1,0:T(8,128)(2,1)S(1)} collective-permute-done((bf16[256,2816]{1,0:T(8,128)(2,1)S(1)}, bf16[256,2816]{1,0:T(8,128)(2,1)S(1)}, u32[]{:S(2)}, u32[]{:S(2)}) %collective-permute-start.43) | collective-permute-done | bytes 1441824 | tf_op jit(solution)/shard_map/ppermute | solution.py:197
  534.8 5.4 shard_map.338
  540.3 5.5 shard_map.339
  548.6 13.0 %collective-permute-done.48 = bf16[256,2816]{1,0:T(8,128)(2,1)} collective-permute-done((bf16[256,2816]{1,0:T(8,128)(2,1)}, bf16[256,2816]{1,0:T(8,128)(2,1)}, u32[]{:S(2)}, u32[]{:S(2)}) %collective-permute-start.48) | collective-permute-done | bytes 1441824 | tf_op jit(solution)/shard_map/ppermute | solution.py:192
  575.1 13.2 %collective-permute-done.56 = bf16[1,1,768,512]{3,2,1,0:T(8,128)(2,1)S(1)} collective-permute-done((bf16[1,1,768,512]{3,2,1,0:T(8,128)(2,1)S(1)}, bf16[1,1,768,512]{3,2,1,0:T(8,128)(2,1)S(1)}, u32[]{:S(2)}, u32[]{:S(2)}) %collective-permute-start.56) | collective-permute-done | bytes 786464 | tf_op jit(solution)/shard_map/ppermute | solution.py:61
  593.2 7.6 shard_map.341
  608.0 19.4 %collective-permute-done.62 = bf16[128,2048]{1,0:T(8,128)(2,1)S(1)} collective-permute-done((bf16[128,2048]{1,0:T(8,128)(2,1)S(1)}, bf16[128,2048]{1,0:T(8,128)(2,1)S(1)}, u32[]{:S(2)}, u32[]{:S(2)}) %collective-permute-start.62) | collective-permute-done | bytes 524320 | tf_op jit(solution)/shard_map/ppermute | solution.py:242
  627.6 8.1 shard_map.342
  641.1 9.1 %shard_map.343 = bf16[3,2,2,256,1024]{4,3,2,1,0:T(8,128)(2,1)} custom-call(s32[4]{0:T(128)S(1)} %pad_add_fusion.1.bits_ref, bf16[2,1,768,512]{3,2,1,0:T(8,128)(2,1)S(1)} %pad_maximum_fusion.1.own0_ref, bf16[2,1,768,512]{3,2,1,0:T(8,128)(2,1)S(1)} %collective-permute-done.60.got0_ref, bf16[1,2,768,512]{3,2,1,0:T(8,128)(2,1)S(1)} %pad_maximum_fusion.2.own1_ref, ...), custom_call_target="tpu_custom_call" | custom-call | flops 1024 | bytes 1024 | tf_op jit(solution)/shard_map/pallas_call | solution.py:418
  660.6 13.5 %collective-permute-done.58 = bf16[256,2816]{1,0:T(8,128)(2,1)} collective-permute-done((bf16[256,2816]{1,0:T(8,128)(2,1)S(1)}, bf16[256,2816]{1,0:T(8,128)(2,1)}, u32[]{:S(2)}, u32[]{:S(2)}) %collective-permute-start.58) | collective-permute-done | bytes 1441824 | tf_op jit(solution)/shard_map/ppermute | solution.py:200
  705.0 13.9 %collective-permute-done.71 = bf16[256,1024]{1,0:T(8,128)(2,1)} collective-permute-done((bf16[256,1024]{1,0:T(8,128)(2,1)}, bf16[256,1024]{1,0:T(8,128)(2,1)}, u32[]{:S(2)}, u32[]{:S(2)}) %collective-permute-start.71) | collective-permute-done | bytes 524320 | tf_op jit(solution)/shard_map/ppermute | solution.py:242
  723.6 25.3 %collective-permute-done.63 = bf16[256,2816]{1,0:T(8,128)(2,1)} collective-permute-done((bf16[256,2816]{1,0:T(8,128)(2,1)}, bf16[256,2816]{1,0:T(8,128)(2,1)}, u32[]{:S(2)}, u32[]{:S(2)}) %collective-permute-start.63) | collective-permute-done | bytes 1441824 | tf_op jit(solution)/shard_map/ppermute | solution.py:200
  749.0 13.9 %shard_map.344 = (f32[256,11264]{1,0:T(8,128)}, f32[256,11264]{1,0:T(8,128)}, f32[256,11264]{1,0:T(8,128)}) custom-call(s32[1]{0:T(128)} %bitcast.8.core_ref, f32[256,11264]{1,0:T(8,128)} %w_ref.11, f32[256,11264]{1,0:T(8,128)} %m_ref.5, f32[256,11264]{1,0:T(8,128)} %v_ref.5, bf16[256,2816]{1,0:T(8,128)(2,1)S(1)} %broadcast_select_fusion.3.refs_0_, ...), custom_call_target="tpu_custom_call" | custom-call | flops 1024 | bytes 1024 | tf_op jit(solution)/shard_map/pallas_call | solution.py:505
  785.9 10.4 %all-to-all-done.1 = f32[8,256,128]{2,1,0:T(8,128)S(1)} async-done(((f32[8,256,128]{2,1,0:T(8,128)}), f32[8,256,128]{2,1,0:T(8,128)S(1)}, u32[]{:S(2)}, u32[]{:S(2)}) %all-to-all-start.1) | async-done | bytes 1048608 | tf_op jit(solution)/shard_map/all_to_all | solution.py:1077
  796.6 11.3 %collective-permute-done.74 = bf16[256,1024]{1,0:T(8,128)(2,1)} collective-permute-done((bf16[256,1024]{1,0:T(8,128)(2,1)}, bf16[256,1024]{1,0:T(8,128)(2,1)}, u32[]{:S(2)}, u32[]{:S(2)}) %collective-permute-start.74) | collective-permute-done | bytes 524320 | tf_op jit(solution)/shard_map/ppermute | solution.py:242
  810.1 14.2 %shard_map.347 = (f32[256,11264]{1,0:T(8,128)}, f32[256,11264]{1,0:T(8,128)}, f32[256,11264]{1,0:T(8,128)}) custom-call(s32[1]{0:T(128)} %bitcast.8.core_ref, f32[256,11264]{1,0:T(8,128)} %w_ref.11, f32[256,11264]{1,0:T(8,128)} %m_ref.5, f32[256,11264]{1,0:T(8,128)} %v_ref.5, ...), custom_call_target="tpu_custom_call", output_to_operand_aliasing={{0}: (6, {}), {1}: (7, {}), {2}: (8, {})} | custom-call | flops 1024 | bytes 1024 | tf_op jit(solution)/shard_map/pallas_call | solution.py:505
  830.1 6.2 shard_map.348
  836.3 17.1 %collective-permute-done.79 = bf16[256,1024]{1,0:T(8,128)(2,1)S(1)} collective-permute-done((bf16[256,1024]{1,0:T(8,128)(2,1)S(1)}, bf16[256,1024]{1,0:T(8,128)(2,1)S(1)}, u32[]{:S(2)}, u32[]{:S(2)}) %collective-permute-start.79) | collective-permute-done | bytes 524320 | tf_op jit(solution)/shard_map/ppermute | solution.py:242
  855.7 6.3 shard_map.349
  862.0 8.8 all_to_all.20
  878.9 7.5 all-to-all-done.2
  887.5 6.2 shard_map.350
  (661 shorter events, 385.9 us)
Async XLA Ops:
  24.2 191.6 %all-gather.3.cloned.1.call-start = ((), (), s32[]{:S(2)}) async-start(), calls=%async_computation.6 | async-start | bytes 4718592 | tf_op jit(solution)/shard_map/all_gather | solution.py:685
  46.2 36.8 %collective-permute-start.3 = (bf16[1536,512]{1,0:T(8,128)(2,1)}, bf16[1536,512]{1,0:T(8,128)(2,1)}, u32[]{:S(2)}, u32[]{:S(2)}) collective-permute-start(bf16[1536,512]{1,0:T(8,128)(2,1)} %convolution_convert_fusion.7), channel_id=1, source_target_pairs={{0,1},{1,0},{2,3},{3,2},{4,5},{5,4},{6,7},{7,6},{8,9},{9,8},{10,11... | collective-permute-start | bytes 4718600 | tf_op jit(solution)/shard_map/ppermute | solution.py:62
  49.3 40.1 %collective-permute-start.5 = (bf16[1536,512]{1,0:T(8,128)(2,1)}, bf16[1536,512]{1,0:T(8,128)(2,1)}, u32[]{:S(2)}, u32[]{:S(2)}) collective-permute-start(bf16[1536,512]{1,0:T(8,128)(2,1)} %convolution_convert_fusion.6), channel_id=1, source_target_pairs={{0,4},{2,6},{4,0},{6,2},{1,5},{3,7},{5,1},{7,3},{8,12},{10,14},{12... | collective-permute-start | bytes 4718600 | tf_op jit(solution)/shard_map/ppermute | solution.py:61
  95.2 22.1 %collective-permute-start.7 = (bf16[768,512]{1,0:T(8,128)(2,1)}, bf16[768,512]{1,0:T(8,128)(2,1)}, u32[]{:S(2)}, u32[]{:S(2)}) collective-permute-start(bf16[768,512]{1,0:T(8,128)(2,1)} %get-tuple-element.485), channel_id=1, source_target_pairs={{0,1},{1,0},{2,3},{3,2},{4,5},{5,4},{6,7},{7,6},{8,9},{9,8},{10,11... | collective-permute-start | bytes 2359304 | tf_op jit(solution)/shard_map/ppermute | solution.py:62
  129.3 695.0 %reduce-scatter.2.cloned.1.call-start = ((), (), s32[]{:S(2)}) async-start(), calls=%async_computation.5 | async-start | bytes 4718592 | tf_op jit(solution)/shard_map/reduce_scatter | solution.py:1037
  189.7 69.1 %collective-permute-start.19 = (bf16[1408,1024]{1,0:T(8,128)(2,1)}, bf16[1408,1024]{1,0:T(8,128)(2,1)}, u32[]{:S(2)}, u32[]{:S(2)}) collective-permute-start(bf16[1408,1024]{1,0:T(8,128)(2,1)} %convolution_convert_fusion.3), channel_id=1, source_target_pairs={{0,1},{1,0},{2,3},{3,2},{4,5},{5,4},{6,7},{7,6},{8,9},{9,8},{10,11... | collective-permute-start | bytes 8650760 | tf_op jit(solution)/shard_map/ppermute | solution.py:62
  193.7 69.6 %collective-permute-start.23 = (bf16[1408,1024]{1,0:T(8,128)(2,1)}, bf16[1408,1024]{1,0:T(8,128)(2,1)}, u32[]{:S(2)}, u32[]{:S(2)}) collective-permute-start(bf16[1408,1024]{1,0:T(8,128)(2,1)} %convolution_convert_fusion.2), channel_id=1, source_target_pairs={{0,4},{2,6},{4,0},{6,2},{1,5},{3,7},{5,1},{7,3},{8,12},{10,14},{12... | collective-permute-start | bytes 8650760 | tf_op jit(solution)/shard_map/ppermute | solution.py:61
  195.2 59.8 %collective-permute-start.20 = (f32[4,2,1,704]{3,0,2,1:T(4,128)S(1)}, f32[4,2,1,704]{3,0,2,1:T(4,128)S(1)}, u32[]{:S(2)}, u32[]{:S(2)}) collective-permute-start(f32[4,2,1,704]{3,0,2,1:T(4,128)S(1)} %get-tuple-element.943), channel_id=1, source_target_pairs={{0,1},{1,0},{2,3},{3,2},{4,5},{5,4},{6,7},{7,6},{8,9},{9,8},{10,11... | collective-permute-start | bytes 67592 | tf_op jit(solution)/shard_map/ppermute | solution.py:62
  261.8 32.4 %collective-permute-start.22 = (bf16[704,1024]{1,0:T(8,128)(2,1)S(1)}, bf16[704,1024]{1,0:T(8,128)(2,1)S(1)}, u32[]{:S(2)}, u32[]{:S(2)}) collective-permute-start(bf16[704,1024]{1,0:T(8,128)(2,1)S(1)} %get-tuple-element.578), channel_id=1, source_target_pairs={{0,4},{2,6},{4,0},{6,2},{1,5},{3,7},{5,1},{7,3},{8,12},{10,14},{12... | collective-permute-start | bytes 4325384 | tf_op jit(solution)/shard_map/ppermute | solution.py:61
  267.2 32.1 %collective-permute-start.24 = (bf16[704,1024]{1,0:T(8,128)(2,1)S(1)}, bf16[704,1024]{1,0:T(8,128)(2,1)S(1)}, u32[]{:S(2)}, u32[]{:S(2)}) collective-permute-start(bf16[704,1024]{1,0:T(8,128)(2,1)S(1)} %get-tuple-element.582), channel_id=1, source_target_pairs={{0,1},{1,0},{2,3},{3,2},{4,5},{5,4},{6,7},{7,6},{8,9},{9,8},{10,11... | collective-permute-start | bytes 4325384 | tf_op jit(solution)/shard_map/ppermute | solution.py:62
  324.6 31.5 %collective-permute-start.30 = (bf16[352,2048]{1,0:T(8,128)(2,1)S(1)}, bf16[352,2048]{1,0:T(8,128)(2,1)S(1)}, u32[]{:S(2)}, u32[]{:S(2)}) collective-permute-start(bf16[352,2048]{1,0:T(8,128)(2,1)S(1)} %get-tuple-element.604), channel_id=1, source_target_pairs={{0,8},{24,16},{1,9},{25,17},{2,10},{26,18},{3,11},{27,19},{4,12},{... | collective-permute-start | bytes 4325384 | tf_op jit(solution)/shard_map/ppermute | solution.py:197
  329.8 30.1 %collective-permute-start.28 = (bf16[2,1,704,512]{3,2,1,0:T(8,128)(2,1)S(1)}, bf16[2,1,704,512]{3,2,1,0:T(8,128)(2,1)S(1)}, u32[]{:S(2)}, u32[]{:S(2)}) collective-permute-start(bf16[2,1,704,512]{3,2,1,0:T(8,128)(2,1)S(1)} %pad_maximum_fusion.3.own0_ref), channel_id=1, source_target_pairs={{0,1},{1,0},{2,3},{3,2},{4,5},{5,4},{6,7},{7,6},{8,9},{9,8},{10,11... | collective-permute-start | bytes 4325384 | tf_op jit(solution)/shard_map/ppermute | solution.py:62
  331.1 30.1 %collective-permute-start.29 = (bf16[1,2,704,512]{3,2,1,0:T(8,128)(2,1)S(1)}, bf16[1,2,704,512]{3,2,1,0:T(8,128)(2,1)S(1)}, u32[]{:S(2)}, u32[]{:S(2)}) collective-permute-start(bf16[1,2,704,512]{3,2,1,0:T(8,128)(2,1)S(1)} %pad_maximum_fusion.4.own1_ref), channel_id=1, source_target_pairs={{0,4},{2,6},{4,0},{6,2},{1,5},{3,7},{5,1},{7,3},{8,12},{10,14},{12... | collective-permute-start | bytes 4325384 | tf_op jit(solution)/shard_map/ppermute | solution.py:61
  332.3 32.4 %collective-permute-start.32 = (f32[2,1024]{1,0:T(2,128)S(1)}, f32[2,1024]{1,0:T(2,128)S(1)}, u32[]{:S(2)}, u32[]{:S(2)}) collective-permute-start(f32[2,1024]{1,0:T(2,128)S(1)} %add.396), channel_id=1, source_target_pairs={{0,4},{2,6},{4,0},{6,2},{1,5},{3,7},{5,1},{7,3},{8,12},{10,14},{12... | collective-permute-start | bytes 24584 | tf_op jit(solution)/shard_map/ppermute | solution.py:61
  366.9 36.2 %collective-permute-start.34 = (bf16[352,2048]{1,0:T(8,128)(2,1)S(1)}, bf16[352,2048]{1,0:T(8,128)(2,1)S(1)}, u32[]{:S(2)}, u32[]{:S(2)}) collective-permute-start(bf16[352,2048]{1,0:T(8,128)(2,1)S(1)} %reduce-precision_convert_fusion.11), channel_id=1, source_target_pairs={{8,16},{16,8},{9,17},{17,9},{10,18},{18,10},{11,19},{19,11},{12,20... | collective-permute-start | bytes 4325384 | tf_op jit(solution)/shard_map/ppermute | solution.py:203
  367.7 35.5 %collective-permute-start.31 = (bf16[352,2048]{1,0:T(8,128)(2,1)S(1)}, bf16[352,2048]{1,0:T(8,128)(2,1)S(1)}, u32[]{:S(2)}, u32[]{:S(2)}) collective-permute-start(bf16[352,2048]{1,0:T(8,128)(2,1)S(1)} %get-tuple-element.623), channel_id=1, source_target_pairs={{0,8},{24,16},{1,9},{25,17},{2,10},{26,18},{3,11},{27,19},{4,12},{... | collective-permute-start | bytes 4325384 | tf_op jit(solution)/shard_map/ppermute | solution.py:197
  379.3 45.2 %collective-permute-start.37 = (bf16[2,1,704,512]{3,2,1,0:T(8,128)(2,1)S(1)}, bf16[2,1,704,512]{3,2,1,0:T(8,128)(2,1)}, u32[]{:S(2)}, u32[]{:S(2)}) collective-permute-start(bf16[2,1,704,512]{3,2,1,0:T(8,128)(2,1)S(1)} %pad_maximum_fusion.5.own0_ref), channel_id=1, source_target_pairs={{0,1},{1,0},{2,3},{3,2},{4,5},{5,4},{6,7},{7,6},{8,9},{9,8},{10,11... | collective-permute-start | bytes 4325384 | tf_op jit(solution)/shard_map/ppermute | solution.py:62
  381.7 42.8 %collective-permute-start.38 = (bf16[1,2,704,512]{3,2,1,0:T(8,128)(2,1)}, bf16[1,2,704,512]{3,2,1,0:T(8,128)(2,1)}, u32[]{:S(2)}, u32[]{:S(2)}) collective-permute-start(bf16[1,2,704,512]{3,2,1,0:T(8,128)(2,1)} %pad_maximum_fusion.6.own1_ref), channel_id=1, source_target_pairs={{0,4},{2,6},{4,0},{6,2},{1,5},{3,7},{5,1},{7,3},{8,12},{10,14},{12... | collective-permute-start | bytes 4325384 | tf_op jit(solution)/shard_map/ppermute | solution.py:61
  413.7 35.2 %collective-permute-start.39 = (bf16[256,2816]{1,0:T(8,128)(2,1)}, bf16[256,2816]{1,0:T(8,128)(2,1)}, u32[]{:S(2)}, u32[]{:S(2)}) collective-permute-start(bf16[256,2816]{1,0:T(8,128)(2,1)} %get-tuple-element.648), channel_id=1, source_target_pairs={{0,8},{24,16},{1,9},{25,17},{2,10},{26,18},{3,11},{27,19},{4,12},{... | collective-permute-start | bytes 4325384 | tf_op jit(solution)/shard_map/ppermute | solution.py:197
  439.0 34.6 %collective-permute-start.40 = (bf16[352,2048]{1,0:T(8,128)(2,1)S(1)}, bf16[352,2048]{1,0:T(8,128)(2,1)S(1)}, u32[]{:S(2)}, u32[]{:S(2)}) collective-permute-start(bf16[352,2048]{1,0:T(8,128)(2,1)S(1)} %reduce-precision_convert_fusion.9), channel_id=1, source_target_pairs={{8,0},{16,24},{9,1},{17,25},{10,2},{18,26},{11,3},{19,27},{12,4},{... | collective-permute-start | bytes 4325384 | tf_op jit(solution)/shard_map/ppermute | solution.py:200
  440.3 33.3 %collective-permute-start.41 = (bf16[352,2048]{1,0:T(8,128)(2,1)S(1)}, bf16[352,2048]{1,0:T(8,128)(2,1)S(1)}, u32[]{:S(2)}, u32[]{:S(2)}) collective-permute-start(bf16[352,2048]{1,0:T(8,128)(2,1)S(1)} %copy-done.100), channel_id=1, source_target_pairs={{8,16},{16,8},{9,17},{17,9},{10,18},{18,10},{11,19},{19,11},{12,20... | collective-permute-start | bytes 4325384 | tf_op jit(solution)/shard_map/ppermute | solution.py:203
  476.3 41.2 %collective-permute-start.45 = (bf16[256,2816]{1,0:T(8,128)(2,1)S(1)}, bf16[256,2816]{1,0:T(8,128)(2,1)S(1)}, u32[]{:S(2)}, u32[]{:S(2)}) collective-permute-start(bf16[256,2816]{1,0:T(8,128)(2,1)S(1)} %reduce-precision_convert_fusion.8), channel_id=1, source_target_pairs={{8,16},{16,8},{9,17},{17,9},{10,18},{18,10},{11,19},{19,11},{12,20... | collective-permute-start | bytes 4325384 | tf_op jit(solution)/shard_map/ppermute | solution.py:203
  477.1 35.5 %collective-permute-start.43 = (bf16[256,2816]{1,0:T(8,128)(2,1)S(1)}, bf16[256,2816]{1,0:T(8,128)(2,1)S(1)}, u32[]{:S(2)}, u32[]{:S(2)}) collective-permute-start(bf16[256,2816]{1,0:T(8,128)(2,1)S(1)} %copy-done.101), channel_id=1, source_target_pairs={{0,8},{24,16},{1,9},{25,17},{2,10},{26,18},{3,11},{27,19},{4,12},{... | collective-permute-start | bytes 4325384 | tf_op jit(solution)/shard_map/ppermute | solution.py:197
  484.6 32.9 %collective-permute-start.44 = (bf16[352,2048]{1,0:T(8,128)(2,1)S(1)}, bf16[352,2048]{1,0:T(8,128)(2,1)S(1)}, u32[]{:S(2)}, u32[]{:S(2)}) collective-permute-start(bf16[352,2048]{1,0:T(8,128)(2,1)S(1)} %reduce-precision_convert_fusion.7), channel_id=1, source_target_pairs={{8,0},{16,24},{9,1},{17,25},{10,2},{18,26},{11,3},{19,27},{12,4},{... | collective-permute-start | bytes 4325384 | tf_op jit(solution)/shard_map/ppermute | solution.py:200
  495.5 24.0 %collective-permute-start.50 = (bf16[2,1,256,512]{3,2,1,0:T(8,128)(2,1)S(1)}, bf16[2,1,256,512]{3,2,1,0:T(8,128)(2,1)S(1)}, u32[]{:S(2)}, u32[]{:S(2)}) collective-permute-start(bf16[2,1,256,512]{3,2,1,0:T(8,128)(2,1)S(1)} %pad_maximum_fusion.8.own0_ref), channel_id=1, source_target_pairs={{0,1},{1,0},{2,3},{3,2},{4,5},{5,4},{6,7},{7,6},{8,9},{9,8},{10,11... | collective-permute-start | bytes 1572872 | tf_op jit(solution)/shard_map/ppermute | solution.py:62
  496.4 23.1 %collective-permute-start.51 = (bf16[1,2,256,512]{3,2,1,0:T(8,128)(2,1)S(1)}, bf16[1,2,256,512]{3,2,1,0:T(8,128)(2,1)S(1)}, u32[]{:S(2)}, u32[]{:S(2)}) collective-permute-start(bf16[1,2,256,512]{3,2,1,0:T(8,128)(2,1)S(1)} %pad_maximum_fusion.10.own1_ref), channel_id=1, source_target_pairs={{0,4},{2,6},{4,0},{6,2},{1,5},{3,7},{5,1},{7,3},{8,12},{10,14},{12... | collective-permute-start | bytes 1572872 | tf_op jit(solution)/shard_map/ppermute | solution.py:61
  523.4 38.3 %collective-permute-start.49 = (bf16[256,2816]{1,0:T(8,128)(2,1)}, bf16[256,2816]{1,0:T(8,128)(2,1)}, u32[]{:S(2)}, u32[]{:S(2)}) collective-permute-start(bf16[256,2816]{1,0:T(8,128)(2,1)} %reduce-precision_convert_fusion.5), channel_id=1, source_target_pairs={{8,16},{16,8},{9,17},{17,9},{10,18},{18,10},{11,19},{19,11},{12,20... | collective-permute-start | bytes 4325384 | tf_op jit(solution)/shard_map/ppermute | solution.py:203
  526.9 34.7 %collective-permute-start.48 = (bf16[256,2816]{1,0:T(8,128)(2,1)}, bf16[256,2816]{1,0:T(8,128)(2,1)}, u32[]{:S(2)}, u32[]{:S(2)}) collective-permute-start(bf16[256,2816]{1,0:T(8,128)(2,1)} %fusion), channel_id=1, source_target_pairs={{0,8},{8,0},{16,24},{24,16},{1,9},{9,1},{17,25},{25,17},{2,10},{10... | collective-permute-start | bytes 4325384 | tf_op jit(solution)/shard_map/ppermute | solution.py:192
  547.8 42.5 %collective-permute-start.55 = (bf16[128,2048]{1,0:T(8,128)(2,1)S(1)}, bf16[128,2048]{1,0:T(8,128)(2,1)S(1)}, u32[]{:S(2)}, u32[]{:S(2)}) collective-permute-start(bf16[128,2048]{1,0:T(8,128)(2,1)S(1)} %get-tuple-element.924), channel_id=1, source_target_pairs={{0,8},{8,0},{16,24},{24,16},{1,9},{9,1},{17,25},{25,17},{2,10},{10... | collective-permute-start | bytes 1572872 | tf_op jit(solution)/shard_map/ppermute | solution.py:242
  565.4 39.7 %collective-permute-start.53 = (bf16[256,2816]{1,0:T(8,128)(2,1)}, bf16[256,2816]{1,0:T(8,128)(2,1)S(1)}, u32[]{:S(2)}, u32[]{:S(2)}) collective-permute-start(bf16[256,2816]{1,0:T(8,128)(2,1)} %fusion.1), channel_id=1, source_target_pairs={{0,8},{8,0},{16,24},{24,16},{1,9},{9,1},{17,25},{25,17},{2,10},{10... | collective-permute-start | bytes 4325384 | tf_op jit(solution)/shard_map/ppermute | solution.py:192
  568.3 37.3 %collective-permute-start.54 = (bf16[256,2816]{1,0:T(8,128)(2,1)S(1)}, bf16[256,2816]{1,0:T(8,128)(2,1)}, u32[]{:S(2)}, u32[]{:S(2)}) collective-permute-start(bf16[256,2816]{1,0:T(8,128)(2,1)S(1)} %reduce-precision_convert_fusion.3), channel_id=1, source_target_pairs={{8,16},{16,8},{9,17},{17,9},{10,18},{18,10},{11,19},{19,11},{12,20... | collective-permute-start | bytes 4325384 | tf_op jit(solution)/shard_map/ppermute | solution.py:203
  588.4 160.6 %collective-permute-start.73 = (bf16[256,2816]{1,0:T(8,128)(2,1)}, bf16[256,2816]{1,0:T(8,128)(2,1)}, u32[]{:S(2)}, u32[]{:S(2)}) collective-permute-start(bf16[256,2816]{1,0:T(8,128)(2,1)} %broadcast_select_fusion.2), channel_id=1, source_target_pairs={{0,2},{2,0},{4,6},{6,4},{1,3},{3,1},{5,7},{7,5},{8,10},{10,8},{12,... | collective-permute-start | bytes 4325384 | tf_op jit(solution)/shard_map/ppermute | solution.py:57
  589.0 48.5 %collective-permute-start.60 = (bf16[2,1,768,512]{3,2,1,0:T(8,128)(2,1)S(1)}, bf16[2,1,768,512]{3,2,1,0:T(8,128)(2,1)S(1)}, u32[]{:S(2)}, u32[]{:S(2)}) collective-permute-start(bf16[2,1,768,512]{3,2,1,0:T(8,128)(2,1)S(1)} %pad_maximum_fusion.1.own0_ref), channel_id=1, source_target_pairs={{0,1},{1,0},{2,3},{3,2},{4,5},{5,4},{6,7},{7,6},{8,9},{9,8},{10,11... | collective-permute-start | bytes 4718600 | tf_op jit(solution)/shard_map/ppermute | solution.py:62
  590.5 36.9 %collective-permute-start.62 = (bf16[128,2048]{1,0:T(8,128)(2,1)S(1)}, bf16[128,2048]{1,0:T(8,128)(2,1)S(1)}, u32[]{:S(2)}, u32[]{:S(2)}) collective-permute-start(bf16[128,2048]{1,0:T(8,128)(2,1)S(1)} %reduce-precision_convert_fusion.19), channel_id=1, source_target_pairs={{0,16},{8,24},{16,0},{24,8},{1,17},{9,25},{17,1},{25,9},{2,18},{10... | collective-permute-start | bytes 1572872 | tf_op jit(solution)/shard_map/ppermute | solution.py:242
  605.1 36.1 %collective-permute-start.61 = (bf16[1,2,768,512]{3,2,1,0:T(8,128)(2,1)S(1)}, bf16[1,2,768,512]{3,2,1,0:T(8,128)(2,1)}, u32[]{:S(2)}, u32[]{:S(2)}) collective-permute-start(bf16[1,2,768,512]{3,2,1,0:T(8,128)(2,1)S(1)} %pad_maximum_fusion.2.own1_ref), channel_id=1, source_target_pairs={{0,4},{2,6},{4,0},{6,2},{1,5},{3,7},{5,1},{7,3},{8,12},{10,14},{12... | collective-permute-start | bytes 4718600 | tf_op jit(solution)/shard_map/ppermute | solution.py:61
  606.2 67.9 %collective-permute-start.59 = (bf16[256,2816]{1,0:T(8,128)(2,1)S(1)}, bf16[256,2816]{1,0:T(8,128)(2,1)}, u32[]{:S(2)}, u32[]{:S(2)}) collective-permute-start(bf16[256,2816]{1,0:T(8,128)(2,1)S(1)} %reduce-precision_convert_fusion.1), channel_id=1, source_target_pairs={{8,16},{16,8},{9,17},{17,9},{10,18},{18,10},{11,19},{19,11},{12,20... | collective-permute-start | bytes 4325384 | tf_op jit(solution)/shard_map/ppermute | solution.py:203
  627.5 57.6 %collective-permute-start.65 = (bf16[128,2048]{1,0:T(8,128)(2,1)S(1)}, bf16[128,2048]{1,0:T(8,128)(2,1)}, u32[]{:S(2)}, u32[]{:S(2)}) collective-permute-start(bf16[128,2048]{1,0:T(8,128)(2,1)S(1)} %reduce-precision_convert_fusion.18), channel_id=1, source_target_pairs={{0,8},{8,0},{16,24},{24,16},{1,9},{9,1},{17,25},{25,17},{2,10},{10... | collective-permute-start | bytes 1572872 | tf_op jit(solution)/shard_map/ppermute | solution.py:242
  637.5 36.5 %collective-permute-start.58 = (bf16[256,2816]{1,0:T(8,128)(2,1)S(1)}, bf16[256,2816]{1,0:T(8,128)(2,1)}, u32[]{:S(2)}, u32[]{:S(2)}) collective-permute-start(bf16[256,2816]{1,0:T(8,128)(2,1)S(1)} %reduce-precision_convert_fusion.2), channel_id=1, source_target_pairs={{8,0},{16,24},{9,1},{17,25},{10,2},{18,26},{11,3},{19,27},{12,4},{... | collective-permute-start | bytes 4325384 | tf_op jit(solution)/shard_map/ppermute | solution.py:200
  655.3 27.6 %collective-permute-start.66 = (bf16[256,1024]{1,0:T(8,128)(2,1)S(1)}, bf16[256,1024]{1,0:T(8,128)(2,1)S(1)}, u32[]{:S(2)}, u32[]{:S(2)}) collective-permute-start(bf16[256,1024]{1,0:T(8,128)(2,1)S(1)} %get-tuple-element.922), channel_id=1, source_target_pairs={{0,8},{8,0},{16,24},{24,16},{1,9},{9,1},{17,25},{25,17},{2,10},{10... | collective-permute-start | bytes 1572872 | tf_op jit(solution)/shard_map/ppermute | solution.py:242
  682.9 36.0 %collective-permute-start.71 = (bf16[256,1024]{1,0:T(8,128)(2,1)}, bf16[256,1024]{1,0:T(8,128)(2,1)}, u32[]{:S(2)}, u32[]{:S(2)}) collective-permute-start(bf16[256,1024]{1,0:T(8,128)(2,1)} %get-tuple-element.918), channel_id=1, source_target_pairs={{0,8},{8,0},{16,24},{24,16},{1,9},{9,1},{17,25},{25,17},{2,10},{10... | collective-permute-start | bytes 1572872 | tf_op jit(solution)/shard_map/ppermute | solution.py:242
  685.1 63.8 %collective-permute-start.63 = (bf16[256,2816]{1,0:T(8,128)(2,1)}, bf16[256,2816]{1,0:T(8,128)(2,1)}, u32[]{:S(2)}, u32[]{:S(2)}) collective-permute-start(bf16[256,2816]{1,0:T(8,128)(2,1)} %reduce-precision_convert_fusion), channel_id=1, source_target_pairs={{8,0},{16,24},{9,1},{17,25},{10,2},{18,26},{11,3},{19,27},{12,4},{... | collective-permute-start | bytes 4325384 | tf_op jit(solution)/shard_map/ppermute | solution.py:200
  693.7 69.2 %collective-permute-start.76 = (bf16[256,1024]{1,0:T(8,128)(2,1)}, bf16[256,1024]{1,0:T(8,128)(2,1)}, u32[]{:S(2)}, u32[]{:S(2)}) collective-permute-start(bf16[256,1024]{1,0:T(8,128)(2,1)} %reduce-precision_convert_fusion.17), channel_id=1, source_target_pairs={{0,16},{8,24},{16,0},{24,8},{1,17},{9,25},{17,1},{25,9},{2,18},{10... | collective-permute-start | bytes 1572872 | tf_op jit(solution)/shard_map/ppermute | solution.py:242
  703.7 106.4 %collective-permute-start.72 = (bf16[256,2816]{1,0:T(8,128)(2,1)}, bf16[256,2816]{1,0:T(8,128)(2,1)}, u32[]{:S(2)}, u32[]{:S(2)}) collective-permute-start(bf16[256,2816]{1,0:T(8,128)(2,1)} %broadcast_select_fusion.4), channel_id=1, source_target_pairs={{0,2},{2,0},{4,6},{6,4},{1,3},{3,1},{5,7},{7,5},{8,10},{10,8},{12,... | collective-permute-start | bytes 4325384 | tf_op jit(solution)/shard_map/ppermute | solution.py:57
  718.9 46.2 %collective-permute-start.75 = (f32[7,256]{1,0:T(8,128)}, f32[7,256]{1,0:T(8,128)S(1)}, u32[]{:S(2)}, u32[]{:S(2)}) collective-permute-start(f32[7,256]{1,0:T(8,128)} %concatenate.107), channel_id=1, source_target_pairs={{0,8},{8,0},{16,24},{24,16},{1,9},{9,1},{17,25},{25,17},{2,10},{10... | collective-permute-start | bytes 21512 | tf_op jit(solution)/shard_map/ppermute | solution.py:1090
  781.5 26.5 %collective-permute-start.74 = (bf16[256,1024]{1,0:T(8,128)(2,1)}, bf16[256,1024]{1,0:T(8,128)(2,1)}, u32[]{:S(2)}, u32[]{:S(2)}) collective-permute-start(bf16[256,1024]{1,0:T(8,128)(2,1)} %reduce-precision_convert_fusion.16), channel_id=1, source_target_pairs={{0,16},{8,24},{16,0},{24,8},{1,17},{9,25},{17,1},{25,9},{2,18},{10... | collective-permute-start | bytes 1572872 | tf_op jit(solution)/shard_map/ppermute | solution.py:242
  781.9 44.4 %collective-permute-start.80 = (bf16[256,1024]{1,0:T(8,128)(2,1)}, bf16[256,1024]{1,0:T(8,128)(2,1)}, u32[]{:S(2)}, u32[]{:S(2)}) collective-permute-start(bf16[256,1024]{1,0:T(8,128)(2,1)} %reduce-precision_convert_fusion.14), channel_id=1, source_target_pairs={{0,8},{8,0},{16,24},{24,16},{1,9},{9,1},{17,25},{25,17},{2,10},{10... | collective-permute-start | bytes 1572872 | tf_op jit(solution)/shard_map/ppermute | solution.py:242
  827.8 25.5 %collective-permute-start.79 = (bf16[256,1024]{1,0:T(8,128)(2,1)S(1)}, bf16[256,1024]{1,0:T(8,128)(2,1)S(1)}, u32[]{:S(2)}, u32[]{:S(2)}) collective-permute-start(bf16[256,1024]{1,0:T(8,128)(2,1)S(1)} %copy-done.110), channel_id=1, source_target_pairs={{0,16},{8,24},{16,0},{24,8},{1,17},{9,25},{17,1},{25,9},{2,18},{10... | collective-permute-start | bytes 1572872 | tf_op jit(solution)/shard_map/ppermute | solution.py:242
  827.9 25.7 %collective-permute-start.78 = (bf16[256,1024]{1,0:T(8,128)(2,1)S(1)}, bf16[256,1024]{1,0:T(8,128)(2,1)S(1)}, u32[]{:S(2)}, u32[]{:S(2)}) collective-permute-start(bf16[256,1024]{1,0:T(8,128)(2,1)S(1)} %copy-done.111), channel_id=1, source_target_pairs={{0,8},{8,0},{16,24},{24,16},{1,9},{9,1},{17,25},{25,17},{2,10},{10... | collective-permute-start | bytes 1572872 | tf_op jit(solution)/shard_map/ppermute | solution.py:242
  (185 other events, 1362.6 us)
Sparse Core Ops, SparseCore 0:
  129.5 48.4 all-gather.2
  521.7 50.4 reduce-scatter.1

commit v10 on v9

--- a/solution.py
+++ b/solution.py
@@ -132,77 +132,6 @@
 
 
 SMALL = pl.CostEstimate(flops=1024, bytes_accessed=1024, transcendentals=0)
-
-
-class RepSum:
-    def __init__(self, order):
-        self.order = order
-        z = lax.axis_index("rep")
-        self.end = (z == 0) | (z == lax.axis_size("rep") - 1)
-        self.queue = []
-        self.flight = []
-        self.depth = 1
-        self.done = {}
-
-    def push(self, name, g):
-        self.queue.append((name, g))
-
-    def busy(self):
-        return bool(self.queue or self.flight)
-
-    def tick(self):
-        old = {}
-        if len(self.flight) >= self.depth or (self.flight and not self.queue):
-            old = self.flight.pop(0)
-        new = self.queue.pop(0) if self.queue else None
-        values = {}
-        if "in" in old:
-            values["g"], values["g_got"] = old["in"][1], old["in_got"]
-        if "mid" in old:
-            values["s"], values["s_got"] = old["mid"][1], old["mid_got"]
-        if new:
-            values["new"] = new[1]
-        both = new and "mid" in old and new[1].shape == old["mid"][1].shape
-        if "out" in old:
-            values["out_got"] = old["out_got"]
-
-        def stage(v):
-            def add(a, b):
-                return lax.reduce_precision(a.astype(f32) + b.astype(f32), 8, 7).astype(bf16)
-
-            out = {}
-            if "g" in v:
-                out["a_sum"] = add(v["g"], v["g_got"])
-            if "s" in v:
-                total = add(v["s"], v["s_got"])
-                out["total"] = jnp.where(self.end, v["new"], total) if both else total
-            if "new" in v and not both:
-                out["new"] = v["new"]
-            if "out_got" in v:
-                out["z_got"] = v["out_got"]
-            return out
-
-        if not values:
-            return
-        out = self.order(stage, values)
-        if "out" in old:
-            self.done[old["out"][0]] = jnp.where(self.end, out["z_got"], old["out"][1])
-        slot = {}
-        if both:
-            got = lax.ppermute(out["total"], "rep", [(0, 1), (1, 0), (2, 3), (3, 2)])
-            slot = {"in": new, "in_got": got, "out": (old["mid"][0], out["total"]), "out_got": got}
-        else:
-            if new:
-                slot["in"] = new
-                slot["in_got"] = lax.ppermute(out["new"], "rep", [(0, 1), (3, 2)])
-            if "mid" in old:
-                slot["out"] = (old["mid"][0], out["total"])
-                slot["out_got"] = lax.ppermute(out["total"], "rep", [(1, 0), (2, 3)])
-        if "in" in old:
-            slot["mid"] = (old["in"][0], out["a_sum"])
-            slot["mid_got"] = lax.ppermute(out["a_sum"], "rep", [(1, 2), (2, 1)])
-        if slot:
-            self.flight.append(slot)
 
 
 def cast_kernel(w_ref, out_ref):
@@ -271,8 +200,8 @@
     u0_ref[...] = gup[:, :half]
     u1_ref[...] = gup[:, half:]
     a, b = ggate.astype(f32), gup.astype(f32)
-    e = jnp.sum(a * gains_ref[0] + b * gains_ref[2], axis=0, keepdims=True)
-    ez = jnp.sum(a * (gate - gains_ref[1]) + b * (up - gains_ref[3]), axis=0, keepdims=True)
+    e = jnp.sum(a * gains_ref[:, 0:1] + b * gains_ref[:, 2:3], axis=0, keepdims=True)
+    ez = jnp.sum(a * (gate - gains_ref[:, 1:2]) + b * (up - gains_ref[:, 3:4]), axis=0, keepdims=True)
     both = jnp.concatenate([e, ez], axis=0)
 
     @pl.when(pl.program_id(0) == 0)
@@ -293,7 +222,7 @@
     return pl.pallas_call(
         gated_kernel,
         grid=(n,),
-        in_specs=[whole] * 5 + [pl.BlockSpec((4, rows // n, 1), lambda i: (0, i, 0))],
+        in_specs=[whole] * 5 + [pl.BlockSpec((rows // n, 4), lambda i: (i, 0))],
         out_specs=[half] * 4 + [whole, pl.BlockSpec((2, t), lambda i: (0, 0))],
         out_shape=[out_half] * 4 + [jax.ShapeDtypeStruct((rows, t), bf16), jax.ShapeDtypeStruct((2, t), f32)],
         compiler_params=pltpu.CompilerParams(vmem_limit_bytes=56 * 1024 * 1024),
@@ -399,34 +328,6 @@
         compiler_params=pltpu.CompilerParams(vmem_limit_bytes=48 * 1024 * 1024),
         cost_estimate=SMALL,
     )(*((a, b) if add is None else (a, b, add)))
-
-
-def last_step_kernel(bits_ref, own0_ref, got0_ref, own1_ref, got1_ref, out_ref):
-    y, s = pl.program_id(1), pl.program_id(2)
-    half = own0_ref.shape[3]
-    ys, ss = bits_ref[2], bits_ref[3]
-    a = jnp.where(s // ss == bits_ref[1], own0_ref[0, 0], got0_ref[0, 0])
-    b = jnp.where(y // ys == bits_ref[0], own1_ref[0, 0], got1_ref[0, 0])
-    out_ref[0, 0, 0, :, :half] = a
-    out_ref[0, 0, 0, :, half:] = b
-
-
-def last_step(parts, got, bits, pre, y_size, s_size):
-    rows, half = parts[0].shape[2] // pre, parts[0].shape[3]
-    along_s = pl.BlockSpec((1, 1, rows, half), lambda p, y, s, bits: (y, s % (s_size // 2), p, 0))
-    along_y = pl.BlockSpec((1, 1, rows, half), lambda p, y, s, bits: (y % (y_size // 2), s, p, 0))
-    return pl.pallas_call(
-        last_step_kernel,
-        grid_spec=pltpu.PrefetchScalarGridSpec(
-            num_scalar_prefetch=1,
-            grid=(pre, y_size, s_size),
-            in_specs=[along_s, along_s, along_y, along_y],
-            out_specs=pl.BlockSpec((1, 1, 1, rows, 2 * half), lambda p, y, s, bits: (p, y, s, 0, 0)),
-        ),
-        out_shape=jax.ShapeDtypeStruct((pre, y_size, s_size, rows, 2 * half), bf16),
-        compiler_params=pltpu.CompilerParams(vmem_limit_bytes=48 * 1024 * 1024),
-        cost_estimate=SMALL,
-    )(bits, parts[0], got[0], parts[1], got[1])
 
 
 def stack_turned_kernel(a_ref, b_ref, out_ref):
@@ -631,7 +532,6 @@
 ):
     at = Plane()
     do = Order()
-    reps = RepSum(do)
     width = tokens.shape[3]
     rows = tokens.shape[1]
     S, Y, nb = at.s_size, at.y_size, at.blocks
@@ -682,7 +582,7 @@
         return jnp.concatenate([blocks, jnp.broadcast_to(extra[None], (nb, 16, rows))], axis=1)
 
     packed = do(pack, x_rows, order)
-    cot_all = lax.all_gather(cotangent.reshape(rows, width), ("shard", "ctx"), axis=0, tiled=True)
+    cot_all = lax.all_gather(do(cast, cotangent.reshape(rows, width)), ("shard", "ctx"), axis=0, tiled=True)
     got = lax.all_to_all(packed, plane, split_axis=0, concat_axis=0, tiled=True)
 
     def chip_rows(w, lead, unit, count):
@@ -785,9 +685,13 @@
             state["parts"] = do(put, state["parts"], state["got"])
 
         def result():
-            ys, ss = Y // 2, S // 2
-            bits = jnp.stack([at.y // ys, at.s // ss, jnp.int32(ys), jnp.int32(ss)]).astype(jnp.int32)
-            return do(lambda p, g: last_step(p, g, bits, pre, Y, S), state["parts"], state["got"])
+            finish()
+            return do(
+                lambda a, b: jnp.concatenate([a, b], axis=3)
+                .reshape(Y, S, pre, -1, T)
+                .transpose(2, 0, 1, 3, 4),
+                *state["parts"],
+            )
 
         return n, start, finish, result
 
@@ -861,7 +765,6 @@
     wd_own = do(cast, w_down)
     wg = do(stack_turned, *wg_parts)
     wu = do(stack_turned, *wu_parts)
-    cot_all = do(lambda c: c, cot_all)
     grad_act = do(lambda w, c: mm(w, c, LAST, f32, tn=256), wd_own, cot_all)
     cot_cols = do(lambda c: lax.dynamic_slice_in_dim(c, my_block * blk, blk, 1).T, cot_all)
     wo_own = do(cast, w_out)
@@ -869,7 +772,7 @@
     gains = do(lambda a, b: a + b, *gains)
     while gain_steps:
         gains = do(lambda a, b: a + b, *gain_step(gains))
-    gains = do(lambda g: g.reshape(4, ffb, 1), gains)
+    gains = do(lambda g: g.reshape(4, ffb).T, gains)
     flying = scatter_rest(flying)
 
     gate0, gate1, up0, up1, act, sums = do(gated, *flying[0], *flying[1], grad_act, gains)
@@ -880,13 +783,6 @@
     def even(count, want):
         n = parts_of(count, want)
         return [(k * (count // n), count // n) for k in range(n)]
-
-    down_rows, up_rows = even(ffb, 2), [(0, blk)]
-
-    def push_pairs(name, g, rows):
-        for k, (at_row, count) in enumerate(rows):
-            reps.push((name, "theirs", k), g[blk + at_row : blk + at_row + count])
-            reps.push((name, "mine", k), g[at_row : at_row + count])
 
     results = {"down": None, "out": None, "up": None, "qkv": None}
     states = {
@@ -905,27 +801,15 @@
             results[name],
         )
 
-    jobs = []
-    for k, (at_row, count) in enumerate(down_rows):
-        jobs.append(("down", [("down", k)], at_row, 0, count, 1024))
-    for name, lead in (("gate", 0), ("up", Y)):
-        for k, (at_row, count) in enumerate(up_rows):
-            jobs.append(("up", [(name, "mine", k), (name, "theirs", k)], at_row, lead, count, S * ffb))
-    received = {}
-
-    def update(limit):
-        for name in list(reps.done):
-            if name[1] == "theirs" and name not in received:
-                received[name] = at.core(reps.done[name])
-        while jobs and limit and all(k in reps.done for k in jobs[0][1]):
-            name, needs, at_row, lead, count, unit = jobs.pop(0)
-            rb = max(n for n in range(8, min(count, 176) + 1, 8) if count % n == 0 and at_row % n == 0)
-            adam(name, [received[k] if k[1] == "theirs" else reps.done[k] for k in needs], at_row, lead, unit, rb)
-            limit -= 1
-
-    def ticks(n):
-        for _ in range(n):
-            reps.tick()
+    def adam_own(name, pair):
+        half = pair.done[0].shape[0]
+        rb = max(n for n in range(8, min(half, 176) + 1, 8) if half % n == 0)
+        for k, g in enumerate(pair.done):
+            adam(name, [g], k * half, 0, width // 2, rb)
+
+    def adam_both(name, pair, lead, unit):
+        mine, theirs = pair.done
+        adam(name, [mine, at.core(theirs)], 0, lead, unit, min(blk, 128))
 
     wide = 2 * FF // 8
 
@@ -935,9 +819,7 @@
     n, start, finish, gate_all = gather_steps([gate0[None, None], gate1[None, None]], 1)
     start(0)
     g_down = do(lambda a, c: mm(a, c, PLAIN, bf16, tn=512), act, cot_all)
-    for k, (at_row, count) in enumerate(down_rows):
-        reps.push(("down", k), g_down[at_row : at_row + count])
-    ticks(1)
+    p_down = PairSum(do, g_down)
 
     steps2 = at.steps(False) + [("core", 1)]
 
@@ -954,7 +836,6 @@
         sums = do(lambda a, b: a + b, sums, sums_got)
         sums_got = sum_send(sums, *tiny.pop(0))
         start(i, sums)
-        ticks(1)
     n, start_up, finish_up, up_all = gather_steps([up0[None, None], up1[None, None]], 1)
     ggate_all = gate_all().reshape(Y * S * ffb, T)
     sums = do(lambda a, b: a + b, sums, sums_got)
@@ -962,15 +843,14 @@
     while tiny:
         sums = sum_step(sums, *tiny.pop(0))
     g_gate = do(lambda x, g: mm(x, g, LAST, bf16, tn=wide), xn2, ggate_all)
-    push_pairs("gate", g_gate, up_rows)
+    p_down.step()
+    p_gate = PairSum(do, g_gate)
     finish_up()
     for i in range(1, n):
         start_up(i)
         if i == 1:
-            ticks(1)
             part_gate = do(lambda w, g: mm(w, g, PLAIN, f32, tn=256), wg, ggate_all)
             out_part = do(lambda w, a: mm(w, a, FIRST, bf16, tm=512), wd_own, act)
-            update(1)
         if i < n - 1:
             finish_up()
     gup_all = up_all().reshape(Y * S * ffb, T)
@@ -988,14 +868,13 @@
     )
     n, start, finish, branch_all = gather_steps(quarter_heads(grad_branch), 1)
     start(0)
-    ticks(1)
+    p_down.step()
+    p_gate.step()
     g_up = do(lambda x, g: mm(x, g, LAST, bf16, tn=wide), xn2, gup_all)
-    push_pairs("up", g_up, up_rows)
+    p_up = PairSum(do, g_up)
     finish()
     for i in range(1, n):
         start(i)
-        if i == 1:
-            ticks(1)
         if i < n - 1:
             finish()
     gbr_c = branch_all()[0]
@@ -1011,30 +890,29 @@
     start(0)
     attn = lanes(*attns)
     g_out = do(lambda a, g: mm(a, g, LAST, bf16, tn=512), attn, gbr)
-    out_pair = PairSum(do, g_out)
-    ticks(1)
+    p_out = PairSum(do, g_out)
+    p_down.step()
+    p_up.step()
     finish()
     for i in range(1, n):
         start(i)
         if i == 1:
-            out_pair.step()
-            update(1)
-            ticks(1)
-            out_pair.step()
-            update(1)
+            p_gate.step()
+            p_out.step()
+            adam_own("down", p_down)
         if i < n - 1:
             finish()
     gqkv = gqkv_done().reshape(3, Y * S * blk, T)
-    pairs = []
+    p_qkv = {}
     for third in (2, 1, 0):
         g = do(lambda x, g: dot(x, g, LAST).astype(bf16), xn1, gqkv[third])
-        pairs.append(PairSum(do, g))
-    ticks(1)
+        p_qkv[third] = PairSum(do, g)
     part = do(lambda w, g: dot(w, g, PLAIN), wq, gqkv.reshape(3 * Y * S * blk, T))
     part_theirs = at.core(part[blk:])
-    pairs[0].step()
-    out_pair.step()
     out_sum = lax.psum_scatter(out_part, plane, scatter_dimension=0, tiled=True)
+    p_gate.step()
+    p_up.step()
+    p_qkv[2].step()
 
     def first_back(a, b, x, mean, inv, gain, gxn2, z2, gqkv0, gqkv1):
         gxn1 = a + b
@@ -1056,11 +934,11 @@
     sums, small, gxn1, z1 = do(
         first_back, part[:blk], part_theirs, x_own, mean1, inv1, own_cols[:, 0:1], gxn2, z2, *gqkvs
     )
-    sums = sum_step(sums, *steps2[0])
-    pairs[1].step()
-    for axis, step in steps2[1:]:
+    adam_both("up", p_gate, 0, S * ffb)
+    p_out.step()
+    p_qkv[1].step()
+    for axis, step in steps2:
         sums = sum_step(sums, axis, step)
-    pairs[2].step()
     input_grad = do(
         lambda h, grad, z, scale, gain, sums: h
         + scale * (grad * gain - sums[0:1] / width - z * (sums[1:2] / width)),
@@ -1077,36 +955,27 @@
         got = lax.all_to_all(split, plane, split_axis=0, concat_axis=0, tiled=True)
         return do(lambda g: g.reshape(width, rows).T, got)
 
-    def adam_qkv(third, pair):
-        mine, theirs = pair.done
-        adam("qkv", [mine, at.core(theirs)], 0, third * Y, S * blk, min(blk, 128))
-
-    ticks(1)
-    update(1)
-    pairs[0].step()
+    p_up.step()
+    p_qkv[2].step()
+    p_qkv[0].step()
+    input_rows = to_rows(input_grad)
+    p_out.step()
+    adam_both("up", p_up, Y, S * ffb)
+    p_qkv[1].step()
+    p_qkv[2].step()
+    adam_own("out", p_out)
+    adam_both("qkv", p_qkv[2], 2 * Y, S * blk)
+    p_qkv[0].step()
+    p_qkv[1].step()
     n_rep = lax.axis_size("rep")
     step = 1
     while step < n_rep:
         other = lax.ppermute(small, "rep", [(i, i ^ step) for i in range(n_rep)])
         small = do(lambda a, b: a + b, small, other)
         step *= 2
-    for k, g in enumerate(out_pair.done):
-        adam("out", [g], k * blk // 2, 0, width // 2, blk // 2)
-    ticks(1)
-    input_rows = to_rows(input_grad)
-    pairs[1].step()
-    update(1)
-    while reps.busy():
-        reps.tick()
-        update(1)
     out_cols = do(lambda h, a: (h + a.astype(f32)).astype(bf16), hidden, out_sum)
-    pairs[0].step()
-    adam_qkv(2, pairs[0])
-    pairs[2].step()
-    pairs[1].step()
-    update(len(jobs))
+    adam_both("qkv", p_qkv[1], Y, S * blk)
     block_output = to_rows(out_cols)
-    adam_qkv(1, pairs[1])
     sent = do(lambda s: jnp.broadcast_to(s.reshape(1, 7, blk), (nb, 7, blk)), small)
     small_all = lax.all_to_all(sent, plane, split_axis=0, concat_axis=0, tiled=True)
 
@@ -1114,8 +983,8 @@
         return adam_update(*a, every.transpose(1, 0, 2).reshape(7, width), 0.3, 0.0)
 
     mn, vn, wn = do(norm_update, small_all, norm_params, m_norm, v_norm)
-    pairs[2].step()
-    adam_qkv(0, pairs[2])
+    p_qkv[0].step()
+    adam_both("qkv", p_qkv[0], 0, S * blk)
     return (
         (block_output.reshape(tokens.shape), input_rows.reshape(tokens.shape))
         + tuple(results["qkv"])

time: 913 us -> 961 us (1.053)
  waiting for transfers between devices: 360 us -> 402 us
  other arithmetic: 68.3 us -> 102 us
  Pallas kernels: 196 us -> 176 us
  local copies, waits for them, and re-layouts: 102 us -> 115 us
    ppermute x12 -> x21, waiting for transfers between devices: 61.6 us -> 216 us  [exchange(): lax.ppermute(x, 'rep', [(i, i ^ step) for i in range(lax.axis_size('rep'))])]
    ppermute x16 -> x0, waiting for transfers between devices: 148 us -> none  [the longest x4 68.3 us: tick(): slot['out_got'] = lax.ppermute(out['total'], 'rep', [(1, 0), (2, 3)])]
    ppermute x16 -> x0, starting transfers between devices: 36.9 us -> none  [the longest x4 20.5 us: tick(): slot['in_got'] = lax.ppermute(out['new'], 'rep', [(0, 1), (3, 2)])]
    ppermute x18, waiting for transfers between devices: 71.6 us -> 93 us  [along(): lax.ppermute(x, 'ctx', [(i, i ^ 2 * step) for i in range(self.ctx_size)])]
    pallas_call x4 -> x0, Pallas kernels: 20.5 us -> none  [last_step(): pl.pallas_call(last_step_kernel, grid_spec=pltpu.PrefetchScalarGridSpec(n...]
    ppermute x12 -> x21, starting transfers between devices: 17.2 us -> 32.7 us  [exchange(): lax.ppermute(x, 'rep', [(i, i ^ step) for i in range(lax.axis_size('rep'))])]
    select_n x8 -> x0, other arithmetic: 14 us -> none  [the longest x6 8.72 us: tick(): self.done[old['out'][0]] = jnp.where(self.end, out['z_got'], old['out'][1])]
    select_n x8 -> x16, other arithmetic: 0.78 us -> 11.9 us  [put(): jnp.where(low, a, b)]
  transfers between devices with their start and end apart: 90 -> 84, of which waited for: 42 -> 38; matrix products, arithmetic and copies ran while one was open for 16% -> 18% of each run, Pallas kernels for 20% -> 17%
where the time goes in v10:
time: 961 us; the launch traced here: 948 us
  waiting for transfers between devices  402 us (42%)
  Pallas kernels  176 us (18%)
  local copies, waits for them, and re-layouts  115 us (12%)
  other arithmetic  102 us (11%)
  starting transfers between devices  94.5 us (10%)
  matrix products  42 us (4%)
  between operations  16.2 us (2%)
    ppermute x21, waiting for transfers between devices, exchange(): lax.ppermute(x, 'rep', [(i, i ^ step) for i in range(lax.axis_size('rep'))])  216 us
    ppermute x18, waiting for transfers between devices, along(): lax.ppermute(x, 'ctx', [(i, i ^ 2 * step) for i in range(self.ctx_size)])  93 us
    pallas_call x9, Pallas kernels, adam_part(): pl.pallas_call(functools.partial(adam_kernel, rate, two), grid_spec=pltpu...  68.8 us
    ppermute x18, waiting for transfers between devices, along(): return lax.ppermute(x, 'shard', [(i, i ^ step) for i in range(self.s_size)])  59 us
    unnamed x266, local copies, waits for them, and re-layouts  57.8 us
    dot_general x22, matrix products, dot(): return lax.dot_general(a, b, dims, preferred_element_type=f32)  42 us
    pallas_call x7, Pallas kernels, mm(): pl.pallas_call(functools.partial(product_kernel, dims), grid=(m // tm, n...  35.8 us
    ppermute x21, starting transfers between devices, exchange(): lax.ppermute(x, 'rep', [(i, i ^ step) for i in range(lax.axis_size('rep'))])  32.7 us
  transfers between devices with their start and end apart: 84, of which 38 were waited for; matrix products, arithmetic and copies ran while one was open for 18% of the time, Pallas kernels for 17%

profile of v10, /device:TPU:0, one launch (start us, length us, event | category | flops | bytes accessed | tf_op | source)
XLA Modules:
  0.0 947.9 jit_solution(9163824109385782876)
XLA Ops:
  20.3 4.8 all-to-all-start
  57.1 4.3 copy-done
  74.4 9.5 %collective-permute-done.3.b_ref.d_ref = bf16[1536,512]{1,0:T(8,128)(2,1)} collective-permute-done((bf16[1536,512]{1,0:T(8,128)(2,1)}, bf16[1536,512]{1,0:T(8,128)(2,1)}, u32[]{:S(2)}, u32[]{:S(2)}) %collective-permute-start.3) | collective-permute-done | bytes 1572896 | tf_op jit(solution)/shard_map/ppermute | solution.py:62
  98.3 10.5 %collective-permute-done.4 = bf16[768,512]{1,0:T(8,128)(2,1)} collective-permute-done((bf16[768,512]{1,0:T(8,128)(2,1)}, bf16[768,512]{1,0:T(8,128)(2,1)}, u32[]{:S(2)}, u32[]{:S(2)}) %collective-permute-start.4) | collective-permute-done | bytes 786464 | tf_op jit(solution)/shard_map/ppermute | solution.py:61
  111.6 5.1 shard_map.316
  121.0 5.1 shard_map.317
  157.1 5.2 pad_maximum_fusion.12
  169.8 6.6 collective-permute-done.12
  202.8 5.0 convolution_convert_fusion.1.a_ref.c_ref
  222.3 6.4 copy.142.b_ref
  230.5 5.6 shard_map.325.grad_ref
  243.7 13.8 %collective-permute-done.20 = f32[4,2,1,704]{3,0,2,1:T(4,128)S(1)} collective-permute-done((f32[4,2,1,704]{3,0,2,1:T(4,128)S(1)}, f32[4,2,1,704]{3,0,2,1:T(4,128)S(1)}, u32[]{:S(2)}, u32[]{:S(2)}) %collective-permute-start.20) | collective-permute-done | bytes 22560 | tf_op jit(solution)/shard_map/ppermute | solution.py:62
  260.7 8.4 collective-permute-done.21
  278.9 26.1 %collective-permute-done.22.gb_ref = bf16[704,1024]{1,0:T(8,128)(2,1)S(1)} collective-permute-done((bf16[704,1024]{1,0:T(8,128)(2,1)S(1)}, bf16[704,1024]{1,0:T(8,128)(2,1)S(1)}, u32[]{:S(2)}, u32[]{:S(2)}) %collective-permute-start.22) | collective-permute-done | bytes 1441824 | tf_op jit(solution)/shard_map/ppermute | solution.py:61
  305.0 5.0 collective-permute-done.24.ub_ref
  311.1 7.5 shard_map.330
  320.7 6.5 copy.144.b_ref
  327.2 5.6 shard_map.331
  341.3 26.3 %collective-permute-done.30 = f32[2,1024]{1,0:T(2,128)S(1)} collective-permute-done((f32[2,1024]{1,0:T(2,128)S(1)}, f32[2,1024]{1,0:T(2,128)S(1)}, u32[]{:S(2)}, u32[]{:S(2)}) %collective-permute-start.30) | collective-permute-done | bytes 8224 | tf_op jit(solution)/shard_map/ppermute | solution.py:61
  374.0 5.7 shard_map.332
  394.3 5.8 shard_map.333
  401.4 5.5 shard_map.334
  406.9 16.0 %collective-permute-done.35 = bf16[2,1,704,512]{3,2,1,0:T(8,128)(2,1)} collective-permute-done((bf16[2,1,704,512]{3,2,1,0:T(8,128)(2,1)}, bf16[2,1,704,512]{3,2,1,0:T(8,128)(2,1)}, u32[]{:S(2)}, u32[]{:S(2)}) %collective-permute-start.35) | collective-permute-done | bytes 1441824 | tf_op jit(solution)/shard_map/ppermute | solution.py:62
  450.1 57.0 %collective-permute-done.41 = bf16[352,2048]{1,0:T(8,128)(2,1)S(1)} collective-permute-done((bf16[352,2048]{1,0:T(8,128)(2,1)S(1)}, bf16[352,2048]{1,0:T(8,128)(2,1)S(1)}, u32[]{:S(2)}, u32[]{:S(2)}) %collective-permute-start.41) | collective-permute-done | bytes 1441824 | tf_op jit(solution)/shard_map/ppermute | solution.py:171
  510.2 5.7 shard_map.335
  520.0 10.6 %collective-permute-done.42 = bf16[2,1,256,512]{3,2,1,0:T(8,128)(2,1)S(1)} collective-permute-done((bf16[2,1,256,512]{3,2,1,0:T(8,128)(2,1)S(1)}, bf16[2,1,256,512]{3,2,1,0:T(8,128)(2,1)S(1)}, u32[]{:S(2)}, u32[]{:S(2)}) %collective-permute-start.42) | collective-permute-done | bytes 524320 | tf_op jit(solution)/shard_map/ppermute | solution.py:62
  546.8 5.5 shard_map.336
  553.2 5.9 shard_map.337
  563.4 68.0 %collective-permute-done.48 = bf16[352,2048]{1,0:T(8,128)(2,1)S(1)} collective-permute-done((bf16[352,2048]{1,0:T(8,128)(2,1)S(1)}, bf16[352,2048]{1,0:T(8,128)(2,1)S(1)}, u32[]{:S(2)}, u32[]{:S(2)}) %collective-permute-start.48) | collective-permute-done | bytes 1441824 | tf_op jit(solution)/shard_map/ppermute | solution.py:171
  639.6 4.8 collective-permute-start.55
  647.9 17.7 %collective-permute-done.51 = bf16[128,2048]{1,0:T(8,128)(2,1)S(1)} collective-permute-done((bf16[128,2048]{1,0:T(8,128)(2,1)}, bf16[128,2048]{1,0:T(8,128)(2,1)S(1)}, u32[]{:S(2)}, u32[]{:S(2)}) %collective-permute-start.51) | collective-permute-done | bytes 524320 | tf_op jit(solution)/shard_map/ppermute | solution.py:171
  666.6 7.7 shard_map.339
  674.3 8.1 shard_map.340
  708.2 19.6 %collective-permute-done.56 = bf16[256,2816]{1,0:T(8,128)(2,1)} collective-permute-done((bf16[256,2816]{1,0:T(8,128)(2,1)}, bf16[256,2816]{1,0:T(8,128)(2,1)}, u32[]{:S(2)}, u32[]{:S(2)}) %collective-permute-start.56) | collective-permute-done | bytes 1441824 | tf_op jit(solution)/shard_map/ppermute | solution.py:171
  732.1 6.8 collective-permute-done.54
  741.0 13.2 %shard_map.341 = (f32[256,11264]{1,0:T(8,128)}, f32[256,11264]{1,0:T(8,128)}, f32[256,11264]{1,0:T(8,128)}) custom-call(s32[1]{0:T(128)} %bitcast.8.core_ref, f32[256,11264]{1,0:T(8,128)} %w_ref.9, f32[256,11264]{1,0:T(8,128)} %m_ref.3, f32[256,11264]{1,0:T(8,128)} %v_ref.3, bf16[256,2816]{1,0:T(8,128)(2,1)S(1)} %get-tuple-element.729.refs_0_, ...), custom_call_target="tpu_custom_call" | custom-call | flops 1024 | bytes 1024 | tf_op jit(solution)/shard_map/pallas_call | solution.py:406
  767.1 25.2 %collective-permute-done.62 = bf16[256,2816]{1,0:T(8,128)(2,1)S(1)} collective-permute-done((bf16[256,2816]{1,0:T(8,128)(2,1)S(1)}, bf16[256,2816]{1,0:T(8,128)(2,1)S(1)}, u32[]{:S(2)}, u32[]{:S(2)}) %collective-permute-start.62) | collective-permute-done | bytes 1441824 | tf_op jit(solution)/shard_map/ppermute | solution.py:171
  793.6 6.0 collective-permute-done.69
  817.0 9.9 %all-to-all-done.1 = f32[8,256,128]{2,1,0:T(8,128)} async-done(((f32[8,256,128]{2,1,0:T(8,128)}), f32[8,256,128]{2,1,0:T(8,128)}, u32[]{:S(2)}, u32[]{:S(2)}) %all-to-all-start.1) | async-done | bytes 1048608 | tf_op jit(solution)/shard_map/all_to_all | solution.py:955
  829.5 8.6 collective-permute-done.67
  840.1 14.2 %shard_map.342 = (f32[256,11264]{1,0:T(8,128)}, f32[256,11264]{1,0:T(8,128)}, f32[256,11264]{1,0:T(8,128)}) custom-call(s32[1]{0:T(128)} %bitcast.8.core_ref, f32[256,11264]{1,0:T(8,128)} %w_ref.9, f32[256,11264]{1,0:T(8,128)} %m_ref.3, f32[256,11264]{1,0:T(8,128)} %v_ref.3, ...), custom_call_target="tpu_custom_call", output_to_operand_aliasing={{0}: (6, {}), {1}: (7, {}), {2}: (8, {})} | custom-call | flops 1024 | bytes 1024 | tf_op jit(solution)/shard_map/pallas_call | solution.py:406
  873.2 6.7 shard_map.345
  879.9 5.8 collective-permute-done.71
  893.2 6.0 collective-permute-done.74
  899.8 4.3 all-to-all-start.3
  913.4 6.3 shard_map.346
  926.1 7.5 all-to-all-done.2
  934.6 6.2 shard_map.347
  (632 shorter events, 394.2 us)
Async XLA Ops:
  25.1 197.1 %all-gather.2.cloned.1.call-start = ((), (), s32[]{:S(2)}) async-start(), calls=%async_computation.5 | async-start | bytes 4718592 | tf_op jit(solution)/shard_map/all_gather | solution.py:585
  47.1 36.8 %collective-permute-start.3 = (bf16[1536,512]{1,0:T(8,128)(2,1)}, bf16[1536,512]{1,0:T(8,128)(2,1)}, u32[]{:S(2)}, u32[]{:S(2)}) collective-permute-start(bf16[1536,512]{1,0:T(8,128)(2,1)} %convolution_convert_fusion.7), channel_id=1, source_target_pairs={{0,1},{1,0},{2,3},{3,2},{4,5},{5,4},{6,7},{7,6},{8,9},{9,8},{10,11... | collective-permute-start | bytes 4718600 | tf_op jit(solution)/shard_map/ppermute | solution.py:62
  50.2 40.1 %collective-permute-start.5 = (bf16[1536,512]{1,0:T(8,128)(2,1)}, bf16[1536,512]{1,0:T(8,128)(2,1)}, u32[]{:S(2)}, u32[]{:S(2)}) collective-permute-start(bf16[1536,512]{1,0:T(8,128)(2,1)} %convolution_convert_fusion.6), channel_id=1, source_target_pairs={{0,4},{2,6},{4,0},{6,2},{1,5},{3,7},{5,1},{7,3},{8,12},{10,14},{12... | collective-permute-start | bytes 4718600 | tf_op jit(solution)/shard_map/ppermute | solution.py:61
  96.1 22.1 %collective-permute-start.7 = (bf16[768,512]{1,0:T(8,128)(2,1)}, bf16[768,512]{1,0:T(8,128)(2,1)}, u32[]{:S(2)}, u32[]{:S(2)}) collective-permute-start(bf16[768,512]{1,0:T(8,128)(2,1)} %get-tuple-element.477), channel_id=1, source_target_pairs={{0,1},{1,0},{2,3},{3,2},{4,5},{5,4},{6,7},{7,6},{8,9},{9,8},{10,11... | collective-permute-start | bytes 2359304 | tf_op jit(solution)/shard_map/ppermute | solution.py:62
  130.2 774.4 %reduce-scatter.2.cloned.1.call-start = ((), (), s32[]{:S(2)}) async-start(), calls=%async_computation.6 | async-start | bytes 4718592 | tf_op jit(solution)/shard_map/reduce_scatter | solution.py:912
  135.4 26.9 %collective-permute-start.9 = (bf16[512,512]{1,0:T(8,128)(2,1)}, bf16[512,512]{1,0:T(8,128)(2,1)}, u32[]{:S(2)}, u32[]{:S(2)}) collective-permute-start(bf16[512,512]{1,0:T(8,128)(2,1)} %convolution_convert_fusion.14), channel_id=1, source_target_pairs={{0,1},{1,0},{2,3},{3,2},{4,5},{5,4},{6,7},{7,6},{8,9},{9,8},{10,11... | collective-permute-start | bytes 1572872 | tf_op jit(solution)/shard_map/ppermute | solution.py:62
  137.6 28.6 %collective-permute-start.13 = (bf16[512,512]{1,0:T(8,128)(2,1)}, bf16[512,512]{1,0:T(8,128)(2,1)}, u32[]{:S(2)}, u32[]{:S(2)}) collective-permute-start(bf16[512,512]{1,0:T(8,128)(2,1)} %convolution_convert_fusion.13), channel_id=1, source_target_pairs={{0,4},{2,6},{4,0},{6,2},{1,5},{3,7},{5,1},{7,3},{8,12},{10,14},{12... | collective-permute-start | bytes 1572872 | tf_op jit(solution)/shard_map/ppermute | solution.py:61
  192.1 77.7 %collective-permute-start.19 = (bf16[1408,1024]{1,0:T(8,128)(2,1)}, bf16[1408,1024]{1,0:T(8,128)(2,1)}, u32[]{:S(2)}, u32[]{:S(2)}) collective-permute-start(bf16[1408,1024]{1,0:T(8,128)(2,1)} %convolution_convert_fusion.3), channel_id=1, source_target_pairs={{0,1},{1,0},{2,3},{3,2},{4,5},{5,4},{6,7},{7,6},{8,9},{9,8},{10,11... | collective-permute-start | bytes 8650760 | tf_op jit(solution)/shard_map/ppermute | solution.py:62
  196.8 77.5 %collective-permute-start.23 = (bf16[1408,1024]{1,0:T(8,128)(2,1)}, bf16[1408,1024]{1,0:T(8,128)(2,1)}, u32[]{:S(2)}, u32[]{:S(2)}) collective-permute-start(bf16[1408,1024]{1,0:T(8,128)(2,1)} %convolution_convert_fusion.2), channel_id=1, source_target_pairs={{0,4},{2,6},{4,0},{6,2},{1,5},{3,7},{5,1},{7,3},{8,12},{10,14},{12... | collective-permute-start | bytes 8650760 | tf_op jit(solution)/shard_map/ppermute | solution.py:61
  201.3 56.1 %collective-permute-start.20 = (f32[4,2,1,704]{3,0,2,1:T(4,128)S(1)}, f32[4,2,1,704]{3,0,2,1:T(4,128)S(1)}, u32[]{:S(2)}, u32[]{:S(2)}) collective-permute-start(f32[4,2,1,704]{3,0,2,1:T(4,128)S(1)} %copy.140), channel_id=1, source_target_pairs={{0,1},{1,0},{2,3},{3,2},{4,5},{5,4},{6,7},{7,6},{8,9},{9,8},{10,11... | collective-permute-start | bytes 67592 | tf_op jit(solution)/shard_map/ppermute | solution.py:62
  272.8 32.2 %collective-permute-start.22 = (bf16[704,1024]{1,0:T(8,128)(2,1)S(1)}, bf16[704,1024]{1,0:T(8,128)(2,1)S(1)}, u32[]{:S(2)}, u32[]{:S(2)}) collective-permute-start(bf16[704,1024]{1,0:T(8,128)(2,1)S(1)} %get-tuple-element.569), channel_id=1, source_target_pairs={{0,4},{2,6},{4,0},{6,2},{1,5},{3,7},{5,1},{7,3},{8,12},{10,14},{12... | collective-permute-start | bytes 4325384 | tf_op jit(solution)/shard_map/ppermute | solution.py:61
  278.2 31.7 %collective-permute-start.24 = (bf16[704,1024]{1,0:T(8,128)(2,1)S(1)}, bf16[704,1024]{1,0:T(8,128)(2,1)S(1)}, u32[]{:S(2)}, u32[]{:S(2)}) collective-permute-start(bf16[704,1024]{1,0:T(8,128)(2,1)S(1)} %get-tuple-element.573), channel_id=1, source_target_pairs={{0,1},{1,0},{2,3},{3,2},{4,5},{5,4},{6,7},{7,6},{8,9},{9,8},{10,11... | collective-permute-start | bytes 4325384 | tf_op jit(solution)/shard_map/ppermute | solution.py:62
  336.8 32.9 %collective-permute-start.28 = (bf16[2,1,704,512]{3,2,1,0:T(8,128)(2,1)S(1)}, bf16[2,1,704,512]{3,2,1,0:T(8,128)(2,1)S(1)}, u32[]{:S(2)}, u32[]{:S(2)}) collective-permute-start(bf16[2,1,704,512]{3,2,1,0:T(8,128)(2,1)S(1)} %pad_maximum_fusion.13), channel_id=1, source_target_pairs={{0,1},{1,0},{2,3},{3,2},{4,5},{5,4},{6,7},{7,6},{8,9},{9,8},{10,11... | collective-permute-start | bytes 4325384 | tf_op jit(solution)/shard_map/ppermute | solution.py:62
  337.7 32.0 %collective-permute-start.29 = (bf16[1,2,704,512]{3,2,1,0:T(8,128)(2,1)S(1)}, bf16[1,2,704,512]{3,2,1,0:T(8,128)(2,1)S(1)}, u32[]{:S(2)}, u32[]{:S(2)}) collective-permute-start(bf16[1,2,704,512]{3,2,1,0:T(8,128)(2,1)S(1)} %pad_maximum_fusion.14), channel_id=1, source_target_pairs={{0,4},{2,6},{4,0},{6,2},{1,5},{3,7},{5,1},{7,3},{8,12},{10,14},{12... | collective-permute-start | bytes 4325384 | tf_op jit(solution)/shard_map/ppermute | solution.py:61
  338.9 40.7 %collective-permute-start.34 = (bf16[352,2048]{1,0:T(8,128)(2,1)}, bf16[352,2048]{1,0:T(8,128)(2,1)S(1)}, u32[]{:S(2)}, u32[]{:S(2)}) collective-permute-start(bf16[352,2048]{1,0:T(8,128)(2,1)} %get-tuple-element.888), channel_id=1, source_target_pairs={{0,8},{8,0},{16,24},{24,16},{1,9},{9,1},{17,25},{25,17},{2,10},{10... | collective-permute-start | bytes 4325384 | tf_op jit(solution)/shard_map/ppermute | solution.py:171
  340.4 27.2 %collective-permute-start.30 = (f32[2,1024]{1,0:T(2,128)S(1)}, f32[2,1024]{1,0:T(2,128)S(1)}, u32[]{:S(2)}, u32[]{:S(2)}) collective-permute-start(f32[2,1024]{1,0:T(2,128)S(1)} %add.390), channel_id=1, source_target_pairs={{0,4},{2,6},{4,0},{6,2},{1,5},{3,7},{5,1},{7,3},{8,12},{10,14},{12... | collective-permute-start | bytes 24584 | tf_op jit(solution)/shard_map/ppermute | solution.py:61
  389.8 33.1 %collective-permute-start.35 = (bf16[2,1,704,512]{3,2,1,0:T(8,128)(2,1)}, bf16[2,1,704,512]{3,2,1,0:T(8,128)(2,1)}, u32[]{:S(2)}, u32[]{:S(2)}) collective-permute-start(bf16[2,1,704,512]{3,2,1,0:T(8,128)(2,1)} %pad_maximum_fusion.15), channel_id=1, source_target_pairs={{0,1},{1,0},{2,3},{3,2},{4,5},{5,4},{6,7},{7,6},{8,9},{9,8},{10,11... | collective-permute-start | bytes 4325384 | tf_op jit(solution)/shard_map/ppermute | solution.py:62
  393.1 32.9 %collective-permute-start.36 = (bf16[1,2,704,512]{3,2,1,0:T(8,128)(2,1)}, bf16[1,2,704,512]{3,2,1,0:T(8,128)(2,1)}, u32[]{:S(2)}, u32[]{:S(2)}) collective-permute-start(bf16[1,2,704,512]{3,2,1,0:T(8,128)(2,1)} %pad_maximum_fusion.16), channel_id=1, source_target_pairs={{0,4},{2,6},{4,0},{6,2},{1,5},{3,7},{5,1},{7,3},{8,12},{10,14},{12... | collective-permute-start | bytes 4325384 | tf_op jit(solution)/shard_map/ppermute | solution.py:61
  442.3 64.8 %collective-permute-start.41 = (bf16[352,2048]{1,0:T(8,128)(2,1)S(1)}, bf16[352,2048]{1,0:T(8,128)(2,1)S(1)}, u32[]{:S(2)}, u32[]{:S(2)}) collective-permute-start(bf16[352,2048]{1,0:T(8,128)(2,1)S(1)} %copy-done.97), channel_id=1, source_target_pairs={{0,16},{8,24},{16,0},{24,8},{1,17},{9,25},{17,1},{25,9},{2,18},{10... | collective-permute-start | bytes 4325384 | tf_op jit(solution)/shard_map/ppermute | solution.py:171
  444.7 64.0 %collective-permute-start.40 = (bf16[256,2816]{1,0:T(8,128)(2,1)S(1)}, bf16[256,2816]{1,0:T(8,128)(2,1)S(1)}, u32[]{:S(2)}, u32[]{:S(2)}) collective-permute-start(bf16[256,2816]{1,0:T(8,128)(2,1)S(1)} %copy-done.115), channel_id=1, source_target_pairs={{0,8},{8,0},{16,24},{24,16},{1,9},{9,1},{17,25},{25,17},{2,10},{10... | collective-permute-start | bytes 4325384 | tf_op jit(solution)/shard_map/ppermute | solution.py:171
  448.1 69.6 %collective-permute-start.38 = (bf16[1,1,256,512]{3,2,1,0:T(8,128)(2,1)S(1)}, bf16[1,1,256,512]{3,2,1,0:T(8,128)(2,1)S(1)}, u32[]{:S(2)}, u32[]{:S(2)}) collective-permute-start(bf16[1,1,256,512]{3,2,1,0:T(8,128)(2,1)S(1)} %get-tuple-element.643), channel_id=1, source_target_pairs={{0,4},{2,6},{4,0},{6,2},{1,5},{3,7},{5,1},{7,3},{8,12},{10,14},{12... | collective-permute-start | bytes 786440 | tf_op jit(solution)/shard_map/ppermute | solution.py:61
  449.2 68.4 %collective-permute-start.39 = (bf16[1,1,256,512]{3,2,1,0:T(8,128)(2,1)S(1)}, bf16[1,1,256,512]{3,2,1,0:T(8,128)(2,1)S(1)}, u32[]{:S(2)}, u32[]{:S(2)}) collective-permute-start(bf16[1,1,256,512]{3,2,1,0:T(8,128)(2,1)S(1)} %get-tuple-element.645), channel_id=1, source_target_pairs={{0,1},{1,0},{2,3},{3,2},{4,5},{5,4},{6,7},{7,6},{8,9},{9,8},{10,11... | collective-permute-start | bytes 786440 | tf_op jit(solution)/shard_map/ppermute | solution.py:62
  535.3 97.4 %collective-permute-start.47 = (bf16[256,2816]{1,0:T(8,128)(2,1)}, bf16[256,2816]{1,0:T(8,128)(2,1)S(1)}, u32[]{:S(2)}, u32[]{:S(2)}) collective-permute-start(bf16[256,2816]{1,0:T(8,128)(2,1)} %get-tuple-element.880), channel_id=1, source_target_pairs={{0,8},{8,0},{16,24},{24,16},{1,9},{9,1},{17,25},{25,17},{2,10},{10... | collective-permute-start | bytes 4325384 | tf_op jit(solution)/shard_map/ppermute | solution.py:171
  536.8 94.6 %collective-permute-start.48 = (bf16[352,2048]{1,0:T(8,128)(2,1)S(1)}, bf16[352,2048]{1,0:T(8,128)(2,1)S(1)}, u32[]{:S(2)}, u32[]{:S(2)}) collective-permute-start(bf16[352,2048]{1,0:T(8,128)(2,1)S(1)} %copy-done.98), channel_id=1, source_target_pairs={{0,8},{8,0},{16,24},{24,16},{1,9},{9,1},{17,25},{25,17},{2,10},{10... | collective-permute-start | bytes 4325384 | tf_op jit(solution)/shard_map/ppermute | solution.py:171
  537.4 107.1 %collective-permute-start.52 = (bf16[256,2816]{1,0:T(8,128)(2,1)}, bf16[256,2816]{1,0:T(8,128)(2,1)}, u32[]{:S(2)}, u32[]{:S(2)}) collective-permute-start(bf16[256,2816]{1,0:T(8,128)(2,1)} %reduce-precision_convert_fusion.3), channel_id=1, source_target_pairs={{0,16},{8,24},{16,0},{24,8},{1,17},{9,25},{17,1},{25,9},{2,18},{10... | collective-permute-start | bytes 4325384 | tf_op jit(solution)/shard_map/ppermute | solution.py:171
  552.2 82.4 %collective-permute-start.45 = (bf16[1,1,768,512]{3,2,1,0:T(8,128)(2,1)S(1)}, bf16[1,1,768,512]{3,2,1,0:T(8,128)(2,1)S(1)}, u32[]{:S(2)}, u32[]{:S(2)}) collective-permute-start(bf16[1,1,768,512]{3,2,1,0:T(8,128)(2,1)S(1)} %bitcast.175), channel_id=1, source_target_pairs={{0,4},{2,6},{4,0},{6,2},{1,5},{3,7},{5,1},{7,3},{8,12},{10,14},{12... | collective-permute-start | bytes 2359304 | tf_op jit(solution)/shard_map/ppermute | solution.py:61
  559.1 75.5 %collective-permute-start.46 = (bf16[1,1,768,512]{3,2,1,0:T(8,128)(2,1)S(1)}, bf16[1,1,768,512]{3,2,1,0:T(8,128)(2,1)S(1)}, u32[]{:S(2)}, u32[]{:S(2)}) collective-permute-start(bf16[1,1,768,512]{3,2,1,0:T(8,128)(2,1)S(1)} %bitcast.178), channel_id=1, source_target_pairs={{0,1},{1,0},{2,3},{3,2},{4,5},{5,4},{6,7},{7,6},{8,9},{9,8},{10,11... | collective-permute-start | bytes 2359304 | tf_op jit(solution)/shard_map/ppermute | solution.py:62
  636.1 46.3 %collective-permute-start.49 = (bf16[2,1,768,512]{3,2,1,0:T(8,128)(2,1)}, bf16[2,1,768,512]{3,2,1,0:T(8,128)(2,1)}, u32[]{:S(2)}, u32[]{:S(2)}) collective-permute-start(bf16[2,1,768,512]{3,2,1,0:T(8,128)(2,1)} %pad_maximum_fusion.10), channel_id=1, source_target_pairs={{0,1},{1,0},{2,3},{3,2},{4,5},{5,4},{6,7},{7,6},{8,9},{9,8},{10,11... | collective-permute-start | bytes 4718600 | tf_op jit(solution)/shard_map/ppermute | solution.py:62
  638.4 46.9 %collective-permute-start.50 = (bf16[1,2,768,512]{3,2,1,0:T(8,128)(2,1)}, bf16[1,2,768,512]{3,2,1,0:T(8,128)(2,1)}, u32[]{:S(2)}, u32[]{:S(2)}) collective-permute-start(bf16[1,2,768,512]{3,2,1,0:T(8,128)(2,1)} %pad_maximum_fusion.11), channel_id=1, source_target_pairs={{0,4},{2,6},{4,0},{6,2},{1,5},{3,7},{5,1},{7,3},{8,12},{10,14},{12... | collective-permute-start | bytes 4718600 | tf_op jit(solution)/shard_map/ppermute | solution.py:61
  639.5 26.1 %collective-permute-start.51 = (bf16[128,2048]{1,0:T(8,128)(2,1)}, bf16[128,2048]{1,0:T(8,128)(2,1)S(1)}, u32[]{:S(2)}, u32[]{:S(2)}) collective-permute-start(bf16[128,2048]{1,0:T(8,128)(2,1)} %get-tuple-element.926), channel_id=1, source_target_pairs={{0,8},{8,0},{16,24},{24,16},{1,9},{9,1},{17,25},{25,17},{2,10},{10... | collective-permute-start | bytes 1572872 | tf_op jit(solution)/shard_map/ppermute | solution.py:171
  639.6 90.3 %collective-permute-start.55 = (bf16[256,2816]{1,0:T(8,128)(2,1)}, bf16[256,2816]{1,0:T(8,128)(2,1)}, u32[]{:S(2)}, u32[]{:S(2)}) collective-permute-start(bf16[256,2816]{1,0:T(8,128)(2,1)} %reduce-precision_convert_fusion.2), channel_id=1, source_target_pairs={{0,16},{8,24},{16,0},{24,8},{1,17},{9,25},{17,1},{25,9},{2,18},{10... | collective-permute-start | bytes 4325384 | tf_op jit(solution)/shard_map/ppermute | solution.py:171
  647.9 79.9 %collective-permute-start.56 = (bf16[256,2816]{1,0:T(8,128)(2,1)}, bf16[256,2816]{1,0:T(8,128)(2,1)}, u32[]{:S(2)}, u32[]{:S(2)}) collective-permute-start(bf16[256,2816]{1,0:T(8,128)(2,1)} %reduce-precision_convert_fusion.1), channel_id=1, source_target_pairs={{0,8},{8,0},{16,24},{24,16},{1,9},{9,1},{17,25},{25,17},{2,10},{10... | collective-permute-start | bytes 4325384 | tf_op jit(solution)/shard_map/ppermute | solution.py:171
  666.6 87.6 %collective-permute-start.59 = (bf16[128,2048]{1,0:T(8,128)(2,1)}, bf16[128,2048]{1,0:T(8,128)(2,1)}, u32[]{:S(2)}, u32[]{:S(2)}) collective-permute-start(bf16[128,2048]{1,0:T(8,128)(2,1)} %reduce-precision_convert_fusion.13), channel_id=1, source_target_pairs={{0,16},{8,24},{16,0},{24,8},{1,17},{9,25},{17,1},{25,9},{2,18},{10... | collective-permute-start | bytes 1572872 | tf_op jit(solution)/shard_map/ppermute | solution.py:171
  698.1 40.8 %collective-permute-start.54 = (bf16[256,1024]{1,0:T(8,128)(2,1)S(1)}, bf16[256,1024]{1,0:T(8,128)(2,1)S(1)}, u32[]{:S(2)}, u32[]{:S(2)}) collective-permute-start(bf16[256,1024]{1,0:T(8,128)(2,1)S(1)} %get-tuple-element.924), channel_id=1, source_target_pairs={{0,8},{8,0},{16,24},{24,16},{1,9},{9,1},{17,25},{25,17},{2,10},{10... | collective-permute-start | bytes 1572872 | tf_op jit(solution)/shard_map/ppermute | solution.py:171
  700.3 55.4 %collective-permute-start.58 = (bf16[256,1024]{1,0:T(8,128)(2,1)}, bf16[256,1024]{1,0:T(8,128)(2,1)}, u32[]{:S(2)}, u32[]{:S(2)}) collective-permute-start(bf16[256,1024]{1,0:T(8,128)(2,1)} %get-tuple-element.922), channel_id=1, source_target_pairs={{0,8},{8,0},{16,24},{24,16},{1,9},{9,1},{17,25},{25,17},{2,10},{10... | collective-permute-start | bytes 1572872 | tf_op jit(solution)/shard_map/ppermute | solution.py:171
  738.9 53.4 %collective-permute-start.62 = (bf16[256,2816]{1,0:T(8,128)(2,1)S(1)}, bf16[256,2816]{1,0:T(8,128)(2,1)S(1)}, u32[]{:S(2)}, u32[]{:S(2)}) collective-permute-start(bf16[256,2816]{1,0:T(8,128)(2,1)S(1)} %reduce-precision_convert_fusion), channel_id=1, source_target_pairs={{0,8},{8,0},{16,24},{24,16},{1,9},{9,1},{17,25},{25,17},{2,10},{10... | collective-permute-start | bytes 4325384 | tf_op jit(solution)/shard_map/ppermute | solution.py:171
  760.9 40.8 %collective-permute-start.68 = (bf16[256,1024]{1,0:T(8,128)(2,1)S(1)}, bf16[256,1024]{1,0:T(8,128)(2,1)S(1)}, u32[]{:S(2)}, u32[]{:S(2)}) collective-permute-start(bf16[256,1024]{1,0:T(8,128)(2,1)S(1)} %copy-done.119), channel_id=1, source_target_pairs={{0,8},{8,0},{16,24},{24,16},{1,9},{9,1},{17,25},{25,17},{2,10},{10... | collective-permute-start | bytes 1572872 | tf_op jit(solution)/shard_map/ppermute | solution.py:171
  762.9 36.7 %collective-permute-start.69 = (bf16[256,1024]{1,0:T(8,128)(2,1)S(1)}, bf16[256,1024]{1,0:T(8,128)(2,1)S(1)}, u32[]{:S(2)}, u32[]{:S(2)}) collective-permute-start(bf16[256,1024]{1,0:T(8,128)(2,1)S(1)} %reduce-precision_convert_fusion.12), channel_id=1, source_target_pairs={{0,16},{8,24},{16,0},{24,8},{1,17},{9,25},{17,1},{25,9},{2,18},{10... | collective-permute-start | bytes 1572872 | tf_op jit(solution)/shard_map/ppermute | solution.py:171
  793.6 46.5 %collective-permute-start.66 = (bf16[256,2816]{1,0:T(8,128)(2,1)}, bf16[256,2816]{1,0:T(8,128)(2,1)}, u32[]{:S(2)}, u32[]{:S(2)}) collective-permute-start(bf16[256,2816]{1,0:T(8,128)(2,1)} %get-tuple-element.873), channel_id=1, source_target_pairs={{0,2},{2,0},{4,6},{6,4},{1,3},{3,1},{5,7},{7,5},{8,10},{10,8},{12,... | collective-permute-start | bytes 4325384 | tf_op jit(solution)/shard_map/ppermute | solution.py:57
  807.7 19.2 %all-to-all-start.1 = ((f32[8,256,128]{2,1,0:T(8,128)}), f32[8,256,128]{2,1,0:T(8,128)}, u32[]{:S(2)}, u32[]{:S(2)}) async-start(f32[8,256,128]{2,1,0:T(8,128)} %bitcast.195), calls=%async_computation.2 | async-start | bytes 2097152 | tf_op jit(solution)/shard_map/all_to_all | solution.py:955
  812.0 26.1 %collective-permute-start.67 = (bf16[128,2048]{1,0:T(8,128)(2,1)S(1)}, bf16[128,2048]{1,0:T(8,128)(2,1)}, u32[]{:S(2)}, u32[]{:S(2)}) collective-permute-start(bf16[128,2048]{1,0:T(8,128)(2,1)S(1)} %reduce-precision_convert_fusion.11), channel_id=1, source_target_pairs={{0,8},{8,0},{16,24},{24,16},{1,9},{9,1},{17,25},{25,17},{2,10},{10... | collective-permute-start | bytes 1572872 | tf_op jit(solution)/shard_map/ppermute | solution.py:171
  816.2 38.1 %collective-permute-start.61 = (bf16[256,1024]{1,0:T(8,128)(2,1)S(1)}, bf16[256,1024]{1,0:T(8,128)(2,1)}, u32[]{:S(2)}, u32[]{:S(2)}) collective-permute-start(bf16[256,1024]{1,0:T(8,128)(2,1)S(1)} %reduce-precision_convert_fusion.10), channel_id=1, source_target_pairs={{0,16},{8,24},{16,0},{24,8},{1,17},{9,25},{17,1},{25,9},{2,18},{10... | collective-permute-start | bytes 1572872 | tf_op jit(solution)/shard_map/ppermute | solution.py:171
  816.9 39.6 %collective-permute-start.72 = (bf16[256,1024]{1,0:T(8,128)(2,1)}, bf16[256,1024]{1,0:T(8,128)(2,1)}, u32[]{:S(2)}, u32[]{:S(2)}) collective-permute-start(bf16[256,1024]{1,0:T(8,128)(2,1)} %reduce-precision_convert_fusion.9), channel_id=1, source_target_pairs={{0,8},{8,0},{16,24},{24,16},{1,9},{9,1},{17,25},{25,17},{2,10},{10... | collective-permute-start | bytes 1572872 | tf_op jit(solution)/shard_map/ppermute | solution.py:171
  858.8 26.9 %collective-permute-start.71 = (bf16[256,1024]{1,0:T(8,128)(2,1)}, bf16[256,1024]{1,0:T(8,128)(2,1)}, u32[]{:S(2)}, u32[]{:S(2)}) collective-permute-start(bf16[256,1024]{1,0:T(8,128)(2,1)} %reduce-precision_convert_fusion.8), channel_id=1, source_target_pairs={{0,16},{8,24},{16,0},{24,8},{1,17},{9,25},{17,1},{25,9},{2,18},{10... | collective-permute-start | bytes 1572872 | tf_op jit(solution)/shard_map/ppermute | solution.py:171
  861.1 26.4 %collective-permute-start.70 = (bf16[256,1024]{1,0:T(8,128)(2,1)}, bf16[256,1024]{1,0:T(8,128)(2,1)}, u32[]{:S(2)}, u32[]{:S(2)}) collective-permute-start(bf16[256,1024]{1,0:T(8,128)(2,1)} %reduce-precision_convert_fusion.7), channel_id=1, source_target_pairs={{0,8},{8,0},{16,24},{24,16},{1,9},{9,1},{17,25},{25,17},{2,10},{10... | collective-permute-start | bytes 1572872 | tf_op jit(solution)/shard_map/ppermute | solution.py:171
  864.0 25.6 %collective-permute-start.57 = (f32[7,256]{1,0:T(8,128)S(1)}, f32[7,256]{1,0:T(8,128)S(1)}, u32[]{:S(2)}, u32[]{:S(2)}) collective-permute-start(f32[7,256]{1,0:T(8,128)S(1)} %concatenate.154), channel_id=1, source_target_pairs={{0,8},{8,0},{16,24},{24,16},{1,9},{9,1},{17,25},{25,17},{2,10},{10... | collective-permute-start | bytes 21512 | tf_op jit(solution)/shard_map/ppermute | solution.py:973
  887.1 22.5 %collective-permute-start.76 = (bf16[256,1024]{1,0:T(8,128)(2,1)S(1)}, bf16[256,1024]{1,0:T(8,128)(2,1)S(1)}, u32[]{:S(2)}, u32[]{:S(2)}) collective-permute-start(bf16[256,1024]{1,0:T(8,128)(2,1)S(1)} %reduce-precision_convert_fusion.6), channel_id=1, source_target_pairs={{0,8},{8,0},{16,24},{24,16},{1,9},{9,1},{17,25},{25,17},{2,10},{10... | collective-permute-start | bytes 1572872 | tf_op jit(solution)/shard_map/ppermute | solution.py:171
  912.3 22.3 %collective-permute-start.77 = (bf16[256,1024]{1,0:T(8,128)(2,1)}, bf16[256,1024]{1,0:T(8,128)(2,1)S(1)}, u32[]{:S(2)}, u32[]{:S(2)}) collective-permute-start(bf16[256,1024]{1,0:T(8,128)(2,1)} %get-tuple-element.911), channel_id=1, source_target_pairs={{0,2},{2,0},{4,6},{6,4},{1,3},{3,1},{5,7},{7,5},{8,10},{10,8},{12,... | collective-permute-start | bytes 1572872 | tf_op jit(solution)/shard_map/ppermute | solution.py:57
  (167 other events, 1187.1 us)
Sparse Core Ops, SparseCore 0:
  130.4 46.7 all-gather.1
  639.6 62.2 reduce-scatter.1

commit v11 on v9

--- a/solution.py
+++ b/solution.py
@@ -271,8 +271,8 @@
     u0_ref[...] = gup[:, :half]
     u1_ref[...] = gup[:, half:]
     a, b = ggate.astype(f32), gup.astype(f32)
-    e = jnp.sum(a * gains_ref[0] + b * gains_ref[2], axis=0, keepdims=True)
-    ez = jnp.sum(a * (gate - gains_ref[1]) + b * (up - gains_ref[3]), axis=0, keepdims=True)
+    e = jnp.sum(a * gains_ref[:, 0:1] + b * gains_ref[:, 2:3], axis=0, keepdims=True)
+    ez = jnp.sum(a * (gate - gains_ref[:, 1:2]) + b * (up - gains_ref[:, 3:4]), axis=0, keepdims=True)
     both = jnp.concatenate([e, ez], axis=0)
 
     @pl.when(pl.program_id(0) == 0)
@@ -293,12 +293,35 @@
     return pl.pallas_call(
         gated_kernel,
         grid=(n,),
-        in_specs=[whole] * 5 + [pl.BlockSpec((4, rows // n, 1), lambda i: (0, i, 0))],
+        in_specs=[whole] * 5 + [pl.BlockSpec((rows // n, 4), lambda i: (i, 0))],
         out_specs=[half] * 4 + [whole, pl.BlockSpec((2, t), lambda i: (0, 0))],
         out_shape=[out_half] * 4 + [jax.ShapeDtypeStruct((rows, t), bf16), jax.ShapeDtypeStruct((2, t), f32)],
         compiler_params=pltpu.CompilerParams(vmem_limit_bytes=56 * 1024 * 1024),
         cost_estimate=SMALL,
     )(ga, gb, ua, ub, grad_act, gains)
+
+
+def own_columns_kernel(block_ref, x_ref, out_ref):
+    out_ref[...] = x_ref[...].T
+
+
+def own_columns(x, block, width):
+    rows = x.shape[0]
+    if width % 128:
+        return lax.dynamic_slice_in_dim(x, block[0] * width, width, 1).T
+    tile = min(rows, 512)
+    return pl.pallas_call(
+        own_columns_kernel,
+        grid_spec=pltpu.PrefetchScalarGridSpec(
+            num_scalar_prefetch=1,
+            grid=(rows // tile,),
+            in_specs=[pl.BlockSpec((tile, width), lambda i, block: (i, block[0]))],
+            out_specs=pl.BlockSpec((width, tile), lambda i, block: (0, i)),
+        ),
+        out_shape=jax.ShapeDtypeStruct((width, rows), bf16),
+        compiler_params=pltpu.CompilerParams(vmem_limit_bytes=48 * 1024 * 1024),
+        cost_estimate=SMALL,
+    )(block, x)
 
 
 def split_kernel(core_ref, w_ref, mine_ref, theirs_ref):
@@ -682,7 +705,7 @@
         return jnp.concatenate([blocks, jnp.broadcast_to(extra[None], (nb, 16, rows))], axis=1)
 
     packed = do(pack, x_rows, order)
-    cot_all = lax.all_gather(cotangent.reshape(rows, width), ("shard", "ctx"), axis=0, tiled=True)
+    cot_all = lax.all_gather(do(cast, cotangent.reshape(rows, width)), ("shard", "ctx"), axis=0, tiled=True)
     got = lax.all_to_all(packed, plane, split_axis=0, concat_axis=0, tiled=True)
 
     def chip_rows(w, lead, unit, count):
@@ -861,27 +884,19 @@
     wd_own = do(cast, w_down)
     wg = do(stack_turned, *wg_parts)
     wu = do(stack_turned, *wu_parts)
-    cot_all = do(lambda c: c, cot_all)
     grad_act = do(lambda w, c: mm(w, c, LAST, f32, tn=256), wd_own, cot_all)
-    cot_cols = do(lambda c: lax.dynamic_slice_in_dim(c, my_block * blk, blk, 1).T, cot_all)
+    cot_cols = do(lambda c: own_columns(c, my_block.reshape(1), blk), cot_all)
     wo_own = do(cast, w_out)
     wq = do(stack_turned, *wq_parts)
     gains = do(lambda a, b: a + b, *gains)
     while gain_steps:
         gains = do(lambda a, b: a + b, *gain_step(gains))
-    gains = do(lambda g: g.reshape(4, ffb, 1), gains)
+    gains = do(lambda g: g.reshape(4, ffb).T, gains)
     flying = scatter_rest(flying)
 
     gate0, gate1, up0, up1, act, sums = do(gated, *flying[0], *flying[1], grad_act, gains)
 
-    def parts_of(count, want):
-        return max(n for n in range(1, want + 1) if count % (16 * n) == 0)
-
-    def even(count, want):
-        n = parts_of(count, want)
-        return [(k * (count // n), count // n) for k in range(n)]
-
-    down_rows, up_rows = even(ffb, 2), [(0, blk)]
+    up_rows = [(0, blk)]
 
     def push_pairs(name, g, rows):
         for k, (at_row, count) in enumerate(rows):
@@ -905,23 +920,8 @@
             results[name],
         )
 
-    jobs = []
-    for k, (at_row, count) in enumerate(down_rows):
-        jobs.append(("down", [("down", k)], at_row, 0, count, 1024))
-    for name, lead in (("gate", 0), ("up", Y)):
-        for k, (at_row, count) in enumerate(up_rows):
-            jobs.append(("up", [(name, "mine", k), (name, "theirs", k)], at_row, lead, count, S * ffb))
-    received = {}
-
-    def update(limit):
-        for name in list(reps.done):
-            if name[1] == "theirs" and name not in received:
-                received[name] = at.core(reps.done[name])
-        while jobs and limit and all(k in reps.done for k in jobs[0][1]):
-            name, needs, at_row, lead, count, unit = jobs.pop(0)
-            rb = max(n for n in range(8, min(count, 176) + 1, 8) if count % n == 0 and at_row % n == 0)
-            adam(name, [received[k] if k[1] == "theirs" else reps.done[k] for k in needs], at_row, lead, unit, rb)
-            limit -= 1
+    def adam_both(name, mine, theirs, lead, unit):
+        adam(name, [mine, theirs], 0, lead, unit, min(blk, 128))
 
     def ticks(n):
         for _ in range(n):
@@ -935,9 +935,7 @@
     n, start, finish, gate_all = gather_steps([gate0[None, None], gate1[None, None]], 1)
     start(0)
     g_down = do(lambda a, c: mm(a, c, PLAIN, bf16, tn=512), act, cot_all)
-    for k, (at_row, count) in enumerate(down_rows):
-        reps.push(("down", k), g_down[at_row : at_row + count])
-    ticks(1)
+    g_down = lax.psum_scatter(g_down, "rep", scatter_dimension=0, tiled=True)
 
     steps2 = at.steps(False) + [("core", 1)]
 
@@ -954,7 +952,6 @@
         sums = do(lambda a, b: a + b, sums, sums_got)
         sums_got = sum_send(sums, *tiny.pop(0))
         start(i, sums)
-        ticks(1)
     n, start_up, finish_up, up_all = gather_steps([up0[None, None], up1[None, None]], 1)
     ggate_all = gate_all().reshape(Y * S * ffb, T)
     sums = do(lambda a, b: a + b, sums, sums_got)
@@ -963,14 +960,15 @@
         sums = sum_step(sums, *tiny.pop(0))
     g_gate = do(lambda x, g: mm(x, g, LAST, bf16, tn=wide), xn2, ggate_all)
     push_pairs("gate", g_gate, up_rows)
+    ticks(1)
     finish_up()
     for i in range(1, n):
         start_up(i)
         if i == 1:
-            ticks(1)
+            g_down = lax.all_gather(do(lambda g: g, g_down), "rep", axis=0, tiled=True)
             part_gate = do(lambda w, g: mm(w, g, PLAIN, f32, tn=256), wg, ggate_all)
             out_part = do(lambda w, a: mm(w, a, FIRST, bf16, tm=512), wd_own, act)
-            update(1)
+            ticks(1)
         if i < n - 1:
             finish_up()
     gup_all = up_all().reshape(Y * S * ffb, T)
@@ -988,7 +986,6 @@
     )
     n, start, finish, branch_all = gather_steps(quarter_heads(grad_branch), 1)
     start(0)
-    ticks(1)
     g_up = do(lambda x, g: mm(x, g, LAST, bf16, tn=wide), xn2, gup_all)
     push_pairs("up", g_up, up_rows)
     finish()
@@ -1011,29 +1008,28 @@
     start(0)
     attn = lanes(*attns)
     g_out = do(lambda a, g: mm(a, g, LAST, bf16, tn=512), attn, gbr)
-    out_pair = PairSum(do, g_out)
+    p_out = PairSum(do, g_out)
     ticks(1)
     finish()
     for i in range(1, n):
         start(i)
         if i == 1:
-            out_pair.step()
-            update(1)
+            p_out.step()
+            adam("down", [g_down], 0, 0, width // 2, 176)
             ticks(1)
-            out_pair.step()
-            update(1)
+            p_out.step()
         if i < n - 1:
             finish()
     gqkv = gqkv_done().reshape(3, Y * S * blk, T)
-    pairs = []
+    p_qkv = {}
     for third in (2, 1, 0):
-        g = do(lambda x, g: dot(x, g, LAST).astype(bf16), xn1, gqkv[third])
-        pairs.append(PairSum(do, g))
-    ticks(1)
+        g = do(lambda x, g: mm(x, g, LAST, bf16, tn=512), xn1, gqkv[third])
+        p_qkv[third] = PairSum(do, g)
+    gate_theirs = at.core(reps.done[("gate", "theirs", 0)])
     part = do(lambda w, g: dot(w, g, PLAIN), wq, gqkv.reshape(3 * Y * S * blk, T))
     part_theirs = at.core(part[blk:])
-    pairs[0].step()
-    out_pair.step()
+    ticks(1)
+    p_qkv[2].step()
     out_sum = lax.psum_scatter(out_part, plane, scatter_dimension=0, tiled=True)
 
     def first_back(a, b, x, mean, inv, gain, gxn2, z2, gqkv0, gqkv1):
@@ -1056,11 +1052,14 @@
     sums, small, gxn1, z1 = do(
         first_back, part[:blk], part_theirs, x_own, mean1, inv1, own_cols[:, 0:1], gxn2, z2, *gqkvs
     )
+    p_qkv[1].step()
+    p_qkv[0].step()
+    adam_both("up", reps.done[("gate", "mine", 0)], gate_theirs, 0, S * ffb)
+    p_out.step()
     sums = sum_step(sums, *steps2[0])
-    pairs[1].step()
+    p_qkv[2].step()
     for axis, step in steps2[1:]:
         sums = sum_step(sums, axis, step)
-    pairs[2].step()
     input_grad = do(
         lambda h, grad, z, scale, gain, sums: h
         + scale * (grad * gain - sums[0:1] / width - z * (sums[1:2] / width)),
@@ -1071,42 +1070,37 @@
         own_cols[:, 0:1],
         sums,
     )
+    while reps.busy():
+        reps.tick()
+    up_theirs = at.core(reps.done[("up", "theirs", 0)])
 
     def to_rows(cols):
         split = do(lambda c: c.reshape(blk, S, at.ctx_size, rows).transpose(2, 1, 0, 3).reshape(nb, blk, rows), cols)
         got = lax.all_to_all(split, plane, split_axis=0, concat_axis=0, tiled=True)
         return do(lambda g: g.reshape(width, rows).T, got)
 
-    def adam_qkv(third, pair):
-        mine, theirs = pair.done
-        adam("qkv", [mine, at.core(theirs)], 0, third * Y, S * blk, min(blk, 128))
-
-    ticks(1)
-    update(1)
-    pairs[0].step()
+    def adam_qkv(third):
+        mine, theirs = p_qkv[third].done
+        adam_both("qkv", mine, at.core(theirs), third * Y, S * blk)
+
+    p_qkv[1].step()
+    input_rows = to_rows(input_grad)
+    p_qkv[0].step()
+    adam_both("up", reps.done[("up", "mine", 0)], up_theirs, Y, S * ffb)
+    for k, g in enumerate(p_out.done):
+        adam("out", [g], k * blk // 2, 0, width // 2, blk // 2)
+    p_qkv[2].step()
+    adam_qkv(2)
     n_rep = lax.axis_size("rep")
     step = 1
     while step < n_rep:
         other = lax.ppermute(small, "rep", [(i, i ^ step) for i in range(n_rep)])
         small = do(lambda a, b: a + b, small, other)
         step *= 2
-    for k, g in enumerate(out_pair.done):
-        adam("out", [g], k * blk // 2, 0, width // 2, blk // 2)
-    ticks(1)
-    input_rows = to_rows(input_grad)
-    pairs[1].step()
-    update(1)
-    while reps.busy():
-        reps.tick()
-        update(1)
+    p_qkv[1].step()
+    adam_qkv(1)
     out_cols = do(lambda h, a: (h + a.astype(f32)).astype(bf16), hidden, out_sum)
-    pairs[0].step()
-    adam_qkv(2, pairs[0])
-    pairs[2].step()
-    pairs[1].step()
-    update(len(jobs))
     block_output = to_rows(out_cols)
-    adam_qkv(1, pairs[1])
     sent = do(lambda s: jnp.broadcast_to(s.reshape(1, 7, blk), (nb, 7, blk)), small)
     small_all = lax.all_to_all(sent, plane, split_axis=0, concat_axis=0, tiled=True)
 
@@ -1114,8 +1108,8 @@
         return adam_update(*a, every.transpose(1, 0, 2).reshape(7, width), 0.3, 0.0)
 
     mn, vn, wn = do(norm_update, small_all, norm_params, m_norm, v_norm)
-    pairs[2].step()
-    adam_qkv(0, pairs[2])
+    p_qkv[0].step()
+    adam_qkv(0)
     return (
         (block_output.reshape(tokens.shape), input_rows.reshape(tokens.shape))
         + tuple(results["qkv"])

time: 913 us -> 908 us (level)
  waiting for transfers between devices: 360 us -> 346 us
  other arithmetic: 68.3 us -> 77.7 us
    ppermute x4 -> x2, waiting for transfers between devices: 68.3 us -> 1.83 us  [tick(): slot['out_got'] = lax.ppermute(out['total'], 'rep', [(1, 0), (2, 3)])]
    ppermute x12, waiting for transfers between devices: 61.6 us -> 90.4 us  [exchange(): lax.ppermute(x, 'rep', [(i, i ^ step) for i in range(lax.axis_size('rep'))])]
    ppermute x18, waiting for transfers between devices: 48.3 us -> 75.5 us  [along(): return lax.ppermute(x, 'shard', [(i, i ^ step) for i in range(self.s_size)])]
    optimization_barrier x5 -> x3, local copies, waits for them, and re-layouts: 16.3 us -> 2.04 us  [__call__(): args, self.last = lax.optimization_barrier((args, self.last))]
    ppermute x2, starting transfers between devices: 2.59 us -> 15.2 us  [tick(): got = lax.ppermute(out['total'], 'rep', [(0, 1), (1, 0), (2, 3), (3, 2)])]
    ppermute x4 -> x2, starting transfers between devices: 20.5 us -> 9.71 us  [tick(): slot['in_got'] = lax.ppermute(out['new'], 'rep', [(0, 1), (3, 2)])]
    ppermute x4 -> x2, waiting for transfers between devices: 62.6 us -> 52.1 us  [tick(): slot['in_got'] = lax.ppermute(out['new'], 'rep', [(0, 1), (3, 2)])]
    another operation x4, local copies, waits for them, and re-layouts: 0.32 us -> 9.52 us  [gain_products(): out.append(jnp.stack([p[0] + p[1], p[2] + p[3]]).reshape(2, Y, S, ffb))]
  transfers between devices with their start and end apart: 90 -> 87, of which waited for: 42 -> 39; matrix products, arithmetic and copies ran while one was open for 16% -> 16% of each run, Pallas kernels for 20% -> 20%
where the time goes in v11:
time: 908 us; the launch traced here: 897 us
  waiting for transfers between devices  346 us (38%)
  Pallas kernels  201 us (22%)
  starting transfers between devices  109 us (12%)
  local copies, waits for them, and re-layouts  103 us (11%)
  other arithmetic  77.7 us (9%)
  matrix products  43.8 us (5%)
  between operations  16.2 us (2%)
    ppermute x12, waiting for transfers between devices, exchange(): lax.ppermute(x, 'rep', [(i, i ^ step) for i in range(lax.axis_size('rep'))])  90.4 us
    ppermute x18, waiting for transfers between devices, along(): lax.ppermute(x, 'ctx', [(i, i ^ 2 * step) for i in range(self.ctx_size)])  77.8 us
    ppermute x18, waiting for transfers between devices, along(): return lax.ppermute(x, 'shard', [(i, i ^ step) for i in range(self.s_size)])  75.5 us
    pallas_call x8, Pallas kernels, adam_part(): pl.pallas_call(functools.partial(adam_kernel, rate, two), grid_spec=pltpu...  67.7 us
    unnamed x281, local copies, waits for them, and re-layouts  57.8 us
    ppermute x2, waiting for transfers between devices, tick(): slot['in_got'] = lax.ppermute(out['new'], 'rep', [(0, 1), (3, 2)])  52.1 us
    dot_general x19, matrix products, dot(): return lax.dot_general(a, b, dims, preferred_element_type=f32)  43.8 us
    pallas_call x10, Pallas kernels, mm(): pl.pallas_call(functools.partial(product_kernel, dims), grid=(m // tm, n...  41.2 us
  transfers between devices with their start and end apart: 87, of which 39 were waited for; matrix products, arithmetic and copies ran while one was open for 16% of the time, Pallas kernels for 20%

profile of v11, /device:TPU:0, one launch (start us, length us, event | category | flops | bytes accessed | tf_op | source)
XLA Modules:
  0.0 896.9 jit_solution(7909008468007533052)
XLA Ops:
  20.3 4.8 all-to-all-start
  74.4 9.5 %collective-permute-done.3.b_ref.d_ref = bf16[1536,512]{1,0:T(8,128)(2,1)} collective-permute-done((bf16[1536,512]{1,0:T(8,128)(2,1)}, bf16[1536,512]{1,0:T(8,128)(2,1)}, u32[]{:S(2)}, u32[]{:S(2)}) %collective-permute-start.3) | collective-permute-done | bytes 1572896 | tf_op jit(solution)/shard_map/ppermute | solution.py:62
  98.3 10.5 %collective-permute-done.4 = bf16[768,512]{1,0:T(8,128)(2,1)} collective-permute-done((bf16[768,512]{1,0:T(8,128)(2,1)}, bf16[768,512]{1,0:T(8,128)(2,1)}, u32[]{:S(2)}, u32[]{:S(2)}) %collective-permute-start.4) | collective-permute-done | bytes 786464 | tf_op jit(solution)/shard_map/ppermute | solution.py:61
  111.6 5.1 shard_map.316
  121.1 5.1 shard_map.317
  155.3 5.1 pad_maximum_fusion.3
  167.9 6.5 collective-permute-done.12
  200.8 5.0 convolution_convert_fusion.1.a_ref.c_ref
  222.1 5.6 shard_map.325.grad_ref
  235.6 19.8 %collective-permute-done.20 = f32[4,2,1,704]{3,0,2,1:T(4,128)S(1)} collective-permute-done((f32[4,2,1,704]{3,0,2,1:T(4,128)S(1)}, f32[4,2,1,704]{3,0,2,1:T(4,128)S(1)}, u32[]{:S(2)}, u32[]{:S(2)}) %collective-permute-start.20) | collective-permute-done | bytes 22560 | tf_op jit(solution)/shard_map/ppermute | solution.py:62
  258.7 8.4 collective-permute-done.21
  276.9 26.1 %collective-permute-done.22.gb_ref = bf16[704,1024]{1,0:T(8,128)(2,1)S(1)} collective-permute-done((bf16[704,1024]{1,0:T(8,128)(2,1)S(1)}, bf16[704,1024]{1,0:T(8,128)(2,1)S(1)}, u32[]{:S(2)}, u32[]{:S(2)}) %collective-permute-start.22) | collective-permute-done | bytes 1441824 | tf_op jit(solution)/shard_map/ppermute | solution.py:61
  303.0 4.9 collective-permute-done.24.ub_ref
  309.1 7.5 shard_map.331
  317.9 6.4 shard_map.332
  328.2 12.6 %collective-permute-done.25 = bf16[1,1,704,512]{3,2,1,0:T(8,128)(2,1)S(1)} collective-permute-done((bf16[1,1,704,512]{3,2,1,0:T(8,128)(2,1)S(1)}, bf16[1,1,704,512]{3,2,1,0:T(8,128)(2,1)S(1)}, u32[]{:S(2)}, u32[]{:S(2)}) %collective-permute-start.25) | collective-permute-done | bytes 720928 | tf_op jit(solution)/shard_map/ppermute | solution.py:61
  345.9 26.5 %collective-permute-done.28.got0_ref = bf16[2,1,704,512]{3,2,1,0:T(8,128)(2,1)S(1)} collective-permute-done((bf16[2,1,704,512]{3,2,1,0:T(8,128)(2,1)S(1)}, bf16[2,1,704,512]{3,2,1,0:T(8,128)(2,1)S(1)}, u32[]{:S(2)}, u32[]{:S(2)}) %collective-permute-start.28) | collective-permute-done | bytes 1441824 | tf_op jit(solution)/shard_map/ppermute | solution.py:62
  378.4 5.7 shard_map.334
  385.9 4.5 collective-permute-start.36
  400.4 5.8 shard_map.335
  407.5 5.3 shard_map.336
  412.9 7.6 collective-permute-done.36
  422.6 7.5 collective-permute-done.34.got0_ref
  432.1 7.1 shard_map.337
  439.2 5.2 convolution_add_fusion.2
  447.8 5.2 collective-permute-start.42
  458.5 5.7 shard_map.338
  468.4 44.6 %collective-permute-done.42 = bf16[256,2816]{1,0:T(8,128)(2,1)S(1)} collective-permute-done((bf16[256,2816]{1,0:T(8,128)(2,1)}, bf16[256,2816]{1,0:T(8,128)(2,1)S(1)}, u32[]{:S(2)}, u32[]{:S(2)}) %collective-permute-start.42) | collective-permute-done | bytes 1441824 | tf_op jit(solution)/shard_map/ppermute | solution.py:197
  522.4 13.2 %collective-permute-start.47 = (bf16[256,2816]{1,0:T(8,128)(2,1)}, bf16[256,2816]{1,0:T(8,128)(2,1)}, u32[]{:S(2)}, u32[]{:S(2)}) collective-permute-start(bf16[256,2816]{1,0:T(8,128)(2,1)} %fusion), channel_id=1, source_target_pairs={{0,8},{8,0},{16,24},{24,16},{1,9},{9,1},{17,25},{25,17},{2,10},{10... | collective-permute-start | bytes 4325384 | tf_op jit(solution)/shard_map/ppermute | solution.py:192
  541.6 5.4 shard_map.340
  547.8 5.5 shard_map.341
  556.5 11.7 %collective-permute-done.47 = bf16[256,2816]{1,0:T(8,128)(2,1)} collective-permute-done((bf16[256,2816]{1,0:T(8,128)(2,1)}, bf16[256,2816]{1,0:T(8,128)(2,1)}, u32[]{:S(2)}, u32[]{:S(2)}) %collective-permute-start.47) | collective-permute-done | bytes 1441824 | tf_op jit(solution)/shard_map/ppermute | solution.py:192
  588.7 14.8 %shard_map.343 = (f32[704,2048]{1,0:T(8,128)}, f32[704,2048]{1,0:T(8,128)}, f32[704,2048]{1,0:T(8,128)}) custom-call(s32[1]{0:T(128)} %bitcast.8.core_ref, f32[704,2048]{1,0:T(8,128)} %w_ref.6, f32[704,2048]{1,0:T(8,128)} %m_ref, f32[704,2048]{1,0:T(8,128)} %v_ref, bf16[704,2048]{1,0:T(8,128)(2,1)S(1)} %copy-done.42), custom_call_target="tpu_custom_call" | custom-call | flops 1024 | bytes 1024 | tf_op jit(solution)/shard_map/pallas_call | solution.py:528
  603.8 7.4 collective-permute-done.53
  617.6 17.2 %collective-permute-done.52 = bf16[128,2048]{1,0:T(8,128)(2,1)} collective-permute-done((bf16[128,2048]{1,0:T(8,128)(2,1)}, bf16[128,2048]{1,0:T(8,128)(2,1)}, u32[]{:S(2)}, u32[]{:S(2)}) %collective-permute-start.52) | collective-permute-done | bytes 524320 | tf_op jit(solution)/shard_map/ppermute | solution.py:242
  648.2 9.7 %shard_map.344 = bf16[3,2,2,256,1024]{4,3,2,1,0:T(8,128)(2,1)} custom-call(s32[4]{0:T(128)S(1)} %pad_add_fusion.1.bits_ref, bf16[2,1,768,512]{3,2,1,0:T(8,128)(2,1)S(1)} %pad_maximum_fusion.1.own0_ref, bf16[2,1,768,512]{3,2,1,0:T(8,128)(2,1)} %collective-permute-done.49.got0_ref, bf16[1,2,768,512]{3,2,1,0:T(8,128)(2,1)S(1)} %pad_maximum_fusion.2.own1_ref, ...), custom_call_target="tpu_custom_call" | custom-call | flops 1024 | bytes 1024 | tf_op jit(solution)/shard_map/pallas_call | solution.py:441
  667.9 5.5 fusion.44
  677.4 24.7 %collective-permute-done.57 = bf16[256,1024]{1,0:T(8,128)(2,1)S(1)} collective-permute-done((bf16[256,1024]{1,0:T(8,128)(2,1)S(1)}, bf16[256,1024]{1,0:T(8,128)(2,1)S(1)}, u32[]{:S(2)}, u32[]{:S(2)}) %collective-permute-start.57) | collective-permute-done | bytes 524320 | tf_op jit(solution)/shard_map/ppermute | solution.py:242
  708.5 17.5 %collective-permute-done.65 = bf16[256,1024]{1,0:T(8,128)(2,1)S(1)} collective-permute-done((bf16[256,1024]{1,0:T(8,128)(2,1)S(1)}, bf16[256,1024]{1,0:T(8,128)(2,1)S(1)}, u32[]{:S(2)}, u32[]{:S(2)}) %collective-permute-start.65) | collective-permute-done | bytes 524320 | tf_op jit(solution)/shard_map/ppermute | solution.py:242
  727.9 13.2 %shard_map.348 = (f32[256,11264]{1,0:T(8,128)}, f32[256,11264]{1,0:T(8,128)}, f32[256,11264]{1,0:T(8,128)}) custom-call(s32[1]{0:T(128)} %bitcast.8.core_ref, f32[256,11264]{1,0:T(8,128)} %w_ref.8, f32[256,11264]{1,0:T(8,128)} %m_ref.2, f32[256,11264]{1,0:T(8,128)} %v_ref.2, bf16[256,2816]{1,0:T(8,128)(2,1)S(1)} %broadcast_select_fusion.3.refs_0_, ...), custom_call_target="tpu_custom_call" | custom-call | flops 1024 | bytes 1024 | tf_op jit(solution)/shard_map/pallas_call | solution.py:528
  753.2 21.5 %collective-permute-done.60 = bf16[256,1024]{1,0:T(8,128)(2,1)S(1)} collective-permute-done((bf16[256,1024]{1,0:T(8,128)(2,1)S(1)}, bf16[256,1024]{1,0:T(8,128)(2,1)S(1)}, u32[]{:S(2)}, u32[]{:S(2)}) %collective-permute-start.60) | collective-permute-done | bytes 524320 | tf_op jit(solution)/shard_map/ppermute | solution.py:242
  787.8 10.2 %all-to-all-done.1 = f32[8,256,128]{2,1,0:T(8,128)} async-done(((f32[8,256,128]{2,1,0:T(8,128)}), f32[8,256,128]{2,1,0:T(8,128)}, u32[]{:S(2)}, u32[]{:S(2)}) %all-to-all-start.1) | async-done | bytes 1048608 | tf_op jit(solution)/shard_map/all_to_all | solution.py:1079
  800.5 9.4 %collective-permute-done.73 = bf16[256,1024]{1,0:T(8,128)(2,1)} collective-permute-done((bf16[256,1024]{1,0:T(8,128)(2,1)}, bf16[256,1024]{1,0:T(8,128)(2,1)}, u32[]{:S(2)}, u32[]{:S(2)}) %collective-permute-start.73) | collective-permute-done | bytes 524320 | tf_op jit(solution)/shard_map/ppermute | solution.py:242
  812.1 14.5 %shard_map.349 = (f32[256,11264]{1,0:T(8,128)}, f32[256,11264]{1,0:T(8,128)}, f32[256,11264]{1,0:T(8,128)}) custom-call(s32[1]{0:T(128)} %bitcast.8.core_ref, f32[256,11264]{1,0:T(8,128)} %w_ref.8, f32[256,11264]{1,0:T(8,128)} %m_ref.2, f32[256,11264]{1,0:T(8,128)} %v_ref.2, ...), custom_call_target="tpu_custom_call", output_to_operand_aliasing={{0}: (6, {}), {1}: (7, {}), {2}: (8, {})} | custom-call | flops 1024 | bytes 1024 | tf_op jit(solution)/shard_map/pallas_call | solution.py:528
  837.7 6.3 shard_map.352
  844.0 5.8 collective-permute-done.70
  865.5 6.3 shard_map.353
  881.4 6.2 shard_map.354
  (638 shorter events, 381.1 us)
Async XLA Ops:
  25.1 195.1 %all-gather.3.cloned.1.call-start = ((), (), s32[]{:S(2)}) async-start(), calls=%async_computation.6 | async-start | bytes 4718592 | tf_op jit(solution)/shard_map/all_gather | solution.py:708
  47.2 36.8 %collective-permute-start.3 = (bf16[1536,512]{1,0:T(8,128)(2,1)}, bf16[1536,512]{1,0:T(8,128)(2,1)}, u32[]{:S(2)}, u32[]{:S(2)}) collective-permute-start(bf16[1536,512]{1,0:T(8,128)(2,1)} %convolution_convert_fusion.7), channel_id=1, source_target_pairs={{0,1},{1,0},{2,3},{3,2},{4,5},{5,4},{6,7},{7,6},{8,9},{9,8},{10,11... | collective-permute-start | bytes 4718600 | tf_op jit(solution)/shard_map/ppermute | solution.py:62
  50.2 40.1 %collective-permute-start.5 = (bf16[1536,512]{1,0:T(8,128)(2,1)}, bf16[1536,512]{1,0:T(8,128)(2,1)}, u32[]{:S(2)}, u32[]{:S(2)}) collective-permute-start(bf16[1536,512]{1,0:T(8,128)(2,1)} %convolution_convert_fusion.6), channel_id=1, source_target_pairs={{0,4},{2,6},{4,0},{6,2},{1,5},{3,7},{5,1},{7,3},{8,12},{10,14},{12... | collective-permute-start | bytes 4718600 | tf_op jit(solution)/shard_map/ppermute | solution.py:61
  96.2 22.1 %collective-permute-start.7 = (bf16[768,512]{1,0:T(8,128)(2,1)}, bf16[768,512]{1,0:T(8,128)(2,1)}, u32[]{:S(2)}, u32[]{:S(2)}) collective-permute-start(bf16[768,512]{1,0:T(8,128)(2,1)} %get-tuple-element.464), channel_id=1, source_target_pairs={{0,1},{1,0},{2,3},{3,2},{4,5},{5,4},{6,7},{7,6},{8,9},{9,8},{10,11... | collective-permute-start | bytes 2359304 | tf_op jit(solution)/shard_map/ppermute | solution.py:62
  128.2 272.0 %reduce-scatter.3.cloned.1.call-start = ((), (), s32[]{:S(2)}) async-start(), calls=%async_computation.7 | async-start | bytes 3604480 | tf_op jit(solution)/shard_map/reduce_scatter | solution.py:938
  133.3 27.1 %collective-permute-start.9 = (bf16[512,512]{1,0:T(8,128)(2,1)}, bf16[512,512]{1,0:T(8,128)(2,1)}, u32[]{:S(2)}, u32[]{:S(2)}) collective-permute-start(bf16[512,512]{1,0:T(8,128)(2,1)} %convolution_convert_fusion.11), channel_id=1, source_target_pairs={{0,1},{1,0},{2,3},{3,2},{4,5},{5,4},{6,7},{7,6},{8,9},{9,8},{10,11... | collective-permute-start | bytes 1572872 | tf_op jit(solution)/shard_map/ppermute | solution.py:62
  135.5 28.8 %collective-permute-start.13 = (bf16[512,512]{1,0:T(8,128)(2,1)}, bf16[512,512]{1,0:T(8,128)(2,1)}, u32[]{:S(2)}, u32[]{:S(2)}) collective-permute-start(bf16[512,512]{1,0:T(8,128)(2,1)} %convolution_convert_fusion.10), channel_id=1, source_target_pairs={{0,4},{2,6},{4,0},{6,2},{1,5},{3,7},{5,1},{7,3},{8,12},{10,14},{12... | collective-permute-start | bytes 1572872 | tf_op jit(solution)/shard_map/ppermute | solution.py:61
  190.1 77.7 %collective-permute-start.19 = (bf16[1408,1024]{1,0:T(8,128)(2,1)}, bf16[1408,1024]{1,0:T(8,128)(2,1)}, u32[]{:S(2)}, u32[]{:S(2)}) collective-permute-start(bf16[1408,1024]{1,0:T(8,128)(2,1)} %convolution_convert_fusion.3), channel_id=1, source_target_pairs={{0,1},{1,0},{2,3},{3,2},{4,5},{5,4},{6,7},{7,6},{8,9},{9,8},{10,11... | collective-permute-start | bytes 8650760 | tf_op jit(solution)/shard_map/ppermute | solution.py:62
  194.8 77.4 %collective-permute-start.23 = (bf16[1408,1024]{1,0:T(8,128)(2,1)}, bf16[1408,1024]{1,0:T(8,128)(2,1)}, u32[]{:S(2)}, u32[]{:S(2)}) collective-permute-start(bf16[1408,1024]{1,0:T(8,128)(2,1)} %convolution_convert_fusion.2), channel_id=1, source_target_pairs={{0,4},{2,6},{4,0},{6,2},{1,5},{3,7},{5,1},{7,3},{8,12},{10,14},{12... | collective-permute-start | bytes 8650760 | tf_op jit(solution)/shard_map/ppermute | solution.py:61
  199.3 56.1 %collective-permute-start.20 = (f32[4,2,1,704]{3,0,2,1:T(4,128)S(1)}, f32[4,2,1,704]{3,0,2,1:T(4,128)S(1)}, u32[]{:S(2)}, u32[]{:S(2)}) collective-permute-start(f32[4,2,1,704]{3,0,2,1:T(4,128)S(1)} %copy.123), channel_id=1, source_target_pairs={{0,1},{1,0},{2,3},{3,2},{4,5},{5,4},{6,7},{7,6},{8,9},{9,8},{10,11... | collective-permute-start | bytes 67592 | tf_op jit(solution)/shard_map/ppermute | solution.py:62
  270.8 32.2 %collective-permute-start.22 = (bf16[704,1024]{1,0:T(8,128)(2,1)S(1)}, bf16[704,1024]{1,0:T(8,128)(2,1)S(1)}, u32[]{:S(2)}, u32[]{:S(2)}) collective-permute-start(bf16[704,1024]{1,0:T(8,128)(2,1)S(1)} %get-tuple-element.556), channel_id=1, source_target_pairs={{0,4},{2,6},{4,0},{6,2},{1,5},{3,7},{5,1},{7,3},{8,12},{10,14},{12... | collective-permute-start | bytes 4325384 | tf_op jit(solution)/shard_map/ppermute | solution.py:61
  276.2 31.7 %collective-permute-start.24 = (bf16[704,1024]{1,0:T(8,128)(2,1)S(1)}, bf16[704,1024]{1,0:T(8,128)(2,1)S(1)}, u32[]{:S(2)}, u32[]{:S(2)}) collective-permute-start(bf16[704,1024]{1,0:T(8,128)(2,1)S(1)} %get-tuple-element.560), channel_id=1, source_target_pairs={{0,1},{1,0},{2,3},{3,2},{4,5},{5,4},{6,7},{7,6},{8,9},{9,8},{10,11... | collective-permute-start | bytes 4325384 | tf_op jit(solution)/shard_map/ppermute | solution.py:62
  324.4 262.4 %all-gather.5.cloned.1.call-start = ((), (), s32[]{:S(2)}) async-start(), calls=%async_computation.9 | async-start | bytes 3604480 | tf_op jit(solution)/shard_map/all_gather | solution.py:968
  342.5 29.9 %collective-permute-start.28 = (bf16[2,1,704,512]{3,2,1,0:T(8,128)(2,1)S(1)}, bf16[2,1,704,512]{3,2,1,0:T(8,128)(2,1)S(1)}, u32[]{:S(2)}, u32[]{:S(2)}) collective-permute-start(bf16[2,1,704,512]{3,2,1,0:T(8,128)(2,1)S(1)} %pad_maximum_fusion.4.own0_ref), channel_id=1, source_target_pairs={{0,1},{1,0},{2,3},{3,2},{4,5},{5,4},{6,7},{7,6},{8,9},{9,8},{10,11... | collective-permute-start | bytes 4325384 | tf_op jit(solution)/shard_map/ppermute | solution.py:62
  343.8 28.8 %collective-permute-start.29 = (bf16[1,2,704,512]{3,2,1,0:T(8,128)(2,1)S(1)}, bf16[1,2,704,512]{3,2,1,0:T(8,128)(2,1)S(1)}, u32[]{:S(2)}, u32[]{:S(2)}) collective-permute-start(bf16[1,2,704,512]{3,2,1,0:T(8,128)(2,1)S(1)} %pad_maximum_fusion.5.own1_ref), channel_id=1, source_target_pairs={{0,4},{2,6},{4,0},{6,2},{1,5},{3,7},{5,1},{7,3},{8,12},{10,14},{12... | collective-permute-start | bytes 4325384 | tf_op jit(solution)/shard_map/ppermute | solution.py:61
  344.6 31.6 %collective-permute-start.30 = (f32[2,1024]{1,0:T(2,128)S(1)}, f32[2,1024]{1,0:T(2,128)S(1)}, u32[]{:S(2)}, u32[]{:S(2)}) collective-permute-start(f32[2,1024]{1,0:T(2,128)S(1)} %add.382), channel_id=1, source_target_pairs={{0,4},{2,6},{4,0},{6,2},{1,5},{3,7},{5,1},{7,3},{8,12},{10,14},{12... | collective-permute-start | bytes 24584 | tf_op jit(solution)/shard_map/ppermute | solution.py:61
  385.9 34.6 %collective-permute-start.36 = (bf16[256,2816]{1,0:T(8,128)(2,1)}, bf16[256,2816]{1,0:T(8,128)(2,1)}, u32[]{:S(2)}, u32[]{:S(2)}) collective-permute-start(bf16[256,2816]{1,0:T(8,128)(2,1)} %get-tuple-element.605), channel_id=1, source_target_pairs={{0,8},{24,16},{1,9},{25,17},{2,10},{26,18},{3,11},{27,19},{4,12},{... | collective-permute-start | bytes 4325384 | tf_op jit(solution)/shard_map/ppermute | solution.py:197
  396.9 33.1 %collective-permute-start.34 = (bf16[2,1,704,512]{3,2,1,0:T(8,128)(2,1)}, bf16[2,1,704,512]{3,2,1,0:T(8,128)(2,1)}, u32[]{:S(2)}, u32[]{:S(2)}) collective-permute-start(bf16[2,1,704,512]{3,2,1,0:T(8,128)(2,1)} %pad_maximum_fusion.6.own0_ref), channel_id=1, source_target_pairs={{0,1},{1,0},{2,3},{3,2},{4,5},{5,4},{6,7},{7,6},{8,9},{9,8},{10,11... | collective-permute-start | bytes 4325384 | tf_op jit(solution)/shard_map/ppermute | solution.py:62
  399.3 32.9 %collective-permute-start.35 = (bf16[1,2,704,512]{3,2,1,0:T(8,128)(2,1)}, bf16[1,2,704,512]{3,2,1,0:T(8,128)(2,1)}, u32[]{:S(2)}, u32[]{:S(2)}) collective-permute-start(bf16[1,2,704,512]{3,2,1,0:T(8,128)(2,1)} %pad_maximum_fusion.7.own1_ref), channel_id=1, source_target_pairs={{0,4},{2,6},{4,0},{6,2},{1,5},{3,7},{5,1},{7,3},{8,12},{10,14},{12... | collective-permute-start | bytes 4325384 | tf_op jit(solution)/shard_map/ppermute | solution.py:61
  446.0 67.0 %collective-permute-start.43 = (bf16[256,2816]{1,0:T(8,128)(2,1)S(1)}, bf16[256,2816]{1,0:T(8,128)(2,1)}, u32[]{:S(2)}, u32[]{:S(2)}) collective-permute-start(bf16[256,2816]{1,0:T(8,128)(2,1)S(1)} %reduce-precision_convert_fusion.7), channel_id=1, source_target_pairs={{8,16},{16,8},{9,17},{17,9},{10,18},{18,10},{11,19},{19,11},{12,20... | collective-permute-start | bytes 4325384 | tf_op jit(solution)/shard_map/ppermute | solution.py:203
  447.8 424.1 %reduce-scatter.5.cloned.1.call-start = ((), (), s32[]{:S(2)}) async-start(), calls=%async_computation.8 | async-start | bytes 4718592 | tf_op jit(solution)/shard_map/reduce_scatter | solution.py:1033
  447.8 65.2 %collective-permute-start.42 = (bf16[256,2816]{1,0:T(8,128)(2,1)}, bf16[256,2816]{1,0:T(8,128)(2,1)S(1)}, u32[]{:S(2)}, u32[]{:S(2)}) collective-permute-start(bf16[256,2816]{1,0:T(8,128)(2,1)} %get-tuple-element.628), channel_id=1, source_target_pairs={{0,8},{24,16},{1,9},{25,17},{2,10},{26,18},{3,11},{27,19},{4,12},{... | collective-permute-start | bytes 4325384 | tf_op jit(solution)/shard_map/ppermute | solution.py:197
  466.1 48.4 %collective-permute-start.40 = (bf16[2,1,256,512]{3,2,1,0:T(8,128)(2,1)S(1)}, bf16[2,1,256,512]{3,2,1,0:T(8,128)(2,1)S(1)}, u32[]{:S(2)}, u32[]{:S(2)}) collective-permute-start(bf16[2,1,256,512]{3,2,1,0:T(8,128)(2,1)S(1)} %pad_maximum_fusion.9.own0_ref), channel_id=1, source_target_pairs={{0,1},{1,0},{2,3},{3,2},{4,5},{5,4},{6,7},{7,6},{8,9},{9,8},{10,11... | collective-permute-start | bytes 1572872 | tf_op jit(solution)/shard_map/ppermute | solution.py:62
  467.2 47.3 %collective-permute-start.41 = (bf16[1,2,256,512]{3,2,1,0:T(8,128)(2,1)S(1)}, bf16[1,2,256,512]{3,2,1,0:T(8,128)(2,1)S(1)}, u32[]{:S(2)}, u32[]{:S(2)}) collective-permute-start(bf16[1,2,256,512]{3,2,1,0:T(8,128)(2,1)S(1)} %pad_maximum_fusion.10.own1_ref), channel_id=1, source_target_pairs={{0,4},{2,6},{4,0},{6,2},{1,5},{3,7},{5,1},{7,3},{8,12},{10,14},{12... | collective-permute-start | bytes 1572872 | tf_op jit(solution)/shard_map/ppermute | solution.py:61
  516.6 51.6 %collective-permute-start.48 = (bf16[256,2816]{1,0:T(8,128)(2,1)}, bf16[256,2816]{1,0:T(8,128)(2,1)}, u32[]{:S(2)}, u32[]{:S(2)}) collective-permute-start(bf16[256,2816]{1,0:T(8,128)(2,1)} %reduce-precision_convert_fusion.6), channel_id=1, source_target_pairs={{8,16},{16,8},{9,17},{17,9},{10,18},{18,10},{11,19},{19,11},{12,20... | collective-permute-start | bytes 4325384 | tf_op jit(solution)/shard_map/ppermute | solution.py:203
  522.4 45.8 %collective-permute-start.47 = (bf16[256,2816]{1,0:T(8,128)(2,1)}, bf16[256,2816]{1,0:T(8,128)(2,1)}, u32[]{:S(2)}, u32[]{:S(2)}) collective-permute-start(bf16[256,2816]{1,0:T(8,128)(2,1)} %fusion), channel_id=1, source_target_pairs={{0,8},{8,0},{16,24},{24,16},{1,9},{9,1},{17,25},{25,17},{2,10},{10... | collective-permute-start | bytes 4325384 | tf_op jit(solution)/shard_map/ppermute | solution.py:192
  547.0 33.6 %collective-permute-start.45 = (bf16[1,1,768,512]{3,2,1,0:T(8,128)(2,1)S(1)}, bf16[1,1,768,512]{3,2,1,0:T(8,128)(2,1)S(1)}, u32[]{:S(2)}, u32[]{:S(2)}) collective-permute-start(bf16[1,1,768,512]{3,2,1,0:T(8,128)(2,1)S(1)} %bitcast.171), channel_id=1, source_target_pairs={{0,4},{2,6},{4,0},{6,2},{1,5},{3,7},{5,1},{7,3},{8,12},{10,14},{12... | collective-permute-start | bytes 2359304 | tf_op jit(solution)/shard_map/ppermute | solution.py:61
  553.3 30.4 %collective-permute-start.46 = (bf16[1,1,768,512]{3,2,1,0:T(8,128)(2,1)S(1)}, bf16[1,1,768,512]{3,2,1,0:T(8,128)(2,1)S(1)}, u32[]{:S(2)}, u32[]{:S(2)}) collective-permute-start(bf16[1,1,768,512]{3,2,1,0:T(8,128)(2,1)S(1)} %bitcast.174), channel_id=1, source_target_pairs={{0,1},{1,0},{2,3},{3,2},{4,5},{5,4},{6,7},{7,6},{8,9},{9,8},{10,11... | collective-permute-start | bytes 2359304 | tf_op jit(solution)/shard_map/ppermute | solution.py:62
  556.5 29.4 %collective-permute-start.51 = (bf16[128,2048]{1,0:T(8,128)(2,1)S(1)}, bf16[128,2048]{1,0:T(8,128)(2,1)S(1)}, u32[]{:S(2)}, u32[]{:S(2)}) collective-permute-start(bf16[128,2048]{1,0:T(8,128)(2,1)S(1)} %get-tuple-element.880), channel_id=1, source_target_pairs={{0,8},{8,0},{16,24},{24,16},{1,9},{9,1},{17,25},{25,17},{2,10},{10... | collective-permute-start | bytes 1572872 | tf_op jit(solution)/shard_map/ppermute | solution.py:242
  571.3 39.9 %collective-permute-start.53 = (bf16[256,2816]{1,0:T(8,128)(2,1)}, bf16[256,2816]{1,0:T(8,128)(2,1)}, u32[]{:S(2)}, u32[]{:S(2)}) collective-permute-start(bf16[256,2816]{1,0:T(8,128)(2,1)} %fusion.1), channel_id=1, source_target_pairs={{0,8},{8,0},{16,24},{24,16},{1,9},{9,1},{17,25},{25,17},{2,10},{10... | collective-permute-start | bytes 4325384 | tf_op jit(solution)/shard_map/ppermute | solution.py:192
  576.2 35.8 %collective-permute-start.54 = (bf16[256,2816]{1,0:T(8,128)(2,1)}, bf16[256,2816]{1,0:T(8,128)(2,1)}, u32[]{:S(2)}, u32[]{:S(2)}) collective-permute-start(bf16[256,2816]{1,0:T(8,128)(2,1)} %reduce-precision_convert_fusion.4), channel_id=1, source_target_pairs={{8,16},{16,8},{9,17},{17,9},{10,18},{18,10},{11,19},{19,11},{12,20... | collective-permute-start | bytes 4325384 | tf_op jit(solution)/shard_map/ppermute | solution.py:203
  580.6 147.3 %collective-permute-start.64 = (bf16[256,2816]{1,0:T(8,128)(2,1)}, bf16[256,2816]{1,0:T(8,128)(2,1)}, u32[]{:S(2)}, u32[]{:S(2)}) collective-permute-start(bf16[256,2816]{1,0:T(8,128)(2,1)} %broadcast_select_fusion.2), channel_id=1, source_target_pairs={{0,2},{2,0},{4,6},{6,4},{1,3},{3,1},{5,7},{7,5},{8,10},{10,8},{12,... | collective-permute-start | bytes 4325384 | tf_op jit(solution)/shard_map/ppermute | solution.py:57
  584.7 55.3 %collective-permute-start.49 = (bf16[2,1,768,512]{3,2,1,0:T(8,128)(2,1)S(1)}, bf16[2,1,768,512]{3,2,1,0:T(8,128)(2,1)}, u32[]{:S(2)}, u32[]{:S(2)}) collective-permute-start(bf16[2,1,768,512]{3,2,1,0:T(8,128)(2,1)S(1)} %pad_maximum_fusion.1.own0_ref), channel_id=1, source_target_pairs={{0,1},{1,0},{2,3},{3,2},{4,5},{5,4},{6,7},{7,6},{8,9},{9,8},{10,11... | collective-permute-start | bytes 4718600 | tf_op jit(solution)/shard_map/ppermute | solution.py:62
  586.7 48.1 %collective-permute-start.52 = (bf16[128,2048]{1,0:T(8,128)(2,1)}, bf16[128,2048]{1,0:T(8,128)(2,1)}, u32[]{:S(2)}, u32[]{:S(2)}) collective-permute-start(bf16[128,2048]{1,0:T(8,128)(2,1)} %reduce-precision_convert_fusion.15), channel_id=1, source_target_pairs={{0,16},{8,24},{16,0},{24,8},{1,17},{9,25},{17,1},{25,9},{2,18},{10... | collective-permute-start | bytes 1572872 | tf_op jit(solution)/shard_map/ppermute | solution.py:242
  611.3 35.8 %collective-permute-start.50 = (bf16[1,2,768,512]{3,2,1,0:T(8,128)(2,1)S(1)}, bf16[1,2,768,512]{3,2,1,0:T(8,128)(2,1)S(1)}, u32[]{:S(2)}, u32[]{:S(2)}) collective-permute-start(bf16[1,2,768,512]{3,2,1,0:T(8,128)(2,1)S(1)} %pad_maximum_fusion.2.own1_ref), channel_id=1, source_target_pairs={{0,4},{2,6},{4,0},{6,2},{1,5},{3,7},{5,1},{7,3},{8,12},{10,14},{12... | collective-permute-start | bytes 4718600 | tf_op jit(solution)/shard_map/ppermute | solution.py:61
  613.7 61.8 %collective-permute-start.59 = (bf16[256,2816]{1,0:T(8,128)(2,1)S(1)}, bf16[256,2816]{1,0:T(8,128)(2,1)}, u32[]{:S(2)}, u32[]{:S(2)}) collective-permute-start(bf16[256,2816]{1,0:T(8,128)(2,1)S(1)} %reduce-precision_convert_fusion.2), channel_id=1, source_target_pairs={{8,16},{16,8},{9,17},{17,9},{10,18},{18,10},{11,19},{19,11},{12,20... | collective-permute-start | bytes 4325384 | tf_op jit(solution)/shard_map/ppermute | solution.py:203
  634.8 38.9 %collective-permute-start.58 = (bf16[256,2816]{1,0:T(8,128)(2,1)S(1)}, bf16[256,2816]{1,0:T(8,128)(2,1)}, u32[]{:S(2)}, u32[]{:S(2)}) collective-permute-start(bf16[256,2816]{1,0:T(8,128)(2,1)S(1)} %reduce-precision_convert_fusion.1), channel_id=1, source_target_pairs={{8,0},{16,24},{9,1},{17,25},{10,2},{18,26},{11,3},{19,27},{12,4},{... | collective-permute-start | bytes 4325384 | tf_op jit(solution)/shard_map/ppermute | solution.py:200
  640.0 101.1 %collective-permute-start.63 = (bf16[128,2048]{1,0:T(8,128)(2,1)}, bf16[128,2048]{1,0:T(8,128)(2,1)}, u32[]{:S(2)}, u32[]{:S(2)}) collective-permute-start(bf16[128,2048]{1,0:T(8,128)(2,1)} %reduce-precision_convert_fusion.14), channel_id=1, source_target_pairs={{0,8},{8,0},{16,24},{24,16},{1,9},{9,1},{17,25},{25,17},{2,10},{10... | collective-permute-start | bytes 1572872 | tf_op jit(solution)/shard_map/ppermute | solution.py:242
  665.8 39.2 %collective-permute-start.55 = (bf16[256,1024]{1,0:T(8,128)(2,1)}, bf16[256,1024]{1,0:T(8,128)(2,1)}, u32[]{:S(2)}, u32[]{:S(2)}) collective-permute-start(bf16[256,1024]{1,0:T(8,128)(2,1)} %get-tuple-element.877), channel_id=1, source_target_pairs={{0,8},{8,0},{16,24},{24,16},{1,9},{9,1},{17,25},{25,17},{2,10},{10... | collective-permute-start | bytes 1572872 | tf_op jit(solution)/shard_map/ppermute | solution.py:242
  673.7 28.5 %collective-permute-start.57 = (bf16[256,1024]{1,0:T(8,128)(2,1)S(1)}, bf16[256,1024]{1,0:T(8,128)(2,1)S(1)}, u32[]{:S(2)}, u32[]{:S(2)}) collective-permute-start(bf16[256,1024]{1,0:T(8,128)(2,1)S(1)} %get-tuple-element.876), channel_id=1, source_target_pairs={{0,8},{8,0},{16,24},{24,16},{1,9},{9,1},{17,25},{25,17},{2,10},{10... | collective-permute-start | bytes 1572872 | tf_op jit(solution)/shard_map/ppermute | solution.py:242
  675.6 26.8 %collective-permute-start.56 = (f32[256,1024]{1,0:T(8,128)S(1)}, f32[256,1024]{1,0:T(8,128)S(1)}, u32[]{:S(2)}, u32[]{:S(2)}) collective-permute-start(f32[256,1024]{1,0:T(8,128)S(1)} %get-tuple-element.847), channel_id=1, source_target_pairs={{0,2},{2,0},{4,6},{6,4},{1,3},{3,1},{5,7},{7,5},{8,10},{10,8},{12,... | collective-permute-start | bytes 3145736 | tf_op jit(solution)/shard_map/ppermute | solution.py:57
  702.2 23.9 %collective-permute-start.65 = (bf16[256,1024]{1,0:T(8,128)(2,1)S(1)}, bf16[256,1024]{1,0:T(8,128)(2,1)S(1)}, u32[]{:S(2)}, u32[]{:S(2)}) collective-permute-start(bf16[256,1024]{1,0:T(8,128)(2,1)S(1)} %get-tuple-element.874), channel_id=1, source_target_pairs={{0,8},{8,0},{16,24},{24,16},{1,9},{9,1},{17,25},{25,17},{2,10},{10... | collective-permute-start | bytes 1572872 | tf_op jit(solution)/shard_map/ppermute | solution.py:242
  702.4 50.8 %collective-permute-start.61 = (bf16[256,2816]{1,0:T(8,128)(2,1)S(1)}, bf16[256,2816]{1,0:T(8,128)(2,1)S(1)}, u32[]{:S(2)}, u32[]{:S(2)}) collective-permute-start(bf16[256,2816]{1,0:T(8,128)(2,1)S(1)} %reduce-precision_convert_fusion), channel_id=1, source_target_pairs={{8,0},{16,24},{9,1},{17,25},{10,2},{18,26},{11,3},{19,27},{12,4},{... | collective-permute-start | bytes 4325384 | tf_op jit(solution)/shard_map/ppermute | solution.py:200
  705.0 39.3 %collective-permute-start.67 = (bf16[256,1024]{1,0:T(8,128)(2,1)S(1)}, bf16[256,1024]{1,0:T(8,128)(2,1)S(1)}, u32[]{:S(2)}, u32[]{:S(2)}) collective-permute-start(bf16[256,1024]{1,0:T(8,128)(2,1)S(1)} %reduce-precision_convert_fusion.13), channel_id=1, source_target_pairs={{0,16},{8,24},{16,0},{24,8},{1,17},{9,25},{17,1},{25,9},{2,18},{10... | collective-permute-start | bytes 1572872 | tf_op jit(solution)/shard_map/ppermute | solution.py:242
  749.6 62.5 %collective-permute-start.72 = (bf16[256,2816]{1,0:T(8,128)(2,1)}, bf16[256,2816]{1,0:T(8,128)(2,1)}, u32[]{:S(2)}, u32[]{:S(2)}) collective-permute-start(bf16[256,2816]{1,0:T(8,128)(2,1)} %broadcast_select_fusion), channel_id=1, source_target_pairs={{0,2},{2,0},{4,6},{6,4},{1,3},{3,1},{5,7},{7,5},{8,10},{10,8},{12,... | collective-permute-start | bytes 4325384 | tf_op jit(solution)/shard_map/ppermute | solution.py:57
  750.1 24.6 %collective-permute-start.60 = (bf16[256,1024]{1,0:T(8,128)(2,1)S(1)}, bf16[256,1024]{1,0:T(8,128)(2,1)S(1)}, u32[]{:S(2)}, u32[]{:S(2)}) collective-permute-start(bf16[256,1024]{1,0:T(8,128)(2,1)S(1)} %reduce-precision_convert_fusion.12), channel_id=1, source_target_pairs={{0,16},{8,24},{16,0},{24,8},{1,17},{9,25},{17,1},{25,9},{2,18},{10... | collective-permute-start | bytes 1572872 | tf_op jit(solution)/shard_map/ppermute | solution.py:242
  783.0 26.9 %collective-permute-start.73 = (bf16[256,1024]{1,0:T(8,128)(2,1)}, bf16[256,1024]{1,0:T(8,128)(2,1)}, u32[]{:S(2)}, u32[]{:S(2)}) collective-permute-start(bf16[256,1024]{1,0:T(8,128)(2,1)} %reduce-precision_convert_fusion.11), channel_id=1, source_target_pairs={{0,16},{8,24},{16,0},{24,8},{1,17},{9,25},{17,1},{25,9},{2,18},{10... | collective-permute-start | bytes 1572872 | tf_op jit(solution)/shard_map/ppermute | solution.py:242
  783.1 50.0 %collective-permute-start.71 = (bf16[256,1024]{1,0:T(8,128)(2,1)}, bf16[256,1024]{1,0:T(8,128)(2,1)}, u32[]{:S(2)}, u32[]{:S(2)}) collective-permute-start(bf16[256,1024]{1,0:T(8,128)(2,1)} %reduce-precision_convert_fusion.10), channel_id=1, source_target_pairs={{0,8},{8,0},{16,24},{24,16},{1,9},{9,1},{17,25},{25,17},{2,10},{10... | collective-permute-start | bytes 1572872 | tf_op jit(solution)/shard_map/ppermute | solution.py:242
  (178 other events, 1284.5 us)
Sparse Core Ops, SparseCore 0:
  128.3 45.7 all-gather.2
  324.5 56.1 reduce-scatter.2
  447.9 83.0 all-gather.4
  534.2 67.4 reduce-scatter.4

commit v12 on v8

--- a/solution.py
+++ b/solution.py
@@ -222,6 +222,70 @@
         compiler_params=pltpu.CompilerParams(vmem_limit_bytes=48 * 1024 * 1024),
         cost_estimate=SMALL,
     )(w)
+
+
+def gated_kernel(ga_ref, gb_ref, ua_ref, ub_ref, grad_ref, gains_ref, ggate_ref, gup_ref, act_ref, sums_ref):
+    gate = ga_ref[...].astype(f32) + gb_ref[...].astype(f32)
+    up = ua_ref[...].astype(f32) + ub_ref[...].astype(f32)
+    sig = jax.nn.sigmoid(gate)
+    silu = gate * sig
+    grad = grad_ref[...]
+    act_ref[...] = (silu * up).astype(bf16)
+    ggate = (grad * up * sig * (1.0 + gate * (1.0 - sig))).astype(bf16)
+    gup = (grad * silu).astype(bf16)
+    ggate_ref[...] = ggate
+    gup_ref[...] = gup
+    a, b = ggate.astype(f32), gup.astype(f32)
+    e = jnp.sum(a * gains_ref[:, 0:1] + b * gains_ref[:, 2:3], axis=0, keepdims=True)
+    ez = jnp.sum(a * (gate - gains_ref[:, 1:2]) + b * (up - gains_ref[:, 3:4]), axis=0, keepdims=True)
+    both = jnp.concatenate([e, ez], axis=0)
+
+    @pl.when(pl.program_id(0) == 0)
+    def _():
+        sums_ref[...] = both
+
+    @pl.when(pl.program_id(0) > 0)
+    def _():
+        sums_ref[...] += both
+
+
+def gated(ga, gb, ua, ub, grad_act, gains):
+    rows, t = grad_act.shape
+    n = max(n for n in (1, 2, 4) if rows % (16 * n) == 0)
+    whole = pl.BlockSpec((rows // n, t), lambda i: (i, 0))
+    out = jax.ShapeDtypeStruct((rows, t), bf16)
+    return pl.pallas_call(
+        gated_kernel,
+        grid=(n,),
+        in_specs=[whole] * 5 + [pl.BlockSpec((rows // n, 4), lambda i: (i, 0))],
+        out_specs=[whole] * 3 + [pl.BlockSpec((2, t), lambda i: (0, 0))],
+        out_shape=[out] * 3 + [jax.ShapeDtypeStruct((2, t), f32)],
+        compiler_params=pltpu.CompilerParams(vmem_limit_bytes=56 * 1024 * 1024),
+        cost_estimate=SMALL,
+    )(ga, gb, ua, ub, grad_act, gains)
+
+
+def own_columns_kernel(block_ref, x_ref, out_ref):
+    out_ref[...] = x_ref[...].T
+
+
+def own_columns(x, block, width):
+    rows = x.shape[0]
+    if width % 128:
+        return lax.dynamic_slice_in_dim(x, block[0] * width, width, 1).T
+    tile = min(rows, 512)
+    return pl.pallas_call(
+        own_columns_kernel,
+        grid_spec=pltpu.PrefetchScalarGridSpec(
+            num_scalar_prefetch=1,
+            grid=(rows // tile,),
+            in_specs=[pl.BlockSpec((tile, width), lambda i, block: (i, block[0]))],
+            out_specs=pl.BlockSpec((width, tile), lambda i, block: (0, i)),
+        ),
+        out_shape=jax.ShapeDtypeStruct((width, rows), bf16),
+        compiler_params=pltpu.CompilerParams(vmem_limit_bytes=48 * 1024 * 1024),
+        cost_estimate=SMALL,
+    )(block, x)
 
 
 def split_kernel(core_ref, w_ref, mine_ref, theirs_ref):
@@ -322,34 +386,6 @@
         compiler_params=pltpu.CompilerParams(vmem_limit_bytes=48 * 1024 * 1024),
         cost_estimate=SMALL,
     )(*((a, b) if add is None else (a, b, add)))
-
-
-def last_step_kernel(bits_ref, own0_ref, got0_ref, own1_ref, got1_ref, out_ref):
-    y, s = pl.program_id(1), pl.program_id(2)
-    half = own0_ref.shape[3]
-    ys, ss = bits_ref[2], bits_ref[3]
-    a = jnp.where(s // ss == bits_ref[1], own0_ref[0, 0], got0_ref[0, 0])
-    b = jnp.where(y // ys == bits_ref[0], own1_ref[0, 0], got1_ref[0, 0])
-    out_ref[0, 0, 0, :, :half] = a
-    out_ref[0, 0, 0, :, half:] = b
-
-
-def last_step(parts, got, bits, pre, y_size, s_size):
-    rows, half = parts[0].shape[2] // pre, parts[0].shape[3]
-    along_s = pl.BlockSpec((1, 1, rows, half), lambda p, y, s, bits: (y, s % (s_size // 2), p, 0))
-    along_y = pl.BlockSpec((1, 1, rows, half), lambda p, y, s, bits: (y % (y_size // 2), s, p, 0))
-    return pl.pallas_call(
-        last_step_kernel,
-        grid_spec=pltpu.PrefetchScalarGridSpec(
-            num_scalar_prefetch=1,
-            grid=(pre, y_size, s_size),
-            in_specs=[along_s, along_s, along_y, along_y],
-            out_specs=pl.BlockSpec((1, 1, 1, rows, 2 * half), lambda p, y, s, bits: (p, y, s, 0, 0)),
-        ),
-        out_shape=jax.ShapeDtypeStruct((pre, y_size, s_size, rows, 2 * half), bf16),
-        compiler_params=pltpu.CompilerParams(vmem_limit_bytes=48 * 1024 * 1024),
-        cost_estimate=SMALL,
-    )(bits, parts[0], got[0], parts[1], got[1])
 
 
 def stack_turned_kernel(a_ref, b_ref, out_ref):
@@ -605,7 +641,7 @@
         return jnp.concatenate([blocks, jnp.broadcast_to(extra[None], (nb, 16, rows))], axis=1)
 
     packed = do(pack, x_rows, order)
-    cot_all = lax.all_gather(cotangent.reshape(rows, width), ("shard", "ctx"), axis=0, tiled=True)
+    cot_all = lax.all_gather(do(cast, cotangent.reshape(rows, width)), ("shard", "ctx"), axis=0, tiled=True)
     got = lax.all_to_all(packed, plane, split_axis=0, concat_axis=0, tiled=True)
 
     def chip_rows(w, lead, unit, count):
@@ -679,40 +715,6 @@
 
     table = do(positions, place)
     flying = scatter_rest(flying)
-
-    def gather_steps(parts, pre):
-        n = len(at.steps(False))
-        state = {"parts": list(parts)}
-
-        def start(i, after=None):
-            if after is not None:
-                state["parts"], _ = lax.optimization_barrier((state["parts"], after))
-            state["got"] = []
-            state["at"] = []
-            for k in range(2):
-                axis, step = list(reversed(at.steps(bool(k))))[i]
-                state["at"].append((axis, step))
-                state["got"].append(at.along(state["parts"][k], axis, step))
-
-        def finish():
-            def put(parts, got):
-                out = []
-                for k in range(2):
-                    axis, step = state["at"][k]
-                    ax = {"y": 0, "s": 1}[axis]
-                    low = (at.index(axis) // step) % 2 == 0
-                    a, b = parts[k], got[k]
-                    out.append(jnp.concatenate([jnp.where(low, a, b), jnp.where(low, b, a)], ax))
-                return out
-
-            state["parts"] = do(put, state["parts"], state["got"])
-
-        def result():
-            ys, ss = Y // 2, S // 2
-            bits = jnp.stack([at.y // ys, at.s // ss, jnp.int32(ys), jnp.int32(ss)]).astype(jnp.int32)
-            return do(lambda p, g: last_step(p, g, bits, pre, Y, S), state["parts"], state["got"])
-
-        return n, start, finish, result
 
     qkvs, attns, attn_got, stats = [], [], [], []
     for k in range(2):
@@ -785,25 +787,16 @@
     wg = do(stack_turned, *wg_parts)
     wu = do(stack_turned, *wu_parts)
     grad_act = do(lambda w, c: mm(w, c, LAST, f32, tn=256), wd_own, cot_all)
-    cot_cols = do(lambda c: lax.dynamic_slice_in_dim(c, my_block * blk, blk, 1).T, cot_all)
+    cot_cols = do(lambda c: own_columns(c, my_block.reshape(1), blk), cot_all)
     wo_own = do(cast, w_out)
     wq = do(stack_turned, *wq_parts)
     gains = do(lambda a, b: a + b, *gains)
     while gain_steps:
         gains = do(lambda a, b: a + b, *gain_step(gains))
-    gains = do(lambda g: g.reshape(4, ffb, 1), gains)
+    gains = do(lambda g: g.reshape(4, ffb).T, gains)
     flying = scatter_rest(flying)
 
-    def gated(ga, gb, ua, ub, grad_act, gains):
-        gate = ga.astype(f32) + gb.astype(f32)
-        up = ua.astype(f32) + ub.astype(f32)
-        sig = jax.nn.sigmoid(gate)
-        silu = gate * sig
-        ggate = (grad_act * up * sig * (1.0 + gate * (1.0 - sig))).astype(bf16)
-        gup = (grad_act * silu).astype(bf16)
-        return ggate, gup, (silu * up).astype(bf16), gate, up
-
-    ggate, gup, act, gate, up = do(gated, *flying[0], *flying[1], grad_act, gains)
+    ggate, gup, act, sums = do(gated, *flying[0], *flying[1], grad_act, gains)
 
     def parts_of(count, want):
         return max(n for n in range(1, want + 1) if count % (16 * n) == 0)
@@ -865,25 +858,22 @@
         for _ in range(n):
             reps.tick()
 
+    same_core = [
+        [(2 * y + c) * S + s for y in range(Y) for s in range(S)] for c in range(2)
+    ]
+
+    def gather_core(x):
+        return lax.all_gather(x, plane, axis=0, tiled=True, axis_index_groups=same_core)
+
     wide = 2 * FF // 8
 
-    def quarter_heads(x):
-        return [x[:, h][None, None] for h in halves]
-
-    n, start, finish, gate_all = gather_steps(quarter_heads(ggate), 1)
-    start(0)
+    ggate_all = gather_core(ggate)
+    gup_all = gather_core(gup)
     g_down = do(lambda a, c: mm(a, c, PLAIN, bf16, tn=512), act, cot_all)
     for k, (at_row, count) in enumerate(down_rows):
         reps.push(("down", k), g_down[at_row : at_row + count])
     ticks(1)
-
-    def norm_sums2(ggate, gup, gate, up, gains):
-        a, b = ggate.astype(f32), gup.astype(f32)
-        e = jnp.sum(a * gains[0] + b * gains[2], axis=0, keepdims=True)
-        ez = jnp.sum(a * (gate - gains[1]) + b * (up - gains[3]), axis=0, keepdims=True)
-        return join(e, ez)
-
-    sums = do(norm_sums2, ggate, gup, gate, up, gains)
+    out_part = do(lambda w, a: mm(w, a, FIRST, bf16, tm=512), wd_own, act)
     steps2 = at.steps(False) + [("core", 1)]
 
     def sum_send(sums, axis, step):
@@ -892,36 +882,15 @@
     def sum_step(sums, axis, step):
         return do(lambda a, b: a + b, sums, sum_send(sums, axis, step))
 
-    tiny = list(steps2)
-    sums_got = sum_send(sums, *tiny.pop(0))
-    for i in range(1, n):
-        finish()
-        sums = do(lambda a, b: a + b, sums, sums_got)
-        sums_got = sum_send(sums, *tiny.pop(0))
-        start(i, sums)
-        ticks(1)
-    n, start_up, finish_up, up_all = gather_steps(quarter_heads(gup), 1)
-    ggate_all = gate_all().reshape(Y * S * ffb, T)
-    sums = do(lambda a, b: a + b, sums, sums_got)
-    start_up(0, sums)
-    while tiny:
-        sums = sum_step(sums, *tiny.pop(0))
+    for axis, step in steps2:
+        sums = sum_step(sums, axis, step)
+    ticks(1)
     g_gate = do(lambda x, g: mm(x, g, LAST, bf16, tn=wide), xn2, ggate_all)
     push_pairs("gate", g_gate, up_rows)
-    finish_up()
-    for i in range(1, n):
-        start_up(i)
-        if i == 1:
-            ticks(1)
-            part_gate = do(lambda w, g: mm(w, g, PLAIN, f32, tn=256), wg, ggate_all)
-            out_part = do(lambda w, a: mm(w, a, FIRST, bf16, tm=512), wd_own, act)
-            update(1)
-        if i < n - 1:
-            finish_up()
-    gup_all = up_all().reshape(Y * S * ffb, T)
-    part = do(lambda w, g, p: dot(w, g, PLAIN) + p, wu, gup_all, part_gate)
+    part_gate = do(lambda w, g: mm(w, g, PLAIN, f32, tn=256), wg, ggate_all)
+    ticks(2)
+    part = do(lambda w, g, p: mm(w, g, PLAIN, f32, tn=256, add=p), wu, gup_all, part_gate)
     part_theirs = at.core(part[blk:])
-    ticks(1)
 
     def branch(a, b, cot, z, scale, gain, sums):
         gxn2 = a + b
@@ -932,55 +901,39 @@
     grad_branch, grad_hidden, gxn2 = do(
         branch, part[:blk], part_theirs, cot_cols, z2, inv2, own_cols[:, 2:3], sums
     )
-    n, start, finish, branch_all = gather_steps(quarter_heads(grad_branch), 1)
-    start(0)
+    gbr = lax.all_gather(grad_branch, plane, axis=0, tiled=True)
     g_up = do(lambda x, g: mm(x, g, LAST, bf16, tn=wide), xn2, gup_all)
     push_pairs("up", g_up, up_rows)
-    finish()
-    for i in range(1, n):
-        start(i)
-        if i == 1:
-            ticks(1)
-        if i < n - 1:
-            finish()
-    gbr_c = branch_all()[0]
-    gbr_o = at.core(gbr_c)
-    gbr = do(lambda a, b: in_order(a, b, 1).reshape(width, T), gbr_c, gbr_o)
-    grad_attn = do(lambda w, g: dot(w, g, PLAIN).astype(bf16), wo_own, gbr)
+    ticks(1)
+    grad_attn = do(lambda w, g: mm(w, g, PLAIN, bf16, tn=256), wo_own, gbr)
 
     gqkvs = []
     for k in range(2):
         dout = grad_attn[:, halves[k]].reshape(heads, HEAD_DIM, H)
         gqkvs.append(do(attend_back, qkvs[k], dout, stats[k], table[seqs[k]]).reshape(3, blk, H))
-    n, start, finish, gqkv_done = gather_steps([g.reshape(1, 1, 3 * blk, H) for g in gqkvs], 3)
-    start(0)
+    gqkv_own = do(lambda a, b: jnp.concatenate([a, b], axis=2).reshape(3 * blk, T), *gqkvs)
+    gqkv = gather_core(gqkv_own)
+    ticks(1)
     attn = lanes(*attns)
     for k in range(2):
         g_out = do(lambda a, g: mm(a, g, LAST, bf16, tn=512), attn, gbr[k * width // 2 : (k + 1) * width // 2])
         reps.push(("out", k), g_out)
-    ticks(1)
-    finish()
-    for i in range(1, n):
-        start(i)
-        if i == 1:
-            update(1)
-            ticks(1)
-            update(1)
-        if i < n - 1:
-            finish()
-    gqkv = gqkv_done().reshape(3, Y * S * blk, T)
+    update(1)
+    ticks(1)
+    update(1)
+    ticks(1)
+    gqkv = do(lambda g: g.reshape(Y * S, 3, blk, T).transpose(1, 0, 2, 3).reshape(3, Y * S * blk, T), gqkv)
+    reps.depth = 2
     for third in (2, 1, 0):
-        g = do(lambda x, g: dot(x, g, LAST).astype(bf16), xn1, gqkv[third])
+        g = do(lambda x, g: mm(x, g, LAST, bf16, tn=512), xn1, gqkv[third])
         push_pairs(third, g, up_rows)
         if third == 2:
             ticks(1)
-    part = do(lambda w, g: dot(w, g, PLAIN), wq, gqkv.reshape(3 * Y * S * blk, T))
+    part = do(lambda w, g: mm(w, g, PLAIN, f32, tn=256), wq, gqkv.reshape(3 * Y * S * blk, T))
     part_theirs = at.core(part[blk:])
-    out_sum = lax.psum_scatter(out_part, plane, scatter_dimension=0, tiled=True)
-    reps.depth = 2
+    out_sum = lax.psum_scatter(do(lambda p: p, out_part), plane, scatter_dimension=0, tiled=True)
     ticks(1)
     update(1)
-    ticks(1)
 
     def first_back(a, b, x, mean, inv, gain, gxn2, z2, gqkv0, gqkv1):
         gxn1 = a + b

time: 866 us -> 889 us (1.027)
  waiting for transfers between devices: 257 us -> 305 us
  matrix products: 47.3 us -> 31.7 us
  other arithmetic: 91.5 us -> 80.6 us
  starting transfers between devices: 145 us -> 136 us
    ppermute x8, waiting for transfers between devices: 32.3 us -> 80.4 us  [tick(): slot['out_got'] = lax.ppermute(out['total'], 'rep', [(1, 0), (2, 3)])]
    ppermute x18 -> x10, waiting for transfers between devices: 102 us -> 67.7 us  [along(): return lax.ppermute(x, 'shard', [(i, i ^ step) for i in range(self.s_size)])]
    ppermute x6, waiting for transfers between devices: 25.3 us -> 49 us  [tick(): got = lax.ppermute(out['total'], 'rep', [(0, 1), (1, 0), (2, 3), (3, 2)])]
    all_gather x1 -> x5, waiting for transfers between devices: 0.01 us -> 23.2 us  [the longest x3 23.2 us: gather_core(): lax.all_gather(x, plane, axis=0, tiled=True, axis_index_groups=same_core)]
    ppermute x8, waiting for transfers between devices: 48.4 us -> 25.8 us  [tick(): slot['in_got'] = lax.ppermute(out['new'], 'rep', [(0, 1), (3, 2)])]
    pallas_call x8 -> x14, Pallas kernels: 35.8 us -> 56.1 us  [mm(): pl.pallas_call(functools.partial(product_kernel, dims), grid=(m // tm, n...]
    dot_general x22 -> x16, matrix products: 47.3 us -> 31.7 us  [dot(): return lax.dot_general(a, b, dims, preferred_element_type=f32)]
    pallas_call x4 -> x2, Pallas kernels: 20.9 us -> 7.92 us  [the longest x1 7.51 us: gated(): pl.pallas_call(gated_kernel, grid=(n,), in_specs=[whole] * 5 + [pl.BlockS...]
  transfers between devices with their start and end apart: 99 -> 86, of which waited for: 39 -> 37; matrix products, arithmetic and copies ran while one was open for 20% -> 16% of each run, Pallas kernels for 21% -> 18%
where the time goes in v12:
time: 889 us; the launch traced here: 877 us
  waiting for transfers between devices  305 us (34%)
  Pallas kernels  196 us (22%)
  starting transfers between devices  136 us (15%)
  local copies, waits for them, and re-layouts  110 us (12%)
  other arithmetic  80.6 us (9%)
  matrix products  31.7 us (4%)
  between operations  16.9 us (2%)
    ppermute x8, waiting for transfers between devices, tick(): slot['out_got'] = lax.ppermute(out['total'], 'rep', [(1, 0), (2, 3)])  80.4 us
    pallas_call x9, Pallas kernels, adam_part(): pl.pallas_call(functools.partial(adam_kernel, rate, two), grid_spec=pltpu...  68.9 us
    ppermute x10, waiting for transfers between devices, along(): return lax.ppermute(x, 'shard', [(i, i ^ step) for i in range(self.s_size)])  67.7 us
    unnamed x303, local copies, waits for them, and re-layouts  59.4 us
    pallas_call x14, Pallas kernels, mm(): pl.pallas_call(functools.partial(product_kernel, dims), grid=(m // tm, n...  56.1 us
    ppermute x8, starting transfers between devices, tick(): slot['in_got'] = lax.ppermute(out['new'], 'rep', [(0, 1), (3, 2)])  49 us
    ppermute x6, waiting for transfers between devices, tick(): got = lax.ppermute(out['total'], 'rep', [(0, 1), (1, 0), (2, 3), (3, 2)])  49 us
    dot_general x16, matrix products, dot(): return lax.dot_general(a, b, dims, preferred_element_type=f32)  31.7 us
  transfers between devices with their start and end apart: 86, of which 37 were waited for; matrix products, arithmetic and copies ran while one was open for 16% of the time, Pallas kernels for 18%

profile of v12, /device:TPU:0, one launch (start us, length us, event | category | flops | bytes accessed | tf_op | source)
XLA Modules:
  0.0 876.7 jit_solution(16427770378379861054)
XLA Ops:
  20.3 4.8 all-to-all-start
  74.4 9.5 %collective-permute-done.3.b_ref.d_ref = bf16[1536,512]{1,0:T(8,128)(2,1)} collective-permute-done((bf16[1536,512]{1,0:T(8,128)(2,1)}, bf16[1536,512]{1,0:T(8,128)(2,1)}, u32[]{:S(2)}, u32[]{:S(2)}) %collective-permute-start.3) | collective-permute-done | bytes 1572896 | tf_op jit(solution)/shard_map/ppermute | solution.py:62
  98.3 10.5 %collective-permute-done.4 = bf16[768,512]{1,0:T(8,128)(2,1)} collective-permute-done((bf16[768,512]{1,0:T(8,128)(2,1)}, bf16[768,512]{1,0:T(8,128)(2,1)}, u32[]{:S(2)}, u32[]{:S(2)}) %collective-permute-start.4) | collective-permute-done | bytes 786464 | tf_op jit(solution)/shard_map/ppermute | solution.py:61
  111.6 5.1 shard_map.316
  121.1 5.1 shard_map.317
  156.4 5.0 pad_maximum_fusion.1
  168.3 6.1 collective-permute-done.14
  201.1 5.0 convolution_convert_fusion.1.a_ref.c_ref
  222.3 5.6 shard_map.325.grad_ref
  235.9 19.8 %collective-permute-done.20 = f32[4,2,1,704]{3,0,2,1:T(4,128)S(1)} collective-permute-done((f32[4,2,1,704]{3,0,2,1:T(4,128)S(1)}, f32[4,2,1,704]{3,0,2,1:T(4,128)S(1)}, u32[]{:S(2)}, u32[]{:S(2)}) %collective-permute-start.20) | collective-permute-done | bytes 22560 | tf_op jit(solution)/shard_map/ppermute | solution.py:62
  258.9 8.3 collective-permute-done.21
  277.6 29.9 %collective-permute-done.24.ub_ref = bf16[704,1024]{1,0:T(8,128)(2,1)S(1)} collective-permute-done((bf16[704,1024]{1,0:T(8,128)(2,1)S(1)}, bf16[704,1024]{1,0:T(8,128)(2,1)S(1)}, u32[]{:S(2)}, u32[]{:S(2)}) %collective-permute-start.24) | collective-permute-done | bytes 1441824 | tf_op jit(solution)/shard_map/ppermute | solution.py:62
  309.6 7.5 shard_map.331
  318.4 5.8 shard_map.332
  331.2 5.3 shard_map.333
  341.6 15.8 %collective-permute-done.25 = bf16[352,2048]{1,0:T(8,128)(2,1)} collective-permute-done((bf16[352,2048]{1,0:T(8,128)(2,1)S(1)}, bf16[352,2048]{1,0:T(8,128)(2,1)}, u32[]{:S(2)}, u32[]{:S(2)}) %collective-permute-start.25) | collective-permute-done | bytes 1441824 | tf_op jit(solution)/shard_map/ppermute | solution.py:197
  362.2 7.3 collective-permute-start.29
  369.5 14.0 %all-gather.10.cloned.1.call-done.b_ref = bf16[2816,1024]{1,0:T(8,128)(2,1)} async-done(((bf16[704,1024]{1,0:T(8,128)(2,1)}), bf16[2816,1024]{1,0:T(8,128)(2,1)}) %all-gather.10.cloned.1.call-update) | async-done | bytes 5767184 | tf_op jit(solution)/shard_map/all_gather | solution.py:866
  383.5 5.8 shard_map.334
  389.3 5.9 shard_map.335.refs_0_
  404.3 6.2 collective-permute-start.31
  410.6 29.2 %collective-permute-done.32 = bf16[352,2048]{1,0:T(8,128)(2,1)S(1)} collective-permute-done((bf16[352,2048]{1,0:T(8,128)(2,1)S(1)}, bf16[352,2048]{1,0:T(8,128)(2,1)S(1)}, u32[]{:S(2)}, u32[]{:S(2)}) %collective-permute-start.32) | collective-permute-done | bytes 1441824 | tf_op jit(solution)/shard_map/ppermute | solution.py:200
  442.5 9.2 %all-gather.8.cloned.1.call-done.b_ref = bf16[2816,1024]{1,0:T(8,128)(2,1)} async-done(((bf16[704,1024]{1,0:T(8,128)(2,1)}), bf16[2816,1024]{1,0:T(8,128)(2,1)}) %all-gather.8.cloned.1.call-update) | async-done | bytes 5767184 | tf_op jit(solution)/shard_map/all_gather | solution.py:866
  451.7 6.6 shard_map.336
  467.4 6.2 collective-permute-start.35
  473.6 5.9 shard_map.337
  480.8 22.3 %collective-permute-done.36 = bf16[352,2048]{1,0:T(8,128)(2,1)S(1)} collective-permute-done((bf16[352,2048]{1,0:T(8,128)(2,1)S(1)}, bf16[352,2048]{1,0:T(8,128)(2,1)S(1)}, u32[]{:S(2)}, u32[]{:S(2)}) %collective-permute-start.36) | collective-permute-done | bytes 1441824 | tf_op jit(solution)/shard_map/ppermute | solution.py:200
  511.9 5.4 shard_map.339
  517.4 5.5 shard_map.340
  529.8 30.3 %collective-permute-done.38 = bf16[256,2816]{1,0:T(8,128)(2,1)S(1)} collective-permute-done((bf16[256,2816]{1,0:T(8,128)(2,1)S(1)}, bf16[256,2816]{1,0:T(8,128)(2,1)S(1)}, u32[]{:S(2)}, u32[]{:S(2)}) %collective-permute-start.38) | collective-permute-done | bytes 1441824 | tf_op jit(solution)/shard_map/ppermute | solution.py:192
  574.4 7.7 shard_map.343
  582.1 13.3 %collective-permute-done.40 = bf16[256,2816]{1,0:T(8,128)(2,1)S(1)} collective-permute-done((bf16[256,2816]{1,0:T(8,128)(2,1)}, bf16[256,2816]{1,0:T(8,128)(2,1)S(1)}, u32[]{:S(2)}, u32[]{:S(2)}) %collective-permute-start.40) | collective-permute-done | bytes 1441824 | tf_op jit(solution)/shard_map/ppermute | solution.py:192
  601.2 10.0 %collective-permute-start.42 = (bf16[256,1024]{1,0:T(8,128)(2,1)S(1)}, bf16[256,1024]{1,0:T(8,128)(2,1)S(1)}, u32[]{:S(2)}, u32[]{:S(2)}) collective-permute-start(bf16[256,1024]{1,0:T(8,128)(2,1)S(1)} %shard_map.341), channel_id=1, source_target_pairs={{0,8},{24,16},{1,9},{25,17},{2,10},{26,18},{3,11},{27,19},{4,12},{... | collective-permute-start | bytes 1572872 | tf_op jit(solution)/shard_map/ppermute | solution.py:197
  612.5 8.1 shard_map.344
  620.6 12.9 %collective-permute-done.43 = bf16[256,2816]{1,0:T(8,128)(2,1)} collective-permute-done((bf16[256,2816]{1,0:T(8,128)(2,1)S(1)}, bf16[256,2816]{1,0:T(8,128)(2,1)}, u32[]{:S(2)}, u32[]{:S(2)}) %collective-permute-start.43) | collective-permute-done | bytes 1441824 | tf_op jit(solution)/shard_map/ppermute | solution.py:200
  636.0 9.6 %collective-permute-start.47 = (bf16[256,1024]{1,0:T(8,128)(2,1)S(1)}, bf16[256,1024]{1,0:T(8,128)(2,1)}, u32[]{:S(2)}, u32[]{:S(2)}) collective-permute-start(bf16[256,1024]{1,0:T(8,128)(2,1)S(1)} %shard_map.342), channel_id=1, source_target_pairs={{0,8},{24,16},{1,9},{25,17},{2,10},{26,18},{3,11},{27,19},{4,12},{... | collective-permute-start | bytes 1572872 | tf_op jit(solution)/shard_map/ppermute | solution.py:197
  661.5 5.9 shard_map.348
  669.0 9.4 %collective-permute-done.48 = bf16[256,2816]{1,0:T(8,128)(2,1)} collective-permute-done((bf16[256,2816]{1,0:T(8,128)(2,1)}, bf16[256,2816]{1,0:T(8,128)(2,1)}, u32[]{:S(2)}, u32[]{:S(2)}) %collective-permute-start.48) | collective-permute-done | bytes 1441824 | tf_op jit(solution)/shard_map/ppermute | solution.py:200
  680.5 13.4 %shard_map.349 = (f32[256,11264]{1,0:T(8,128)}, f32[256,11264]{1,0:T(8,128)}, f32[256,11264]{1,0:T(8,128)}) custom-call(s32[1]{0:T(128)} %bitcast.8.core_ref, f32[256,11264]{1,0:T(8,128)} %w_ref.9, f32[256,11264]{1,0:T(8,128)} %m_ref.3, f32[256,11264]{1,0:T(8,128)} %v_ref.3, bf16[256,2816]{1,0:T(8,128)(2,1)S(1)} %broadcast_select_fusion.5.refs_0_, ...), custom_call_target="tpu_custom_call" | custom-call | flops 1024 | bytes 1024 | tf_op jit(solution)/shard_map/pallas_call | solution.py:464
  709.3 7.5 collective-permute-done.51
  733.9 13.7 %all-to-all-done.1 = f32[8,256,128]{2,1,0:T(8,128)} async-done(((f32[8,256,128]{2,1,0:T(8,128)}), f32[8,256,128]{2,1,0:T(8,128)}, u32[]{:S(2)}, u32[]{:S(2)}) %all-to-all-start.1) | async-done | bytes 1048608 | tf_op jit(solution)/shard_map/all_to_all | solution.py:974
  759.3 14.3 %shard_map.350 = (f32[256,11264]{1,0:T(8,128)}, f32[256,11264]{1,0:T(8,128)}, f32[256,11264]{1,0:T(8,128)}) custom-call(s32[1]{0:T(128)} %bitcast.8.core_ref, f32[256,11264]{1,0:T(8,128)} %w_ref.9, f32[256,11264]{1,0:T(8,128)} %m_ref.3, f32[256,11264]{1,0:T(8,128)} %v_ref.3, ...), custom_call_target="tpu_custom_call", output_to_operand_aliasing={{0}: (6, {}), {1}: (7, {}), {2}: (8, {})} | custom-call | flops 1024 | bytes 1024 | tf_op jit(solution)/shard_map/pallas_call | solution.py:464
  780.1 8.6 collective-permute-done.60
  800.6 5.0 collective-permute-start.63
  815.5 5.4 collective-permute-done.63
  826.8 6.2 shard_map.353
  841.1 6.2 shard_map.354
  861.9 6.3 shard_map.355
  (658 shorter events, 387.0 us)
Async XLA Ops:
  25.1 195.4 %all-gather.6.cloned.1.call-start = ((), (), s32[]{:S(2)}) async-start(), calls=%async_computation.5 | async-start | bytes 4718592 | tf_op jit(solution)/shard_map/all_gather | solution.py:644
  47.1 36.8 %collective-permute-start.3 = (bf16[1536,512]{1,0:T(8,128)(2,1)}, bf16[1536,512]{1,0:T(8,128)(2,1)}, u32[]{:S(2)}, u32[]{:S(2)}) collective-permute-start(bf16[1536,512]{1,0:T(8,128)(2,1)} %convolution_convert_fusion.7), channel_id=1, source_target_pairs={{0,1},{1,0},{2,3},{3,2},{4,5},{5,4},{6,7},{7,6},{8,9},{9,8},{10,11... | collective-permute-start | bytes 4718600 | tf_op jit(solution)/shard_map/ppermute | solution.py:62
  50.2 40.1 %collective-permute-start.5 = (bf16[1536,512]{1,0:T(8,128)(2,1)}, bf16[1536,512]{1,0:T(8,128)(2,1)}, u32[]{:S(2)}, u32[]{:S(2)}) collective-permute-start(bf16[1536,512]{1,0:T(8,128)(2,1)} %convolution_convert_fusion.6), channel_id=1, source_target_pairs={{0,4},{2,6},{4,0},{6,2},{1,5},{3,7},{5,1},{7,3},{8,12},{10,14},{12... | collective-permute-start | bytes 4718600 | tf_op jit(solution)/shard_map/ppermute | solution.py:61
  96.1 22.1 %collective-permute-start.7 = (bf16[768,512]{1,0:T(8,128)(2,1)}, bf16[768,512]{1,0:T(8,128)(2,1)}, u32[]{:S(2)}, u32[]{:S(2)}) collective-permute-start(bf16[768,512]{1,0:T(8,128)(2,1)} %get-tuple-element.474), channel_id=1, source_target_pairs={{0,1},{1,0},{2,3},{3,2},{4,5},{5,4},{6,7},{7,6},{8,9},{9,8},{10,11... | collective-permute-start | bytes 2359304 | tf_op jit(solution)/shard_map/ppermute | solution.py:62
  128.2 255.3 %all-gather.10.cloned.1.call-start = ((), (), s32[]{:S(2)}) async-start(), calls=%async_computation.7 | async-start | bytes 7208960 | tf_op jit(solution)/shard_map/all_gather | solution.py:866
  133.3 28.1 %collective-permute-start.9 = (bf16[512,512]{1,0:T(8,128)(2,1)}, bf16[512,512]{1,0:T(8,128)(2,1)}, u32[]{:S(2)}, u32[]{:S(2)}) collective-permute-start(bf16[512,512]{1,0:T(8,128)(2,1)} %convolution_convert_fusion.11), channel_id=1, source_target_pairs={{0,1},{1,0},{2,3},{3,2},{4,5},{5,4},{6,7},{7,6},{8,9},{9,8},{10,11... | collective-permute-start | bytes 1572872 | tf_op jit(solution)/shard_map/ppermute | solution.py:62
  135.4 28.0 %collective-permute-start.13 = (bf16[512,512]{1,0:T(8,128)(2,1)}, bf16[512,512]{1,0:T(8,128)(2,1)}, u32[]{:S(2)}, u32[]{:S(2)}) collective-permute-start(bf16[512,512]{1,0:T(8,128)(2,1)} %convolution_convert_fusion.10), channel_id=1, source_target_pairs={{0,4},{2,6},{4,0},{6,2},{1,5},{3,7},{5,1},{7,3},{8,12},{10,14},{12... | collective-permute-start | bytes 1572872 | tf_op jit(solution)/shard_map/ppermute | solution.py:61
  190.4 77.6 %collective-permute-start.19 = (bf16[1408,1024]{1,0:T(8,128)(2,1)}, bf16[1408,1024]{1,0:T(8,128)(2,1)}, u32[]{:S(2)}, u32[]{:S(2)}) collective-permute-start(bf16[1408,1024]{1,0:T(8,128)(2,1)} %convolution_convert_fusion.3), channel_id=1, source_target_pairs={{0,1},{1,0},{2,3},{3,2},{4,5},{5,4},{6,7},{7,6},{8,9},{9,8},{10,11... | collective-permute-start | bytes 8650760 | tf_op jit(solution)/shard_map/ppermute | solution.py:62
  194.9 76.1 %collective-permute-start.23 = (bf16[1408,1024]{1,0:T(8,128)(2,1)}, bf16[1408,1024]{1,0:T(8,128)(2,1)}, u32[]{:S(2)}, u32[]{:S(2)}) collective-permute-start(bf16[1408,1024]{1,0:T(8,128)(2,1)} %convolution_convert_fusion.2), channel_id=1, source_target_pairs={{0,4},{2,6},{4,0},{6,2},{1,5},{3,7},{5,1},{7,3},{8,12},{10,14},{12... | collective-permute-start | bytes 8650760 | tf_op jit(solution)/shard_map/ppermute | solution.py:61
  199.6 56.1 %collective-permute-start.20 = (f32[4,2,1,704]{3,0,2,1:T(4,128)S(1)}, f32[4,2,1,704]{3,0,2,1:T(4,128)S(1)}, u32[]{:S(2)}, u32[]{:S(2)}) collective-permute-start(f32[4,2,1,704]{3,0,2,1:T(4,128)S(1)} %copy.125), channel_id=1, source_target_pairs={{0,1},{1,0},{2,3},{3,2},{4,5},{5,4},{6,7},{7,6},{8,9},{9,8},{10,11... | collective-permute-start | bytes 67592 | tf_op jit(solution)/shard_map/ppermute | solution.py:62
  275.5 32.0 %collective-permute-start.24 = (bf16[704,1024]{1,0:T(8,128)(2,1)S(1)}, bf16[704,1024]{1,0:T(8,128)(2,1)S(1)}, u32[]{:S(2)}, u32[]{:S(2)}) collective-permute-start(bf16[704,1024]{1,0:T(8,128)(2,1)S(1)} %get-tuple-element.570), channel_id=1, source_target_pairs={{0,1},{1,0},{2,3},{3,2},{4,5},{5,4},{6,7},{7,6},{8,9},{9,8},{10,11... | collective-permute-start | bytes 4325384 | tf_op jit(solution)/shard_map/ppermute | solution.py:62
  276.7 31.7 %collective-permute-start.22 = (bf16[704,1024]{1,0:T(8,128)(2,1)S(1)}, bf16[704,1024]{1,0:T(8,128)(2,1)S(1)}, u32[]{:S(2)}, u32[]{:S(2)}) collective-permute-start(bf16[704,1024]{1,0:T(8,128)(2,1)S(1)} %get-tuple-element.566), channel_id=1, source_target_pairs={{0,4},{2,6},{4,0},{6,2},{1,5},{3,7},{5,1},{7,3},{8,12},{10,14},{12... | collective-permute-start | bytes 4325384 | tf_op jit(solution)/shard_map/ppermute | solution.py:61
  317.1 134.6 %all-gather.8.cloned.1.call-start = ((), (), s32[]{:S(2)}) async-start(), calls=%async_computation.6 | async-start | bytes 7208960 | tf_op jit(solution)/shard_map/all_gather | solution.py:866
  317.8 188.3 %all-gather.12.cloned.1.call-start = ((), (), s32[]{:S(2)}) async-start(), calls=%async_computation.8 | async-start | bytes 4718592 | tf_op jit(solution)/shard_map/all_gather | solution.py:904
  325.6 31.7 %collective-permute-start.25 = (bf16[352,2048]{1,0:T(8,128)(2,1)S(1)}, bf16[352,2048]{1,0:T(8,128)(2,1)}, u32[]{:S(2)}, u32[]{:S(2)}) collective-permute-start(bf16[352,2048]{1,0:T(8,128)(2,1)S(1)} %get-tuple-element.592), channel_id=1, source_target_pairs={{0,8},{24,16},{1,9},{25,17},{2,10},{26,18},{3,11},{27,19},{4,12},{... | collective-permute-start | bytes 4325384 | tf_op jit(solution)/shard_map/ppermute | solution.py:197
  360.4 36.1 %collective-permute-start.30 = (bf16[352,2048]{1,0:T(8,128)(2,1)}, bf16[352,2048]{1,0:T(8,128)(2,1)}, u32[]{:S(2)}, u32[]{:S(2)}) collective-permute-start(bf16[352,2048]{1,0:T(8,128)(2,1)} %reduce-precision_convert_fusion.11), channel_id=1, source_target_pairs={{8,16},{16,8},{9,17},{17,9},{10,18},{18,10},{11,19},{19,11},{12,20... | collective-permute-start | bytes 4325384 | tf_op jit(solution)/shard_map/ppermute | solution.py:203
  362.2 34.4 %collective-permute-start.29 = (bf16[352,2048]{1,0:T(8,128)(2,1)}, bf16[352,2048]{1,0:T(8,128)(2,1)}, u32[]{:S(2)}, u32[]{:S(2)}) collective-permute-start(bf16[352,2048]{1,0:T(8,128)(2,1)} %get-tuple-element.602), channel_id=1, source_target_pairs={{0,8},{24,16},{1,9},{25,17},{2,10},{26,18},{3,11},{27,19},{4,12},{... | collective-permute-start | bytes 4325384 | tf_op jit(solution)/shard_map/ppermute | solution.py:197
  403.1 36.8 %collective-permute-start.32 = (bf16[352,2048]{1,0:T(8,128)(2,1)S(1)}, bf16[352,2048]{1,0:T(8,128)(2,1)S(1)}, u32[]{:S(2)}, u32[]{:S(2)}) collective-permute-start(bf16[352,2048]{1,0:T(8,128)(2,1)S(1)} %reduce-precision_convert_fusion.10), channel_id=1, source_target_pairs={{8,0},{16,24},{9,1},{17,25},{10,2},{18,26},{11,3},{19,27},{12,4},{... | collective-permute-start | bytes 4325384 | tf_op jit(solution)/shard_map/ppermute | solution.py:200
  404.3 36.7 %collective-permute-start.31 = (bf16[256,2816]{1,0:T(8,128)(2,1)S(1)}, bf16[256,2816]{1,0:T(8,128)(2,1)S(1)}, u32[]{:S(2)}, u32[]{:S(2)}) collective-permute-start(bf16[256,2816]{1,0:T(8,128)(2,1)S(1)} %get-tuple-element.604), channel_id=1, source_target_pairs={{0,8},{24,16},{1,9},{25,17},{2,10},{26,18},{3,11},{27,19},{4,12},{... | collective-permute-start | bytes 4325384 | tf_op jit(solution)/shard_map/ppermute | solution.py:197
  463.3 185.1 %all-gather.14.cloned.1.call-start = ((), (), s32[]{:S(2)}) async-start(), calls=%async_computation.9 | async-start | bytes 7864320 | tf_op jit(solution)/shard_map/all_gather | solution.py:866
  463.3 39.8 %collective-permute-start.37 = (bf16[256,2816]{1,0:T(8,128)(2,1)}, bf16[256,2816]{1,0:T(8,128)(2,1)S(1)}, u32[]{:S(2)}, u32[]{:S(2)}) collective-permute-start(bf16[256,2816]{1,0:T(8,128)(2,1)} %reduce-precision_convert_fusion.8), channel_id=1, source_target_pairs={{8,16},{16,8},{9,17},{17,9},{10,18},{18,10},{11,19},{19,11},{12,20... | collective-permute-start | bytes 4325384 | tf_op jit(solution)/shard_map/ppermute | solution.py:203
  466.1 37.0 %collective-permute-start.36 = (bf16[352,2048]{1,0:T(8,128)(2,1)S(1)}, bf16[352,2048]{1,0:T(8,128)(2,1)S(1)}, u32[]{:S(2)}, u32[]{:S(2)}) collective-permute-start(bf16[352,2048]{1,0:T(8,128)(2,1)S(1)} %reduce-precision_convert_fusion.7), channel_id=1, source_target_pairs={{8,0},{16,24},{9,1},{17,25},{10,2},{18,26},{11,3},{19,27},{12,4},{... | collective-permute-start | bytes 4325384 | tf_op jit(solution)/shard_map/ppermute | solution.py:200
  467.4 37.0 %collective-permute-start.35 = (bf16[256,2816]{1,0:T(8,128)(2,1)S(1)}, bf16[256,2816]{1,0:T(8,128)(2,1)S(1)}, u32[]{:S(2)}, u32[]{:S(2)}) collective-permute-start(bf16[256,2816]{1,0:T(8,128)(2,1)S(1)} %copy-done.112), channel_id=1, source_target_pairs={{0,8},{24,16},{1,9},{25,17},{2,10},{26,18},{3,11},{27,19},{4,12},{... | collective-permute-start | bytes 4325384 | tf_op jit(solution)/shard_map/ppermute | solution.py:197
  524.2 328.6 %reduce-scatter.2.cloned.1.call-start = ((), (), s32[]{:S(2)}) async-start(), calls=%async_computation.10 | async-start | bytes 4718592 | tf_op jit(solution)/shard_map/reduce_scatter | solution.py:934
  527.2 32.9 %collective-permute-start.38 = (bf16[256,2816]{1,0:T(8,128)(2,1)S(1)}, bf16[256,2816]{1,0:T(8,128)(2,1)S(1)}, u32[]{:S(2)}, u32[]{:S(2)}) collective-permute-start(bf16[256,2816]{1,0:T(8,128)(2,1)S(1)} %fusion), channel_id=1, source_target_pairs={{0,8},{8,0},{16,24},{24,16},{1,9},{9,1},{17,25},{25,17},{2,10},{10... | collective-permute-start | bytes 4325384 | tf_op jit(solution)/shard_map/ppermute | solution.py:192
  529.0 31.0 %collective-permute-start.39 = (bf16[256,2816]{1,0:T(8,128)(2,1)S(1)}, bf16[256,2816]{1,0:T(8,128)(2,1)S(1)}, u32[]{:S(2)}, u32[]{:S(2)}) collective-permute-start(bf16[256,2816]{1,0:T(8,128)(2,1)S(1)} %copy-done.115), channel_id=1, source_target_pairs={{8,16},{16,8},{9,17},{17,9},{10,18},{18,10},{11,19},{19,11},{12,20... | collective-permute-start | bytes 4325384 | tf_op jit(solution)/shard_map/ppermute | solution.py:203
  561.7 33.7 %collective-permute-start.40 = (bf16[256,2816]{1,0:T(8,128)(2,1)}, bf16[256,2816]{1,0:T(8,128)(2,1)S(1)}, u32[]{:S(2)}, u32[]{:S(2)}) collective-permute-start(bf16[256,2816]{1,0:T(8,128)(2,1)} %fusion.1), channel_id=1, source_target_pairs={{0,8},{8,0},{16,24},{24,16},{1,9},{9,1},{17,25},{25,17},{2,10},{10... | collective-permute-start | bytes 4325384 | tf_op jit(solution)/shard_map/ppermute | solution.py:192
  566.9 28.6 %collective-permute-start.41 = (bf16[256,2816]{1,0:T(8,128)(2,1)}, bf16[256,2816]{1,0:T(8,128)(2,1)}, u32[]{:S(2)}, u32[]{:S(2)}) collective-permute-start(bf16[256,2816]{1,0:T(8,128)(2,1)} %reduce-precision_convert_fusion.4), channel_id=1, source_target_pairs={{8,16},{16,8},{9,17},{17,9},{10,18},{18,10},{11,19},{19,11},{12,20... | collective-permute-start | bytes 4325384 | tf_op jit(solution)/shard_map/ppermute | solution.py:203
  598.1 35.3 %collective-permute-start.43 = (bf16[256,2816]{1,0:T(8,128)(2,1)S(1)}, bf16[256,2816]{1,0:T(8,128)(2,1)}, u32[]{:S(2)}, u32[]{:S(2)}) collective-permute-start(bf16[256,2816]{1,0:T(8,128)(2,1)S(1)} %reduce-precision_convert_fusion.2), channel_id=1, source_target_pairs={{8,0},{16,24},{9,1},{17,25},{10,2},{18,26},{11,3},{19,27},{12,4},{... | collective-permute-start | bytes 4325384 | tf_op jit(solution)/shard_map/ppermute | solution.py:200
  600.1 33.4 %collective-permute-start.44 = (bf16[256,2816]{1,0:T(8,128)(2,1)S(1)}, bf16[256,2816]{1,0:T(8,128)(2,1)S(1)}, u32[]{:S(2)}, u32[]{:S(2)}) collective-permute-start(bf16[256,2816]{1,0:T(8,128)(2,1)S(1)} %reduce-precision_convert_fusion.1), channel_id=1, source_target_pairs={{8,16},{16,8},{9,17},{17,9},{10,18},{18,10},{11,19},{19,11},{12,20... | collective-permute-start | bytes 4325384 | tf_op jit(solution)/shard_map/ppermute | solution.py:203
  612.5 68.0 %collective-permute-start.46 = (bf16[256,2816]{1,0:T(8,128)(2,1)}, bf16[256,2816]{1,0:T(8,128)(2,1)}, u32[]{:S(2)}, u32[]{:S(2)}) collective-permute-start(bf16[256,2816]{1,0:T(8,128)(2,1)} %broadcast_select_fusion.4), channel_id=1, source_target_pairs={{0,2},{2,0},{4,6},{6,4},{1,3},{3,1},{5,7},{7,5},{8,10},{10,8},{12,... | collective-permute-start | bytes 4325384 | tf_op jit(solution)/shard_map/ppermute | solution.py:57
  634.5 34.5 %collective-permute-start.49 = (bf16[256,1024]{1,0:T(8,128)(2,1)}, bf16[256,1024]{1,0:T(8,128)(2,1)}, u32[]{:S(2)}, u32[]{:S(2)}) collective-permute-start(bf16[256,1024]{1,0:T(8,128)(2,1)} %reduce-precision_convert_fusion.27), channel_id=1, source_target_pairs={{8,16},{16,8},{9,17},{17,9},{10,18},{18,10},{11,19},{19,11},{12,20... | collective-permute-start | bytes 1572872 | tf_op jit(solution)/shard_map/ppermute | solution.py:203
  636.0 33.0 %collective-permute-start.47 = (bf16[256,1024]{1,0:T(8,128)(2,1)S(1)}, bf16[256,1024]{1,0:T(8,128)(2,1)}, u32[]{:S(2)}, u32[]{:S(2)}) collective-permute-start(bf16[256,1024]{1,0:T(8,128)(2,1)S(1)} %shard_map.342), channel_id=1, source_target_pairs={{0,8},{24,16},{1,9},{25,17},{2,10},{26,18},{3,11},{27,19},{4,12},{... | collective-permute-start | bytes 1572872 | tf_op jit(solution)/shard_map/ppermute | solution.py:197
  647.1 31.4 %collective-permute-start.48 = (bf16[256,2816]{1,0:T(8,128)(2,1)}, bf16[256,2816]{1,0:T(8,128)(2,1)}, u32[]{:S(2)}, u32[]{:S(2)}) collective-permute-start(bf16[256,2816]{1,0:T(8,128)(2,1)} %reduce-precision_convert_fusion), channel_id=1, source_target_pairs={{8,0},{16,24},{9,1},{17,25},{10,2},{18,26},{11,3},{19,27},{12,4},{... | collective-permute-start | bytes 4325384 | tf_op jit(solution)/shard_map/ppermute | solution.py:200
  667.7 26.2 %collective-permute-start.45 = (f32[256,1024]{1,0:T(8,128)S(1)}, f32[256,1024]{1,0:T(8,128)S(1)}, u32[]{:S(2)}, u32[]{:S(2)}) collective-permute-start(f32[256,1024]{1,0:T(8,128)S(1)} %get-tuple-element.869), channel_id=1, source_target_pairs={{0,2},{2,0},{4,6},{6,4},{1,3},{3,1},{5,7},{7,5},{8,10},{10,8},{12,... | collective-permute-start | bytes 3145736 | tf_op jit(solution)/shard_map/ppermute | solution.py:57
  701.0 54.9 %collective-permute-start.57 = (bf16[256,2816]{1,0:T(8,128)(2,1)}, bf16[256,2816]{1,0:T(8,128)(2,1)}, u32[]{:S(2)}, u32[]{:S(2)}) collective-permute-start(bf16[256,2816]{1,0:T(8,128)(2,1)} %broadcast_select_fusion.2), channel_id=1, source_target_pairs={{0,2},{2,0},{4,6},{6,4},{1,3},{3,1},{5,7},{7,5},{8,10},{10,8},{12,... | collective-permute-start | bytes 4325384 | tf_op jit(solution)/shard_map/ppermute | solution.py:57
  701.0 52.6 %collective-permute-start.59 = (bf16[256,1024]{1,0:T(8,128)(2,1)}, bf16[256,1024]{1,0:T(8,128)(2,1)}, u32[]{:S(2)}, u32[]{:S(2)}) collective-permute-start(bf16[256,1024]{1,0:T(8,128)(2,1)} %reduce-precision_convert_fusion.26), channel_id=1, source_target_pairs={{8,16},{16,8},{9,17},{17,9},{10,18},{18,10},{11,19},{19,11},{12,20... | collective-permute-start | bytes 1572872 | tf_op jit(solution)/shard_map/ppermute | solution.py:203
  709.2 41.0 %collective-permute-start.58 = (bf16[256,1024]{1,0:T(8,128)(2,1)}, bf16[256,1024]{1,0:T(8,128)(2,1)}, u32[]{:S(2)}, u32[]{:S(2)}) collective-permute-start(bf16[256,1024]{1,0:T(8,128)(2,1)} %fusion.4), channel_id=1, source_target_pairs={{0,8},{8,0},{16,24},{24,16},{1,9},{9,1},{17,25},{25,17},{2,10},{10... | collective-permute-start | bytes 1572872 | tf_op jit(solution)/shard_map/ppermute | solution.py:192
  722.0 25.6 %all-to-all-start.1 = ((f32[8,256,128]{2,1,0:T(8,128)}), f32[8,256,128]{2,1,0:T(8,128)}, u32[]{:S(2)}, u32[]{:S(2)}) async-start(f32[8,256,128]{2,1,0:T(8,128)} %bitcast.77), calls=%async_computation.2 | async-start | bytes 2097152 | tf_op jit(solution)/shard_map/all_to_all | solution.py:974
  730.0 44.7 %collective-permute-start.50 = (f32[7,256]{1,0:T(8,128)S(1)}, f32[7,256]{1,0:T(8,128)S(1)}, u32[]{:S(2)}, u32[]{:S(2)}) collective-permute-start(f32[7,256]{1,0:T(8,128)S(1)} %concatenate.78), channel_id=1, source_target_pairs={{0,8},{8,0},{16,24},{24,16},{1,9},{9,1},{17,25},{25,17},{2,10},{10... | collective-permute-start | bytes 21512 | tf_op jit(solution)/shard_map/ppermute | solution.py:984
  732.5 41.2 %collective-permute-start.56 = (bf16[256,1024]{1,0:T(8,128)(2,1)}, bf16[256,1024]{1,0:T(8,128)(2,1)}, u32[]{:S(2)}, u32[]{:S(2)}) collective-permute-start(bf16[256,1024]{1,0:T(8,128)(2,1)} %reduce-precision_convert_fusion.25), channel_id=1, source_target_pairs={{8,16},{16,8},{9,17},{17,9},{10,18},{18,10},{11,19},{19,11},{12,20... | collective-permute-start | bytes 1572872 | tf_op jit(solution)/shard_map/ppermute | solution.py:203
  750.2 23.4 %collective-permute-start.55 = (bf16[256,1024]{1,0:T(8,128)(2,1)S(1)}, bf16[256,1024]{1,0:T(8,128)(2,1)S(1)}, u32[]{:S(2)}, u32[]{:S(2)}) collective-permute-start(bf16[256,1024]{1,0:T(8,128)(2,1)S(1)} %copy-done.130), channel_id=1, source_target_pairs={{0,8},{24,16},{1,9},{25,17},{2,10},{26,18},{3,11},{27,19},{4,12},{... | collective-permute-start | bytes 1572872 | tf_op jit(solution)/shard_map/ppermute | solution.py:197
  754.9 37.3 %collective-permute-start.62 = (bf16[256,1024]{1,0:T(8,128)(2,1)S(1)}, bf16[256,1024]{1,0:T(8,128)(2,1)S(1)}, u32[]{:S(2)}, u32[]{:S(2)}) collective-permute-start(bf16[256,1024]{1,0:T(8,128)(2,1)S(1)} %reduce-precision_convert_fusion.23), channel_id=1, source_target_pairs={{8,16},{16,8},{9,17},{17,9},{10,18},{18,10},{11,19},{19,11},{12,20... | collective-permute-start | bytes 1572872 | tf_op jit(solution)/shard_map/ppermute | solution.py:203
  757.2 35.0 %collective-permute-start.61 = (bf16[256,1024]{1,0:T(8,128)(2,1)S(1)}, bf16[256,1024]{1,0:T(8,128)(2,1)S(1)}, u32[]{:S(2)}, u32[]{:S(2)}) collective-permute-start(bf16[256,1024]{1,0:T(8,128)(2,1)S(1)} %fusion.5), channel_id=1, source_target_pairs={{0,8},{8,0},{16,24},{24,16},{1,9},{9,1},{17,25},{25,17},{2,10},{10... | collective-permute-start | bytes 1572872 | tf_op jit(solution)/shard_map/ppermute | solution.py:192
  793.2 27.7 %collective-permute-start.64 = (bf16[256,1024]{1,0:T(8,128)(2,1)}, bf16[256,1024]{1,0:T(8,128)(2,1)}, u32[]{:S(2)}, u32[]{:S(2)}) collective-permute-start(bf16[256,1024]{1,0:T(8,128)(2,1)} %reduce-precision_convert_fusion.20), channel_id=1, source_target_pairs={{8,16},{16,8},{9,17},{17,9},{10,18},{18,10},{11,19},{19,11},{12,20... | collective-permute-start | bytes 1572872 | tf_op jit(solution)/shard_map/ppermute | solution.py:203
  795.8 38.0 %collective-permute-start.69 = (bf16[256,1024]{1,0:T(8,128)(2,1)}, bf16[256,1024]{1,0:T(8,128)(2,1)}, u32[]{:S(2)}, u32[]{:S(2)}) collective-permute-start(bf16[256,1024]{1,0:T(8,128)(2,1)} %reduce-precision_convert_fusion.14), channel_id=1, source_target_pairs={{8,0},{16,24},{9,1},{17,25},{10,2},{18,26},{11,3},{19,27},{12,4},{... | collective-permute-start | bytes 1572872 | tf_op jit(solution)/shard_map/ppermute | solution.py:200
  798.1 35.7 %collective-permute-start.70 = (bf16[256,1024]{1,0:T(8,128)(2,1)}, bf16[256,1024]{1,0:T(8,128)(2,1)}, u32[]{:S(2)}, u32[]{:S(2)}) collective-permute-start(bf16[256,1024]{1,0:T(8,128)(2,1)} %reduce-precision_convert_fusion.17), channel_id=1, source_target_pairs={{8,16},{16,8},{9,17},{17,9},{10,18},{18,10},{11,19},{19,11},{12,20... | collective-permute-start | bytes 1572872 | tf_op jit(solution)/shard_map/ppermute | solution.py:203
  807.2 25.8 %all-to-all-start.3 = ((f32[8,7,256]{2,1,0:T(8,128)}), f32[8,7,256]{2,1,0:T(8,128)S(1)}, u32[]{:S(2)}, u32[]{:S(2)}) async-start(f32[8,7,256]{2,1,0:T(8,128)} %broadcast_in_dim.51), calls=%async_computation.4 | async-start | bytes 131072 | tf_op jit(solution)/shard_map/all_to_all | solution.py:990
  (188 other events, 1177.6 us)
Sparse Core Ops, SparseCore 0:
  128.3 42.7 all-gather.5
  317.2 66.1 all-gather.9
  385.9 65.7 all-gather.7
  463.4 36.7 all-gather.11
  524.4 69.3 all-gather.13
  701.2 61.2 reduce-scatter.1

commit v13 on v8

--- a/solution.py
+++ b/solution.py
@@ -219,9 +219,32 @@
         in_specs=[spec],
         out_specs=spec,
         out_shape=jax.ShapeDtypeStruct(w.shape, bf16),
-        compiler_params=pltpu.CompilerParams(vmem_limit_bytes=48 * 1024 * 1024),
+        compiler_params=pltpu.CompilerParams(vmem_limit_bytes=60 * 1024 * 1024),
         cost_estimate=SMALL,
     )(w)
+
+
+def own_columns_kernel(block_ref, x_ref, out_ref):
+    out_ref[...] = x_ref[...].T
+
+
+def own_columns(x, block, width):
+    rows = x.shape[0]
+    if width % 128:
+        return lax.dynamic_slice_in_dim(x, block[0] * width, width, 1).T
+    tile = min(rows, 512)
+    return pl.pallas_call(
+        own_columns_kernel,
+        grid_spec=pltpu.PrefetchScalarGridSpec(
+            num_scalar_prefetch=1,
+            grid=(rows // tile,),
+            in_specs=[pl.BlockSpec((tile, width), lambda i, block: (i, block[0]))],
+            out_specs=pl.BlockSpec((width, tile), lambda i, block: (0, i)),
+        ),
+        out_shape=jax.ShapeDtypeStruct((width, rows), bf16),
+        compiler_params=pltpu.CompilerParams(vmem_limit_bytes=60 * 1024 * 1024),
+        cost_estimate=SMALL,
+    )(block, x)
 
 
 def split_kernel(core_ref, w_ref, mine_ref, theirs_ref):
@@ -245,7 +268,7 @@
             out_specs=[half, half],
         ),
         out_shape=[out, out],
-        compiler_params=pltpu.CompilerParams(vmem_limit_bytes=32 * 1024 * 1024),
+        compiler_params=pltpu.CompilerParams(vmem_limit_bytes=60 * 1024 * 1024),
         cost_estimate=SMALL,
     )(core, w)
 
@@ -288,7 +311,7 @@
             out_specs=[out_spec, out_spec],
         ),
         out_shape=[out, out],
-        compiler_params=pltpu.CompilerParams(vmem_limit_bytes=32 * 1024 * 1024),
+        compiler_params=pltpu.CompilerParams(vmem_limit_bytes=60 * 1024 * 1024),
         cost_estimate=SMALL,
     )(place, mine, got, mine, got)
 
@@ -319,7 +342,7 @@
         + ([] if add is None else [out]),
         out_specs=out,
         out_shape=jax.ShapeDtypeStruct((m, n), dtype),
-        compiler_params=pltpu.CompilerParams(vmem_limit_bytes=48 * 1024 * 1024),
+        compiler_params=pltpu.CompilerParams(vmem_limit_bytes=60 * 1024 * 1024),
         cost_estimate=SMALL,
     )(*((a, b) if add is None else (a, b, add)))
 
@@ -347,7 +370,7 @@
             out_specs=pl.BlockSpec((1, 1, 1, rows, 2 * half), lambda p, y, s, bits: (p, y, s, 0, 0)),
         ),
         out_shape=jax.ShapeDtypeStruct((pre, y_size, s_size, rows, 2 * half), bf16),
-        compiler_params=pltpu.CompilerParams(vmem_limit_bytes=48 * 1024 * 1024),
+        compiler_params=pltpu.CompilerParams(vmem_limit_bytes=60 * 1024 * 1024),
         cost_estimate=SMALL,
     )(bits, parts[0], got[0], parts[1], got[1])
 
@@ -368,7 +391,7 @@
         in_specs=[spec, spec],
         out_specs=pl.BlockSpec((2 * width, rows // n), lambda i: (0, i)),
         out_shape=jax.ShapeDtypeStruct((2 * width, rows), bf16),
-        compiler_params=pltpu.CompilerParams(vmem_limit_bytes=48 * 1024 * 1024),
+        compiler_params=pltpu.CompilerParams(vmem_limit_bytes=60 * 1024 * 1024),
         cost_estimate=SMALL,
     )(a, b)
 
@@ -396,7 +419,7 @@
             out_specs=[out_spec, out_spec],
         ),
         out_shape=[out, out],
-        compiler_params=pltpu.CompilerParams(vmem_limit_bytes=48 * 1024 * 1024),
+        compiler_params=pltpu.CompilerParams(vmem_limit_bytes=60 * 1024 * 1024),
         cost_estimate=SMALL,
     )(bit, kept, got, kept, got)
 
@@ -435,7 +458,7 @@
         ),
         out_shape=[out] * 3,
         input_output_aliases=aliases,
-        compiler_params=pltpu.CompilerParams(vmem_limit_bytes=48 * 1024 * 1024),
+        compiler_params=pltpu.CompilerParams(vmem_limit_bytes=60 * 1024 * 1024),
         cost_estimate=SMALL,
     )(core, w, m, v, *grads, *extra)
 
@@ -484,7 +507,7 @@
             jax.ShapeDtypeStruct((heads, hd, t), bf16),
             jax.ShapeDtypeStruct((seqs, heads, 2, seq), f32),
         ],
-        compiler_params=pltpu.CompilerParams(vmem_limit_bytes=32 * 1024 * 1024),
+        compiler_params=pltpu.CompilerParams(vmem_limit_bytes=60 * 1024 * 1024),
         cost_estimate=SMALL,
     )(kept, got, bias, table)
 
@@ -527,7 +550,7 @@
         ],
         out_specs=big,
         out_shape=jax.ShapeDtypeStruct((3, heads, hd, t), bf16),
-        compiler_params=pltpu.CompilerParams(vmem_limit_bytes=32 * 1024 * 1024),
+        compiler_params=pltpu.CompilerParams(vmem_limit_bytes=60 * 1024 * 1024),
         cost_estimate=SMALL,
     )(qkv, dout, stats, table)
 
@@ -605,7 +628,7 @@
         return jnp.concatenate([blocks, jnp.broadcast_to(extra[None], (nb, 16, rows))], axis=1)
 
     packed = do(pack, x_rows, order)
-    cot_all = lax.all_gather(cotangent.reshape(rows, width), ("shard", "ctx"), axis=0, tiled=True)
+    cot_all = lax.all_gather(do(cast, cotangent.reshape(rows, width)), ("shard", "ctx"), axis=0, tiled=True)
     got = lax.all_to_all(packed, plane, split_axis=0, concat_axis=0, tiled=True)
 
     def chip_rows(w, lead, unit, count):
@@ -785,7 +808,7 @@
     wg = do(stack_turned, *wg_parts)
     wu = do(stack_turned, *wu_parts)
     grad_act = do(lambda w, c: mm(w, c, LAST, f32, tn=256), wd_own, cot_all)
-    cot_cols = do(lambda c: lax.dynamic_slice_in_dim(c, my_block * blk, blk, 1).T, cot_all)
+    cot_cols = do(lambda c: own_columns(c, my_block.reshape(1), blk), cot_all)
     wo_own = do(cast, w_out)
     wq = do(stack_turned, *wq_parts)
     gains = do(lambda a, b: a + b, *gains)
@@ -845,20 +868,23 @@
     for k in range(2):
         jobs.append(("out", [("out", k)], 0, k, blk, width // 2))
     for third in (2, 1, 0):
-        for k, (at_row, count) in enumerate(up_rows):
-            jobs.append(
-                ("qkv", [(third, "mine", k), (third, "theirs", k)], at_row, third * Y, count, S * blk)
-            )
+        jobs.append(("qkv", [(third, 0), (third, 1, "theirs")], 0, third * Y, blk, S * blk))
     received = {}
 
     def update(limit):
         for name in list(reps.done):
-            if name[1] == "theirs" and name not in received:
+            if name in ("out", 0, 1, 2):
+                g = reps.done.pop(name)
+                half = g.shape[0] // 2
+                reps.done[(name, 0)] = g[:half]
+                reps.done[(name, 1) if name == "out" else (name, 1, "theirs")] = g[half:]
+        for name in list(reps.done):
+            if "theirs" in name and name not in received:
                 received[name] = at.core(reps.done[name])
         while jobs and limit and all(k in reps.done for k in jobs[0][1]):
             name, needs, at_row, lead, count, unit = jobs.pop(0)
             rb = max(n for n in range(8, min(count, 176) + 1, 8) if count % n == 0 and at_row % n == 0)
-            adam(name, [received[k] if k[1] == "theirs" else reps.done[k] for k in needs], at_row, lead, unit, rb)
+            adam(name, [received[k] if "theirs" in k else reps.done[k] for k in needs], at_row, lead, unit, rb)
             limit -= 1
 
     def ticks(n):
@@ -955,9 +981,12 @@
     n, start, finish, gqkv_done = gather_steps([g.reshape(1, 1, 3 * blk, H) for g in gqkvs], 3)
     start(0)
     attn = lanes(*attns)
-    for k in range(2):
-        g_out = do(lambda a, g: mm(a, g, LAST, bf16, tn=512), attn, gbr[k * width // 2 : (k + 1) * width // 2])
-        reps.push(("out", k), g_out)
+    g_out = do(
+        lambda a, g: join(*[mm(a, g[k * width // 2 : (k + 1) * width // 2], LAST, bf16, tn=512) for k in range(2)]),
+        attn,
+        gbr,
+    )
+    reps.push("out", g_out)
     ticks(1)
     finish()
     for i in range(1, n):
@@ -971,7 +1000,7 @@
     gqkv = gqkv_done().reshape(3, Y * S * blk, T)
     for third in (2, 1, 0):
         g = do(lambda x, g: dot(x, g, LAST).astype(bf16), xn1, gqkv[third])
-        push_pairs(third, g, up_rows)
+        reps.push(third, g)
         if third == 2:
             ticks(1)
     part = do(lambda w, g: dot(w, g, PLAIN), wq, gqkv.reshape(3 * Y * S * blk, T))

time: 866 us -> 874 us (level)
  Pallas kernels: 190 us -> 277 us
  waiting for transfers between devices: 257 us -> 192 us
  local copies, waits for them, and re-layouts: 105 us -> 60.8 us
  other arithmetic: 91.5 us -> 112 us
    unnamed x295 -> x166, local copies, waits for them, and re-layouts: 55.5 us -> 16.4 us
    ppermute x6 -> x3, waiting for transfers between devices: 25.3 us -> 5.55 us  [tick(): got = lax.ppermute(out['total'], 'rep', [(0, 1), (1, 0), (2, 3), (3, 2)])]
    ppermute x18, waiting for transfers between devices: 102 us -> 84.1 us  [along(): return lax.ppermute(x, 'shard', [(i, i ^ step) for i in range(self.s_size)])]
    pallas_call x6, Pallas kernels: 7.17 us -> 25.4 us  [arrange(): pl.pallas_call(arrange_kernel, grid_spec=pltpu.PrefetchScalarGridSpec(num...]
    pallas_call x3, Pallas kernels: 7.09 us -> 22.7 us  [stack_turned(): pl.pallas_call(stack_turned_kernel, grid=(n,), in_specs=[spec, spec], out...]
    ppermute x18, waiting for transfers between devices: 31.6 us -> 16.2 us  [along(): lax.ppermute(x, 'ctx', [(i, i ^ 2 * step) for i in range(self.ctx_size)])]
    pallas_call x8, Pallas kernels: 35.8 us -> 49.2 us  [mm(): pl.pallas_call(functools.partial(product_kernel, dims), grid=(m // tm, n...]
    optimization_barrier x4 -> x2, local copies, waits for them, and re-layouts: 14.6 us -> 1.95 us  [__call__(): args, self.last = lax.optimization_barrier((args, self.last))]
  transfers between devices with their start and end apart: 99 -> 90, of which waited for: 39 -> 29; matrix products, arithmetic and copies ran while one was open for 20% -> 22% of each run, Pallas kernels for 21% -> 29%
where the time goes in v13:
time: 874 us; the launch traced here: 860 us
  Pallas kernels  277 us (32%)
  waiting for transfers between devices  192 us (22%)
  starting transfers between devices  150 us (17%)
  other arithmetic  112 us (13%)
  local copies, waits for them, and re-layouts  60.8 us (7%)
  matrix products  51.8 us (6%)
  between operations  16.1 us (2%)
    ppermute x18, waiting for transfers between devices, along(): return lax.ppermute(x, 'shard', [(i, i ^ step) for i in range(self.s_size)])  84.1 us
    pallas_call x9, Pallas kernels, adam_part(): pl.pallas_call(functools.partial(adam_kernel, rate, two), grid_spec=pltpu...  71.7 us
    ppermute x7, starting transfers between devices, tick(): slot['in_got'] = lax.ppermute(out['new'], 'rep', [(0, 1), (3, 2)])  52.1 us
    dot_general x22, matrix products, dot(): return lax.dot_general(a, b, dims, preferred_element_type=f32)  51.8 us
    pallas_call x8, Pallas kernels, mm(): pl.pallas_call(functools.partial(product_kernel, dims), grid=(m // tm, n...  49.2 us
    convert_element_type x17, other arithmetic, add(): lax.reduce_precision(a.astype(f32) + b.astype(f32), 8, 7).astype(bf16)  39.9 us
    ppermute x7, waiting for transfers between devices, tick(): slot['in_got'] = lax.ppermute(out['new'], 'rep', [(0, 1), (3, 2)])  39.1 us
    pallas_call x4, Pallas kernels, last_step(): pl.pallas_call(last_step_kernel, grid_spec=pltpu.PrefetchScalarGridSpec(n...  30.5 us
  transfers between devices with their start and end apart: 90, of which 29 were waited for; matrix products, arithmetic and copies ran while one was open for 22% of the time, Pallas kernels for 29%

profile of v13, /device:TPU:0, one launch (start us, length us, event | category | flops | bytes accessed | tf_op | source)
XLA Modules:
  0.0 860.2 jit_solution(4571357449657096347)
XLA Ops:
  14.8 6.2 shard_map.306
  28.8 6.0 shard_map.307
  34.8 6.0 shard_map.308
  74.6 9.8 %collective-permute-done.3.b_ref.d_ref = bf16[1536,512]{1,0:T(8,128)(2,1)} collective-permute-done((bf16[1536,512]{1,0:T(8,128)(2,1)}, bf16[1536,512]{1,0:T(8,128)(2,1)}, u32[]{:S(2)}, u32[]{:S(2)}) %collective-permute-start.3) | collective-permute-done | bytes 1572896 | tf_op jit(solution)/shard_map/ppermute | solution.py:62
  97.3 10.3 %collective-permute-done.4 = bf16[768,512]{1,0:T(8,128)(2,1)} collective-permute-done((bf16[768,512]{1,0:T(8,128)(2,1)}, bf16[768,512]{1,0:T(8,128)(2,1)}, u32[]{:S(2)}, u32[]{:S(2)}) %collective-permute-start.4) | collective-permute-done | bytes 786464 | tf_op jit(solution)/shard_map/ppermute | solution.py:61
  108.6 5.6 shard_map.316
  115.3 5.6 shard_map.317
  157.6 11.3 %collective-permute-done.14 = bf16[256,512]{1,0:T(8,128)(2,1)S(1)} collective-permute-done((bf16[256,512]{1,0:T(8,128)(2,1)}, bf16[256,512]{1,0:T(8,128)(2,1)S(1)}, u32[]{:S(2)}, u32[]{:S(2)}) %collective-permute-start.14) | collective-permute-done | bytes 262176 | tf_op jit(solution)/shard_map/ppermute | solution.py:62
  192.5 5.1 convolution_convert_fusion.1.a_ref.c_ref
  205.3 8.0 shard_map.323.a_ref
  213.3 8.0 shard_map.324
  221.3 7.4 shard_map.325
  233.3 6.7 shard_map.328
  240.1 10.8 %collective-permute-done.20 = f32[4,2,1,704]{3,2,1,0:T(1,128)S(1)} collective-permute-done((f32[4,2,1,704]{3,2,1,0:T(1,128)S(1)}, f32[4,2,1,704]{3,2,1,0:T(1,128)S(1)}, u32[]{:S(2)}, u32[]{:S(2)}) %collective-permute-start.20) | collective-permute-done | bytes 22560 | tf_op jit(solution)/shard_map/ppermute | solution.py:62
  268.2 30.7 %collective-permute-done.24 = bf16[704,1024]{1,0:T(8,128)(2,1)S(1)} collective-permute-done((bf16[704,1024]{1,0:T(8,128)(2,1)}, bf16[704,1024]{1,0:T(8,128)(2,1)S(1)}, u32[]{:S(2)}, u32[]{:S(2)}) %collective-permute-start.24) | collective-permute-done | bytes 1441824 | tf_op jit(solution)/shard_map/ppermute | solution.py:62
  300.5 6.2 multiply_convert_fusion
  309.8 6.9 shard_map.331
  335.3 16.6 %collective-permute-done.30 = bf16[352,2048]{1,0:T(8,128)(2,1)S(1)} collective-permute-done((bf16[352,2048]{1,0:T(8,128)(2,1)S(1)}, bf16[352,2048]{1,0:T(8,128)(2,1)S(1)}, u32[]{:S(2)}, u32[]{:S(2)}) %collective-permute-start.30) | collective-permute-done | bytes 1441824 | tf_op jit(solution)/shard_map/ppermute | solution.py:197
  352.4 7.7 collective-permute-done.28.got0_ref
  361.2 7.2 shard_map.332
  376.7 6.9 shard_map.333
  392.9 13.9 %collective-permute-done.31 = bf16[352,2048]{1,0:T(8,128)(2,1)} collective-permute-done((bf16[352,2048]{1,0:T(8,128)(2,1)S(1)}, bf16[352,2048]{1,0:T(8,128)(2,1)}, u32[]{:S(2)}, u32[]{:S(2)}) %collective-permute-start.31) | collective-permute-done | bytes 1441824 | tf_op jit(solution)/shard_map/ppermute | solution.py:197
  413.8 7.6 collective-permute-start.40
  421.3 7.9 shard_map.334
  429.2 7.2 shard_map.335
  436.4 7.2 shard_map.336
  443.6 7.3 convolution_add_fusion.2
  460.6 8.3 collective-permute-start.47
  472.8 6.9 shard_map.337
  484.0 6.5 collective-permute-done.48
  490.5 8.6 collective-permute-done.47
  527.3 7.2 shard_map.339
  534.6 7.1 shard_map.340
  567.8 8.3 collective-permute-done.52
  579.9 7.8 shard_map.343
  587.7 5.5 collective-permute-done.57
  593.3 9.3 %collective-permute-start.59 = (bf16[512,1024]{1,0:T(8,128)(2,1)}, bf16[512,1024]{1,0:T(8,128)(2,1)}, u32[]{:S(2)}, u32[]{:S(2)}) collective-permute-start(bf16[512,1024]{1,0:T(8,128)(2,1)} %pad_maximum_fusion.7), channel_id=1, source_target_pairs={{0,8},{24,16},{1,9},{25,17},{2,10},{26,18},{3,11},{27,19},{4,12},{... | collective-permute-start | bytes 3145736 | tf_op jit(solution)/shard_map/ppermute | solution.py:197
  613.3 7.8 shard_map.344
  621.2 11.4 %shard_map.345 = bf16[3,2,2,256,1024]{4,3,2,1,0:T(8,128)(2,1)} custom-call(s32[4]{0:T(128)} %pad_add_fusion.1.bits_ref, bf16[2,1,768,512]{3,2,1,0:T(8,128)(2,1)} %copy-done.25, bf16[2,1,768,512]{3,2,1,0:T(8,128)(2,1)} %collective-permute-done.55.got0_ref, bf16[1,2,768,512]{3,2,1,0:T(8,128)(2,1)} %pad_maximum_fusion.2.own1_ref, ...), custom_call_target="tpu_custom_call" | custom-call | flops 1024 | bytes 1024 | tf_op jit(solution)/shard_map/pallas_call | solution.py:364
  647.0 12.4 %collective-permute-start.63 = (bf16[512,1024]{1,0:T(8,128)(2,1)}, bf16[512,1024]{1,0:T(8,128)(2,1)}, u32[]{:S(2)}, u32[]{:S(2)}) collective-permute-start(bf16[512,1024]{1,0:T(8,128)(2,1)} %convolution_convert_fusion.10), channel_id=1, source_target_pairs={{0,8},{24,16},{1,9},{25,17},{2,10},{26,18},{3,11},{27,19},{4,12},{... | collective-permute-start | bytes 3145736 | tf_op jit(solution)/shard_map/ppermute | solution.py:197
  670.1 6.6 collective-permute-start.68
  676.7 14.3 %shard_map.346 = (f32[256,11264]{1,0:T(8,128)}, f32[256,11264]{1,0:T(8,128)}, f32[256,11264]{1,0:T(8,128)}) custom-call(s32[1]{0:T(128)} %bitcast.8.core_ref, f32[256,11264]{1,0:T(8,128)} %w_ref.9, f32[256,11264]{1,0:T(8,128)} %m_ref.3, f32[256,11264]{1,0:T(8,128)} %v_ref.3, bf16[256,2816]{1,0:T(8,128)(2,1)} %broadcast_select_fusion.5.refs_0_, ...), custom_call_target="tpu_custom_call" | custom-call | flops 1024 | bytes 1024 | tf_op jit(solution)/shard_map/pallas_call | solution.py:451
  729.9 8.3 all-to-all-done.1
  753.2 14.4 %shard_map.347 = (f32[256,11264]{1,0:T(8,128)}, f32[256,11264]{1,0:T(8,128)}, f32[256,11264]{1,0:T(8,128)}) custom-call(s32[1]{0:T(128)} %bitcast.8.core_ref, f32[256,11264]{1,0:T(8,128)} %w_ref.9, f32[256,11264]{1,0:T(8,128)} %m_ref.3, f32[256,11264]{1,0:T(8,128)} %v_ref.3, ...), custom_call_target="tpu_custom_call", output_to_operand_aliasing={{0}: (6, {}), {1}: (7, {}), {2}: (8, {})} | custom-call | flops 1024 | bytes 1024 | tf_op jit(solution)/shard_map/pallas_call | solution.py:451
  806.6 14.3 %collective-permute-done.79 = bf16[512,1024]{1,0:T(8,128)(2,1)} collective-permute-done((bf16[512,1024]{1,0:T(8,128)(2,1)}, bf16[512,1024]{1,0:T(8,128)(2,1)}, u32[]{:S(2)}, u32[]{:S(2)}) %collective-permute-start.79) | collective-permute-done | bytes 1048608 | tf_op jit(solution)/shard_map/ppermute | solution.py:200
  830.3 6.8 shard_map.350
  838.7 6.7 shard_map.351
  846.2 6.7 shard_map.352
  (542 shorter events, 418.6 us)
Async XLA Ops:
  26.2 195.1 %all-gather.2.cloned.1.call-start = ((), (), s32[]{:S(2)}) async-start(), calls=%async_computation.5 | async-start | bytes 4718592 | tf_op jit(solution)/shard_map/all_gather | solution.py:631
  47.4 37.0 %collective-permute-start.3 = (bf16[1536,512]{1,0:T(8,128)(2,1)}, bf16[1536,512]{1,0:T(8,128)(2,1)}, u32[]{:S(2)}, u32[]{:S(2)}) collective-permute-start(bf16[1536,512]{1,0:T(8,128)(2,1)} %convolution_convert_fusion.7), channel_id=1, source_target_pairs={{0,1},{1,0},{2,3},{3,2},{4,5},{5,4},{6,7},{7,6},{8,9},{9,8},{10,11... | collective-permute-start | bytes 4718600 | tf_op jit(solution)/shard_map/ppermute | solution.py:62
  51.4 38.6 %collective-permute-start.5 = (bf16[1536,512]{1,0:T(8,128)(2,1)}, bf16[1536,512]{1,0:T(8,128)(2,1)S(1)}, u32[]{:S(2)}, u32[]{:S(2)}) collective-permute-start(bf16[1536,512]{1,0:T(8,128)(2,1)} %convolution_convert_fusion.6), channel_id=1, source_target_pairs={{0,4},{2,6},{4,0},{6,2},{1,5},{3,7},{5,1},{7,3},{8,12},{10,14},{12... | collective-permute-start | bytes 4718600 | tf_op jit(solution)/shard_map/ppermute | solution.py:61
  121.5 664.5 %reduce-scatter.2.cloned.1.call-start = ((), (), s32[]{:S(2)}) async-start(), calls=%async_computation.6 | async-start | bytes 4718592 | tf_op jit(solution)/shard_map/reduce_scatter | solution.py:1008
  185.6 69.5 %collective-permute-start.19 = (bf16[1408,1024]{1,0:T(8,128)(2,1)}, bf16[1408,1024]{1,0:T(8,128)(2,1)}, u32[]{:S(2)}, u32[]{:S(2)}) collective-permute-start(bf16[1408,1024]{1,0:T(8,128)(2,1)} %convolution_convert_fusion.3), channel_id=1, source_target_pairs={{0,1},{1,0},{2,3},{3,2},{4,5},{5,4},{6,7},{7,6},{8,9},{9,8},{10,11... | collective-permute-start | bytes 8650760 | tf_op jit(solution)/shard_map/ppermute | solution.py:62
  190.4 69.5 %collective-permute-start.23 = (bf16[1408,1024]{1,0:T(8,128)(2,1)}, bf16[1408,1024]{1,0:T(8,128)(2,1)S(1)}, u32[]{:S(2)}, u32[]{:S(2)}) collective-permute-start(bf16[1408,1024]{1,0:T(8,128)(2,1)} %convolution_convert_fusion.2), channel_id=1, source_target_pairs={{0,4},{2,6},{4,0},{6,2},{1,5},{3,7},{5,1},{7,3},{8,12},{10,14},{12... | collective-permute-start | bytes 8650760 | tf_op jit(solution)/shard_map/ppermute | solution.py:61
  191.0 59.9 %collective-permute-start.20 = (f32[4,2,1,704]{3,2,1,0:T(1,128)S(1)}, f32[4,2,1,704]{3,2,1,0:T(1,128)S(1)}, u32[]{:S(2)}, u32[]{:S(2)}) collective-permute-start(f32[4,2,1,704]{3,2,1,0:T(1,128)S(1)} %get-tuple-element.944), channel_id=1, source_target_pairs={{0,1},{1,0},{2,3},{3,2},{4,5},{5,4},{6,7},{7,6},{8,9},{9,8},{10,11... | collective-permute-start | bytes 67592 | tf_op jit(solution)/shard_map/ppermute | solution.py:62
  266.1 32.7 %collective-permute-start.24 = (bf16[704,1024]{1,0:T(8,128)(2,1)}, bf16[704,1024]{1,0:T(8,128)(2,1)S(1)}, u32[]{:S(2)}, u32[]{:S(2)}) collective-permute-start(bf16[704,1024]{1,0:T(8,128)(2,1)} %get-tuple-element.578), channel_id=1, source_target_pairs={{0,1},{1,0},{2,3},{3,2},{4,5},{5,4},{6,7},{7,6},{8,9},{9,8},{10,11... | collective-permute-start | bytes 4325384 | tf_op jit(solution)/shard_map/ppermute | solution.py:62
  267.2 32.2 %collective-permute-start.22 = (bf16[704,1024]{1,0:T(8,128)(2,1)}, bf16[704,1024]{1,0:T(8,128)(2,1)S(1)}, u32[]{:S(2)}, u32[]{:S(2)}) collective-permute-start(bf16[704,1024]{1,0:T(8,128)(2,1)} %get-tuple-element.574), channel_id=1, source_target_pairs={{0,4},{2,6},{4,0},{6,2},{1,5},{3,7},{5,1},{7,3},{8,12},{10,14},{12... | collective-permute-start | bytes 4325384 | tf_op jit(solution)/shard_map/ppermute | solution.py:61
  320.1 31.8 %collective-permute-start.30 = (bf16[352,2048]{1,0:T(8,128)(2,1)S(1)}, bf16[352,2048]{1,0:T(8,128)(2,1)S(1)}, u32[]{:S(2)}, u32[]{:S(2)}) collective-permute-start(bf16[352,2048]{1,0:T(8,128)(2,1)S(1)} %get-tuple-element.600), channel_id=1, source_target_pairs={{0,8},{24,16},{1,9},{25,17},{2,10},{26,18},{3,11},{27,19},{4,12},{... | collective-permute-start | bytes 4325384 | tf_op jit(solution)/shard_map/ppermute | solution.py:197
  330.2 29.9 %collective-permute-start.28 = (bf16[2,1,704,512]{3,2,1,0:T(8,128)(2,1)S(1)}, bf16[2,1,704,512]{3,2,1,0:T(8,128)(2,1)S(1)}, u32[]{:S(2)}, u32[]{:S(2)}) collective-permute-start(bf16[2,1,704,512]{3,2,1,0:T(8,128)(2,1)S(1)} %pad_maximum_fusion.3.own0_ref), channel_id=1, source_target_pairs={{0,1},{1,0},{2,3},{3,2},{4,5},{5,4},{6,7},{7,6},{8,9},{9,8},{10,11... | collective-permute-start | bytes 4325384 | tf_op jit(solution)/shard_map/ppermute | solution.py:62
  331.4 29.7 %collective-permute-start.29 = (bf16[1,2,704,512]{3,2,1,0:T(8,128)(2,1)S(1)}, bf16[1,2,704,512]{3,2,1,0:T(8,128)(2,1)}, u32[]{:S(2)}, u32[]{:S(2)}) collective-permute-start(bf16[1,2,704,512]{3,2,1,0:T(8,128)(2,1)S(1)} %pad_maximum_fusion.4.own1_ref), channel_id=1, source_target_pairs={{0,4},{2,6},{4,0},{6,2},{1,5},{3,7},{5,1},{7,3},{8,12},{10,14},{12... | collective-permute-start | bytes 4325384 | tf_op jit(solution)/shard_map/ppermute | solution.py:61
  334.1 34.3 %collective-permute-start.32 = (f32[2,1024]{1,0:T(2,128)S(1)}, f32[2,1024]{1,0:T(2,128)S(1)}, u32[]{:S(2)}, u32[]{:S(2)}) collective-permute-start(f32[2,1024]{1,0:T(2,128)S(1)} %add.410), channel_id=1, source_target_pairs={{0,4},{2,6},{4,0},{6,2},{1,5},{3,7},{5,1},{7,3},{8,12},{10,14},{12... | collective-permute-start | bytes 24584 | tf_op jit(solution)/shard_map/ppermute | solution.py:61
  372.2 34.6 %collective-permute-start.31 = (bf16[352,2048]{1,0:T(8,128)(2,1)S(1)}, bf16[352,2048]{1,0:T(8,128)(2,1)}, u32[]{:S(2)}, u32[]{:S(2)}) collective-permute-start(bf16[352,2048]{1,0:T(8,128)(2,1)S(1)} %copy-done.28), channel_id=1, source_target_pairs={{0,8},{24,16},{1,9},{25,17},{2,10},{26,18},{3,11},{27,19},{4,12},{... | collective-permute-start | bytes 4325384 | tf_op jit(solution)/shard_map/ppermute | solution.py:197
  386.3 50.1 %collective-permute-start.38 = (bf16[1,2,704,512]{3,2,1,0:T(8,128)(2,1)}, bf16[1,2,704,512]{3,2,1,0:T(8,128)(2,1)}, u32[]{:S(2)}, u32[]{:S(2)}) collective-permute-start(bf16[1,2,704,512]{3,2,1,0:T(8,128)(2,1)} %pad_maximum_fusion.6.own1_ref), channel_id=1, source_target_pairs={{0,4},{2,6},{4,0},{6,2},{1,5},{3,7},{5,1},{7,3},{8,12},{10,14},{12... | collective-permute-start | bytes 4325384 | tf_op jit(solution)/shard_map/ppermute | solution.py:61
  390.0 46.4 %collective-permute-start.37 = (bf16[2,1,704,512]{3,2,1,0:T(8,128)(2,1)}, bf16[2,1,704,512]{3,2,1,0:T(8,128)(2,1)}, u32[]{:S(2)}, u32[]{:S(2)}) collective-permute-start(bf16[2,1,704,512]{3,2,1,0:T(8,128)(2,1)} %pad_maximum_fusion.5.own0_ref), channel_id=1, source_target_pairs={{0,1},{1,0},{2,3},{3,2},{4,5},{5,4},{6,7},{7,6},{8,9},{9,8},{10,11... | collective-permute-start | bytes 4325384 | tf_op jit(solution)/shard_map/ppermute | solution.py:62
  408.8 42.3 %collective-permute-start.41 = (bf16[352,2048]{1,0:T(8,128)(2,1)S(1)}, bf16[352,2048]{1,0:T(8,128)(2,1)}, u32[]{:S(2)}, u32[]{:S(2)}) collective-permute-start(bf16[352,2048]{1,0:T(8,128)(2,1)S(1)} %reduce-precision_convert_fusion.9), channel_id=1, source_target_pairs={{8,0},{16,24},{9,1},{17,25},{10,2},{18,26},{11,3},{19,27},{12,4},{... | collective-permute-start | bytes 4325384 | tf_op jit(solution)/shard_map/ppermute | solution.py:200
  412.0 39.1 %collective-permute-start.42 = (bf16[352,2048]{1,0:T(8,128)(2,1)S(1)}, bf16[352,2048]{1,0:T(8,128)(2,1)}, u32[]{:S(2)}, u32[]{:S(2)}) collective-permute-start(bf16[352,2048]{1,0:T(8,128)(2,1)S(1)} %reduce-precision_convert_fusion.10), channel_id=1, source_target_pairs={{8,16},{16,8},{9,17},{17,9},{10,18},{18,10},{11,19},{19,11},{12,20... | collective-permute-start | bytes 4325384 | tf_op jit(solution)/shard_map/ppermute | solution.py:203
  413.8 37.4 %collective-permute-start.40 = (bf16[256,2816]{1,0:T(8,128)(2,1)}, bf16[256,2816]{1,0:T(8,128)(2,1)}, u32[]{:S(2)}, u32[]{:S(2)}) collective-permute-start(bf16[256,2816]{1,0:T(8,128)(2,1)} %get-tuple-element.635), channel_id=1, source_target_pairs={{0,8},{24,16},{1,9},{25,17},{2,10},{26,18},{3,11},{27,19},{4,12},{... | collective-permute-start | bytes 4325384 | tf_op jit(solution)/shard_map/ppermute | solution.py:197
  454.2 36.3 %collective-permute-start.48 = (bf16[352,2048]{1,0:T(8,128)(2,1)}, bf16[352,2048]{1,0:T(8,128)(2,1)}, u32[]{:S(2)}, u32[]{:S(2)}) collective-permute-start(bf16[352,2048]{1,0:T(8,128)(2,1)} %reduce-precision_convert_fusion.7), channel_id=1, source_target_pairs={{8,0},{16,24},{9,1},{17,25},{10,2},{18,26},{11,3},{19,27},{12,4},{... | collective-permute-start | bytes 4325384 | tf_op jit(solution)/shard_map/ppermute | solution.py:200
  458.8 31.7 %collective-permute-start.49 = (bf16[256,2816]{1,0:T(8,128)(2,1)}, bf16[256,2816]{1,0:T(8,128)(2,1)}, u32[]{:S(2)}, u32[]{:S(2)}) collective-permute-start(bf16[256,2816]{1,0:T(8,128)(2,1)} %reduce-precision_convert_fusion.8), channel_id=1, source_target_pairs={{8,16},{16,8},{9,17},{17,9},{10,18},{18,10},{11,19},{19,11},{12,20... | collective-permute-start | bytes 4325384 | tf_op jit(solution)/shard_map/ppermute | solution.py:203
  460.6 38.5 %collective-permute-start.47 = (bf16[256,2816]{1,0:T(8,128)(2,1)}, bf16[256,2816]{1,0:T(8,128)(2,1)}, u32[]{:S(2)}, u32[]{:S(2)}) collective-permute-start(bf16[256,2816]{1,0:T(8,128)(2,1)} %get-tuple-element.653), channel_id=1, source_target_pairs={{0,8},{24,16},{1,9},{25,17},{2,10},{26,18},{3,11},{27,19},{4,12},{... | collective-permute-start | bytes 4325384 | tf_op jit(solution)/shard_map/ppermute | solution.py:197
  512.4 42.3 %collective-permute-start.54 = (bf16[256,2816]{1,0:T(8,128)(2,1)}, bf16[256,2816]{1,0:T(8,128)(2,1)}, u32[]{:S(2)}, u32[]{:S(2)}) collective-permute-start(bf16[256,2816]{1,0:T(8,128)(2,1)} %reduce-precision_convert_fusion.6), channel_id=1, source_target_pairs={{8,16},{16,8},{9,17},{17,9},{10,18},{18,10},{11,19},{19,11},{12,20... | collective-permute-start | bytes 4325384 | tf_op jit(solution)/shard_map/ppermute | solution.py:203
  517.7 36.9 %collective-permute-start.53 = (bf16[256,2816]{1,0:T(8,128)(2,1)}, bf16[256,2816]{1,0:T(8,128)(2,1)}, u32[]{:S(2)}, u32[]{:S(2)}) collective-permute-start(bf16[256,2816]{1,0:T(8,128)(2,1)} %fusion.5), channel_id=1, source_target_pairs={{0,8},{8,0},{16,24},{24,16},{1,9},{9,1},{17,25},{25,17},{2,10},{10... | collective-permute-start | bytes 4325384 | tf_op jit(solution)/shard_map/ppermute | solution.py:192
  560.2 33.1 %collective-permute-start.57 = (bf16[256,2816]{1,0:T(8,128)(2,1)}, bf16[256,2816]{1,0:T(8,128)(2,1)}, u32[]{:S(2)}, u32[]{:S(2)}) collective-permute-start(bf16[256,2816]{1,0:T(8,128)(2,1)} %fusion.6), channel_id=1, source_target_pairs={{0,8},{8,0},{16,24},{24,16},{1,9},{9,1},{17,25},{25,17},{2,10},{10... | collective-permute-start | bytes 4325384 | tf_op jit(solution)/shard_map/ppermute | solution.py:192
  563.3 30.0 %collective-permute-start.58 = (bf16[256,2816]{1,0:T(8,128)(2,1)}, bf16[256,2816]{1,0:T(8,128)(2,1)}, u32[]{:S(2)}, u32[]{:S(2)}) collective-permute-start(bf16[256,2816]{1,0:T(8,128)(2,1)} %reduce-precision_convert_fusion.4), channel_id=1, source_target_pairs={{8,16},{16,8},{9,17},{17,9},{10,18},{18,10},{11,19},{19,11},{12,20... | collective-permute-start | bytes 4325384 | tf_op jit(solution)/shard_map/ppermute | solution.py:203
  576.4 44.8 %collective-permute-start.55 = (bf16[2,1,768,512]{3,2,1,0:T(8,128)(2,1)S(1)}, bf16[2,1,768,512]{3,2,1,0:T(8,128)(2,1)}, u32[]{:S(2)}, u32[]{:S(2)}) collective-permute-start(bf16[2,1,768,512]{3,2,1,0:T(8,128)(2,1)S(1)} %pad_maximum_fusion.1.own0_ref), channel_id=1, source_target_pairs={{0,1},{1,0},{2,3},{3,2},{4,5},{5,4},{6,7},{7,6},{8,9},{9,8},{10,11... | collective-permute-start | bytes 4718600 | tf_op jit(solution)/shard_map/ppermute | solution.py:62
  579.3 41.8 %collective-permute-start.56 = (bf16[1,2,768,512]{3,2,1,0:T(8,128)(2,1)}, bf16[1,2,768,512]{3,2,1,0:T(8,128)(2,1)}, u32[]{:S(2)}, u32[]{:S(2)}) collective-permute-start(bf16[1,2,768,512]{3,2,1,0:T(8,128)(2,1)} %pad_maximum_fusion.2.own1_ref), channel_id=1, source_target_pairs={{0,4},{2,6},{4,0},{6,2},{1,5},{3,7},{5,1},{7,3},{8,12},{10,14},{12... | collective-permute-start | bytes 4718600 | tf_op jit(solution)/shard_map/ppermute | solution.py:61
  593.3 45.3 %collective-permute-start.59 = (bf16[512,1024]{1,0:T(8,128)(2,1)}, bf16[512,1024]{1,0:T(8,128)(2,1)}, u32[]{:S(2)}, u32[]{:S(2)}) collective-permute-start(bf16[512,1024]{1,0:T(8,128)(2,1)} %pad_maximum_fusion.7), channel_id=1, source_target_pairs={{0,8},{24,16},{1,9},{25,17},{2,10},{26,18},{3,11},{27,19},{4,12},{... | collective-permute-start | bytes 3145736 | tf_op jit(solution)/shard_map/ppermute | solution.py:197
  605.8 33.5 %collective-permute-start.60 = (bf16[256,2816]{1,0:T(8,128)(2,1)}, bf16[256,2816]{1,0:T(8,128)(2,1)}, u32[]{:S(2)}, u32[]{:S(2)}) collective-permute-start(bf16[256,2816]{1,0:T(8,128)(2,1)} %reduce-precision_convert_fusion.1), channel_id=1, source_target_pairs={{8,0},{16,24},{9,1},{17,25},{10,2},{18,26},{11,3},{19,27},{12,4},{... | collective-permute-start | bytes 4325384 | tf_op jit(solution)/shard_map/ppermute | solution.py:200
  609.9 29.4 %collective-permute-start.61 = (bf16[256,2816]{1,0:T(8,128)(2,1)}, bf16[256,2816]{1,0:T(8,128)(2,1)S(1)}, u32[]{:S(2)}, u32[]{:S(2)}) collective-permute-start(bf16[256,2816]{1,0:T(8,128)(2,1)} %reduce-precision_convert_fusion.2), channel_id=1, source_target_pairs={{8,16},{16,8},{9,17},{17,9},{10,18},{18,10},{11,19},{19,11},{12,20... | collective-permute-start | bytes 4325384 | tf_op jit(solution)/shard_map/ppermute | solution.py:203
  621.1 48.9 %collective-permute-start.66 = (bf16[256,2816]{1,0:T(8,128)(2,1)}, bf16[256,2816]{1,0:T(8,128)(2,1)}, u32[]{:S(2)}, u32[]{:S(2)}) collective-permute-start(bf16[256,2816]{1,0:T(8,128)(2,1)} %broadcast_select_fusion.4), channel_id=1, source_target_pairs={{0,2},{2,0},{4,6},{6,4},{1,3},{3,1},{5,7},{7,5},{8,10},{10,8},{12,... | collective-permute-start | bytes 4325384 | tf_op jit(solution)/shard_map/ppermute | solution.py:57
  641.5 49.5 %collective-permute-start.65 = (bf16[512,1024]{1,0:T(8,128)(2,1)S(1)}, bf16[512,1024]{1,0:T(8,128)(2,1)}, u32[]{:S(2)}, u32[]{:S(2)}) collective-permute-start(bf16[512,1024]{1,0:T(8,128)(2,1)S(1)} %reduce-precision_convert_fusion.19), channel_id=1, source_target_pairs={{8,16},{16,8},{9,17},{17,9},{10,18},{18,10},{11,19},{19,11},{12,20... | collective-permute-start | bytes 3145736 | tf_op jit(solution)/shard_map/ppermute | solution.py:203
  647.0 44.0 %collective-permute-start.63 = (bf16[512,1024]{1,0:T(8,128)(2,1)}, bf16[512,1024]{1,0:T(8,128)(2,1)}, u32[]{:S(2)}, u32[]{:S(2)}) collective-permute-start(bf16[512,1024]{1,0:T(8,128)(2,1)} %convolution_convert_fusion.10), channel_id=1, source_target_pairs={{0,8},{24,16},{1,9},{25,17},{2,10},{26,18},{3,11},{27,19},{4,12},{... | collective-permute-start | bytes 3145736 | tf_op jit(solution)/shard_map/ppermute | solution.py:197
  661.2 32.7 %collective-permute-start.64 = (bf16[256,2816]{1,0:T(8,128)(2,1)S(1)}, bf16[256,2816]{1,0:T(8,128)(2,1)}, u32[]{:S(2)}, u32[]{:S(2)}) collective-permute-start(bf16[256,2816]{1,0:T(8,128)(2,1)S(1)} %reduce-precision_convert_fusion), channel_id=1, source_target_pairs={{8,0},{16,24},{9,1},{17,25},{10,2},{18,26},{11,3},{19,27},{12,4},{... | collective-permute-start | bytes 4325384 | tf_op jit(solution)/shard_map/ppermute | solution.py:200
  667.4 28.4 %collective-permute-start.62 = (f32[256,1024]{1,0:T(8,128)}, f32[256,1024]{1,0:T(8,128)}, u32[]{:S(2)}, u32[]{:S(2)}) collective-permute-start(f32[256,1024]{1,0:T(8,128)} %get-tuple-element.898), channel_id=1, source_target_pairs={{0,2},{2,0},{4,6},{6,4},{1,3},{3,1},{5,7},{7,5},{8,10},{10,8},{12,... | collective-permute-start | bytes 3145736 | tf_op jit(solution)/shard_map/ppermute | solution.py:57
  670.1 39.7 %collective-permute-start.68 = (bf16[512,1024]{1,0:T(8,128)(2,1)}, bf16[512,1024]{1,0:T(8,128)(2,1)}, u32[]{:S(2)}, u32[]{:S(2)}) collective-permute-start(bf16[512,1024]{1,0:T(8,128)(2,1)} %convolution_convert_fusion.9), channel_id=1, source_target_pairs={{0,8},{24,16},{1,9},{25,17},{2,10},{26,18},{3,11},{27,19},{4,12},{... | collective-permute-start | bytes 3145736 | tf_op jit(solution)/shard_map/ppermute | solution.py:197
  704.0 36.9 %collective-permute-start.75 = (bf16[512,1024]{1,0:T(8,128)(2,1)S(1)}, bf16[512,1024]{1,0:T(8,128)(2,1)}, u32[]{:S(2)}, u32[]{:S(2)}) collective-permute-start(bf16[512,1024]{1,0:T(8,128)(2,1)S(1)} %reduce-precision_convert_fusion.18), channel_id=1, source_target_pairs={{8,16},{16,8},{9,17},{17,9},{10,18},{18,10},{11,19},{19,11},{12,20... | collective-permute-start | bytes 3145736 | tf_op jit(solution)/shard_map/ppermute | solution.py:203
  709.0 31.8 %collective-permute-start.74 = (bf16[512,1024]{1,0:T(8,128)(2,1)}, bf16[512,1024]{1,0:T(8,128)(2,1)}, u32[]{:S(2)}, u32[]{:S(2)}) collective-permute-start(bf16[512,1024]{1,0:T(8,128)(2,1)} %fusion.9), channel_id=1, source_target_pairs={{0,8},{8,0},{16,24},{24,16},{1,9},{9,1},{17,25},{25,17},{2,10},{10... | collective-permute-start | bytes 3145736 | tf_op jit(solution)/shard_map/ppermute | solution.py:192
  726.0 27.3 %collective-permute-start.73 = (bf16[256,2816]{1,0:T(8,128)(2,1)}, bf16[256,2816]{1,0:T(8,128)(2,1)}, u32[]{:S(2)}, u32[]{:S(2)}) collective-permute-start(bf16[256,2816]{1,0:T(8,128)(2,1)} %broadcast_select_fusion.2), channel_id=1, source_target_pairs={{0,2},{2,0},{4,6},{6,4},{1,3},{3,1},{5,7},{7,5},{8,10},{10,8},{12,... | collective-permute-start | bytes 4325384 | tf_op jit(solution)/shard_map/ppermute | solution.py:57
  729.0 40.0 %collective-permute-start.72 = (bf16[512,1024]{1,0:T(8,128)(2,1)}, bf16[512,1024]{1,0:T(8,128)(2,1)S(1)}, u32[]{:S(2)}, u32[]{:S(2)}) collective-permute-start(bf16[512,1024]{1,0:T(8,128)(2,1)} %reduce-precision_convert_fusion.17), channel_id=1, source_target_pairs={{8,16},{16,8},{9,17},{17,9},{10,18},{18,10},{11,19},{19,11},{12,20... | collective-permute-start | bytes 3145736 | tf_op jit(solution)/shard_map/ppermute | solution.py:203
  743.4 38.6 %collective-permute-start.77 = (bf16[512,1024]{1,0:T(8,128)(2,1)}, bf16[512,1024]{1,0:T(8,128)(2,1)}, u32[]{:S(2)}, u32[]{:S(2)}) collective-permute-start(bf16[512,1024]{1,0:T(8,128)(2,1)} %reduce-precision_convert_fusion.13), channel_id=1, source_target_pairs={{8,0},{16,24},{9,1},{17,25},{10,2},{18,26},{11,3},{19,27},{12,4},{... | collective-permute-start | bytes 3145736 | tf_op jit(solution)/shard_map/ppermute | solution.py:200
  746.5 35.5 %collective-permute-start.78 = (bf16[512,1024]{1,0:T(8,128)(2,1)S(1)}, bf16[512,1024]{1,0:T(8,128)(2,1)}, u32[]{:S(2)}, u32[]{:S(2)}) collective-permute-start(bf16[512,1024]{1,0:T(8,128)(2,1)S(1)} %reduce-precision_convert_fusion.15), channel_id=1, source_target_pairs={{8,16},{16,8},{9,17},{17,9},{10,18},{18,10},{11,19},{19,11},{12,20... | collective-permute-start | bytes 3145736 | tf_op jit(solution)/shard_map/ppermute | solution.py:203
  772.4 28.2 %collective-permute-start.80 = (bf16[512,1024]{1,0:T(8,128)(2,1)S(1)}, bf16[512,1024]{1,0:T(8,128)(2,1)}, u32[]{:S(2)}, u32[]{:S(2)}) collective-permute-start(bf16[512,1024]{1,0:T(8,128)(2,1)S(1)} %reduce-precision_convert_fusion.14), channel_id=1, source_target_pairs={{8,0},{16,24},{9,1},{17,25},{10,2},{18,26},{11,3},{19,27},{12,4},{... | collective-permute-start | bytes 3145736 | tf_op jit(solution)/shard_map/ppermute | solution.py:200
  784.7 36.3 %collective-permute-start.79 = (bf16[512,1024]{1,0:T(8,128)(2,1)}, bf16[512,1024]{1,0:T(8,128)(2,1)}, u32[]{:S(2)}, u32[]{:S(2)}) collective-permute-start(bf16[512,1024]{1,0:T(8,128)(2,1)} %reduce-precision_convert_fusion.12), channel_id=1, source_target_pairs={{8,0},{16,24},{9,1},{17,25},{10,2},{18,26},{11,3},{19,27},{12,4},{... | collective-permute-start | bytes 3145736 | tf_op jit(solution)/shard_map/ppermute | solution.py:200
  789.1 34.4 %all-to-all-start.2 = ((bf16[8,256,128]{2,1,0:T(8,128)(2,1)}), bf16[8,256,128]{2,1,0:T(8,128)(2,1)S(1)}, u32[]{:S(2)}, u32[]{:S(2)}) async-start(bf16[8,256,128]{2,1,0:T(8,128)(2,1)} %bitcast.92), calls=%async_computation.3 | async-start | bytes 1048576 | tf_op jit(solution)/shard_map/all_to_all | solution.py:1050
  795.6 34.0 %collective-permute-start.83 = (bf16[256,1024]{1,0:T(8,128)(2,1)}, bf16[256,1024]{1,0:T(8,128)(2,1)S(1)}, u32[]{:S(2)}, u32[]{:S(2)}) collective-permute-start(bf16[256,1024]{1,0:T(8,128)(2,1)} %get-tuple-element.918), channel_id=1, source_target_pairs={{0,2},{2,0},{4,6},{6,4},{1,3},{3,1},{5,7},{7,5},{8,10},{10,8},{12,... | collective-permute-start | bytes 1572872 | tf_op jit(solution)/shard_map/ppermute | solution.py:57
  803.0 34.9 %collective-permute-start.82 = (bf16[256,1024]{1,0:T(8,128)(2,1)}, bf16[256,1024]{1,0:T(8,128)(2,1)S(1)}, u32[]{:S(2)}, u32[]{:S(2)}) collective-permute-start(bf16[256,1024]{1,0:T(8,128)(2,1)} %get-tuple-element.920), channel_id=1, source_target_pairs={{0,2},{2,0},{4,6},{6,4},{1,3},{3,1},{5,7},{7,5},{8,10},{10,8},{12,... | collective-permute-start | bytes 1572872 | tf_op jit(solution)/shard_map/ppermute | solution.py:57
  (122 other events, 1111.4 us)
Sparse Core Ops, SparseCore 0:
  121.6 47.4 all-gather.1
  509.8 52.3 reduce-scatter.1

commit v14 on v13

--- a/solution.py
+++ b/solution.py
@@ -219,9 +219,54 @@
         in_specs=[spec],
         out_specs=spec,
         out_shape=jax.ShapeDtypeStruct(w.shape, bf16),
-        compiler_params=pltpu.CompilerParams(vmem_limit_bytes=60 * 1024 * 1024),
+        compiler_params=pltpu.CompilerParams(vmem_limit_bytes=48 * 1024 * 1024),
         cost_estimate=SMALL,
     )(w)
+
+
+def gated_kernel(ga_ref, gb_ref, ua_ref, ub_ref, grad_ref, gains_ref, g0_ref, g1_ref, u0_ref, u1_ref, act_ref, sums_ref):
+    half = g0_ref.shape[1]
+    gate = ga_ref[...].astype(f32) + gb_ref[...].astype(f32)
+    up = ua_ref[...].astype(f32) + ub_ref[...].astype(f32)
+    sig = jax.nn.sigmoid(gate)
+    silu = gate * sig
+    grad = grad_ref[...]
+    act_ref[...] = (silu * up).astype(bf16)
+    ggate = (grad * up * sig * (1.0 + gate * (1.0 - sig))).astype(bf16)
+    gup = (grad * silu).astype(bf16)
+    g0_ref[...] = ggate[:, :half]
+    g1_ref[...] = ggate[:, half:]
+    u0_ref[...] = gup[:, :half]
+    u1_ref[...] = gup[:, half:]
+    a, b = ggate.astype(f32), gup.astype(f32)
+    e = jnp.sum(a * gains_ref[:, 0:1] + b * gains_ref[:, 2:3], axis=0, keepdims=True)
+    ez = jnp.sum(a * (gate - gains_ref[:, 1:2]) + b * (up - gains_ref[:, 3:4]), axis=0, keepdims=True)
+    both = jnp.concatenate([e, ez], axis=0)
+
+    @pl.when(pl.program_id(0) == 0)
+    def _():
+        sums_ref[...] = both
+
+    @pl.when(pl.program_id(0) > 0)
+    def _():
+        sums_ref[...] += both
+
+
+def gated(ga, gb, ua, ub, grad_act, gains):
+    rows, t = grad_act.shape
+    n = max(n for n in (1, 2, 4) if rows % (16 * n) == 0)
+    whole = pl.BlockSpec((rows // n, t), lambda i: (i, 0))
+    half = pl.BlockSpec((rows // n, t // 2), lambda i: (i, 0))
+    out_half = jax.ShapeDtypeStruct((rows, t // 2), bf16)
+    return pl.pallas_call(
+        gated_kernel,
+        grid=(n,),
+        in_specs=[whole] * 5 + [pl.BlockSpec((rows // n, 4), lambda i: (i, 0))],
+        out_specs=[half] * 4 + [whole, pl.BlockSpec((2, t), lambda i: (0, 0))],
+        out_shape=[out_half] * 4 + [jax.ShapeDtypeStruct((rows, t), bf16), jax.ShapeDtypeStruct((2, t), f32)],
+        compiler_params=pltpu.CompilerParams(vmem_limit_bytes=56 * 1024 * 1024),
+        cost_estimate=SMALL,
+    )(ga, gb, ua, ub, grad_act, gains)
 
 
 def own_columns_kernel(block_ref, x_ref, out_ref):
@@ -242,7 +287,7 @@
             out_specs=pl.BlockSpec((width, tile), lambda i, block: (0, i)),
         ),
         out_shape=jax.ShapeDtypeStruct((width, rows), bf16),
-        compiler_params=pltpu.CompilerParams(vmem_limit_bytes=60 * 1024 * 1024),
+        compiler_params=pltpu.CompilerParams(vmem_limit_bytes=48 * 1024 * 1024),
         cost_estimate=SMALL,
     )(block, x)
 
@@ -268,7 +313,7 @@
             out_specs=[half, half],
         ),
         out_shape=[out, out],
-        compiler_params=pltpu.CompilerParams(vmem_limit_bytes=60 * 1024 * 1024),
+        compiler_params=pltpu.CompilerParams(vmem_limit_bytes=32 * 1024 * 1024),
         cost_estimate=SMALL,
     )(core, w)
 
@@ -311,7 +356,7 @@
             out_specs=[out_spec, out_spec],
         ),
         out_shape=[out, out],
-        compiler_params=pltpu.CompilerParams(vmem_limit_bytes=60 * 1024 * 1024),
+        compiler_params=pltpu.CompilerParams(vmem_limit_bytes=32 * 1024 * 1024),
         cost_estimate=SMALL,
     )(place, mine, got, mine, got)
 
@@ -342,7 +387,7 @@
         + ([] if add is None else [out]),
         out_specs=out,
         out_shape=jax.ShapeDtypeStruct((m, n), dtype),
-        compiler_params=pltpu.CompilerParams(vmem_limit_bytes=60 * 1024 * 1024),
+        compiler_params=pltpu.CompilerParams(vmem_limit_bytes=48 * 1024 * 1024),
         cost_estimate=SMALL,
     )(*((a, b) if add is None else (a, b, add)))
 
@@ -370,7 +415,7 @@
             out_specs=pl.BlockSpec((1, 1, 1, rows, 2 * half), lambda p, y, s, bits: (p, y, s, 0, 0)),
         ),
         out_shape=jax.ShapeDtypeStruct((pre, y_size, s_size, rows, 2 * half), bf16),
-        compiler_params=pltpu.CompilerParams(vmem_limit_bytes=60 * 1024 * 1024),
+        compiler_params=pltpu.CompilerParams(vmem_limit_bytes=48 * 1024 * 1024),
         cost_estimate=SMALL,
     )(bits, parts[0], got[0], parts[1], got[1])
 
@@ -391,7 +436,7 @@
         in_specs=[spec, spec],
         out_specs=pl.BlockSpec((2 * width, rows // n), lambda i: (0, i)),
         out_shape=jax.ShapeDtypeStruct((2 * width, rows), bf16),
-        compiler_params=pltpu.CompilerParams(vmem_limit_bytes=60 * 1024 * 1024),
+        compiler_params=pltpu.CompilerParams(vmem_limit_bytes=48 * 1024 * 1024),
         cost_estimate=SMALL,
     )(a, b)
 
@@ -419,7 +464,7 @@
             out_specs=[out_spec, out_spec],
         ),
         out_shape=[out, out],
-        compiler_params=pltpu.CompilerParams(vmem_limit_bytes=60 * 1024 * 1024),
+        compiler_params=pltpu.CompilerParams(vmem_limit_bytes=48 * 1024 * 1024),
         cost_estimate=SMALL,
     )(bit, kept, got, kept, got)
 
@@ -458,7 +503,7 @@
         ),
         out_shape=[out] * 3,
         input_output_aliases=aliases,
-        compiler_params=pltpu.CompilerParams(vmem_limit_bytes=60 * 1024 * 1024),
+        compiler_params=pltpu.CompilerParams(vmem_limit_bytes=48 * 1024 * 1024),
         cost_estimate=SMALL,
     )(core, w, m, v, *grads, *extra)
 
@@ -507,7 +552,7 @@
             jax.ShapeDtypeStruct((heads, hd, t), bf16),
             jax.ShapeDtypeStruct((seqs, heads, 2, seq), f32),
         ],
-        compiler_params=pltpu.CompilerParams(vmem_limit_bytes=60 * 1024 * 1024),
+        compiler_params=pltpu.CompilerParams(vmem_limit_bytes=32 * 1024 * 1024),
         cost_estimate=SMALL,
     )(kept, got, bias, table)
 
@@ -550,7 +595,7 @@
         ],
         out_specs=big,
         out_shape=jax.ShapeDtypeStruct((3, heads, hd, t), bf16),
-        compiler_params=pltpu.CompilerParams(vmem_limit_bytes=60 * 1024 * 1024),
+        compiler_params=pltpu.CompilerParams(vmem_limit_bytes=32 * 1024 * 1024),
         cost_estimate=SMALL,
     )(qkv, dout, stats, table)
 
@@ -814,19 +859,10 @@
     gains = do(lambda a, b: a + b, *gains)
     while gain_steps:
         gains = do(lambda a, b: a + b, *gain_step(gains))
-    gains = do(lambda g: g.reshape(4, ffb, 1), gains)
+    gains = do(lambda g: g.reshape(4, ffb).T, gains)
     flying = scatter_rest(flying)
 
-    def gated(ga, gb, ua, ub, grad_act, gains):
-        gate = ga.astype(f32) + gb.astype(f32)
-        up = ua.astype(f32) + ub.astype(f32)
-        sig = jax.nn.sigmoid(gate)
-        silu = gate * sig
-        ggate = (grad_act * up * sig * (1.0 + gate * (1.0 - sig))).astype(bf16)
-        gup = (grad_act * silu).astype(bf16)
-        return ggate, gup, (silu * up).astype(bf16), gate, up
-
-    ggate, gup, act, gate, up = do(gated, *flying[0], *flying[1], grad_act, gains)
+    gate0, gate1, up0, up1, act, sums = do(gated, *flying[0], *flying[1], grad_act, gains)
 
     def parts_of(count, want):
         return max(n for n in range(1, want + 1) if count % (16 * n) == 0)
@@ -896,20 +932,13 @@
     def quarter_heads(x):
         return [x[:, h][None, None] for h in halves]
 
-    n, start, finish, gate_all = gather_steps(quarter_heads(ggate), 1)
+    n, start, finish, gate_all = gather_steps([gate0[None, None], gate1[None, None]], 1)
     start(0)
     g_down = do(lambda a, c: mm(a, c, PLAIN, bf16, tn=512), act, cot_all)
     for k, (at_row, count) in enumerate(down_rows):
         reps.push(("down", k), g_down[at_row : at_row + count])
     ticks(1)
 
-    def norm_sums2(ggate, gup, gate, up, gains):
-        a, b = ggate.astype(f32), gup.astype(f32)
-        e = jnp.sum(a * gains[0] + b * gains[2], axis=0, keepdims=True)
-        ez = jnp.sum(a * (gate - gains[1]) + b * (up - gains[3]), axis=0, keepdims=True)
-        return join(e, ez)
-
-    sums = do(norm_sums2, ggate, gup, gate, up, gains)
     steps2 = at.steps(False) + [("core", 1)]
 
     def sum_send(sums, axis, step):
@@ -926,7 +955,7 @@
         sums_got = sum_send(sums, *tiny.pop(0))
         start(i, sums)
         ticks(1)
-    n, start_up, finish_up, up_all = gather_steps(quarter_heads(gup), 1)
+    n, start_up, finish_up, up_all = gather_steps([up0[None, None], up1[None, None]], 1)
     ggate_all = gate_all().reshape(Y * S * ffb, T)
     sums = do(lambda a, b: a + b, sums, sums_got)
     start_up(0, sums)
@@ -941,7 +970,6 @@
             ticks(1)
             part_gate = do(lambda w, g: mm(w, g, PLAIN, f32, tn=256), wg, ggate_all)
             out_part = do(lambda w, a: mm(w, a, FIRST, bf16, tm=512), wd_own, act)
-            update(1)
         if i < n - 1:
             finish_up()
     gup_all = up_all().reshape(Y * S * ffb, T)
@@ -966,6 +994,7 @@
     for i in range(1, n):
         start(i)
         if i == 1:
+            update(1)
             ticks(1)
         if i < n - 1:
             finish()
@@ -987,6 +1016,7 @@
         gbr,
     )
     reps.push("out", g_out)
+    update(1)
     ticks(1)
     finish()
     for i in range(1, n):
@@ -998,6 +1028,7 @@
         if i < n - 1:
             finish()
     gqkv = gqkv_done().reshape(3, Y * S * blk, T)
+    out_sum = lax.psum_scatter(do(lambda p: p, out_part), plane, scatter_dimension=0, tiled=True)
     for third in (2, 1, 0):
         g = do(lambda x, g: dot(x, g, LAST).astype(bf16), xn1, gqkv[third])
         reps.push(third, g)
@@ -1005,11 +1036,6 @@
             ticks(1)
     part = do(lambda w, g: dot(w, g, PLAIN), wq, gqkv.reshape(3 * Y * S * blk, T))
     part_theirs = at.core(part[blk:])
-    out_sum = lax.psum_scatter(out_part, plane, scatter_dimension=0, tiled=True)
-    reps.depth = 2
-    ticks(1)
-    update(1)
-    ticks(1)
 
     def first_back(a, b, x, mean, inv, gain, gxn2, z2, gqkv0, gqkv1):
         gxn1 = a + b
@@ -1035,8 +1061,9 @@
         sums = sum_step(sums, axis, step)
     ticks(1)
     input_grad = do(
-        lambda h, grad, z, scale, gain, sums: h
-        + scale * (grad * gain - sums[0:1] / width - z * (sums[1:2] / width)),
+        lambda h, grad, z, scale, gain, sums: (
+            h + scale * (grad * gain - sums[0:1] / width - z * (sums[1:2] / width))
+        ).astype(bf16),
         grad_hidden,
         gxn1,
         z1,
@@ -1050,8 +1077,7 @@
         got = lax.all_to_all(split, plane, split_axis=0, concat_axis=0, tiled=True)
         return do(lambda g: g.reshape(width, rows).T, got)
 
-    input_rows = to_rows(input_grad)
-    ticks(1)
+    input_rows = to_rows(input_grad).astype(f32)
     update(1)
     ticks(1)
     n_rep = lax.axis_size("rep")
@@ -1060,25 +1086,23 @@
         other = lax.ppermute(small, "rep", [(i, i ^ step) for i in range(n_rep)])
         small = do(lambda a, b: a + b, small, other)
         step *= 2
+    sent = do(lambda s: jnp.broadcast_to(s.reshape(1, 7, blk), (nb, 7, blk)), small)
+    small_all = lax.all_to_all(sent, plane, split_axis=0, concat_axis=0, tiled=True)
+
+    def norm_update(every, *a):
+        return adam_update(*a, every.transpose(1, 0, 2).reshape(7, width), 0.3, 0.0)
+
+    mn, vn, wn = do(norm_update, small_all, norm_params, m_norm, v_norm)
     update(1)
     ticks(1)
-    sent = do(lambda s: jnp.broadcast_to(s.reshape(1, 7, blk), (nb, 7, blk)), small)
-    small_all = lax.all_to_all(sent, plane, split_axis=0, concat_axis=0, tiled=True)
-
+    update(2)
+    ticks(1)
+    update(1)
     out_cols = do(lambda h, a: (h + a.astype(f32)).astype(bf16), hidden, out_sum)
     block_output = to_rows(out_cols)
-    ticks(1)
-    update(1)
-    ticks(1)
-    update(1)
-
-    def norm_update(every, *a):
-        return adam_update(*a, every.transpose(1, 0, 2).reshape(7, width), 0.3, 0.0)
-
-    mn, vn, wn = do(norm_update, small_all, norm_params, m_norm, v_norm)
     while reps.busy():
         reps.tick()
-        update(1)
+        update(2)
     update(len(jobs))
     return (
         (block_output.reshape(tokens.shape), input_rows.reshape(tokens.shape))

time: 874 us -> 848 us (0.970)
  Pallas kernels: 277 us -> 196 us
  waiting for transfers between devices: 192 us -> 263 us
  local copies, waits for them, and re-layouts: 60.8 us -> 99.1 us
  other arithmetic: 112 us -> 79.1 us
  starting transfers between devices: 150 us -> 123 us
  blocking collectives: 0 us -> 11.7 us
    unnamed x166 -> x275, local copies, waits for them, and re-layouts: 16.4 us -> 55.4 us
    ppermute x7 -> x6, waiting for transfers between devices: 39.1 us -> 63.1 us  [tick(): slot['in_got'] = lax.ppermute(out['new'], 'rep', [(0, 1), (3, 2)])]
    ppermute x3 -> x4, waiting for transfers between devices: 5.55 us -> 27.5 us  [tick(): got = lax.ppermute(out['total'], 'rep', [(0, 1), (1, 0), (2, 3), (3, 2)])]
    pallas_call x6, Pallas kernels: 25.4 us -> 6.96 us  [arrange(): pl.pallas_call(arrange_kernel, grid_spec=pltpu.PrefetchScalarGridSpec(num...]
    ppermute x2, waiting for transfers between devices: 4.83 us -> 22.1 us  [body(): other = lax.ppermute(small, 'rep', [(i, i ^ step) for i in range(n_rep)])]
    pallas_call x3, Pallas kernels: 22.7 us -> 7.3 us  [stack_turned(): pl.pallas_call(stack_turned_kernel, grid=(n,), in_specs=[spec, spec], out...]
    convert_element_type x17 -> x16, other arithmetic: 39.9 us -> 24.9 us  [add(): lax.reduce_precision(a.astype(f32) + b.astype(f32), 8, 7).astype(bf16)]
    pallas_call x8, Pallas kernels: 49.2 us -> 35.9 us  [mm(): pl.pallas_call(functools.partial(product_kernel, dims), grid=(m // tm, n...]
  transfers between devices with their start and end apart: 90 -> 88, of which waited for: 29 -> 38; matrix products, arithmetic and copies ran while one was open for 22% -> 17% of each run, Pallas kernels for 29% -> 22%
where the time goes in v14:
time: 848 us; the launch traced here: 836 us
  waiting for transfers between devices  263 us (31%)
  Pallas kernels  196 us (23%)
  starting transfers between devices  123 us (15%)
  local copies, waits for them, and re-layouts  99.1 us (12%)
  other arithmetic  79.1 us (9%)
  matrix products  46.4 us (5%)
  between operations  16.6 us (2%)
  blocking collectives  11.7 us (1%)
    ppermute x18, waiting for transfers between devices, along(): return lax.ppermute(x, 'shard', [(i, i ^ step) for i in range(self.s_size)])  86.5 us
    pallas_call x9, Pallas kernels, adam_part(): pl.pallas_call(functools.partial(adam_kernel, rate, two), grid_spec=pltpu...  68 us
    ppermute x6, waiting for transfers between devices, tick(): slot['in_got'] = lax.ppermute(out['new'], 'rep', [(0, 1), (3, 2)])  63.1 us
    unnamed x275, local copies, waits for them, and re-layouts  55.4 us
    dot_general x22, matrix products, dot(): return lax.dot_general(a, b, dims, preferred_element_type=f32)  46.4 us
    ppermute x6, starting transfers between devices, tick(): slot['in_got'] = lax.ppermute(out['new'], 'rep', [(0, 1), (3, 2)])  39.2 us
    pallas_call x8, Pallas kernels, mm(): pl.pallas_call(functools.partial(product_kernel, dims), grid=(m // tm, n...  35.9 us
    ppermute x4, waiting for transfers between devices, tick(): got = lax.ppermute(out['total'], 'rep', [(0, 1), (1, 0), (2, 3), (3, 2)])  27.5 us
  transfers between devices with their start and end apart: 88, of which 38 were waited for; matrix products, arithmetic and copies ran while one was open for 17% of the time, Pallas kernels for 22%

profile of v14, /device:TPU:0, one launch (start us, length us, event | category | flops | bytes accessed | tf_op | source)
XLA Modules:
  0.0 835.6 jit_solution(17743981270972924284)
XLA Ops:
  20.3 4.8 all-to-all-start
  56.5 4.3 copy-done
  73.7 9.5 %collective-permute-done.3.b_ref.d_ref = bf16[1536,512]{1,0:T(8,128)(2,1)} collective-permute-done((bf16[1536,512]{1,0:T(8,128)(2,1)}, bf16[1536,512]{1,0:T(8,128)(2,1)}, u32[]{:S(2)}, u32[]{:S(2)}) %collective-permute-start.3) | collective-permute-done | bytes 1572896 | tf_op jit(solution)/shard_map/ppermute | solution.py:62
  97.7 10.5 %collective-permute-done.4 = bf16[768,512]{1,0:T(8,128)(2,1)} collective-permute-done((bf16[768,512]{1,0:T(8,128)(2,1)}, bf16[768,512]{1,0:T(8,128)(2,1)}, u32[]{:S(2)}, u32[]{:S(2)}) %collective-permute-start.4) | collective-permute-done | bytes 786464 | tf_op jit(solution)/shard_map/ppermute | solution.py:61
  111.0 5.1 shard_map.316
  120.4 5.1 shard_map.317
  155.8 5.0 pad_maximum_fusion.3
  167.9 5.9 collective-permute-done.14
  200.8 5.1 convolution_convert_fusion.1.a_ref.c_ref
  222.0 5.6 shard_map.325.grad_ref
  235.0 20.3 %collective-permute-done.20 = f32[4,2,1,704]{3,0,2,1:T(4,128)S(1)} collective-permute-done((f32[4,2,1,704]{3,0,2,1:T(4,128)S(1)}, f32[4,2,1,704]{3,0,2,1:T(4,128)S(1)}, u32[]{:S(2)}, u32[]{:S(2)}) %collective-permute-start.20) | collective-permute-done | bytes 22560 | tf_op jit(solution)/shard_map/ppermute | solution.py:62
  258.6 8.3 collective-permute-done.21
  277.2 29.9 %collective-permute-done.24.ub_ref = bf16[704,1024]{1,0:T(8,128)(2,1)S(1)} collective-permute-done((bf16[704,1024]{1,0:T(8,128)(2,1)S(1)}, bf16[704,1024]{1,0:T(8,128)(2,1)S(1)}, u32[]{:S(2)}, u32[]{:S(2)}) %collective-permute-start.24) | collective-permute-done | bytes 1441824 | tf_op jit(solution)/shard_map/ppermute | solution.py:62
  309.0 7.5 shard_map.331
  321.1 5.5 shard_map.332
  337.5 21.8 %collective-permute-done.30 = bf16[352,2048]{1,0:T(8,128)(2,1)S(1)} collective-permute-done((bf16[352,2048]{1,0:T(8,128)(2,1)S(1)}, bf16[352,2048]{1,0:T(8,128)(2,1)S(1)}, u32[]{:S(2)}, u32[]{:S(2)}) %collective-permute-start.30) | collective-permute-done | bytes 1441824 | tf_op jit(solution)/shard_map/ppermute | solution.py:197
  371.7 6.1 collective-permute-start.31
  377.8 5.7 shard_map.334
  390.4 18.8 %collective-permute-done.31 = bf16[352,2048]{1,0:T(8,128)(2,1)S(1)} collective-permute-done((bf16[352,2048]{1,0:T(8,128)(2,1)}, bf16[352,2048]{1,0:T(8,128)(2,1)S(1)}, u32[]{:S(2)}, u32[]{:S(2)}) %collective-permute-start.31) | collective-permute-done | bytes 1441824 | tf_op jit(solution)/shard_map/ppermute | solution.py:197
  418.7 7.5 collective-permute-start.40
  426.2 5.8 shard_map.335
  433.3 5.3 shard_map.336
  438.7 6.9 shard_map.337
  445.6 5.2 convolution_add_fusion.2
  451.0 4.3 collective-permute-done.40
  463.3 6.5 collective-permute-start.47
  475.3 5.9 shard_map.338
  484.8 7.6 shard_map.339
  492.5 8.4 %collective-permute-done.47 = bf16[256,2816]{1,0:T(8,128)(2,1)S(1)} collective-permute-done((bf16[256,2816]{1,0:T(8,128)(2,1)S(1)}, bf16[256,2816]{1,0:T(8,128)(2,1)S(1)}, u32[]{:S(2)}, u32[]{:S(2)}) %collective-permute-start.47) | collective-permute-done | bytes 1441824 | tf_op jit(solution)/shard_map/ppermute | solution.py:197
  518.0 5.4 shard_map.341
  523.5 5.5 shard_map.342
  532.5 8.2 shard_map.345
  540.7 4.5 collective-permute-done.53
  552.6 11.8 %collective-permute-done.52 = bf16[1,1,768,512]{3,2,1,0:T(8,128)(2,1)S(1)} collective-permute-done((bf16[1,1,768,512]{3,2,1,0:T(8,128)(2,1)S(1)}, bf16[1,1,768,512]{3,2,1,0:T(8,128)(2,1)S(1)}, u32[]{:S(2)}, u32[]{:S(2)}) %collective-permute-start.52) | collective-permute-done | bytes 786464 | tf_op jit(solution)/shard_map/ppermute | solution.py:62
  567.4 14.4 %collective-permute-done.57 = bf16[256,2816]{1,0:T(8,128)(2,1)S(1)} collective-permute-done((bf16[256,2816]{1,0:T(8,128)(2,1)S(1)}, bf16[256,2816]{1,0:T(8,128)(2,1)S(1)}, u32[]{:S(2)}, u32[]{:S(2)}) %collective-permute-start.57) | collective-permute-done | bytes 1441824 | tf_op jit(solution)/shard_map/ppermute | solution.py:192
  581.8 6.0 collective-permute-start.60
  590.7 13.1 %shard_map.346 = (f32[256,11264]{1,0:T(8,128)}, f32[256,11264]{1,0:T(8,128)}, f32[256,11264]{1,0:T(8,128)}) custom-call(s32[1]{0:T(128)} %bitcast.8.core_ref, f32[256,11264]{1,0:T(8,128)} %w_ref.9, f32[256,11264]{1,0:T(8,128)} %m_ref.3, f32[256,11264]{1,0:T(8,128)} %v_ref.3, bf16[256,2816]{1,0:T(8,128)(2,1)S(1)} %broadcast_select_fusion.3.refs_0_, ...), custom_call_target="tpu_custom_call" | custom-call | flops 1024 | bytes 1024 | tf_op jit(solution)/shard_map/pallas_call | solution.py:496
  603.8 9.1 %shard_map.347 = bf16[3,2,2,256,1024]{4,3,2,1,0:T(8,128)(2,1)} custom-call(s32[4]{0:T(128)S(1)} %pad_add_fusion.1.bits_ref, bf16[2,1,768,512]{3,2,1,0:T(8,128)(2,1)S(1)} %pad_maximum_fusion.1.own0_ref, bf16[2,1,768,512]{3,2,1,0:T(8,128)(2,1)S(1)} %collective-permute-done.55.got0_ref, bf16[1,2,768,512]{3,2,1,0:T(8,128)(2,1)S(1)} %pad_maximum_fusion.2.own1_ref, ...), custom_call_target="tpu_custom_call" | custom-call | flops 1024 | bytes 1024 | tf_op jit(solution)/shard_map/pallas_call | solution.py:409
  634.5 9.7 %collective-permute-start.63 = (bf16[512,1024]{1,0:T(8,128)(2,1)S(1)}, bf16[512,1024]{1,0:T(8,128)(2,1)S(1)}, u32[]{:S(2)}, u32[]{:S(2)}) collective-permute-start(bf16[512,1024]{1,0:T(8,128)(2,1)S(1)} %convolution_convert_fusion.10), channel_id=1, source_target_pairs={{0,8},{24,16},{1,9},{25,17},{2,10},{26,18},{3,11},{27,19},{4,12},{... | collective-permute-start | bytes 3145736 | tf_op jit(solution)/shard_map/ppermute | solution.py:197
  656.8 9.8 %collective-permute-done.63 = bf16[512,1024]{1,0:T(8,128)(2,1)S(1)} collective-permute-done((bf16[512,1024]{1,0:T(8,128)(2,1)S(1)}, bf16[512,1024]{1,0:T(8,128)(2,1)S(1)}, u32[]{:S(2)}, u32[]{:S(2)}) %collective-permute-start.63) | collective-permute-done | bytes 1048608 | tf_op jit(solution)/shard_map/ppermute | solution.py:197
  678.1 13.8 %shard_map.348 = (f32[256,11264]{1,0:T(8,128)}, f32[256,11264]{1,0:T(8,128)}, f32[256,11264]{1,0:T(8,128)}) custom-call(s32[1]{0:T(128)} %bitcast.8.core_ref, f32[256,11264]{1,0:T(8,128)} %w_ref.9, f32[256,11264]{1,0:T(8,128)} %m_ref.3, f32[256,11264]{1,0:T(8,128)} %v_ref.3, ...), custom_call_target="tpu_custom_call", output_to_operand_aliasing={{0}: (6, {}), {1}: (7, {}), {2}: (8, {})} | custom-call | flops 1024 | bytes 1024 | tf_op jit(solution)/shard_map/pallas_call | solution.py:496
  691.8 8.6 %collective-permute-done.70 = bf16[512,1024]{1,0:T(8,128)(2,1)} collective-permute-done((bf16[512,1024]{1,0:T(8,128)(2,1)}, bf16[512,1024]{1,0:T(8,128)(2,1)}, u32[]{:S(2)}, u32[]{:S(2)}) %collective-permute-start.70) | collective-permute-done | bytes 1048608 | tf_op jit(solution)/shard_map/ppermute | solution.py:192
  710.3 21.9 %collective-permute-done.75 = f32[7,256]{1,0:T(8,128)S(1)} collective-permute-done((f32[7,256]{1,0:T(8,128)S(1)}, f32[7,256]{1,0:T(8,128)S(1)}, u32[]{:S(2)}, u32[]{:S(2)}) %collective-permute-start.75) | collective-permute-done | bytes 7200 | tf_op jit(solution)/shard_map/ppermute | solution.py:1086
  761.8 6.2 shard_map.351
  768.1 15.8 %collective-permute-done.77 = bf16[512,1024]{1,0:T(8,128)(2,1)S(1)} collective-permute-done((bf16[512,1024]{1,0:T(8,128)(2,1)S(1)}, bf16[512,1024]{1,0:T(8,128)(2,1)S(1)}, u32[]{:S(2)}, u32[]{:S(2)}) %collective-permute-start.77) | collective-permute-done | bytes 1048608 | tf_op jit(solution)/shard_map/ppermute | solution.py:200
  789.7 11.7 %all_to_all.20 = bf16[8,256,128]{2,1,0:T(8,128)(2,1)S(1)} all-to-all(bf16[8,256,128]{2,1,0:T(8,128)(2,1)S(1)} %bitcast.196), channel_id=1, replica_groups=mesh['rep'=4,'ctx'=4,'shard'=2] {'ctx','shard'}, dimensions={0} | all-to-all | bytes 1048576 | tf_op jit(solution)/shard_map/all_to_all | solution.py:1077
  802.4 6.2 shard_map.352
  820.2 6.2 shard_map.353
  (646 shorter events, 383.0 us)
Async XLA Ops:
  25.2 195.0 %all-gather.2.cloned.1.call-start = ((), (), s32[]{:S(2)}) async-start(), calls=%async_computation.5 | async-start | bytes 4718592 | tf_op jit(solution)/shard_map/all_gather | solution.py:676
  46.5 36.8 %collective-permute-start.3 = (bf16[1536,512]{1,0:T(8,128)(2,1)}, bf16[1536,512]{1,0:T(8,128)(2,1)}, u32[]{:S(2)}, u32[]{:S(2)}) collective-permute-start(bf16[1536,512]{1,0:T(8,128)(2,1)} %convolution_convert_fusion.7), channel_id=1, source_target_pairs={{0,1},{1,0},{2,3},{3,2},{4,5},{5,4},{6,7},{7,6},{8,9},{9,8},{10,11... | collective-permute-start | bytes 4718600 | tf_op jit(solution)/shard_map/ppermute | solution.py:62
  49.6 40.1 %collective-permute-start.5 = (bf16[1536,512]{1,0:T(8,128)(2,1)}, bf16[1536,512]{1,0:T(8,128)(2,1)}, u32[]{:S(2)}, u32[]{:S(2)}) collective-permute-start(bf16[1536,512]{1,0:T(8,128)(2,1)} %convolution_convert_fusion.6), channel_id=1, source_target_pairs={{0,4},{2,6},{4,0},{6,2},{1,5},{3,7},{5,1},{7,3},{8,12},{10,14},{12... | collective-permute-start | bytes 4718600 | tf_op jit(solution)/shard_map/ppermute | solution.py:61
  95.5 22.1 %collective-permute-start.7 = (bf16[768,512]{1,0:T(8,128)(2,1)}, bf16[768,512]{1,0:T(8,128)(2,1)}, u32[]{:S(2)}, u32[]{:S(2)}) collective-permute-start(bf16[768,512]{1,0:T(8,128)(2,1)} %get-tuple-element.484), channel_id=1, source_target_pairs={{0,1},{1,0},{2,3},{3,2},{4,5},{5,4},{6,7},{7,6},{8,9},{9,8},{10,11... | collective-permute-start | bytes 2359304 | tf_op jit(solution)/shard_map/ppermute | solution.py:62
  127.6 684.8 %reduce-scatter.2.cloned.1.call-start = ((), (), s32[]{:S(2)}) async-start(), calls=%async_computation.6 | async-start | bytes 4718592 | tf_op jit(solution)/shard_map/reduce_scatter | solution.py:1031
  132.7 28.0 %collective-permute-start.9 = (bf16[512,512]{1,0:T(8,128)(2,1)}, bf16[512,512]{1,0:T(8,128)(2,1)}, u32[]{:S(2)}, u32[]{:S(2)}) collective-permute-start(bf16[512,512]{1,0:T(8,128)(2,1)} %convolution_convert_fusion.14), channel_id=1, source_target_pairs={{0,1},{1,0},{2,3},{3,2},{4,5},{5,4},{6,7},{7,6},{8,9},{9,8},{10,11... | collective-permute-start | bytes 1572872 | tf_op jit(solution)/shard_map/ppermute | solution.py:62
  134.9 27.9 %collective-permute-start.13 = (bf16[512,512]{1,0:T(8,128)(2,1)}, bf16[512,512]{1,0:T(8,128)(2,1)}, u32[]{:S(2)}, u32[]{:S(2)}) collective-permute-start(bf16[512,512]{1,0:T(8,128)(2,1)} %convolution_convert_fusion.13), channel_id=1, source_target_pairs={{0,4},{2,6},{4,0},{6,2},{1,5},{3,7},{5,1},{7,3},{8,12},{10,14},{12... | collective-permute-start | bytes 1572872 | tf_op jit(solution)/shard_map/ppermute | solution.py:61
  190.0 77.6 %collective-permute-start.19 = (bf16[1408,1024]{1,0:T(8,128)(2,1)}, bf16[1408,1024]{1,0:T(8,128)(2,1)}, u32[]{:S(2)}, u32[]{:S(2)}) collective-permute-start(bf16[1408,1024]{1,0:T(8,128)(2,1)} %convolution_convert_fusion.3), channel_id=1, source_target_pairs={{0,1},{1,0},{2,3},{3,2},{4,5},{5,4},{6,7},{7,6},{8,9},{9,8},{10,11... | collective-permute-start | bytes 8650760 | tf_op jit(solution)/shard_map/ppermute | solution.py:62
  194.3 76.3 %collective-permute-start.23 = (bf16[1408,1024]{1,0:T(8,128)(2,1)}, bf16[1408,1024]{1,0:T(8,128)(2,1)}, u32[]{:S(2)}, u32[]{:S(2)}) collective-permute-start(bf16[1408,1024]{1,0:T(8,128)(2,1)} %convolution_convert_fusion.2), channel_id=1, source_target_pairs={{0,4},{2,6},{4,0},{6,2},{1,5},{3,7},{5,1},{7,3},{8,12},{10,14},{12... | collective-permute-start | bytes 8650760 | tf_op jit(solution)/shard_map/ppermute | solution.py:61
  199.3 56.0 %collective-permute-start.20 = (f32[4,2,1,704]{3,0,2,1:T(4,128)S(1)}, f32[4,2,1,704]{3,0,2,1:T(4,128)S(1)}, u32[]{:S(2)}, u32[]{:S(2)}) collective-permute-start(f32[4,2,1,704]{3,0,2,1:T(4,128)S(1)} %copy.126), channel_id=1, source_target_pairs={{0,1},{1,0},{2,3},{3,2},{4,5},{5,4},{6,7},{7,6},{8,9},{9,8},{10,11... | collective-permute-start | bytes 67592 | tf_op jit(solution)/shard_map/ppermute | solution.py:62
  275.1 32.0 %collective-permute-start.24 = (bf16[704,1024]{1,0:T(8,128)(2,1)S(1)}, bf16[704,1024]{1,0:T(8,128)(2,1)S(1)}, u32[]{:S(2)}, u32[]{:S(2)}) collective-permute-start(bf16[704,1024]{1,0:T(8,128)(2,1)S(1)} %get-tuple-element.580), channel_id=1, source_target_pairs={{0,1},{1,0},{2,3},{3,2},{4,5},{5,4},{6,7},{7,6},{8,9},{9,8},{10,11... | collective-permute-start | bytes 4325384 | tf_op jit(solution)/shard_map/ppermute | solution.py:62
  276.1 31.7 %collective-permute-start.22 = (bf16[704,1024]{1,0:T(8,128)(2,1)S(1)}, bf16[704,1024]{1,0:T(8,128)(2,1)S(1)}, u32[]{:S(2)}, u32[]{:S(2)}) collective-permute-start(bf16[704,1024]{1,0:T(8,128)(2,1)S(1)} %get-tuple-element.576), channel_id=1, source_target_pairs={{0,4},{2,6},{4,0},{6,2},{1,5},{3,7},{5,1},{7,3},{8,12},{10,14},{12... | collective-permute-start | bytes 4325384 | tf_op jit(solution)/shard_map/ppermute | solution.py:61
  328.1 31.1 %collective-permute-start.30 = (bf16[352,2048]{1,0:T(8,128)(2,1)S(1)}, bf16[352,2048]{1,0:T(8,128)(2,1)S(1)}, u32[]{:S(2)}, u32[]{:S(2)}) collective-permute-start(bf16[352,2048]{1,0:T(8,128)(2,1)S(1)} %get-tuple-element.602), channel_id=1, source_target_pairs={{0,8},{24,16},{1,9},{25,17},{2,10},{26,18},{3,11},{27,19},{4,12},{... | collective-permute-start | bytes 4325384 | tf_op jit(solution)/shard_map/ppermute | solution.py:197
  334.3 29.7 %collective-permute-start.28 = (bf16[2,1,704,512]{3,2,1,0:T(8,128)(2,1)S(1)}, bf16[2,1,704,512]{3,2,1,0:T(8,128)(2,1)S(1)}, u32[]{:S(2)}, u32[]{:S(2)}) collective-permute-start(bf16[2,1,704,512]{3,2,1,0:T(8,128)(2,1)S(1)} %pad_maximum_fusion.4.own0_ref), channel_id=1, source_target_pairs={{0,1},{1,0},{2,3},{3,2},{4,5},{5,4},{6,7},{7,6},{8,9},{9,8},{10,11... | collective-permute-start | bytes 4325384 | tf_op jit(solution)/shard_map/ppermute | solution.py:62
  335.4 29.4 %collective-permute-start.29 = (bf16[1,2,704,512]{3,2,1,0:T(8,128)(2,1)S(1)}, bf16[1,2,704,512]{3,2,1,0:T(8,128)(2,1)S(1)}, u32[]{:S(2)}, u32[]{:S(2)}) collective-permute-start(bf16[1,2,704,512]{3,2,1,0:T(8,128)(2,1)S(1)} %pad_maximum_fusion.5.own1_ref), channel_id=1, source_target_pairs={{0,4},{2,6},{4,0},{6,2},{1,5},{3,7},{5,1},{7,3},{8,12},{10,14},{12... | collective-permute-start | bytes 4325384 | tf_op jit(solution)/shard_map/ppermute | solution.py:61
  336.9 31.4 %collective-permute-start.32 = (f32[2,1024]{1,0:T(2,128)S(1)}, f32[2,1024]{1,0:T(2,128)S(1)}, u32[]{:S(2)}, u32[]{:S(2)}) collective-permute-start(f32[2,1024]{1,0:T(2,128)S(1)} %add.386), channel_id=1, source_target_pairs={{0,4},{2,6},{4,0},{6,2},{1,5},{3,7},{5,1},{7,3},{8,12},{10,14},{12... | collective-permute-start | bytes 24584 | tf_op jit(solution)/shard_map/ppermute | solution.py:61
  370.9 19.5 %collective-permute-start.34 = (bf16[352,2048]{1,0:T(8,128)(2,1)}, bf16[352,2048]{1,0:T(8,128)(2,1)S(1)}, u32[]{:S(2)}, u32[]{:S(2)}) collective-permute-start(bf16[352,2048]{1,0:T(8,128)(2,1)} %reduce-precision_convert_fusion.11), channel_id=1, source_target_pairs={{8,16},{16,8},{9,17},{17,9},{10,18},{18,10},{11,19},{19,11},{12,20... | collective-permute-start | bytes 4325384 | tf_op jit(solution)/shard_map/ppermute | solution.py:203
  371.7 37.6 %collective-permute-start.31 = (bf16[352,2048]{1,0:T(8,128)(2,1)}, bf16[352,2048]{1,0:T(8,128)(2,1)S(1)}, u32[]{:S(2)}, u32[]{:S(2)}) collective-permute-start(bf16[352,2048]{1,0:T(8,128)(2,1)} %get-tuple-element.621), channel_id=1, source_target_pairs={{0,8},{24,16},{1,9},{25,17},{2,10},{26,18},{3,11},{27,19},{4,12},{... | collective-permute-start | bytes 4325384 | tf_op jit(solution)/shard_map/ppermute | solution.py:197
  385.2 53.5 %collective-permute-start.38 = (bf16[1,2,704,512]{3,2,1,0:T(8,128)(2,1)S(1)}, bf16[1,2,704,512]{3,2,1,0:T(8,128)(2,1)}, u32[]{:S(2)}, u32[]{:S(2)}) collective-permute-start(bf16[1,2,704,512]{3,2,1,0:T(8,128)(2,1)S(1)} %pad_maximum_fusion.7.own1_ref), channel_id=1, source_target_pairs={{0,4},{2,6},{4,0},{6,2},{1,5},{3,7},{5,1},{7,3},{8,12},{10,14},{12... | collective-permute-start | bytes 4325384 | tf_op jit(solution)/shard_map/ppermute | solution.py:61
  387.5 51.2 %collective-permute-start.37 = (bf16[2,1,704,512]{3,2,1,0:T(8,128)(2,1)}, bf16[2,1,704,512]{3,2,1,0:T(8,128)(2,1)}, u32[]{:S(2)}, u32[]{:S(2)}) collective-permute-start(bf16[2,1,704,512]{3,2,1,0:T(8,128)(2,1)} %pad_maximum_fusion.6.own0_ref), channel_id=1, source_target_pairs={{0,1},{1,0},{2,3},{3,2},{4,5},{5,4},{6,7},{7,6},{8,9},{9,8},{10,11... | collective-permute-start | bytes 4325384 | tf_op jit(solution)/shard_map/ppermute | solution.py:62
  412.3 38.7 %collective-permute-start.41 = (bf16[352,2048]{1,0:T(8,128)(2,1)}, bf16[352,2048]{1,0:T(8,128)(2,1)}, u32[]{:S(2)}, u32[]{:S(2)}) collective-permute-start(bf16[352,2048]{1,0:T(8,128)(2,1)} %reduce-precision_convert_fusion.9), channel_id=1, source_target_pairs={{8,0},{16,24},{9,1},{17,25},{10,2},{18,26},{11,3},{19,27},{12,4},{... | collective-permute-start | bytes 4325384 | tf_op jit(solution)/shard_map/ppermute | solution.py:200
  416.9 34.1 %collective-permute-start.42 = (bf16[352,2048]{1,0:T(8,128)(2,1)}, bf16[352,2048]{1,0:T(8,128)(2,1)}, u32[]{:S(2)}, u32[]{:S(2)}) collective-permute-start(bf16[352,2048]{1,0:T(8,128)(2,1)} %reduce-precision_convert_fusion.10), channel_id=1, source_target_pairs={{8,16},{16,8},{9,17},{17,9},{10,18},{18,10},{11,19},{19,11},{12,20... | collective-permute-start | bytes 4325384 | tf_op jit(solution)/shard_map/ppermute | solution.py:203
  418.7 36.6 %collective-permute-start.40 = (bf16[256,2816]{1,0:T(8,128)(2,1)}, bf16[256,2816]{1,0:T(8,128)(2,1)}, u32[]{:S(2)}, u32[]{:S(2)}) collective-permute-start(bf16[256,2816]{1,0:T(8,128)(2,1)} %get-tuple-element.639), channel_id=1, source_target_pairs={{0,8},{24,16},{1,9},{25,17},{2,10},{26,18},{3,11},{27,19},{4,12},{... | collective-permute-start | bytes 4325384 | tf_op jit(solution)/shard_map/ppermute | solution.py:197
  457.7 34.7 %collective-permute-start.48 = (bf16[352,2048]{1,0:T(8,128)(2,1)S(1)}, bf16[352,2048]{1,0:T(8,128)(2,1)S(1)}, u32[]{:S(2)}, u32[]{:S(2)}) collective-permute-start(bf16[352,2048]{1,0:T(8,128)(2,1)S(1)} %reduce-precision_convert_fusion.7), channel_id=1, source_target_pairs={{8,0},{16,24},{9,1},{17,25},{10,2},{18,26},{11,3},{19,27},{12,4},{... | collective-permute-start | bytes 4325384 | tf_op jit(solution)/shard_map/ppermute | solution.py:200
  461.4 31.1 %collective-permute-start.49 = (bf16[256,2816]{1,0:T(8,128)(2,1)S(1)}, bf16[256,2816]{1,0:T(8,128)(2,1)}, u32[]{:S(2)}, u32[]{:S(2)}) collective-permute-start(bf16[256,2816]{1,0:T(8,128)(2,1)S(1)} %reduce-precision_convert_fusion.8), channel_id=1, source_target_pairs={{8,16},{16,8},{9,17},{17,9},{10,18},{18,10},{11,19},{19,11},{12,20... | collective-permute-start | bytes 4325384 | tf_op jit(solution)/shard_map/ppermute | solution.py:203
  463.3 37.6 %collective-permute-start.47 = (bf16[256,2816]{1,0:T(8,128)(2,1)S(1)}, bf16[256,2816]{1,0:T(8,128)(2,1)S(1)}, u32[]{:S(2)}, u32[]{:S(2)}) collective-permute-start(bf16[256,2816]{1,0:T(8,128)(2,1)S(1)} %copy-done.99), channel_id=1, source_target_pairs={{0,8},{24,16},{1,9},{25,17},{2,10},{26,18},{3,11},{27,19},{4,12},{... | collective-permute-start | bytes 4325384 | tf_op jit(solution)/shard_map/ppermute | solution.py:197
  482.5 19.7 %collective-permute-start.45 = (bf16[2,1,256,512]{3,2,1,0:T(8,128)(2,1)S(1)}, bf16[2,1,256,512]{3,2,1,0:T(8,128)(2,1)S(1)}, u32[]{:S(2)}, u32[]{:S(2)}) collective-permute-start(bf16[2,1,256,512]{3,2,1,0:T(8,128)(2,1)S(1)} %pad_maximum_fusion.10.own0_ref), channel_id=1, source_target_pairs={{0,1},{1,0},{2,3},{3,2},{4,5},{5,4},{6,7},{7,6},{8,9},{9,8},{10,11... | collective-permute-start | bytes 1572872 | tf_op jit(solution)/shard_map/ppermute | solution.py:62
  504.4 40.8 %collective-permute-start.54 = (bf16[256,2816]{1,0:T(8,128)(2,1)}, bf16[256,2816]{1,0:T(8,128)(2,1)}, u32[]{:S(2)}, u32[]{:S(2)}) collective-permute-start(bf16[256,2816]{1,0:T(8,128)(2,1)} %reduce-precision_convert_fusion.6), channel_id=1, source_target_pairs={{8,16},{16,8},{9,17},{17,9},{10,18},{18,10},{11,19},{19,11},{12,20... | collective-permute-start | bytes 4325384 | tf_op jit(solution)/shard_map/ppermute | solution.py:203
  510.1 35.0 %collective-permute-start.53 = (bf16[256,2816]{1,0:T(8,128)(2,1)}, bf16[256,2816]{1,0:T(8,128)(2,1)S(1)}, u32[]{:S(2)}, u32[]{:S(2)}) collective-permute-start(bf16[256,2816]{1,0:T(8,128)(2,1)} %fusion), channel_id=1, source_target_pairs={{0,8},{8,0},{16,24},{24,16},{1,9},{9,1},{17,25},{25,17},{2,10},{10... | collective-permute-start | bytes 4325384 | tf_op jit(solution)/shard_map/ppermute | solution.py:192
  548.9 32.8 %collective-permute-start.57 = (bf16[256,2816]{1,0:T(8,128)(2,1)S(1)}, bf16[256,2816]{1,0:T(8,128)(2,1)S(1)}, u32[]{:S(2)}, u32[]{:S(2)}) collective-permute-start(bf16[256,2816]{1,0:T(8,128)(2,1)S(1)} %fusion.1), channel_id=1, source_target_pairs={{0,8},{8,0},{16,24},{24,16},{1,9},{9,1},{17,25},{25,17},{2,10},{10... | collective-permute-start | bytes 4325384 | tf_op jit(solution)/shard_map/ppermute | solution.py:192
  551.1 30.6 %collective-permute-start.58 = (bf16[256,2816]{1,0:T(8,128)(2,1)S(1)}, bf16[256,2816]{1,0:T(8,128)(2,1)S(1)}, u32[]{:S(2)}, u32[]{:S(2)}) collective-permute-start(bf16[256,2816]{1,0:T(8,128)(2,1)S(1)} %reduce-precision_convert_fusion.4), channel_id=1, source_target_pairs={{8,16},{16,8},{9,17},{17,9},{10,18},{18,10},{11,19},{19,11},{12,20... | collective-permute-start | bytes 4325384 | tf_op jit(solution)/shard_map/ppermute | solution.py:203
  552.5 37.3 %collective-permute-start.59 = (bf16[256,2816]{1,0:T(8,128)(2,1)S(1)}, bf16[256,2816]{1,0:T(8,128)(2,1)S(1)}, u32[]{:S(2)}, u32[]{:S(2)}) collective-permute-start(bf16[256,2816]{1,0:T(8,128)(2,1)S(1)} %broadcast_select_fusion.2), channel_id=1, source_target_pairs={{0,2},{2,0},{4,6},{6,4},{1,3},{3,1},{5,7},{7,5},{8,10},{10,8},{12,... | collective-permute-start | bytes 4325384 | tf_op jit(solution)/shard_map/ppermute | solution.py:57
  565.6 38.2 %collective-permute-start.56 = (bf16[1,2,768,512]{3,2,1,0:T(8,128)(2,1)S(1)}, bf16[1,2,768,512]{3,2,1,0:T(8,128)(2,1)}, u32[]{:S(2)}, u32[]{:S(2)}) collective-permute-start(bf16[1,2,768,512]{3,2,1,0:T(8,128)(2,1)S(1)} %pad_maximum_fusion.2.own1_ref), channel_id=1, source_target_pairs={{0,4},{2,6},{4,0},{6,2},{1,5},{3,7},{5,1},{7,3},{8,12},{10,14},{12... | collective-permute-start | bytes 4718600 | tf_op jit(solution)/shard_map/ppermute | solution.py:61
  566.5 37.3 %collective-permute-start.55 = (bf16[2,1,768,512]{3,2,1,0:T(8,128)(2,1)S(1)}, bf16[2,1,768,512]{3,2,1,0:T(8,128)(2,1)S(1)}, u32[]{:S(2)}, u32[]{:S(2)}) collective-permute-start(bf16[2,1,768,512]{3,2,1,0:T(8,128)(2,1)S(1)} %pad_maximum_fusion.1.own0_ref), channel_id=1, source_target_pairs={{0,1},{1,0},{2,3},{3,2},{4,5},{5,4},{6,7},{7,6},{8,9},{9,8},{10,11... | collective-permute-start | bytes 4718600 | tf_op jit(solution)/shard_map/ppermute | solution.py:62
  581.8 36.1 %collective-permute-start.60 = (bf16[512,1024]{1,0:T(8,128)(2,1)}, bf16[512,1024]{1,0:T(8,128)(2,1)S(1)}, u32[]{:S(2)}, u32[]{:S(2)}) collective-permute-start(bf16[512,1024]{1,0:T(8,128)(2,1)} %pad_maximum_fusion.8), channel_id=1, source_target_pairs={{0,8},{24,16},{1,9},{25,17},{2,10},{26,18},{3,11},{27,19},{4,12},{... | collective-permute-start | bytes 3145736 | tf_op jit(solution)/shard_map/ppermute | solution.py:197
  588.1 33.4 %collective-permute-start.61 = (bf16[256,2816]{1,0:T(8,128)(2,1)S(1)}, bf16[256,2816]{1,0:T(8,128)(2,1)}, u32[]{:S(2)}, u32[]{:S(2)}) collective-permute-start(bf16[256,2816]{1,0:T(8,128)(2,1)S(1)} %reduce-precision_convert_fusion.1), channel_id=1, source_target_pairs={{8,0},{16,24},{9,1},{17,25},{10,2},{18,26},{11,3},{19,27},{12,4},{... | collective-permute-start | bytes 4325384 | tf_op jit(solution)/shard_map/ppermute | solution.py:200
  589.8 31.7 %collective-permute-start.62 = (bf16[256,2816]{1,0:T(8,128)(2,1)S(1)}, bf16[256,2816]{1,0:T(8,128)(2,1)S(1)}, u32[]{:S(2)}, u32[]{:S(2)}) collective-permute-start(bf16[256,2816]{1,0:T(8,128)(2,1)S(1)} %reduce-precision_convert_fusion.2), channel_id=1, source_target_pairs={{8,16},{16,8},{9,17},{17,9},{10,18},{18,10},{11,19},{19,11},{12,20... | collective-permute-start | bytes 4325384 | tf_op jit(solution)/shard_map/ppermute | solution.py:203
  632.0 38.5 %collective-permute-start.64 = (bf16[256,2816]{1,0:T(8,128)(2,1)S(1)}, bf16[256,2816]{1,0:T(8,128)(2,1)S(1)}, u32[]{:S(2)}, u32[]{:S(2)}) collective-permute-start(bf16[256,2816]{1,0:T(8,128)(2,1)S(1)} %reduce-precision_convert_fusion), channel_id=1, source_target_pairs={{8,0},{16,24},{9,1},{17,25},{10,2},{18,26},{11,3},{19,27},{12,4},{... | collective-permute-start | bytes 4325384 | tf_op jit(solution)/shard_map/ppermute | solution.py:200
  633.8 23.0 %collective-permute-start.65 = (bf16[512,1024]{1,0:T(8,128)(2,1)S(1)}, bf16[512,1024]{1,0:T(8,128)(2,1)S(1)}, u32[]{:S(2)}, u32[]{:S(2)}) collective-permute-start(bf16[512,1024]{1,0:T(8,128)(2,1)S(1)} %reduce-precision_convert_fusion.19), channel_id=1, source_target_pairs={{8,16},{16,8},{9,17},{17,9},{10,18},{18,10},{11,19},{19,11},{12,20... | collective-permute-start | bytes 3145736 | tf_op jit(solution)/shard_map/ppermute | solution.py:203
  634.5 32.1 %collective-permute-start.63 = (bf16[512,1024]{1,0:T(8,128)(2,1)S(1)}, bf16[512,1024]{1,0:T(8,128)(2,1)S(1)}, u32[]{:S(2)}, u32[]{:S(2)}) collective-permute-start(bf16[512,1024]{1,0:T(8,128)(2,1)S(1)} %convolution_convert_fusion.10), channel_id=1, source_target_pairs={{0,8},{24,16},{1,9},{25,17},{2,10},{26,18},{3,11},{27,19},{4,12},{... | collective-permute-start | bytes 3145736 | tf_op jit(solution)/shard_map/ppermute | solution.py:197
  656.3 21.8 %collective-permute-start.72 = (bf16[256,2816]{1,0:T(8,128)(2,1)}, bf16[256,2816]{1,0:T(8,128)(2,1)S(1)}, u32[]{:S(2)}, u32[]{:S(2)}) collective-permute-start(bf16[256,2816]{1,0:T(8,128)(2,1)} %broadcast_select_fusion), channel_id=1, source_target_pairs={{0,2},{2,0},{4,6},{6,4},{1,3},{3,1},{5,7},{7,5},{8,10},{10,8},{12,... | collective-permute-start | bytes 4325384 | tf_op jit(solution)/shard_map/ppermute | solution.py:57
  672.0 19.8 %collective-permute-start.71 = (bf16[512,1024]{1,0:T(8,128)(2,1)}, bf16[512,1024]{1,0:T(8,128)(2,1)}, u32[]{:S(2)}, u32[]{:S(2)}) collective-permute-start(bf16[512,1024]{1,0:T(8,128)(2,1)} %reduce-precision_convert_fusion.17), channel_id=1, source_target_pairs={{8,16},{16,8},{9,17},{17,9},{10,18},{18,10},{11,19},{19,11},{12,20... | collective-permute-start | bytes 3145736 | tf_op jit(solution)/shard_map/ppermute | solution.py:203
  675.4 25.1 %collective-permute-start.70 = (bf16[512,1024]{1,0:T(8,128)(2,1)}, bf16[512,1024]{1,0:T(8,128)(2,1)}, u32[]{:S(2)}, u32[]{:S(2)}) collective-permute-start(bf16[512,1024]{1,0:T(8,128)(2,1)} %fusion.4), channel_id=1, source_target_pairs={{0,8},{8,0},{16,24},{24,16},{1,9},{9,1},{17,25},{25,17},{2,10},{10... | collective-permute-start | bytes 3145736 | tf_op jit(solution)/shard_map/ppermute | solution.py:192
  703.1 48.2 %collective-permute-start.74 = (bf16[512,1024]{1,0:T(8,128)(2,1)}, bf16[512,1024]{1,0:T(8,128)(2,1)}, u32[]{:S(2)}, u32[]{:S(2)}) collective-permute-start(bf16[512,1024]{1,0:T(8,128)(2,1)} %reduce-precision_convert_fusion.15), channel_id=1, source_target_pairs={{8,16},{16,8},{9,17},{17,9},{10,18},{18,10},{11,19},{19,11},{12,20... | collective-permute-start | bytes 3145736 | tf_op jit(solution)/shard_map/ppermute | solution.py:203
  707.9 43.4 %collective-permute-start.73 = (bf16[512,1024]{1,0:T(8,128)(2,1)}, bf16[512,1024]{1,0:T(8,128)(2,1)}, u32[]{:S(2)}, u32[]{:S(2)}) collective-permute-start(bf16[512,1024]{1,0:T(8,128)(2,1)} %fusion.5), channel_id=1, source_target_pairs={{0,8},{8,0},{16,24},{24,16},{1,9},{9,1},{17,25},{25,17},{2,10},{10... | collective-permute-start | bytes 3145736 | tf_op jit(solution)/shard_map/ppermute | solution.py:192
  710.2 22.0 %collective-permute-start.75 = (f32[7,256]{1,0:T(8,128)S(1)}, f32[7,256]{1,0:T(8,128)S(1)}, u32[]{:S(2)}, u32[]{:S(2)}) collective-permute-start(f32[7,256]{1,0:T(8,128)S(1)} %concatenate.111), channel_id=1, source_target_pairs={{0,8},{8,0},{16,24},{24,16},{1,9},{9,1},{17,25},{25,17},{2,10},{10... | collective-permute-start | bytes 21512 | tf_op jit(solution)/shard_map/ppermute | solution.py:1086
  755.6 28.3 %collective-permute-start.77 = (bf16[512,1024]{1,0:T(8,128)(2,1)S(1)}, bf16[512,1024]{1,0:T(8,128)(2,1)S(1)}, u32[]{:S(2)}, u32[]{:S(2)}) collective-permute-start(bf16[512,1024]{1,0:T(8,128)(2,1)S(1)} %reduce-precision_convert_fusion.14), channel_id=1, source_target_pairs={{8,0},{16,24},{9,1},{17,25},{10,2},{18,26},{11,3},{19,27},{12,4},{... | collective-permute-start | bytes 3145736 | tf_op jit(solution)/shard_map/ppermute | solution.py:200
  784.3 26.6 %collective-permute-start.81 = (bf16[512,1024]{1,0:T(8,128)(2,1)S(1)}, bf16[512,1024]{1,0:T(8,128)(2,1)}, u32[]{:S(2)}, u32[]{:S(2)}) collective-permute-start(bf16[512,1024]{1,0:T(8,128)(2,1)S(1)} %reduce-precision_convert_fusion.12), channel_id=1, source_target_pairs={{8,0},{16,24},{9,1},{17,25},{10,2},{18,26},{11,3},{19,27},{12,4},{... | collective-permute-start | bytes 3145736 | tf_op jit(solution)/shard_map/ppermute | solution.py:200
  (176 other events, 1067.1 us)
Sparse Core Ops, SparseCore 0:
  127.7 42.5 all-gather.1
  676.6 49.7 reduce-scatter.1

commit v15 on v14

--- a/solution.py
+++ b/solution.py
@@ -121,13 +121,11 @@
 
 class Order:
     def __init__(self):
-        self.last = None
+        self.token = lax.create_token()
 
     def __call__(self, stage, *args):
-        if self.last is not None:
-            args, self.last = lax.optimization_barrier((args, self.last))
-        out = stage(*args)
-        self.last = jax.tree.leaves(out)[0]
+        args, token = lax.optimization_barrier((args, self.token))
+        out, self.token = lax.optimization_barrier((stage(*args), token))
         return out
 
 

time: 848 us -> 865 us (1.020)
  local copies, waits for them, and re-layouts: 99.1 us -> 84 us
  Pallas kernels: 196 us -> 207 us
  waiting for transfers between devices: 263 us -> 274 us
    ppermute x18, waiting for transfers between devices: 86.5 us -> 42.3 us  [along(): return lax.ppermute(x, 'shard', [(i, i ^ step) for i in range(self.s_size)])]
    ppermute x18, waiting for transfers between devices: 27 us -> 67.1 us  [along(): lax.ppermute(x, 'ctx', [(i, i ^ 2 * step) for i in range(self.ctx_size)])]
    ppermute x6, waiting for transfers between devices: 25.6 us -> 45.3 us  [tick(): slot['out_got'] = lax.ppermute(out['total'], 'rep', [(1, 0), (2, 3)])]
    ppermute x6, waiting for transfers between devices: 63.1 us -> 51 us  [tick(): slot['in_got'] = lax.ppermute(out['new'], 'rep', [(0, 1), (3, 2)])]
    pallas_call x3, Pallas kernels: 7.3 us -> 16.8 us  [stack_turned(): pl.pallas_call(stack_turned_kernel, grid=(n,), in_specs=[spec, spec], out...]
    another operation x4, local copies, waits for them, and re-layouts: 9.52 us -> 0.32 us  [gain_products(): out.append(jnp.stack([p[0] + p[1], p[2] + p[3]]).reshape(2, Y, S, ffb))]
    unnamed x275 -> x262, local copies, waits for them, and re-layouts: 55.4 us -> 53.9 us
  transfers between devices with their start and end apart: 88 -> 88, of which waited for: 38 -> 42; matrix products, arithmetic and copies ran while one was open for 17% -> 16% of each run, Pallas kernels for 22% -> 22%
where the time goes in v15:
time: 865 us; the launch traced here: 852 us
  waiting for transfers between devices  274 us (32%)
  Pallas kernels  207 us (24%)
  starting transfers between devices  120 us (14%)
  other arithmetic  87.1 us (10%)
  local copies, waits for them, and re-layouts  84 us (10%)
  matrix products  51.2 us (6%)
  between operations  16.7 us (2%)
  blocking collectives  11.7 us (1%)
    pallas_call x9, Pallas kernels, adam_part(): pl.pallas_call(functools.partial(adam_kernel, rate, two), grid_spec=pltpu...  67.4 us
    ppermute x18, waiting for transfers between devices, along(): lax.ppermute(x, 'ctx', [(i, i ^ 2 * step) for i in range(self.ctx_size)])  67.1 us
    unnamed x262, local copies, waits for them, and re-layouts  53.9 us
    dot_general x22, matrix products, dot(): return lax.dot_general(a, b, dims, preferred_element_type=f32)  51.2 us
    ppermute x6, waiting for transfers between devices, tick(): slot['in_got'] = lax.ppermute(out['new'], 'rep', [(0, 1), (3, 2)])  51 us
    ppermute x6, waiting for transfers between devices, tick(): slot['out_got'] = lax.ppermute(out['total'], 'rep', [(1, 0), (2, 3)])  45.3 us
    ppermute x18, waiting for transfers between devices, along(): return lax.ppermute(x, 'shard', [(i, i ^ step) for i in range(self.s_size)])  42.3 us
    pallas_call x8, Pallas kernels, mm(): pl.pallas_call(functools.partial(product_kernel, dims), grid=(m // tm, n...  35.6 us
  transfers between devices with their start and end apart: 88, of which 42 were waited for; matrix products, arithmetic and copies ran while one was open for 16% of the time, Pallas kernels for 22%

profile of v15, /device:TPU:0, one launch (start us, length us, event | category | flops | bytes accessed | tf_op | source)
XLA Modules:
  0.0 851.6 jit_solution(6543728094795429533)
XLA Ops:
  74.0 11.7 %collective-permute-done.3.b_ref.d_ref = bf16[1536,512]{1,0:T(8,128)(2,1)} collective-permute-done((bf16[1536,512]{1,0:T(8,128)(2,1)}, bf16[1536,512]{1,0:T(8,128)(2,1)}, u32[]{:S(2)}, u32[]{:S(2)}) %collective-permute-start.3) | collective-permute-done | bytes 1572896 | tf_op jit(solution)/shard_map/ppermute | solution.py:62
  100.1 10.5 %collective-permute-done.4 = bf16[768,512]{1,0:T(8,128)(2,1)} collective-permute-done((bf16[768,512]{1,0:T(8,128)(2,1)}, bf16[768,512]{1,0:T(8,128)(2,1)}, u32[]{:S(2)}, u32[]{:S(2)}) %collective-permute-start.4) | collective-permute-done | bytes 786464 | tf_op jit(solution)/shard_map/ppermute | solution.py:61
  113.4 5.2 shard_map.316
  122.9 5.1 shard_map.317
  160.4 8.0 collective-permute-done.13.b_ref.d_ref
  171.1 7.3 collective-permute-done.12
  203.9 5.0 convolution_convert_fusion.1.a_ref.c_ref
  216.8 6.5 shard_map.323.a_ref
  224.8 6.4 shard_map.324
  234.6 5.6 shard_map.325.grad_ref
  247.6 11.8 %collective-permute-done.20 = f32[4,2,1,704]{3,0,2,1:T(4,128)S(1)} collective-permute-done((f32[4,2,1,704]{3,0,2,1:T(4,128)S(1)}, f32[4,2,1,704]{3,0,2,1:T(4,128)S(1)}, u32[]{:S(2)}, u32[]{:S(2)}) %collective-permute-start.20) | collective-permute-done | bytes 22560 | tf_op jit(solution)/shard_map/ppermute | solution.py:62
  262.0 8.9 %collective-permute-done.21 = f32[4,1,1,704]{0,3,2,1:T(8,128)S(1)} collective-permute-done((f32[4,1,1,704]{0,3,2,1:T(8,128)S(1)}, f32[4,1,1,704]{0,3,2,1:T(8,128)S(1)}, u32[]{:S(2)}, u32[]{:S(2)}) %collective-permute-start.21) | collective-permute-done | bytes 11296 | tf_op jit(solution)/shard_map/ppermute | solution.py:61
  281.0 25.8 %collective-permute-done.22.gb_ref = bf16[704,1024]{1,0:T(8,128)(2,1)S(1)} collective-permute-done((bf16[704,1024]{1,0:T(8,128)(2,1)S(1)}, bf16[704,1024]{1,0:T(8,128)(2,1)S(1)}, u32[]{:S(2)}, u32[]{:S(2)}) %collective-permute-start.22) | collective-permute-done | bytes 1441824 | tf_op jit(solution)/shard_map/ppermute | solution.py:61
  312.6 7.5 shard_map.331
  323.5 5.4 shard_map.332
  341.2 21.7 %collective-permute-done.30 = bf16[352,2048]{1,0:T(8,128)(2,1)S(1)} collective-permute-done((bf16[352,2048]{1,0:T(8,128)(2,1)S(1)}, bf16[352,2048]{1,0:T(8,128)(2,1)S(1)}, u32[]{:S(2)}, u32[]{:S(2)}) %collective-permute-start.30) | collective-permute-done | bytes 1441824 | tf_op jit(solution)/shard_map/ppermute | solution.py:195
  378.9 5.7 shard_map.334
  393.5 16.3 %collective-permute-done.31 = bf16[352,2048]{1,0:T(8,128)(2,1)S(1)} collective-permute-done((bf16[352,2048]{1,0:T(8,128)(2,1)}, bf16[352,2048]{1,0:T(8,128)(2,1)S(1)}, u32[]{:S(2)}, u32[]{:S(2)}) %collective-permute-start.31) | collective-permute-done | bytes 1441824 | tf_op jit(solution)/shard_map/ppermute | solution.py:195
  416.1 6.7 collective-permute-start.40
  425.9 5.8 shard_map.335
  433.1 5.3 shard_map.336
  438.4 6.9 shard_map.337
  445.3 5.2 convolution_add_fusion.2
  452.8 5.3 collective-permute-done.41
  462.8 7.4 collective-permute-start.47
  478.7 5.7 shard_map.338
  486.8 7.6 shard_map.339
  494.5 4.9 collective-permute-done.47
  522.2 5.5 shard_map.341
  527.7 5.4 shard_map.342
  538.1 8.2 shard_map.345
  561.8 23.9 %collective-permute-done.57 = bf16[256,2816]{1,0:T(8,128)(2,1)S(1)} collective-permute-done((bf16[256,2816]{1,0:T(8,128)(2,1)S(1)}, bf16[256,2816]{1,0:T(8,128)(2,1)S(1)}, u32[]{:S(2)}, u32[]{:S(2)}) %collective-permute-start.57) | collective-permute-done | bytes 1441824 | tf_op jit(solution)/shard_map/ppermute | solution.py:190
  586.5 6.6 collective-permute-start.60
  596.5 13.1 %shard_map.346 = (f32[256,11264]{1,0:T(8,128)}, f32[256,11264]{1,0:T(8,128)}, f32[256,11264]{1,0:T(8,128)}) custom-call(s32[1]{0:T(128)} %bitcast.8.core_ref, f32[256,11264]{1,0:T(8,128)} %w_ref.9, f32[256,11264]{1,0:T(8,128)} %m_ref.3, f32[256,11264]{1,0:T(8,128)} %v_ref.3, bf16[256,2816]{1,0:T(8,128)(2,1)S(1)} %broadcast_select_fusion.3.refs_0_, ...), custom_call_target="tpu_custom_call" | custom-call | flops 1024 | bytes 1024 | tf_op jit(solution)/shard_map/pallas_call | solution.py:494
  609.5 9.1 %shard_map.347 = bf16[3,2,2,256,1024]{4,3,2,1,0:T(8,128)(2,1)} custom-call(s32[4]{0:T(128)S(1)} %pad_add_fusion.1.bits_ref, bf16[2,1,768,512]{3,2,1,0:T(8,128)(2,1)S(1)} %pad_maximum_fusion.1.own0_ref, bf16[2,1,768,512]{3,2,1,0:T(8,128)(2,1)S(1)} %collective-permute-done.55.got0_ref, bf16[1,2,768,512]{3,2,1,0:T(8,128)(2,1)S(1)} %pad_maximum_fusion.2.own1_ref, ...), custom_call_target="tpu_custom_call" | custom-call | flops 1024 | bytes 1024 | tf_op jit(solution)/shard_map/pallas_call | solution.py:407
  641.7 5.8 collective-permute-start.63
  663.6 6.1 collective-permute-done.63
  669.7 13.3 %collective-permute-done.64 = bf16[256,2816]{1,0:T(8,128)(2,1)} collective-permute-done((bf16[256,2816]{1,0:T(8,128)(2,1)S(1)}, bf16[256,2816]{1,0:T(8,128)(2,1)}, u32[]{:S(2)}, u32[]{:S(2)}) %collective-permute-start.64) | collective-permute-done | bytes 1441824 | tf_op jit(solution)/shard_map/ppermute | solution.py:198
  697.8 7.7 all-to-all-done.1
  706.5 13.1 %shard_map.348 = (f32[256,11264]{1,0:T(8,128)}, f32[256,11264]{1,0:T(8,128)}, f32[256,11264]{1,0:T(8,128)}) custom-call(s32[1]{0:T(128)} %bitcast.8.core_ref, f32[256,11264]{1,0:T(8,128)} %w_ref.9, f32[256,11264]{1,0:T(8,128)} %m_ref.3, f32[256,11264]{1,0:T(8,128)} %v_ref.3, ...), custom_call_target="tpu_custom_call", output_to_operand_aliasing={{0}: (6, {}), {1}: (7, {}), {2}: (8, {})} | custom-call | flops 1024 | bytes 1024 | tf_op jit(solution)/shard_map/pallas_call | solution.py:494
  725.4 5.5 collective-permute-start.73
  732.9 22.4 %collective-permute-done.75 = f32[7,256]{1,0:T(8,128)S(1)} collective-permute-done((f32[7,256]{1,0:T(8,128)S(1)}, f32[7,256]{1,0:T(8,128)S(1)}, u32[]{:S(2)}, u32[]{:S(2)}) %collective-permute-start.75) | collective-permute-done | bytes 7200 | tf_op jit(solution)/shard_map/ppermute | solution.py:1084
  785.2 6.2 shard_map.351
  791.4 13.7 %collective-permute-done.77 = bf16[512,1024]{1,0:T(8,128)(2,1)S(1)} collective-permute-done((bf16[512,1024]{1,0:T(8,128)(2,1)S(1)}, bf16[512,1024]{1,0:T(8,128)(2,1)S(1)}, u32[]{:S(2)}, u32[]{:S(2)}) %collective-permute-start.77) | collective-permute-done | bytes 1048608 | tf_op jit(solution)/shard_map/ppermute | solution.py:198
  807.7 6.3 shard_map.352
  815.6 11.7 %all_to_all.20 = bf16[8,256,128]{2,1,0:T(8,128)(2,1)S(1)} all-to-all(bf16[8,256,128]{2,1,0:T(8,128)(2,1)S(1)} %bitcast.194), channel_id=1, replica_groups=mesh['rep'=4,'ctx'=4,'shard'=2] {'ctx','shard'}, dimensions={0} | all-to-all | bytes 1048576 | tf_op jit(solution)/shard_map/all_to_all | solution.py:1075
  828.3 6.4 collective-permute-done.81
  838.1 6.2 shard_map.353
  (633 shorter events, 403.7 us)
Async XLA Ops:
  25.2 207.6 %all-gather.2.cloned.1.call-start = ((), (), s32[]{:S(2)}) async-start(), calls=%async_computation.5 | async-start | bytes 4718592 | tf_op jit(solution)/shard_map/all_gather | solution.py:674
  48.9 36.8 %collective-permute-start.3 = (bf16[1536,512]{1,0:T(8,128)(2,1)}, bf16[1536,512]{1,0:T(8,128)(2,1)}, u32[]{:S(2)}, u32[]{:S(2)}) collective-permute-start(bf16[1536,512]{1,0:T(8,128)(2,1)} %convolution_convert_fusion.7), channel_id=1, source_target_pairs={{0,1},{1,0},{2,3},{3,2},{4,5},{5,4},{6,7},{7,6},{8,9},{9,8},{10,11... | collective-permute-start | bytes 4718600 | tf_op jit(solution)/shard_map/ppermute | solution.py:62
  52.0 40.1 %collective-permute-start.5 = (bf16[1536,512]{1,0:T(8,128)(2,1)}, bf16[1536,512]{1,0:T(8,128)(2,1)}, u32[]{:S(2)}, u32[]{:S(2)}) collective-permute-start(bf16[1536,512]{1,0:T(8,128)(2,1)} %convolution_convert_fusion.6), channel_id=1, source_target_pairs={{0,4},{2,6},{4,0},{6,2},{1,5},{3,7},{5,1},{7,3},{8,12},{10,14},{12... | collective-permute-start | bytes 4718600 | tf_op jit(solution)/shard_map/ppermute | solution.py:61
  130.5 683.4 %reduce-scatter.2.cloned.1.call-start = ((), (), s32[]{:S(2)}) async-start(), calls=%async_computation.6 | async-start | bytes 4718592 | tf_op jit(solution)/shard_map/reduce_scatter | solution.py:1029
  194.1 77.6 %collective-permute-start.19 = (bf16[1408,1024]{1,0:T(8,128)(2,1)}, bf16[1408,1024]{1,0:T(8,128)(2,1)}, u32[]{:S(2)}, u32[]{:S(2)}) collective-permute-start(bf16[1408,1024]{1,0:T(8,128)(2,1)} %convolution_convert_fusion.3), channel_id=1, source_target_pairs={{0,1},{1,0},{2,3},{3,2},{4,5},{5,4},{6,7},{7,6},{8,9},{9,8},{10,11... | collective-permute-start | bytes 8650760 | tf_op jit(solution)/shard_map/ppermute | solution.py:62
  198.2 77.4 %collective-permute-start.23 = (bf16[1408,1024]{1,0:T(8,128)(2,1)}, bf16[1408,1024]{1,0:T(8,128)(2,1)}, u32[]{:S(2)}, u32[]{:S(2)}) collective-permute-start(bf16[1408,1024]{1,0:T(8,128)(2,1)} %convolution_convert_fusion.2), channel_id=1, source_target_pairs={{0,4},{2,6},{4,0},{6,2},{1,5},{3,7},{5,1},{7,3},{8,12},{10,14},{12... | collective-permute-start | bytes 8650760 | tf_op jit(solution)/shard_map/ppermute | solution.py:61
  201.0 58.4 %collective-permute-start.20 = (f32[4,2,1,704]{3,0,2,1:T(4,128)S(1)}, f32[4,2,1,704]{3,0,2,1:T(4,128)S(1)}, u32[]{:S(2)}, u32[]{:S(2)}) collective-permute-start(f32[4,2,1,704]{3,0,2,1:T(4,128)S(1)} %constant_dynamic-slice_fusion.2), channel_id=1, source_target_pairs={{0,1},{1,0},{2,3},{3,2},{4,5},{5,4},{6,7},{7,6},{8,9},{9,8},{10,11... | collective-permute-start | bytes 67592 | tf_op jit(solution)/shard_map/ppermute | solution.py:62
  274.7 32.1 %collective-permute-start.22 = (bf16[704,1024]{1,0:T(8,128)(2,1)S(1)}, bf16[704,1024]{1,0:T(8,128)(2,1)S(1)}, u32[]{:S(2)}, u32[]{:S(2)}) collective-permute-start(bf16[704,1024]{1,0:T(8,128)(2,1)S(1)} %get-tuple-element.1178), channel_id=1, source_target_pairs={{0,4},{2,6},{4,0},{6,2},{1,5},{3,7},{5,1},{7,3},{8,12},{10,14},{12... | collective-permute-start | bytes 4325384 | tf_op jit(solution)/shard_map/ppermute | solution.py:61
  279.8 31.7 %collective-permute-start.24 = (bf16[704,1024]{1,0:T(8,128)(2,1)S(1)}, bf16[704,1024]{1,0:T(8,128)(2,1)S(1)}, u32[]{:S(2)}, u32[]{:S(2)}) collective-permute-start(bf16[704,1024]{1,0:T(8,128)(2,1)S(1)} %get-tuple-element.1188), channel_id=1, source_target_pairs={{0,1},{1,0},{2,3},{3,2},{4,5},{5,4},{6,7},{7,6},{8,9},{9,8},{10,11... | collective-permute-start | bytes 4325384 | tf_op jit(solution)/shard_map/ppermute | solution.py:62
  331.6 31.3 %collective-permute-start.30 = (bf16[352,2048]{1,0:T(8,128)(2,1)S(1)}, bf16[352,2048]{1,0:T(8,128)(2,1)S(1)}, u32[]{:S(2)}, u32[]{:S(2)}) collective-permute-start(bf16[352,2048]{1,0:T(8,128)(2,1)S(1)} %get-tuple-element.1233), channel_id=1, source_target_pairs={{0,8},{24,16},{1,9},{25,17},{2,10},{26,18},{3,11},{27,19},{4,12},{... | collective-permute-start | bytes 4325384 | tf_op jit(solution)/shard_map/ppermute | solution.py:195
  338.2 29.6 %collective-permute-start.28 = (bf16[2,1,704,512]{3,2,1,0:T(8,128)(2,1)S(1)}, bf16[2,1,704,512]{3,2,1,0:T(8,128)(2,1)S(1)}, u32[]{:S(2)}, u32[]{:S(2)}) collective-permute-start(bf16[2,1,704,512]{3,2,1,0:T(8,128)(2,1)S(1)} %pad_maximum_fusion.3.own0_ref), channel_id=1, source_target_pairs={{0,1},{1,0},{2,3},{3,2},{4,5},{5,4},{6,7},{7,6},{8,9},{9,8},{10,11... | collective-permute-start | bytes 4325384 | tf_op jit(solution)/shard_map/ppermute | solution.py:62
  339.1 29.3 %collective-permute-start.29 = (bf16[1,2,704,512]{3,2,1,0:T(8,128)(2,1)S(1)}, bf16[1,2,704,512]{3,2,1,0:T(8,128)(2,1)S(1)}, u32[]{:S(2)}, u32[]{:S(2)}) collective-permute-start(bf16[1,2,704,512]{3,2,1,0:T(8,128)(2,1)S(1)} %pad_maximum_fusion.4.own1_ref), channel_id=1, source_target_pairs={{0,4},{2,6},{4,0},{6,2},{1,5},{3,7},{5,1},{7,3},{8,12},{10,14},{12... | collective-permute-start | bytes 4325384 | tf_op jit(solution)/shard_map/ppermute | solution.py:61
  340.4 31.6 %collective-permute-start.32 = (f32[2,1024]{1,0:T(2,128)S(1)}, f32[2,1024]{1,0:T(2,128)S(1)}, u32[]{:S(2)}, u32[]{:S(2)}) collective-permute-start(f32[2,1024]{1,0:T(2,128)S(1)} %add.386), channel_id=1, source_target_pairs={{0,4},{2,6},{4,0},{6,2},{1,5},{3,7},{5,1},{7,3},{8,12},{10,14},{12... | collective-permute-start | bytes 24584 | tf_op jit(solution)/shard_map/ppermute | solution.py:61
  374.1 35.7 %collective-permute-start.31 = (bf16[352,2048]{1,0:T(8,128)(2,1)}, bf16[352,2048]{1,0:T(8,128)(2,1)S(1)}, u32[]{:S(2)}, u32[]{:S(2)}) collective-permute-start(bf16[352,2048]{1,0:T(8,128)(2,1)} %get-tuple-element.1271), channel_id=1, source_target_pairs={{0,8},{24,16},{1,9},{25,17},{2,10},{26,18},{3,11},{27,19},{4,12},{... | collective-permute-start | bytes 4325384 | tf_op jit(solution)/shard_map/ppermute | solution.py:195
  378.1 31.7 %collective-permute-start.34 = (bf16[352,2048]{1,0:T(8,128)(2,1)}, bf16[352,2048]{1,0:T(8,128)(2,1)S(1)}, u32[]{:S(2)}, u32[]{:S(2)}) collective-permute-start(bf16[352,2048]{1,0:T(8,128)(2,1)} %reduce-precision_convert_fusion.11), channel_id=1, source_target_pairs={{8,16},{16,8},{9,17},{17,9},{10,18},{18,10},{11,19},{19,11},{12,20... | collective-permute-start | bytes 4325384 | tf_op jit(solution)/shard_map/ppermute | solution.py:201
  389.8 48.6 %collective-permute-start.37 = (bf16[2,1,704,512]{3,2,1,0:T(8,128)(2,1)S(1)}, bf16[2,1,704,512]{3,2,1,0:T(8,128)(2,1)}, u32[]{:S(2)}, u32[]{:S(2)}) collective-permute-start(bf16[2,1,704,512]{3,2,1,0:T(8,128)(2,1)S(1)} %pad_maximum_fusion.5.own0_ref), channel_id=1, source_target_pairs={{0,1},{1,0},{2,3},{3,2},{4,5},{5,4},{6,7},{7,6},{8,9},{9,8},{10,11... | collective-permute-start | bytes 4325384 | tf_op jit(solution)/shard_map/ppermute | solution.py:62
  390.5 47.8 %collective-permute-start.38 = (bf16[1,2,704,512]{3,2,1,0:T(8,128)(2,1)}, bf16[1,2,704,512]{3,2,1,0:T(8,128)(2,1)}, u32[]{:S(2)}, u32[]{:S(2)}) collective-permute-start(bf16[1,2,704,512]{3,2,1,0:T(8,128)(2,1)} %pad_maximum_fusion.6.own1_ref), channel_id=1, source_target_pairs={{0,4},{2,6},{4,0},{6,2},{1,5},{3,7},{5,1},{7,3},{8,12},{10,14},{12... | collective-permute-start | bytes 4325384 | tf_op jit(solution)/shard_map/ppermute | solution.py:61
  416.1 36.7 %collective-permute-start.40 = (bf16[256,2816]{1,0:T(8,128)(2,1)}, bf16[256,2816]{1,0:T(8,128)(2,1)}, u32[]{:S(2)}, u32[]{:S(2)}) collective-permute-start(bf16[256,2816]{1,0:T(8,128)(2,1)} %get-tuple-element.1313), channel_id=1, source_target_pairs={{0,8},{24,16},{1,9},{25,17},{2,10},{26,18},{3,11},{27,19},{4,12},{... | collective-permute-start | bytes 4325384 | tf_op jit(solution)/shard_map/ppermute | solution.py:195
  422.8 35.2 %collective-permute-start.41 = (bf16[352,2048]{1,0:T(8,128)(2,1)}, bf16[352,2048]{1,0:T(8,128)(2,1)}, u32[]{:S(2)}, u32[]{:S(2)}) collective-permute-start(bf16[352,2048]{1,0:T(8,128)(2,1)} %reduce-precision_convert_fusion.9), channel_id=1, source_target_pairs={{8,0},{16,24},{9,1},{17,25},{10,2},{18,26},{11,3},{19,27},{12,4},{... | collective-permute-start | bytes 4325384 | tf_op jit(solution)/shard_map/ppermute | solution.py:198
  424.1 34.0 %collective-permute-start.42 = (bf16[352,2048]{1,0:T(8,128)(2,1)}, bf16[352,2048]{1,0:T(8,128)(2,1)}, u32[]{:S(2)}, u32[]{:S(2)}) collective-permute-start(bf16[352,2048]{1,0:T(8,128)(2,1)} %reduce-precision_convert_fusion.10), channel_id=1, source_target_pairs={{8,16},{16,8},{9,17},{17,9},{10,18},{18,10},{11,19},{19,11},{12,20... | collective-permute-start | bytes 4325384 | tf_op jit(solution)/shard_map/ppermute | solution.py:201
  450.7 24.1 %collective-permute-start.39 = (f32[256,1024]{1,0:T(8,128)S(1)}, f32[256,1024]{1,0:T(8,128)S(1)}, u32[]{:S(2)}, u32[]{:S(2)}) collective-permute-start(f32[256,1024]{1,0:T(8,128)S(1)} %get-tuple-element.1755), channel_id=1, source_target_pairs={{0,2},{2,0},{4,6},{6,4},{1,3},{3,1},{5,7},{7,5},{8,10},{10,8},{12,... | collective-permute-start | bytes 3145736 | tf_op jit(solution)/shard_map/ppermute | solution.py:57
  462.8 36.6 %collective-permute-start.47 = (bf16[256,2816]{1,0:T(8,128)(2,1)S(1)}, bf16[256,2816]{1,0:T(8,128)(2,1)S(1)}, u32[]{:S(2)}, u32[]{:S(2)}) collective-permute-start(bf16[256,2816]{1,0:T(8,128)(2,1)S(1)} %copy-done.95), channel_id=1, source_target_pairs={{0,8},{24,16},{1,9},{25,17},{2,10},{26,18},{3,11},{27,19},{4,12},{... | collective-permute-start | bytes 4325384 | tf_op jit(solution)/shard_map/ppermute | solution.py:195
  470.1 33.5 %collective-permute-start.48 = (bf16[352,2048]{1,0:T(8,128)(2,1)S(1)}, bf16[352,2048]{1,0:T(8,128)(2,1)S(1)}, u32[]{:S(2)}, u32[]{:S(2)}) collective-permute-start(bf16[352,2048]{1,0:T(8,128)(2,1)S(1)} %reduce-precision_convert_fusion.7), channel_id=1, source_target_pairs={{8,0},{16,24},{9,1},{17,25},{10,2},{18,26},{11,3},{19,27},{12,4},{... | collective-permute-start | bytes 4325384 | tf_op jit(solution)/shard_map/ppermute | solution.py:198
  471.4 32.2 %collective-permute-start.49 = (bf16[256,2816]{1,0:T(8,128)(2,1)S(1)}, bf16[256,2816]{1,0:T(8,128)(2,1)}, u32[]{:S(2)}, u32[]{:S(2)}) collective-permute-start(bf16[256,2816]{1,0:T(8,128)(2,1)S(1)} %reduce-precision_convert_fusion.8), channel_id=1, source_target_pairs={{8,16},{16,8},{9,17},{17,9},{10,18},{18,10},{11,19},{19,11},{12,20... | collective-permute-start | bytes 4325384 | tf_op jit(solution)/shard_map/ppermute | solution.py:201
  484.9 23.7 %collective-permute-start.45 = (bf16[2,1,256,512]{3,2,1,0:T(8,128)(2,1)S(1)}, bf16[2,1,256,512]{3,2,1,0:T(8,128)(2,1)S(1)}, u32[]{:S(2)}, u32[]{:S(2)}) collective-permute-start(bf16[2,1,256,512]{3,2,1,0:T(8,128)(2,1)S(1)} %pad_maximum_fusion.12.own0_ref), channel_id=1, source_target_pairs={{0,1},{1,0},{2,3},{3,2},{4,5},{5,4},{6,7},{7,6},{8,9},{9,8},{10,11... | collective-permute-start | bytes 1572872 | tf_op jit(solution)/shard_map/ppermute | solution.py:62
  485.9 22.7 %collective-permute-start.46 = (bf16[1,2,256,512]{3,2,1,0:T(8,128)(2,1)S(1)}, bf16[1,2,256,512]{3,2,1,0:T(8,128)(2,1)S(1)}, u32[]{:S(2)}, u32[]{:S(2)}) collective-permute-start(bf16[1,2,256,512]{3,2,1,0:T(8,128)(2,1)S(1)} %pad_maximum_fusion.13.own1_ref), channel_id=1, source_target_pairs={{0,4},{2,6},{4,0},{6,2},{1,5},{3,7},{5,1},{7,3},{8,12},{10,14},{12... | collective-permute-start | bytes 1572872 | tf_op jit(solution)/shard_map/ppermute | solution.py:61
  510.6 35.9 %collective-permute-start.53 = (bf16[256,2816]{1,0:T(8,128)(2,1)}, bf16[256,2816]{1,0:T(8,128)(2,1)}, u32[]{:S(2)}, u32[]{:S(2)}) collective-permute-start(bf16[256,2816]{1,0:T(8,128)(2,1)} %fusion), channel_id=1, source_target_pairs={{0,8},{8,0},{16,24},{24,16},{1,9},{9,1},{17,25},{25,17},{2,10},{10... | collective-permute-start | bytes 4325384 | tf_op jit(solution)/shard_map/ppermute | solution.py:190
  514.0 32.6 %collective-permute-start.54 = (bf16[256,2816]{1,0:T(8,128)(2,1)}, bf16[256,2816]{1,0:T(8,128)(2,1)}, u32[]{:S(2)}, u32[]{:S(2)}) collective-permute-start(bf16[256,2816]{1,0:T(8,128)(2,1)} %reduce-precision_convert_fusion.6), channel_id=1, source_target_pairs={{8,16},{16,8},{9,17},{17,9},{10,18},{18,10},{11,19},{19,11},{12,20... | collective-permute-start | bytes 4325384 | tf_op jit(solution)/shard_map/ppermute | solution.py:201
  533.2 23.5 %collective-permute-start.51 = (bf16[1,1,768,512]{3,2,1,0:T(8,128)(2,1)S(1)}, bf16[1,1,768,512]{3,2,1,0:T(8,128)(2,1)}, u32[]{:S(2)}, u32[]{:S(2)}) collective-permute-start(bf16[1,1,768,512]{3,2,1,0:T(8,128)(2,1)S(1)} %bitcast.168), channel_id=1, source_target_pairs={{0,4},{2,6},{4,0},{6,2},{1,5},{3,7},{5,1},{7,3},{8,12},{10,14},{12... | collective-permute-start | bytes 2359304 | tf_op jit(solution)/shard_map/ppermute | solution.py:61
  550.5 35.2 %collective-permute-start.57 = (bf16[256,2816]{1,0:T(8,128)(2,1)S(1)}, bf16[256,2816]{1,0:T(8,128)(2,1)S(1)}, u32[]{:S(2)}, u32[]{:S(2)}) collective-permute-start(bf16[256,2816]{1,0:T(8,128)(2,1)S(1)} %fusion.1), channel_id=1, source_target_pairs={{0,8},{8,0},{16,24},{24,16},{1,9},{9,1},{17,25},{25,17},{2,10},{10... | collective-permute-start | bytes 4325384 | tf_op jit(solution)/shard_map/ppermute | solution.py:190
  554.2 31.5 %collective-permute-start.58 = (bf16[256,2816]{1,0:T(8,128)(2,1)S(1)}, bf16[256,2816]{1,0:T(8,128)(2,1)S(1)}, u32[]{:S(2)}, u32[]{:S(2)}) collective-permute-start(bf16[256,2816]{1,0:T(8,128)(2,1)S(1)} %reduce-precision_convert_fusion.4), channel_id=1, source_target_pairs={{8,16},{16,8},{9,17},{17,9},{10,18},{18,10},{11,19},{19,11},{12,20... | collective-permute-start | bytes 4325384 | tf_op jit(solution)/shard_map/ppermute | solution.py:201
  556.6 37.8 %collective-permute-start.59 = (bf16[256,2816]{1,0:T(8,128)(2,1)S(1)}, bf16[256,2816]{1,0:T(8,128)(2,1)S(1)}, u32[]{:S(2)}, u32[]{:S(2)}) collective-permute-start(bf16[256,2816]{1,0:T(8,128)(2,1)S(1)} %broadcast_select_fusion.2), channel_id=1, source_target_pairs={{0,2},{2,0},{4,6},{6,4},{1,3},{3,1},{5,7},{7,5},{8,10},{10,8},{12,... | collective-permute-start | bytes 4325384 | tf_op jit(solution)/shard_map/ppermute | solution.py:57
  559.5 50.0 %collective-permute-start.55 = (bf16[2,1,768,512]{3,2,1,0:T(8,128)(2,1)S(1)}, bf16[2,1,768,512]{3,2,1,0:T(8,128)(2,1)S(1)}, u32[]{:S(2)}, u32[]{:S(2)}) collective-permute-start(bf16[2,1,768,512]{3,2,1,0:T(8,128)(2,1)S(1)} %pad_maximum_fusion.1.own0_ref), channel_id=1, source_target_pairs={{0,1},{1,0},{2,3},{3,2},{4,5},{5,4},{6,7},{7,6},{8,9},{9,8},{10,11... | collective-permute-start | bytes 4718600 | tf_op jit(solution)/shard_map/ppermute | solution.py:62
  560.8 48.7 %collective-permute-start.56 = (bf16[1,2,768,512]{3,2,1,0:T(8,128)(2,1)S(1)}, bf16[1,2,768,512]{3,2,1,0:T(8,128)(2,1)}, u32[]{:S(2)}, u32[]{:S(2)}) collective-permute-start(bf16[1,2,768,512]{3,2,1,0:T(8,128)(2,1)S(1)} %pad_maximum_fusion.2.own1_ref), channel_id=1, source_target_pairs={{0,4},{2,6},{4,0},{6,2},{1,5},{3,7},{5,1},{7,3},{8,12},{10,14},{12... | collective-permute-start | bytes 4718600 | tf_op jit(solution)/shard_map/ppermute | solution.py:61
  586.5 38.1 %collective-permute-start.60 = (bf16[512,1024]{1,0:T(8,128)(2,1)S(1)}, bf16[512,1024]{1,0:T(8,128)(2,1)}, u32[]{:S(2)}, u32[]{:S(2)}) collective-permute-start(bf16[512,1024]{1,0:T(8,128)(2,1)S(1)} %pad_maximum_fusion.8), channel_id=1, source_target_pairs={{0,8},{24,16},{1,9},{25,17},{2,10},{26,18},{3,11},{27,19},{4,12},{... | collective-permute-start | bytes 3145736 | tf_op jit(solution)/shard_map/ppermute | solution.py:195
  593.0 34.0 %collective-permute-start.61 = (bf16[256,2816]{1,0:T(8,128)(2,1)S(1)}, bf16[256,2816]{1,0:T(8,128)(2,1)S(1)}, u32[]{:S(2)}, u32[]{:S(2)}) collective-permute-start(bf16[256,2816]{1,0:T(8,128)(2,1)S(1)} %reduce-precision_convert_fusion.1), channel_id=1, source_target_pairs={{8,0},{16,24},{9,1},{17,25},{10,2},{18,26},{11,3},{19,27},{12,4},{... | collective-permute-start | bytes 4325384 | tf_op jit(solution)/shard_map/ppermute | solution.py:198
  594.3 32.7 %collective-permute-start.62 = (bf16[256,2816]{1,0:T(8,128)(2,1)S(1)}, bf16[256,2816]{1,0:T(8,128)(2,1)}, u32[]{:S(2)}, u32[]{:S(2)}) collective-permute-start(bf16[256,2816]{1,0:T(8,128)(2,1)S(1)} %reduce-precision_convert_fusion.2), channel_id=1, source_target_pairs={{8,16},{16,8},{9,17},{17,9},{10,18},{18,10},{11,19},{19,11},{12,20... | collective-permute-start | bytes 4325384 | tf_op jit(solution)/shard_map/ppermute | solution.py:201
  641.7 28.0 %collective-permute-start.63 = (bf16[512,1024]{1,0:T(8,128)(2,1)}, bf16[512,1024]{1,0:T(8,128)(2,1)}, u32[]{:S(2)}, u32[]{:S(2)}) collective-permute-start(bf16[512,1024]{1,0:T(8,128)(2,1)} %convolution_convert_fusion.10), channel_id=1, source_target_pairs={{0,8},{24,16},{1,9},{25,17},{2,10},{26,18},{3,11},{27,19},{4,12},{... | collective-permute-start | bytes 3145736 | tf_op jit(solution)/shard_map/ppermute | solution.py:195
  647.5 35.6 %collective-permute-start.64 = (bf16[256,2816]{1,0:T(8,128)(2,1)S(1)}, bf16[256,2816]{1,0:T(8,128)(2,1)}, u32[]{:S(2)}, u32[]{:S(2)}) collective-permute-start(bf16[256,2816]{1,0:T(8,128)(2,1)S(1)} %reduce-precision_convert_fusion), channel_id=1, source_target_pairs={{8,0},{16,24},{9,1},{17,25},{10,2},{18,26},{11,3},{19,27},{12,4},{... | collective-permute-start | bytes 4325384 | tf_op jit(solution)/shard_map/ppermute | solution.py:198
  663.2 43.3 %collective-permute-start.72 = (bf16[256,2816]{1,0:T(8,128)(2,1)}, bf16[256,2816]{1,0:T(8,128)(2,1)S(1)}, u32[]{:S(2)}, u32[]{:S(2)}) collective-permute-start(bf16[256,2816]{1,0:T(8,128)(2,1)} %broadcast_select_fusion), channel_id=1, source_target_pairs={{0,2},{2,0},{4,6},{6,4},{1,3},{3,1},{5,7},{7,5},{8,10},{10,8},{12,... | collective-permute-start | bytes 4325384 | tf_op jit(solution)/shard_map/ppermute | solution.py:57
  689.5 30.1 %collective-permute-start.70 = (bf16[512,1024]{1,0:T(8,128)(2,1)}, bf16[512,1024]{1,0:T(8,128)(2,1)}, u32[]{:S(2)}, u32[]{:S(2)}) collective-permute-start(bf16[512,1024]{1,0:T(8,128)(2,1)} %fusion.4), channel_id=1, source_target_pairs={{0,8},{8,0},{16,24},{24,16},{1,9},{9,1},{17,25},{25,17},{2,10},{10... | collective-permute-start | bytes 3145736 | tf_op jit(solution)/shard_map/ppermute | solution.py:190
  689.5 30.1 %collective-permute-start.71 = (bf16[512,1024]{1,0:T(8,128)(2,1)}, bf16[512,1024]{1,0:T(8,128)(2,1)}, u32[]{:S(2)}, u32[]{:S(2)}) collective-permute-start(bf16[512,1024]{1,0:T(8,128)(2,1)} %reduce-precision_convert_fusion.18), channel_id=1, source_target_pairs={{8,16},{16,8},{9,17},{17,9},{10,18},{18,10},{11,19},{19,11},{12,20... | collective-permute-start | bytes 3145736 | tf_op jit(solution)/shard_map/ppermute | solution.py:201
  725.4 49.0 %collective-permute-start.73 = (bf16[512,1024]{1,0:T(8,128)(2,1)}, bf16[512,1024]{1,0:T(8,128)(2,1)}, u32[]{:S(2)}, u32[]{:S(2)}) collective-permute-start(bf16[512,1024]{1,0:T(8,128)(2,1)} %fusion.5), channel_id=1, source_target_pairs={{0,8},{8,0},{16,24},{24,16},{1,9},{9,1},{17,25},{25,17},{2,10},{10... | collective-permute-start | bytes 3145736 | tf_op jit(solution)/shard_map/ppermute | solution.py:190
  730.9 43.5 %collective-permute-start.74 = (bf16[512,1024]{1,0:T(8,128)(2,1)}, bf16[512,1024]{1,0:T(8,128)(2,1)}, u32[]{:S(2)}, u32[]{:S(2)}) collective-permute-start(bf16[512,1024]{1,0:T(8,128)(2,1)} %reduce-precision_convert_fusion.16), channel_id=1, source_target_pairs={{8,16},{16,8},{9,17},{17,9},{10,18},{18,10},{11,19},{19,11},{12,20... | collective-permute-start | bytes 3145736 | tf_op jit(solution)/shard_map/ppermute | solution.py:201
  732.6 22.7 %collective-permute-start.75 = (f32[7,256]{1,0:T(8,128)S(1)}, f32[7,256]{1,0:T(8,128)S(1)}, u32[]{:S(2)}, u32[]{:S(2)}) collective-permute-start(f32[7,256]{1,0:T(8,128)S(1)} %concatenate.111), channel_id=1, source_target_pairs={{0,8},{8,0},{16,24},{24,16},{1,9},{9,1},{17,25},{25,17},{2,10},{10... | collective-permute-start | bytes 21512 | tf_op jit(solution)/shard_map/ppermute | solution.py:1084
  778.0 27.1 %collective-permute-start.77 = (bf16[512,1024]{1,0:T(8,128)(2,1)S(1)}, bf16[512,1024]{1,0:T(8,128)(2,1)S(1)}, u32[]{:S(2)}, u32[]{:S(2)}) collective-permute-start(bf16[512,1024]{1,0:T(8,128)(2,1)S(1)} %reduce-precision_convert_fusion.13), channel_id=1, source_target_pairs={{8,0},{16,24},{9,1},{17,25},{10,2},{18,26},{11,3},{19,27},{12,4},{... | collective-permute-start | bytes 3145736 | tf_op jit(solution)/shard_map/ppermute | solution.py:198
  779.3 25.8 %collective-permute-start.78 = (bf16[512,1024]{1,0:T(8,128)(2,1)S(1)}, bf16[512,1024]{1,0:T(8,128)(2,1)S(1)}, u32[]{:S(2)}, u32[]{:S(2)}) collective-permute-start(bf16[512,1024]{1,0:T(8,128)(2,1)S(1)} %reduce-precision_convert_fusion.14), channel_id=1, source_target_pairs={{8,16},{16,8},{9,17},{17,9},{10,18},{18,10},{11,19},{19,11},{12,20... | collective-permute-start | bytes 3145736 | tf_op jit(solution)/shard_map/ppermute | solution.py:201
  805.8 28.9 %collective-permute-start.81 = (bf16[512,1024]{1,0:T(8,128)(2,1)S(1)}, bf16[512,1024]{1,0:T(8,128)(2,1)}, u32[]{:S(2)}, u32[]{:S(2)}) collective-permute-start(bf16[512,1024]{1,0:T(8,128)(2,1)S(1)} %reduce-precision_convert_fusion.12), channel_id=1, source_target_pairs={{8,0},{16,24},{9,1},{17,25},{10,2},{18,26},{11,3},{19,27},{12,4},{... | collective-permute-start | bytes 3145736 | tf_op jit(solution)/shard_map/ppermute | solution.py:198
  (171 other events, 1012.6 us)
Sparse Core Ops, SparseCore 0:
  130.7 50.7 all-gather.1
  658.0 54.2 reduce-scatter.1
